TPU v7x, 128 devices: a whole 4x4x4 slice. The times are simulated.
128 devices in a mesh: ctx: 8 (over z_hi, y), exp: 16 (over x, z_lo, core).
Axes of the slice: x: 4, y: 4, z: 4 (z_hi: 2, z_lo: 2; z = z_hi * 2 + z_lo), core: 2. Of those that a mesh axis runs over, the one named last changes fastest.
Arguments:
- tokens: bfloat16 [16, 1024, 1536], P('exp', 'ctx'), may hold values from -6 to 6
- routes: int32 [16, 1024, 6], P('exp', 'ctx'), may hold values from 0 to 31, all different within a row; in each aligned block of 128 rows (0 to 127, 128 to 255, ..., all dimensions but the last counted through in order) at most 48 rows name the same one
- route_gates: float32 [16, 1024, 6], P('exp', 'ctx'), may hold values from 0.1 to 0.25
- norm_attn: bfloat16 [1536], P('exp'), may hold values from 0.099609375 to 1.8984375
- norm_ffn: bfloat16 [1536], P('exp'), may hold values from 0.099609375 to 1.8984375
- query_weight: bfloat16 [1536, 1536], P('exp'), may hold values from -0.3125 to 0.3125
- key_weight: bfloat16 [1536, 512], P('exp'), may hold values from -0.15625 to 0.15625
- value_weight: bfloat16 [1536, 512], P('exp'), may hold values from -0.15625 to 0.15625
- out_weight: bfloat16 [1536, 1536], P('exp'), may hold values from -0.625 to 0.625
- shared_gate: bfloat16 [1536, 1024], P('exp'), may hold values from -0.15625 to 0.15625
- shared_up: bfloat16 [1536, 1024], P('exp'), may hold values from -0.15625 to 0.15625
- shared_down: bfloat16 [1024, 1536], P('exp'), may hold values from -0.375 to 0.375
- expert_gate: bfloat16 [32, 1536, 512], P('exp'), may hold values from -0.15625 to 0.15625
- expert_up: bfloat16 [32, 1536, 512], P('exp'), may hold values from -0.15625 to 0.15625
- expert_down: bfloat16 [32, 512, 1536], P('exp'), may hold values from -0.75 to 0.75
- cotangent: bfloat16 [16, 1024, 1536], P('exp', 'ctx'), may hold values from -6 to 6
Outputs:
- mixed: bfloat16 [16, 1024, 1536], P('exp', 'ctx')
- input_grad: bfloat16 [16, 1024, 1536], P('exp', 'ctx')
- grad_norm_attn: float32 [1536], P('exp')
- grad_norm_ffn: float32 [1536], P('exp')
- grad_query: float32 [1536, 1536], P('exp')
- grad_key: float32 [1536, 512], P('exp')
- grad_value: float32 [1536, 512], P('exp')
- grad_out: float32 [1536, 1536], P('exp')
- grad_shared_gate: float32 [1536, 1024], P('exp')
- grad_shared_up: float32 [1536, 1024], P('exp')
- grad_shared_down: float32 [1024, 1536], P('exp')
- grad_expert_gate: float32 [32, 1536, 512], P('exp')
- grad_expert_up: float32 [32, 1536, 512], P('exp')
- grad_expert_down: float32 [32, 512, 1536], P('exp')
Inputs may be any that keep to these rules, and one draw needn't show every extreme that they name: `routes`: each token names 6 different experts. Among the 128 tokens of one device (aligned blocks of positions) no expert is named by more than 48 tokens, and in some blocks one is named by exactly 48.
All inputs are finite; a program needn't handle non-finite values.
Results may differ from a plain program's by a relative error of at most 0.028.
Values may be sent and summed in bfloat16 or wider, within the bound.
No kernel may reach another device: no remote copies, remote signals or barrier semaphores. Data moves between devices by JAX's collectives and lax.ppermute only.
A program may use at most 192 MiB of HBM per device.

v0:
```python
import jax
import jax.numpy as jnp
from jax import lax
from jax.sharding import PartitionSpec as P

HEADS = 12
KV_HEADS = 4
HEAD_DIM = 128
TOPK = 6
GROUP = 3


epsilon = 1e-05
masked_score = -1e30
top_precision = lax.Precision.HIGHEST


def silu_slope(operand):
    sigmoid_v = jax.nn.sigmoid(operand)
    return sigmoid_v * (1.0 + operand * (1.0 - sigmoid_v))


def norm_back(grad_normed, normed, inv_root):
    return inv_root * (
        grad_normed - normed * jnp.mean(grad_normed * normed, axis=-1, keepdims=True)
    )


def on_device(
    tokens,
    routes,
    route_gates,
    norm_attn,
    norm_ffn,
    query_weight,
    key_weight,
    value_weight,
    out_weight,
    shared_gate,
    shared_up,
    shared_down,
    expert_gate,
    expert_up,
    expert_down,
    cotangent,
):
    gathered = (
        lax.all_gather(norm_attn, "exp", axis=0, tiled=True),
        lax.all_gather(norm_ffn, "exp", axis=0, tiled=True),
        lax.all_gather(query_weight, "exp", axis=0, tiled=True),
        lax.all_gather(key_weight, "exp", axis=0, tiled=True),
        lax.all_gather(value_weight, "exp", axis=0, tiled=True),
        lax.all_gather(out_weight, "exp", axis=0, tiled=True),
        lax.all_gather(shared_gate, "exp", axis=0, tiled=True),
        lax.all_gather(shared_up, "exp", axis=0, tiled=True),
        lax.all_gather(shared_down, "exp", axis=0, tiled=True),
    )
    gain_attn = gathered[0].astype(jnp.float32)
    gain_ffn = gathered[1].astype(jnp.float32)
    wquery, wkeys, wvalues, wattn_out, wsgate, wsup, wsdown = gathered[2:]
    block_len = tokens.shape[1]
    model_width = tokens.shape[2]
    head_scale = HEAD_DIM ** (-0.5)
    inputs = tokens[0].astype(jnp.float32)
    first_row = lax.axis_index("ctx") * block_len
    final_row = first_row + block_len - 1
    query_rows = first_row + jnp.arange(block_len, dtype=jnp.int32)
    scale_one = lax.rsqrt(jnp.mean(inputs * inputs, axis=-1, keepdims=True) + epsilon)
    normed_one = inputs * scale_one
    hidden_one = (normed_one * gain_attn).astype(jnp.bfloat16)
    queries = (
        jnp.dot(hidden_one, wquery, preferred_element_type=jnp.float32)
        .astype(jnp.bfloat16)
        .reshape(block_len, KV_HEADS, GROUP, HEAD_DIM)
    )
    key_rows = jnp.dot(hidden_one, wkeys, preferred_element_type=jnp.float32).astype(jnp.bfloat16)
    value_rows = jnp.dot(hidden_one, wvalues, preferred_element_type=jnp.float32).astype(
        jnp.bfloat16
    )

    def piece_scores(key_piece):
        part_keys = key_piece.reshape(-1, KV_HEADS, HEAD_DIM)
        columns = jnp.arange(part_keys.shape[0], dtype=jnp.int32)
        allowed = query_rows[:, None] >= columns[None, :]
        raw_scores = (
            jnp.einsum("tgjd,sgd->gjts", queries, part_keys, preferred_element_type=jnp.float32)
            * head_scale
        )
        return (jnp.where(allowed, raw_scores, masked_score), allowed, part_keys)

    start_state = (
        jnp.full((KV_HEADS, GROUP, block_len), masked_score, jnp.float32),
        jnp.zeros((KV_HEADS, GROUP, block_len), jnp.float32),
        jnp.zeros((KV_HEADS, GROUP, block_len, HEAD_DIM), jnp.float32),
    )
    pieces = (
        lax.all_gather(key_rows, "ctx", axis=0, tiled=True),
        lax.all_gather(value_rows, "ctx", axis=0, tiled=True),
    )

    def compute(current):
        running_max, accumulated_sum, running_out = current
        raw_scores, allowed, part_keys = piece_scores(pieces[0])
        part_values = pieces[1].reshape(-1, KV_HEADS, HEAD_DIM)
        new_max = jnp.maximum(running_max, jnp.max(raw_scores, axis=-1))
        weights = jnp.where(allowed, jnp.exp(raw_scores - new_max[..., None]), 0.0)
        accumulated_sum = jnp.sum(weights, axis=-1)
        running_out = jnp.einsum(
            "gjts,sgd->gjtd", weights, part_values.astype(jnp.float32), precision=top_precision
        )
        return (new_max, accumulated_sum, running_out)

    running_max, accumulated_sum, running_out = lax.cond(
        jnp.int32(0) <= final_row, compute, lambda current: current, start_state
    )
    log_total = running_max + jnp.log(accumulated_sum)
    attended_heads = running_out / accumulated_sum[..., None]
    attended = (
        attended_heads.transpose(2, 0, 1, 3)
        .reshape(block_len, HEADS * HEAD_DIM)
        .astype(jnp.bfloat16)
    )
    middle = inputs + jnp.dot(attended, wattn_out, preferred_element_type=jnp.float32)
    second_scale = lax.rsqrt(jnp.mean(middle * middle, axis=-1, keepdims=True) + epsilon)
    normed_two = middle * second_scale
    hidden_two = (normed_two * gain_ffn).astype(jnp.bfloat16)
    shared_pre_gate = jnp.dot(hidden_two, wsgate, preferred_element_type=jnp.float32)
    shared_pre_up = jnp.dot(hidden_two, wsup, preferred_element_type=jnp.float32)
    shared_hidden = (jax.nn.silu(shared_pre_gate) * shared_pre_up).astype(jnp.bfloat16)
    shared_out = jnp.dot(shared_hidden, wsdown, preferred_element_type=jnp.float32)
    local_experts = expert_gate.shape[0]
    groups_exp = lax.axis_size("exp")
    experts_all = local_experts * groups_exp
    capacity = min(block_len, 12 * block_len // experts_all)
    pair_expert = routes[0].reshape(-1)
    onehot = (pair_expert[:, None] == jnp.arange(experts_all, dtype=jnp.int32)[None, :]).astype(
        jnp.int32
    )
    earlier = jnp.cumsum(onehot, axis=0) - onehot
    pair_slots = jnp.sum(earlier * onehot, axis=1)
    pair_flat = pair_expert * capacity + pair_slots
    pair_token = jnp.arange(pair_expert.shape[0], dtype=jnp.int32) // TOPK
    slot_token = (
        jnp.full((experts_all * capacity,), block_len, jnp.int32).at[pair_flat].set(pair_token)
    )
    slot_gate = (
        jnp.zeros((experts_all * capacity,), jnp.float32)
        .at[pair_flat]
        .set(route_gates[0].reshape(-1))
    )
    padded_two = jnp.concatenate([hidden_two, jnp.zeros((1, model_width), jnp.bfloat16)], axis=0)
    outgoing = padded_two[slot_token].reshape(groups_exp, local_experts * capacity, model_width)
    arrived = lax.all_to_all(outgoing, "exp", split_axis=0, concat_axis=0, tiled=True).reshape(
        groups_exp, local_experts, capacity, model_width
    )
    pre_gate = jnp.einsum(
        "sjcd,jdf->sjcf", arrived, expert_gate, preferred_element_type=jnp.float32
    )
    pre_up = jnp.einsum("sjcd,jdf->sjcf", arrived, expert_up, preferred_element_type=jnp.float32)
    expert_hidden = (jax.nn.silu(pre_gate) * pre_up).astype(jnp.bfloat16)
    expert_out = jnp.einsum(
        "sjcf,jfd->sjcd", expert_hidden, expert_down, preferred_element_type=jnp.float32
    ).astype(jnp.bfloat16)
    returned = lax.all_to_all(
        expert_out.reshape(groups_exp, local_experts * capacity, model_width),
        "exp",
        split_axis=0,
        concat_axis=0,
        tiled=True,
    )
    returned = returned.reshape(experts_all * capacity, model_width)
    picked = returned[pair_flat].astype(jnp.float32).reshape(block_len, TOPK, model_width)
    routed = jnp.sum(route_gates[0][..., None] * picked, axis=1)
    mixed = (middle + shared_out + routed).astype(jnp.bfloat16)[None]
    upstream = cotangent[0]
    upstream_f = upstream.astype(jnp.float32)
    padded_up = jnp.concatenate([upstream_f, jnp.zeros((1, model_width), jnp.float32)], axis=0)
    grad_send = (
        (slot_gate[:, None] * padded_up[slot_token])
        .astype(jnp.bfloat16)
        .reshape(groups_exp, local_experts * capacity, model_width)
    )
    grad_arrived = lax.all_to_all(
        grad_send, "exp", split_axis=0, concat_axis=0, tiled=True
    ).reshape(groups_exp, local_experts, capacity, model_width)
    grad_hidden_e = jnp.einsum(
        "sjcd,jfd->sjcf", grad_arrived, expert_down, preferred_element_type=jnp.float32
    )
    grad_edown = jnp.einsum(
        "sjcf,sjcd->jfd", expert_hidden, grad_arrived, preferred_element_type=jnp.float32
    )
    grad_pre_gate = (grad_hidden_e * pre_up * silu_slope(pre_gate)).astype(jnp.bfloat16)
    grad_pre_up = (grad_hidden_e * jax.nn.silu(pre_gate)).astype(jnp.bfloat16)
    grad_egate = jnp.einsum(
        "sjcd,sjcf->jdf", arrived, grad_pre_gate, preferred_element_type=jnp.float32
    )
    grad_expert_up_weight = jnp.einsum(
        "sjcd,sjcf->jdf", arrived, grad_pre_up, preferred_element_type=jnp.float32
    )
    grad_back = jnp.einsum(
        "sjcf,jdf->sjcd", grad_pre_gate, expert_gate, preferred_element_type=jnp.float32
    ) + jnp.einsum("sjcf,jdf->sjcd", grad_pre_up, expert_up, preferred_element_type=jnp.float32)
    grad_back = grad_back.astype(jnp.bfloat16).reshape(
        groups_exp, local_experts * capacity, model_width
    )
    grad_home = lax.all_to_all(grad_back, "exp", split_axis=0, concat_axis=0, tiled=True).reshape(
        experts_all * capacity, model_width
    )
    grad_routed = jnp.sum(
        grad_home[pair_flat].astype(jnp.float32).reshape(block_len, TOPK, model_width), axis=1
    )
    grad_shared_hid = jnp.dot(upstream, wsdown.T, preferred_element_type=jnp.float32)
    grad_shared_down_weight = jnp.dot(shared_hidden.T, upstream, preferred_element_type=jnp.float32)
    grad_sgate = (grad_shared_hid * shared_pre_up * silu_slope(shared_pre_gate)).astype(
        jnp.bfloat16
    )
    grad_sup = (grad_shared_hid * jax.nn.silu(shared_pre_gate)).astype(jnp.bfloat16)
    grad_wsgate = jnp.dot(hidden_two.T, grad_sgate, preferred_element_type=jnp.float32)
    grad_wsup = jnp.dot(hidden_two.T, grad_sup, preferred_element_type=jnp.float32)
    grad_two = (
        jnp.dot(grad_sgate, wsgate.T, preferred_element_type=jnp.float32)
        + jnp.dot(grad_sup, wsup.T, preferred_element_type=jnp.float32)
        + grad_routed
    )
    grad_gain_ffn = jnp.sum(grad_two * normed_two, axis=0)
    grad_middle = upstream_f + norm_back(grad_two * gain_ffn, normed_two, second_scale)
    grad_attn = grad_middle.astype(jnp.bfloat16)
    grad_wout = jnp.dot(attended.T, grad_attn, preferred_element_type=jnp.float32)
    grad_heads = (
        jnp.dot(grad_attn, wattn_out.T, preferred_element_type=jnp.float32)
        .astype(jnp.bfloat16)
        .reshape(block_len, KV_HEADS, GROUP, HEAD_DIM)
    )
    grad_heads_f = grad_heads.astype(jnp.float32)
    row_difference = jnp.einsum("tgjd,gjtd->gjt", grad_heads_f, attended_heads)
    length_all = block_len * lax.axis_size("ctx")
    kv_width = key_rows.shape[1]
    back_state = (
        jnp.zeros((KV_HEADS, GROUP, block_len, HEAD_DIM), jnp.float32),
        jnp.zeros((length_all, kv_width), jnp.float32),
        jnp.zeros((length_all, kv_width), jnp.float32),
    )
    attend_pieces = (
        lax.all_gather(key_rows, "ctx", axis=0, tiled=True),
        lax.all_gather(value_rows, "ctx", axis=0, tiled=True),
    )

    def compute(current):
        raw_scores, allowed, part_keys = piece_scores(attend_pieces[0])
        part_values = attend_pieces[1].reshape(-1, KV_HEADS, HEAD_DIM)
        piece_len = part_keys.shape[0]
        weights = jnp.where(allowed, jnp.exp(raw_scores - log_total[..., None]), 0.0)
        grad_weights = jnp.einsum(
            "tgjd,sgd->gjts", grad_heads, part_values, preferred_element_type=jnp.float32
        )
        grad_raw = (weights * (grad_weights - row_difference[..., None])).astype(jnp.bfloat16)
        grad_query_acc = (
            jnp.einsum("gjts,sgd->gjtd", grad_raw, part_keys, preferred_element_type=jnp.float32)
            * head_scale
        )
        part_grad_keys = (
            jnp.einsum("gjts,tgjd->sgd", grad_raw, queries, preferred_element_type=jnp.float32)
            * head_scale
        )
        part_grad_values = jnp.einsum(
            "gjts,tgjd->sgd", weights, grad_heads_f, precision=top_precision
        )
        grad_keys_all = part_grad_keys.reshape(piece_len, kv_width)
        grad_values_all = part_grad_values.reshape(piece_len, kv_width)
        return (grad_query_acc, grad_keys_all, grad_values_all)

    grad_query_acc, grad_keys_all, grad_values_all = lax.cond(
        jnp.int32(0) <= final_row, compute, lambda current: current, back_state
    )
    grad_keys, grad_values = (
        lax.psum_scatter(
            grad_keys_all.astype(jnp.bfloat16), "ctx", scatter_dimension=0, tiled=True
        ).astype(jnp.float32),
        lax.psum_scatter(
            grad_values_all.astype(jnp.bfloat16), "ctx", scatter_dimension=0, tiled=True
        ).astype(jnp.float32),
    )
    grad_query_low = (
        grad_query_acc.transpose(2, 0, 1, 3)
        .reshape(block_len, HEADS * HEAD_DIM)
        .astype(jnp.bfloat16)
    )
    grad_keys_low = grad_keys.astype(jnp.bfloat16)
    grad_values_low = grad_values.astype(jnp.bfloat16)
    grad_wquery = jnp.dot(hidden_one.T, grad_query_low, preferred_element_type=jnp.float32)
    grad_wkeys = jnp.dot(hidden_one.T, grad_keys_low, preferred_element_type=jnp.float32)
    grad_wvalues = jnp.dot(hidden_one.T, grad_values_low, preferred_element_type=jnp.float32)
    grad_one = (
        jnp.dot(grad_query_low, wquery.T, preferred_element_type=jnp.float32)
        + jnp.dot(grad_keys_low, wkeys.T, preferred_element_type=jnp.float32)
        + jnp.dot(grad_values_low, wvalues.T, preferred_element_type=jnp.float32)
    )
    grad_gain_attn = jnp.sum(grad_one * normed_one, axis=0)
    input_grad = (grad_middle + norm_back(grad_one * gain_attn, normed_one, scale_one)).astype(
        jnp.bfloat16
    )[None]
    shares = (
        lax.psum_scatter(
            grad_gain_attn.astype(jnp.bfloat16), "exp", scatter_dimension=0, tiled=True
        ).astype(jnp.float32),
        lax.psum_scatter(
            grad_gain_ffn.astype(jnp.bfloat16), "exp", scatter_dimension=0, tiled=True
        ).astype(jnp.float32),
        lax.psum_scatter(
            grad_wquery.astype(jnp.bfloat16), "exp", scatter_dimension=0, tiled=True
        ).astype(jnp.float32),
        lax.psum_scatter(
            grad_wkeys.astype(jnp.bfloat16), "exp", scatter_dimension=0, tiled=True
        ).astype(jnp.float32),
        lax.psum_scatter(
            grad_wvalues.astype(jnp.bfloat16), "exp", scatter_dimension=0, tiled=True
        ).astype(jnp.float32),
        lax.psum_scatter(
            grad_wout.astype(jnp.bfloat16), "exp", scatter_dimension=0, tiled=True
        ).astype(jnp.float32),
        lax.psum_scatter(
            grad_wsgate.astype(jnp.bfloat16), "exp", scatter_dimension=0, tiled=True
        ).astype(jnp.float32),
        lax.psum_scatter(
            grad_wsup.astype(jnp.bfloat16), "exp", scatter_dimension=0, tiled=True
        ).astype(jnp.float32),
        lax.psum_scatter(
            grad_shared_down_weight.astype(jnp.bfloat16), "exp", scatter_dimension=0, tiled=True
        ).astype(jnp.float32),
    )
    summed = (
        lax.psum(shares[0].astype(jnp.bfloat16), "ctx").astype(jnp.float32),
        lax.psum(shares[1].astype(jnp.bfloat16), "ctx").astype(jnp.float32),
        lax.psum(shares[2].astype(jnp.bfloat16), "ctx").astype(jnp.float32),
        lax.psum(shares[3].astype(jnp.bfloat16), "ctx").astype(jnp.float32),
        lax.psum(shares[4].astype(jnp.bfloat16), "ctx").astype(jnp.float32),
        lax.psum(shares[5].astype(jnp.bfloat16), "ctx").astype(jnp.float32),
        lax.psum(shares[6].astype(jnp.bfloat16), "ctx").astype(jnp.float32),
        lax.psum(shares[7].astype(jnp.bfloat16), "ctx").astype(jnp.float32),
        lax.psum(shares[8].astype(jnp.bfloat16), "ctx").astype(jnp.float32),
        lax.psum(grad_egate.astype(jnp.bfloat16), "ctx").astype(jnp.float32),
        lax.psum(grad_expert_up_weight.astype(jnp.bfloat16), "ctx").astype(jnp.float32),
        lax.psum(grad_edown.astype(jnp.bfloat16), "ctx").astype(jnp.float32),
    )
    owned_grads = summed[:9]
    expert_grads = summed[9:]
    return (
        mixed,
        input_grad,
        owned_grads[0],
        owned_grads[1],
        owned_grads[2],
        owned_grads[3],
        owned_grads[4],
        owned_grads[5],
        owned_grads[6],
        owned_grads[7],
        owned_grads[8],
        expert_grads[0],
        expert_grads[1],
        expert_grads[2],
    )


def solution(mesh):
    placed = (
        P("exp", "ctx", None),
        P("exp", "ctx", None),
        P("exp", "ctx", None),
        P("exp"),
        P("exp"),
        P("exp", None),
        P("exp", None),
        P("exp", None),
        P("exp", None),
        P("exp", None),
        P("exp", None),
        P("exp", None),
        P("exp", None, None),
        P("exp", None, None),
        P("exp", None, None),
        P("exp", "ctx", None),
    )
    return jax.shard_map(
        on_device,
        mesh=mesh,
        in_specs=placed,
        out_specs=(
            P("exp", "ctx", None),
            P("exp", "ctx", None),
            P("exp"),
            P("exp"),
            P("exp", None),
            P("exp", None),
            P("exp", None),
            P("exp", None),
            P("exp", None),
            P("exp", None),
            P("exp", None),
            P("exp", None, None),
            P("exp", None, None),
            P("exp", None, None),
        ),
        check_vma=False,
    )
```

profile of v0, /device:TPU:0, one launch (start us, length us, event | category | flops | bytes accessed | tf_op | source)
XLA Modules:
  0.0 1565.2 jit_solution(8177701253405250503)
XLA Ops:
  13.2 31.9 %all-reduce.7 = (bf16[1536]{0:T(1024)(128)(2,1)S(1)}, bf16[1536]{0:T(1024)(128)(2,1)}) all-reduce(bf16[1536]{0:T(1024)(128)(2,1)S(1)} %dynamic-update-slice, bf16[1536]{0:T(1024)(128)(2,1)S(1)} %dynamic-update-slice.1), channel_id=1, replica_groups=mesh['ctx'=8,'exp'=16] {'exp'}, use_global_device_ids=true, to_apply=%add.2 | all-reduce | flops 3072 | bytes 12288
  49.0 31.5 %all-gather.10.cloned.1.call-done = bf16[1536,512]{1,0:T(8,128)(2,1)} async-done(((bf16[96,512]{1,0:T(8,128)(2,1)}), bf16[1536,512]{1,0:T(8,128)(2,1)}) %all-gather.10.cloned.1.call-update) | async-done | bytes 1572880 | tf_op jit(solution)/shard_map/all_gather | solution.py:51
  110.8 9.9 all-gather.14.cloned.1.call-done
  126.6 44.4 %all-gather.18.cloned.1.call-done = bf16[1024,512]{1,0:T(8,128)(2,1)} async-done(((bf16[128,512]{1,0:T(8,128)(2,1)}), bf16[1024,512]{1,0:T(8,128)(2,1)}) %all-gather.18.cloned.1.call-update) | async-done | bytes 1048592 | tf_op jit(solution)/shard_map/all_gather | solution.py:98
  171.0 48.9 %all-gather.12.cloned.1.call-done = bf16[1024,512]{1,0:T(8,128)(2,1)} async-done(((bf16[128,512]{1,0:T(8,128)(2,1)}), bf16[1024,512]{1,0:T(8,128)(2,1)}) %all-gather.12.cloned.1.call-update) | async-done | bytes 1048592 | tf_op jit(solution)/shard_map/all_gather | solution.py:97
  219.9 21.1 %conditional.2 = (f32[4,3,128]{2,1,0:T(4,128)}, f32[4,3,128]{2,1,0:T(4,128)}, f32[4,3,128]{2,1,0:T(4,128)}, f32[4,3,128,128]{2,3,1,0:T(8,128)}) conditional(s32[]{:T(128)} %convert_element_type.239, () %tuple.26, (s32[128]{0:T(128)}, bf16[1024,512]{1,0:T(8,128)(2,1)}, bf16[128,4,3,128]{0,3,2,1:T(8,128)(2,1)}, bf16[1024,512]{1,0:T(8,128)(2,1)}) %tuple.96), branch_computations={%region_1.0_spmd, %region_2.5_spmd} | conditional | flops 2837576192 | bytes 52609624 | solution.py:113
  232.9 8.1 fusion.1
  243.3 15.2 all-gather.20.cloned.1.call-done
  264.5 11.6 gather_fusion
  283.4 11.7 gather_fusion.2
  303.6 6.4 multiply_convert_fusion
  310.0 55.5 %all-to-all-done = bf16[16,96,1536]{2,1,0:T(8,128)(2,1)} async-done(((bf16[16,96,1536]{2,1,0:T(8,128)(2,1)}), bf16[16,96,1536]{2,1,0:T(8,128)(2,1)}, u32[]{:S(2)}, u32[]{:S(2)}) %all-to-all-start) | async-done | bytes 4718624 | tf_op jit(solution)/shard_map/all_to_all | solution.py:153
  365.5 6.3 all-to-all-start.2
  372.6 7.7 fusion.36
  380.3 6.6 fusion.38
  386.9 54.2 %all-to-all-done.2 = bf16[16,96,1536]{2,1,0:T(8,128)(2,1)} async-done(((bf16[16,96,1536]{2,1,0:T(8,128)(2,1)}), bf16[16,96,1536]{2,1,0:T(8,128)(2,1)}, u32[]{:S(2)}, u32[]{:S(2)}) %all-to-all-start.2) | async-done | bytes 4718624 | tf_op jit(solution)/shard_map/all_to_all | solution.py:183
  441.1 8.3 fusion.48
  452.0 4.8 fusion.40
  459.5 9.9 all-to-all-start.3
  484.9 45.4 %all-to-all-done.3 = bf16[16,96,1536]{2,1,0:T(8,128)(2,1)} async-done(((bf16[16,96,1536]{2,1,0:T(8,128)(2,1)}), bf16[16,96,1536]{2,1,0:T(8,128)(2,1)}, u32[]{:S(2)}, u32[]{:S(2)}) %all-to-all-start.3) | async-done | bytes 4718624 | tf_op jit(solution)/shard_map/all_to_all | solution.py:206
  530.3 9.0 gather_fusion.3
  539.3 4.9 reshape.201
  544.2 5.6 reduce_sum.97
  564.3 28.3 %conditional.3 = (bf16[4,3,128,128]{3,2,1,0:T(8,128)(2,1)}, bf16[1024,512]{0,1:T(8,128)(2,1)}, bf16[1024,512]{0,1:T(8,128)(2,1)}) conditional(s32[]{:T(128)} %convert_element_type.239, () %tuple.28, (s32[128]{0:T(128)S(1)}, bf16[1024,512]{1,0:T(8,128)(2,1)}, bf16[128,4,3,128]{0,3,2,1:T(8,128)(2,1)}, f32[4,3,128]{2,1,0:T(4,128)}, ...), branch_computations={%region_14.15_spmd, %region_15.16_spmd.clone} | conditional | flops 4045799424 | bytes 68463288 | solution.py:272
  566.4 5.0 fusion.28
  576.7 5.6 fusion.15
  586.5 6.1 fusion.19
  609.0 65.5 %reduce-scatter.28.cloned.1.call-done = bf16[128,512]{1,0:T(8,128)(2,1)} async-done(((bf16[1024,512]{1,0:T(8,128)(2,1)}), bf16[128,512]{1,0:T(8,128)(2,1)}) %reduce-scatter.28.cloned.1.call-update) | async-done | bytes 131088
  677.3 72.9 %reduce-scatter.30.cloned.1.call-done = bf16[128,512]{1,0:T(8,128)(2,1)} async-done(((bf16[1024,512]{1,0:T(8,128)(2,1)}), bf16[128,512]{1,0:T(8,128)(2,1)}) %reduce-scatter.30.cloned.1.call-update) | async-done | bytes 131088
  759.7 4.9 convolution_convert_fusion
  764.7 7.3 bitcast_convert_fusion
  772.0 7.6 bitcast_convert_fusion.1
  779.6 7.5 bitcast_convert_fusion.2
  787.1 30.5 %reduce-scatter.22.cloned.1.call-done = bf16[96,1024]{1,0:T(8,128)(2,1)} async-done(((bf16[1536,1024]{1,0:T(8,128)(2,1)}), bf16[96,1024]{1,0:T(8,128)(2,1)}) %reduce-scatter.22.cloned.1.call-update) | async-done | bytes 196624 | tf_op jit(solution)/shard_map/reduce_scatter | solution.py:321
  817.6 66.7 %reduce-scatter.24.cloned.1.call-done = bf16[96,1024]{1,0:T(8,128)(2,1)} async-done(((bf16[1536,1024]{1,0:T(8,128)(2,1)}), bf16[96,1024]{1,0:T(8,128)(2,1)}) %reduce-scatter.24.cloned.1.call-update) | async-done | bytes 196624 | tf_op jit(solution)/shard_map/reduce_scatter | solution.py:324
  884.3 66.3 %reduce-scatter.26.cloned.1.call-done = bf16[64,1536]{1,0:T(8,128)(2,1)} async-done(((bf16[1024,1536]{1,0:T(8,128)(2,1)}), bf16[64,1536]{1,0:T(8,128)(2,1)}) %reduce-scatter.26.cloned.1.call-update) | async-done | bytes 196624 | tf_op jit(solution)/shard_map/reduce_scatter | solution.py:327
  950.6 63.4 %reduce-scatter.16.cloned.1.call-done = bf16[96,512]{1,0:T(8,128)(2,1)} async-done(((bf16[1536,512]{1,0:T(8,128)(2,1)}), bf16[96,512]{1,0:T(8,128)(2,1)}) %reduce-scatter.16.cloned.1.call-update) | async-done | bytes 98320 | tf_op jit(solution)/shard_map/reduce_scatter | solution.py:312
  1014.1 63.5 %reduce-scatter.18.cloned.1.call-done = bf16[96,512]{1,0:T(8,128)(2,1)} async-done(((bf16[1536,512]{1,0:T(8,128)(2,1)}), bf16[96,512]{1,0:T(8,128)(2,1)}) %reduce-scatter.18.cloned.1.call-update) | async-done | bytes 98320 | tf_op jit(solution)/shard_map/reduce_scatter | solution.py:315
  1077.6 69.7 %reduce-scatter.14.cloned.1.call-done = bf16[96,1536]{1,0:T(8,128)(2,1)} async-done(((bf16[1536,1536]{1,0:T(8,128)(2,1)}), bf16[96,1536]{1,0:T(8,128)(2,1)}) %reduce-scatter.14.cloned.1.call-update) | async-done | bytes 294928 | tf_op jit(solution)/shard_map/reduce_scatter | solution.py:309
  1147.4 70.2 %reduce-scatter.20.cloned.1.call-done = bf16[96,1536]{1,0:T(8,128)(2,1)} async-done(((bf16[1536,1536]{1,0:T(8,128)(2,1)}), bf16[96,1536]{1,0:T(8,128)(2,1)}) %reduce-scatter.20.cloned.1.call-update) | async-done | bytes 294928 | tf_op jit(solution)/shard_map/reduce_scatter | solution.py:318
  1224.3 4.9 all-to-all-start.1
  1229.8 154.3 %all-to-all-done.1 = bf16[16,96,1536]{2,1,0:T(8,128)(2,1)} async-done(((bf16[16,96,1536]{2,1,0:T(8,128)(2,1)}), bf16[16,96,1536]{2,1,0:T(8,128)(2,1)}, u32[]{:S(2)}, u32[]{:S(2)}) %all-to-all-start.1) | async-done | bytes 4718624 | tf_op jit(solution)/shard_map/all_to_all | solution.py:164
  1384.1 9.2 gather_fusion.1
  1393.3 4.9 reshape.200
  1398.2 5.4 multiply_reduce_fusion.1
  1412.1 97.6 %all-reduce.6 = (bf16[1536]{0:T(1024)(128)(2,1)}, bf16[1536]{0:T(1024)(128)(2,1)}) all-reduce(bf16[1536]{0:T(1024)(128)(2,1)} %get-tuple-element.113, bf16[1536]{0:T(1024)(128)(2,1)S(1)} %copy-done.41), channel_id=4, replica_groups=mesh['ctx'=8,'exp'=16] {'exp'}, use_global_device_ids=true, to_apply=%region_20.21.clone | all-reduce | flops 3072 | bytes 12288
  1511.8 23.0 %all-reduce.8 = (bf16[96]{0:T(256)(128)(2,1)}, bf16[96]{0:T(256)(128)(2,1)}) all-reduce(bf16[96]{0:T(256)(128)(2,1)} %dynamic-slice.3, bf16[96]{0:T(256)(128)(2,1)S(1)} %dynamic-slice.5), channel_id=1, replica_groups=mesh['ctx'=8,'exp'=16] {'ctx'}, use_global_device_ids=true, to_apply=%region_21.22 | all-reduce | flops 192 | bytes 768 | tf_op jit(solution)/shard_map/psum | solution.py:332
  1540.2 5.6 convert_element_type.299
  (239 shorter events, 193.7 us)
Async XLA Ops:
  7.2 433.9 %copy-start = (bf16[2,512,1536]{2,1,0:T(8,128)(2,1)S(1)}, bf16[2,512,1536]{2,1,0:T(8,128)(2,1)}, u32[]{:S(2)}) copy-start(bf16[2,512,1536]{2,1,0:T(8,128)(2,1)} %param.34) | copy-start | bytes 9437188
  7.2 73.3 %copy-start.1 = (bf16[1,128,1536]{2,1,0:T(8,128)(2,1)S(1)}, bf16[1,128,1536]{2,1,0:T(8,128)(2,1)}, u32[]{:S(2)}) copy-start(bf16[1,128,1536]{2,1,0:T(8,128)(2,1)} %param.20) | copy-start | bytes 1179652
  7.2 77.1 %copy-start.42 = (s32[1,128,6]{1,0,2:T(1,128)S(1)}, s32[1,128,6]{1,0,2:T(1,128)}, u32[]{:S(2)}) copy-start(s32[1,128,6]{1,0,2:T(1,128)} %param.21) | copy-start | bytes 9220
  7.2 39.1 %all-gather.16.cloned.1.call-start = ((), (), s32[]{:S(2)}) async-start(), calls=%async_computation.16 | async-start | bytes 1671168 | tf_op jit(solution)/shard_map/all_gather | solution.py:52
  8.0 72.5 %all-gather.10.cloned.1.call-start = ((), (), s32[]{:S(2)}) async-start(), calls=%async_computation.13 | async-start | bytes 1671168 | tf_op jit(solution)/shard_map/all_gather | solution.py:51
  8.7 112.1 %all-gather.14.cloned.1.call-start = ((), (), s32[]{:S(2)}) async-start(), calls=%async_computation.15 | async-start | bytes 5013504 | tf_op jit(solution)/shard_map/all_gather | solution.py:50
  9.4 161.6 %all-gather.18.cloned.1.call-start = ((), (), s32[]{:S(2)}) async-start(), calls=%async_computation.17 | async-start | bytes 1179648 | tf_op jit(solution)/shard_map/all_gather | solution.py:98
  46.3 41.9 %copy-start.39 = (f32[128]{0:T(128)}, f32[128]{0:T(128)S(1)}, u32[]{:S(2)}) copy-start(f32[128]{0:T(128)S(1)} %add_rsqrt_fusion.1) | copy-start | bytes 1540
  49.0 170.9 %all-gather.12.cloned.1.call-start = ((), (), s32[]{:S(2)}) async-start(), calls=%async_computation.14 | async-start | bytes 1179648 | tf_op jit(solution)/shard_map/all_gather | solution.py:97
  83.0 175.6 %all-gather.20.cloned.1.call-start = ((), (), s32[]{:S(2)}) async-start(), calls=%async_computation.18 | async-start | bytes 5013504 | tf_op jit(solution)/shard_map/all_gather | solution.py:53
  83.6 387.3 %all-gather.22.cloned.1.call-start = ((), (), s32[]{:S(2)}) async-start(), calls=%async_computation.19 | async-start | bytes 3342336 | tf_op jit(solution)/shard_map/all_gather | solution.py:54
  276.1 89.5 %all-to-all-start = ((bf16[16,96,1536]{2,1,0:T(8,128)(2,1)}), bf16[16,96,1536]{2,1,0:T(8,128)(2,1)}, u32[]{:S(2)}, u32[]{:S(2)}) async-start(bf16[16,96,1536]{2,1,0:T(8,128)(2,1)} %bitcast.271), calls=%async_computation | async-start | bytes 9437184 | tf_op jit(solution)/shard_map/all_to_all | solution.py:153
  280.6 193.7 %all-gather.24.cloned.1.call-start = ((), (), s32[]{:S(2)}) async-start(), calls=%async_computation.20 | async-start | bytes 3342336 | tf_op jit(solution)/shard_map/all_gather | solution.py:55
  365.5 75.5 %all-to-all-start.2 = ((bf16[16,96,1536]{2,1,0:T(8,128)(2,1)}), bf16[16,96,1536]{2,1,0:T(8,128)(2,1)}, u32[]{:S(2)}, u32[]{:S(2)}) async-start(bf16[16,96,1536]{2,1,0:T(8,128)(2,1)} %multiply_convert_fusion), calls=%async_computation.2 | async-start | bytes 9437184 | tf_op jit(solution)/shard_map/all_to_all | solution.py:183
  371.8 105.9 %all-gather.26.cloned.1.call-start = ((), (), s32[]{:S(2)}) async-start(), calls=%async_computation.21 | async-start | bytes 3342336 | tf_op jit(solution)/shard_map/all_gather | solution.py:56
  372.6 7.7 copy-start.12
  441.1 8.3 copy-start.13
  459.5 70.9 %all-to-all-start.3 = ((bf16[16,96,1536]{2,1,0:T(8,128)(2,1)}), bf16[16,96,1536]{2,1,0:T(8,128)(2,1)}, u32[]{:S(2)}, u32[]{:S(2)}) async-start(bf16[16,96,1536]{2,1,0:T(8,128)(2,1)} %bitcast.269), calls=%async_computation.3 | async-start | bytes 9437184 | tf_op jit(solution)/shard_map/all_to_all | solution.py:206
  469.4 205.1 %reduce-scatter.28.cloned.1.call-start = ((), (), s32[]{:S(2)}) async-start(), calls=%async_computation.29 | async-start | bytes 1179648
  477.7 5.1 copy-start.6
  549.8 4.7 copy-start.44
  555.6 8.6 copy-start.45
  576.6 5.6 copy-start.24
  576.6 7.7 copy-start.9
  594.8 155.4 %reduce-scatter.30.cloned.1.call-start = ((), (), s32[]{:S(2)}) async-start(), calls=%async_computation.30 | async-start | bytes 1179648
  597.2 220.4 %reduce-scatter.22.cloned.1.call-start = ((), (), s32[]{:S(2)}) async-start(), calls=%async_computation.26 | async-start | bytes 3342336 | tf_op jit(solution)/shard_map/reduce_scatter | solution.py:321
  601.0 283.3 %reduce-scatter.24.cloned.1.call-start = ((), (), s32[]{:S(2)}) async-start(), calls=%async_computation.27 | async-start | bytes 3342336 | tf_op jit(solution)/shard_map/reduce_scatter | solution.py:324
  604.7 345.9 %reduce-scatter.26.cloned.1.call-start = ((), (), s32[]{:S(2)}) async-start(), calls=%async_computation.28 | async-start | bytes 3342336 | tf_op jit(solution)/shard_map/reduce_scatter | solution.py:327
  605.2 69.3 %copy-start.40 = (f32[128]{0:T(128)S(1)}, f32[128]{0:T(128)}, u32[]{:S(2)}) copy-start(f32[128]{0:T(128)} %copy-done.39) | copy-start | bytes 1540
  608.9 405.1 %reduce-scatter.16.cloned.1.call-start = ((), (), s32[]{:S(2)}) async-start(), calls=%async_computation.23 | async-start | bytes 1671168 | tf_op jit(solution)/shard_map/reduce_scatter | solution.py:312
  677.3 400.3 %reduce-scatter.18.cloned.1.call-start = ((), (), s32[]{:S(2)}) async-start(), calls=%async_computation.24 | async-start | bytes 1671168 | tf_op jit(solution)/shard_map/reduce_scatter | solution.py:315
  752.9 394.4 %reduce-scatter.14.cloned.1.call-start = ((), (), s32[]{:S(2)}) async-start(), calls=%async_computation.22 | async-start | bytes 5013504 | tf_op jit(solution)/shard_map/reduce_scatter | solution.py:309
  759.6 457.9 %reduce-scatter.20.cloned.1.call-start = ((), (), s32[]{:S(2)}) async-start(), calls=%async_computation.25 | async-start | bytes 5013504 | tf_op jit(solution)/shard_map/reduce_scatter | solution.py:318
  764.6 775.6 %all-reduce.12.cloned.1.call-start = ((), (), s32[]{:S(2)}) async-start(), calls=%async_computation.31 | async-start | bytes 21626880 | tf_op jit(solution)/shard_map/psum | solution.py:334
  764.6 7.3 copy-start.21
  772.0 7.6 copy-start.19
  1224.3 159.8 %copy-start.38 = (s32[1024]{0:T(1024)S(1)}, s32[1024]{0:T(1024)}, u32[]{:S(2)}) copy-start(s32[1024]{0:T(1024)} %pad_clamp_fusion.1) | copy-start | bytes 12292
  1224.3 159.8 %all-to-all-start.1 = ((bf16[16,96,1536]{2,1,0:T(8,128)(2,1)}), bf16[16,96,1536]{2,1,0:T(8,128)(2,1)}, u32[]{:S(2)}, u32[]{:S(2)}) async-start(bf16[16,96,1536]{2,1,0:T(8,128)(2,1)} %bitcast.270), calls=%async_computation.1 | async-start | bytes 9437184 | tf_op jit(solution)/shard_map/all_to_all | solution.py:164
  1398.2 5.4 copy-start.4
  1398.2 5.4 copy-start.14
  1398.2 5.4 copy-start.26
  1405.0 4.9 copy-start.17
  1405.0 4.9 copy-start.28
  1540.2 5.6 copy-start.16
  1549.4 5.4 copy-start.34
  1549.4 6.1 copy-start.33
  1549.5 6.9 copy-start.32
  1553.0 4.8 copy-start.36
  (23 other events, 64.6 us)
Sparse Core Ops, SparseCore 0:
  9.8 35.6 all-gather.15
  47.1 33.3 all-gather.9
  82.2 38.5 all-gather.13
  123.5 47.4 all-gather.17
  173.8 46.0 all-gather.11
  221.5 37.0 all-gather.19
  260.3 65.1 all-gather.21
  327.2 46.7 all-gather.23
  375.7 78.8 all-gather.25
  594.9 79.4 reduce-scatter.27
  679.1 70.9 reduce-scatter.29
  753.0 64.5 reduce-scatter.21
  820.0 64.2 reduce-scatter.23
  886.6 64.0 reduce-scatter.25
  952.9 61.1 reduce-scatter.15
  1016.4 61.1 reduce-scatter.17
  1080.4 66.8 reduce-scatter.13
  1150.2 67.2 reduce-scatter.19
  1220.9 272.1 all-reduce.11
where the time goes:
time: 1570 us
  waiting for transfers between devices  1030 us (66%)
  matrix products  158 us (10%)
  blocking collectives  153 us (10%)
  local copies, waits for them, and re-layouts  108 us (7%)
  other arithmetic  70.5 us (4%)
  starting transfers between devices  27.6 us (2%)
  between operations  15.9 us (1%)
    all_to_all x1, waiting for transfers between devices, on_device(): lax.all_to_all(expert_out.reshape(groups_exp, local_experts * capacity, m...  154 us
    unnamed x21, waiting for transfers between devices  143 us
    unnamed x2, blocking collectives  130 us
    reduce_scatter x1, waiting for transfers between devices, on_device(): lax.psum_scatter(grad_wout.astype(jnp.bfloat16), 'exp', scatter_dimension...  70.2 us
    reduce_scatter x1, waiting for transfers between devices, on_device(): lax.psum_scatter(grad_wquery.astype(jnp.bfloat16), 'exp', scatter_dimensi...  69.7 us
    reduce_scatter x1, waiting for transfers between devices, on_device(): lax.psum_scatter(grad_wsup.astype(jnp.bfloat16), 'exp', scatter_dimension...  66.7 us
    reduce_scatter x1, waiting for transfers between devices, on_device(): lax.psum_scatter(grad_shared_down_weight.astype(jnp.bfloat16), 'exp', sca...  66.3 us
    reduce_scatter x1, waiting for transfers between devices, on_device(): lax.psum_scatter(grad_wvalues.astype(jnp.bfloat16), 'exp', scatter_dimens...  63.5 us
  transfers between devices with their start and end apart: 23, of which 18 were waited for; matrix products, arithmetic and copies ran while one was open for 16% of the time, Pallas kernels for 0%

commit v1 on v0

v1 whole, which is shorter than its diff:
```python
import jax
import jax.numpy as jnp
from jax import lax
from jax.sharding import PartitionSpec as P

HEADS = 12
KV_HEADS = 4
HEAD_DIM = 128
TOPK = 6
GROUP = 3
BLOCK = 128
WIDTH = 1536
KV_WIDTH = KV_HEADS * HEAD_DIM
CAP = 48
N_EXP = 16
N_CTX = 8
LOCAL_E = 2
FF_E = 512
SHARED = 64
META = 128

epsilon = 1e-05
masked_score = -1e30
f32 = jnp.float32
bf16 = jnp.bfloat16

same_core = [[2 * i + c for i in range(8)] for c in range(2)]
core_swap = [(i, i ^ 1) for i in range(N_EXP)]
y_groups = [[0, 1, 2, 3], [4, 5, 6, 7]]
z_swap = [(i, i ^ 4) for i in range(N_CTX)]


def silu_slope(operand):
    sigmoid_v = jax.nn.sigmoid(operand)
    return sigmoid_v * (1.0 + operand * (1.0 - sigmoid_v))


def norm_back(grad_normed, normed, inv_root):
    return inv_root * (
        grad_normed - normed * jnp.mean(grad_normed * normed, axis=-1, keepdims=True)
    )


def mm(a, b, dims=None):
    if dims is None:
        return jnp.dot(a, b, preferred_element_type=f32)
    return lax.dot_general(a, b, (dims, ((), ())), preferred_element_type=f32)


def swap_all(rows, axis, groups=None):
    return lax.all_to_all(
        rows, axis, split_axis=0, concat_axis=0, tiled=True, axis_index_groups=groups
    )


def pick(parts, at):
    return lax.dynamic_index_in_dim(parts, at, 0, keepdims=False)


def add_low(a, b):
    return (a.astype(f32) + b.astype(f32)).astype(bf16)


def reduce_exp(parts, core):
    by_core = parts.reshape(8, 2, BLOCK, WIDTH)
    keep = lax.dynamic_index_in_dim(by_core, core, 1, keepdims=False)
    send = lax.dynamic_index_in_dim(by_core, 1 - core, 1, keepdims=False)
    got = lax.ppermute(send, "exp", core_swap)
    pieces = swap_all(add_low(keep, got), "exp", same_core)
    return jnp.sum(pieces.astype(f32), axis=0)


def sum_ctx_y(grad, z_at):
    rows, cols = grad.shape
    piece = rows // N_CTX
    pieces = swap_all(grad.reshape(4, 2, piece, cols), "ctx", y_groups)
    summed = jnp.sum(pieces.astype(f32), axis=0).astype(bf16)
    got = lax.ppermute(pick(summed, 1 - z_at), "ctx", z_swap)
    own = add_low(pick(summed, z_at), got)
    other = lax.ppermute(own, "ctx", z_swap)
    pair = jnp.where(z_at == 0, jnp.stack([own, other]), jnp.stack([other, own]))
    return swap_all(jnp.broadcast_to(pair, (4, 2, piece, cols)), "ctx", y_groups).reshape(rows, cols)


def sum_ctx_z(grad, z_at):
    rows, cols = grad.shape
    piece = rows // N_CTX
    halves = grad.reshape(2, 4, piece, cols)
    got = lax.ppermute(pick(halves, 1 - z_at), "ctx", z_swap)
    pieces = swap_all(add_low(pick(halves, z_at), got), "ctx", y_groups)
    own = jnp.sum(pieces.astype(f32), axis=0).astype(bf16)
    side = swap_all(jnp.broadcast_to(own, (4, piece, cols)), "ctx", y_groups)
    other = lax.ppermute(side, "ctx", z_swap)
    pair = jnp.where(z_at == 0, jnp.stack([side, other]), jnp.stack([other, side]))
    return pair.reshape(rows, cols)


def sum_ctx_small(grad):
    rows, cols = grad.shape
    pieces = swap_all(grad.reshape(N_CTX, rows // N_CTX, cols), "ctx")
    own = jnp.sum(pieces.astype(f32), axis=0).astype(bf16)
    return swap_all(jnp.broadcast_to(own, (N_CTX,) + own.shape), "ctx").reshape(rows, cols)


def on_device(
    tokens,
    routes,
    route_gates,
    norm_attn,
    norm_ffn,
    query_weight,
    key_weight,
    value_weight,
    out_weight,
    shared_gate,
    shared_up,
    shared_down,
    expert_gate,
    expert_up,
    expert_down,
    cotangent,
):
    exp_at = lax.axis_index("exp")
    ctx_at = lax.axis_index("ctx")
    core = exp_at % 2
    z_at = ctx_at // 4
    head_scale = HEAD_DIM ** (-0.5)

    w_attn = lax.all_gather(
        jnp.concatenate([query_weight, key_weight, value_weight], axis=1), "exp", axis=0, tiled=True
    )
    w_out = lax.all_gather(out_weight, "exp", axis=0, tiled=True)
    gains = jnp.concatenate([norm_attn, norm_ffn])
    gains = swap_all(jnp.broadcast_to(gains, (N_EXP, gains.shape[0])), "exp")
    gain_attn = gains[:, :96].reshape(WIDTH).astype(f32)
    gain_ffn = gains[:, 96:].reshape(WIDTH).astype(f32)
    shared_cols = jnp.concatenate(
        [shared_gate.reshape(96, N_EXP, SHARED), shared_up.reshape(96, N_EXP, SHARED)], axis=2
    ).transpose(1, 0, 2)
    w_shared = swap_all(shared_cols, "exp").reshape(WIDTH, 2 * SHARED)
    gates_high = route_gates[0].astype(bf16)
    gates_low = (route_gates[0] - gates_high.astype(f32)).astype(bf16)
    meta = jnp.concatenate(
        [
            routes[0].astype(bf16),
            gates_high,
            gates_low,
            jnp.zeros((BLOCK, META - 3 * TOPK), bf16),
        ],
        axis=1,
    )
    up_meta = lax.all_gather(
        jnp.concatenate([cotangent[0], meta], axis=1), "exp", axis=0, tiled=True
    )

    inputs = tokens[0].astype(f32)
    scale_one = lax.rsqrt(jnp.mean(inputs * inputs, axis=-1, keepdims=True) + epsilon)
    normed_one = inputs * scale_one
    hidden_one = (normed_one * gain_attn).astype(bf16)
    qkv = mm(hidden_one, w_attn).astype(bf16)
    queries = qkv[:, :WIDTH].reshape(BLOCK, KV_HEADS, GROUP, HEAD_DIM)
    own_kv = qkv[:, WIDTH:]

    y_at = ctx_at % 4
    block_of, kv_pieces = [], []
    from_z = lax.ppermute(own_kv, "ctx", [(i, i + 4) for i in range(4)])
    for step in range(4):
        if step == 0:
            kv_pieces.append(own_kv)
        else:
            kv_pieces.append(
                lax.ppermute(
                    own_kv,
                    "ctx",
                    [(4 * z + y, 4 * z + (y + step) % 4) for z in range(2) for y in range(4)],
                )
            )
        block_of.append(4 * z_at + (y_at - step) % 4)
    for step in range(4):
        if step == 0:
            kv_pieces.append(from_z)
        else:
            kv_pieces.append(
                lax.ppermute(from_z, "ctx", [(4 + y, 4 + (y + step) % 4) for y in range(4)])
            )
        block_of.append(jnp.where(z_at == 0, N_CTX, (y_at - step) % 4))
    kv_all = jnp.concatenate(kv_pieces, axis=0)
    keys = kv_all[:, :KV_WIDTH].reshape(-1, KV_HEADS, HEAD_DIM)
    values = kv_all[:, KV_WIDTH:].reshape(-1, KV_HEADS, HEAD_DIM)
    row_in = jnp.arange(BLOCK, dtype=jnp.int32)
    key_at = (jnp.stack(block_of)[:, None] * BLOCK + row_in[None, :]).reshape(-1)
    allowed = (ctx_at * BLOCK + row_in)[:, None] >= key_at[None, :]

    raw_scores = jnp.where(
        allowed,
        jnp.einsum("tgjd,sgd->gjts", queries, keys, preferred_element_type=f32) * head_scale,
        masked_score,
    )
    row_max = jnp.max(raw_scores, axis=-1)
    weights = jnp.exp(raw_scores - row_max[..., None])
    row_sum = jnp.sum(weights, axis=-1)
    running_out = jnp.einsum(
        "gjts,sgd->gjtd", weights.astype(bf16), values, preferred_element_type=f32
    )
    log_total = row_max + jnp.log(row_sum)
    attended_heads = running_out / row_sum[..., None]
    attended = attended_heads.transpose(2, 0, 1, 3).reshape(BLOCK, WIDTH).astype(bf16)
    middle = inputs + mm(attended, w_out)
    second_scale = lax.rsqrt(jnp.mean(middle * middle, axis=-1, keepdims=True) + epsilon)
    normed_two = middle * second_scale
    hidden_two = (normed_two * gain_ffn).astype(bf16)

    hidden_all = lax.all_gather(hidden_two, "exp", axis=0, tiled=True)
    routes_all = up_meta[:, WIDTH : WIDTH + TOPK].astype(f32)
    gates_all = up_meta[:, WIDTH + TOPK : WIDTH + 2 * TOPK].astype(f32) + up_meta[
        :, WIDTH + 2 * TOPK : WIDTH + 3 * TOPK
    ].astype(f32)
    local_id = (exp_at * LOCAL_E + jnp.arange(LOCAL_E, dtype=jnp.int32)).astype(f32)
    hit = (routes_all[None] == local_id[:, None, None]).astype(f32)
    mask = jnp.sum(hit, axis=-1).reshape(LOCAL_E, N_EXP, BLOCK)
    gate_of = jnp.sum(hit * gates_all[None], axis=-1).reshape(LOCAL_E, N_EXP, BLOCK)
    before = (row_in[:, None] > row_in[None, :]).astype(bf16)
    rank = jnp.einsum("ut,ebt->ebu", before, mask.astype(bf16), preferred_element_type=f32)
    slots = jnp.arange(CAP, dtype=jnp.int32).astype(f32)
    place_f = jnp.where(
        (mask[..., None] > 0.5) & (rank[..., None] == slots), jnp.float32(1.0), jnp.float32(0.0)
    )
    place = place_f.astype(bf16)
    slot_gate = jnp.sum(place_f * gate_of[..., None], axis=2)
    upstream_all = up_meta[:, :WIDTH].reshape(N_EXP, BLOCK, WIDTH)
    rows_e = N_EXP * CAP
    grad_eo = (
        slot_gate[..., None]
        * jnp.einsum("ebts,btd->ebsd", place, upstream_all, preferred_element_type=f32)
    ).astype(bf16).reshape(LOCAL_E, rows_e, WIDTH)
    grad_eh = jnp.einsum("erd,efd->erf", grad_eo, expert_down, preferred_element_type=f32)
    upstream_rows = upstream_all.reshape(N_EXP * BLOCK, WIDTH)
    grad_sh = mm(upstream_rows, shared_down, ((1,), (1,)))

    hidden_blocks = hidden_all.reshape(N_EXP, BLOCK, WIDTH)
    arrived = (
        jnp.einsum("ebts,btd->ebsd", place, hidden_blocks, preferred_element_type=f32)
        .astype(bf16)
        .reshape(LOCAL_E, rows_e, WIDTH)
    )
    pre_gate = jnp.einsum("erd,edf->erf", arrived, expert_gate, preferred_element_type=f32)
    pre_up = jnp.einsum("erd,edf->erf", arrived, expert_up, preferred_element_type=f32)
    expert_hidden = (jax.nn.silu(pre_gate) * pre_up).astype(bf16)
    grad_pre_gate = (grad_eh * pre_up * silu_slope(pre_gate)).astype(bf16)
    grad_pre_up = (grad_eh * jax.nn.silu(pre_gate)).astype(bf16)
    pair_in = (
        jnp.einsum("erf,edf->erd", grad_pre_gate, expert_gate, preferred_element_type=f32)
        + jnp.einsum("erf,edf->erd", grad_pre_up, expert_up, preferred_element_type=f32)
    ).astype(bf16)
    shared_pre = mm(hidden_all, w_shared)
    shared_pre_gate, shared_pre_up = shared_pre[:, :SHARED], shared_pre[:, SHARED:]
    shared_hidden = (jax.nn.silu(shared_pre_gate) * shared_pre_up).astype(bf16)
    grad_shared_pre = jnp.concatenate(
        [
            (grad_sh * shared_pre_up * silu_slope(shared_pre_gate)).astype(bf16),
            (grad_sh * jax.nn.silu(shared_pre_gate)).astype(bf16),
        ],
        axis=1,
    )
    grad_two_part = (
        jnp.einsum(
            "ebts,ebsd->btd",
            place,
            pair_in.reshape(LOCAL_E, N_EXP, CAP, WIDTH),
            preferred_element_type=f32,
        )
        + mm(grad_shared_pre, w_shared, ((1,), (1,))).reshape(N_EXP, BLOCK, WIDTH)
    ).astype(bf16)
    grad_two = reduce_exp(grad_two_part, core)

    grad_edown = jnp.einsum("erf,erd->efd", expert_hidden, grad_eo, preferred_element_type=f32)
    grad_egate = jnp.einsum("erd,erf->edf", arrived, grad_pre_gate, preferred_element_type=f32)
    grad_eup = jnp.einsum("erd,erf->edf", arrived, grad_pre_up, preferred_element_type=f32)
    sum_edown = sum_ctx_y(grad_edown.astype(bf16).reshape(LOCAL_E * FF_E, WIDTH), z_at)
    sum_egate = sum_ctx_y(grad_egate.astype(bf16).reshape(LOCAL_E * WIDTH, FF_E), z_at)
    sum_eup = sum_ctx_z(grad_eup.astype(bf16).reshape(LOCAL_E * WIDTH, FF_E), z_at)

    expert_out = jnp.einsum("erf,efd->erd", expert_hidden, expert_down, preferred_element_type=f32)
    gated_out = (
        expert_out.astype(bf16).astype(f32) * slot_gate.reshape(LOCAL_E, rows_e, 1)
    ).astype(bf16)
    out_part = (
        jnp.einsum(
            "ebts,ebsd->btd",
            place,
            gated_out.reshape(LOCAL_E, N_EXP, CAP, WIDTH),
            preferred_element_type=f32,
        )
        + mm(shared_hidden, shared_down).reshape(N_EXP, BLOCK, WIDTH)
    ).astype(bf16)
    mixed = (middle + reduce_exp(out_part, core)).astype(bf16)[None]

    grad_sdown = mm(shared_hidden, upstream_rows, ((0,), (0,)))
    grad_scols = mm(hidden_all, grad_shared_pre, ((0,), (0,))).astype(bf16)
    grad_scols = swap_all(grad_scols.reshape(N_EXP, 96, 2 * SHARED), "exp").transpose(1, 0, 2)

    upstream_f = cotangent[0].astype(f32)
    grad_gain_ffn = jnp.sum(grad_two * normed_two, axis=0)
    grad_middle = upstream_f + norm_back(grad_two * gain_ffn, normed_two, second_scale)
    grad_attn = grad_middle.astype(bf16)
    grad_heads = mm(grad_attn, w_out, ((1,), (1,))).astype(bf16)
    grad_heads = grad_heads.reshape(BLOCK, KV_HEADS, GROUP, HEAD_DIM)
    grad_heads_f = grad_heads.astype(f32)
    row_difference = jnp.einsum("tgjd,gjtd->gjt", grad_heads_f, attended_heads)
    weights_b = jnp.exp(raw_scores - log_total[..., None])
    grad_weights = jnp.einsum("tgjd,sgd->gjts", grad_heads, values, preferred_element_type=f32)
    grad_raw = (weights_b * (grad_weights - row_difference[..., None])).astype(bf16)
    grad_query = (
        jnp.einsum("gjts,sgd->tgjd", grad_raw, keys, preferred_element_type=f32) * head_scale
    ).reshape(BLOCK, WIDTH).astype(bf16)
    part_keys = (
        jnp.einsum("gjts,tgjd->sgd", grad_raw, queries, preferred_element_type=f32) * head_scale
    ).reshape(-1, KV_WIDTH)
    part_values = jnp.einsum(
        "gjts,tgjd->sgd", weights_b.astype(bf16), grad_heads, preferred_element_type=f32
    ).reshape(-1, KV_WIDTH)
    part_kv = jnp.concatenate([part_keys, part_values], axis=1).astype(bf16)
    part_kv = part_kv.reshape(2, 4, BLOCK, 2 * KV_WIDTH)

    grad_kv = part_kv[0, 0].astype(f32)
    grad_z = part_kv[1, 0].astype(f32)
    for step in range(1, 4):
        grad_kv = grad_kv + lax.ppermute(
            part_kv[0, step],
            "ctx",
            [(4 * z + (y + step) % 4, 4 * z + y) for z in range(2) for y in range(4)],
        ).astype(f32)
        grad_z = grad_z + lax.ppermute(
            part_kv[1, step], "ctx", [(4 + (y + step) % 4, 4 + y) for y in range(4)]
        ).astype(f32)
    grad_kv = grad_kv + lax.ppermute(
        grad_z.astype(bf16), "ctx", [(i + 4, i) for i in range(4)]
    ).astype(f32)
    grad_kv = grad_kv.astype(bf16)

    grad_qkv = jnp.concatenate([grad_query, grad_kv], axis=1)
    grad_one = mm(grad_qkv, w_attn, ((1,), (1,)))
    grad_gain_attn = jnp.sum(grad_one * normed_one, axis=0)
    input_grad = (
        grad_middle + norm_back(grad_one * gain_attn, normed_one, scale_one)
    ).astype(bf16)[None]

    hidden_one_all = lax.all_gather(hidden_one, "exp", axis=0, tiled=True)
    grad_attn_all = lax.all_gather(grad_attn, "exp", axis=0, tiled=True)
    attended_cols = swap_all(
        attended.reshape(BLOCK, N_EXP, 96).transpose(1, 0, 2), "exp"
    ).reshape(N_EXP * BLOCK, 96)
    grad_wout = mm(attended_cols, grad_attn_all, ((0,), (0,)))

    cols = jnp.concatenate(
        [
            grad_query.reshape(BLOCK, N_EXP, 96),
            grad_kv[:, :KV_WIDTH].reshape(BLOCK, N_EXP, 32),
            grad_kv[:, KV_WIDTH:].reshape(BLOCK, N_EXP, 32),
        ],
        axis=2,
    ).transpose(1, 0, 2)
    cols = swap_all(cols, "exp").reshape(N_EXP * BLOCK, 160)
    grad_cols = mm(hidden_one_all, cols, ((0,), (0,))).astype(bf16).reshape(N_EXP, 96, 160)
    gain_parts = jnp.stack(
        [grad_gain_attn.reshape(N_EXP, 96), grad_gain_ffn.reshape(N_EXP, 96)], axis=-1
    ).astype(bf16)
    back = swap_all(
        jnp.concatenate([grad_cols, gain_parts, jnp.zeros((N_EXP, 96, 30), bf16)], axis=2), "exp"
    )
    gain_sum = jnp.sum(back[:, :, 160:162].astype(f32), axis=0).astype(bf16)
    back = back.transpose(1, 0, 2)

    early = sum_ctx_small(
        jnp.concatenate(
            [
                grad_wout.astype(bf16),
                grad_sdown.astype(bf16),
                grad_scols[:, :, :SHARED].reshape(96 * 1024 // WIDTH, WIDTH),
                grad_scols[:, :, SHARED:].reshape(96 * 1024 // WIDTH, WIDTH),
            ],
            axis=0,
        )
    )
    late = sum_ctx_small(
        jnp.concatenate(
            [
                back[:, :, :96].reshape(96, WIDTH),
                back[:, :, 96:128].reshape(96, KV_WIDTH),
                back[:, :, 128:160].reshape(96, KV_WIDTH),
                jnp.pad(gain_sum, ((0, 0), (0, 126))),
            ],
            axis=1,
        )
    ).astype(f32)
    early = early.astype(f32)
    return (
        mixed,
        input_grad,
        late[:, 2560],
        late[:, 2561],
        late[:, :WIDTH],
        late[:, WIDTH : WIDTH + KV_WIDTH],
        late[:, WIDTH + KV_WIDTH : WIDTH + 2 * KV_WIDTH],
        early[:96],
        early[160:224].reshape(96, 1024),
        early[224:288].reshape(96, 1024),
        early[96:160],
        sum_egate.astype(f32).reshape(LOCAL_E, WIDTH, FF_E),
        sum_eup.astype(f32).reshape(LOCAL_E, WIDTH, FF_E),
        sum_edown.astype(f32).reshape(LOCAL_E, FF_E, WIDTH),
    )


def solution(mesh):
    token_spec = P("exp", "ctx", None)
    rows = P("exp", None)
    expert = P("exp", None, None)
    placed = (token_spec,) * 3 + (P("exp"),) * 2 + (rows,) * 7 + (expert,) * 3 + (token_spec,)
    return jax.shard_map(
        on_device,
        mesh=mesh,
        in_specs=placed,
        out_specs=(token_spec,) * 2 + (P("exp"),) * 2 + (rows,) * 7 + (expert,) * 3,
        check_vma=False,
    )
```

time: 1570 us -> 834 us (0.53)
  waiting for transfers between devices: 1030 us -> 289 us
  blocking collectives: 153 us -> 0 us
  starting transfers between devices: 27.6 us -> 132 us
  local copies, waits for them, and re-layouts: 108 us -> 162 us
  matrix products: 158 us -> 138 us
  other arithmetic: 70.5 us -> 87 us
    reduce_scatter x7 -> x0, waiting for transfers between devices: 430 us -> none  [the longest x1 70.2 us: on_device(): lax.psum_scatter(grad_wout.astype(jnp.bfloat16), 'exp', scatter_dimension...]
    all_to_all x4 -> x18, waiting for transfers between devices: 309 us -> 163 us  [swap_all(): lax.all_to_all(rows, axis, split_axis=0, concat_axis=0, tiled=True, axis_...]
    unnamed x21 -> x6, waiting for transfers between devices: 143 us -> 0.78 us
    unnamed x2 -> x0, blocking collectives: 130 us -> none
    all_gather x9 -> x6, waiting for transfers between devices: 150 us -> 88 us  [the longest x1 32.8 us: on_device(): lax.all_gather(jnp.concatenate([cotangent[0], meta], axis=1), 'exp', axis...]
    all_to_all x4 -> x18, starting transfers between devices: 25.7 us -> 84.6 us  [swap_all(): lax.all_to_all(rows, axis, split_axis=0, concat_axis=0, tiled=True, axis_...]
    ppermute x0 -> x22, starting transfers between devices: none -> 47 us  [the longest x2 14.4 us: sum_ctx_y(): other = lax.ppermute(own, 'ctx', z_swap)]
    gather x4 -> x0, local copies, waits for them, and re-layouts: 41.4 us -> none  [the longest x1 11.7 us: on_device(): padded_up[slot_token]]
  transfers between devices with their start and end apart: 23 -> 46, of which waited for: 18 -> 23; matrix products, arithmetic and copies ran while one was open for 16% -> 44% of each run, Pallas kernels for 0% -> 0%
where the time goes in v1:
time: 834 us; the launch traced here: 824 us
  waiting for transfers between devices  289 us (35%)
  local copies, waits for them, and re-layouts  162 us (19%)
  matrix products  138 us (17%)
  starting transfers between devices  132 us (16%)
  other arithmetic  87 us (10%)
  between operations  15.9 us (2%)
    all_to_all x18, waiting for transfers between devices, swap_all(): lax.all_to_all(rows, axis, split_axis=0, concat_axis=0, tiled=True, axis_...  163 us
    all_to_all x18, starting transfers between devices, swap_all(): lax.all_to_all(rows, axis, split_axis=0, concat_axis=0, tiled=True, axis_...  84.6 us
    dot_general x8, matrix products, mm(): return lax.dot_general(a, b, (dims, ((), ())), preferred_element_type=f32)  40.9 us
    all_gather x1, waiting for transfers between devices, on_device(): lax.all_gather(jnp.concatenate([cotangent[0], meta], axis=1), 'exp', axis...  32.8 us
    unnamed x154, local copies, waits for them, and re-layouts  31.3 us
    all_gather x1, waiting for transfers between devices, on_device(): hidden_all = lax.all_gather(hidden_two, 'exp', axis=0, tiled=True)  28.3 us
    all_gather x1, waiting for transfers between devices, on_device(): lax.all_gather(jnp.concatenate([query_weight, key_weight, value_weight],...  26.8 us
    ppermute x3, waiting for transfers between devices, on_device(): lax.ppermute(part_kv[0, step], 'ctx', [(4 * z + (y + step) % 4, 4 * z + y...  21.9 us
  transfers between devices with their start and end apart: 46, of which 23 were waited for; matrix products, arithmetic and copies ran while one was open for 44% of the time, Pallas kernels for 0%

profile of v1, /device:TPU:0, one launch (start us, length us, event | category | flops | bytes accessed | tf_op | source)
XLA Modules:
  0.0 823.7 jit_solution(2353103855664177753)
XLA Ops:
  13.4 6.1 concatenate.61
  20.9 5.8 all-to-all-start
  35.9 26.8 %all-gather.7.cloned.1.call-done = bf16[1536,2560]{1,0:T(8,128)(2,1)} async-done(((bf16[96,2560]{1,0:T(8,128)(2,1)}), bf16[1536,2560]{1,0:T(8,128)(2,1)}) %all-gather.7.cloned.1.call-update) | async-done | bytes 7864336 | tf_op jit(solution)/shard_map/all_gather | solution.py:129
  70.5 5.6 collective-permute-start.3
  135.6 32.8 %all-gather.11.cloned.1.call-done = bf16[2048,1664]{0,1:T(8,128)(2,1)} async-done(((bf16[128,1664]{0,1:T(8,128)(2,1)}), bf16[2048,1664]{0,1:T(8,128)(2,1)}) %all-gather.11.cloned.1.call-update) | async-done | bytes 6815760 | tf_op jit(solution)/shard_map/all_gather | solution.py:152
  171.7 6.6 slice.159
  178.3 8.6 %copy.343 = bf16[2048,1536]{1,0:T(8,128)(2,1)} copy(bf16[2048,1536]{0,1:T(8,128)(2,1)} %slice.159) | data formatting | bytes 12582912 | tf_op jit(solution)/shard_map/reshape | solution.py:230
  194.9 28.3 %all-gather.13.cloned.1.call-done = bf16[2048,1536]{0,1:T(8,128)(2,1)} async-done(((bf16[128,1536]{0,1:T(8,128)(2,1)}), bf16[2048,1536]{0,1:T(8,128)(2,1)}) %all-gather.13.cloned.1.call-update) | async-done | bytes 6291472 | tf_op jit(solution)/shard_map/all_gather | solution.py:213
  223.2 8.6 %copy.342 = bf16[2048,1536]{1,0:T(8,128)(2,1)} copy(bf16[2048,1536]{0,1:T(8,128)(2,1)} %all-gather.13.cloned.1.call-done) | data formatting | bytes 12582912 | tf_op jit(solution)/shard_map/reshape | solution.py:240
  244.6 5.2 multiply_convert_fusion.1
  251.0 5.3 fusion.128
  260.2 5.0 multiply_convert_fusion.6
  268.9 8.0 add_convert_fusion
  285.3 7.5 convolution_convert_fusion.2
  297.4 5.4 fusion.3
  302.8 33.2 %all-to-all-done.12 = bf16[4,2,384,512]{3,2,1,0:T(8,128)(2,1)} async-done(((bf16[4,2,384,512]{3,2,1,0:T(8,128)(2,1)}), bf16[4,2,384,512]{3,2,1,0:T(8,128)(2,1)}, u32[]{:S(2)}, u32[]{:S(2)}) %all-to-all-start.12) | async-done | bytes 3145760 | tf_op jit(solution)/shard_map/all_to_all | solution.py:51
  336.0 4.9 all-to-all-start.3
  344.9 5.5 convolution_convert_fusion.1
  363.3 23.2 %all-to-all-done.3 = bf16[8,128,1536]{2,1,0:T(8,128)(2,1)} async-done(((bf16[8,128,1536]{2,1,0:T(8,128)(2,1)}), bf16[8,128,1536]{2,1,0:T(8,128)(2,1)}, u32[]{:S(2)}, u32[]{:S(2)}) %all-to-all-start.3) | async-done | bytes 3145760 | tf_op jit(solution)/shard_map/all_to_all | solution.py:51
  386.5 4.8 all-to-all-start.16
  393.2 6.9 fusion.1
  434.6 5.4 convolution_convert_fusion.6
  442.6 8.4 %all-to-all-done.14 = bf16[4,384,512]{2,1,0:T(8,128)(2,1)S(1)} async-done(((bf16[4,384,512]{2,1,0:T(8,128)(2,1)}), bf16[4,384,512]{2,1,0:T(8,128)(2,1)S(1)}, u32[]{:S(2)}, u32[]{:S(2)}) %all-to-all-start.14) | async-done | bytes 1572896 | tf_op jit(solution)/shard_map/all_to_all | solution.py:51
  476.9 9.7 %all-to-all-done.9 = bf16[16,96,128]{2,1,0:T(8,128)(2,1)S(1)} async-done(((bf16[16,96,128]{2,1,0:T(8,128)(2,1)}), bf16[16,96,128]{2,1,0:T(8,128)(2,1)S(1)}, u32[]{:S(2)}, u32[]{:S(2)}) %all-to-all-start.9) | async-done | bytes 393248 | tf_op jit(solution)/shard_map/all_to_all | solution.py:51
  492.3 5.6 fusion.6
  502.6 5.6 fusion.29
  508.2 5.6 all-to-all-done.15
  516.9 4.9 all-to-all-start.13
  543.9 21.9 %collective-permute-done.11 = bf16[128,1024]{0,1:T(8,128)(2,1)S(1)} collective-permute-done((bf16[128,1024]{0,1:T(8,128)(2,1)S(1)}, bf16[128,1024]{0,1:T(8,128)(2,1)S(1)}, u32[]{:S(2)}, u32[]{:S(2)}) %collective-permute-start.11) | collective-permute-done | bytes 262176 | tf_op jit(solution)/shard_map/ppermute | solution.py:328
  565.7 13.7 %collective-permute-start.21 = (bf16[128,1536]{1,0:T(8,128)(2,1)}, bf16[128,1536]{1,0:T(8,128)(2,1)S(1)}, u32[]{:S(2)}, u32[]{:S(2)}) collective-permute-start(bf16[128,1536]{1,0:T(8,128)(2,1)} %fusion.49), channel_id=1, source_target_pairs={{0,64},{16,80},{32,96},{48,112},{64,0},{80,16},{96,32},{112,48},{1... | collective-permute-start | bytes 1179656 | tf_op jit(solution)/shard_map/ppermute | solution.py:80
  579.4 5.2 collective-permute-done.15
  592.2 11.0 %all-to-all-done.4 = bf16[16,128,160]{1,2,0:T(8,128)(2,1)S(1)} async-done(((bf16[16,128,160]{1,2,0:T(8,128)(2,1)}), bf16[16,128,160]{1,2,0:T(8,128)(2,1)S(1)}, u32[]{:S(2)}, u32[]{:S(2)}) %all-to-all-start.4) | async-done | bytes 655392 | tf_op jit(solution)/shard_map/all_to_all | solution.py:51
  612.1 7.0 fusion.47
  621.3 5.9 convolution_convert_fusion.4
  632.1 14.1 %all-to-all-done.17 = bf16[4,2,128,1536]{3,2,1,0:T(8,128)(2,1)S(1)} async-done(((bf16[4,2,128,1536]{3,2,1,0:T(8,128)(2,1)}), bf16[4,2,128,1536]{3,2,1,0:T(8,128)(2,1)S(1)}, u32[]{:S(2)}, u32[]{:S(2)}) %all-to-all-start.17) | async-done | bytes 3145760 | tf_op jit(solution)/shard_map/all_to_all | solution.py:51
  650.4 5.4 fusion.4
  655.9 8.2 all-to-all-done.5
  664.1 4.7 all-to-all-start.2
  668.8 5.6 convolution_convert_fusion.8
  701.9 12.3 %all-to-all-done.2 = bf16[8,128,1536]{2,1,0:T(8,128)(2,1)} async-done(((bf16[8,128,1536]{2,1,0:T(8,128)(2,1)}), bf16[8,128,1536]{2,1,0:T(8,128)(2,1)}, u32[]{:S(2)}, u32[]{:S(2)}) %all-to-all-start.2) | async-done | bytes 3145760 | tf_op jit(solution)/shard_map/all_to_all | solution.py:51
  718.5 5.0 convolution_convert_fusion.7
  726.7 17.4 %all-to-all-done.6 = bf16[8,12,2688]{2,1,0:T(8,128)(2,1)} async-done(((bf16[8,12,2688]{2,1,0:T(8,128)(2,1)}), bf16[8,12,2688]{2,1,0:T(8,128)(2,1)}, u32[]{:S(2)}, u32[]{:S(2)}) %all-to-all-start.6) | async-done | bytes 516128 | tf_op jit(solution)/shard_map/all_to_all | solution.py:51
  744.1 5.6 all-to-all-start.10
  749.7 5.5 convert.50
  758.8 5.8 fusion.16
  766.7 7.3 all-to-all-start.7
  780.7 5.3 all-to-all-done.7
  800.1 6.9 all-to-all-done.11
  (366 shorter events, 344.8 us)
Async XLA Ops:
  7.2 237.4 %copy-start = (bf16[2,512,1536]{2,1,0:T(8,128)(2,1)S(1)}, bf16[2,512,1536]{2,1,0:T(8,128)(2,1)}, u32[]{:S(2)}) copy-start(bf16[2,512,1536]{2,1,0:T(8,128)(2,1)} %param.30) | copy-start | bytes 9437188
  7.2 55.5 %all-gather.7.cloned.1.call-start = ((), (), s32[]{:S(2)}) async-start(), calls=%async_computation.18 | async-start | bytes 8355840 | tf_op jit(solution)/shard_map/all_gather | solution.py:129
  9.3 107.3 %all-gather.9.cloned.1.call-start = ((), (), s32[]{:S(2)}) async-start(), calls=%async_computation.19 | async-start | bytes 5013504 | tf_op jit(solution)/shard_map/all_gather | solution.py:132
  10.1 158.4 %all-gather.11.cloned.1.call-start = ((), (), s32[]{:S(2)}) async-start(), calls=%async_computation.20 | async-start | bytes 7241728 | tf_op jit(solution)/shard_map/all_gather | solution.py:152
  20.9 12.0 %all-to-all-start = ((bf16[16,1,192]{2,1,0:T(2,128)(2,1)}), bf16[16,1,192]{2,1,0:T(2,128)(2,1)S(1)}, u32[]{:S(2)}, u32[]{:S(2)}) async-start(bf16[16,1,192]{2,1,0:T(2,128)(2,1)} %broadcast_in_dim.37), calls=%async_computation | async-start | bytes 32768 | tf_op jit(solution)/shard_map/all_to_all | solution.py:51
  26.7 196.5 %all-gather.13.cloned.1.call-start = ((), (), s32[]{:S(2)}) async-start(), calls=%async_computation.21 | async-start | bytes 6684672 | tf_op jit(solution)/shard_map/all_gather | solution.py:213
  69.0 19.7 %collective-permute-start = (bf16[128,1024]{1,0:T(8,128)(2,1)}, bf16[128,1024]{1,0:T(8,128)(2,1)}, u32[]{:S(2)}, u32[]{:S(2)}) collective-permute-start(bf16[128,1024]{1,0:T(8,128)(2,1)} %get-tuple-element.75), channel_id=1, source_target_pairs={{0,16},{16,32},{32,48},{48,0},{64,80},{80,96},{96,112},{112,64},{1... | collective-permute-start | bytes 786440 | tf_op jit(solution)/shard_map/ppermute | solution.py:172
  70.5 16.9 %collective-permute-start.3 = (bf16[128,1024]{1,0:T(8,128)(2,1)}, bf16[128,1024]{1,0:T(8,128)(2,1)}, u32[]{:S(2)}, u32[]{:S(2)}) collective-permute-start(bf16[128,1024]{1,0:T(8,128)(2,1)} %get-tuple-element.75), channel_id=1, source_target_pairs={{0,64},{16,80},{32,96},{48,112},{1,65},{17,81},{33,97},{49,113},{2... | collective-permute-start | bytes 786440 | tf_op jit(solution)/shard_map/ppermute | solution.py:166
  76.1 15.5 %collective-permute-start.1 = (bf16[128,1024]{1,0:T(8,128)(2,1)}, bf16[128,1024]{1,0:T(8,128)(2,1)}, u32[]{:S(2)}, u32[]{:S(2)}) collective-permute-start(bf16[128,1024]{1,0:T(8,128)(2,1)} %get-tuple-element.75), channel_id=1, source_target_pairs={{0,32},{16,48},{32,0},{48,16},{64,96},{80,112},{96,64},{112,80},{1... | collective-permute-start | bytes 786440 | tf_op jit(solution)/shard_map/ppermute | solution.py:172
  78.8 14.5 %collective-permute-start.2 = (bf16[128,1024]{1,0:T(8,128)(2,1)}, bf16[128,1024]{1,0:T(8,128)(2,1)}, u32[]{:S(2)}, u32[]{:S(2)}) collective-permute-start(bf16[128,1024]{1,0:T(8,128)(2,1)} %get-tuple-element.75), channel_id=1, source_target_pairs={{0,48},{16,0},{32,16},{48,32},{64,112},{80,64},{96,80},{112,96},{1... | collective-permute-start | bytes 786440 | tf_op jit(solution)/shard_map/ppermute | solution.py:172
  87.3 9.3 %collective-permute-start.4 = (bf16[128,1024]{1,0:T(8,128)(2,1)}, bf16[128,1024]{1,0:T(8,128)(2,1)S(1)}, u32[]{:S(2)}, u32[]{:S(2)}) collective-permute-start(bf16[128,1024]{1,0:T(8,128)(2,1)} %collective-permute-done.3), channel_id=1, source_target_pairs={{64,80},{80,96},{96,112},{112,64},{65,81},{81,97},{97,113},{113,65... | collective-permute-start | bytes 786440 | tf_op jit(solution)/shard_map/ppermute | solution.py:184
  88.0 9.3 %collective-permute-start.5 = (bf16[128,1024]{1,0:T(8,128)(2,1)}, bf16[128,1024]{1,0:T(8,128)(2,1)S(1)}, u32[]{:S(2)}, u32[]{:S(2)}) collective-permute-start(bf16[128,1024]{1,0:T(8,128)(2,1)} %collective-permute-done.3), channel_id=1, source_target_pairs={{64,96},{80,112},{96,64},{112,80},{65,97},{81,113},{97,65},{113,81... | collective-permute-start | bytes 786440 | tf_op jit(solution)/shard_map/ppermute | solution.py:184
  88.7 9.4 %collective-permute-start.6 = (bf16[128,1024]{1,0:T(8,128)(2,1)}, bf16[128,1024]{1,0:T(8,128)(2,1)S(1)}, u32[]{:S(2)}, u32[]{:S(2)}) collective-permute-start(bf16[128,1024]{1,0:T(8,128)(2,1)} %collective-permute-done.3), channel_id=1, source_target_pairs={{64,112},{80,64},{96,80},{112,96},{65,113},{81,65},{97,81},{113,97... | collective-permute-start | bytes 786440 | tf_op jit(solution)/shard_map/ppermute | solution.py:184
  130.6 125.6 %all-to-all-start.1 = ((bf16[16,96,128]{2,1,0:T(8,128)(2,1)}), bf16[16,96,128]{2,1,0:T(8,128)(2,1)}, u32[]{:S(2)}, u32[]{:S(2)}) async-start(bf16[16,96,128]{2,1,0:T(8,128)(2,1)} %copy.276), calls=%async_computation.1 | async-start | bytes 786432 | tf_op jit(solution)/shard_map/all_to_all | solution.py:51
  134.8 486.4 %all-gather.15.cloned.1.call-start = ((), (), s32[]{:S(2)}) async-start(), calls=%async_computation.22 | async-start | bytes 6684672 | tf_op jit(solution)/shard_map/all_gather | solution.py:348
  285.3 12.1 %collective-permute-start.8 = (bf16[8,128,1536]{2,1,0:T(8,128)(2,1)}, bf16[8,128,1536]{2,1,0:T(8,128)(2,1)}, u32[]{:S(2)}, u32[]{:S(2)}) collective-permute-start(bf16[8,128,1536]{2,1,0:T(8,128)(2,1)} %dynamic-slice_bitcast_fusion), channel_id=1, source_target_pairs={{0,1},{1,0},{2,3},{3,2},{4,5},{5,4},{6,7},{7,6},{8,9},{9,8},{10,11... | collective-permute-start | bytes 9437192 | tf_op jit(solution)/shard_map/ppermute | solution.py:68
  292.7 43.2 %all-to-all-start.12 = ((bf16[4,2,384,512]{3,2,1,0:T(8,128)(2,1)}), bf16[4,2,384,512]{3,2,1,0:T(8,128)(2,1)}, u32[]{:S(2)}, u32[]{:S(2)}) async-start(bf16[4,2,384,512]{3,2,1,0:T(8,128)(2,1)} %bitcast.321), calls=%async_computation.12 | async-start | bytes 6291456 | tf_op jit(solution)/shard_map/all_to_all | solution.py:51
  336.0 50.6 %all-to-all-start.3 = ((bf16[8,128,1536]{2,1,0:T(8,128)(2,1)}), bf16[8,128,1536]{2,1,0:T(8,128)(2,1)}, u32[]{:S(2)}, u32[]{:S(2)}) async-start(bf16[8,128,1536]{2,1,0:T(8,128)(2,1)} %fusion.3), calls=%async_computation.3 | async-start | bytes 6291456 | tf_op jit(solution)/shard_map/all_to_all | solution.py:51
  351.7 61.6 %collective-permute-start.18 = (bf16[4,384,512]{2,1,0:T(8,128)(2,1)}, bf16[4,384,512]{2,1,0:T(8,128)(2,1)}, u32[]{:S(2)}, u32[]{:S(2)}) collective-permute-start(bf16[4,384,512]{2,1,0:T(8,128)(2,1)} %dynamic-slice_bitcast_fusion.2), channel_id=1, source_target_pairs={{0,64},{16,80},{32,96},{48,112},{64,0},{80,16},{96,32},{112,48},{1... | collective-permute-start | bytes 4718600 | tf_op jit(solution)/shard_map/ppermute | solution.py:89
  386.5 41.8 %all-to-all-start.16 = ((bf16[4,2,128,1536]{3,2,1,0:T(8,128)(2,1)}), bf16[4,2,128,1536]{3,2,1,0:T(8,128)(2,1)}, u32[]{:S(2)}, u32[]{:S(2)}) async-start(bf16[4,2,128,1536]{3,2,1,0:T(8,128)(2,1)} %bitcast.98), calls=%async_computation.16 | async-start | bytes 6291456 | tf_op jit(solution)/shard_map/all_to_all | solution.py:51
  402.9 17.5 %collective-permute-start.16 = (bf16[384,512]{1,0:T(8,128)(2,1)S(1)}, bf16[384,512]{1,0:T(8,128)(2,1)S(1)}, u32[]{:S(2)}, u32[]{:S(2)}) collective-permute-start(bf16[384,512]{1,0:T(8,128)(2,1)S(1)} %dynamic-slice_bitcast_fusion.4), channel_id=1, source_target_pairs={{0,64},{16,80},{32,96},{48,112},{64,0},{80,16},{96,32},{112,48},{1... | collective-permute-start | bytes 1179656 | tf_op jit(solution)/shard_map/ppermute | solution.py:78
  409.8 240.6 %collective-permute-start.7 = (bf16[8,128,1536]{2,1,0:T(8,128)(2,1)}, bf16[8,128,1536]{2,1,0:T(8,128)(2,1)}, u32[]{:S(2)}, u32[]{:S(2)}) collective-permute-start(bf16[8,128,1536]{2,1,0:T(8,128)(2,1)} %dynamic-slice_bitcast_fusion.1), channel_id=1, source_target_pairs={{0,1},{1,0},{2,3},{3,2},{4,5},{5,4},{6,7},{7,6},{8,9},{9,8},{10,11... | collective-permute-start | bytes 9437192 | tf_op jit(solution)/shard_map/ppermute | solution.py:68
  421.2 39.3 %collective-permute-start.17 = (bf16[384,512]{1,0:T(8,128)(2,1)}, bf16[384,512]{1,0:T(8,128)(2,1)}, u32[]{:S(2)}, u32[]{:S(2)}) collective-permute-start(bf16[384,512]{1,0:T(8,128)(2,1)} %fusion.50), channel_id=1, source_target_pairs={{0,64},{16,80},{32,96},{48,112},{64,0},{80,16},{96,32},{112,48},{1... | collective-permute-start | bytes 1179656 | tf_op jit(solution)/shard_map/ppermute | solution.py:80
  428.3 22.7 %all-to-all-start.14 = ((bf16[4,384,512]{2,1,0:T(8,128)(2,1)}), bf16[4,384,512]{2,1,0:T(8,128)(2,1)S(1)}, u32[]{:S(2)}, u32[]{:S(2)}) async-start(bf16[4,384,512]{2,1,0:T(8,128)(2,1)} %fusion.17), calls=%async_computation.14 | async-start | bytes 3145728 | tf_op jit(solution)/shard_map/all_to_all | solution.py:51
  431.9 286.5 %all-gather.17.cloned.1.call-start = ((), (), s32[]{:S(2)}) async-start(), calls=%async_computation.23 | async-start | bytes 6684672 | tf_op jit(solution)/shard_map/all_gather | solution.py:349
  451.1 15.4 %all-to-all-start.8 = ((bf16[16,128,96]{1,2,0:T(8,128)(2,1)}), bf16[16,128,96]{1,2,0:T(8,128)(2,1)S(1)}, u32[]{:S(2)}, u32[]{:S(2)}) async-start(bf16[16,128,96]{1,2,0:T(8,128)(2,1)} %bitcast.84), calls=%async_computation.8 | async-start | bytes 786432 | tf_op jit(solution)/shard_map/all_to_all | solution.py:51
  456.5 76.2 %collective-permute-start.20 = (bf16[128,1536]{1,0:T(8,128)(2,1)}, bf16[128,1536]{1,0:T(8,128)(2,1)}, u32[]{:S(2)}, u32[]{:S(2)}) collective-permute-start(bf16[128,1536]{1,0:T(8,128)(2,1)} %dynamic-slice_bitcast_fusion.3), channel_id=1, source_target_pairs={{0,64},{16,80},{32,96},{48,112},{64,0},{80,16},{96,32},{112,48},{1... | collective-permute-start | bytes 1179656 | tf_op jit(solution)/shard_map/ppermute | solution.py:78
  467.2 19.4 %all-to-all-start.9 = ((bf16[16,96,128]{2,1,0:T(8,128)(2,1)}), bf16[16,96,128]{2,1,0:T(8,128)(2,1)S(1)}, u32[]{:S(2)}, u32[]{:S(2)}) async-start(bf16[16,96,128]{2,1,0:T(8,128)(2,1)} %bitcast.334), calls=%async_computation.9 | async-start | bytes 786432 | tf_op jit(solution)/shard_map/all_to_all | solution.py:51
  487.9 26.0 %all-to-all-start.15 = ((bf16[4,384,512]{2,1,0:T(8,128)(2,1)}), bf16[4,384,512]{2,1,0:T(8,128)(2,1)}, u32[]{:S(2)}, u32[]{:S(2)}) async-start(bf16[4,384,512]{2,1,0:T(8,128)(2,1)} %broadcast_in_dim.81), calls=%async_computation.15 | async-start | bytes 3145728 | tf_op jit(solution)/shard_map/all_to_all | solution.py:51
  516.9 70.4 %all-to-all-start.13 = ((bf16[4,2,384,512]{3,2,1,0:T(8,128)(2,1)}), bf16[4,2,384,512]{3,2,1,0:T(8,128)(2,1)}, u32[]{:S(2)}, u32[]{:S(2)}) async-start(bf16[4,2,384,512]{3,2,1,0:T(8,128)(2,1)} %broadcast_in_dim.80), calls=%async_computation.13 | async-start | bytes 6291456 | tf_op jit(solution)/shard_map/all_to_all | solution.py:51
  530.6 5.9 collective-permute-start.14
  531.3 7.9 collective-permute-start.13
  532.0 8.7 %collective-permute-start.12 = (bf16[128,1024]{0,1:T(8,128)(2,1)S(1)}, bf16[128,1024]{0,1:T(8,128)(2,1)S(1)}, u32[]{:S(2)}, u32[]{:S(2)}) collective-permute-start(bf16[128,1024]{0,1:T(8,128)(2,1)S(1)} %get-tuple-element.58), channel_id=1, source_target_pairs={{80,64},{96,80},{112,96},{64,112},{81,65},{97,81},{113,97},{65,113... | collective-permute-start | bytes 786440 | tf_op jit(solution)/shard_map/ppermute | solution.py:333
  534.5 31.2 %collective-permute-start.11 = (bf16[128,1024]{0,1:T(8,128)(2,1)S(1)}, bf16[128,1024]{0,1:T(8,128)(2,1)S(1)}, u32[]{:S(2)}, u32[]{:S(2)}) collective-permute-start(bf16[128,1024]{0,1:T(8,128)(2,1)S(1)} %get-tuple-element.59), channel_id=1, source_target_pairs={{48,0},{0,16},{16,32},{32,48},{112,64},{64,80},{80,96},{96,112},{4... | collective-permute-start | bytes 786440 | tf_op jit(solution)/shard_map/ppermute | solution.py:328
  536.5 42.9 %collective-permute-start.10 = (bf16[128,1024]{0,1:T(8,128)(2,1)S(1)}, bf16[128,1024]{0,1:T(8,128)(2,1)S(1)}, u32[]{:S(2)}, u32[]{:S(2)}) collective-permute-start(bf16[128,1024]{0,1:T(8,128)(2,1)S(1)} %get-tuple-element.60), channel_id=1, source_target_pairs={{32,0},{48,16},{0,32},{16,48},{96,64},{112,80},{64,96},{80,112},{3... | collective-permute-start | bytes 786440 | tf_op jit(solution)/shard_map/ppermute | solution.py:328
  539.2 40.2 %collective-permute-start.9 = (bf16[128,1024]{0,1:T(8,128)(2,1)S(1)}, bf16[128,1024]{0,1:T(8,128)(2,1)S(1)}, u32[]{:S(2)}, u32[]{:S(2)}) collective-permute-start(bf16[128,1024]{0,1:T(8,128)(2,1)S(1)} %get-tuple-element.55), channel_id=1, source_target_pairs={{16,0},{32,16},{48,32},{0,48},{80,64},{96,80},{112,96},{64,112},{1... | collective-permute-start | bytes 786440 | tf_op jit(solution)/shard_map/ppermute | solution.py:328
  541.8 42.8 %collective-permute-start.15 = (bf16[128,1024]{0,1:T(8,128)(2,1)S(1)}, bf16[128,1024]{0,1:T(8,128)(2,1)S(1)}, u32[]{:S(2)}, u32[]{:S(2)}) collective-permute-start(bf16[128,1024]{0,1:T(8,128)(2,1)S(1)} %fusion.61), channel_id=1, source_target_pairs={{64,0},{80,16},{96,32},{112,48},{65,1},{81,17},{97,33},{113,49},{6... | collective-permute-start | bytes 786440 | tf_op jit(solution)/shard_map/ppermute | solution.py:336
  543.8 42.6 %copy-start.27 = (bf16[4,128,3,128]{3,1,2,0:T(8,128)(2,1)}, bf16[4,128,3,128]{3,1,2,0:T(8,128)(2,1)S(1)}, u32[]{:S(2)}) copy-start(bf16[4,128,3,128]{3,1,2,0:T(8,128)(2,1)S(1)} %fusion.33) | copy-start | bytes 1179652
  565.7 25.2 %collective-permute-start.21 = (bf16[128,1536]{1,0:T(8,128)(2,1)}, bf16[128,1536]{1,0:T(8,128)(2,1)S(1)}, u32[]{:S(2)}, u32[]{:S(2)}) collective-permute-start(bf16[128,1536]{1,0:T(8,128)(2,1)} %fusion.49), channel_id=1, source_target_pairs={{0,64},{16,80},{32,96},{48,112},{64,0},{80,16},{96,32},{112,48},{1... | collective-permute-start | bytes 1179656 | tf_op jit(solution)/shard_map/ppermute | solution.py:80
  587.3 15.8 %all-to-all-start.4 = ((bf16[16,128,160]{1,2,0:T(8,128)(2,1)}), bf16[16,128,160]{1,2,0:T(8,128)(2,1)S(1)}, u32[]{:S(2)}, u32[]{:S(2)}) async-start(bf16[16,128,160]{1,2,0:T(8,128)(2,1)} %maximum_bitcast_fusion), calls=%async_computation.4 | async-start | bytes 1310720 | tf_op jit(solution)/shard_map/all_to_all | solution.py:51
  605.1 41.0 %all-to-all-start.17 = ((bf16[4,2,128,1536]{3,2,1,0:T(8,128)(2,1)}), bf16[4,2,128,1536]{3,2,1,0:T(8,128)(2,1)S(1)}, u32[]{:S(2)}, u32[]{:S(2)}) async-start(bf16[4,2,128,1536]{3,2,1,0:T(8,128)(2,1)} %broadcast_in_dim.82), calls=%async_computation.17 | async-start | bytes 6291456 | tf_op jit(solution)/shard_map/all_to_all | solution.py:51
  646.1 18.0 %all-to-all-start.5 = ((bf16[16,96,192]{2,1,0:T(8,128)(2,1)}), bf16[16,96,192]{2,1,0:T(8,128)(2,1)}, u32[]{:S(2)}, u32[]{:S(2)}) async-start(bf16[16,96,192]{2,1,0:T(8,128)(2,1)} %maximum_maximum_fusion), calls=%async_computation.5 | async-start | bytes 1572864 | tf_op jit(solution)/shard_map/all_to_all | solution.py:51
  664.1 50.1 %all-to-all-start.2 = ((bf16[8,128,1536]{2,1,0:T(8,128)(2,1)}), bf16[8,128,1536]{2,1,0:T(8,128)(2,1)}, u32[]{:S(2)}, u32[]{:S(2)}) async-start(bf16[8,128,1536]{2,1,0:T(8,128)(2,1)} %fusion.4), calls=%async_computation.2 | async-start | bytes 6291456 | tf_op jit(solution)/shard_map/all_to_all | solution.py:51
  682.0 76.8 %collective-permute-start.19 = (bf16[4,384,512]{2,1,0:T(8,128)(2,1)}, bf16[4,384,512]{2,1,0:T(8,128)(2,1)}, u32[]{:S(2)}, u32[]{:S(2)}) collective-permute-start(bf16[4,384,512]{2,1,0:T(8,128)(2,1)} %all-to-all-done.15), channel_id=1, source_target_pairs={{0,64},{16,80},{32,96},{48,112},{64,0},{80,16},{96,32},{112,48},{1... | collective-permute-start | bytes 4718600 | tf_op jit(solution)/shard_map/ppermute | solution.py:93
  714.2 29.9 %all-to-all-start.6 = ((bf16[8,12,2688]{2,1,0:T(8,128)(2,1)}), bf16[8,12,2688]{2,1,0:T(8,128)(2,1)}, u32[]{:S(2)}, u32[]{:S(2)}) async-start(bf16[8,12,2688]{2,1,0:T(8,128)(2,1)} %pad_maximum_fusion.1), calls=%async_computation.6 | async-start | bytes 1376256 | tf_op jit(solution)/shard_map/all_to_all | solution.py:51
  744.1 21.7 %all-to-all-start.10 = ((bf16[8,36,1536]{2,1,0:T(8,128)(2,1)}), bf16[8,36,1536]{2,1,0:T(8,128)(2,1)}, u32[]{:S(2)}, u32[]{:S(2)}) async-start(bf16[8,36,1536]{2,1,0:T(8,128)(2,1)} %reshape.376), calls=%async_computation.10 | async-start | bytes 1966080 | tf_op jit(solution)/shard_map/all_to_all | solution.py:51
  766.7 19.3 %all-to-all-start.7 = ((bf16[8,12,2688]{2,1,0:T(8,128)(2,1)}), bf16[8,12,2688]{2,1,0:T(8,128)(2,1)}, u32[]{:S(2)}, u32[]{:S(2)}) async-start(bf16[8,12,2688]{2,1,0:T(8,128)(2,1)} %broadcast_in_dim.78), calls=%async_computation.7 | async-start | bytes 1376256 | tf_op jit(solution)/shard_map/all_to_all | solution.py:51
  787.0 19.9 %all-to-all-start.11 = ((bf16[8,36,1536]{2,1,0:T(8,128)(2,1)}), bf16[8,36,1536]{2,1,0:T(8,128)(2,1)}, u32[]{:S(2)}, u32[]{:S(2)}) async-start(bf16[8,36,1536]{2,1,0:T(8,128)(2,1)} %broadcast_in_dim.79), calls=%async_computation.11 | async-start | bytes 1966080 | tf_op jit(solution)/shard_map/all_to_all | solution.py:51
  (68 other events, 520.0 us)
Sparse Core Ops, SparseCore 0:
  10.3 52.3 all-gather.6
  64.4 43.6 all-gather.8
  110.3 58.0 all-gather.10
  170.5 52.7 all-gather.12
  225.2 52.3 all-gather.14
  434.7 65.3 all-gather.16

commit v2 on v1

v2 whole, which is shorter than its diff:
```python
import jax
import jax.numpy as jnp
from jax import lax
from jax.sharding import PartitionSpec as P
from jax.experimental import pallas as pl
from jax.experimental.pallas import tpu as pltpu

HEADS = 12
KV_HEADS = 4
HEAD_DIM = 128
TOPK = 6
GROUP = 3
BLOCK = 128
WIDTH = 1536
KV_WIDTH = KV_HEADS * HEAD_DIM
CAP = 48
N_EXP = 16
N_CTX = 8
LOCAL_E = 2
FF_E = 512
SHARED = 64
META = 128
HALF = 8
ROWS = HALF * CAP

epsilon = 1e-05
masked_score = -1e30
f32 = jnp.float32
bf16 = jnp.bfloat16
log2_e = 1.4426950408889634
score_scale = HEAD_DIM ** (-0.5) * log2_e

NN = (((1,), (0,)), ((), ()))
NT = (((1,), (1,)), ((), ()))
TN = (((0,), (0,)), ((), ()))


def dg(a, b, dims):
    return lax.dot_general(a, b, dims, preferred_element_type=f32)


def params(mib):
    return pltpu.CompilerParams(vmem_limit_bytes=mib * 1024 * 1024)


def whole(shape):
    return pl.BlockSpec(shape, lambda *_: (0,) * len(shape), pipeline_mode=pl.Buffered(1))


def sigmoid(v):
    return 1.0 / (1.0 + jnp.exp(-v))


def allowed_scores(ctx_at):
    rows = lax.broadcasted_iota(jnp.int32, (GROUP * BLOCK, N_CTX * BLOCK), 0) % BLOCK
    cols = lax.broadcasted_iota(jnp.int32, (GROUP * BLOCK, N_CTX * BLOCK), 1)
    return rows + ctx_at * BLOCK >= cols


def stack_heads(block):
    return jnp.concatenate([block[:, j * HEAD_DIM : (j + 1) * HEAD_DIM] for j in range(GROUP)], axis=0)


def unstack_heads(rows):
    return jnp.concatenate([rows[j * BLOCK : (j + 1) * BLOCK] for j in range(GROUP)], axis=1)


def attend_kernel(ctx_ref, q_ref, k_ref, v_ref, att_ref, attf_ref, log_ref):
    q = stack_heads(q_ref[...])
    keys = k_ref[...].reshape(N_CTX * BLOCK, HEAD_DIM)
    values = v_ref[...].reshape(N_CTX * BLOCK, HEAD_DIM)
    scores = jnp.where(allowed_scores(ctx_ref[0]), dg(q, keys, NT) * score_scale, masked_score)
    top = jnp.max(scores, axis=-1, keepdims=True)
    weights = jnp.exp2(scores - top)
    total = jnp.sum(weights, axis=-1, keepdims=True)
    out = dg(weights.astype(bf16), values, NN) * (1.0 / total)
    out = unstack_heads(out)
    attf_ref[...] = out
    att_ref[...] = out.astype(bf16)
    log_ref[...] = jnp.broadcast_to(top + jnp.log2(total), (GROUP * BLOCK, HEAD_DIM))


def kv_specs():
    return [
        pl.BlockSpec((N_CTX, BLOCK, HEAD_DIM), lambda g: (0, 0, 2 * g)),
        pl.BlockSpec((N_CTX, BLOCK, HEAD_DIM), lambda g: (0, 0, 2 * g + 1)),
    ]


def head_spec():
    return pl.BlockSpec((BLOCK, GROUP * HEAD_DIM), lambda g: (0, g))


def attend(ctx_at, qkv, kv_all):
    return pl.pallas_call(
        attend_kernel,
        grid=(KV_HEADS,),
        in_specs=[pl.BlockSpec(memory_space=pltpu.SMEM), head_spec()] + kv_specs(),
        out_specs=[
            head_spec(),
            head_spec(),
            pl.BlockSpec((GROUP * BLOCK, HEAD_DIM), lambda g: (g, 0)),
        ],
        out_shape=[
            jax.ShapeDtypeStruct((BLOCK, WIDTH), bf16),
            jax.ShapeDtypeStruct((BLOCK, WIDTH), f32),
            jax.ShapeDtypeStruct((HEADS * BLOCK, HEAD_DIM), f32),
        ],
        compiler_params=params(48),
        name="attend",
    )(ctx_at, qkv, kv_all, kv_all)


def attend_back_kernel(
    ctx_ref, q_ref, ga_ref, attf_ref, log_ref, k_ref, v_ref, dq_ref, dkv_ref
):
    q = stack_heads(q_ref[...])
    grad = stack_heads(ga_ref[...])
    delta = jnp.sum(grad.astype(f32) * stack_heads(attf_ref[...]), axis=-1, keepdims=True)
    keys = k_ref[...].reshape(N_CTX * BLOCK, HEAD_DIM)
    values = v_ref[...].reshape(N_CTX * BLOCK, HEAD_DIM)
    scores = jnp.where(allowed_scores(ctx_ref[0]), dg(q, keys, NT) * score_scale, masked_score)
    weights = jnp.exp2(scores - log_ref[:, :1])
    grad_weights = dg(grad, values, NT)
    grad_raw = (weights * (grad_weights - delta)).astype(bf16)
    scale = HEAD_DIM ** (-0.5)
    dq_ref[...] = unstack_heads(dg(grad_raw, keys, NN) * scale).astype(bf16)
    grad_k = (dg(grad_raw, q, TN) * scale).astype(bf16)
    grad_v = dg(weights.astype(bf16), grad, TN).astype(bf16)
    dkv_ref[:, :, :HEAD_DIM] = grad_k.reshape(N_CTX, BLOCK, HEAD_DIM)
    dkv_ref[:, :, HEAD_DIM:] = grad_v.reshape(N_CTX, BLOCK, HEAD_DIM)


def attend_back(ctx_at, qkv, grad_att, att_f, logs, kv_all):
    part = pl.BlockSpec((N_CTX, BLOCK, 2 * HEAD_DIM), lambda g: (0, 0, g))
    return pl.pallas_call(
        attend_back_kernel,
        grid=(KV_HEADS,),
        in_specs=[
            pl.BlockSpec(memory_space=pltpu.SMEM),
            head_spec(),
            head_spec(),
            head_spec(),
            pl.BlockSpec((GROUP * BLOCK, HEAD_DIM), lambda g: (g, 0)),
        ]
        + kv_specs(),
        out_specs=[head_spec(), part],
        out_shape=[
            jax.ShapeDtypeStruct((BLOCK, WIDTH), bf16),
            jax.ShapeDtypeStruct((N_CTX, BLOCK, 2 * KV_WIDTH), bf16),
        ],
        compiler_params=params(48),
        name="attend_back",
    )(ctx_at, qkv, grad_att, att_f, logs, kv_all, kv_all)


def middle_kernel(att_ref, w_ref, x_ref, gain_ref, middle_ref, hidden_ref):
    middle = x_ref[...].astype(f32) + dg(att_ref[...], w_ref[...], NN)
    inv = lax.rsqrt(jnp.mean(middle * middle, axis=-1, keepdims=True) + epsilon)
    middle_ref[...] = middle
    hidden_ref[...] = (middle * inv * gain_ref[...]).astype(bf16)


def middle_norm(attended, w_out, tokens, gain):
    return pl.pallas_call(
        middle_kernel,
        out_shape=[
            jax.ShapeDtypeStruct((BLOCK, WIDTH), f32),
            jax.ShapeDtypeStruct((BLOCK, WIDTH), bf16),
        ],
        compiler_params=params(32),
        name="middle_norm",
    )(attended, w_out, tokens, gain)


def norm_back(grad_normed, normed, inv_root):
    return inv_root * (
        grad_normed - normed * jnp.mean(grad_normed * normed, axis=-1, keepdims=True)
    )


def middle_back_kernel(
    pieces_ref, middle_ref, up_ref, gain_ref, w_ref, gm_ref, ga_ref, gh_ref, gg_ref
):
    grad_two = pieces_ref[0].astype(f32)
    for i in range(1, HALF):
        grad_two = grad_two + pieces_ref[i].astype(f32)
    middle = middle_ref[...]
    inv = lax.rsqrt(jnp.mean(middle * middle, axis=-1, keepdims=True) + epsilon)
    normed = middle * inv
    gg_ref[...] = jnp.sum(grad_two * normed, axis=0, keepdims=True)
    grad_middle = up_ref[...].astype(f32) + norm_back(grad_two * gain_ref[...], normed, inv)
    gm_ref[...] = grad_middle
    grad_attn = grad_middle.astype(bf16)
    ga_ref[...] = grad_attn
    gh_ref[...] = dg(grad_attn, w_ref[...], NT).astype(bf16)


def middle_back(pieces, middle, upstream, gain, w_out):
    return pl.pallas_call(
        middle_back_kernel,
        out_shape=[
            jax.ShapeDtypeStruct((BLOCK, WIDTH), f32),
            jax.ShapeDtypeStruct((BLOCK, WIDTH), bf16),
            jax.ShapeDtypeStruct((BLOCK, WIDTH), bf16),
            jax.ShapeDtypeStruct((1, WIDTH), f32),
        ],
        compiler_params=params(48),
        name="middle_back",
    )(pieces, middle, upstream, gain, w_out)


def place_kernel(
    at_ref, own_ref, other_ref, down_ref, sdown_ref, place_ref, geo_ref, geh_ref, gsh_ref, gate_ref
):
    step = pl.program_id(0)
    lane = lax.broadcasted_iota(jnp.int32, (BLOCK, META), 1)
    row = lax.broadcasted_iota(jnp.int32, (BLOCK, META), 0)
    before = (row > lane).astype(bf16)
    slot = (lane % 64).astype(f32)
    first_id = (at_ref[0] * LOCAL_E).astype(f32)
    row_id = first_id + (row >= 64).astype(f32)

    def run(up_ref):
        for chip in range(HALF):
            meta = up_ref[chip, :, WIDTH:].astype(f32)
            named = lane < TOPK
            zero = jnp.zeros((BLOCK, META), f32)
            hit0 = jnp.where(named & (meta == first_id), 1.0, zero)
            hit1 = jnp.where(named & (meta == first_id + 1.0), 1.0, zero)
            mask = jnp.where(
                lane < 64,
                jnp.sum(hit0, axis=1, keepdims=True),
                jnp.sum(hit1, axis=1, keepdims=True),
            )
            rank = dg(before, mask.astype(bf16), NN)
            place = jnp.where((mask > 0.5) & (rank == slot), 1.0, zero).astype(bf16)
            place_ref[chip, 0] = place
            rows = dg(place, up_ref[chip], TN)
            slot_meta = rows[:, WIDTH:]
            gates = pltpu.roll(slot_meta, META - TOPK, 1) + pltpu.roll(
                slot_meta, META - 2 * TOPK, 1
            )
            gate = jnp.sum(
                jnp.where(named & (slot_meta == row_id), gates, zero), axis=1, keepdims=True
            )
            geo = (gate * rows[:, :WIDTH]).astype(bf16)
            wide_gate = jnp.broadcast_to(gate, (BLOCK, META))
            at = chip * CAP
            for e in range(LOCAL_E):
                geo_ref[e, 0, at : at + CAP] = geo[64 * e : 64 * e + CAP]
                gate_ref[e, 0, at : at + CAP] = wide_gate[64 * e : 64 * e + CAP]
            gsh_ref[chip, 0] = dg(up_ref[chip, :, :WIDTH], sdown_ref[...], NT)
        for e in range(LOCAL_E):
            geh_ref[e, 0] = dg(geo_ref[e, 0], down_ref[e], NT)

    @pl.when(step == 0)
    def _():
        run(other_ref)

    @pl.when(step == 1)
    def _():
        run(own_ref)


def by_core(cols):
    return pl.BlockSpec(
        (HALF, 1, BLOCK, cols),
        lambda s, at: (0, jnp.where(s == 0, 1 - at[0] % 2, at[0] % 2), 0, 0),
    )


def by_step(cols):
    return pl.BlockSpec((LOCAL_E, 1, ROWS, cols), lambda s, at: (0, s, 0, 0))


def place_rows(exp_at, own_up, other_up, expert_down, shared_two):
    return pl.pallas_call(
        place_kernel,
        grid_spec=pltpu.PrefetchScalarGridSpec(
            num_scalar_prefetch=1,
            grid=(2,),
            in_specs=[
                whole((HALF, BLOCK, WIDTH + META)),
                whole((HALF, BLOCK, WIDTH + META)),
                whole((LOCAL_E, FF_E, WIDTH)),
                whole((2 * SHARED, WIDTH)),
            ],
            out_specs=[by_core(META), by_step(WIDTH), by_step(FF_E), by_core(META), by_step(META)],
        ),
        out_shape=[
            jax.ShapeDtypeStruct((HALF, 2, BLOCK, META), bf16),
            jax.ShapeDtypeStruct((LOCAL_E, 2, ROWS, WIDTH), bf16),
            jax.ShapeDtypeStruct((LOCAL_E, 2, ROWS, FF_E), f32),
            jax.ShapeDtypeStruct((HALF, 2, BLOCK, META), f32),
            jax.ShapeDtypeStruct((LOCAL_E, 2, ROWS, META), f32),
        ],
        compiler_params=params(56),
        name="place_rows",
    )(exp_at, own_up, other_up, expert_down, shared_two)


def expert_kernel(
    at_ref,
    hid_ref,
    place_ref,
    geh_ref,
    gsh_ref,
    wg_ref,
    wu_ref,
    ws_ref,
    part_ref,
    x_ref,
    act_ref,
    dgu_ref,
    sact_ref,
    sgrad_ref,
):
    for chip in range(HALF):
        rows = dg(place_ref[chip, 0], hid_ref[chip, 0], TN).astype(bf16)
        at = chip * CAP
        for e in range(LOCAL_E):
            x_ref[e, 0, at : at + CAP] = rows[64 * e : 64 * e + CAP]
    pairs = []
    for e in range(LOCAL_E):
        pre_gate = dg(x_ref[e, 0], wg_ref[e], NN)
        pre_up = dg(x_ref[e, 0], wu_ref[e], NN)
        sig = sigmoid(pre_gate)
        act = pre_gate * sig
        act_ref[e, 0] = (act * pre_up).astype(bf16)
        geh = geh_ref[e, 0]
        d_gate = (geh * pre_up * (sig * (1.0 + pre_gate * (1.0 - sig)))).astype(bf16)
        d_up = (geh * act).astype(bf16)
        dgu_ref[e, 0, :, :FF_E] = d_gate
        dgu_ref[e, 0, :, FF_E:] = d_up
        pairs.append((dg(d_gate, wg_ref[e], NT) + dg(d_up, wu_ref[e], NT)).astype(bf16))
    lane = lax.broadcasted_iota(jnp.int32, (BLOCK, 2 * SHARED), 1) < SHARED
    gap = jnp.zeros((64 - CAP, WIDTH), bf16)
    for chip in range(HALF):
        pre = dg(hid_ref[chip, 0], ws_ref[...], NN)
        turned = pltpu.roll(pre, SHARED, 1)
        gate, up = jnp.where(lane, pre, turned), jnp.where(lane, turned, pre)
        sig = sigmoid(gate)
        act = gate * sig
        sact_ref[chip, 0] = jnp.where(lane, act * up, 0.0).astype(bf16)
        slope = sig * (1.0 + gate * (1.0 - sig))
        sgrad = (gsh_ref[chip, 0] * jnp.where(lane, up * slope, act)).astype(bf16)
        sgrad_ref[chip, 0] = sgrad
        at = chip * CAP
        stacked = jnp.concatenate([pairs[0][at : at + CAP], gap, pairs[1][at : at + CAP], gap], 0)
        part_ref[0, chip] = (
            dg(place_ref[chip, 0], stacked, NN) + dg(sgrad, ws_ref[...], NT)
        ).astype(bf16)


def expert_back(exp_at, hidden, place, geh, gsh, wg, wu, ws):
    return pl.pallas_call(
        expert_kernel,
        grid_spec=pltpu.PrefetchScalarGridSpec(
            num_scalar_prefetch=1,
            grid=(2,),
            in_specs=[
                by_core(WIDTH),
                by_core(META),
                by_step(FF_E),
                by_core(META),
                whole((LOCAL_E, WIDTH, FF_E)),
                whole((LOCAL_E, WIDTH, FF_E)),
                whole((WIDTH, 2 * SHARED)),
            ],
            out_specs=[
                pl.BlockSpec((1, HALF, BLOCK, WIDTH), lambda s, at: (s, 0, 0, 0)),
                by_step(WIDTH),
                by_step(FF_E),
                by_step(2 * FF_E),
                by_core(META),
                by_core(META),
            ],
        ),
        out_shape=[
            jax.ShapeDtypeStruct((2, HALF, BLOCK, WIDTH), bf16),
            jax.ShapeDtypeStruct((LOCAL_E, 2, ROWS, WIDTH), bf16),
            jax.ShapeDtypeStruct((LOCAL_E, 2, ROWS, FF_E), bf16),
            jax.ShapeDtypeStruct((LOCAL_E, 2, ROWS, 2 * FF_E), bf16),
            jax.ShapeDtypeStruct((HALF, 2, BLOCK, META), bf16),
            jax.ShapeDtypeStruct((HALF, 2, BLOCK, META), bf16),
        ],
        compiler_params=params(60),
        name="expert_back",
    )(exp_at, hidden, place, geh, gsh, wg, wu, ws)


def output_kernel(at_ref, act_ref, gate_ref, place_ref, sact_ref, wd_ref, sd_ref, part_ref):
    outs = []
    for e in range(LOCAL_E):
        out = dg(act_ref[e, 0], wd_ref[e], NN).astype(bf16).astype(f32)
        outs.append((out * gate_ref[e, 0, :, :1]).astype(bf16))
    gap = jnp.zeros((64 - CAP, WIDTH), bf16)
    for chip in range(HALF):
        at = chip * CAP
        stacked = jnp.concatenate([outs[0][at : at + CAP], gap, outs[1][at : at + CAP], gap], 0)
        part_ref[0, chip] = (
            dg(place_ref[chip, 0], stacked, NN) + dg(sact_ref[chip, 0], sd_ref[...], NN)
        ).astype(bf16)


def expert_output(exp_at, act, gate, place, sact, wd, sd):
    return pl.pallas_call(
        output_kernel,
        grid_spec=pltpu.PrefetchScalarGridSpec(
            num_scalar_prefetch=1,
            grid=(2,),
            in_specs=[
                by_step(FF_E),
                by_step(META),
                by_core(META),
                by_core(META),
                whole((LOCAL_E, FF_E, WIDTH)),
                whole((2 * SHARED, WIDTH)),
            ],
            out_specs=pl.BlockSpec((1, HALF, BLOCK, WIDTH), lambda s, at: (s, 0, 0, 0)),
        ),
        out_shape=jax.ShapeDtypeStruct((2, HALF, BLOCK, WIDTH), bf16),
        compiler_params=params(48),
        name="expert_output",
    )(exp_at, act, gate, place, sact, wd, sd)


def turn_kernel(dq_ref, pieces_ref, ga_ref, gqkv_ref, cols_ref):
    total = pieces_ref[0].astype(f32)
    for i in range(1, N_CTX):
        total = total + pieces_ref[i].astype(f32)
    grad_kv = total.astype(bf16)
    gqkv_ref[:, :WIDTH] = dq_ref[...]
    gqkv_ref[:, WIDTH:] = grad_kv
    turned = jnp.concatenate([dq_ref[...].T, grad_kv.T], axis=0)
    turned_out = ga_ref[...].T
    for j in range(N_EXP):
        cols_ref[j, :160] = turned[160 * j : 160 * j + 160]
        cols_ref[j, 160:] = turned_out[96 * j : 96 * j + 96]


def turn_cols(dq, pieces, grad_attn):
    return pl.pallas_call(
        turn_kernel,
        out_shape=[
            jax.ShapeDtypeStruct((BLOCK, WIDTH + 2 * KV_WIDTH), bf16),
            jax.ShapeDtypeStruct((N_EXP, 256, BLOCK), bf16),
        ],
        compiler_params=params(32),
        name="turn_cols",
    )(dq, pieces, grad_attn)


def input_kernel(gqkv_ref, w_ref, x_ref, gain_ref, gm_ref, out_ref, gg_ref):
    grad_one = dg(gqkv_ref[...], w_ref[...], NT)
    inputs = x_ref[...].astype(f32)
    inv = lax.rsqrt(jnp.mean(inputs * inputs, axis=-1, keepdims=True) + epsilon)
    normed = inputs * inv
    gg_ref[...] = jnp.sum(grad_one * normed, axis=0, keepdims=True)
    out_ref[...] = (gm_ref[...] + norm_back(grad_one * gain_ref[...], normed, inv)).astype(bf16)


def input_back(grad_qkv, w_attn, tokens, gain, grad_middle):
    return pl.pallas_call(
        input_kernel,
        out_shape=[
            jax.ShapeDtypeStruct((BLOCK, WIDTH), bf16),
            jax.ShapeDtypeStruct((1, WIDTH), f32),
        ],
        compiler_params=params(48),
        name="input_back",
    )(grad_qkv, w_attn, tokens, gain, grad_middle)


def cols_kernel(cols_ref, rows_ref, out_ref):
    lhs = jnp.concatenate([cols_ref[j] for j in range(N_EXP)], axis=1)
    row = lax.broadcasted_iota(jnp.int32, (256, N_EXP * BLOCK), 0)
    zero = jnp.zeros_like(lhs)
    attn = dg(jnp.where(row < 160, lhs, zero), rows_ref[:, :WIDTH], NN)
    out = dg(jnp.where(row < 160, zero, lhs), rows_ref[:, WIDTH:], NN)
    out_ref[...] = (attn + out).T.astype(bf16).reshape(N_EXP, 96, 256)


def cols_grad(cols, rows_all):
    return pl.pallas_call(
        cols_kernel,
        out_shape=jax.ShapeDtypeStruct((N_EXP, 96, 256), bf16),
        compiler_params=params(56),
        name="cols_grad",
    )(cols, rows_all)


same_core = [[2 * i + c for i in range(8)] for c in range(2)]
core_swap = [(i, i ^ 1) for i in range(N_EXP)]


def swap_all(rows, axis, groups=None):
    return lax.all_to_all(
        rows, axis, split_axis=0, concat_axis=0, tiled=True, axis_index_groups=groups
    )


def after(value, *others):
    return lax.optimization_barrier((value,) + others)[0]


def add_low(a, b):
    return (a.astype(f32) + b.astype(f32)).astype(bf16)


def on_device(
    tokens,
    routes,
    route_gates,
    norm_attn,
    norm_ffn,
    query_weight,
    key_weight,
    value_weight,
    out_weight,
    shared_gate,
    shared_up,
    shared_down,
    expert_gate,
    expert_up,
    expert_down,
    cotangent,
):
    exp_at = lax.axis_index("exp").astype(jnp.int32)
    ctx_at = lax.axis_index("ctx").astype(jnp.int32)
    chip = exp_at // 2
    exp_s, ctx_s = exp_at.reshape(1), ctx_at.reshape(1)

    heads = [w[:, i * 128 : i * 128 + 128] for i in range(4) for w in (key_weight, value_weight)]
    w_attn = lax.all_gather(
        jnp.concatenate([query_weight] + heads, axis=1), "exp", axis=0, tiled=True
    )
    w_out = lax.all_gather(out_weight, "exp", axis=0, tiled=True)
    gains = jnp.concatenate([norm_attn, norm_ffn])
    gains = swap_all(jnp.broadcast_to(gains, (N_EXP, gains.shape[0])), "exp")
    gain_attn = gains[:, :96].reshape(1, WIDTH).astype(f32)
    gain_ffn = gains[:, 96:].reshape(1, WIDTH).astype(f32)

    gates_high = route_gates[0].astype(bf16)
    gates_low = (route_gates[0] - gates_high.astype(f32)).astype(bf16)
    pad = jnp.zeros((BLOCK, META - 3 * TOPK), bf16)
    up_meta = jnp.concatenate(
        [cotangent[0], routes[0].astype(bf16), gates_high, gates_low, pad], axis=1
    )
    up_pieces = [up_meta] + [
        lax.ppermute(up_meta, "exp", [(i, i ^ (2 * k)) for i in range(N_EXP)]) for k in range(1, 8)
    ]
    shared_cols = jnp.concatenate(
        [shared_gate.reshape(96, N_EXP, SHARED), shared_up.reshape(96, N_EXP, SHARED)], axis=2
    ).transpose(1, 0, 2)
    w_shared = swap_all(shared_cols, "exp").reshape(WIDTH, 2 * SHARED)
    shared_two = jnp.concatenate([shared_down, shared_down], axis=0)

    inputs = tokens[0].astype(f32)
    scale_one = lax.rsqrt(jnp.mean(inputs * inputs, axis=-1, keepdims=True) + epsilon)
    hidden_one = (inputs * scale_one * gain_attn).astype(bf16)
    hidden_one = after(hidden_one, w_shared)
    qkv = dg(hidden_one, w_attn, NN).astype(bf16)
    own_kv = qkv[:, WIDTH:]
    kv_all = swap_all(jnp.broadcast_to(own_kv, (N_CTX,) + own_kv.shape), "ctx")

    up_own = jnp.zeros((HALF,) + up_meta.shape, bf16)
    for k, piece in enumerate(up_pieces):
        up_own = lax.dynamic_update_index_in_dim(up_own, after(piece, own_kv), chip ^ k, 0)
    up_other = lax.ppermute(up_own, "exp", core_swap)

    attended, att_f, logs = attend(ctx_s, qkv, kv_all)
    middle, hidden_two = middle_norm(attended, w_out, tokens[0], gain_ffn)

    hidden_all = lax.all_gather(hidden_two, "exp", axis=0, tiled=True)
    hidden_all = hidden_all.reshape(HALF, 2, BLOCK, WIDTH)
    rows_all = lax.all_gather(
        after(jnp.concatenate([hidden_one, attended], axis=1), hidden_two),
        "exp",
        axis=0,
        tiled=True,
    )
    place, grad_eo, grad_eh, grad_sh, slot_gate = place_rows(
        exp_s, after(up_own, hidden_two), up_other, expert_down, shared_two
    )
    part, arrived, act, grad_gu, shared_act, shared_grad = expert_back(
        exp_s, hidden_all, place, grad_eh, grad_sh, expert_gate, expert_up, w_shared
    )
    summed = add_low(part[1], lax.ppermute(part[0], "exp", core_swap))
    grad_two = swap_all(summed, "exp", same_core)

    rows_e = 2 * ROWS
    act_late = after(act, summed).reshape(LOCAL_E, rows_e, FF_E)
    arrived_late = after(arrived, summed).reshape(LOCAL_E, rows_e, WIDTH)
    shared_grad_late = after(shared_grad, summed).reshape(N_EXP * BLOCK, META)
    grad_scols = dg(hidden_all.reshape(N_EXP * BLOCK, WIDTH), shared_grad_late, TN).astype(bf16)
    grad_scols = swap_all(grad_scols.reshape(N_EXP, 96, META), "exp")
    grad_egu = jnp.einsum(
        "erd,erf->edf",
        arrived_late,
        grad_gu.reshape(LOCAL_E, rows_e, 2 * FF_E),
        preferred_element_type=f32,
    ).astype(bf16)
    grad_edown = jnp.einsum(
        "erf,erd->efd",
        act_late,
        grad_eo.reshape(LOCAL_E, rows_e, WIDTH),
        preferred_element_type=f32,
    ).astype(bf16)
    core = exp_at % 2
    act_pair = shared_act.reshape(HALF, 2, BLOCK, META)
    act_own = lax.dynamic_index_in_dim(act_pair, core, 1, keepdims=False)
    act_other = lax.dynamic_index_in_dim(act_pair, 1 - core, 1, keepdims=False)
    flat = (HALF * BLOCK, -1)
    grad_sdown = (
        dg(act_own.reshape(flat), up_own.reshape(flat), TN)
        + dg(act_other.reshape(flat), up_other.reshape(flat), TN)
    )[:SHARED, :WIDTH].astype(bf16)
    grad_egu, grad_edown, grad_sdown, grad_scols = lax.psum(
        (grad_egu, grad_edown, grad_sdown, grad_scols), "ctx"
    )

    grad_middle, grad_attn, grad_heads, grad_gain_ffn = middle_back(
        grad_two, middle, cotangent[0], gain_ffn, w_out
    )
    grad_query, part_kv = attend_back(ctx_s, qkv, grad_heads, att_f, logs, kv_all)
    kv_pieces = swap_all(part_kv, "ctx")

    out_part = expert_output(
        exp_s, after(act, part_kv), slot_gate, place, shared_act, expert_down, shared_two
    )
    out_sum = add_low(out_part[1], lax.ppermute(out_part[0], "exp", core_swap))

    grad_qkv, cols = turn_cols(grad_query, kv_pieces, grad_attn)
    cols = swap_all(cols, "exp")
    input_grad, grad_gain_attn = input_back(
        grad_qkv, w_attn, tokens[0], gain_attn, grad_middle
    )
    grad_cols = cols_grad(cols, rows_all)
    gain_rows = jnp.concatenate(
        [grad_gain_attn.reshape(N_EXP, 1, 96), grad_gain_ffn.reshape(N_EXP, 1, 96)], axis=1
    ).astype(bf16)
    gain_rows = jnp.pad(gain_rows, ((0, 0), (0, 14), (0, 160)))
    back = swap_all(jnp.concatenate([grad_cols, gain_rows], axis=1), "exp")
    pieces = swap_all(back.reshape(N_CTX, 2, 112, 256), "ctx")
    own = jnp.sum(pieces.astype(f32), axis=0).astype(bf16)
    late = swap_all(jnp.broadcast_to(own, (N_CTX, 2, 112, 256)), "ctx").reshape(N_EXP, 112, 256)

    out_pieces = swap_all(after(out_sum, cols), "exp", same_core)
    mixed = (middle + jnp.sum(out_pieces.astype(f32), axis=0)).astype(bf16)[None]

    grad_wqkv = late[:, :96, :160].transpose(1, 0, 2).reshape(96, WIDTH + 2 * KV_WIDTH)
    grad_wkv = grad_wqkv[:, WIDTH:].reshape(96, KV_HEADS, 2, HEAD_DIM)
    gain_sum = jnp.sum(late[:, 96:98, :96].astype(f32), axis=0)
    return (
        mixed,
        input_grad[None],
        gain_sum[0],
        gain_sum[1],
        grad_wqkv[:, :WIDTH].astype(f32),
        grad_wkv[:, :, 0].reshape(96, KV_WIDTH).astype(f32),
        grad_wkv[:, :, 1].reshape(96, KV_WIDTH).astype(f32),
        late[:, :96, 160:].transpose(1, 0, 2).reshape(96, WIDTH).astype(f32),
        grad_scols[:, :, :SHARED].transpose(1, 0, 2).reshape(96, 1024).astype(f32),
        grad_scols[:, :, SHARED:].transpose(1, 0, 2).reshape(96, 1024).astype(f32),
        grad_sdown.astype(f32),
        grad_egu[:, :, :FF_E].astype(f32),
        grad_egu[:, :, FF_E:].astype(f32),
        grad_edown.astype(f32),
    )


def solution(mesh):
    token_spec = P("exp", "ctx", None)
    rows = P("exp", None)
    expert = P("exp", None, None)
    placed = (token_spec,) * 3 + (P("exp"),) * 2 + (rows,) * 7 + (expert,) * 3 + (token_spec,)
    return jax.shard_map(
        on_device,
        mesh=mesh,
        in_specs=placed,
        out_specs=(token_spec,) * 2 + (P("exp"),) * 2 + (rows,) * 7 + (expert,) * 3,
        check_vma=False,
    )
```

time: 834 us -> 737 us (0.88)
  matrix products: 138 us -> 26.5 us
  local copies, waits for them, and re-layouts: 162 us -> 51 us
  blocking collectives: 0 us -> 95.5 us
  Pallas kernels: 0 us -> 89.5 us
  other arithmetic: 87 us -> 38.5 us
  waiting for transfers between devices: 289 us -> 275 us
    dot_general x32 -> x6, matrix products: 138 us -> 26.5 us  [the longest x4 12.3 us: dg(): return lax.dot_general(a, b, dims, preferred_element_type=f32)]
    all_to_all x0 -> x2, blocking collectives: none -> 95.5 us  [swap_all(): lax.all_to_all(rows, axis, split_axis=0, concat_axis=0, tiled=True, axis_...]
    pallas_call x0 -> x10, Pallas kernels: none -> 89.5 us  [the longest x1 28.6 us: expert_back(): pl.pallas_call(expert_kernel, grid_spec=pltpu.PrefetchScalarGridSpec(num_...]
    all_to_all x18 -> x9, starting transfers between devices: 84.6 us -> 127 us  [swap_all(): lax.all_to_all(rows, axis, split_axis=0, concat_axis=0, tiled=True, axis_...]
    ppermute x22 -> x10, starting transfers between devices: 47 us -> 10.8 us  [the longest x7 10.1 us: on_device(): lax.ppermute(up_meta, 'exp', [(i, i ^ 2 * k) for i in range(N_EXP)])]
    reshape x11 -> x2, local copies, waits for them, and re-layouts: 34.9 us -> 0.18 us  [the longest x1 0.09 us: on_device(): grad_gain_ffn.reshape(N_EXP, 1, 96)]
    all_gather x4 -> x2, waiting for transfers between devices: 59.6 us -> 26.6 us  [the longest x1 26.6 us: on_device(): lax.all_gather(jnp.concatenate([query_weight] + heads, axis=1), 'exp', ax...]
    ppermute x22 -> x10, waiting for transfers between devices: 37 us -> 67.3 us  [the longest x7 55.1 us: on_device(): lax.ppermute(up_meta, 'exp', [(i, i ^ 2 * k) for i in range(N_EXP)])]
  transfers between devices with their start and end apart: 46 -> 24, of which waited for: 23 -> 17; matrix products, arithmetic and copies ran while one was open for 44% -> 12% of each run, Pallas kernels for 0% -> 12%
where the time goes in v2:
time: 737 us; the launch traced here: 728 us
  waiting for transfers between devices  275 us (37%)
  starting transfers between devices  138 us (19%)
  blocking collectives  95.5 us (13%)
  Pallas kernels  89.5 us (12%)
  local copies, waits for them, and re-layouts  51 us (7%)
  other arithmetic  38.5 us (5%)
  matrix products  26.5 us (4%)
  between operations  14.7 us (2%)
    all_to_all x9, waiting for transfers between devices, swap_all(): lax.all_to_all(rows, axis, split_axis=0, concat_axis=0, tiled=True, axis_...  172 us
    all_to_all x9, starting transfers between devices, swap_all(): lax.all_to_all(rows, axis, split_axis=0, concat_axis=0, tiled=True, axis_...  127 us
    all_to_all x2, blocking collectives, swap_all(): lax.all_to_all(rows, axis, split_axis=0, concat_axis=0, tiled=True, axis_...  95.5 us
    ppermute x7, waiting for transfers between devices, on_device(): lax.ppermute(up_meta, 'exp', [(i, i ^ 2 * k) for i in range(N_EXP)])  55.1 us
    pallas_call x1, Pallas kernels, expert_back(): pl.pallas_call(expert_kernel, grid_spec=pltpu.PrefetchScalarGridSpec(num_...  28.6 us
    unnamed x119, local copies, waits for them, and re-layouts  28.3 us
    all_gather x1, waiting for transfers between devices, on_device(): lax.all_gather(jnp.concatenate([query_weight] + heads, axis=1), 'exp', ax...  26.6 us
    pallas_call x1, Pallas kernels, place_rows(): pl.pallas_call(place_kernel, grid_spec=pltpu.PrefetchScalarGridSpec(num_s...  14.8 us
  transfers between devices with their start and end apart: 24, of which 17 were waited for; matrix products, arithmetic and copies ran while one was open for 12% of the time, Pallas kernels for 12%

profile of v2, /device:TPU:0, one launch (start us, length us, event | category | flops | bytes accessed | tf_op | source)
XLA Modules:
  0.0 728.3 jit_solution(14939576308078181571)
XLA Ops:
  17.2 5.8 all-to-all-start
  29.1 4.1 all-to-all-start.1
  33.6 11.4 %all-to-all-done.1 = bf16[16,96,128]{2,1,0:T(8,128)(2,1)S(1)} async-done(((bf16[16,96,128]{2,1,0:T(8,128)(2,1)}), bf16[16,96,128]{2,1,0:T(8,128)(2,1)S(1)}, u32[]{:S(2)}, u32[]{:S(2)}) %all-to-all-start.1) | async-done | bytes 393248 | tf_op jit(solution)/shard_map/all_to_all | solution.py:499
  45.0 26.6 %all-gather.5.cloned.1.call-done.w_ref = bf16[1536,2560]{1,0:T(8,128)(2,1)} async-done(((bf16[96,2560]{1,0:T(8,128)(2,1)}), bf16[1536,2560]{1,0:T(8,128)(2,1)}) %all-gather.5.cloned.1.call-update) | async-done | bytes 7864336 | tf_op jit(solution)/shard_map/all_gather | solution.py:536
  71.6 4.4 convolution_convert_fusion.2.q_ref
  77.7 6.7 all-to-all-start.2
  84.5 32.8 %all-to-all-done.2.k_ref.v_ref = bf16[8,128,1024]{2,1,0:T(8,128)(2,1)S(1)} async-done(((bf16[8,128,1024]{2,1,0:T(8,128)(2,1)}), bf16[8,128,1024]{2,1,0:T(8,128)(2,1)S(1)}, u32[]{:S(2)}, u32[]{:S(2)}) %all-to-all-start.2) | async-done | bytes 2097184 | tf_op jit(solution)/shard_map/all_to_all | solution.py:499
  117.3 5.9 attend.1
  125.9 7.8 %all-gather.7.cloned.1.call-done.w_ref = bf16[1536,1536]{1,0:T(8,128)(2,1)} async-done(((bf16[96,1536]{1,0:T(8,128)(2,1)}), bf16[1536,1536]{1,0:T(8,128)(2,1)}) %all-gather.7.cloned.1.call-update) | async-done | bytes 4718608 | tf_op jit(solution)/shard_map/all_gather | solution.py:539
  133.7 2.3 copy-done.1
  150.0 8.4 %collective-permute-done = bf16[128,1664]{1,0:T(8,128)(2,1)S(1)} collective-permute-done((bf16[128,1664]{1,0:T(8,128)(2,1)S(1)}, bf16[128,1664]{1,0:T(8,128)(2,1)S(1)}, u32[]{:S(2)}, u32[]{:S(2)}) %collective-permute-start) | collective-permute-done | bytes 426016 | tf_op jit(solution)/shard_map/ppermute | solution.py:552
  158.6 3.0 collective-permute-done.1
  163.6 16.0 %collective-permute-done.2 = bf16[128,1664]{1,0:T(8,128)(2,1)S(1)} collective-permute-done((bf16[128,1664]{1,0:T(8,128)(2,1)S(1)}, bf16[128,1664]{1,0:T(8,128)(2,1)S(1)}, u32[]{:S(2)}, u32[]{:S(2)}) %collective-permute-start.2) | collective-permute-done | bytes 426016 | tf_op jit(solution)/shard_map/ppermute | solution.py:552
  179.6 15.6 %collective-permute-done.3 = bf16[128,1664]{1,0:T(8,128)(2,1)S(1)} collective-permute-done((bf16[128,1664]{1,0:T(8,128)(2,1)S(1)}, bf16[128,1664]{1,0:T(8,128)(2,1)S(1)}, u32[]{:S(2)}, u32[]{:S(2)}) %collective-permute-start.3) | collective-permute-done | bytes 426016 | tf_op jit(solution)/shard_map/ppermute | solution.py:552
  195.2 12.1 %collective-permute-done.4 = bf16[128,1664]{1,0:T(8,128)(2,1)S(1)} collective-permute-done((bf16[128,1664]{1,0:T(8,128)(2,1)S(1)}, bf16[128,1664]{1,0:T(8,128)(2,1)S(1)}, u32[]{:S(2)}, u32[]{:S(2)}) %collective-permute-start.4) | collective-permute-done | bytes 426016 | tf_op jit(solution)/shard_map/ppermute | solution.py:552
  210.6 6.4 collective-permute-done.7.other_ref
  218.7 14.8 %place_rows.1 = (bf16[8,2,128,128]{3,2,1,0:T(8,128)(2,1)}, bf16[2,2,384,1536]{3,2,1,0:T(8,128)(2,1)}, f32[2,2,384,512]{3,2,1,0:T(8,128)}, f32[8,2,128,128]{3,2,1,0:T(8,128)}, f32[2,2,384,128]{3,2,1,0:T(8,128)}) custom-call(s32[1]{0:T(128)} %bitcast.6.at_ref, bf16[8,128,1664]{2,1,0:T(8,128)(2,1)} %copy-done.27, bf16[8,128,1664]{2,1,0:T(8,128)(2,1)} %copy-done.29, ...), custom_call_target="tpu_custom_call" | custom-call | tf_op jit(solution)/shard_map/place_rows/pallas_call | solution.py:278
  233.5 28.6 %expert_back.1 = (bf16[2,8,128,1536]{3,2,1,0:T(8,128)(2,1)}, bf16[2,2,384,1536]{3,2,1,0:T(8,128)(2,1)}, bf16[2,2,384,512]{3,2,1,0:T(8,128)(2,1)}, bf16[2,2,384,1...) custom-call(s32[1]{0:T(128)} %bitcast.6.at_ref, ...), custom_call_target="tpu_custom_call" | custom-call | tf_op jit(solution)/shard_map/expert_back/pallas_call | solution.py:357
  262.1 4.0 slice_bitcast_fusion.2
  266.3 5.8 collective-permute-done.8
  272.1 5.5 fusion.1
  277.7 2.6 convolution_convert_fusion.3
  280.3 8.5 %all-to-all-start.10 = ((bf16[16,96,128]{2,1,0:T(8,128)(2,1)}), bf16[16,96,128]{2,1,0:T(8,128)(2,1)S(1)}, u32[]{:S(2)}, u32[]{:S(2)}) async-start(bf16[16,96,128]{2,1,0:T(8,128)(2,1)} %bitcast.127), calls=%async_computation.10 | async-start | bytes 786432 | tf_op jit(solution)/shard_map/all_to_all | solution.py:499
  288.7 3.7 fusion.16
  294.0 4.8 all-to-all-done.10
  299.6 3.6 all-to-all-start.3
  305.3 7.2 convolution_convert_fusion.1
  312.6 7.0 convolution_convert_fusion
  319.6 34.2 %all-to-all-done.3.pieces_ref = bf16[8,128,1536]{2,1,0:T(8,128)(2,1)S(1)} async-done(((bf16[8,128,1536]{2,1,0:T(8,128)(2,1)}), bf16[8,128,1536]{2,1,0:T(8,128)(2,1)S(1)}, u32[]{:S(2)}, u32[]{:S(2)}) %all-to-all-start.3) | async-done | bytes 3145760 | tf_op jit(solution)/shard_map/all_to_all | solution.py:499
  355.9 4.8 middle_back.1
  361.6 7.1 attend_back.1
  368.8 9.8 %expert_output.1 = bf16[2,8,128,1536]{3,2,1,0:T(8,128)(2,1)} custom-call(s32[1]{0:T(128)} %bitcast.6.at_ref, bf16[2,2,384,512]{3,2,1,0:T(8,128)(2,1)S(1)} %copy-done.15, f32[2,2,384,128]{3,2,1,0:T(8,128)S(1)} %copy-done.19, bf16[8,2,128,128]{3,2,1,0:T(8,128)(2,1)S(1)} %copy-done.10, bf16[8,2,128,128]{3,2,1,0:T(8,128)(2,1)S(1)} %copy-done.12, ...), custom_call_target="tpu_custom_call" | custom-call | tf_op jit(solution)/shard_map/expert_output/pallas_call | solution.py:408
  378.6 3.8 slice_bitcast_fusion
  382.4 77.4 %all_to_all.59.pieces_ref = bf16[8,128,1024]{2,1,0:T(8,128)(2,1)S(1)} all-to-all(bf16[8,128,1024]{2,1,0:T(8,128)(2,1)S(1)} %get-tuple-element.77), channel_id=1, replica_groups=mesh['ctx'=8,'exp'=16] {'ctx'}, dimensions={0} | all-to-all | bytes 4194304 | tf_op jit(solution)/shard_map/all_to_all | solution.py:499
  461.2 63.0 %all-to-all-start.5 = ((bf16[16,256,128]{2,1,0:T(8,128)(2,1)}), bf16[16,256,128]{2,1,0:T(8,128)(2,1)S(1)}, u32[]{:S(2)}, u32[]{:S(2)}) async-start(bf16[16,256,128]{2,1,0:T(8,128)(2,1)} %get-tuple-element.83), calls=%async_computation.5 | async-start | bytes 2097152 | tf_op jit(solution)/shard_map/all_to_all | solution.py:499
  524.3 5.5 fusion
  529.8 47.1 %all-to-all-done.5.cols_ref = bf16[16,256,128]{2,1,0:T(8,128)(2,1)S(1)} async-done(((bf16[16,256,128]{2,1,0:T(8,128)(2,1)}), bf16[16,256,128]{2,1,0:T(8,128)(2,1)S(1)}, u32[]{:S(2)}, u32[]{:S(2)}) %all-to-all-start.5) | async-done | bytes 1048608 | tf_op jit(solution)/shard_map/all_to_all | solution.py:499
  576.9 26.9 %all-to-all-start.6 = ((bf16[8,128,1536]{2,1,0:T(8,128)(2,1)}), bf16[8,128,1536]{2,1,0:T(8,128)(2,1)}, u32[]{:S(2)}, u32[]{:S(2)}) async-start(bf16[8,128,1536]{2,1,0:T(8,128)(2,1)} %fusion), calls=%async_computation.6 | async-start | bytes 6291456 | tf_op jit(solution)/shard_map/all_to_all | solution.py:499
  604.0 6.8 input_back.1
  611.0 9.3 %cols_grad.1 = bf16[16,96,256]{2,1,0:T(8,128)(2,1)} custom-call(bf16[16,256,128]{2,1,0:T(8,128)(2,1)} %copy-done.31, bf16[2048,3072]{1,0:T(8,128)(2,1)} %all-gather.11.cloned.1.call-done.rows_ref), custom_call_target="tpu_custom_call" | custom-call | tf_op jit(solution)/shard_map/cols_grad/pallas_call | solution.py:486
  621.5 28.1 %all-to-all-done.6 = bf16[8,128,1536]{2,1,0:T(8,128)(2,1)} async-done(((bf16[8,128,1536]{2,1,0:T(8,128)(2,1)}), bf16[8,128,1536]{2,1,0:T(8,128)(2,1)}, u32[]{:S(2)}, u32[]{:S(2)}) %all-to-all-start.6) | async-done | bytes 3145760 | tf_op jit(solution)/shard_map/all_to_all | solution.py:499
  649.6 18.1 %all_to_all.60 = bf16[16,112,256]{2,1,0:T(8,128)(2,1)} all-to-all(bf16[16,112,256]{2,1,0:T(8,128)(2,1)S(1)} %pad_maximum_fusion), channel_id=1, replica_groups=mesh['ctx'=8,'exp'=16] {'exp'}, dimensions={0} | all-to-all | bytes 1835008 | tf_op jit(solution)/shard_map/all_to_all | solution.py:499
  667.7 4.4 all-to-all-start.8
  672.2 2.4 convert_reduce_fusion
  675.4 12.4 %all-to-all-done.8 = bf16[8,2,112,256]{3,2,1,0:T(8,128)(2,1)S(1)} async-done(((bf16[8,2,112,256]{3,2,1,0:T(8,128)(2,1)}), bf16[8,2,112,256]{3,2,1,0:T(8,128)(2,1)S(1)}, u32[]{:S(2)}, u32[]{:S(2)}) %all-to-all-start.8) | async-done | bytes 917536 | tf_op jit(solution)/shard_map/all_to_all | solution.py:499
  689.0 3.6 all-to-all-start.9
  701.1 5.6 convert_element_type.185
  706.7 6.5 slice_convert_fusion
  (209 shorter events, 71.2 us)
Async XLA Ops:
  7.2 26.2 %copy-start.4 = (bf16[1,128,1536]{2,1,0:T(8,128)(2,1)S(1)}, bf16[1,128,1536]{2,1,0:T(8,128)(2,1)}, u32[]{:S(2)}) copy-start(bf16[1,128,1536]{2,1,0:T(8,128)(2,1)} %param.16) | copy-start | bytes 1179652
  7.2 64.4 %all-gather.5.cloned.1.call-start = ((), (), s32[]{:S(2)}) async-start(), calls=%async_computation.11 | async-start | bytes 8355840 | tf_op jit(solution)/shard_map/all_gather | solution.py:536
  15.1 118.7 %all-gather.7.cloned.1.call-start = ((), (), s32[]{:S(2)}) async-start(), calls=%async_computation.12 | async-start | bytes 5013504 | tf_op jit(solution)/shard_map/all_gather | solution.py:539
  17.2 11.9 %all-to-all-start = ((bf16[16,1,192]{2,1,0:T(2,128)(2,1)}), bf16[16,1,192]{2,1,0:T(2,128)(2,1)S(1)}, u32[]{:S(2)}, u32[]{:S(2)}) async-start(bf16[16,1,192]{2,1,0:T(2,128)(2,1)} %broadcast_in_dim.47), calls=%async_computation | async-start | bytes 32768 | tf_op jit(solution)/shard_map/all_to_all | solution.py:499
  29.1 15.9 %all-to-all-start.1 = ((bf16[16,96,128]{2,1,0:T(8,128)(2,1)}), bf16[16,96,128]{2,1,0:T(8,128)(2,1)S(1)}, u32[]{:S(2)}, u32[]{:S(2)}) async-start(bf16[16,96,128]{2,1,0:T(8,128)(2,1)} %copy.113), calls=%async_computation.1 | async-start | bytes 786432 | tf_op jit(solution)/shard_map/all_to_all | solution.py:499
  33.3 42.7 %copy-start.37 = (f32[16,96]{1,0:T(8,128)}, f32[16,96]{1,0:T(8,128)S(1)}, u32[]{:S(2)}) copy-start(f32[16,96]{1,0:T(8,128)S(1)} %get-tuple-element.185) | copy-start | bytes 18436
  33.6 42.5 %copy-start.30 = (bf16[128,1536]{1,0:T(8,128)(2,1)}, bf16[128,1536]{1,0:T(8,128)(2,1)S(1)}, u32[]{:S(2)}) copy-start(bf16[128,1536]{1,0:T(8,128)(2,1)S(1)} %fusion.4) | copy-start | bytes 1179652
  45.0 31.0 %copy-start.33 = (bf16[16,96,128]{2,1,0:T(8,128)(2,1)}, bf16[16,96,128]{2,1,0:T(8,128)(2,1)S(1)}, u32[]{:S(2)}) copy-start(bf16[16,96,128]{2,1,0:T(8,128)(2,1)S(1)} %all-to-all-done.1) | copy-start | bytes 1179652
  76.1 41.3 %copy-start.2 = (bf16[128,2560]{1,0:T(8,128)(2,1)}, bf16[128,2560]{1,0:T(8,128)(2,1)S(1)}, u32[]{:S(2)}) copy-start(bf16[128,2560]{1,0:T(8,128)(2,1)S(1)} %convolution_convert_fusion.2.q_ref) | copy-start | bytes 1966084
  77.7 39.6 %all-to-all-start.2 = ((bf16[8,128,1024]{2,1,0:T(8,128)(2,1)}), bf16[8,128,1024]{2,1,0:T(8,128)(2,1)S(1)}, u32[]{:S(2)}, u32[]{:S(2)}) async-start(bf16[8,128,1024]{2,1,0:T(8,128)(2,1)} %broadcast_in_dim.48), calls=%async_computation.2 | async-start | bytes 4194304 | tf_op jit(solution)/shard_map/all_to_all | solution.py:499
  84.4 149.1 %all-gather.9.cloned.1.call-start = ((), (), s32[]{:S(2)}) async-start(), calls=%async_computation.13 | async-start | bytes 6684672 | tf_op jit(solution)/shard_map/all_gather | solution.py:576
  117.3 20.6 %copy-start = (bf16[8,128,1024]{2,1,0:T(8,128)(2,1)}, bf16[8,128,1024]{2,1,0:T(8,128)(2,1)S(1)}, u32[]{:S(2)}) copy-start(bf16[8,128,1024]{2,1,0:T(8,128)(2,1)S(1)} %all-to-all-done.2.k_ref.v_ref) | copy-start | bytes 6291460
  139.6 471.4 %all-gather.11.cloned.1.call-start = ((), (), s32[]{:S(2)}) async-start(), calls=%async_computation.14 | async-start | bytes 13369344 | tf_op jit(solution)/shard_map/all_gather | solution.py:578
  142.2 16.3 %collective-permute-start = (bf16[128,1664]{1,0:T(8,128)(2,1)S(1)}, bf16[128,1664]{1,0:T(8,128)(2,1)S(1)}, u32[]{:S(2)}, u32[]{:S(2)}) collective-permute-start(bf16[128,1664]{1,0:T(8,128)(2,1)S(1)} %concatenate.28), channel_id=1, source_target_pairs={{0,2},{1,3},{2,0},{3,1},{4,6},{5,7},{6,4},{7,5},{8,10},{9,11},{10,... | collective-permute-start | bytes 1277960 | tf_op jit(solution)/shard_map/ppermute | solution.py:552
  143.6 18.0 %collective-permute-start.1 = (bf16[128,1664]{1,0:T(8,128)(2,1)S(1)}, bf16[128,1664]{1,0:T(8,128)(2,1)S(1)}, u32[]{:S(2)}, u32[]{:S(2)}) collective-permute-start(bf16[128,1664]{1,0:T(8,128)(2,1)S(1)} %concatenate.28), channel_id=1, source_target_pairs={{0,4},{1,5},{2,6},{3,7},{4,0},{5,1},{6,2},{7,3},{8,12},{9,13},{10,... | collective-permute-start | bytes 1277960 | tf_op jit(solution)/shard_map/ppermute | solution.py:552
  145.0 34.6 %collective-permute-start.2 = (bf16[128,1664]{1,0:T(8,128)(2,1)S(1)}, bf16[128,1664]{1,0:T(8,128)(2,1)S(1)}, u32[]{:S(2)}, u32[]{:S(2)}) collective-permute-start(bf16[128,1664]{1,0:T(8,128)(2,1)S(1)} %concatenate.28), channel_id=1, source_target_pairs={{0,6},{1,7},{2,4},{3,5},{4,2},{5,3},{6,0},{7,1},{8,14},{9,15},{10,... | collective-permute-start | bytes 1277960 | tf_op jit(solution)/shard_map/ppermute | solution.py:552
  145.7 49.5 %collective-permute-start.3 = (bf16[128,1664]{1,0:T(8,128)(2,1)S(1)}, bf16[128,1664]{1,0:T(8,128)(2,1)S(1)}, u32[]{:S(2)}, u32[]{:S(2)}) collective-permute-start(bf16[128,1664]{1,0:T(8,128)(2,1)S(1)} %concatenate.28), channel_id=1, source_target_pairs={{0,8},{1,9},{2,10},{3,11},{4,12},{5,13},{6,14},{7,15},{8,0},{9,1},... | collective-permute-start | bytes 1277960 | tf_op jit(solution)/shard_map/ppermute | solution.py:552
  147.7 59.6 %collective-permute-start.4 = (bf16[128,1664]{1,0:T(8,128)(2,1)S(1)}, bf16[128,1664]{1,0:T(8,128)(2,1)S(1)}, u32[]{:S(2)}, u32[]{:S(2)}) collective-permute-start(bf16[128,1664]{1,0:T(8,128)(2,1)S(1)} %concatenate.28), channel_id=1, source_target_pairs={{0,10},{1,11},{2,8},{3,9},{4,14},{5,15},{6,12},{7,13},{8,2},{9,3},... | collective-permute-start | bytes 1277960 | tf_op jit(solution)/shard_map/ppermute | solution.py:552
  158.5 48.8 %collective-permute-start.5 = (bf16[128,1664]{1,0:T(8,128)(2,1)S(1)}, bf16[128,1664]{1,0:T(8,128)(2,1)}, u32[]{:S(2)}, u32[]{:S(2)}) collective-permute-start(bf16[128,1664]{1,0:T(8,128)(2,1)S(1)} %concatenate.28), channel_id=1, source_target_pairs={{0,12},{1,13},{2,14},{3,15},{4,8},{5,9},{6,10},{7,11},{8,4},{9,5},... | collective-permute-start | bytes 1277960 | tf_op jit(solution)/shard_map/ppermute | solution.py:552
  161.6 45.7 %collective-permute-start.6 = (bf16[128,1664]{1,0:T(8,128)(2,1)S(1)}, bf16[128,1664]{1,0:T(8,128)(2,1)}, u32[]{:S(2)}, u32[]{:S(2)}) collective-permute-start(bf16[128,1664]{1,0:T(8,128)(2,1)S(1)} %concatenate.28), channel_id=1, source_target_pairs={{0,14},{1,15},{2,12},{3,13},{4,10},{5,11},{6,8},{7,9},{8,6},{9,7},... | collective-permute-start | bytes 1277960 | tf_op jit(solution)/shard_map/ppermute | solution.py:552
  210.0 7.0 copy-start.27
  210.0 7.0 collective-permute-start.7
  262.1 15.6 %slice-start = ((s8[6291456]{0:T(1024)(128)(4,1)}), s8[2097152]{0:T(1024)(128)(4,1)S(1)}, s32[]{:S(2)}) async-start(s8[6291456]{0:T(1024)(128)(4,1)} %bitcast.108), calls=%async_computation.16 | async-start | bytes 4194304
  266.1 6.1 collective-permute-start.8
  266.3 11.4 %slice-start.1 = ((s8[6291456]{0:T(1024)(128)(4,1)}), s8[4194304]{0:T(1024)(128)(4,1)S(1)}, s32[]{:S(2)}) async-start(s8[6291456]{0:T(1024)(128)(4,1)} %bitcast.108), calls=%async_computation.17 | async-start | bytes 8388608
  266.3 11.4 %copy-start.42 = (bf16[8,2,128,128]{3,2,1,0:T(8,128)(2,1)S(1)}, bf16[8,2,128,128]{3,2,1,0:T(8,128)(2,1)}, u32[]{:S(2)}) copy-start(bf16[8,2,128,128]{3,2,1,0:T(8,128)(2,1)} %get-tuple-element.92) | copy-start | bytes 1572868
  280.3 18.6 %all-to-all-start.10 = ((bf16[16,96,128]{2,1,0:T(8,128)(2,1)}), bf16[16,96,128]{2,1,0:T(8,128)(2,1)S(1)}, u32[]{:S(2)}, u32[]{:S(2)}) async-start(bf16[16,96,128]{2,1,0:T(8,128)(2,1)} %bitcast.127), calls=%async_computation.10 | async-start | bytes 786432 | tf_op jit(solution)/shard_map/all_to_all | solution.py:499
  299.6 54.2 %all-to-all-start.3 = ((bf16[8,128,1536]{2,1,0:T(8,128)(2,1)}), bf16[8,128,1536]{2,1,0:T(8,128)(2,1)S(1)}, u32[]{:S(2)}, u32[]{:S(2)}) async-start(bf16[8,128,1536]{2,1,0:T(8,128)(2,1)} %fusion.1), calls=%async_computation.3 | async-start | bytes 6291456 | tf_op jit(solution)/shard_map/all_to_all | solution.py:499
  303.3 389.3 %all-reduce.4.cloned.1.call-start = ((), (), s32[]{:S(2)}) async-start(), calls=%async_computation.15 | async-start | bytes 20054016 | tf_op jit(solution)/shard_map/psum | solution.py:620
  303.3 9.2 %slice-start.4 = ((s8[4718592]{0:T(1024)(128)(4,1)}), s8[4194304]{0:T(1024)(128)(4,1)S(1)}, s32[]{:S(2)}) async-start(s8[4718592]{0:T(1024)(128)(4,1)} %bitcast.130), calls=%async_computation.20 | async-start | bytes 8388608
  305.3 7.2 slice-start.5
  305.3 7.2 copy-start.41
  361.6 7.2 copy-start.9
  361.6 7.2 copy-start.10
  361.6 7.2 copy-start.12
  361.6 7.2 copy-start.15
  361.6 7.2 copy-start.19
  382.4 141.9 %collective-permute-start.9 = (bf16[8,128,1536]{2,1,0:T(8,128)(2,1)}, bf16[8,128,1536]{2,1,0:T(8,128)(2,1)}, u32[]{:S(2)}, u32[]{:S(2)}) collective-permute-start(bf16[8,128,1536]{2,1,0:T(8,128)(2,1)} %slice_bitcast_fusion), channel_id=1, source_target_pairs={{0,1},{1,0},{2,3},{3,2},{4,5},{5,4},{6,7},{7,6},{8,9},{9,8},{10,11... | collective-permute-start | bytes 9437192 | tf_op jit(solution)/shard_map/ppermute | solution.py:633
  461.2 115.7 %all-to-all-start.5 = ((bf16[16,256,128]{2,1,0:T(8,128)(2,1)}), bf16[16,256,128]{2,1,0:T(8,128)(2,1)S(1)}, u32[]{:S(2)}, u32[]{:S(2)}) async-start(bf16[16,256,128]{2,1,0:T(8,128)(2,1)} %get-tuple-element.83), calls=%async_computation.5 | async-start | bytes 2097152 | tf_op jit(solution)/shard_map/all_to_all | solution.py:499
  529.8 74.0 %copy-start.38 = (f32[16,96]{1,0:T(8,128)S(1)}, f32[16,96]{1,0:T(8,128)}, u32[]{:S(2)}) copy-start(f32[16,96]{1,0:T(8,128)} %copy-done.37) | copy-start | bytes 18436
  529.8 74.3 %copy-start.21 = (f32[128,1536]{1,0:T(8,128)S(1)}, f32[128,1536]{1,0:T(8,128)}, u32[]{:S(2)}) copy-start(f32[128,1536]{1,0:T(8,128)} %copy-done.20) | copy-start | bytes 2359300
  576.9 34.0 %copy-start.31 = (bf16[16,256,128]{2,1,0:T(8,128)(2,1)}, bf16[16,256,128]{2,1,0:T(8,128)(2,1)S(1)}, u32[]{:S(2)}) copy-start(bf16[16,256,128]{2,1,0:T(8,128)(2,1)S(1)} %all-to-all-done.5.cols_ref) | copy-start | bytes 3145732
  576.9 72.7 %all-to-all-start.6 = ((bf16[8,128,1536]{2,1,0:T(8,128)(2,1)}), bf16[8,128,1536]{2,1,0:T(8,128)(2,1)}, u32[]{:S(2)}, u32[]{:S(2)}) async-start(bf16[8,128,1536]{2,1,0:T(8,128)(2,1)} %fusion), calls=%async_computation.6 | async-start | bytes 6291456 | tf_op jit(solution)/shard_map/all_to_all | solution.py:499
  621.5 53.0 %copy-start.7 = (f32[128,1536]{1,0:T(8,128)S(1)}, f32[128,1536]{1,0:T(8,128)}, u32[]{:S(2)}) copy-start(f32[128,1536]{1,0:T(8,128)} %copy-done.5) | copy-start | bytes 2359300
  667.7 20.1 %all-to-all-start.8 = ((bf16[8,2,112,256]{3,2,1,0:T(8,128)(2,1)}), bf16[8,2,112,256]{3,2,1,0:T(8,128)(2,1)S(1)}, u32[]{:S(2)}, u32[]{:S(2)}) async-start(bf16[8,2,112,256]{3,2,1,0:T(8,128)(2,1)} %bitcast.25), calls=%async_computation.8 | async-start | bytes 1835008 | tf_op jit(solution)/shard_map/all_to_all | solution.py:499
  689.0 24.3 %all-to-all-start.9 = ((bf16[8,2,112,256]{3,2,1,0:T(8,128)(2,1)}), bf16[8,2,112,256]{3,2,1,0:T(8,128)(2,1)S(1)}, u32[]{:S(2)}, u32[]{:S(2)}) async-start(bf16[8,2,112,256]{3,2,1,0:T(8,128)(2,1)} %broadcast_in_dim.61), calls=%async_computation.9 | async-start | bytes 1835008 | tf_op jit(solution)/shard_map/all_to_all | solution.py:499
  692.6 7.8 %copy-start.36 = (bf16[64,1536]{1,0:T(8,128)(2,1)S(1)}, bf16[64,1536]{1,0:T(8,128)(2,1)}, u32[]{:S(2)}) copy-start(bf16[64,1536]{1,0:T(8,128)(2,1)} %get-tuple-element.171) | copy-start | bytes 589828
  696.0 10.7 %slice-start.2 = ((s8[6291456]{0:T(1024)(128)(4,1)}), s8[2097152]{0:T(1024)(128)(4,1)S(1)}, s32[]{:S(2)}) async-start(s8[6291456]{0:T(1024)(128)(4,1)} %bitcast.110), calls=%async_computation.18 | async-start | bytes 4194304
  (25 other events, 70.7 us)
Sparse Core Ops, SparseCore 0:
  15.2 56.4 all-gather.4
  73.3 60.3 all-gather.6
  139.8 78.9 all-gather.8
  220.3 76.4 all-gather.10
  319.7 256.5 all-reduce.3

commit v3 on v2

--- a/solution.py
+++ b/solution.py
@@ -82,8 +82,8 @@
 
 def kv_specs():
     return [
-        pl.BlockSpec((N_CTX, BLOCK, HEAD_DIM), lambda g: (0, 0, 2 * g)),
-        pl.BlockSpec((N_CTX, BLOCK, HEAD_DIM), lambda g: (0, 0, 2 * g + 1)),
+        pl.BlockSpec((N_CTX, BLOCK, HEAD_DIM), lambda g: (0, 0, g)),
+        pl.BlockSpec((N_CTX, BLOCK, HEAD_DIM), lambda g: (0, 0, KV_HEADS + g)),
     ]
 
 
@@ -161,16 +161,28 @@
     hidden_ref[...] = (middle * inv * gain_ref[...]).astype(bf16)
 
 
-def middle_norm(attended, w_out, tokens, gain):
+def w_cols(width, at):
+    return pl.BlockSpec((WIDTH, width), lambda *_: (0, at), pipeline_mode=pl.Buffered(1))
+
+
+def middle_norm(attended, w_all, tokens, gain):
     return pl.pallas_call(
         middle_kernel,
+        grid=(1,),
+        in_specs=[
+            whole((BLOCK, WIDTH)),
+            w_cols(WIDTH, 1),
+            whole((BLOCK, WIDTH)),
+            whole((1, WIDTH)),
+        ],
+        out_specs=[whole((BLOCK, WIDTH)), whole((BLOCK, WIDTH))],
         out_shape=[
             jax.ShapeDtypeStruct((BLOCK, WIDTH), f32),
             jax.ShapeDtypeStruct((BLOCK, WIDTH), bf16),
         ],
         compiler_params=params(32),
         name="middle_norm",
-    )(attended, w_out, tokens, gain)
+    )(attended, w_all, tokens, gain)
 
 
 def norm_back(grad_normed, normed, inv_root):
@@ -196,9 +208,18 @@
     gh_ref[...] = dg(grad_attn, w_ref[...], NT).astype(bf16)
 
 
-def middle_back(pieces, middle, upstream, gain, w_out):
+def middle_back(pieces, middle, upstream, gain, w_all):
     return pl.pallas_call(
         middle_back_kernel,
+        grid=(1,),
+        in_specs=[
+            whole((HALF, BLOCK, WIDTH)),
+            whole((BLOCK, WIDTH)),
+            whole((BLOCK, WIDTH)),
+            whole((1, WIDTH)),
+            w_cols(WIDTH, 1),
+        ],
+        out_specs=[whole((BLOCK, WIDTH))] * 3 + [whole((1, WIDTH))],
         out_shape=[
             jax.ShapeDtypeStruct((BLOCK, WIDTH), f32),
             jax.ShapeDtypeStruct((BLOCK, WIDTH), bf16),
@@ -207,7 +228,7 @@
         ],
         compiler_params=params(48),
         name="middle_back",
-    )(pieces, middle, upstream, gain, w_out)
+    )(pieces, middle, upstream, gain, w_all)
 
 
 def place_kernel(
@@ -430,7 +451,9 @@
     total = pieces_ref[0].astype(f32)
     for i in range(1, N_CTX):
         total = total + pieces_ref[i].astype(f32)
-    grad_kv = total.astype(bf16)
+    total = total.astype(bf16)
+    parts = [total[:, i * HEAD_DIM : (i + 1) * HEAD_DIM] for i in range(2 * KV_HEADS)]
+    grad_kv = jnp.concatenate(parts[0::2] + parts[1::2], axis=1)
     gqkv_ref[:, :WIDTH] = dq_ref[...]
     gqkv_ref[:, WIDTH:] = grad_kv
     turned = jnp.concatenate([dq_ref[...].T, grad_kv.T], axis=0)
@@ -452,8 +475,8 @@
     )(dq, pieces, grad_attn)
 
 
-def input_kernel(gqkv_ref, w_ref, x_ref, gain_ref, gm_ref, out_ref, gg_ref):
-    grad_one = dg(gqkv_ref[...], w_ref[...], NT)
+def input_kernel(gqkv_ref, wq_ref, wkv_ref, x_ref, gain_ref, gm_ref, out_ref, gg_ref):
+    grad_one = dg(gqkv_ref[:, :WIDTH], wq_ref[...], NT) + dg(gqkv_ref[:, WIDTH:], wkv_ref[...], NT)
     inputs = x_ref[...].astype(f32)
     inv = lax.rsqrt(jnp.mean(inputs * inputs, axis=-1, keepdims=True) + epsilon)
     normed = inputs * inv
@@ -461,16 +484,26 @@
     out_ref[...] = (gm_ref[...] + norm_back(grad_one * gain_ref[...], normed, inv)).astype(bf16)
 
 
-def input_back(grad_qkv, w_attn, tokens, gain, grad_middle):
+def input_back(grad_qkv, w_all, tokens, gain, grad_middle):
     return pl.pallas_call(
         input_kernel,
+        grid=(1,),
+        in_specs=[
+            whole((BLOCK, WIDTH + 2 * KV_WIDTH)),
+            w_cols(WIDTH, 0),
+            w_cols(2 * KV_WIDTH, 3),
+            whole((BLOCK, WIDTH)),
+            whole((1, WIDTH)),
+            whole((BLOCK, WIDTH)),
+        ],
+        out_specs=[whole((BLOCK, WIDTH)), whole((1, WIDTH))],
         out_shape=[
             jax.ShapeDtypeStruct((BLOCK, WIDTH), bf16),
             jax.ShapeDtypeStruct((1, WIDTH), f32),
         ],
         compiler_params=params(48),
         name="input_back",
-    )(grad_qkv, w_attn, tokens, gain, grad_middle)
+    )(grad_qkv, w_all, w_all, tokens, gain, grad_middle)
 
 
 def cols_kernel(cols_ref, rows_ref, out_ref):
@@ -489,6 +522,162 @@
         compiler_params=params(56),
         name="cols_grad",
     )(cols, rows_all)
+
+
+def norm_rows_kernel(x_ref, gain_ref, out_ref):
+    inputs = x_ref[0].astype(f32)
+    inv = lax.rsqrt(jnp.mean(inputs * inputs, axis=-1, keepdims=True) + epsilon)
+    out_ref[0] = (inputs * inv * gain_ref[...]).astype(bf16)
+
+
+def norm_rows(rows, gain):
+    count = rows.shape[0]
+    spec = pl.BlockSpec((1, BLOCK, WIDTH), lambda i: (i, 0, 0))
+    return pl.pallas_call(
+        norm_rows_kernel,
+        grid=(count,),
+        in_specs=[spec, whole((1, WIDTH))],
+        out_specs=spec,
+        out_shape=jax.ShapeDtypeStruct(rows.shape, bf16),
+        compiler_params=params(32),
+        name="norm_rows",
+    )(rows, gain)
+
+
+def project_kernel(own_ref, seq_ref, w_ref, q_ref, kv_ref):
+    step = pl.program_id(0)
+
+    @pl.when(step < 3)
+    def _():
+        q_ref[...] = dg(own_ref[0], w_ref[...], NN).astype(bf16)
+
+    @pl.when(step >= 3)
+    def _():
+        rows = seq_ref[...].reshape(N_CTX * BLOCK, WIDTH)
+        kv_ref[...] = dg(rows, w_ref[...], NN).astype(bf16).reshape(N_CTX, BLOCK, KV_WIDTH)
+
+
+def project(own, seq, w_all):
+    return pl.pallas_call(
+        project_kernel,
+        grid=(5,),
+        in_specs=[
+            whole((1, BLOCK, WIDTH)),
+            whole((N_CTX, BLOCK, WIDTH)),
+            pl.BlockSpec((WIDTH, KV_WIDTH), lambda i: (0, jnp.where(i < 3, i, i + 3))),
+        ],
+        out_specs=[
+            pl.BlockSpec((BLOCK, KV_WIDTH), lambda i: (0, jnp.minimum(i, 2))),
+            pl.BlockSpec((N_CTX, BLOCK, KV_WIDTH), lambda i: (0, 0, jnp.maximum(i - 3, 0))),
+        ],
+        out_shape=[
+            jax.ShapeDtypeStruct((BLOCK, WIDTH), bf16),
+            jax.ShapeDtypeStruct((N_CTX, BLOCK, 2 * KV_WIDTH), bf16),
+        ],
+        compiler_params=params(48),
+        name="project",
+    )(own, seq, w_all)
+
+
+PIECE = 2 * WIDTH + WIDTH * BLOCK // HEAD_DIM
+
+
+def expert_weights_kernel(at_ref, x_ref, geo_ref, act_ref, dgate_ref, dup_ref, *refs):
+    outs, turned = refs[:8], refs[8]
+    step = pl.program_id(0)
+
+    @pl.when(step == 0)
+    def _():
+        for e in range(LOCAL_E):
+            turned[e] = x_ref[e].T
+
+    for r in range(4):
+
+        @pl.when(step == r)
+        def _():
+            for side in range(2):
+                e = at_ref[1] if side == 0 else 1 - at_ref[1]
+                out = outs[2 * r + side]
+                rhs = jnp.concatenate([dgate_ref[e], dup_ref[e]], axis=1)
+                both = dg(turned[e], rhs, NN).astype(bf16)
+                out[:WIDTH] = both[:, :HEAD_DIM]
+                out[WIDTH : 2 * WIDTH] = both[:, HEAD_DIM:]
+                down = dg(act_ref[e], geo_ref[e], TN).astype(bf16)
+                for m in range(WIDTH // HEAD_DIM):
+                    at = 2 * WIDTH + m * BLOCK
+                    out[at : at + BLOCK] = down[:, m * HEAD_DIM : (m + 1) * HEAD_DIM]
+
+
+def expert_weights(at, arrived, grad_eo, act, grad_gu):
+    rows = 2 * ROWS
+    lanes = lambda shift: pl.BlockSpec(
+        (LOCAL_E, rows, HEAD_DIM), lambda r, at: (0, 0, shift + (at[0] ^ r))
+    )
+    piece = jax.ShapeDtypeStruct((PIECE, HEAD_DIM), bf16)
+    return pl.pallas_call(
+        expert_weights_kernel,
+        grid_spec=pltpu.PrefetchScalarGridSpec(
+            num_scalar_prefetch=1,
+            grid=(4,),
+            in_specs=[
+                whole((LOCAL_E, rows, WIDTH)),
+                whole((LOCAL_E, rows, WIDTH)),
+                lanes(0),
+                lanes(0),
+                lanes(4),
+            ],
+            out_specs=[whole((PIECE, HEAD_DIM))] * 8,
+            scratch_shapes=[pltpu.VMEM((LOCAL_E, WIDTH, rows), bf16)],
+        ),
+        out_shape=[piece] * 8,
+        compiler_params=params(56),
+        name="expert_weights",
+    )(at, arrived, grad_eo, act, grad_gu, grad_gu)
+
+
+def unpack_kernel(at_ref, *refs):
+    pieces, (gate_ref, up_ref, down_ref) = refs[:8], refs[8:]
+    step = pl.program_id(0)
+    for i in range(8):
+
+        @pl.when(step == i)
+        def _():
+            piece = pieces[i]
+            gate_ref[0] = piece[:WIDTH].astype(f32)
+            up_ref[0] = piece[WIDTH : 2 * WIDTH].astype(f32)
+            for m in range(WIDTH // HEAD_DIM):
+                at = 2 * WIDTH + m * BLOCK
+                down_ref[0, :, m * HEAD_DIM : (m + 1) * HEAD_DIM] = piece[at : at + BLOCK].astype(
+                    f32
+                )
+
+
+def unpack_experts(at, pieces):
+    cols = pl.BlockSpec(
+        (1, WIDTH, HEAD_DIM), lambda s, at: (at[1] ^ (s // 4), 0, at[0] ^ (s % 4))
+    )
+    return pl.pallas_call(
+        unpack_kernel,
+        grid_spec=pltpu.PrefetchScalarGridSpec(
+            num_scalar_prefetch=1,
+            grid=(8,),
+            in_specs=[whole((PIECE, HEAD_DIM))] * 8,
+            out_specs=[
+                cols,
+                cols,
+                pl.BlockSpec(
+                    (1, BLOCK, WIDTH), lambda s, at: (at[1] ^ (s // 4), at[0] ^ (s % 4), 0)
+                ),
+            ],
+        ),
+        out_shape=[
+            jax.ShapeDtypeStruct((LOCAL_E, WIDTH, FF_E), f32),
+            jax.ShapeDtypeStruct((LOCAL_E, WIDTH, FF_E), f32),
+            jax.ShapeDtypeStruct((LOCAL_E, FF_E, WIDTH), f32),
+        ],
+        compiler_params=params(48),
+        name="unpack_experts",
+    )(at, *pieces)
 
 
 same_core = [[2 * i + c for i in range(8)] for c in range(2)]
@@ -532,16 +721,15 @@
     chip = exp_at // 2
     exp_s, ctx_s = exp_at.reshape(1), ctx_at.reshape(1)
 
-    heads = [w[:, i * 128 : i * 128 + 128] for i in range(4) for w in (key_weight, value_weight)]
-    w_attn = lax.all_gather(
-        jnp.concatenate([query_weight] + heads, axis=1), "exp", axis=0, tiled=True
-    )
-    w_out = lax.all_gather(out_weight, "exp", axis=0, tiled=True)
-    gains = jnp.concatenate([norm_attn, norm_ffn])
-    gains = swap_all(jnp.broadcast_to(gains, (N_EXP, gains.shape[0])), "exp")
-    gain_attn = gains[:, :96].reshape(1, WIDTH).astype(f32)
-    gain_ffn = gains[:, 96:].reshape(1, WIDTH).astype(f32)
-
+    y_at, z_at = ctx_at % 4, ctx_at // 4
+    yz_s = jnp.stack([y_at, z_at])
+
+    w_all = lax.all_gather(
+        jnp.concatenate([query_weight, out_weight, key_weight, value_weight], axis=1),
+        "exp",
+        axis=0,
+        tiled=True,
+    )
     gates_high = route_gates[0].astype(bf16)
     gates_low = (route_gates[0] - gates_high.astype(f32)).astype(bf16)
     pad = jnp.zeros((BLOCK, META - 3 * TOPK), bf16)
@@ -551,32 +739,32 @@
     up_pieces = [up_meta] + [
         lax.ppermute(up_meta, "exp", [(i, i ^ (2 * k)) for i in range(N_EXP)]) for k in range(1, 8)
     ]
+    gains = jnp.concatenate([norm_attn, norm_ffn])
+    gains = swap_all(jnp.broadcast_to(gains, (N_EXP, gains.shape[0])), "exp")
+    gain_attn = gains[:, :96].reshape(1, WIDTH).astype(f32)
+    gain_ffn = gains[:, 96:].reshape(1, WIDTH).astype(f32)
+    tokens_seq = swap_all(jnp.broadcast_to(tokens, (N_CTX, BLOCK, WIDTH)), "ctx")
     shared_cols = jnp.concatenate(
         [shared_gate.reshape(96, N_EXP, SHARED), shared_up.reshape(96, N_EXP, SHARED)], axis=2
     ).transpose(1, 0, 2)
     w_shared = swap_all(shared_cols, "exp").reshape(WIDTH, 2 * SHARED)
     shared_two = jnp.concatenate([shared_down, shared_down], axis=0)
-
-    inputs = tokens[0].astype(f32)
-    scale_one = lax.rsqrt(jnp.mean(inputs * inputs, axis=-1, keepdims=True) + epsilon)
-    hidden_one = (inputs * scale_one * gain_attn).astype(bf16)
-    hidden_one = after(hidden_one, w_shared)
-    qkv = dg(hidden_one, w_attn, NN).astype(bf16)
-    own_kv = qkv[:, WIDTH:]
-    kv_all = swap_all(jnp.broadcast_to(own_kv, (N_CTX,) + own_kv.shape), "ctx")
-
     up_own = jnp.zeros((HALF,) + up_meta.shape, bf16)
     for k, piece in enumerate(up_pieces):
-        up_own = lax.dynamic_update_index_in_dim(up_own, after(piece, own_kv), chip ^ k, 0)
+        up_own = lax.dynamic_update_index_in_dim(up_own, piece, chip ^ k, 0)
     up_other = lax.ppermute(up_own, "exp", core_swap)
 
-    attended, att_f, logs = attend(ctx_s, qkv, kv_all)
-    middle, hidden_two = middle_norm(attended, w_out, tokens[0], gain_ffn)
+    hidden_one = norm_rows(tokens, gain_attn)
+    hidden_seq = norm_rows(tokens_seq, gain_attn)
+    hidden_seq = after(hidden_seq, w_shared, up_own)
+    queries, kv_all = project(hidden_one, hidden_seq, w_all)
+    attended, att_f, logs = attend(ctx_s, queries, kv_all)
+    middle, hidden_two = middle_norm(attended, w_all, tokens[0], gain_ffn)
 
     hidden_all = lax.all_gather(hidden_two, "exp", axis=0, tiled=True)
     hidden_all = hidden_all.reshape(HALF, 2, BLOCK, WIDTH)
     rows_all = lax.all_gather(
-        after(jnp.concatenate([hidden_one, attended], axis=1), hidden_two),
+        after(jnp.concatenate([hidden_one[0], attended], axis=1), hidden_two),
         "exp",
         axis=0,
         tiled=True,
@@ -591,25 +779,24 @@
     grad_two = swap_all(summed, "exp", same_core)
 
     rows_e = 2 * ROWS
-    act_late = after(act, summed).reshape(LOCAL_E, rows_e, FF_E)
-    arrived_late = after(arrived, summed).reshape(LOCAL_E, rows_e, WIDTH)
-    shared_grad_late = after(shared_grad, summed).reshape(N_EXP * BLOCK, META)
+    p = expert_weights(
+        yz_s,
+        after(arrived, summed).reshape(LOCAL_E, rows_e, WIDTH),
+        grad_eo.reshape(LOCAL_E, rows_e, WIDTH),
+        act.reshape(LOCAL_E, rows_e, FF_E),
+        grad_gu.reshape(LOCAL_E, rows_e, 2 * FF_E),
+    )
+
+    def to(rows, k):
+        return lax.ppermute(rows, "ctx", [(i, i ^ k) for i in range(N_CTX)])
+
+    relay_a, relay_b = to(p[4], 1), to(p[5], 3)
+    got_10, got_31 = to(p[2], 1), to(p[7], 3)
+
+    shared_grad_late = after(shared_grad, p[0]).reshape(N_EXP * BLOCK, META)
     grad_scols = dg(hidden_all.reshape(N_EXP * BLOCK, WIDTH), shared_grad_late, TN).astype(bf16)
-    grad_scols = swap_all(grad_scols.reshape(N_EXP, 96, META), "exp")
-    grad_egu = jnp.einsum(
-        "erd,erf->edf",
-        arrived_late,
-        grad_gu.reshape(LOCAL_E, rows_e, 2 * FF_E),
-        preferred_element_type=f32,
-    ).astype(bf16)
-    grad_edown = jnp.einsum(
-        "erf,erd->efd",
-        act_late,
-        grad_eo.reshape(LOCAL_E, rows_e, WIDTH),
-        preferred_element_type=f32,
-    ).astype(bf16)
     core = exp_at % 2
-    act_pair = shared_act.reshape(HALF, 2, BLOCK, META)
+    act_pair = after(shared_act, p[0])
     act_own = lax.dynamic_index_in_dim(act_pair, core, 1, keepdims=False)
     act_other = lax.dynamic_index_in_dim(act_pair, 1 - core, 1, keepdims=False)
     flat = (HALF * BLOCK, -1)
@@ -617,57 +804,87 @@
         dg(act_own.reshape(flat), up_own.reshape(flat), TN)
         + dg(act_other.reshape(flat), up_other.reshape(flat), TN)
     )[:SHARED, :WIDTH].astype(bf16)
-    grad_egu, grad_edown, grad_sdown, grad_scols = lax.psum(
-        (grad_egu, grad_edown, grad_sdown, grad_scols), "ctx"
+    out_part = expert_output(
+        exp_s, after(act, p[0]), slot_gate, place, shared_act, expert_down, shared_two
     )
 
     grad_middle, grad_attn, grad_heads, grad_gain_ffn = middle_back(
-        grad_two, middle, cotangent[0], gain_ffn, w_out
-    )
-    grad_query, part_kv = attend_back(ctx_s, qkv, grad_heads, att_f, logs, kv_all)
+        grad_two, middle, cotangent[0], gain_ffn, w_all
+    )
+    grad_query, part_kv = attend_back(ctx_s, queries, grad_heads, att_f, logs, kv_all)
     kv_pieces = swap_all(part_kv, "ctx")
 
-    out_part = expert_output(
-        exp_s, after(act, part_kv), slot_gate, place, shared_act, expert_down, shared_two
-    )
-    out_sum = add_low(out_part[1], lax.ppermute(out_part[0], "exp", core_swap))
+    relay_a, relay_b = after((relay_a, relay_b), part_kv)
+    got_11, got_30 = to(add_low(p[3], relay_b), 1), to(add_low(p[6], relay_a), 3)
+    out_other = lax.ppermute(after(out_part[0], part_kv), "exp", core_swap)
+    out_sum = add_low(out_part[1], out_other)
 
     grad_qkv, cols = turn_cols(grad_query, kv_pieces, grad_attn)
+    cols_sent = cols
     cols = swap_all(cols, "exp")
+    got_11, got_30, out_sum = after((got_11, got_30, out_sum), cols_sent)
+    out_pieces = swap_all(out_sum, "exp", same_core)
+    across = to(
+        (p[1].astype(f32) + got_11.astype(f32) + got_31.astype(f32)).astype(bf16), 4
+    )
     input_grad, grad_gain_attn = input_back(
-        grad_qkv, w_attn, tokens[0], gain_attn, grad_middle
+        grad_qkv, w_all, tokens[0], gain_attn, grad_middle
     )
     grad_cols = cols_grad(cols, rows_all)
     gain_rows = jnp.concatenate(
         [grad_gain_attn.reshape(N_EXP, 1, 96), grad_gain_ffn.reshape(N_EXP, 1, 96)], axis=1
     ).astype(bf16)
     gain_rows = jnp.pad(gain_rows, ((0, 0), (0, 14), (0, 160)))
-    back = swap_all(jnp.concatenate([grad_cols, gain_rows], axis=1), "exp")
-    pieces = swap_all(back.reshape(N_CTX, 2, 112, 256), "ctx")
-    own = jnp.sum(pieces.astype(f32), axis=0).astype(bf16)
-    late = swap_all(jnp.broadcast_to(own, (N_CTX, 2, 112, 256)), "ctx").reshape(N_EXP, 112, 256)
-
-    out_pieces = swap_all(after(out_sum, cols), "exp", same_core)
+    sent = jnp.concatenate(
+        [
+            jnp.concatenate([grad_cols, gain_rows], axis=1),
+            jnp.pad(grad_scols.reshape(N_EXP, 96, META), ((0, 0), (0, 16), (0, 0))),
+        ],
+        axis=2,
+    )
+    back = swap_all(sent, "exp")
+
+    own = (
+        p[0].astype(f32)
+        + got_10.astype(f32)
+        + got_30.astype(f32)
+        + after(across, sent).astype(f32)
+    ).astype(bf16)
+    at_1, at_3, at_z = to(own, 1), to(own, 3), to(own, 4)
+
+    small = jnp.concatenate(
+        [back.reshape(N_CTX, 224, 384), grad_sdown.reshape(N_CTX, 32, 384)], axis=1
+    )
+    pieces = swap_all(small, "ctx")
+    late_own = jnp.sum(pieces.astype(f32), axis=0).astype(bf16)
+    at_2 = to(after(at_3, small), 1)
+    at_z1, at_z3 = to(after(at_z, small), 1), to(after(at_z, small), 3)
+    late = swap_all(jnp.broadcast_to(late_own, (N_CTX, 256, 384)), "ctx")
+    at_z2 = to(after(at_z1, late_own), 3)
+    grad_sdown = late[:, 224:].reshape(SHARED, WIDTH).astype(f32)
+    late = late[:, :224].reshape(N_EXP, 112, 384)
+
     mixed = (middle + jnp.sum(out_pieces.astype(f32), axis=0)).astype(bf16)[None]
-
     grad_wqkv = late[:, :96, :160].transpose(1, 0, 2).reshape(96, WIDTH + 2 * KV_WIDTH)
-    grad_wkv = grad_wqkv[:, WIDTH:].reshape(96, KV_HEADS, 2, HEAD_DIM)
     gain_sum = jnp.sum(late[:, 96:98, :96].astype(f32), axis=0)
+    grad_egate, grad_eup, grad_edown = unpack_experts(
+        yz_s, (own, at_1, at_2, at_3, at_z, at_z1, at_z2, at_z3)
+    )
     return (
         mixed,
         input_grad[None],
         gain_sum[0],
         gain_sum[1],
         grad_wqkv[:, :WIDTH].astype(f32),
-        grad_wkv[:, :, 0].reshape(96, KV_WIDTH).astype(f32),
-        grad_wkv[:, :, 1].reshape(96, KV_WIDTH).astype(f32),
-        late[:, :96, 160:].transpose(1, 0, 2).reshape(96, WIDTH).astype(f32),
-        grad_scols[:, :, :SHARED].transpose(1, 0, 2).reshape(96, 1024).astype(f32),
-        grad_scols[:, :, SHARED:].transpose(1, 0, 2).reshape(96, 1024).astype(f32),
-        grad_sdown.astype(f32),
-        grad_egu[:, :, :FF_E].astype(f32),
-        grad_egu[:, :, FF_E:].astype(f32),
-        grad_edown.astype(f32),
+        grad_wqkv[:, WIDTH : WIDTH + KV_WIDTH].astype(f32),
+        grad_wqkv[:, WIDTH + KV_WIDTH :].astype(f32),
+        late[:, :96, 160:256].transpose(1, 0, 2).reshape(96, WIDTH).astype(f32),
+        late[:, :96, 256 : 256 + SHARED].transpose(1, 0, 2).reshape(96, 1024).astype(f32),
+        late[:, :96, 256 + SHARED :].transpose(1, 0, 2).reshape(96, 1024).astype(f32),
+        grad_sdown,
+        grad_egate,
+        grad_eup,
+        grad_edown,
     )
 
 

time: 737 us -> 721 us (0.978)
  blocking collectives: 95.5 us -> 0 us
  waiting for transfers between devices: 275 us -> 364 us
  starting transfers between devices: 138 us -> 90.1 us
  Pallas kernels: 89.5 us -> 129 us
  matrix products: 26.5 us -> 7.94 us
  local copies, waits for them, and re-layouts: 51 us -> 65.9 us
    ppermute x1 -> x15, waiting for transfers between devices: 0.01 us -> 187 us  [the longest x14 187 us: to(): return lax.ppermute(rows, 'ctx', [(i, i ^ k) for i in range(N_CTX)])]
    all_to_all x2 -> x0, blocking collectives: 95.5 us -> none  [swap_all(): lax.all_to_all(rows, axis, split_axis=0, concat_axis=0, tiled=True, axis_...]
    all_to_all x9 -> x10, starting transfers between devices: 127 us -> 52.9 us  [swap_all(): lax.all_to_all(rows, axis, split_axis=0, concat_axis=0, tiled=True, axis_...]
    ppermute x7, waiting for transfers between devices: 55.1 us -> 1.51 us  [on_device(): lax.ppermute(up_meta, 'exp', [(i, i ^ 2 * k) for i in range(N_EXP)])]
    pallas_call x3 -> x8, Pallas kernels: 12.5 us -> 51.2 us  [the longest x1 18.4 us: expert_weights(): pl.pallas_call(expert_weights_kernel, grid_spec=pltpu.PrefetchScalarGridS...]
    all_gather x3 -> x2, waiting for transfers between devices: 34.4 us -> 0.01 us  [the longest x1 0.01 us: on_device(): lax.all_gather(jnp.concatenate([query_weight, out_weight, key_weight, val...]
    ppermute x1 -> x15, starting transfers between devices: 0.01 us -> 24.3 us  [the longest x14 24.3 us: to(): return lax.ppermute(rows, 'ctx', [(i, i ^ k) for i in range(N_CTX)])]
    all_to_all x9 -> x10, waiting for transfers between devices: 172 us -> 149 us  [swap_all(): lax.all_to_all(rows, axis, split_axis=0, concat_axis=0, tiled=True, axis_...]
  transfers between devices with their start and end apart: 24 -> 37, of which waited for: 17 -> 16; matrix products, arithmetic and copies ran while one was open for 12% -> 9% of each run, Pallas kernels for 12% -> 16%
where the time goes in v3:
time: 721 us; the launch traced here: 710 us
  waiting for transfers between devices  364 us (50%)
  Pallas kernels  129 us (18%)
  starting transfers between devices  90.1 us (12%)
  local copies, waits for them, and re-layouts  65.9 us (9%)
  other arithmetic  38.6 us (5%)
  between operations  14.7 us (2%)
  matrix products  7.94 us (1%)
    ppermute x14, waiting for transfers between devices, to(): return lax.ppermute(rows, 'ctx', [(i, i ^ k) for i in range(N_CTX)])  187 us
    all_to_all x10, waiting for transfers between devices, swap_all(): lax.all_to_all(rows, axis, split_axis=0, concat_axis=0, tiled=True, axis_...  149 us
    all_to_all x10, starting transfers between devices, swap_all(): lax.all_to_all(rows, axis, split_axis=0, concat_axis=0, tiled=True, axis_...  52.9 us
    unnamed x131, local copies, waits for them, and re-layouts  32 us
    pallas_call x1, Pallas kernels, expert_back(): pl.pallas_call(expert_kernel, grid_spec=pltpu.PrefetchScalarGridSpec(num_...  28.9 us
    ppermute x14, starting transfers between devices, to(): return lax.ppermute(rows, 'ctx', [(i, i ^ k) for i in range(N_CTX)])  24.3 us
    pallas_call x1, Pallas kernels, expert_weights(): pl.pallas_call(expert_weights_kernel, grid_spec=pltpu.PrefetchScalarGridS...  18.4 us
    pallas_call x1, Pallas kernels, place_rows(): pl.pallas_call(place_kernel, grid_spec=pltpu.PrefetchScalarGridSpec(num_s...  15 us
  transfers between devices with their start and end apart: 37, of which 16 were waited for; matrix products, arithmetic and copies ran while one was open for 9% of the time, Pallas kernels for 16%

profile of v3, /device:TPU:0, one launch (start us, length us, event | category | flops | bytes accessed | tf_op | source)
XLA Modules:
  0.0 709.9 jit_solution(14434064616190376377)
XLA Ops:
  14.1 3.1 collective-permute-start.3
  19.8 4.4 all-to-all-start
  29.5 53.9 %all-to-all-done = bf16[16,1,192]{2,1,0:T(2,128)(2,1)S(1)} async-done(((bf16[16,1,192]{2,1,0:T(2,128)(2,1)}), bf16[16,1,192]{2,1,0:T(2,128)(2,1)S(1)}, u32[]{:S(2)}, u32[]{:S(2)}) %all-to-all-start) | async-done | bytes 6176 | tf_op jit(solution)/shard_map/all_to_all | solution.py:688
  85.4 8.1 %all-to-all-start.1 = ((bf16[8,128,1536]{2,1,0:T(8,128)(2,1)}), bf16[8,128,1536]{2,1,0:T(8,128)(2,1)S(1)}, u32[]{:S(2)}, u32[]{:S(2)}) async-start(bf16[8,128,1536]{2,1,0:T(8,128)(2,1)} %broadcast_in_dim.52), calls=%async_computation.1 | async-start | bytes 6291456 | tf_op jit(solution)/shard_map/all_to_all | solution.py:688
  99.1 3.1 collective-permute-start.6
  111.7 37.8 %all-to-all-done.1.x_ref = bf16[8,128,1536]{2,1,0:T(8,128)(2,1)S(1)} async-done(((bf16[8,128,1536]{2,1,0:T(8,128)(2,1)}), bf16[8,128,1536]{2,1,0:T(8,128)(2,1)S(1)}, u32[]{:S(2)}, u32[]{:S(2)}) %all-to-all-start.1) | async-done | bytes 3145760 | tf_op jit(solution)/shard_map/all_to_all | solution.py:688
  149.5 4.2 all-to-all-start.2
  158.9 4.1 all-to-all-done.2
  165.9 7.6 %project.1 = (bf16[128,1536]{1,0:T(8,128)(2,1)S(1)}, bf16[8,128,1024]{2,1,0:T(8,128)(2,1)S(1)}) custom-call(bf16[1,128,1536]{2,1,0:T(8,128)(2,1)S(1)} %copy-done.7, bf16[8,128,1536]{2,1,0:T(8,128)(2,1)S(1)} %copy-done.3, bf16[1536,4096]{1,0:T(8,128)(2,1)} %all-gather.4.cloned.1.call-done.w_ref.wq_ref.wkv_ref), custom_call_target="tpu_custom_call" | custom-call | tf_op jit(solution)/shard_map/project/pallas_call | solution.py:561
  173.6 5.8 attend.1
  179.4 5.1 copy-done
  188.7 6.2 collective-permute-done.7.other_ref
  196.6 15.0 %place_rows.1 = (bf16[8,2,128,128]{3,2,1,0:T(8,128)(2,1)}, bf16[2,2,384,1536]{3,2,1,0:T(8,128)(2,1)}, f32[2,2,384,512]{3,2,1,0:T(8,128)}, f32[8,2,128,128]{3,2,1,0:T(8,128)}, f32[2,2,384,128]{3,2,1,0:T(8,128)}) custom-call(s32[1]{0:T(128)} %bitcast.19.at_ref, bf16[8,128,1664]{2,1,0:T(8,128)(2,1)} %bitcast_dynamic-update-slice_fusion.own_ref, ...), custom_call_target="tpu_custom_call" | custom-call | tf_op jit(solution)/shard_map/place_rows/pallas_call | solution.py:299
  211.6 14.4 %all-gather.6.cloned.1.call-done = bf16[2048,1536]{1,0:T(8,128)(2,1)} async-done(((bf16[128,1536]{1,0:T(8,128)(2,1)}), bf16[2048,1536]{1,0:T(8,128)(2,1)}) %all-gather.6.cloned.1.call-update) | async-done | bytes 6291472 | tf_op jit(solution)/shard_map/all_gather | solution.py:764
  226.0 28.9 %expert_back.1 = (bf16[2,8,128,1536]{3,2,1,0:T(8,128)(2,1)}, bf16[2,2,384,1536]{3,2,1,0:T(8,128)(2,1)}, bf16[2,2,384,512]{3,2,1,0:T(8,128)(2,1)}, bf16[2,2,384,1...) custom-call(s32[1]{0:T(128)} %bitcast.19.at_ref, ...), custom_call_target="tpu_custom_call" | custom-call | tf_op jit(solution)/shard_map/expert_back/pallas_call | solution.py:378
  257.6 5.5 collective-permute-done.8
  263.0 2.6 fusion.1
  265.6 5.0 all-to-all-start.3
  271.3 18.4 %expert_weights.1 = (bf16[4608,128]{1,0:T(8,128)(2,1)}, bf16[4608,128]{1,0:T(8,128)(2,1)}, bf16[4608,128]{1,0:T(8,128)(2,1)}, bf16[4608,128]{1,0:T(8,128)(2,1)},...) custom-call(s32[2]{0:T(128)} %pad_add_fusion.at_ref, ...), custom_call_target="tpu_custom_call" | custom-call | tf_op jit(solution)/shard_map/expert_weights/pallas_call | solution.py:617
  289.7 2.7 collective-permute-start.10
  293.8 41.7 %all-to-all-done.3.pieces_ref = bf16[8,128,1536]{2,1,0:T(8,128)(2,1)S(1)} async-done(((bf16[8,128,1536]{2,1,0:T(8,128)(2,1)}), bf16[8,128,1536]{2,1,0:T(8,128)(2,1)S(1)}, u32[]{:S(2)}, u32[]{:S(2)}) %all-to-all-start.3) | async-done | bytes 3145760 | tf_op jit(solution)/shard_map/all_to_all | solution.py:688
  337.6 4.8 middle_back.1
  344.1 7.1 attend_back.1
  353.2 7.0 all-to-all-start.4
  360.3 3.7 fusion.13
  366.3 10.1 %expert_output.1 = bf16[2,8,128,1536]{3,2,1,0:T(8,128)(2,1)} custom-call(s32[1]{0:T(128)} %bitcast.19.at_ref, bf16[2,2,384,512]{3,2,1,0:T(8,128)(2,1)S(1)} %copy-done.4, f32[2,2,384,128]{3,2,1,0:T(8,128)S(1)} %copy-done.23, bf16[8,2,128,128]{3,2,1,0:T(8,128)(2,1)S(1)} %copy-done.14, bf16[8,2,128,128]{3,2,1,0:T(8,128)(2,1)S(1)} %copy-done.15, ...), custom_call_target="tpu_custom_call" | custom-call | tf_op jit(solution)/shard_map/expert_output/pallas_call | solution.py:429
  376.4 2.6 convolution_convert_fusion
  381.1 7.5 %all-to-all-done.4.pieces_ref = bf16[8,128,1024]{2,1,0:T(8,128)(2,1)S(1)} async-done(((bf16[8,128,1024]{2,1,0:T(8,128)(2,1)}), bf16[8,128,1024]{2,1,0:T(8,128)(2,1)S(1)}, u32[]{:S(2)}, u32[]{:S(2)}) %all-to-all-start.4) | async-done | bytes 2097184 | tf_op jit(solution)/shard_map/all_to_all | solution.py:688
  391.1 3.8 all-to-all-start.6
  394.9 3.0 add_convert_fusion.2
  400.0 6.9 input_back.1
  407.1 4.2 all-to-all-done.6.cols_ref
  412.3 9.3 %cols_grad.1 = bf16[16,96,256]{2,1,0:T(8,128)(2,1)} custom-call(bf16[16,256,128]{2,1,0:T(8,128)(2,1)} %copy-done.40, bf16[2048,3072]{1,0:T(8,128)(2,1)} %all-gather.8.cloned.1.call-done.rows_ref), custom_call_target="tpu_custom_call" | custom-call | tf_op jit(solution)/shard_map/cols_grad/pallas_call | solution.py:519
  424.0 3.7 all-to-all-start.7
  432.5 5.4 fusion
  437.9 20.8 %collective-permute-done.11 = bf16[4608,128]{1,0:T(8,128)(2,1)S(1)} collective-permute-done((bf16[4608,128]{1,0:T(8,128)(2,1)}, bf16[4608,128]{1,0:T(8,128)(2,1)S(1)}, u32[]{:S(2)}, u32[]{:S(2)}) %collective-permute-start.11) | collective-permute-done | bytes 1179680 | tf_op jit(solution)/shard_map/ppermute | solution.py:791
  461.1 5.5 all-to-all-start.8
  468.7 3.6 collective-permute-start.16
  473.8 38.6 %collective-permute-done.16 = bf16[4608,128]{1,0:T(8,128)(2,1)} collective-permute-done((bf16[4608,128]{1,0:T(8,128)(2,1)S(1)}, bf16[4608,128]{1,0:T(8,128)(2,1)}, u32[]{:S(2)}, u32[]{:S(2)}) %collective-permute-start.16) | collective-permute-done | bytes 1179680 | tf_op jit(solution)/shard_map/ppermute | solution.py:791
  513.5 4.6 all-to-all-start.5
  521.7 2.7 collective-permute-start.18
  524.4 54.4 %collective-permute-done.20.refs_4_ = bf16[4608,128]{1,0:T(8,128)(2,1)S(1)} collective-permute-done((bf16[4608,128]{1,0:T(8,128)(2,1)S(1)}, bf16[4608,128]{1,0:T(8,128)(2,1)S(1)}, u32[]{:S(2)}, u32[]{:S(2)}) %collective-permute-start.20) | collective-permute-done | bytes 1179680 | tf_op jit(solution)/shard_map/ppermute | solution.py:791
  582.8 6.5 all-to-all-start.9
  594.0 13.8 %collective-permute-done.21.refs_5_ = bf16[4608,128]{1,0:T(8,128)(2,1)} collective-permute-done((bf16[4608,128]{1,0:T(8,128)(2,1)S(1)}, bf16[4608,128]{1,0:T(8,128)(2,1)}, u32[]{:S(2)}, u32[]{:S(2)}) %collective-permute-start.21) | collective-permute-done | bytes 1179680 | tf_op jit(solution)/shard_map/ppermute | solution.py:791
  607.8 2.9 collective-permute-start.22
  613.9 36.0 %collective-permute-done.17.refs_1_ = bf16[4608,128]{1,0:T(8,128)(2,1)S(1)} collective-permute-done((bf16[4608,128]{1,0:T(8,128)(2,1)S(1)}, bf16[4608,128]{1,0:T(8,128)(2,1)S(1)}, u32[]{:S(2)}, u32[]{:S(2)}) %collective-permute-start.17) | collective-permute-done | bytes 1179680 | tf_op jit(solution)/shard_map/ppermute | solution.py:791
  649.9 23.4 %collective-permute-done.19.refs_2_ = bf16[4608,128]{1,0:T(8,128)(2,1)S(1)} collective-permute-done((bf16[4608,128]{1,0:T(8,128)(2,1)}, bf16[4608,128]{1,0:T(8,128)(2,1)S(1)}, u32[]{:S(2)}, u32[]{:S(2)}) %collective-permute-start.19) | collective-permute-done | bytes 1179680 | tf_op jit(solution)/shard_map/ppermute | solution.py:791
  674.3 10.0 %unpack_experts.1 = (f32[2,1536,512]{2,1,0:T(8,128)}, f32[2,1536,512]{2,1,0:T(8,128)}, f32[2,512,1536]{2,1,0:T(8,128)}) custom-call(s32[2]{0:T(128)S(1)} %copy-done.34, bf16[4608,128]{1,0:T(8,128)(2,1)S(1)} %add_convert_fusion.refs_0_, bf16[4608,128]{1,0:T(8,128)(2,1)S(1)} %collective-permute-done.17.refs_1_, ...), custom_call_target="tpu_custom_call" | custom-call | tf_op jit(solution)/shard_map/unpack_experts/pallas_call | solution.py:659
  (241 shorter events, 115.6 us)
Async XLA Ops:
  7.2 11.9 %copy-start.57 = (bf16[96]{0:T(256)(128)(2,1)S(1)}, bf16[96]{0:T(256)(128)(2,1)}, u32[]{:S(2)}) copy-start(bf16[96]{0:T(256)(128)(2,1)} %param.19) | copy-start | bytes 580
  7.2 155.8 %all-gather.4.cloned.1.call-start = ((), (), s32[]{:S(2)}) async-start(), calls=%async_computation.10 | async-start | bytes 13369344 | tf_op jit(solution)/shard_map/all_gather | solution.py:727
  10.6 17.4 %copy-start.50 = (bf16[96,1024]{1,0:T(8,128)(2,1)S(1)}, bf16[96,1024]{1,0:T(8,128)(2,1)}, u32[]{:S(2)}) copy-start(bf16[96,1024]{1,0:T(8,128)(2,1)} %param.25) | copy-start | bytes 589828
  10.6 86.1 %collective-permute-start = (bf16[128,1664]{1,0:T(8,128)(2,1)}, bf16[128,1664]{1,0:T(8,128)(2,1)}, u32[]{:S(2)}, u32[]{:S(2)}) collective-permute-start(bf16[128,1664]{1,0:T(8,128)(2,1)} %concatenate.33), channel_id=1, source_target_pairs={{0,2},{1,3},{2,0},{3,1},{4,6},{5,7},{6,4},{7,5},{8,10},{9,11},{10,... | collective-permute-start | bytes 1277960 | tf_op jit(solution)/shard_map/ppermute | solution.py:740
  12.6 86.5 %collective-permute-start.1 = (bf16[128,1664]{1,0:T(8,128)(2,1)}, bf16[128,1664]{1,0:T(8,128)(2,1)}, u32[]{:S(2)}, u32[]{:S(2)}) collective-permute-start(bf16[128,1664]{1,0:T(8,128)(2,1)} %concatenate.33), channel_id=1, source_target_pairs={{0,4},{1,5},{2,6},{3,7},{4,0},{5,1},{6,2},{7,3},{8,12},{9,13},{10,... | collective-permute-start | bytes 1277960 | tf_op jit(solution)/shard_map/ppermute | solution.py:740
  14.1 89.9 %collective-permute-start.2 = (bf16[128,1664]{1,0:T(8,128)(2,1)}, bf16[128,1664]{1,0:T(8,128)(2,1)}, u32[]{:S(2)}, u32[]{:S(2)}) collective-permute-start(bf16[128,1664]{1,0:T(8,128)(2,1)} %concatenate.33), channel_id=1, source_target_pairs={{0,6},{1,7},{2,4},{3,5},{4,2},{5,3},{6,0},{7,1},{8,14},{9,15},{10,... | collective-permute-start | bytes 1277960 | tf_op jit(solution)/shard_map/ppermute | solution.py:740
  14.1 91.7 %collective-permute-start.3 = (bf16[128,1664]{1,0:T(8,128)(2,1)}, bf16[128,1664]{1,0:T(8,128)(2,1)}, u32[]{:S(2)}, u32[]{:S(2)}) collective-permute-start(bf16[128,1664]{1,0:T(8,128)(2,1)} %concatenate.33), channel_id=1, source_target_pairs={{0,8},{1,9},{2,10},{3,11},{4,12},{5,13},{6,14},{7,15},{8,0},{9,1},... | collective-permute-start | bytes 1277960 | tf_op jit(solution)/shard_map/ppermute | solution.py:740
  17.2 90.5 %collective-permute-start.4 = (bf16[128,1664]{1,0:T(8,128)(2,1)}, bf16[128,1664]{1,0:T(8,128)(2,1)}, u32[]{:S(2)}, u32[]{:S(2)}) collective-permute-start(bf16[128,1664]{1,0:T(8,128)(2,1)} %concatenate.33), channel_id=1, source_target_pairs={{0,10},{1,11},{2,8},{3,9},{4,14},{5,15},{6,12},{7,13},{8,2},{9,3},... | collective-permute-start | bytes 1277960 | tf_op jit(solution)/shard_map/ppermute | solution.py:740
  19.8 63.7 %all-to-all-start = ((bf16[16,1,192]{2,1,0:T(2,128)(2,1)}), bf16[16,1,192]{2,1,0:T(2,128)(2,1)S(1)}, u32[]{:S(2)}, u32[]{:S(2)}) async-start(bf16[16,1,192]{2,1,0:T(2,128)(2,1)} %broadcast_in_dim.50), calls=%async_computation | async-start | bytes 32768 | tf_op jit(solution)/shard_map/all_to_all | solution.py:688
  26.2 57.3 %copy-start.5 = (bf16[1,128,1536]{2,1,0:T(8,128)(2,1)S(1)}, bf16[1,128,1536]{2,1,0:T(8,128)(2,1)}, u32[]{:S(2)}) copy-start(bf16[1,128,1536]{2,1,0:T(8,128)(2,1)} %x_ref.1) | copy-start | bytes 1179652
  85.4 64.1 %all-to-all-start.1 = ((bf16[8,128,1536]{2,1,0:T(8,128)(2,1)}), bf16[8,128,1536]{2,1,0:T(8,128)(2,1)S(1)}, u32[]{:S(2)}, u32[]{:S(2)}) async-start(bf16[8,128,1536]{2,1,0:T(8,128)(2,1)} %broadcast_in_dim.52), calls=%async_computation.1 | async-start | bytes 6291456 | tf_op jit(solution)/shard_map/all_to_all | solution.py:688
  96.7 14.2 %collective-permute-start.5 = (bf16[128,1664]{1,0:T(8,128)(2,1)}, bf16[128,1664]{1,0:T(8,128)(2,1)S(1)}, u32[]{:S(2)}, u32[]{:S(2)}) collective-permute-start(bf16[128,1664]{1,0:T(8,128)(2,1)} %concatenate.33), channel_id=1, source_target_pairs={{0,12},{1,13},{2,14},{3,15},{4,8},{5,9},{6,10},{7,11},{8,4},{9,5},... | collective-permute-start | bytes 1277960 | tf_op jit(solution)/shard_map/ppermute | solution.py:740
  99.1 54.7 %collective-permute-start.6 = (bf16[128,1664]{1,0:T(8,128)(2,1)}, bf16[128,1664]{1,0:T(8,128)(2,1)}, u32[]{:S(2)}, u32[]{:S(2)}) collective-permute-start(bf16[128,1664]{1,0:T(8,128)(2,1)} %concatenate.33), channel_id=1, source_target_pairs={{0,14},{1,15},{2,12},{3,13},{4,10},{5,11},{6,8},{7,9},{8,6},{9,7},... | collective-permute-start | bytes 1277960 | tf_op jit(solution)/shard_map/ppermute | solution.py:740
  149.5 13.5 %all-to-all-start.2 = ((bf16[16,96,128]{2,1,0:T(8,128)(2,1)}), bf16[16,96,128]{2,1,0:T(8,128)(2,1)}, u32[]{:S(2)}, u32[]{:S(2)}) async-start(bf16[16,96,128]{2,1,0:T(8,128)(2,1)} %copy.116), calls=%async_computation.2 | async-start | bytes 786432 | tf_op jit(solution)/shard_map/all_to_all | solution.py:688
  153.8 72.2 %all-gather.6.cloned.1.call-start = ((), (), s32[]{:S(2)}) async-start(), calls=%async_computation.11 | async-start | bytes 6684672 | tf_op jit(solution)/shard_map/all_gather | solution.py:764
  173.6 12.7 %copy-start.1 = (bf16[8,128,1024]{2,1,0:T(8,128)(2,1)}, bf16[8,128,1024]{2,1,0:T(8,128)(2,1)S(1)}, u32[]{:S(2)}) copy-start(bf16[8,128,1024]{2,1,0:T(8,128)(2,1)S(1)} %get-tuple-element.72.k_ref.v_ref) | copy-start | bytes 6291460
  173.6 12.7 %copy-start.17 = (bf16[128,1536]{1,0:T(8,128)(2,1)}, bf16[128,1536]{1,0:T(8,128)(2,1)S(1)}, u32[]{:S(2)}) copy-start(bf16[128,1536]{1,0:T(8,128)(2,1)S(1)} %get-tuple-element.71.q_ref) | copy-start | bytes 1179652
  187.2 224.1 %all-gather.8.cloned.1.call-start = ((), (), s32[]{:S(2)}) async-start(), calls=%async_computation.12 | async-start | bytes 13369344 | tf_op jit(solution)/shard_map/all_gather | solution.py:766
  188.3 6.6 collective-permute-start.7
  257.3 5.7 collective-permute-start.8
  265.6 69.8 %all-to-all-start.3 = ((bf16[8,128,1536]{2,1,0:T(8,128)(2,1)}), bf16[8,128,1536]{2,1,0:T(8,128)(2,1)S(1)}, u32[]{:S(2)}, u32[]{:S(2)}) async-start(bf16[8,128,1536]{2,1,0:T(8,128)(2,1)} %fusion.1), calls=%async_computation.3 | async-start | bytes 6291456 | tf_op jit(solution)/shard_map/all_to_all | solution.py:688
  289.7 91.4 %collective-permute-start.10 = (bf16[4608,128]{1,0:T(8,128)(2,1)}, bf16[4608,128]{1,0:T(8,128)(2,1)}, u32[]{:S(2)}, u32[]{:S(2)}) collective-permute-start(bf16[4608,128]{1,0:T(8,128)(2,1)} %get-tuple-element.88), channel_id=1, source_target_pairs={{0,48},{16,32},{32,16},{48,0},{64,112},{80,96},{96,80},{112,64},{1... | collective-permute-start | bytes 3538952 | tf_op jit(solution)/shard_map/ppermute | solution.py:791
  292.4 88.7 %collective-permute-start.9 = (bf16[4608,128]{1,0:T(8,128)(2,1)}, bf16[4608,128]{1,0:T(8,128)(2,1)}, u32[]{:S(2)}, u32[]{:S(2)}) collective-permute-start(bf16[4608,128]{1,0:T(8,128)(2,1)} %get-tuple-element.87), channel_id=1, source_target_pairs={{0,16},{16,0},{32,48},{48,32},{64,80},{80,64},{96,112},{112,96},{1... | collective-permute-start | bytes 3538952 | tf_op jit(solution)/shard_map/ppermute | solution.py:791
  292.6 173.9 %collective-permute-start.15 = (bf16[4608,128]{1,0:T(8,128)(2,1)}, bf16[4608,128]{1,0:T(8,128)(2,1)}, u32[]{:S(2)}, u32[]{:S(2)}) collective-permute-start(bf16[4608,128]{1,0:T(8,128)(2,1)} %get-tuple-element.118), channel_id=1, source_target_pairs={{0,48},{16,32},{32,16},{48,0},{64,112},{80,96},{96,80},{112,64},{1... | collective-permute-start | bytes 3538952 | tf_op jit(solution)/shard_map/ppermute | solution.py:791
  353.2 35.4 %all-to-all-start.4 = ((bf16[8,128,1024]{2,1,0:T(8,128)(2,1)}), bf16[8,128,1024]{2,1,0:T(8,128)(2,1)S(1)}, u32[]{:S(2)}, u32[]{:S(2)}) async-start(bf16[8,128,1024]{2,1,0:T(8,128)(2,1)} %copy-done.16), calls=%async_computation.4 | async-start | bytes 4194304 | tf_op jit(solution)/shard_map/all_to_all | solution.py:688
  364.1 12.3 %slice-start = ((s8[6291456]{0:T(1024)(128)(4,1)}), s8[4194304]{0:T(1024)(128)(4,1)S(1)}, s32[]{:S(2)}) async-start(s8[6291456]{0:T(1024)(128)(4,1)} %bitcast.103), calls=%async_computation.13 | async-start | bytes 8388608
  381.1 51.4 %collective-permute-start.13 = (bf16[8,128,1536]{2,1,0:T(8,128)(2,1)}, bf16[8,128,1536]{2,1,0:T(8,128)(2,1)}, u32[]{:S(2)}, u32[]{:S(2)}) collective-permute-start(bf16[8,128,1536]{2,1,0:T(8,128)(2,1)} %slice_bitcast_fusion), channel_id=1, source_target_pairs={{0,1},{1,0},{2,3},{3,2},{4,5},{5,4},{6,7},{7,6},{8,9},{9,8},{10,11... | collective-permute-start | bytes 9437192 | tf_op jit(solution)/shard_map/ppermute | solution.py:819
  391.1 20.2 %all-to-all-start.6 = ((bf16[16,256,128]{2,1,0:T(8,128)(2,1)}), bf16[16,256,128]{2,1,0:T(8,128)(2,1)S(1)}, u32[]{:S(2)}, u32[]{:S(2)}) async-start(bf16[16,256,128]{2,1,0:T(8,128)(2,1)} %get-tuple-element.103), calls=%async_computation.6 | async-start | bytes 2097152 | tf_op jit(solution)/shard_map/all_to_all | solution.py:688
  397.8 40.1 %collective-permute-start.12 = (bf16[4608,128]{1,0:T(8,128)(2,1)}, bf16[4608,128]{1,0:T(8,128)(2,1)}, u32[]{:S(2)}, u32[]{:S(2)}) collective-permute-start(bf16[4608,128]{1,0:T(8,128)(2,1)} %add_convert_fusion.2), channel_id=1, source_target_pairs={{0,48},{16,32},{32,16},{48,0},{64,112},{80,96},{96,80},{112,64},{1... | collective-permute-start | bytes 3538952 | tf_op jit(solution)/shard_map/ppermute | solution.py:791
  407.1 14.4 %copy-start.49 = (bf16[1536,128]{1,0:T(8,128)(2,1)S(1)}, bf16[1536,128]{1,0:T(8,128)(2,1)}, u32[]{:S(2)}) copy-start(bf16[1536,128]{1,0:T(8,128)(2,1)} %convolution_convert_fusion) | copy-start | bytes 1179652
  424.0 34.7 %all-to-all-start.7 = ((bf16[16,112,384]{2,1,0:T(8,128)(2,1)}), bf16[16,112,384]{2,1,0:T(8,128)(2,1)S(1)}, u32[]{:S(2)}, u32[]{:S(2)}) async-start(bf16[16,112,384]{2,1,0:T(8,128)(2,1)} %fusion.3), calls=%async_computation.7 | async-start | bytes 2752512 | tf_op jit(solution)/shard_map/all_to_all | solution.py:688
  430.3 28.4 %collective-permute-start.11 = (bf16[4608,128]{1,0:T(8,128)(2,1)}, bf16[4608,128]{1,0:T(8,128)(2,1)S(1)}, u32[]{:S(2)}, u32[]{:S(2)}) collective-permute-start(bf16[4608,128]{1,0:T(8,128)(2,1)} %add_convert_fusion.3), channel_id=1, source_target_pairs={{0,16},{16,0},{32,48},{48,32},{64,80},{80,64},{96,112},{112,96},{1... | collective-permute-start | bytes 3538952 | tf_op jit(solution)/shard_map/ppermute | solution.py:791
  461.1 51.3 %all-to-all-start.8 = ((bf16[8,256,384]{2,1,0:T(8,128)(2,1)}), bf16[8,256,384]{2,1,0:T(8,128)(2,1)S(1)}, u32[]{:S(2)}, u32[]{:S(2)}) async-start(bf16[8,256,384]{2,1,0:T(8,128)(2,1)} %pad_maximum_fusion), calls=%async_computation.8 | async-start | bytes 3145728 | tf_op jit(solution)/shard_map/all_to_all | solution.py:688
  468.7 43.7 %collective-permute-start.16 = (bf16[4608,128]{1,0:T(8,128)(2,1)S(1)}, bf16[4608,128]{1,0:T(8,128)(2,1)}, u32[]{:S(2)}, u32[]{:S(2)}) collective-permute-start(bf16[4608,128]{1,0:T(8,128)(2,1)S(1)} %add_convert_fusion.1), channel_id=1, source_target_pairs={{0,64},{16,80},{32,96},{48,112},{64,0},{80,16},{96,32},{112,48},{1... | collective-permute-start | bytes 3538952 | tf_op jit(solution)/shard_map/ppermute | solution.py:791
  472.3 45.9 %copy-start.44 = (bf16[4608,128]{1,0:T(8,128)(2,1)S(1)}, bf16[4608,128]{1,0:T(8,128)(2,1)}, u32[]{:S(2)}) copy-start(bf16[4608,128]{1,0:T(8,128)(2,1)} %get-tuple-element.96) | copy-start | bytes 3538948
  472.3 45.9 %collective-permute-start.14 = (bf16[4608,128]{1,0:T(8,128)(2,1)}, bf16[4608,128]{1,0:T(8,128)(2,1)}, u32[]{:S(2)}, u32[]{:S(2)}) collective-permute-start(bf16[4608,128]{1,0:T(8,128)(2,1)} %get-tuple-element.114), channel_id=1, source_target_pairs={{0,16},{16,0},{32,48},{48,32},{64,80},{80,64},{96,112},{112,96},{1... | collective-permute-start | bytes 3538952 | tf_op jit(solution)/shard_map/ppermute | solution.py:791
  513.5 68.0 %all-to-all-start.5 = ((bf16[8,128,1536]{2,1,0:T(8,128)(2,1)}), bf16[8,128,1536]{2,1,0:T(8,128)(2,1)}, u32[]{:S(2)}, u32[]{:S(2)}) async-start(bf16[8,128,1536]{2,1,0:T(8,128)(2,1)} %fusion), calls=%async_computation.5 | async-start | bytes 6291456 | tf_op jit(solution)/shard_map/all_to_all | solution.py:688
  520.8 58.0 %collective-permute-start.20 = (bf16[4608,128]{1,0:T(8,128)(2,1)S(1)}, bf16[4608,128]{1,0:T(8,128)(2,1)S(1)}, u32[]{:S(2)}, u32[]{:S(2)}) collective-permute-start(bf16[4608,128]{1,0:T(8,128)(2,1)S(1)} %add_convert_fusion.refs_0_), channel_id=1, source_target_pairs={{0,64},{16,80},{32,96},{48,112},{64,0},{80,16},{96,32},{112,48},{1... | collective-permute-start | bytes 3538952 | tf_op jit(solution)/shard_map/ppermute | solution.py:791
  521.7 71.7 %collective-permute-start.18 = (bf16[4608,128]{1,0:T(8,128)(2,1)S(1)}, bf16[4608,128]{1,0:T(8,128)(2,1)}, u32[]{:S(2)}, u32[]{:S(2)}) collective-permute-start(bf16[4608,128]{1,0:T(8,128)(2,1)S(1)} %add_convert_fusion.refs_0_), channel_id=1, source_target_pairs={{0,48},{16,32},{32,16},{48,0},{64,112},{80,96},{96,80},{112,64},{1... | collective-permute-start | bytes 3538952 | tf_op jit(solution)/shard_map/ppermute | solution.py:791
  578.8 29.0 %collective-permute-start.21 = (bf16[4608,128]{1,0:T(8,128)(2,1)S(1)}, bf16[4608,128]{1,0:T(8,128)(2,1)}, u32[]{:S(2)}, u32[]{:S(2)}) collective-permute-start(bf16[4608,128]{1,0:T(8,128)(2,1)S(1)} %collective-permute-done.20.refs_4_), channel_id=1, source_target_pairs={{0,16},{16,0},{32,48},{48,32},{64,80},{80,64},{96,112},{112,96},{1... | collective-permute-start | bytes 3538952 | tf_op jit(solution)/shard_map/ppermute | solution.py:791
  582.8 101.4 %all-to-all-start.9 = ((bf16[8,256,384]{2,1,0:T(8,128)(2,1)}), bf16[8,256,384]{2,1,0:T(8,128)(2,1)}, u32[]{:S(2)}, u32[]{:S(2)}) async-start(bf16[8,256,384]{2,1,0:T(8,128)(2,1)} %broadcast_in_dim.65), calls=%async_computation.9 | async-start | bytes 3145728 | tf_op jit(solution)/shard_map/all_to_all | solution.py:688
  589.4 23.7 %copy-start.11 = (f32[128,1536]{1,0:T(8,128)S(1)}, f32[128,1536]{1,0:T(8,128)}, u32[]{:S(2)}) copy-start(f32[128,1536]{1,0:T(8,128)} %copy-done.9) | copy-start | bytes 2359300
  589.4 84.9 %copy-start.34 = (s32[2]{0:T(128)S(1)}, s32[2]{0:T(128)}, u32[]{:S(2)}) copy-start(s32[2]{0:T(128)} %pad_add_fusion.at_ref) | copy-start | bytes 28
  589.4 60.5 %collective-permute-start.17 = (bf16[4608,128]{1,0:T(8,128)(2,1)S(1)}, bf16[4608,128]{1,0:T(8,128)(2,1)S(1)}, u32[]{:S(2)}, u32[]{:S(2)}) collective-permute-start(bf16[4608,128]{1,0:T(8,128)(2,1)S(1)} %add_convert_fusion.refs_0_), channel_id=1, source_target_pairs={{0,16},{16,0},{32,48},{48,32},{64,80},{80,64},{96,112},{112,96},{1... | collective-permute-start | bytes 3538952 | tf_op jit(solution)/shard_map/ppermute | solution.py:791
  591.4 58.5 %collective-permute-start.23 = (bf16[4608,128]{1,0:T(8,128)(2,1)S(1)}, bf16[4608,128]{1,0:T(8,128)(2,1)S(1)}, u32[]{:S(2)}, u32[]{:S(2)}) collective-permute-start(bf16[4608,128]{1,0:T(8,128)(2,1)S(1)} %collective-permute-done.20.refs_4_), channel_id=1, source_target_pairs={{0,48},{16,32},{32,16},{48,0},{64,112},{80,96},{96,80},{112,64},{1... | collective-permute-start | bytes 3538952 | tf_op jit(solution)/shard_map/ppermute | solution.py:791
  593.5 79.8 %collective-permute-start.19 = (bf16[4608,128]{1,0:T(8,128)(2,1)}, bf16[4608,128]{1,0:T(8,128)(2,1)S(1)}, u32[]{:S(2)}, u32[]{:S(2)}) collective-permute-start(bf16[4608,128]{1,0:T(8,128)(2,1)} %collective-permute-done.18.refs_3_), channel_id=1, source_target_pairs={{0,16},{16,0},{32,48},{48,32},{64,80},{80,64},{96,112},{112,96},{1... | collective-permute-start | bytes 3538952 | tf_op jit(solution)/shard_map/ppermute | solution.py:791
  607.8 65.4 %collective-permute-start.22 = (bf16[4608,128]{1,0:T(8,128)(2,1)}, bf16[4608,128]{1,0:T(8,128)(2,1)S(1)}, u32[]{:S(2)}, u32[]{:S(2)}) collective-permute-start(bf16[4608,128]{1,0:T(8,128)(2,1)} %collective-permute-done.21.refs_5_), channel_id=1, source_target_pairs={{0,48},{16,32},{32,16},{48,0},{64,112},{80,96},{96,80},{112,64},{1... | collective-permute-start | bytes 3538952 | tf_op jit(solution)/shard_map/ppermute | solution.py:791
  649.9 23.4 %copy-start.41 = (bf16[4608,128]{1,0:T(8,128)(2,1)}, bf16[4608,128]{1,0:T(8,128)(2,1)S(1)}, u32[]{:S(2)}) copy-start(bf16[4608,128]{1,0:T(8,128)(2,1)S(1)} %collective-permute-done.23.refs_7_) | copy-start | bytes 3538948
  (49 other events, 191.1 us)
Sparse Core Ops, SparseCore 0:
  10.3 140.5 all-gather.3
  187.3 38.6 all-gather.5
  227.7 106.3 all-gather.7

commit v4 on v3

--- a/solution.py
+++ b/solution.py
@@ -232,9 +232,8 @@
 
 
 def place_kernel(
-    at_ref, own_ref, other_ref, down_ref, sdown_ref, place_ref, geo_ref, geh_ref, gsh_ref, gate_ref
+    at_ref, up_ref, down_ref, sdown_ref, place_ref, geo_ref, geh_ref, gsh_ref, gate_ref
 ):
-    step = pl.program_id(0)
     lane = lax.broadcasted_iota(jnp.int32, (BLOCK, META), 1)
     row = lax.broadcasted_iota(jnp.int32, (BLOCK, META), 0)
     before = (row > lane).astype(bf16)
@@ -242,46 +241,37 @@
     first_id = (at_ref[0] * LOCAL_E).astype(f32)
     row_id = first_id + (row >= 64).astype(f32)
 
-    def run(up_ref):
-        for chip in range(HALF):
-            meta = up_ref[chip, :, WIDTH:].astype(f32)
-            named = lane < TOPK
-            zero = jnp.zeros((BLOCK, META), f32)
-            hit0 = jnp.where(named & (meta == first_id), 1.0, zero)
-            hit1 = jnp.where(named & (meta == first_id + 1.0), 1.0, zero)
-            mask = jnp.where(
-                lane < 64,
-                jnp.sum(hit0, axis=1, keepdims=True),
-                jnp.sum(hit1, axis=1, keepdims=True),
-            )
-            rank = dg(before, mask.astype(bf16), NN)
-            place = jnp.where((mask > 0.5) & (rank == slot), 1.0, zero).astype(bf16)
-            place_ref[chip, 0] = place
-            rows = dg(place, up_ref[chip], TN)
-            slot_meta = rows[:, WIDTH:]
-            gates = pltpu.roll(slot_meta, META - TOPK, 1) + pltpu.roll(
-                slot_meta, META - 2 * TOPK, 1
-            )
-            gate = jnp.sum(
-                jnp.where(named & (slot_meta == row_id), gates, zero), axis=1, keepdims=True
-            )
-            geo = (gate * rows[:, :WIDTH]).astype(bf16)
-            wide_gate = jnp.broadcast_to(gate, (BLOCK, META))
-            at = chip * CAP
-            for e in range(LOCAL_E):
-                geo_ref[e, 0, at : at + CAP] = geo[64 * e : 64 * e + CAP]
-                gate_ref[e, 0, at : at + CAP] = wide_gate[64 * e : 64 * e + CAP]
-            gsh_ref[chip, 0] = dg(up_ref[chip, :, :WIDTH], sdown_ref[...], NT)
+    for chip in range(HALF):
+        meta = up_ref[chip, 0, :, WIDTH:].astype(f32)
+        named = lane < TOPK
+        zero = jnp.zeros((BLOCK, META), f32)
+        hit0 = jnp.where(named & (meta == first_id), 1.0, zero)
+        hit1 = jnp.where(named & (meta == first_id + 1.0), 1.0, zero)
+        mask = jnp.where(
+            lane < 64,
+            jnp.sum(hit0, axis=1, keepdims=True),
+            jnp.sum(hit1, axis=1, keepdims=True),
+        )
+        rank = dg(before, mask.astype(bf16), NN)
+        place = jnp.where((mask > 0.5) & (rank == slot), 1.0, zero).astype(bf16)
+        place_ref[chip, 0] = place
+        rows = dg(place, up_ref[chip, 0], TN)
+        slot_meta = rows[:, WIDTH:]
+        gates = pltpu.roll(slot_meta, META - TOPK, 1) + pltpu.roll(
+            slot_meta, META - 2 * TOPK, 1
+        )
+        gate = jnp.sum(
+            jnp.where(named & (slot_meta == row_id), gates, zero), axis=1, keepdims=True
+        )
+        geo = (gate * rows[:, :WIDTH]).astype(bf16)
+        wide_gate = jnp.broadcast_to(gate, (BLOCK, META))
+        at = chip * CAP
         for e in range(LOCAL_E):
-            geh_ref[e, 0] = dg(geo_ref[e, 0], down_ref[e], NT)
-
-    @pl.when(step == 0)
-    def _():
-        run(other_ref)
-
-    @pl.when(step == 1)
-    def _():
-        run(own_ref)
+            geo_ref[e, 0, at : at + CAP] = geo[64 * e : 64 * e + CAP]
+            gate_ref[e, 0, at : at + CAP] = wide_gate[64 * e : 64 * e + CAP]
+        gsh_ref[chip, 0] = dg(up_ref[chip, 0, :, :WIDTH], sdown_ref[...], NT)
+    for e in range(LOCAL_E):
+        geh_ref[e, 0] = dg(geo_ref[e, 0], down_ref[e], NT)
 
 
 def by_core(cols):
@@ -295,15 +285,14 @@
     return pl.BlockSpec((LOCAL_E, 1, ROWS, cols), lambda s, at: (0, s, 0, 0))
 
 
-def place_rows(exp_at, own_up, other_up, expert_down, shared_two):
+def place_rows(exp_at, up_all, expert_down, shared_two):
     return pl.pallas_call(
         place_kernel,
         grid_spec=pltpu.PrefetchScalarGridSpec(
             num_scalar_prefetch=1,
             grid=(2,),
             in_specs=[
-                whole((HALF, BLOCK, WIDTH + META)),
-                whole((HALF, BLOCK, WIDTH + META)),
+                by_core(WIDTH + META),
                 whole((LOCAL_E, FF_E, WIDTH)),
                 whole((2 * SHARED, WIDTH)),
             ],
@@ -318,7 +307,7 @@
         ],
         compiler_params=params(56),
         name="place_rows",
-    )(exp_at, own_up, other_up, expert_down, shared_two)
+    )(exp_at, up_all, expert_down, shared_two)
 
 
 def expert_kernel(
@@ -506,22 +495,22 @@
     )(grad_qkv, w_all, w_all, tokens, gain, grad_middle)
 
 
-def cols_kernel(cols_ref, rows_ref, out_ref):
+def cols_kernel(cols_ref, hidden_ref, att_ref, out_ref):
     lhs = jnp.concatenate([cols_ref[j] for j in range(N_EXP)], axis=1)
     row = lax.broadcasted_iota(jnp.int32, (256, N_EXP * BLOCK), 0)
     zero = jnp.zeros_like(lhs)
-    attn = dg(jnp.where(row < 160, lhs, zero), rows_ref[:, :WIDTH], NN)
-    out = dg(jnp.where(row < 160, zero, lhs), rows_ref[:, WIDTH:], NN)
+    attn = dg(jnp.where(row < 160, lhs, zero), hidden_ref[...], NN)
+    out = dg(jnp.where(row < 160, zero, lhs), att_ref[...], NN)
     out_ref[...] = (attn + out).T.astype(bf16).reshape(N_EXP, 96, 256)
 
 
-def cols_grad(cols, rows_all):
+def cols_grad(cols, hidden_all, att_all):
     return pl.pallas_call(
         cols_kernel,
         out_shape=jax.ShapeDtypeStruct((N_EXP, 96, 256), bf16),
         compiler_params=params(56),
         name="cols_grad",
-    )(cols, rows_all)
+    )(cols, hidden_all, att_all)
 
 
 def norm_rows_kernel(x_ref, gain_ref, out_ref):
@@ -678,6 +667,31 @@
         compiler_params=params(48),
         name="unpack_experts",
     )(at, *pieces)
+
+
+def relay_kernel(p3, p6, relay_a, relay_b, add_a, add_b):
+    add_a[...] = (p6[...].astype(f32) + relay_a[...].astype(f32)).astype(bf16)
+    add_b[...] = (p3[...].astype(f32) + relay_b[...].astype(f32)).astype(bf16)
+
+
+def side_kernel(p0, p1, got_10, got_31, got_11, got_30, own, side):
+    own[...] = p0[...].astype(f32) + got_10[...].astype(f32) + got_30[...].astype(f32)
+    side[...] = (
+        p1[...].astype(f32) + got_31[...].astype(f32) + got_11[...].astype(f32)
+    ).astype(bf16)
+
+
+def piece_sums(kernel, kinds, *pieces):
+    spec = pl.BlockSpec((PIECE // 4, HEAD_DIM), lambda i: (i, 0))
+    return pl.pallas_call(
+        kernel,
+        grid=(4,),
+        in_specs=[spec] * len(pieces),
+        out_specs=[spec] * len(kinds),
+        out_shape=[jax.ShapeDtypeStruct((PIECE, HEAD_DIM), kind) for kind in kinds],
+        compiler_params=params(32),
+        name="piece_sums",
+    )(*pieces)
 
 
 same_core = [[2 * i + c for i in range(8)] for c in range(2)]
@@ -718,28 +732,21 @@
 ):
     exp_at = lax.axis_index("exp").astype(jnp.int32)
     ctx_at = lax.axis_index("ctx").astype(jnp.int32)
-    chip = exp_at // 2
     exp_s, ctx_s = exp_at.reshape(1), ctx_at.reshape(1)
 
     y_at, z_at = ctx_at % 4, ctx_at // 4
     yz_s = jnp.stack([y_at, z_at])
 
-    w_all = lax.all_gather(
-        jnp.concatenate([query_weight, out_weight, key_weight, value_weight], axis=1),
-        "exp",
-        axis=0,
-        tiled=True,
-    )
+    w_cat = jnp.concatenate([query_weight, out_weight, key_weight, value_weight], axis=1)
+    w_all = lax.all_gather(w_cat, "exp", axis=0, tiled=True)
     gates_high = route_gates[0].astype(bf16)
     gates_low = (route_gates[0] - gates_high.astype(f32)).astype(bf16)
     pad = jnp.zeros((BLOCK, META - 3 * TOPK), bf16)
     up_meta = jnp.concatenate(
         [cotangent[0], routes[0].astype(bf16), gates_high, gates_low, pad], axis=1
     )
-    up_pieces = [up_meta] + [
-        lax.ppermute(up_meta, "exp", [(i, i ^ (2 * k)) for i in range(N_EXP)]) for k in range(1, 8)
-    ]
-    gains = jnp.concatenate([norm_attn, norm_ffn])
+    up_all = lax.all_gather(after(up_meta, w_cat), "exp", axis=0, tiled=True)
+    gains = after(jnp.concatenate([norm_attn, norm_ffn]), w_cat)
     gains = swap_all(jnp.broadcast_to(gains, (N_EXP, gains.shape[0])), "exp")
     gain_attn = gains[:, :96].reshape(1, WIDTH).astype(f32)
     gain_ffn = gains[:, 96:].reshape(1, WIDTH).astype(f32)
@@ -749,28 +756,22 @@
     ).transpose(1, 0, 2)
     w_shared = swap_all(shared_cols, "exp").reshape(WIDTH, 2 * SHARED)
     shared_two = jnp.concatenate([shared_down, shared_down], axis=0)
-    up_own = jnp.zeros((HALF,) + up_meta.shape, bf16)
-    for k, piece in enumerate(up_pieces):
-        up_own = lax.dynamic_update_index_in_dim(up_own, piece, chip ^ k, 0)
-    up_other = lax.ppermute(up_own, "exp", core_swap)
 
     hidden_one = norm_rows(tokens, gain_attn)
     hidden_seq = norm_rows(tokens_seq, gain_attn)
-    hidden_seq = after(hidden_seq, w_shared, up_own)
+    hidden_seq = after(hidden_seq, w_shared)
     queries, kv_all = project(hidden_one, hidden_seq, w_all)
     attended, att_f, logs = attend(ctx_s, queries, kv_all)
     middle, hidden_two = middle_norm(attended, w_all, tokens[0], gain_ffn)
 
     hidden_all = lax.all_gather(hidden_two, "exp", axis=0, tiled=True)
     hidden_all = hidden_all.reshape(HALF, 2, BLOCK, WIDTH)
-    rows_all = lax.all_gather(
-        after(jnp.concatenate([hidden_one[0], attended], axis=1), hidden_two),
-        "exp",
-        axis=0,
-        tiled=True,
-    )
+    hidden_one_all = lax.all_gather(after(hidden_one[0], hidden_two), "exp", axis=0, tiled=True)
     place, grad_eo, grad_eh, grad_sh, slot_gate = place_rows(
-        exp_s, after(up_own, hidden_two), up_other, expert_down, shared_two
+        exp_s,
+        after(up_all, hidden_two).reshape(HALF, 2, BLOCK, WIDTH + META),
+        expert_down,
+        shared_two,
     )
     part, arrived, act, grad_gu, shared_act, shared_grad = expert_back(
         exp_s, hidden_all, place, grad_eh, grad_sh, expert_gate, expert_up, w_shared
@@ -790,47 +791,36 @@
     def to(rows, k):
         return lax.ppermute(rows, "ctx", [(i, i ^ k) for i in range(N_CTX)])
 
-    relay_a, relay_b = to(p[4], 1), to(p[5], 3)
-    got_10, got_31 = to(p[2], 1), to(p[7], 3)
-
+    relay_a, relay_b, got_10, got_31 = to(p[4], 1), to(p[5], 3), to(p[2], 1), to(p[7], 3)
     shared_grad_late = after(shared_grad, p[0]).reshape(N_EXP * BLOCK, META)
     grad_scols = dg(hidden_all.reshape(N_EXP * BLOCK, WIDTH), shared_grad_late, TN).astype(bf16)
-    core = exp_at % 2
-    act_pair = after(shared_act, p[0])
-    act_own = lax.dynamic_index_in_dim(act_pair, core, 1, keepdims=False)
-    act_other = lax.dynamic_index_in_dim(act_pair, 1 - core, 1, keepdims=False)
-    flat = (HALF * BLOCK, -1)
-    grad_sdown = (
-        dg(act_own.reshape(flat), up_own.reshape(flat), TN)
-        + dg(act_other.reshape(flat), up_other.reshape(flat), TN)
-    )[:SHARED, :WIDTH].astype(bf16)
-    out_part = expert_output(
-        exp_s, after(act, p[0]), slot_gate, place, shared_act, expert_down, shared_two
-    )
-
+    act_late = after(shared_act, p[0]).reshape(N_EXP * BLOCK, META)
+    grad_sdown = dg(act_late, up_all, TN)[:SHARED, :WIDTH].astype(bf16)
+
+    add_a, add_b = piece_sums(relay_kernel, (bf16, bf16), p[3], p[6], relay_a, relay_b)
+    got_11, got_30 = to(add_b, 1), to(add_a, 3)
+    grad_two = after(grad_two, add_a)
     grad_middle, grad_attn, grad_heads, grad_gain_ffn = middle_back(
         grad_two, middle, cotangent[0], gain_ffn, w_all
     )
+    att_all = lax.all_gather(after(attended, grad_two), "exp", axis=0, tiled=True)
     grad_query, part_kv = attend_back(ctx_s, queries, grad_heads, att_f, logs, kv_all)
     kv_pieces = swap_all(part_kv, "ctx")
 
-    relay_a, relay_b = after((relay_a, relay_b), part_kv)
-    got_11, got_30 = to(add_low(p[3], relay_b), 1), to(add_low(p[6], relay_a), 3)
-    out_other = lax.ppermute(after(out_part[0], part_kv), "exp", core_swap)
-    out_sum = add_low(out_part[1], out_other)
-
-    grad_qkv, cols = turn_cols(grad_query, kv_pieces, grad_attn)
-    cols_sent = cols
-    cols = swap_all(cols, "exp")
-    got_11, got_30, out_sum = after((got_11, got_30, out_sum), cols_sent)
-    out_pieces = swap_all(out_sum, "exp", same_core)
-    across = to(
-        (p[1].astype(f32) + got_11.astype(f32) + got_31.astype(f32)).astype(bf16), 4
-    )
+    out_part = expert_output(
+        exp_s, after(act, part_kv), slot_gate, place, shared_act, expert_down, shared_two
+    )
+
+    grad_qkv, cols_sent = turn_cols(grad_query, kv_pieces, grad_attn)
+    cols = swap_all(cols_sent, "exp")
+    own_part, side = piece_sums(
+        side_kernel, (f32, bf16), p[0], p[1], got_10, got_31, after(got_11, cols_sent), got_30
+    )
+    across = to(side, 4)
     input_grad, grad_gain_attn = input_back(
         grad_qkv, w_all, tokens[0], gain_attn, grad_middle
     )
-    grad_cols = cols_grad(cols, rows_all)
+    grad_cols = cols_grad(cols, hidden_one_all, att_all)
     gain_rows = jnp.concatenate(
         [grad_gain_attn.reshape(N_EXP, 1, 96), grad_gain_ffn.reshape(N_EXP, 1, 96)], axis=1
     ).astype(bf16)
@@ -843,36 +833,27 @@
         axis=2,
     )
     back = swap_all(sent, "exp")
-
-    own = (
-        p[0].astype(f32)
-        + got_10.astype(f32)
-        + got_30.astype(f32)
-        + after(across, sent).astype(f32)
-    ).astype(bf16)
+    own = (own_part + after(across, sent).astype(f32)).astype(bf16)
     at_1, at_3, at_z = to(own, 1), to(own, 3), to(own, 4)
+    out_other = lax.ppermute(after(out_part[0], own), "exp", core_swap)
+    out_sum = add_low(out_part[1], out_other)
 
     small = jnp.concatenate(
         [back.reshape(N_CTX, 224, 384), grad_sdown.reshape(N_CTX, 32, 384)], axis=1
     )
     pieces = swap_all(small, "ctx")
     late_own = jnp.sum(pieces.astype(f32), axis=0).astype(bf16)
-    at_2 = to(after(at_3, small), 1)
-    at_z1, at_z3 = to(after(at_z, small), 1), to(after(at_z, small), 3)
     late = swap_all(jnp.broadcast_to(late_own, (N_CTX, 256, 384)), "ctx")
-    at_z2 = to(after(at_z1, late_own), 3)
+    at_1, at_3, at_z = after((at_1, at_3, at_z), late_own)
+    at_2, at_z1, at_z3 = to(at_3, 1), to(at_z, 1), to(at_z, 3)
+    out_pieces = swap_all(after(out_sum, late_own), "exp", same_core)
+    at_z2 = to(at_z1, 3)
+    mixed = (middle + jnp.sum(out_pieces.astype(f32), axis=0)).astype(bf16)[None]
     grad_sdown = late[:, 224:].reshape(SHARED, WIDTH).astype(f32)
     late = late[:, :224].reshape(N_EXP, 112, 384)
-
-    mixed = (middle + jnp.sum(out_pieces.astype(f32), axis=0)).astype(bf16)[None]
     grad_wqkv = late[:, :96, :160].transpose(1, 0, 2).reshape(96, WIDTH + 2 * KV_WIDTH)
     gain_sum = jnp.sum(late[:, 96:98, :96].astype(f32), axis=0)
-    grad_egate, grad_eup, grad_edown = unpack_experts(
-        yz_s, (own, at_1, at_2, at_3, at_z, at_z1, at_z2, at_z3)
-    )
-    return (
-        mixed,
-        input_grad[None],
+    dense = (
         gain_sum[0],
         gain_sum[1],
         grad_wqkv[:, :WIDTH].astype(f32),
@@ -882,10 +863,10 @@
         late[:, :96, 256 : 256 + SHARED].transpose(1, 0, 2).reshape(96, 1024).astype(f32),
         late[:, :96, 256 + SHARED :].transpose(1, 0, 2).reshape(96, 1024).astype(f32),
         grad_sdown,
-        grad_egate,
-        grad_eup,
-        grad_edown,
-    )
+    )
+    own = after(own, mixed, *dense)
+    experts = unpack_experts(yz_s, (own, at_1, at_2, at_3, at_z, at_z1, at_z2, at_z3))
+    return (mixed, input_grad[None]) + dense + tuple(experts)
 
 
 def solution(mesh):

time: 721 us -> 655 us (0.908)
  waiting for transfers between devices: 364 us -> 300 us
  starting transfers between devices: 90.1 us -> 75.7 us
  blocking collectives: 0 us -> 11.7 us
  other arithmetic: 38.6 us -> 30.5 us
    ppermute x14, waiting for transfers between devices: 187 us -> 97.8 us  [to(): return lax.ppermute(rows, 'ctx', [(i, i ^ k) for i in range(N_CTX)])]
    all_gather x2 -> x4, waiting for transfers between devices: 0.01 us -> 47.9 us  [the longest x1 25.8 us: on_device(): w_all = lax.all_gather(w_cat, 'exp', axis=0, tiled=True)]
    all_to_all x10 -> x9, waiting for transfers between devices: 149 us -> 117 us  [swap_all(): lax.all_to_all(rows, axis, split_axis=0, concat_axis=0, tiled=True, axis_...]
    all_gather x1, waiting for transfers between devices: 14.4 us -> 31.3 us  [on_device(): hidden_all = lax.all_gather(hidden_two, 'exp', axis=0, tiled=True)]
    unnamed x131 -> x122, local copies, waits for them, and re-layouts: 32 us -> 46.9 us
    dynamic_update_slice x8 -> x0, local copies, waits for them, and re-layouts: 13.5 us -> none  [on_device(): up_own = lax.dynamic_update_index_in_dim(up_own, piece, chip ^ k, 0)]
    ppermute x9 -> x1, starting transfers between devices: 12.5 us -> 0.48 us  [on_device(): out_other = lax.ppermute(after(out_part[0], own), 'exp', core_swap)]
    all_to_all x0 -> x1, blocking collectives: none -> 11.7 us  [swap_all(): lax.all_to_all(rows, axis, split_axis=0, concat_axis=0, tiled=True, axis_...]
  transfers between devices with their start and end apart: 37 -> 30, of which waited for: 16 -> 21; matrix products, arithmetic and copies ran while one was open for 9% -> 12% of each run, Pallas kernels for 16% -> 19%
where the time goes in v4:
time: 655 us; the launch traced here: 647 us
  waiting for transfers between devices  300 us (46%)
  Pallas kernels  132 us (20%)
  starting transfers between devices  75.7 us (12%)
  local copies, waits for them, and re-layouts  72.2 us (11%)
  other arithmetic  30.5 us (5%)
  between operations  14.6 us (2%)
  blocking collectives  11.7 us (2%)
  matrix products  9.56 us (1%)
    all_to_all x9, waiting for transfers between devices, swap_all(): lax.all_to_all(rows, axis, split_axis=0, concat_axis=0, tiled=True, axis_...  117 us
    ppermute x14, waiting for transfers between devices, to(): return lax.ppermute(rows, 'ctx', [(i, i ^ k) for i in range(N_CTX)])  97.8 us
    unnamed x122, local copies, waits for them, and re-layouts  46.9 us
    all_to_all x9, starting transfers between devices, swap_all(): lax.all_to_all(rows, axis, split_axis=0, concat_axis=0, tiled=True, axis_...  46.9 us
    all_gather x1, waiting for transfers between devices, on_device(): hidden_all = lax.all_gather(hidden_two, 'exp', axis=0, tiled=True)  31.3 us
    pallas_call x1, Pallas kernels, expert_back(): pl.pallas_call(expert_kernel, grid_spec=pltpu.PrefetchScalarGridSpec(num_...  28.6 us
    ppermute x14, starting transfers between devices, to(): return lax.ppermute(rows, 'ctx', [(i, i ^ k) for i in range(N_CTX)])  27.8 us
    all_gather x1, waiting for transfers between devices, on_device(): w_all = lax.all_gather(w_cat, 'exp', axis=0, tiled=True)  25.8 us
  transfers between devices with their start and end apart: 30, of which 21 were waited for; matrix products, arithmetic and copies ran while one was open for 12% of the time, Pallas kernels for 19%

profile of v4, /device:TPU:0, one launch (start us, length us, event | category | flops | bytes accessed | tf_op | source)
XLA Modules:
  0.0 646.7 jit_solution(12939470028086388718)
XLA Ops:
  14.7 11.7 %all_to_all.54 = bf16[16,1,192]{2,1,0:T(2,128)(2,1)S(1)} all-to-all(bf16[16,1,192]{2,1,0:T(2,128)(2,1)S(1)} %broadcast_in_dim.22), channel_id=1, replica_groups=mesh['ctx'=8,'exp'=16] {'exp'}, dimensions={0} | all-to-all | bytes 12288 | tf_op jit(solution)/shard_map/all_to_all | solution.py:702
  28.4 7.5 %all-to-all-start.1 = ((bf16[8,128,1536]{2,1,0:T(8,128)(2,1)}), bf16[8,128,1536]{2,1,0:T(8,128)(2,1)S(1)}, u32[]{:S(2)}, u32[]{:S(2)}) async-start(bf16[8,128,1536]{2,1,0:T(8,128)(2,1)} %broadcast_in_dim.24), calls=%async_computation.1 | async-start | bytes 6291456 | tf_op jit(solution)/shard_map/all_to_all | solution.py:702
  43.4 39.5 %all-to-all-done.1.x_ref = bf16[8,128,1536]{2,1,0:T(8,128)(2,1)S(1)} async-done(((bf16[8,128,1536]{2,1,0:T(8,128)(2,1)}), bf16[8,128,1536]{2,1,0:T(8,128)(2,1)S(1)}, u32[]{:S(2)}, u32[]{:S(2)}) %all-to-all-start.1) | async-done | bytes 3145760 | tf_op jit(solution)/shard_map/all_to_all | solution.py:702
  82.9 4.2 all-to-all-start.2
  92.9 5.8 all-to-all-done.2
  98.7 25.8 %all-gather.6.cloned.1.call-done.w_ref.wq_ref.wkv_ref = bf16[1536,4096]{1,0:T(8,128)(2,1)} async-done(((bf16[96,4096]{1,0:T(8,128)(2,1)}), bf16[1536,4096]{1,0:T(8,128)(2,1)}) %all-gather.6.cloned.1.call-update) | async-done | bytes 12582928 | tf_op jit(solution)/shard_map/all_gather | solution.py:741
  126.4 7.8 %project.1 = (bf16[128,1536]{1,0:T(8,128)(2,1)S(1)}, bf16[8,128,1024]{2,1,0:T(8,128)(2,1)S(1)}) custom-call(bf16[1,128,1536]{2,1,0:T(8,128)(2,1)} %norm_rows.2.own_ref, bf16[8,128,1536]{2,1,0:T(8,128)(2,1)S(1)} %copy-done.3, bf16[1536,4096]{1,0:T(8,128)(2,1)} %all-gather.6.cloned.1.call-done.w_ref.wq_ref.wkv_ref), custom_call_target="tpu_custom_call" | custom-call | tf_op jit(solution)/shard_map/project/pallas_call | solution.py:550
  134.2 5.8 attend.1
  141.9 4.9 copy-done
  150.1 22.0 %all-gather.10.cloned.1.call-done = bf16[2048,1664]{1,0:T(8,128)(2,1)} async-done(((bf16[128,1664]{1,0:T(8,128)(2,1)}), bf16[2048,1664]{1,0:T(8,128)(2,1)}) %all-gather.10.cloned.1.call-update) | async-done | bytes 6815760 | tf_op jit(solution)/shard_map/all_gather | solution.py:748
  172.1 14.2 %place_rows.1 = (bf16[8,2,128,128]{3,2,1,0:T(8,128)(2,1)}, bf16[2,2,384,1536]{3,2,1,0:T(8,128)(2,1)}, f32[2,2,384,512]{3,2,1,0:T(8,128)}, f32[8,2,128,128]{3,2,1,0:T(8,128)}, f32[2,2,384,128]{3,2,1,0:T(8,128)}) custom-call(s32[1]{0:T(128)} %bitcast.6.at_ref, bf16[8,2,128,1664]{3,2,1,0:T(8,128)(2,1)} %bitcast.75, bf16[2,512,1536]{2,1,0:T(8,128)(2,1)} %wd_ref.1, ...), custom_call_target="tpu_custom_call" | custom-call | tf_op jit(solution)/shard_map/place_rows/pallas_call | solution.py:289
  186.3 31.3 %all-gather.8.cloned.1.call-done = bf16[2048,1536]{1,0:T(8,128)(2,1)} async-done(((bf16[128,1536]{1,0:T(8,128)(2,1)}), bf16[2048,1536]{1,0:T(8,128)(2,1)}) %all-gather.8.cloned.1.call-update) | async-done | bytes 6291472 | tf_op jit(solution)/shard_map/all_gather | solution.py:767
  217.6 28.6 %expert_back.1 = (bf16[2,8,128,1536]{3,2,1,0:T(8,128)(2,1)}, bf16[2,2,384,1536]{3,2,1,0:T(8,128)(2,1)}, bf16[2,2,384,512]{3,2,1,0:T(8,128)(2,1)}, bf16[2,2,384,1...) custom-call(s32[1]{0:T(128)} %bitcast.6.at_ref, ...), custom_call_target="tpu_custom_call" | custom-call | tf_op jit(solution)/shard_map/expert_back/pallas_call | solution.py:367
  248.9 5.8 collective-permute-done
  254.7 2.6 fusion.1
  257.3 4.8 all-to-all-start.3
  262.7 18.1 %expert_weights.1 = (bf16[4608,128]{1,0:T(8,128)(2,1)}, bf16[4608,128]{1,0:T(8,128)(2,1)}, bf16[4608,128]{1,0:T(8,128)(2,1)}, bf16[4608,128]{1,0:T(8,128)(2,1)},...) custom-call(s32[2]{0:T(128)} %pad_add_fusion.at_ref, ...), custom_call_target="tpu_custom_call" | custom-call | tf_op jit(solution)/shard_map/expert_weights/pallas_call | solution.py:606
  284.5 24.5 %collective-permute-done.1.relay_a = bf16[4608,128]{1,0:T(8,128)(2,1)S(1)} collective-permute-done((bf16[4608,128]{1,0:T(8,128)(2,1)}, bf16[4608,128]{1,0:T(8,128)(2,1)S(1)}, u32[]{:S(2)}, u32[]{:S(2)}) %collective-permute-start.1) | collective-permute-done | bytes 1179680 | tf_op jit(solution)/shard_map/ppermute | solution.py:792
  319.0 4.8 middle_back.1
  326.0 6.9 %attend_back.1 = (bf16[128,1536]{1,0:T(8,128)(2,1)S(1)}, bf16[8,128,1024]{2,1,0:T(8,128)(2,1)S(1)}) custom-call(s32[1]{0:T(128)} %bitcast.ctx_ref, bf16[128,1536]{1,0:T(8,128)(2,1)S(1)} %copy-done.16, bf16[128,1536]{1,0:T(8,128)(2,1)S(1)} %get-tuple-element.100.ga_ref, f32[128,1536]{1,0:T(8,128)S(1)} %copy-done.29, f32[1536,128]{1,0:T(8,128)S(1)} %copy-done.31, ...), custom_call_target="tpu_custom_call" | custom-call | tf_op jit(solution)/shard_map/attend_back/pallas_call | solution.py:136
  335.0 5.6 all-to-all-start.4
  342.7 3.2 collective-permute-start.4
  345.9 27.1 %all-to-all-done.4.pieces_ref = bf16[8,128,1024]{2,1,0:T(8,128)(2,1)S(1)} async-done(((bf16[8,128,1024]{2,1,0:T(8,128)(2,1)}), bf16[8,128,1024]{2,1,0:T(8,128)(2,1)S(1)}, u32[]{:S(2)}, u32[]{:S(2)}) %all-to-all-start.4) | async-done | bytes 2097184 | tf_op jit(solution)/shard_map/all_to_all | solution.py:702
  376.6 15.8 %collective-permute-done.5.got_11 = bf16[4608,128]{1,0:T(8,128)(2,1)} collective-permute-done((bf16[4608,128]{1,0:T(8,128)(2,1)}, bf16[4608,128]{1,0:T(8,128)(2,1)}, u32[]{:S(2)}, u32[]{:S(2)}) %collective-permute-start.5) | collective-permute-done | bytes 1179680 | tf_op jit(solution)/shard_map/ppermute | solution.py:792
  392.3 22.9 %collective-permute-done.3.got_10 = bf16[4608,128]{1,0:T(8,128)(2,1)} collective-permute-done((bf16[4608,128]{1,0:T(8,128)(2,1)}, bf16[4608,128]{1,0:T(8,128)(2,1)}, u32[]{:S(2)}, u32[]{:S(2)}) %collective-permute-start.3) | collective-permute-done | bytes 1179680 | tf_op jit(solution)/shard_map/ppermute | solution.py:792
  416.4 4.3 piece_sums.3
  420.8 3.0 collective-permute-start.7
  423.8 5.5 convolution_convert_fusion
  429.3 5.1 all-to-all-start.5
  435.7 9.8 %expert_output.1 = bf16[2,8,128,1536]{3,2,1,0:T(8,128)(2,1)} custom-call(s32[1]{0:T(128)} %bitcast.6.at_ref, bf16[2,2,384,512]{3,2,1,0:T(8,128)(2,1)S(1)} %copy-done.4, f32[2,2,384,128]{3,2,1,0:T(8,128)S(1)} %copy-done.27, bf16[8,2,128,128]{3,2,1,0:T(8,128)(2,1)S(1)} %copy-done.13, bf16[8,2,128,128]{3,2,1,0:T(8,128)(2,1)S(1)} %copy-done.6, ...), custom_call_target="tpu_custom_call" | custom-call | tf_op jit(solution)/shard_map/expert_output/pallas_call | solution.py:418
  445.4 3.9 slice_bitcast_fusion
  449.3 6.9 %input_back.1 = (bf16[128,1536]{1,0:T(8,128)(2,1)}, f32[1,1536]{1,0:T(1,128)S(1)}) custom-call(bf16[128,2560]{1,0:T(8,128)(2,1)S(1)} %copy-done.33, bf16[1536,4096]{1,0:T(8,128)(2,1)} %all-gather.6.cloned.1.call-done.w_ref.wq_ref.wkv_ref, bf16[1536,4096]{1,0:T(8,128)(2,1)} %all-gather.6.cloned.1.call-done.w_ref.wq_ref.wkv_ref, ...), custom_call_target="tpu_custom_call" | custom-call | tf_op jit(solution)/shard_map/input_back/pallas_call | solution.py:477
  456.4 4.4 all-to-all-done.5.cols_ref
  460.8 9.3 %cols_grad.1 = bf16[16,96,256]{2,1,0:T(8,128)(2,1)} custom-call(bf16[16,256,128]{2,1,0:T(8,128)(2,1)} %all-to-all-done.5.cols_ref, bf16[2048,1536]{1,0:T(8,128)(2,1)} %all-gather.12.cloned.1.call-done.hidden_ref, bf16[2048,1536]{1,0:T(8,128)(2,1)} %all-gather.14.cloned.1.call-done.att_ref), custom_call_target="tpu_custom_call" | custom-call | tf_op jit(solution)/shard_map/cols_grad/pallas_call | solution.py:508
  472.5 5.6 all-to-all-start.6
  480.8 4.1 fusion.12
  485.1 13.0 %all-to-all-done.6 = bf16[16,112,384]{2,1,0:T(8,128)(2,1)S(1)} async-done(((bf16[16,112,384]{2,1,0:T(8,128)(2,1)}), bf16[16,112,384]{2,1,0:T(8,128)(2,1)S(1)}, u32[]{:S(2)}, u32[]{:S(2)}) %all-to-all-start.6) | async-done | bytes 1376288 | tf_op jit(solution)/shard_map/all_to_all | solution.py:702
  499.4 4.3 all-to-all-start.7
  507.7 3.0 collective-permute-start.11
  510.7 16.4 %all-to-all-done.7 = bf16[8,256,384]{2,1,0:T(8,128)(2,1)} async-done(((bf16[8,256,384]{2,1,0:T(8,128)(2,1)}), bf16[8,256,384]{2,1,0:T(8,128)(2,1)}, u32[]{:S(2)}, u32[]{:S(2)}) %all-to-all-start.7) | async-done | bytes 1572896 | tf_op jit(solution)/shard_map/all_to_all | solution.py:702
  530.1 4.3 all-to-all-start.9
  534.4 15.7 %collective-permute-done.9.refs_1_ = bf16[4608,128]{1,0:T(8,128)(2,1)S(1)} collective-permute-done((bf16[4608,128]{1,0:T(8,128)(2,1)S(1)}, bf16[4608,128]{1,0:T(8,128)(2,1)S(1)}, u32[]{:S(2)}, u32[]{:S(2)}) %collective-permute-start.9) | collective-permute-done | bytes 1179680 | tf_op jit(solution)/shard_map/ppermute | solution.py:792
  552.7 5.4 fusion
  558.1 10.7 %all-to-all-done.9 = bf16[8,256,384]{2,1,0:T(8,128)(2,1)} async-done(((bf16[8,256,384]{2,1,0:T(8,128)(2,1)}), bf16[8,256,384]{2,1,0:T(8,128)(2,1)}, u32[]{:S(2)}, u32[]{:S(2)}) %all-to-all-start.9) | async-done | bytes 1572896 | tf_op jit(solution)/shard_map/all_to_all | solution.py:702
  568.8 5.4 all-to-all-start.8
  574.2 4.7 collective-permute-start.15
  578.9 13.7 %collective-permute-done.13.refs_5_ = bf16[4608,128]{1,0:T(8,128)(2,1)} collective-permute-done((bf16[4608,128]{1,0:T(8,128)(2,1)}, bf16[4608,128]{1,0:T(8,128)(2,1)}, u32[]{:S(2)}, u32[]{:S(2)}) %collective-permute-start.13) | collective-permute-done | bytes 1179680 | tf_op jit(solution)/shard_map/ppermute | solution.py:792
  629.3 10.7 %unpack_experts.1 = (f32[2,1536,512]{2,1,0:T(8,128)}, f32[2,1536,512]{2,1,0:T(8,128)}, f32[2,512,1536]{2,1,0:T(8,128)}) custom-call(s32[2]{0:T(128)S(1)} %copy-done.41, bf16[4608,128]{1,0:T(8,128)(2,1)S(1)} %add_convert_fusion.refs_0_, bf16[4608,128]{1,0:T(8,128)(2,1)S(1)} %collective-permute-done.9.refs_1_, ...), custom_call_target="tpu_custom_call" | custom-call | tf_op jit(solution)/shard_map/unpack_experts/pallas_call | solution.py:648
  (207 shorter events, 111.5 us)
Async XLA Ops:
  7.2 7.4 %copy-start.52 = (bf16[96]{0:T(256)(128)(2,1)S(1)}, bf16[96]{0:T(256)(128)(2,1)}, u32[]{:S(2)}) copy-start(bf16[96]{0:T(256)(128)(2,1)} %param.20) | copy-start | bytes 580
  7.2 7.4 %copy-start.53 = (bf16[96]{0:T(256)(128)(2,1)S(1)}, bf16[96]{0:T(256)(128)(2,1)}, u32[]{:S(2)}) copy-start(bf16[96]{0:T(256)(128)(2,1)} %param.19) | copy-start | bytes 580
  7.2 19.2 %copy-start.5 = (bf16[1,128,1536]{2,1,0:T(8,128)(2,1)S(1)}, bf16[1,128,1536]{2,1,0:T(8,128)(2,1)}, u32[]{:S(2)}) copy-start(bf16[1,128,1536]{2,1,0:T(8,128)(2,1)} %x_ref.1) | copy-start | bytes 1179652
  7.2 117.3 %all-gather.6.cloned.1.call-start = ((), (), s32[]{:S(2)}) async-start(), calls=%async_computation.10 | async-start | bytes 13369344 | tf_op jit(solution)/shard_map/all_gather | solution.py:741
  12.0 160.1 %all-gather.10.cloned.1.call-start = ((), (), s32[]{:S(2)}) async-start(), calls=%async_computation.12 | async-start | bytes 7241728 | tf_op jit(solution)/shard_map/all_gather | solution.py:748
  28.4 54.5 %all-to-all-start.1 = ((bf16[8,128,1536]{2,1,0:T(8,128)(2,1)}), bf16[8,128,1536]{2,1,0:T(8,128)(2,1)S(1)}, u32[]{:S(2)}, u32[]{:S(2)}) async-start(bf16[8,128,1536]{2,1,0:T(8,128)(2,1)} %broadcast_in_dim.24), calls=%async_computation.1 | async-start | bytes 6291456 | tf_op jit(solution)/shard_map/all_to_all | solution.py:702
  82.9 15.9 %all-to-all-start.2 = ((bf16[16,96,128]{2,1,0:T(8,128)(2,1)}), bf16[16,96,128]{2,1,0:T(8,128)(2,1)}, u32[]{:S(2)}, u32[]{:S(2)}) async-start(bf16[16,96,128]{2,1,0:T(8,128)(2,1)} %copy.117), calls=%async_computation.2 | async-start | bytes 786432 | tf_op jit(solution)/shard_map/all_to_all | solution.py:702
  87.1 130.5 %all-gather.8.cloned.1.call-start = ((), (), s32[]{:S(2)}) async-start(), calls=%async_computation.11 | async-start | bytes 6684672 | tf_op jit(solution)/shard_map/all_gather | solution.py:767
  134.2 13.5 %copy-start.1 = (bf16[8,128,1024]{2,1,0:T(8,128)(2,1)}, bf16[8,128,1024]{2,1,0:T(8,128)(2,1)S(1)}, u32[]{:S(2)}) copy-start(bf16[8,128,1024]{2,1,0:T(8,128)(2,1)S(1)} %get-tuple-element.79.k_ref.v_ref) | copy-start | bytes 6291460
  134.2 13.5 %copy-start.15 = (bf16[128,1536]{1,0:T(8,128)(2,1)}, bf16[128,1536]{1,0:T(8,128)(2,1)S(1)}, u32[]{:S(2)}) copy-start(bf16[128,1536]{1,0:T(8,128)(2,1)S(1)} %get-tuple-element.78.q_ref) | copy-start | bytes 1179652
  141.9 44.5 %copy-start.17 = (bf16[128,1536]{1,0:T(8,128)(2,1)}, bf16[128,1536]{1,0:T(8,128)(2,1)S(1)}, u32[]{:S(2)}) copy-start(bf16[128,1536]{1,0:T(8,128)(2,1)S(1)} %get-tuple-element.119.att_ref) | copy-start | bytes 1179652
  149.4 307.0 %all-gather.12.cloned.1.call-start = ((), (), s32[]{:S(2)}) async-start(), calls=%async_computation.13 | async-start | bytes 6684672 | tf_op jit(solution)/shard_map/all_gather | solution.py:769
  150.1 22.1 %copy-start.10 = (bf16[128,1536]{1,0:T(8,128)(2,1)}, bf16[128,1536]{1,0:T(8,128)(2,1)S(1)}, u32[]{:S(2)}) copy-start(bf16[128,1536]{1,0:T(8,128)(2,1)S(1)} %constant_dynamic-update-slice_fusion.4.sdown_ref.sd_ref) | copy-start | bytes 1179652
  246.2 8.5 %copy-start.45 = (bf16[2,8,128,1536]{3,2,1,0:T(8,128)(2,1)S(1)}, bf16[2,8,128,1536]{3,2,1,0:T(8,128)(2,1)}, u32[]{:S(2)}) copy-start(bf16[2,8,128,1536]{3,2,1,0:T(8,128)(2,1)} %get-tuple-element.89) | copy-start | bytes 18874372
  248.6 6.1 collective-permute-start
  257.3 59.5 %all-to-all-start.3 = ((bf16[8,128,1536]{2,1,0:T(8,128)(2,1)}), bf16[8,128,1536]{2,1,0:T(8,128)(2,1)S(1)}, u32[]{:S(2)}, u32[]{:S(2)}) async-start(bf16[8,128,1536]{2,1,0:T(8,128)(2,1)} %fusion.1), calls=%async_computation.3 | async-start | bytes 6291456 | tf_op jit(solution)/shard_map/all_to_all | solution.py:702
  262.1 198.7 %all-gather.14.cloned.1.call-start = ((), (), s32[]{:S(2)}) async-start(), calls=%async_computation.14 | async-start | bytes 6684672 | tf_op jit(solution)/shard_map/all_gather | solution.py:806
  280.8 28.2 %collective-permute-start.1 = (bf16[4608,128]{1,0:T(8,128)(2,1)}, bf16[4608,128]{1,0:T(8,128)(2,1)S(1)}, u32[]{:S(2)}, u32[]{:S(2)}) collective-permute-start(bf16[4608,128]{1,0:T(8,128)(2,1)} %get-tuple-element.96), channel_id=1, source_target_pairs={{0,16},{16,0},{32,48},{48,32},{64,80},{80,64},{96,112},{112,96},{1... | collective-permute-start | bytes 3538952 | tf_op jit(solution)/shard_map/ppermute | solution.py:792
  282.3 29.1 %collective-permute-start.2 = (bf16[4608,128]{1,0:T(8,128)(2,1)}, bf16[4608,128]{1,0:T(8,128)(2,1)S(1)}, u32[]{:S(2)}, u32[]{:S(2)}) collective-permute-start(bf16[4608,128]{1,0:T(8,128)(2,1)} %get-tuple-element.97), channel_id=1, source_target_pairs={{0,48},{16,32},{32,16},{48,0},{64,112},{80,96},{96,80},{112,64},{1... | collective-permute-start | bytes 3538952 | tf_op jit(solution)/shard_map/ppermute | solution.py:792
  319.0 7.0 %copy-start.31 = (f32[1536,128]{1,0:T(8,128)S(1)}, f32[1536,128]{1,0:T(8,128)}, u32[]{:S(2)}) copy-start(f32[1536,128]{1,0:T(8,128)} %copy-done.30) | copy-start | bytes 2359300
  335.0 38.1 %all-to-all-start.4 = ((bf16[8,128,1024]{2,1,0:T(8,128)(2,1)}), bf16[8,128,1024]{2,1,0:T(8,128)(2,1)S(1)}, u32[]{:S(2)}, u32[]{:S(2)}) async-start(bf16[8,128,1024]{2,1,0:T(8,128)(2,1)} %copy-done.14), calls=%async_computation.4 | async-start | bytes 4194304 | tf_op jit(solution)/shard_map/all_to_all | solution.py:702
  340.6 51.7 %collective-permute-start.5 = (bf16[4608,128]{1,0:T(8,128)(2,1)}, bf16[4608,128]{1,0:T(8,128)(2,1)}, u32[]{:S(2)}, u32[]{:S(2)}) collective-permute-start(bf16[4608,128]{1,0:T(8,128)(2,1)} %copy-done.43), channel_id=1, source_target_pairs={{0,16},{16,0},{32,48},{48,32},{64,80},{80,64},{96,112},{112,96},{1... | collective-permute-start | bytes 3538952 | tf_op jit(solution)/shard_map/ppermute | solution.py:792
  342.6 72.6 %collective-permute-start.3 = (bf16[4608,128]{1,0:T(8,128)(2,1)}, bf16[4608,128]{1,0:T(8,128)(2,1)}, u32[]{:S(2)}, u32[]{:S(2)}) collective-permute-start(bf16[4608,128]{1,0:T(8,128)(2,1)} %get-tuple-element.109), channel_id=1, source_target_pairs={{0,16},{16,0},{32,48},{48,32},{64,80},{80,64},{96,112},{112,96},{1... | collective-permute-start | bytes 3538952 | tf_op jit(solution)/shard_map/ppermute | solution.py:792
  342.7 72.6 %collective-permute-start.4 = (bf16[4608,128]{1,0:T(8,128)(2,1)}, bf16[4608,128]{1,0:T(8,128)(2,1)}, u32[]{:S(2)}, u32[]{:S(2)}) collective-permute-start(bf16[4608,128]{1,0:T(8,128)(2,1)} %get-tuple-element.110), channel_id=1, source_target_pairs={{0,48},{16,32},{32,16},{48,0},{64,112},{80,96},{96,80},{112,64},{1... | collective-permute-start | bytes 3538952 | tf_op jit(solution)/shard_map/ppermute | solution.py:792
  345.9 70.6 %collective-permute-start.6 = (bf16[4608,128]{1,0:T(8,128)(2,1)}, bf16[4608,128]{1,0:T(8,128)(2,1)}, u32[]{:S(2)}, u32[]{:S(2)}) collective-permute-start(bf16[4608,128]{1,0:T(8,128)(2,1)} %copy-done.42), channel_id=1, source_target_pairs={{0,48},{16,32},{32,16},{48,0},{64,112},{80,96},{96,80},{112,64},{1... | collective-permute-start | bytes 3538952 | tf_op jit(solution)/shard_map/ppermute | solution.py:792
  373.1 43.4 %copy-start.20 = (bf16[4608,128]{1,0:T(8,128)(2,1)S(1)}, bf16[4608,128]{1,0:T(8,128)(2,1)}, u32[]{:S(2)}) copy-start(bf16[4608,128]{1,0:T(8,128)(2,1)} %get-tuple-element.107.p0) | copy-start | bytes 3538948
  373.1 43.4 %copy-start.21 = (bf16[4608,128]{1,0:T(8,128)(2,1)S(1)}, bf16[4608,128]{1,0:T(8,128)(2,1)}, u32[]{:S(2)}) copy-start(bf16[4608,128]{1,0:T(8,128)(2,1)} %get-tuple-element.108.p1) | copy-start | bytes 3538948
  376.6 47.2 %copy-start.24 = (bf16[16,256,128]{2,1,0:T(8,128)(2,1)}, bf16[16,256,128]{2,1,0:T(8,128)(2,1)S(1)}, u32[]{:S(2)}) copy-start(bf16[16,256,128]{2,1,0:T(8,128)(2,1)S(1)} %get-tuple-element.114) | copy-start | bytes 3145732
  416.4 7.3 %copy-start.51 = (bf16[8,2,128,128]{3,2,1,0:T(8,128)(2,1)S(1)}, bf16[8,2,128,128]{3,2,1,0:T(8,128)(2,1)}, u32[]{:S(2)}) copy-start(bf16[8,2,128,128]{3,2,1,0:T(8,128)(2,1)} %get-tuple-element.125) | copy-start | bytes 1572868
  420.8 57.3 %collective-permute-start.7 = (bf16[4608,128]{1,0:T(8,128)(2,1)}, bf16[4608,128]{1,0:T(8,128)(2,1)}, u32[]{:S(2)}, u32[]{:S(2)}) collective-permute-start(bf16[4608,128]{1,0:T(8,128)(2,1)} %get-tuple-element.117), channel_id=1, source_target_pairs={{0,64},{16,80},{32,96},{48,112},{64,0},{80,16},{96,32},{112,48},{1... | collective-permute-start | bytes 3538952 | tf_op jit(solution)/shard_map/ppermute | solution.py:792
  423.7 10.6 %copy-start.40 = (f32[1,1536]{1,0:T(1,128)S(1)}, f32[1,1536]{1,0:T(1,128)}, u32[]{:S(2)}) copy-start(f32[1,1536]{1,0:T(1,128)} %copy-done.39) | copy-start | bytes 18436
  423.7 10.8 %copy-start.6 = (bf16[8,2,128,128]{3,2,1,0:T(8,128)(2,1)S(1)}, bf16[8,2,128,128]{3,2,1,0:T(8,128)(2,1)}, u32[]{:S(2)}) copy-start(bf16[8,2,128,128]{3,2,1,0:T(8,128)(2,1)} %get-tuple-element.128.sact_ref) | copy-start | bytes 1572868
  423.8 10.7 %copy-start.11 = (bf16[128,1536]{1,0:T(8,128)(2,1)S(1)}, bf16[128,1536]{1,0:T(8,128)(2,1)}, u32[]{:S(2)}) copy-start(bf16[128,1536]{1,0:T(8,128)(2,1)} %copy-done.10) | copy-start | bytes 1179652
  423.8 10.7 %copy-start.13 = (bf16[8,2,128,128]{3,2,1,0:T(8,128)(2,1)S(1)}, bf16[8,2,128,128]{3,2,1,0:T(8,128)(2,1)}, u32[]{:S(2)}) copy-start(bf16[8,2,128,128]{3,2,1,0:T(8,128)(2,1)} %get-tuple-element.85.place_ref) | copy-start | bytes 1572868
  429.3 31.6 %all-to-all-start.5 = ((bf16[16,256,128]{2,1,0:T(8,128)(2,1)}), bf16[16,256,128]{2,1,0:T(8,128)(2,1)}, u32[]{:S(2)}, u32[]{:S(2)}) async-start(bf16[16,256,128]{2,1,0:T(8,128)(2,1)} %copy-done.24), calls=%async_computation.5 | async-start | bytes 2097152 | tf_op jit(solution)/shard_map/all_to_all | solution.py:702
  456.4 13.7 %copy-start.50 = (bf16[1536,128]{1,0:T(8,128)(2,1)S(1)}, bf16[1536,128]{1,0:T(8,128)(2,1)}, u32[]{:S(2)}) copy-start(bf16[1536,128]{1,0:T(8,128)(2,1)} %convolution_convert_fusion) | copy-start | bytes 1179652
  472.5 25.6 %all-to-all-start.6 = ((bf16[16,112,384]{2,1,0:T(8,128)(2,1)}), bf16[16,112,384]{2,1,0:T(8,128)(2,1)S(1)}, u32[]{:S(2)}, u32[]{:S(2)}) async-start(bf16[16,112,384]{2,1,0:T(8,128)(2,1)} %fusion.3), calls=%async_computation.6 | async-start | bytes 2752512 | tf_op jit(solution)/shard_map/all_to_all | solution.py:702
  480.3 72.3 %collective-permute-start.8 = (bf16[8,128,1536]{2,1,0:T(8,128)(2,1)}, bf16[8,128,1536]{2,1,0:T(8,128)(2,1)}, u32[]{:S(2)}, u32[]{:S(2)}) collective-permute-start(bf16[8,128,1536]{2,1,0:T(8,128)(2,1)} %slice_bitcast_fusion), channel_id=1, source_target_pairs={{0,1},{1,0},{2,3},{3,2},{4,5},{5,4},{6,7},{7,6},{8,9},{9,8},{10,11... | collective-permute-start | bytes 9437192 | tf_op jit(solution)/shard_map/ppermute | solution.py:838
  499.4 27.7 %all-to-all-start.7 = ((bf16[8,256,384]{2,1,0:T(8,128)(2,1)}), bf16[8,256,384]{2,1,0:T(8,128)(2,1)}, u32[]{:S(2)}, u32[]{:S(2)}) async-start(bf16[8,256,384]{2,1,0:T(8,128)(2,1)} %pad_maximum_fusion), calls=%async_computation.7 | async-start | bytes 3145728 | tf_op jit(solution)/shard_map/all_to_all | solution.py:702
  503.7 46.4 %collective-permute-start.9 = (bf16[4608,128]{1,0:T(8,128)(2,1)S(1)}, bf16[4608,128]{1,0:T(8,128)(2,1)S(1)}, u32[]{:S(2)}, u32[]{:S(2)}) collective-permute-start(bf16[4608,128]{1,0:T(8,128)(2,1)S(1)} %add_convert_fusion.refs_0_), channel_id=1, source_target_pairs={{0,16},{16,0},{32,48},{48,32},{64,80},{80,64},{96,112},{112,96},{1... | collective-permute-start | bytes 3538952 | tf_op jit(solution)/shard_map/ppermute | solution.py:792
  505.6 45.2 %collective-permute-start.10 = (bf16[4608,128]{1,0:T(8,128)(2,1)S(1)}, bf16[4608,128]{1,0:T(8,128)(2,1)}, u32[]{:S(2)}, u32[]{:S(2)}) collective-permute-start(bf16[4608,128]{1,0:T(8,128)(2,1)S(1)} %add_convert_fusion.refs_0_), channel_id=1, source_target_pairs={{0,48},{16,32},{32,16},{48,0},{64,112},{80,96},{96,80},{112,64},{1... | collective-permute-start | bytes 3538952 | tf_op jit(solution)/shard_map/ppermute | solution.py:792
  507.7 43.2 %collective-permute-start.11 = (bf16[4608,128]{1,0:T(8,128)(2,1)S(1)}, bf16[4608,128]{1,0:T(8,128)(2,1)}, u32[]{:S(2)}, u32[]{:S(2)}) collective-permute-start(bf16[4608,128]{1,0:T(8,128)(2,1)S(1)} %add_convert_fusion.refs_0_), channel_id=1, source_target_pairs={{0,64},{16,80},{32,96},{48,112},{64,0},{80,16},{96,32},{112,48},{1... | collective-permute-start | bytes 3538952 | tf_op jit(solution)/shard_map/ppermute | solution.py:792
  530.1 38.8 %all-to-all-start.9 = ((bf16[8,256,384]{2,1,0:T(8,128)(2,1)}), bf16[8,256,384]{2,1,0:T(8,128)(2,1)}, u32[]{:S(2)}, u32[]{:S(2)}) async-start(bf16[8,256,384]{2,1,0:T(8,128)(2,1)} %broadcast_in_dim.28), calls=%async_computation.9 | async-start | bytes 3145728 | tf_op jit(solution)/shard_map/all_to_all | solution.py:702
  550.9 41.7 %collective-permute-start.13 = (bf16[4608,128]{1,0:T(8,128)(2,1)}, bf16[4608,128]{1,0:T(8,128)(2,1)}, u32[]{:S(2)}, u32[]{:S(2)}) collective-permute-start(bf16[4608,128]{1,0:T(8,128)(2,1)} %collective-permute-done.11.refs_4_), channel_id=1, source_target_pairs={{0,16},{16,0},{32,48},{48,32},{64,80},{80,64},{96,112},{112,96},{1... | collective-permute-start | bytes 3538952 | tf_op jit(solution)/shard_map/ppermute | solution.py:792
  568.8 56.3 %all-to-all-start.8 = ((bf16[8,128,1536]{2,1,0:T(8,128)(2,1)}), bf16[8,128,1536]{2,1,0:T(8,128)(2,1)}, u32[]{:S(2)}, u32[]{:S(2)}) async-start(bf16[8,128,1536]{2,1,0:T(8,128)(2,1)} %fusion), calls=%async_computation.8 | async-start | bytes 6291456 | tf_op jit(solution)/shard_map/all_to_all | solution.py:702
  574.2 54.2 %collective-permute-start.15 = (bf16[4608,128]{1,0:T(8,128)(2,1)}, bf16[4608,128]{1,0:T(8,128)(2,1)}, u32[]{:S(2)}, u32[]{:S(2)}) collective-permute-start(bf16[4608,128]{1,0:T(8,128)(2,1)} %collective-permute-done.11.refs_4_), channel_id=1, source_target_pairs={{0,48},{16,32},{32,16},{48,0},{64,112},{80,96},{96,80},{112,64},{1... | collective-permute-start | bytes 3538952 | tf_op jit(solution)/shard_map/ppermute | solution.py:792
  578.9 49.5 %collective-permute-start.12 = (bf16[4608,128]{1,0:T(8,128)(2,1)}, bf16[4608,128]{1,0:T(8,128)(2,1)}, u32[]{:S(2)}, u32[]{:S(2)}) collective-permute-start(bf16[4608,128]{1,0:T(8,128)(2,1)} %collective-permute-done.10.refs_3_), channel_id=1, source_target_pairs={{0,16},{16,0},{32,48},{48,32},{64,80},{80,64},{96,112},{112,96},{1... | collective-permute-start | bytes 3538952 | tf_op jit(solution)/shard_map/ppermute | solution.py:792
  592.7 36.6 %collective-permute-start.14 = (bf16[4608,128]{1,0:T(8,128)(2,1)}, bf16[4608,128]{1,0:T(8,128)(2,1)}, u32[]{:S(2)}, u32[]{:S(2)}) collective-permute-start(bf16[4608,128]{1,0:T(8,128)(2,1)} %collective-permute-done.13.refs_5_), channel_id=1, source_target_pairs={{0,48},{16,32},{32,16},{48,0},{64,112},{80,96},{96,80},{112,64},{1... | collective-permute-start | bytes 3538952 | tf_op jit(solution)/shard_map/ppermute | solution.py:792
  (36 other events, 91.5 us)
Sparse Core Ops, SparseCore 0:
  12.2 112.3 all-gather.5
  126.8 45.2 all-gather.9
  174.4 43.1 all-gather.7
  219.8 43.1 all-gather.11
  317.0 65.0 all-gather.13

commit v5 on v4

--- a/solution.py
+++ b/solution.py
@@ -43,6 +43,10 @@
     return pltpu.CompilerParams(vmem_limit_bytes=mib * 1024 * 1024)
 
 
+def cost(us):
+    return pl.CostEstimate(flops=0, bytes_accessed=int(us * 3690000), transcendentals=0)
+
+
 def whole(shape):
     return pl.BlockSpec(shape, lambda *_: (0,) * len(shape), pipeline_mode=pl.Buffered(1))
 
@@ -106,6 +110,7 @@
             jax.ShapeDtypeStruct((BLOCK, WIDTH), f32),
             jax.ShapeDtypeStruct((HEADS * BLOCK, HEAD_DIM), f32),
         ],
+        cost_estimate=cost(6),
         compiler_params=params(48),
         name="attend",
     )(ctx_at, qkv, kv_all, kv_all)
@@ -149,6 +154,7 @@
             jax.ShapeDtypeStruct((BLOCK, WIDTH), bf16),
             jax.ShapeDtypeStruct((N_CTX, BLOCK, 2 * KV_WIDTH), bf16),
         ],
+        cost_estimate=cost(7),
         compiler_params=params(48),
         name="attend_back",
     )(ctx_at, qkv, grad_att, att_f, logs, kv_all, kv_all)
@@ -180,6 +186,7 @@
             jax.ShapeDtypeStruct((BLOCK, WIDTH), f32),
             jax.ShapeDtypeStruct((BLOCK, WIDTH), bf16),
         ],
+        cost_estimate=cost(2),
         compiler_params=params(32),
         name="middle_norm",
     )(attended, w_all, tokens, gain)
@@ -226,6 +233,7 @@
             jax.ShapeDtypeStruct((BLOCK, WIDTH), bf16),
             jax.ShapeDtypeStruct((1, WIDTH), f32),
         ],
+        cost_estimate=cost(5),
         compiler_params=params(48),
         name="middle_back",
     )(pieces, middle, upstream, gain, w_all)
@@ -305,6 +313,7 @@
             jax.ShapeDtypeStruct((HALF, 2, BLOCK, META), f32),
             jax.ShapeDtypeStruct((LOCAL_E, 2, ROWS, META), f32),
         ],
+        cost_estimate=cost(14),
         compiler_params=params(56),
         name="place_rows",
     )(exp_at, up_all, expert_down, shared_two)
@@ -395,6 +404,7 @@
             jax.ShapeDtypeStruct((HALF, 2, BLOCK, META), bf16),
             jax.ShapeDtypeStruct((HALF, 2, BLOCK, META), bf16),
         ],
+        cost_estimate=cost(28),
         compiler_params=params(60),
         name="expert_back",
     )(exp_at, hidden, place, geh, gsh, wg, wu, ws)
@@ -409,7 +419,7 @@
     for chip in range(HALF):
         at = chip * CAP
         stacked = jnp.concatenate([outs[0][at : at + CAP], gap, outs[1][at : at + CAP], gap], 0)
-        part_ref[0, chip] = (
+        part_ref[chip, 0] = (
             dg(place_ref[chip, 0], stacked, NN) + dg(sact_ref[chip, 0], sd_ref[...], NN)
         ).astype(bf16)
 
@@ -428,9 +438,10 @@
                 whole((LOCAL_E, FF_E, WIDTH)),
                 whole((2 * SHARED, WIDTH)),
             ],
-            out_specs=pl.BlockSpec((1, HALF, BLOCK, WIDTH), lambda s, at: (s, 0, 0, 0)),
+            out_specs=by_core(WIDTH),
         ),
-        out_shape=jax.ShapeDtypeStruct((2, HALF, BLOCK, WIDTH), bf16),
+        out_shape=jax.ShapeDtypeStruct((HALF, 2, BLOCK, WIDTH), bf16),
+        cost_estimate=cost(10),
         compiler_params=params(48),
         name="expert_output",
     )(exp_at, act, gate, place, sact, wd, sd)
@@ -448,8 +459,10 @@
     turned = jnp.concatenate([dq_ref[...].T, grad_kv.T], axis=0)
     turned_out = ga_ref[...].T
     for j in range(N_EXP):
-        cols_ref[j, :160] = turned[160 * j : 160 * j + 160]
-        cols_ref[j, 160:] = turned_out[96 * j : 96 * j + 96]
+        cols_ref[j, :128] = turned[128 * j : 128 * j + 128]
+        cols_ref[j, 128:160] = turned[2048 + 32 * j : 2048 + 32 * j + 32]
+        cols_ref[j, 160:192] = turned_out[1024 + 32 * j : 1024 + 32 * j + 32]
+        cols_ref[j, 192:] = turned_out[64 * j : 64 * j + 64]
 
 
 def turn_cols(dq, pieces, grad_attn):
@@ -459,6 +472,7 @@
             jax.ShapeDtypeStruct((BLOCK, WIDTH + 2 * KV_WIDTH), bf16),
             jax.ShapeDtypeStruct((N_EXP, 256, BLOCK), bf16),
         ],
+        cost_estimate=cost(2),
         compiler_params=params(32),
         name="turn_cols",
     )(dq, pieces, grad_attn)
@@ -490,27 +504,91 @@
             jax.ShapeDtypeStruct((BLOCK, WIDTH), bf16),
             jax.ShapeDtypeStruct((1, WIDTH), f32),
         ],
+        cost_estimate=cost(7),
         compiler_params=params(48),
         name="input_back",
     )(grad_qkv, w_all, w_all, tokens, gain, grad_middle)
 
 
-def cols_kernel(cols_ref, hidden_ref, att_ref, out_ref):
+def cols_kernel(cols_ref, rows_ref, gain_ref, shared_ref, out_ref):
     lhs = jnp.concatenate([cols_ref[j] for j in range(N_EXP)], axis=1)
     row = lax.broadcasted_iota(jnp.int32, (256, N_EXP * BLOCK), 0)
     zero = jnp.zeros_like(lhs)
-    attn = dg(jnp.where(row < 160, lhs, zero), hidden_ref[...], NN)
-    out = dg(jnp.where(row < 160, zero, lhs), att_ref[...], NN)
-    out_ref[...] = (attn + out).T.astype(bf16).reshape(N_EXP, 96, 256)
-
-
-def cols_grad(cols, hidden_all, att_all):
+    attn = dg(jnp.where(row < 160, lhs, zero), rows_ref[:, :WIDTH], NN)
+    out = dg(jnp.where(row < 160, zero, lhs), rows_ref[:, WIDTH:], NN)
+    out_ref[:, :96, :256] = (attn + out).T.astype(bf16).reshape(N_EXP, 96, 256)
+    out_ref[:, 96:, :256] = gain_ref[...]
+    out_ref[:, :96, 256:] = shared_ref[...]
+    out_ref[:, 96:, 256:] = jnp.zeros((N_EXP, 16, META), bf16)
+
+
+def cols_grad(cols, rows_all, gain_rows, shared_cols):
     return pl.pallas_call(
         cols_kernel,
-        out_shape=jax.ShapeDtypeStruct((N_EXP, 96, 256), bf16),
+        out_shape=jax.ShapeDtypeStruct((N_EXP, 112, 384), bf16),
+        cost_estimate=cost(9),
         compiler_params=params(56),
         name="cols_grad",
-    )(cols, hidden_all, att_all)
+    )(cols, rows_all, gain_rows, shared_cols)
+
+
+def finish_kernel(late_ref, gain_ref, q_ref, k_ref, v_ref, out_ref, sg_ref, su_ref, sd_ref):
+    lane = lax.broadcasted_iota(jnp.int32, (96, 128), 1)
+
+    def tile(j, m):
+        return late_ref[j // 2, 112 * (j % 2) : 112 * (j % 2) + 96, 128 * m : 128 * m + 128].astype(
+            f32
+        )
+
+    def half(a, b, first):
+        if first:
+            return jnp.where(lane < 64, a, pltpu.roll(b, 64, 1))
+        return jnp.where(lane < 64, pltpu.roll(a, 64, 1), b)
+
+    def quarter(tiles, start):
+        total = jnp.zeros((96, 128), f32)
+        for i, one in enumerate(tiles):
+            shift = (32 * i - start) % 128
+            moved = one if shift == 0 else pltpu.roll(one, shift, 1)
+            total = jnp.where((lane >= 32 * i) & (lane < 32 * i + 32), moved, total)
+        return total
+
+    gains = jnp.zeros((16, 128), f32)
+    for j in range(N_EXP):
+        at = 112 * (j % 2) + 96
+        gains = gains + late_ref[j // 2, at : at + 16, :128].astype(f32)
+        whole_tile = tile(j, 0)
+        if j < 12:
+            q_ref[:, 128 * j : 128 * j + 128] = whole_tile
+        else:
+            k_ref[:, 128 * (j - 12) : 128 * (j - 12) + 128] = whole_tile
+    gain_ref[...] = gains
+    for m in range(N_EXP // 2):
+        at = 128 * m
+        a, b = tile(2 * m, 2), tile(2 * m + 1, 2)
+        sg_ref[:, at : at + 128] = half(a, b, True)
+        su_ref[:, at : at + 128] = half(a, b, False)
+        out_ref[:, at : at + 128] = half(tile(2 * m, 1), tile(2 * m + 1, 1), False)
+    for m in range(N_EXP // 4):
+        at = 128 * m
+        tiles = [tile(4 * m + i, 1) for i in range(4)]
+        v_ref[:, at : at + 128] = quarter(tiles, 0)
+        out_ref[:, 1024 + at : 1024 + at + 128] = quarter(tiles, 32)
+    for c in range(N_CTX):
+        rows = late_ref[c, 224:].astype(f32)
+        for q in range(4):
+            sd_ref[8 * c : 8 * c + 8, 384 * q : 384 * q + 384] = rows[8 * q : 8 * q + 8]
+
+
+def finish(late):
+    shapes = [(16, 128), (96, 1536), (96, 512), (96, 512), (96, 1536), (96, 1024), (96, 1024)]
+    return pl.pallas_call(
+        finish_kernel,
+        out_shape=[jax.ShapeDtypeStruct(s, f32) for s in shapes + [(SHARED, WIDTH)]],
+        cost_estimate=cost(5),
+        compiler_params=params(32),
+        name="finish",
+    )(late)
 
 
 def norm_rows_kernel(x_ref, gain_ref, out_ref):
@@ -522,12 +600,14 @@
 def norm_rows(rows, gain):
     count = rows.shape[0]
     spec = pl.BlockSpec((1, BLOCK, WIDTH), lambda i: (i, 0, 0))
+    turned = pl.BlockSpec((1, BLOCK, WIDTH), lambda i: ((i % 2) * 4 + i // 2, 0, 0))
     return pl.pallas_call(
         norm_rows_kernel,
         grid=(count,),
         in_specs=[spec, whole((1, WIDTH))],
-        out_specs=spec,
+        out_specs=spec if count == 1 else turned,
         out_shape=jax.ShapeDtypeStruct(rows.shape, bf16),
+        cost_estimate=cost(2),
         compiler_params=params(32),
         name="norm_rows",
     )(rows, gain)
@@ -563,6 +643,7 @@
             jax.ShapeDtypeStruct((BLOCK, WIDTH), bf16),
             jax.ShapeDtypeStruct((N_CTX, BLOCK, 2 * KV_WIDTH), bf16),
         ],
+        cost_estimate=cost(8),
         compiler_params=params(48),
         name="project",
     )(own, seq, w_all)
@@ -571,63 +652,61 @@
 PIECE = 2 * WIDTH + WIDTH * BLOCK // HEAD_DIM
 
 
-def expert_weights_kernel(at_ref, x_ref, geo_ref, act_ref, dgate_ref, dup_ref, *refs):
-    outs, turned = refs[:8], refs[8]
+def expert_weights_kernel(
+    halves, at_ref, x_ref, geo_ref, act_ref, dgate_ref, dup_ref, *refs
+):
+    outs, turned = refs[:-1], refs[-1]
     step = pl.program_id(0)
 
-    @pl.when(step == 0)
+    @pl.when(step % 2 == 0)
     def _():
-        for e in range(LOCAL_E):
-            turned[e] = x_ref[e].T
-
-    for r in range(4):
-
-        @pl.when(step == r)
+        turned[...] = x_ref[0].T
+
+    rhs = jnp.concatenate([dgate_ref[0], dup_ref[0]], axis=1)
+    both = dg(turned[...], rhs, NN).astype(bf16)
+    down = dg(act_ref[0], geo_ref[0], TN).astype(bf16)
+    for i in range(4):
+
+        @pl.when(step == i)
         def _():
-            for side in range(2):
-                e = at_ref[1] if side == 0 else 1 - at_ref[1]
-                out = outs[2 * r + side]
-                rhs = jnp.concatenate([dgate_ref[e], dup_ref[e]], axis=1)
-                both = dg(turned[e], rhs, NN).astype(bf16)
-                out[:WIDTH] = both[:, :HEAD_DIM]
-                out[WIDTH : 2 * WIDTH] = both[:, HEAD_DIM:]
-                down = dg(act_ref[e], geo_ref[e], TN).astype(bf16)
-                for m in range(WIDTH // HEAD_DIM):
-                    at = 2 * WIDTH + m * BLOCK
-                    out[at : at + BLOCK] = down[:, m * HEAD_DIM : (m + 1) * HEAD_DIM]
-
-
-def expert_weights(at, arrived, grad_eo, act, grad_gu):
+            start = (i % 2) * PIECE if halves else 0
+            out = outs[i // 2 if halves else i].at[pl.ds(start, PIECE)]
+            out[:WIDTH] = both[:, :HEAD_DIM]
+            out[WIDTH : 2 * WIDTH] = both[:, HEAD_DIM:]
+            for m in range(WIDTH // HEAD_DIM):
+                at = 2 * WIDTH + m * BLOCK
+                out[at : at + BLOCK] = down[:, m * HEAD_DIM : (m + 1) * HEAD_DIM]
+
+
+def expert_weights(yz, steps, halves, arrived, grad_eo, act, grad_gu):
     rows = 2 * ROWS
-    lanes = lambda shift: pl.BlockSpec(
-        (LOCAL_E, rows, HEAD_DIM), lambda r, at: (0, 0, shift + (at[0] ^ r))
-    )
-    piece = jax.ShapeDtypeStruct((PIECE, HEAD_DIM), bf16)
-    return pl.pallas_call(
-        expert_weights_kernel,
+    at = jnp.stack([yz[0] ^ r for r, _ in steps] + [yz[1] ^ side for _, side in steps])
+    rows_of = pl.BlockSpec((1, rows, WIDTH), lambda s, at: (at[4 + s], 0, 0))
+
+    def lanes(shift):
+        return pl.BlockSpec((1, rows, HEAD_DIM), lambda s, at: (at[4 + s], 0, shift + at[s]))
+
+    count, length = (2, 2 * PIECE) if halves else (4, PIECE)
+    return pl.pallas_call(
+        lambda *refs: expert_weights_kernel(halves, *refs),
         grid_spec=pltpu.PrefetchScalarGridSpec(
             num_scalar_prefetch=1,
             grid=(4,),
-            in_specs=[
-                whole((LOCAL_E, rows, WIDTH)),
-                whole((LOCAL_E, rows, WIDTH)),
-                lanes(0),
-                lanes(0),
-                lanes(4),
-            ],
-            out_specs=[whole((PIECE, HEAD_DIM))] * 8,
-            scratch_shapes=[pltpu.VMEM((LOCAL_E, WIDTH, rows), bf16)],
+            in_specs=[rows_of, rows_of, lanes(0), lanes(0), lanes(4)],
+            out_specs=[whole((length, HEAD_DIM))] * count,
+            scratch_shapes=[pltpu.VMEM((WIDTH, rows), bf16)],
         ),
-        out_shape=[piece] * 8,
+        out_shape=[jax.ShapeDtypeStruct((length, HEAD_DIM), bf16)] * count,
+        cost_estimate=cost(9),
         compiler_params=params(56),
         name="expert_weights",
     )(at, arrived, grad_eo, act, grad_gu, grad_gu)
 
 
 def unpack_kernel(at_ref, *refs):
-    pieces, (gate_ref, up_ref, down_ref) = refs[:8], refs[8:]
+    pieces, (gate_ref, up_ref, down_ref) = refs[:4], refs[-3:]
     step = pl.program_id(0)
-    for i in range(8):
+    for i in range(4):
 
         @pl.when(step == i)
         def _():
@@ -641,61 +720,66 @@
                 )
 
 
-def unpack_experts(at, pieces):
-    cols = pl.BlockSpec(
-        (1, WIDTH, HEAD_DIM), lambda s, at: (at[1] ^ (s // 4), 0, at[0] ^ (s % 4))
-    )
+def unpack_experts(at, side, pieces, filled=()):
+    cols = pl.BlockSpec((1, WIDTH, HEAD_DIM), lambda s, at: (at[1] ^ side, 0, at[0] ^ s))
+    rows = pl.BlockSpec((1, BLOCK, WIDTH), lambda s, at: (at[1] ^ side, at[0] ^ s, 0))
+    anywhere = pl.BlockSpec(memory_space=pl.ANY)
     return pl.pallas_call(
         unpack_kernel,
         grid_spec=pltpu.PrefetchScalarGridSpec(
             num_scalar_prefetch=1,
-            grid=(8,),
-            in_specs=[whole((PIECE, HEAD_DIM))] * 8,
-            out_specs=[
-                cols,
-                cols,
-                pl.BlockSpec(
-                    (1, BLOCK, WIDTH), lambda s, at: (at[1] ^ (s // 4), at[0] ^ (s % 4), 0)
-                ),
-            ],
+            grid=(4,),
+            in_specs=[whole((PIECE, HEAD_DIM))] * 4 + [anywhere] * len(filled),
+            out_specs=[cols, cols, rows],
         ),
         out_shape=[
             jax.ShapeDtypeStruct((LOCAL_E, WIDTH, FF_E), f32),
             jax.ShapeDtypeStruct((LOCAL_E, WIDTH, FF_E), f32),
             jax.ShapeDtypeStruct((LOCAL_E, FF_E, WIDTH), f32),
         ],
+        input_output_aliases={5 + i: i for i in range(len(filled))},
+        cost_estimate=cost(5),
         compiler_params=params(48),
         name="unpack_experts",
-    )(at, *pieces)
-
-
-def relay_kernel(p3, p6, relay_a, relay_b, add_a, add_b):
+    )(at, *pieces, *filled)
+
+
+def relay_kernel(
+    p0, p1, p3, p6, relay_a, relay_b, got_10, got_31, add_a, add_b, part_0, part_1
+):
     add_a[...] = (p6[...].astype(f32) + relay_a[...].astype(f32)).astype(bf16)
     add_b[...] = (p3[...].astype(f32) + relay_b[...].astype(f32)).astype(bf16)
-
-
-def side_kernel(p0, p1, got_10, got_31, got_11, got_30, own, side):
-    own[...] = p0[...].astype(f32) + got_10[...].astype(f32) + got_30[...].astype(f32)
-    side[...] = (
-        p1[...].astype(f32) + got_31[...].astype(f32) + got_11[...].astype(f32)
-    ).astype(bf16)
+    part_0[...] = p0[...].astype(f32) + got_10[...].astype(f32)
+    part_1[...] = p1[...].astype(f32) + got_31[...].astype(f32)
+
+
+def side_kernel(part_0, part_1, got_11, got_30, own, side):
+    own[...] = part_0[...] + got_30[...].astype(f32)
+    side[...] = (part_1[...] + got_11[...].astype(f32)).astype(bf16)
 
 
 def piece_sums(kernel, kinds, *pieces):
-    spec = pl.BlockSpec((PIECE // 4, HEAD_DIM), lambda i: (i, 0))
+    specs, arrays = [], []
+    for piece in pieces:
+        array, second = piece if isinstance(piece, tuple) else (piece, 0)
+        specs.append(pl.BlockSpec((PIECE // 4, HEAD_DIM), lambda i, at=4 * second: (i + at, 0)))
+        arrays.append(array)
     return pl.pallas_call(
         kernel,
         grid=(4,),
-        in_specs=[spec] * len(pieces),
-        out_specs=[spec] * len(kinds),
+        in_specs=specs,
+        out_specs=[pl.BlockSpec((PIECE // 4, HEAD_DIM), lambda i: (i, 0))] * len(kinds),
         out_shape=[jax.ShapeDtypeStruct((PIECE, HEAD_DIM), kind) for kind in kinds],
+        cost_estimate=cost(4),
         compiler_params=params(32),
         name="piece_sums",
-    )(*pieces)
+    )(*arrays)
 
 
 same_core = [[2 * i + c for i in range(8)] for c in range(2)]
 core_swap = [(i, i ^ 1) for i in range(N_EXP)]
+y_groups = [[0, 1, 2, 3], [4, 5, 6, 7]]
+z_swap = [(i, i ^ 4) for i in range(N_CTX)]
 
 
 def swap_all(rows, axis, groups=None):
@@ -750,7 +834,14 @@
     gains = swap_all(jnp.broadcast_to(gains, (N_EXP, gains.shape[0])), "exp")
     gain_attn = gains[:, :96].reshape(1, WIDTH).astype(f32)
     gain_ffn = gains[:, 96:].reshape(1, WIDTH).astype(f32)
-    tokens_seq = swap_all(jnp.broadcast_to(tokens, (N_CTX, BLOCK, WIDTH)), "ctx")
+    tokens_z = lax.ppermute(after(tokens, w_cat), "ctx", z_swap)
+    pair = jnp.where(
+        z_at == 0,
+        jnp.concatenate([tokens, tokens_z], axis=0),
+        jnp.concatenate([tokens_z, tokens], axis=0),
+    )
+    tokens_seq = swap_all(jnp.broadcast_to(pair, (4, 2, BLOCK, WIDTH)), "ctx", y_groups)
+    tokens_seq = tokens_seq.reshape(N_CTX, BLOCK, WIDTH)
     shared_cols = jnp.concatenate(
         [shared_gate.reshape(96, N_EXP, SHARED), shared_up.reshape(96, N_EXP, SHARED)], axis=2
     ).transpose(1, 0, 2)
@@ -766,7 +857,12 @@
 
     hidden_all = lax.all_gather(hidden_two, "exp", axis=0, tiled=True)
     hidden_all = hidden_all.reshape(HALF, 2, BLOCK, WIDTH)
-    hidden_one_all = lax.all_gather(after(hidden_one[0], hidden_two), "exp", axis=0, tiled=True)
+    rows_all = lax.all_gather(
+        after(jnp.concatenate([hidden_one[0], attended], axis=1), hidden_two),
+        "exp",
+        axis=0,
+        tiled=True,
+    )
     place, grad_eo, grad_eh, grad_sh, slot_gate = place_rows(
         exp_s,
         after(up_all, hidden_two).reshape(HALF, 2, BLOCK, WIDTH + META),
@@ -780,93 +876,94 @@
     grad_two = swap_all(summed, "exp", same_core)
 
     rows_e = 2 * ROWS
-    p = expert_weights(
-        yz_s,
+    operands = (
         after(arrived, summed).reshape(LOCAL_E, rows_e, WIDTH),
         grad_eo.reshape(LOCAL_E, rows_e, WIDTH),
         act.reshape(LOCAL_E, rows_e, FF_E),
         grad_gu.reshape(LOCAL_E, rows_e, 2 * FF_E),
     )
+    for_1, for_3 = expert_weights(yz_s, ((2, 0), (1, 0), (2, 1), (3, 1)), True, *operands)
+    operands = (after(operands[0], for_1),) + operands[1:]
+    p0, p6, p1, p3 = expert_weights(yz_s, ((0, 0), (3, 0), (0, 1), (1, 1)), False, *operands)
 
     def to(rows, k):
         return lax.ppermute(rows, "ctx", [(i, i ^ k) for i in range(N_CTX)])
 
-    relay_a, relay_b, got_10, got_31 = to(p[4], 1), to(p[5], 3), to(p[2], 1), to(p[7], 3)
-    shared_grad_late = after(shared_grad, p[0]).reshape(N_EXP * BLOCK, META)
+    from_1, from_3 = to(for_1, 1), to(for_3, 3)
+    shared_grad_late = after(shared_grad, p0).reshape(N_EXP * BLOCK, META)
     grad_scols = dg(hidden_all.reshape(N_EXP * BLOCK, WIDTH), shared_grad_late, TN).astype(bf16)
-    act_late = after(shared_act, p[0]).reshape(N_EXP * BLOCK, META)
+    act_late = after(shared_act, p0).reshape(N_EXP * BLOCK, META)
     grad_sdown = dg(act_late, up_all, TN)[:SHARED, :WIDTH].astype(bf16)
 
-    add_a, add_b = piece_sums(relay_kernel, (bf16, bf16), p[3], p[6], relay_a, relay_b)
-    got_11, got_30 = to(add_b, 1), to(add_a, 3)
-    grad_two = after(grad_two, add_a)
+    out_part = expert_output(
+        exp_s, after(act, p0), slot_gate, place, shared_act, expert_down, shared_two
+    )
+
+    grad_two = after(grad_two, out_part)
     grad_middle, grad_attn, grad_heads, grad_gain_ffn = middle_back(
         grad_two, middle, cotangent[0], gain_ffn, w_all
     )
-    att_all = lax.all_gather(after(attended, grad_two), "exp", axis=0, tiled=True)
     grad_query, part_kv = attend_back(ctx_s, queries, grad_heads, att_f, logs, kv_all)
-    kv_pieces = swap_all(part_kv, "ctx")
-
-    out_part = expert_output(
-        exp_s, after(act, part_kv), slot_gate, place, shared_act, expert_down, shared_two
-    )
+
+    from_1, from_3 = after((from_1, from_3), grad_heads)
+    add_a, add_b, part_0, part_1 = piece_sums(
+        relay_kernel,
+        (bf16, bf16, f32, f32),
+        p0,
+        p1,
+        p3,
+        p6,
+        (from_1, 0),
+        (from_3, 0),
+        (from_1, 1),
+        (from_3, 1),
+    )
+    got_11, got_30 = to(add_b, 1), to(add_a, 3)
+    kv_pieces = swap_all(after(part_kv, add_a), "ctx")
 
     grad_qkv, cols_sent = turn_cols(grad_query, kv_pieces, grad_attn)
     cols = swap_all(cols_sent, "exp")
-    own_part, side = piece_sums(
-        side_kernel, (f32, bf16), p[0], p[1], got_10, got_31, after(got_11, cols_sent), got_30
-    )
-    across = to(side, 4)
     input_grad, grad_gain_attn = input_back(
         grad_qkv, w_all, tokens[0], gain_attn, grad_middle
     )
-    grad_cols = cols_grad(cols, hidden_one_all, att_all)
+    cols = after(cols, input_grad)
+    own_part, side = piece_sums(
+        side_kernel, (f32, bf16), part_0, part_1, after(got_11, cols), got_30
+    )
+    across = to(side, 4)
     gain_rows = jnp.concatenate(
         [grad_gain_attn.reshape(N_EXP, 1, 96), grad_gain_ffn.reshape(N_EXP, 1, 96)], axis=1
     ).astype(bf16)
     gain_rows = jnp.pad(gain_rows, ((0, 0), (0, 14), (0, 160)))
-    sent = jnp.concatenate(
-        [
-            jnp.concatenate([grad_cols, gain_rows], axis=1),
-            jnp.pad(grad_scols.reshape(N_EXP, 96, META), ((0, 0), (0, 16), (0, 0))),
-        ],
-        axis=2,
+    sent = cols_grad(
+        after(cols, side),
+        rows_all,
+        gain_rows,
+        grad_scols.reshape(N_EXP, 96, META),
     )
     back = swap_all(sent, "exp")
     own = (own_part + after(across, sent).astype(f32)).astype(bf16)
     at_1, at_3, at_z = to(own, 1), to(own, 3), to(own, 4)
-    out_other = lax.ppermute(after(out_part[0], own), "exp", core_swap)
-    out_sum = add_low(out_part[1], out_other)
-
+
+    sdown_rows = grad_sdown.reshape(N_CTX, 8, 4, 384).transpose(0, 2, 1, 3)
     small = jnp.concatenate(
-        [back.reshape(N_CTX, 224, 384), grad_sdown.reshape(N_CTX, 32, 384)], axis=1
-    )
+        [back.reshape(N_CTX, 224, 384), sdown_rows.reshape(N_CTX, 32, 384)], axis=1
+    )
+    small, at_1, at_3, at_z = lax.optimization_barrier((small, at_1, at_3, at_z))
     pieces = swap_all(small, "ctx")
+    at_z1, at_z3 = to(at_z, 1), to(at_z, 3)
     late_own = jnp.sum(pieces.astype(f32), axis=0).astype(bf16)
+    late_own, at_z1, at_z3 = lax.optimization_barrier((late_own, at_z1, at_z3))
     late = swap_all(jnp.broadcast_to(late_own, (N_CTX, 256, 384)), "ctx")
-    at_1, at_3, at_z = after((at_1, at_3, at_z), late_own)
-    at_2, at_z1, at_z3 = to(at_3, 1), to(at_z, 1), to(at_z, 3)
-    out_pieces = swap_all(after(out_sum, late_own), "exp", same_core)
-    at_z2 = to(at_z1, 3)
-    mixed = (middle + jnp.sum(out_pieces.astype(f32), axis=0)).astype(bf16)[None]
-    grad_sdown = late[:, 224:].reshape(SHARED, WIDTH).astype(f32)
-    late = late[:, :224].reshape(N_EXP, 112, 384)
-    grad_wqkv = late[:, :96, :160].transpose(1, 0, 2).reshape(96, WIDTH + 2 * KV_WIDTH)
-    gain_sum = jnp.sum(late[:, 96:98, :96].astype(f32), axis=0)
-    dense = (
-        gain_sum[0],
-        gain_sum[1],
-        grad_wqkv[:, :WIDTH].astype(f32),
-        grad_wqkv[:, WIDTH : WIDTH + KV_WIDTH].astype(f32),
-        grad_wqkv[:, WIDTH + KV_WIDTH :].astype(f32),
-        late[:, :96, 160:256].transpose(1, 0, 2).reshape(96, WIDTH).astype(f32),
-        late[:, :96, 256 : 256 + SHARED].transpose(1, 0, 2).reshape(96, 1024).astype(f32),
-        late[:, :96, 256 + SHARED :].transpose(1, 0, 2).reshape(96, 1024).astype(f32),
-        grad_sdown,
-    )
-    own = after(own, mixed, *dense)
-    experts = unpack_experts(yz_s, (own, at_1, at_2, at_3, at_z, at_z1, at_z2, at_z3))
-    return (mixed, input_grad[None]) + dense + tuple(experts)
+    at_2, at_z2 = to(after(at_3, late_own), 1), to(at_z1, 3)
+    gain_sum, *dense = finish(late)
+    out_rows = lax.psum_scatter(
+        after(out_part, own).reshape(N_EXP * BLOCK, WIDTH), "exp", scatter_dimension=0, tiled=True
+    )
+    mixed = (middle + out_rows.astype(f32)).astype(bf16)[None]
+    near = unpack_experts(yz_s, 0, after((own, at_1, at_2, at_3), mixed, *dense))
+    experts = unpack_experts(yz_s, 1, (at_z, at_z1, at_z2, at_z3), near)
+    return (mixed, input_grad[None], gain_sum[0, :96], gain_sum[1, :96], *dense, *experts)
 
 
 def solution(mesh):

time: 655 us -> 622 us (0.950)
  local copies, waits for them, and re-layouts: 72.2 us -> 46.9 us
  other arithmetic: 30.5 us -> 13.6 us
  Pallas kernels: 132 us -> 147 us
  blocking collectives: 11.7 us -> 0 us
    all_to_all x9, waiting for transfers between devices: 117 us -> 145 us  [swap_all(): lax.all_to_all(rows, axis, split_axis=0, concat_axis=0, tiled=True, axis_...]
    all_gather x1, waiting for transfers between devices: 25.8 us -> 1.74 us  [on_device(): w_all = lax.all_gather(w_cat, 'exp', axis=0, tiled=True)]
    unnamed x122 -> x129, local copies, waits for them, and re-layouts: 46.9 us -> 34.1 us
    pallas_call x4 -> x6, Pallas kernels: 32.5 us -> 44.9 us  [the longest x2 26.6 us: expert_weights(): pl.pallas_call(lambda *refs: expert_weights_kernel(halves, *refs), grid_s...]
    all_to_all x1 -> x0, blocking collectives: 11.7 us -> none  [swap_all(): lax.all_to_all(rows, axis, split_axis=0, concat_axis=0, tiled=True, axis_...]
    convert_element_type x5 -> x0, local copies, waits for them, and re-layouts: 7.72 us -> none  [the longest x2 3.67 us: on_device(): late[:, :96, 160:256].transpose(1, 0, 2).reshape(96, WIDTH).astype(f32)]
    convert_element_type x5 -> x0, other arithmetic: 7.47 us -> none  [the longest x1 2.56 us: on_device(): late[:, :96, 256 + SHARED:].transpose(1, 0, 2).reshape(96, 1024).astype(f32)]
    ppermute x14 -> x12, waiting for transfers between devices: 97.8 us -> 91.5 us  [to(): return lax.ppermute(rows, 'ctx', [(i, i ^ k) for i in range(N_CTX)])]
  transfers between devices with their start and end apart: 30 -> 28, of which waited for: 21 -> 21; matrix products, arithmetic and copies ran while one was open for 12% -> 6% of each run, Pallas kernels for 19% -> 23%
where the time goes in v5:
time: 622 us; the launch traced here: 614 us
  waiting for transfers between devices  302 us (49%)
  Pallas kernels  147 us (24%)
  starting transfers between devices  80 us (13%)
  local copies, waits for them, and re-layouts  46.9 us (8%)
  between operations  14.7 us (2%)
  other arithmetic  13.6 us (2%)
  matrix products  9.47 us (2%)
    all_to_all x9, waiting for transfers between devices, swap_all(): lax.all_to_all(rows, axis, split_axis=0, concat_axis=0, tiled=True, axis_...  145 us
    ppermute x12, waiting for transfers between devices, to(): return lax.ppermute(rows, 'ctx', [(i, i ^ k) for i in range(N_CTX)])  91.5 us
    all_to_all x9, starting transfers between devices, swap_all(): lax.all_to_all(rows, axis, split_axis=0, concat_axis=0, tiled=True, axis_...  51.7 us
    unnamed x129, local copies, waits for them, and re-layouts  34.1 us
    all_gather x1, waiting for transfers between devices, on_device(): hidden_all = lax.all_gather(hidden_two, 'exp', axis=0, tiled=True)  31.6 us
    pallas_call x1, Pallas kernels, expert_back(): pl.pallas_call(expert_kernel, grid_spec=pltpu.PrefetchScalarGridSpec(num_...  28.8 us
    pallas_call x2, Pallas kernels, expert_weights(): pl.pallas_call(lambda *refs: expert_weights_kernel(halves, *refs), grid_s...  26.6 us
    ppermute x12, starting transfers between devices, to(): return lax.ppermute(rows, 'ctx', [(i, i ^ k) for i in range(N_CTX)])  23.8 us
  transfers between devices with their start and end apart: 28, of which 21 were waited for; matrix products, arithmetic and copies ran while one was open for 6% of the time, Pallas kernels for 23%

profile of v5, /device:TPU:0, one launch (start us, length us, event | category | flops | bytes accessed | tf_op | source)
XLA Modules:
  0.0 613.9 jit_solution(962049014807474340)
XLA Ops:
  13.3 4.1 collective-permute-start
  18.0 4.8 all-to-all-start
  22.9 6.1 %collective-permute-done = bf16[1,128,1536]{2,1,0:T(8,128)(2,1)S(1)} collective-permute-done((bf16[1,128,1536]{2,1,0:T(8,128)(2,1)S(1)}, bf16[1,128,1536]{2,1,0:T(8,128)(2,1)S(1)}, u32[]{:S(2)}, u32[]{:S(2)}) %collective-permute-start) | collective-permute-done | bytes 393248 | tf_op jit(solution)/shard_map/ppermute | solution.py:837
  31.7 4.6 all-to-all-start.1
  43.9 30.5 %all-to-all-done.1 = bf16[4,2,128,1536]{3,2,1,0:T(8,128)(2,1)S(1)} async-done(((bf16[4,2,128,1536]{3,2,1,0:T(8,128)(2,1)}), bf16[4,2,128,1536]{3,2,1,0:T(8,128)(2,1)S(1)}, u32[]{:S(2)}, u32[]{:S(2)}) %all-to-all-start.1) | async-done | bytes 3145760 | tf_op jit(solution)/shard_map/all_to_all | solution.py:786
  74.3 5.2 all-to-all-start.2
  85.3 5.1 all-to-all-done.2
  95.1 7.7 %project.1 = (bf16[128,1536]{1,0:T(8,128)(2,1)S(1)}, bf16[8,128,1024]{2,1,0:T(8,128)(2,1)S(1)}) custom-call(bf16[1,128,1536]{2,1,0:T(8,128)(2,1)S(1)} %copy-done.9, bf16[8,128,1536]{2,1,0:T(8,128)(2,1)S(1)} %copy-done.4, bf16[1536,4096]{1,0:T(8,128)(2,1)} %all-gather.5.cloned.1.call-done.w_ref.wq_ref.wkv_ref), custom_call_target="tpu_custom_call" | custom-call | bytes 29520000 | tf_op jit(solution)/shard_map/project/pallas_call | solution.py:630
  102.8 5.8 attend.1
  108.6 5.4 copy-done
  117.8 20.8 %all-gather.9.cloned.1.call-done = bf16[2048,1664]{1,0:T(8,128)(2,1)} async-done(((bf16[128,1664]{1,0:T(8,128)(2,1)}), bf16[2048,1664]{1,0:T(8,128)(2,1)}) %all-gather.9.cloned.1.call-update) | async-done | bytes 6815760 | tf_op jit(solution)/shard_map/all_gather | solution.py:832
  138.6 13.9 %place_rows.1 = (bf16[8,2,128,128]{3,2,1,0:T(8,128)(2,1)}, bf16[2,2,384,1536]{3,2,1,0:T(8,128)(2,1)}, f32[2,2,384,512]{3,2,1,0:T(8,128)}, f32[8,2,128,128]{3,2,1,0:T(8,128)}, f32[2,2,384,128]{3,2,1,0:T(8,128)}) custom-call(s32[1]{0:T(128)} %bitcast.7.at_ref, bf16[8,2,128,1664]{3,2,1,0:T(8,128)(2,1)} %bitcast.69, bf16[2,512,1536]{2,1,0:T(8,128)(2,1)} %wd_ref.1, ...), custom_call_target="tpu_custom_call" | custom-call | bytes 51660000 | tf_op jit(solution)/shard_map/place_rows/pallas_call | solution.py:297
  152.5 31.6 %all-gather.7.cloned.1.call-done = bf16[2048,1536]{1,0:T(8,128)(2,1)} async-done(((bf16[128,1536]{1,0:T(8,128)(2,1)}), bf16[2048,1536]{1,0:T(8,128)(2,1)}) %all-gather.7.cloned.1.call-update) | async-done | bytes 6291472 | tf_op jit(solution)/shard_map/all_gather | solution.py:858
  184.1 28.8 %expert_back.1 = (bf16[2,8,128,1536]{3,2,1,0:T(8,128)(2,1)}, bf16[2,2,384,1536]{3,2,1,0:T(8,128)(2,1)}, bf16[2,2,384,512]{3,2,1,0:T(8,128)(2,1)}, bf16[2,2,384,1...) custom-call(s32[1]{0:T(128)} %bitcast.7.at_ref, ...), custom_call_target="tpu_custom_call" | custom-call | bytes 103320000 | tf_op jit(solution)/shard_map/expert_back/pallas_call | solution.py:376
  215.6 5.5 collective-permute-done.1
  223.6 4.8 all-to-all-start.3
  229.1 13.1 %expert_weights.2 = (bf16[9216,128]{1,0:T(8,128)(2,1)}, bf16[9216,128]{1,0:T(8,128)(2,1)}) custom-call(s32[8]{0:T(128)} %stack.40.refs_0_, bf16[2,768,1536]{2,1,0:T(8,128)(2,1)} %bitcast.77, bf16[2,768,1536]{2,1,0:T(8,128)(2,1)} %bitcast.75, bf16[2,768,512]{2,1,0:T(8,128)(2,1)} %bitcast.60, bf16[2,768,1024]{2,1,0:T(8,128)(2,1)} %bitcast.70, ...), custom_call_target="tpu_custom_call" | custom-call | bytes 33210000 | tf_op jit(solution)/shard_map/expert_weights/pallas_call | solution.py:690
  246.4 13.5 %expert_weights.3 = (bf16[4608,128]{1,0:T(8,128)(2,1)}, bf16[4608,128]{1,0:T(8,128)(2,1)}, bf16[4608,128]{1,0:T(8,128)(2,1)}, bf16[4608,128]{1,0:T(8,128)(2,1)}) custom-call(s32[8]{0:T(128)} %stack.38.refs_0_, bf16[2,768,1536]{2,1,0:T(8,128)(2,1)} %bitcast.78, bf16[2,768,1536]{2,1,0:T(8,128)(2,1)} %bitcast.76, bf16[2,768,512]{2,1,0:T(8,128)(2,1)} %bitcast.61, ...), custom_call_target="tpu_custom_call" | custom-call | bytes 33210000 | tf_op jit(solution)/shard_map/expert_weights/pallas_call | solution.py:690
  259.9 9.8 %expert_output.1 = bf16[8,2,128,1536]{3,2,1,0:T(8,128)(2,1)} custom-call(s32[1]{0:T(128)} %bitcast.7.at_ref, bf16[2,2,384,512]{3,2,1,0:T(8,128)(2,1)S(1)} %copy-done.2, f32[2,2,384,128]{3,2,1,0:T(8,128)S(1)} %copy-done.36, bf16[8,2,128,128]{3,2,1,0:T(8,128)(2,1)S(1)} %copy-done.22, bf16[8,2,128,128]{3,2,1,0:T(8,128)(2,1)S(1)} %copy-done.6, ...), custom_call_target="tpu_custom_call" | custom-call | bytes 36900000 | tf_op jit(solution)/shard_map/expert_output/pallas_call | solution.py:428
  269.8 23.7 %all-to-all-done.3.pieces_ref = bf16[8,128,1536]{2,1,0:T(8,128)(2,1)S(1)} async-done(((bf16[8,128,1536]{2,1,0:T(8,128)(2,1)}), bf16[8,128,1536]{2,1,0:T(8,128)(2,1)S(1)}, u32[]{:S(2)}, u32[]{:S(2)}) %all-to-all-start.3) | async-done | bytes 3145760 | tf_op jit(solution)/shard_map/all_to_all | solution.py:786
  295.6 4.8 middle_back.1
  302.0 7.0 %attend_back.1 = (bf16[128,1536]{1,0:T(8,128)(2,1)S(1)}, bf16[8,128,1024]{2,1,0:T(8,128)(2,1)S(1)}) custom-call(s32[1]{0:T(128)} %bitcast.ctx_ref, bf16[128,1536]{1,0:T(8,128)(2,1)S(1)} %copy-done.25, bf16[128,1536]{1,0:T(8,128)(2,1)S(1)} %get-tuple-element.130.ga_ref, f32[128,1536]{1,0:T(8,128)S(1)} %copy-done.38, f32[1536,128]{1,0:T(8,128)S(1)} %copy-done.40, ...), custom_call_target="tpu_custom_call" | custom-call | bytes 25830000 | tf_op jit(solution)/shard_map/attend_back/pallas_call | solution.py:141
  309.1 4.3 piece_sums.2
  318.2 6.9 %all-to-all-start.4 = ((bf16[8,128,1024]{2,1,0:T(8,128)(2,1)}), bf16[8,128,1024]{2,1,0:T(8,128)(2,1)S(1)}, u32[]{:S(2)}, u32[]{:S(2)}) async-start(bf16[8,128,1024]{2,1,0:T(8,128)(2,1)} %copy-done.23), calls=%async_computation.4 | async-start | bytes 4194304 | tf_op jit(solution)/shard_map/all_to_all | solution.py:786
  329.2 24.7 %all-to-all-done.4.pieces_ref = bf16[8,128,1024]{2,1,0:T(8,128)(2,1)S(1)} async-done(((bf16[8,128,1024]{2,1,0:T(8,128)(2,1)}), bf16[8,128,1024]{2,1,0:T(8,128)(2,1)S(1)}, u32[]{:S(2)}, u32[]{:S(2)}) %all-to-all-start.4) | async-done | bytes 2097184 | tf_op jit(solution)/shard_map/all_to_all | solution.py:786
  358.3 4.4 all-to-all-start.5
  363.8 7.0 %input_back.1 = (bf16[128,1536]{1,0:T(8,128)(2,1)}, f32[1,1536]{1,0:T(1,128)S(1)}) custom-call(bf16[128,2560]{1,0:T(8,128)(2,1)S(1)} %copy-done.42, bf16[1536,4096]{1,0:T(8,128)(2,1)} %all-gather.5.cloned.1.call-done.w_ref.wq_ref.wkv_ref, bf16[1536,4096]{1,0:T(8,128)(2,1)} %all-gather.5.cloned.1.call-done.w_ref.wq_ref.wkv_ref, ...), custom_call_target="tpu_custom_call" | custom-call | bytes 25830000 | tf_op jit(solution)/shard_map/input_back/pallas_call | solution.py:491
  370.9 8.3 %all-to-all-done.5.cols_ref = bf16[16,256,128]{2,1,0:T(8,128)(2,1)} async-done(((bf16[16,256,128]{2,1,0:T(8,128)(2,1)}), bf16[16,256,128]{2,1,0:T(8,128)(2,1)}, u32[]{:S(2)}, u32[]{:S(2)}) %all-to-all-start.5) | async-done | bytes 1048608 | tf_op jit(solution)/shard_map/all_to_all | solution.py:786
  380.9 2.6 piece_sums.3
  385.5 5.4 convolution_convert_fusion
  391.8 9.6 %cols_grad.1 = bf16[16,112,384]{2,1,0:T(8,128)(2,1)} custom-call(bf16[16,256,128]{2,1,0:T(8,128)(2,1)} %all-to-all-done.5.cols_ref, bf16[2048,3072]{1,0:T(8,128)(2,1)} %all-gather.11.cloned.1.call-done.rows_ref, bf16[16,16,256]{2,1,0:T(8,128)(2,1)} %fusion.7.gain_ref, bf16[16,96,128]{2,1,0:T(8,128)(2,1)} %bitcast.83), custom_call_target="tpu_custom_call" | custom-call | bytes 33210000 | tf_op jit(solution)/shard_map/cols_grad/pallas_call | solution.py:526
  401.4 11.3 %collective-permute-done.6 = bf16[4608,128]{1,0:T(8,128)(2,1)S(1)} collective-permute-done((bf16[4608,128]{1,0:T(8,128)(2,1)S(1)}, bf16[4608,128]{1,0:T(8,128)(2,1)S(1)}, u32[]{:S(2)}, u32[]{:S(2)}) %collective-permute-start.6) | collective-permute-done | bytes 1179680 | tf_op jit(solution)/shard_map/ppermute | solution.py:890
  413.0 4.5 all-to-all-start.6
  420.6 3.0 collective-permute-start.9
  423.6 4.1 fusion.9
  427.7 11.7 %all-to-all-done.6 = bf16[16,112,384]{2,1,0:T(8,128)(2,1)} async-done(((bf16[16,112,384]{2,1,0:T(8,128)(2,1)}), bf16[16,112,384]{2,1,0:T(8,128)(2,1)}, u32[]{:S(2)}, u32[]{:S(2)}) %all-to-all-start.6) | async-done | bytes 1376288 | tf_op jit(solution)/shard_map/all_to_all | solution.py:786
  439.4 2.7 pad_maximum_fusion
  442.0 4.0 collective-permute-done.7.refs_1_
  446.1 2.7 collective-permute-done.8.refs_3_
  448.7 39.9 %collective-permute-done.9.refs_0_ = bf16[4608,128]{1,0:T(8,128)(2,1)} collective-permute-done((bf16[4608,128]{1,0:T(8,128)(2,1)S(1)}, bf16[4608,128]{1,0:T(8,128)(2,1)}, u32[]{:S(2)}, u32[]{:S(2)}) %collective-permute-start.9) | collective-permute-done | bytes 1179680 | tf_op jit(solution)/shard_map/ppermute | solution.py:890
  488.7 7.0 %all-to-all-start.7 = ((bf16[8,256,384]{2,1,0:T(8,128)(2,1)}), bf16[8,256,384]{2,1,0:T(8,128)(2,1)}, u32[]{:S(2)}, u32[]{:S(2)}) async-start(bf16[8,256,384]{2,1,0:T(8,128)(2,1)} %pad_maximum_fusion), calls=%async_computation.8 | async-start | bytes 3145728 | tf_op jit(solution)/shard_map/all_to_all | solution.py:786
  499.8 23.2 %all-to-all-done.7 = bf16[8,256,384]{2,1,0:T(8,128)(2,1)} async-done(((bf16[8,256,384]{2,1,0:T(8,128)(2,1)}), bf16[8,256,384]{2,1,0:T(8,128)(2,1)}, u32[]{:S(2)}, u32[]{:S(2)}) %all-to-all-start.7) | async-done | bytes 1572896 | tf_op jit(solution)/shard_map/all_to_all | solution.py:786
  524.6 15.8 %collective-permute-done.10.refs_1_ = bf16[4608,128]{1,0:T(8,128)(2,1)S(1)} collective-permute-done((bf16[4608,128]{1,0:T(8,128)(2,1)}, bf16[4608,128]{1,0:T(8,128)(2,1)S(1)}, u32[]{:S(2)}, u32[]{:S(2)}) %collective-permute-start.10) | collective-permute-done | bytes 1179680 | tf_op jit(solution)/shard_map/ppermute | solution.py:890
  542.2 9.4 %all-to-all-start.8 = ((bf16[8,256,384]{2,1,0:T(8,128)(2,1)}), bf16[8,256,384]{2,1,0:T(8,128)(2,1)S(1)}, u32[]{:S(2)}, u32[]{:S(2)}) async-start(bf16[8,256,384]{2,1,0:T(8,128)(2,1)} %broadcast_in_dim.23), calls=%async_computation.9 | async-start | bytes 3145728 | tf_op jit(solution)/shard_map/all_to_all | solution.py:786
  555.7 17.1 %all-to-all-done.8.late_ref = bf16[8,256,384]{2,1,0:T(8,128)(2,1)S(1)} async-done(((bf16[8,256,384]{2,1,0:T(8,128)(2,1)}), bf16[8,256,384]{2,1,0:T(8,128)(2,1)S(1)}, u32[]{:S(2)}, u32[]{:S(2)}) %all-to-all-start.8) | async-done | bytes 1572896 | tf_op jit(solution)/shard_map/all_to_all | solution.py:786
  576.9 17.3 %collective-permute-done.13.refs_2_ = bf16[4608,128]{1,0:T(8,128)(2,1)} collective-permute-done((bf16[4608,128]{1,0:T(8,128)(2,1)}, bf16[4608,128]{1,0:T(8,128)(2,1)}, u32[]{:S(2)}, u32[]{:S(2)}) %collective-permute-start.13) | collective-permute-done | bytes 1179680 | tf_op jit(solution)/shard_map/ppermute | solution.py:890
  594.2 6.5 %unpack_experts.2 = (f32[2,1536,512]{2,1,0:T(8,128)}, f32[2,1536,512]{2,1,0:T(8,128)}, f32[2,512,1536]{2,1,0:T(8,128)}) custom-call(s32[2]{0:T(128)S(1)} %pad_add_fusion.at_ref, bf16[4608,128]{1,0:T(8,128)(2,1)S(1)} %add_convert_fusion.refs_0_, bf16[4608,128]{1,0:T(8,128)(2,1)} %collective-permute-done.7.refs_1_, ...), custom_call_target="tpu_custom_call" | custom-call | bytes 18450000 | tf_op jit(solution)/shard_map/unpack_experts/pallas_call | solution.py:727
  600.7 6.5 %unpack_experts.3 = (f32[2,1536,512]{2,1,0:T(8,128)}, f32[2,1536,512]{2,1,0:T(8,128)}, f32[2,512,1536]{2,1,0:T(8,128)}) custom-call(s32[2]{0:T(128)S(1)} %pad_add_fusion.at_ref, bf16[4608,128]{1,0:T(8,128)(2,1)} %collective-permute-done.9.refs_0_, bf16[4608,128]{1,0:T(8,128)(2,1)S(1)} %copy-done.29, ...), custom_call_target="tpu_custom_call", output_to_operand_aliasing={{0}: (5, {}), {1}: (6, {}), {2}: (7, {})} | custom-call | bytes 18450000 | tf_op jit(solution)/shard_map/unpack_experts/pallas_call | solution.py:727
  (197 shorter events, 82.6 us)
Async XLA Ops:
  7.2 10.1 %copy-start.59 = (bf16[96]{0:T(256)(128)(2,1)S(1)}, bf16[96]{0:T(256)(128)(2,1)}, u32[]{:S(2)}) copy-start(bf16[96]{0:T(256)(128)(2,1)} %param.19) | copy-start | bytes 580
  7.2 10.1 %copy-start.58 = (bf16[96]{0:T(256)(128)(2,1)S(1)}, bf16[96]{0:T(256)(128)(2,1)}, u32[]{:S(2)}) copy-start(bf16[96]{0:T(256)(128)(2,1)} %param.20) | copy-start | bytes 580
  7.2 85.0 %all-gather.5.cloned.1.call-start = ((), (), s32[]{:S(2)}) async-start(), calls=%async_computation.10 | async-start | bytes 13369344 | tf_op jit(solution)/shard_map/all_gather | solution.py:825
  12.0 126.6 %all-gather.9.cloned.1.call-start = ((), (), s32[]{:S(2)}) async-start(), calls=%async_computation.12 | async-start | bytes 7241728 | tf_op jit(solution)/shard_map/all_gather | solution.py:832
  13.3 15.8 %collective-permute-start = (bf16[1,128,1536]{2,1,0:T(8,128)(2,1)S(1)}, bf16[1,128,1536]{2,1,0:T(8,128)(2,1)S(1)}, u32[]{:S(2)}, u32[]{:S(2)}) collective-permute-start(bf16[1,128,1536]{2,1,0:T(8,128)(2,1)S(1)} %copy-done.5), channel_id=1, source_target_pairs={{0,64},{16,80},{32,96},{48,112},{64,0},{80,16},{96,32},{112,48},{1... | collective-permute-start | bytes 1179656 | tf_op jit(solution)/shard_map/ppermute | solution.py:837
  18.0 11.7 %all-to-all-start = ((bf16[16,1,192]{2,1,0:T(2,128)(2,1)}), bf16[16,1,192]{2,1,0:T(2,128)(2,1)S(1)}, u32[]{:S(2)}, u32[]{:S(2)}) async-start(bf16[16,1,192]{2,1,0:T(2,128)(2,1)} %broadcast_in_dim.18), calls=%async_computation | async-start | bytes 32768 | tf_op jit(solution)/shard_map/all_to_all | solution.py:786
  31.7 42.6 %all-to-all-start.1 = ((bf16[4,2,128,1536]{3,2,1,0:T(8,128)(2,1)}), bf16[4,2,128,1536]{3,2,1,0:T(8,128)(2,1)S(1)}, u32[]{:S(2)}, u32[]{:S(2)}) async-start(bf16[4,2,128,1536]{3,2,1,0:T(8,128)(2,1)} %broadcast_in_dim.19), calls=%async_computation.1 | async-start | bytes 6291456 | tf_op jit(solution)/shard_map/all_to_all | solution.py:786
  74.3 16.1 %all-to-all-start.2 = ((bf16[16,96,128]{2,1,0:T(8,128)(2,1)}), bf16[16,96,128]{2,1,0:T(8,128)(2,1)}, u32[]{:S(2)}, u32[]{:S(2)}) async-start(bf16[16,96,128]{2,1,0:T(8,128)(2,1)} %copy.60), calls=%async_computation.2 | async-start | bytes 786432 | tf_op jit(solution)/shard_map/all_to_all | solution.py:786
  79.5 104.6 %all-gather.7.cloned.1.call-start = ((), (), s32[]{:S(2)}) async-start(), calls=%async_computation.11 | async-start | bytes 6684672 | tf_op jit(solution)/shard_map/all_gather | solution.py:858
  102.8 12.2 %copy-start.1 = (bf16[8,128,1024]{2,1,0:T(8,128)(2,1)}, bf16[8,128,1024]{2,1,0:T(8,128)(2,1)S(1)}, u32[]{:S(2)}) copy-start(bf16[8,128,1024]{2,1,0:T(8,128)(2,1)S(1)} %get-tuple-element.104.k_ref.v_ref) | copy-start | bytes 6291460
  116.6 275.2 %all-gather.11.cloned.1.call-start = ((), (), s32[]{:S(2)}) async-start(), calls=%async_computation.13 | async-start | bytes 13369344 | tf_op jit(solution)/shard_map/all_gather | solution.py:860
  117.8 20.9 %copy-start.14 = (bf16[128,1536]{1,0:T(8,128)(2,1)}, bf16[128,1536]{1,0:T(8,128)(2,1)S(1)}, u32[]{:S(2)}) copy-start(bf16[128,1536]{1,0:T(8,128)(2,1)S(1)} %constant_dynamic-update-slice_fusion.4.sdown_ref.sd_ref) | copy-start | bytes 1179652
  213.0 8.1 %copy-start.52 = (bf16[2,8,128,1536]{3,2,1,0:T(8,128)(2,1)S(1)}, bf16[2,8,128,1536]{3,2,1,0:T(8,128)(2,1)}, u32[]{:S(2)}) copy-start(bf16[2,8,128,1536]{3,2,1,0:T(8,128)(2,1)} %get-tuple-element.115) | copy-start | bytes 18874372
  215.3 5.7 collective-permute-start.1
  223.6 69.9 %all-to-all-start.3 = ((bf16[8,128,1536]{2,1,0:T(8,128)(2,1)}), bf16[8,128,1536]{2,1,0:T(8,128)(2,1)S(1)}, u32[]{:S(2)}, u32[]{:S(2)}) async-start(bf16[8,128,1536]{2,1,0:T(8,128)(2,1)} %fusion), calls=%async_computation.3 | async-start | bytes 6291456 | tf_op jit(solution)/shard_map/all_to_all | solution.py:786
  242.2 59.7 %collective-permute-start.2 = (bf16[9216,128]{1,0:T(8,128)(2,1)}, bf16[9216,128]{1,0:T(8,128)(2,1)}, u32[]{:S(2)}, u32[]{:S(2)}) collective-permute-start(bf16[9216,128]{1,0:T(8,128)(2,1)} %get-tuple-element.119), channel_id=1, source_target_pairs={{0,16},{16,0},{32,48},{48,32},{64,80},{80,64},{96,112},{112,96},{1... | collective-permute-start | bytes 7077896 | tf_op jit(solution)/shard_map/ppermute | solution.py:890
  243.7 58.3 %collective-permute-start.3 = (bf16[9216,128]{1,0:T(8,128)(2,1)}, bf16[9216,128]{1,0:T(8,128)(2,1)}, u32[]{:S(2)}, u32[]{:S(2)}) collective-permute-start(bf16[9216,128]{1,0:T(8,128)(2,1)} %get-tuple-element.128), channel_id=1, source_target_pairs={{0,48},{16,32},{32,16},{48,0},{64,112},{80,96},{96,80},{112,64},{1... | collective-permute-start | bytes 7077896 | tf_op jit(solution)/shard_map/ppermute | solution.py:890
  246.3 13.6 %copy-start.2 = (bf16[2,2,384,512]{3,2,1,0:T(8,128)(2,1)S(1)}, bf16[2,2,384,512]{3,2,1,0:T(8,128)(2,1)}, u32[]{:S(2)}) copy-start(bf16[2,2,384,512]{3,2,1,0:T(8,128)(2,1)} %get-tuple-element.122.act_ref) | copy-start | bytes 4718596
  246.3 13.6 %copy-start.6 = (bf16[8,2,128,128]{3,2,1,0:T(8,128)(2,1)S(1)}, bf16[8,2,128,128]{3,2,1,0:T(8,128)(2,1)}, u32[]{:S(2)}) copy-start(bf16[8,2,128,128]{3,2,1,0:T(8,128)(2,1)} %get-tuple-element.159.sact_ref) | copy-start | bytes 1572868
  246.3 13.6 %copy-start.15 = (bf16[128,1536]{1,0:T(8,128)(2,1)S(1)}, bf16[128,1536]{1,0:T(8,128)(2,1)}, u32[]{:S(2)}) copy-start(bf16[128,1536]{1,0:T(8,128)(2,1)} %copy-done.14) | copy-start | bytes 1179652
  246.4 13.6 %copy-start.22 = (bf16[8,2,128,128]{3,2,1,0:T(8,128)(2,1)S(1)}, bf16[8,2,128,128]{3,2,1,0:T(8,128)(2,1)}, u32[]{:S(2)}) copy-start(bf16[8,2,128,128]{3,2,1,0:T(8,128)(2,1)} %get-tuple-element.110.place_ref) | copy-start | bytes 1572868
  246.4 13.6 %copy-start.36 = (f32[2,2,384,128]{3,2,1,0:T(8,128)S(1)}, f32[2,2,384,128]{3,2,1,0:T(8,128)}, u32[]{:S(2)}) copy-start(f32[2,2,384,128]{3,2,1,0:T(8,128)} %get-tuple-element.123.gate_ref) | copy-start | bytes 2359300
  301.9 7.1 %copy-start.44 = (bf16[128,1536]{1,0:T(8,128)(2,1)}, bf16[128,1536]{1,0:T(8,128)(2,1)S(1)}, u32[]{:S(2)}) copy-start(bf16[128,1536]{1,0:T(8,128)(2,1)S(1)} %get-tuple-element.142.ga_ref) | copy-start | bytes 1179652
  301.9 7.1 %copy-start.30 = (bf16[4608,128]{1,0:T(8,128)(2,1)S(1)}, bf16[4608,128]{1,0:T(8,128)(2,1)}, u32[]{:S(2)}) copy-start(bf16[4608,128]{1,0:T(8,128)(2,1)} %get-tuple-element.121.p0) | copy-start | bytes 3538948
  302.0 7.1 %copy-start.31 = (bf16[4608,128]{1,0:T(8,128)(2,1)S(1)}, bf16[4608,128]{1,0:T(8,128)(2,1)}, u32[]{:S(2)}) copy-start(bf16[4608,128]{1,0:T(8,128)(2,1)} %get-tuple-element.127.p6) | copy-start | bytes 3538948
  302.0 7.1 %copy-start.32 = (bf16[4608,128]{1,0:T(8,128)(2,1)S(1)}, bf16[4608,128]{1,0:T(8,128)(2,1)}, u32[]{:S(2)}) copy-start(bf16[4608,128]{1,0:T(8,128)(2,1)} %get-tuple-element.125.p1) | copy-start | bytes 3538948
  302.0 7.1 %copy-start.33 = (bf16[4608,128]{1,0:T(8,128)(2,1)S(1)}, bf16[4608,128]{1,0:T(8,128)(2,1)}, u32[]{:S(2)}) copy-start(bf16[4608,128]{1,0:T(8,128)(2,1)} %get-tuple-element.126.p3) | copy-start | bytes 3538948
  318.2 35.7 %all-to-all-start.4 = ((bf16[8,128,1024]{2,1,0:T(8,128)(2,1)}), bf16[8,128,1024]{2,1,0:T(8,128)(2,1)S(1)}, u32[]{:S(2)}, u32[]{:S(2)}) async-start(bf16[8,128,1024]{2,1,0:T(8,128)(2,1)} %copy-done.23), calls=%async_computation.4 | async-start | bytes 4194304 | tf_op jit(solution)/shard_map/all_to_all | solution.py:786
  325.1 54.1 %collective-permute-start.4 = (bf16[4608,128]{1,0:T(8,128)(2,1)}, bf16[4608,128]{1,0:T(8,128)(2,1)}, u32[]{:S(2)}, u32[]{:S(2)}) collective-permute-start(bf16[4608,128]{1,0:T(8,128)(2,1)} %copy-done.51), channel_id=1, source_target_pairs={{0,16},{16,0},{32,48},{48,32},{64,80},{80,64},{96,112},{112,96},{1... | collective-permute-start | bytes 3538952 | tf_op jit(solution)/shard_map/ppermute | solution.py:890
  327.1 52.0 %collective-permute-start.5 = (bf16[4608,128]{1,0:T(8,128)(2,1)}, bf16[4608,128]{1,0:T(8,128)(2,1)}, u32[]{:S(2)}, u32[]{:S(2)}) collective-permute-start(bf16[4608,128]{1,0:T(8,128)(2,1)} %copy-done.50), channel_id=1, source_target_pairs={{0,48},{16,32},{32,16},{48,0},{64,112},{80,96},{96,80},{112,64},{1... | collective-permute-start | bytes 3538952 | tf_op jit(solution)/shard_map/ppermute | solution.py:890
  358.3 20.8 %all-to-all-start.5 = ((bf16[16,256,128]{2,1,0:T(8,128)(2,1)}), bf16[16,256,128]{2,1,0:T(8,128)(2,1)}, u32[]{:S(2)}, u32[]{:S(2)}) async-start(bf16[16,256,128]{2,1,0:T(8,128)(2,1)} %get-tuple-element.143), calls=%async_computation.5 | async-start | bytes 2097152 | tf_op jit(solution)/shard_map/all_to_all | solution.py:786
  362.7 212.4 %reduce-scatter.2.cloned.1.call-start = ((), (), s32[]{:S(2)}) async-start(), calls=%async_computation.14 | async-start | bytes 6684672 | tf_op jit(solution)/shard_map/reduce_scatter | solution.py:960
  363.8 15.3 %copy-start.17 = (f32[4608,128]{1,0:T(8,128)S(1)}, f32[4608,128]{1,0:T(8,128)}, u32[]{:S(2)}) copy-start(f32[4608,128]{1,0:T(8,128)} %copy-done.16) | copy-start | bytes 7077892
  383.5 7.4 %copy-start.20 = (f32[4608,128]{1,0:T(8,128)}, f32[4608,128]{1,0:T(8,128)S(1)}, u32[]{:S(2)}) copy-start(f32[4608,128]{1,0:T(8,128)S(1)} %get-tuple-element.149) | copy-start | bytes 7077892
  383.5 29.3 %collective-permute-start.6 = (bf16[4608,128]{1,0:T(8,128)(2,1)S(1)}, bf16[4608,128]{1,0:T(8,128)(2,1)S(1)}, u32[]{:S(2)}, u32[]{:S(2)}) collective-permute-start(bf16[4608,128]{1,0:T(8,128)(2,1)S(1)} %get-tuple-element.150), channel_id=1, source_target_pairs={{0,64},{16,80},{32,96},{48,112},{64,0},{80,16},{96,32},{112,48},{1... | collective-permute-start | bytes 3538952 | tf_op jit(solution)/shard_map/ppermute | solution.py:890
  391.8 21.0 %copy-start.21 = (f32[4608,128]{1,0:T(8,128)S(1)}, f32[4608,128]{1,0:T(8,128)}, u32[]{:S(2)}) copy-start(f32[4608,128]{1,0:T(8,128)} %copy-done.20) | copy-start | bytes 7077892
  413.0 10.6 %copy-start.7 = (bf16[8,2,128,128]{3,2,1,0:T(8,128)(2,1)S(1)}, bf16[8,2,128,128]{3,2,1,0:T(8,128)(2,1)}, u32[]{:S(2)}) copy-start(bf16[8,2,128,128]{3,2,1,0:T(8,128)(2,1)} %get-tuple-element.159.sact_ref) | copy-start | bytes 1572868
  413.0 26.4 %all-to-all-start.6 = ((bf16[16,112,384]{2,1,0:T(8,128)(2,1)}), bf16[16,112,384]{2,1,0:T(8,128)(2,1)}, u32[]{:S(2)}, u32[]{:S(2)}) async-start(bf16[16,112,384]{2,1,0:T(8,128)(2,1)} %cols_grad.1), calls=%async_computation.7 | async-start | bytes 2752512 | tf_op jit(solution)/shard_map/all_to_all | solution.py:786
  417.6 28.5 %collective-permute-start.7 = (bf16[4608,128]{1,0:T(8,128)(2,1)S(1)}, bf16[4608,128]{1,0:T(8,128)(2,1)}, u32[]{:S(2)}, u32[]{:S(2)}) collective-permute-start(bf16[4608,128]{1,0:T(8,128)(2,1)S(1)} %add_convert_fusion.refs_0_), channel_id=1, source_target_pairs={{0,16},{16,0},{32,48},{48,32},{64,80},{80,64},{96,112},{112,96},{1... | collective-permute-start | bytes 3538952 | tf_op jit(solution)/shard_map/ppermute | solution.py:890
  419.7 29.1 %collective-permute-start.8 = (bf16[4608,128]{1,0:T(8,128)(2,1)S(1)}, bf16[4608,128]{1,0:T(8,128)(2,1)}, u32[]{:S(2)}, u32[]{:S(2)}) collective-permute-start(bf16[4608,128]{1,0:T(8,128)(2,1)S(1)} %add_convert_fusion.refs_0_), channel_id=1, source_target_pairs={{0,48},{16,32},{32,16},{48,0},{64,112},{80,96},{96,80},{112,64},{1... | collective-permute-start | bytes 3538952 | tf_op jit(solution)/shard_map/ppermute | solution.py:890
  420.6 68.1 %collective-permute-start.9 = (bf16[4608,128]{1,0:T(8,128)(2,1)S(1)}, bf16[4608,128]{1,0:T(8,128)(2,1)}, u32[]{:S(2)}, u32[]{:S(2)}) collective-permute-start(bf16[4608,128]{1,0:T(8,128)(2,1)S(1)} %add_convert_fusion.refs_0_), channel_id=1, source_target_pairs={{0,64},{16,80},{32,96},{48,112},{64,0},{80,16},{96,32},{112,48},{1... | collective-permute-start | bytes 3538952 | tf_op jit(solution)/shard_map/ppermute | solution.py:890
  488.7 34.3 %all-to-all-start.7 = ((bf16[8,256,384]{2,1,0:T(8,128)(2,1)}), bf16[8,256,384]{2,1,0:T(8,128)(2,1)}, u32[]{:S(2)}, u32[]{:S(2)}) async-start(bf16[8,256,384]{2,1,0:T(8,128)(2,1)} %pad_maximum_fusion), calls=%async_computation.8 | async-start | bytes 3145728 | tf_op jit(solution)/shard_map/all_to_all | solution.py:786
  495.7 44.7 %collective-permute-start.10 = (bf16[4608,128]{1,0:T(8,128)(2,1)}, bf16[4608,128]{1,0:T(8,128)(2,1)S(1)}, u32[]{:S(2)}, u32[]{:S(2)}) collective-permute-start(bf16[4608,128]{1,0:T(8,128)(2,1)} %collective-permute-done.9.refs_0_), channel_id=1, source_target_pairs={{0,16},{16,0},{32,48},{48,32},{64,80},{80,64},{96,112},{112,96},{1... | collective-permute-start | bytes 3538952 | tf_op jit(solution)/shard_map/ppermute | solution.py:890
  497.7 43.2 %collective-permute-start.11 = (bf16[4608,128]{1,0:T(8,128)(2,1)}, bf16[4608,128]{1,0:T(8,128)(2,1)}, u32[]{:S(2)}, u32[]{:S(2)}) collective-permute-start(bf16[4608,128]{1,0:T(8,128)(2,1)} %collective-permute-done.9.refs_0_), channel_id=1, source_target_pairs={{0,48},{16,32},{32,16},{48,0},{64,112},{80,96},{96,80},{112,64},{1... | collective-permute-start | bytes 3538952 | tf_op jit(solution)/shard_map/ppermute | solution.py:890
  542.2 33.0 %copy-start.13 = (f32[128,1536]{1,0:T(8,128)S(1)}, f32[128,1536]{1,0:T(8,128)}, u32[]{:S(2)}) copy-start(f32[128,1536]{1,0:T(8,128)} %copy-done.11) | copy-start | bytes 2359300
  542.2 30.7 %all-to-all-start.8 = ((bf16[8,256,384]{2,1,0:T(8,128)(2,1)}), bf16[8,256,384]{2,1,0:T(8,128)(2,1)S(1)}, u32[]{:S(2)}, u32[]{:S(2)}) async-start(bf16[8,256,384]{2,1,0:T(8,128)(2,1)} %broadcast_in_dim.23), calls=%async_computation.9 | async-start | bytes 3145728 | tf_op jit(solution)/shard_map/all_to_all | solution.py:786
  551.6 42.7 %collective-permute-start.13 = (bf16[4608,128]{1,0:T(8,128)(2,1)}, bf16[4608,128]{1,0:T(8,128)(2,1)}, u32[]{:S(2)}, u32[]{:S(2)}) collective-permute-start(bf16[4608,128]{1,0:T(8,128)(2,1)} %collective-permute-done.8.refs_3_), channel_id=1, source_target_pairs={{0,16},{16,0},{32,48},{48,32},{64,80},{80,64},{96,112},{112,96},{1... | collective-permute-start | bytes 3538952 | tf_op jit(solution)/shard_map/ppermute | solution.py:890
  553.6 47.1 %collective-permute-start.12 = (bf16[4608,128]{1,0:T(8,128)(2,1)}, bf16[4608,128]{1,0:T(8,128)(2,1)}, u32[]{:S(2)}, u32[]{:S(2)}) collective-permute-start(bf16[4608,128]{1,0:T(8,128)(2,1)} %copy-done.28), channel_id=1, source_target_pairs={{0,48},{16,32},{32,16},{48,0},{64,112},{80,96},{96,80},{112,64},{1... | collective-permute-start | bytes 3538952 | tf_op jit(solution)/shard_map/ppermute | solution.py:890
  (40 other events, 123.5 us)
Sparse Core Ops, SparseCore 0:
  12.2 79.9 all-gather.4
  94.5 44.0 all-gather.8
  140.9 43.1 all-gather.6
  185.7 106.3 all-gather.10
  413.1 128.0 reduce-scatter.1

commit v6 on v5

--- a/solution.py
+++ b/solution.py
@@ -116,28 +116,78 @@
     )(ctx_at, qkv, kv_all, kv_all)
 
 
+SEQ = N_CTX * BLOCK
+AT_QUERY, AT_MIXED, AT_OUT = SEQ, SEQ + BLOCK, SEQ + 2 * BLOCK
+AT_SHARED = SEQ + 3 * BLOCK
+AT_DOWN = AT_SHARED + 16 * N_EXP
+AT_GAIN = AT_DOWN + 96
+SENT_ROWS = AT_GAIN + 16
+
+
+def halves(a, b, lane):
+    low = jnp.where(lane < 64, a, pltpu.roll(b, 64, 1))
+    high = jnp.where(lane < 64, pltpu.roll(a, 64, 1), b)
+    return low, high
+
+
 def attend_back_kernel(
-    ctx_ref, q_ref, ga_ref, attf_ref, log_ref, k_ref, v_ref, dq_ref, dkv_ref
+    ctx_ref,
+    q_ref,
+    ga_ref,
+    attf_ref,
+    log_ref,
+    k_ref,
+    v_ref,
+    all_ga_ref,
+    extra_ref,
+    gain_ref,
+    dq_ref,
+    sent_ref,
+    kept_ref,
 ):
+    group = pl.program_id(0)
     q = stack_heads(q_ref[...])
     grad = stack_heads(ga_ref[...])
     delta = jnp.sum(grad.astype(f32) * stack_heads(attf_ref[...]), axis=-1, keepdims=True)
-    keys = k_ref[...].reshape(N_CTX * BLOCK, HEAD_DIM)
-    values = v_ref[...].reshape(N_CTX * BLOCK, HEAD_DIM)
+    keys = k_ref[...].reshape(SEQ, HEAD_DIM)
+    values = v_ref[...].reshape(SEQ, HEAD_DIM)
     scores = jnp.where(allowed_scores(ctx_ref[0]), dg(q, keys, NT) * score_scale, masked_score)
     weights = jnp.exp2(scores - log_ref[:, :1])
     grad_weights = dg(grad, values, NT)
     grad_raw = (weights * (grad_weights - delta)).astype(bf16)
     scale = HEAD_DIM ** (-0.5)
-    dq_ref[...] = unstack_heads(dg(grad_raw, keys, NN) * scale).astype(bf16)
-    grad_k = (dg(grad_raw, q, TN) * scale).astype(bf16)
-    grad_v = dg(weights.astype(bf16), grad, TN).astype(bf16)
-    dkv_ref[:, :, :HEAD_DIM] = grad_k.reshape(N_CTX, BLOCK, HEAD_DIM)
-    dkv_ref[:, :, HEAD_DIM:] = grad_v.reshape(N_CTX, BLOCK, HEAD_DIM)
-
-
-def attend_back(ctx_at, qkv, grad_att, att_f, logs, kv_all):
-    part = pl.BlockSpec((N_CTX, BLOCK, 2 * HEAD_DIM), lambda g: (0, 0, g))
+    dq = unstack_heads(dg(grad_raw, keys, NN) * scale)
+    dq_ref[...] = dq.astype(bf16)
+    kept_ref[group] = dq
+    grad_k = dg(grad_raw, q, TN) * scale
+    grad_v = dg(weights.astype(bf16), grad, TN)
+    low, high = halves(grad_k, grad_v, lax.broadcasted_iota(jnp.int32, (SEQ, HEAD_DIM), 1))
+    sent_ref[2 * group, :SEQ] = low.astype(bf16)
+    sent_ref[2 * group + 1, :SEQ] = high.astype(bf16)
+
+    @pl.when(group == KV_HEADS - 1)
+    def _():
+        lane = lax.broadcasted_iota(jnp.int32, (BLOCK, HEAD_DIM), 1)
+
+        def dq_tile(m):
+            return kept_ref[m // GROUP, :, HEAD_DIM * (m % GROUP) : HEAD_DIM * (m % GROUP + 1)]
+
+        def ga_tile(m):
+            return all_ga_ref[:, HEAD_DIM * m : HEAD_DIM * (m + 1)].astype(f32)
+
+        for m in range(KV_HEADS):
+            low, high = halves(dq_tile(N_CTX + m), ga_tile(N_CTX + m), lane)
+            sent_ref[2 * m, AT_MIXED:AT_OUT] = low.astype(bf16)
+            sent_ref[2 * m + 1, AT_MIXED:AT_OUT] = high.astype(bf16)
+        gains = gain_ref[...].astype(bf16)
+        for c in range(N_CTX):
+            sent_ref[c, AT_QUERY:AT_MIXED] = dq_tile(c).astype(bf16)
+            sent_ref[c, AT_OUT:AT_SHARED] = ga_tile(c).astype(bf16)
+            sent_ref[c, AT_SHARED:AT_GAIN] = extra_ref[c]
+            sent_ref[c, AT_GAIN:] = gains
+
+
+def attend_back(ctx_at, qkv, grad_att, att_f, logs, kv_all, grad_attn, extra, gain_rows):
     return pl.pallas_call(
         attend_back_kernel,
         grid=(KV_HEADS,),
@@ -148,16 +198,22 @@
             head_spec(),
             pl.BlockSpec((GROUP * BLOCK, HEAD_DIM), lambda g: (g, 0)),
         ]
-        + kv_specs(),
-        out_specs=[head_spec(), part],
+        + kv_specs()
+        + [
+            whole((BLOCK, WIDTH)),
+            whole((N_CTX, AT_GAIN - AT_SHARED, HEAD_DIM)),
+            whole((16, HEAD_DIM)),
+        ],
+        out_specs=[head_spec(), whole((N_CTX, SENT_ROWS, HEAD_DIM))],
         out_shape=[
             jax.ShapeDtypeStruct((BLOCK, WIDTH), bf16),
-            jax.ShapeDtypeStruct((N_CTX, BLOCK, 2 * KV_WIDTH), bf16),
-        ],
-        cost_estimate=cost(7),
+            jax.ShapeDtypeStruct((N_CTX, SENT_ROWS, HEAD_DIM), bf16),
+        ],
+        scratch_shapes=[pltpu.VMEM((KV_HEADS, BLOCK, GROUP * HEAD_DIM), f32)],
+        cost_estimate=cost(9),
         compiler_params=params(48),
         name="attend_back",
-    )(ctx_at, qkv, grad_att, att_f, logs, kv_all, kv_all)
+    )(ctx_at, qkv, grad_att, att_f, logs, kv_all, kv_all, grad_attn, extra, gain_rows)
 
 
 def middle_kernel(att_ref, w_ref, x_ref, gain_ref, middle_ref, hidden_ref):
@@ -207,7 +263,10 @@
     middle = middle_ref[...]
     inv = lax.rsqrt(jnp.mean(middle * middle, axis=-1, keepdims=True) + epsilon)
     normed = middle * inv
-    gg_ref[...] = jnp.sum(grad_two * normed, axis=0, keepdims=True)
+    gains = jnp.sum(grad_two * normed, axis=0, keepdims=True)
+    gg_ref[...] = jnp.zeros((16, HEAD_DIM), f32)
+    for m in range(HEADS):
+        gg_ref[m : m + 1] = gains[:, HEAD_DIM * m : HEAD_DIM * (m + 1)]
     grad_middle = up_ref[...].astype(f32) + norm_back(grad_two * gain_ref[...], normed, inv)
     gm_ref[...] = grad_middle
     grad_attn = grad_middle.astype(bf16)
@@ -226,12 +285,12 @@
             whole((1, WIDTH)),
             w_cols(WIDTH, 1),
         ],
-        out_specs=[whole((BLOCK, WIDTH))] * 3 + [whole((1, WIDTH))],
+        out_specs=[whole((BLOCK, WIDTH))] * 3 + [whole((16, HEAD_DIM))],
         out_shape=[
             jax.ShapeDtypeStruct((BLOCK, WIDTH), f32),
             jax.ShapeDtypeStruct((BLOCK, WIDTH), bf16),
             jax.ShapeDtypeStruct((BLOCK, WIDTH), bf16),
-            jax.ShapeDtypeStruct((1, WIDTH), f32),
+            jax.ShapeDtypeStruct((16, HEAD_DIM), f32),
         ],
         cost_estimate=cost(5),
         compiler_params=params(48),
@@ -447,148 +506,210 @@
     )(exp_at, act, gate, place, sact, wd, sd)
 
 
-def turn_kernel(dq_ref, pieces_ref, ga_ref, gqkv_ref, cols_ref):
-    total = pieces_ref[0].astype(f32)
-    for i in range(1, N_CTX):
-        total = total + pieces_ref[i].astype(f32)
-    total = total.astype(bf16)
-    parts = [total[:, i * HEAD_DIM : (i + 1) * HEAD_DIM] for i in range(2 * KV_HEADS)]
-    grad_kv = jnp.concatenate(parts[0::2] + parts[1::2], axis=1)
-    gqkv_ref[:, :WIDTH] = dq_ref[...]
-    gqkv_ref[:, WIDTH:] = grad_kv
-    turned = jnp.concatenate([dq_ref[...].T, grad_kv.T], axis=0)
-    turned_out = ga_ref[...].T
-    for j in range(N_EXP):
-        cols_ref[j, :128] = turned[128 * j : 128 * j + 128]
-        cols_ref[j, 128:160] = turned[2048 + 32 * j : 2048 + 32 * j + 32]
-        cols_ref[j, 160:192] = turned_out[1024 + 32 * j : 1024 + 32 * j + 32]
-        cols_ref[j, 192:] = turned_out[64 * j : 64 * j + 64]
-
-
-def turn_cols(dq, pieces, grad_attn):
-    return pl.pallas_call(
-        turn_kernel,
+def columns_kernel(got_ref, hidden_ref, att_ref, sent_ref, kv_ref, down_ref):
+    total = got_ref[0, :SEQ].astype(f32)
+    for src in range(1, N_CTX):
+        total = total + got_ref[src, :SEQ].astype(f32)
+    grad_kv = total.astype(bf16)
+    kv_ref[...] = grad_kv.reshape(N_CTX, BLOCK, HEAD_DIM)
+
+    def rows_of(at, order):
+        return jnp.concatenate([got_ref[src, at : at + BLOCK] for src in order], axis=0)
+
+    in_order = list(range(N_CTX))
+    y_order = [(i % 2) * 4 + i // 2 for i in range(N_CTX)]
+    lane = lax.broadcasted_iota(jnp.int32, (SEQ, HEAD_DIM), 1)
+    zero = jnp.zeros((SEQ, HEAD_DIM), bf16)
+    mixed_q = jnp.where(lane < 64, rows_of(AT_MIXED, in_order), zero)
+    mixed_o = jnp.where(lane < 64, zero, rows_of(AT_MIXED, y_order))
+    left = jnp.concatenate([rows_of(AT_QUERY, in_order).T, mixed_q.T, grad_kv.T], axis=0)
+    right = jnp.concatenate([mixed_o.T, rows_of(AT_OUT, y_order).T], axis=0)
+    by_hidden = dg(left, hidden_ref[...].reshape(SEQ, WIDTH), NN)
+    by_att = dg(right, att_ref[...].reshape(SEQ, WIDTH), NN)
+    tiles = [
+        by_hidden[:BLOCK],
+        by_hidden[BLOCK : 2 * BLOCK] + by_att[:BLOCK],
+        by_att[BLOCK:],
+        by_hidden[2 * BLOCK :],
+    ]
+    for t, tile in enumerate(tiles):
+        sent_ref[:, :96, HEAD_DIM * t : HEAD_DIM * (t + 1)] = (
+            tile.T.astype(bf16).reshape(N_EXP, 96, HEAD_DIM)
+        )
+
+    def summed(start, stop):
+        out = got_ref[0, start:stop].astype(f32)
+        for src in range(1, N_CTX):
+            out = out + got_ref[src, start:stop].astype(f32)
+        return out
+
+    down_ref[...] = summed(AT_DOWN, AT_GAIN).astype(bf16)
+    shared = summed(AT_SHARED, AT_DOWN)
+    gains = summed(AT_GAIN, SENT_ROWS)
+    row = lax.broadcasted_iota(jnp.int32, (16, HEAD_DIM), 0)
+    one_lane = lax.broadcasted_iota(jnp.int32, (1, HEAD_DIM), 1)
+    for i in range(N_EXP):
+        m, offset = (96 * i) // HEAD_DIM, (96 * i) % HEAD_DIM
+        gain = gains[m : m + 1]
+        if offset:
+            shift = HEAD_DIM - offset
+            gain = jnp.where(
+                one_lane < shift,
+                pltpu.roll(gain, shift, 1),
+                pltpu.roll(gains[m + 1 : m + 2], shift, 1),
+            )
+        rows = jnp.where(row == 12, jnp.broadcast_to(gain, (16, HEAD_DIM)), shared[16 * i : 16 * i + 16])
+        sent_ref[i, 96:, :HEAD_DIM] = rows.astype(bf16)
+        sent_ref[i, 96:, HEAD_DIM:] = jnp.zeros((16, 512 - HEAD_DIM), bf16)
+
+
+def column_grads(got, hidden_seq, att_seq):
+    return pl.pallas_call(
+        columns_kernel,
         out_shape=[
-            jax.ShapeDtypeStruct((BLOCK, WIDTH + 2 * KV_WIDTH), bf16),
-            jax.ShapeDtypeStruct((N_EXP, 256, BLOCK), bf16),
-        ],
-        cost_estimate=cost(2),
+            jax.ShapeDtypeStruct((N_EXP, 112, 512), bf16),
+            jax.ShapeDtypeStruct((N_CTX, BLOCK, HEAD_DIM), bf16),
+            jax.ShapeDtypeStruct((96, HEAD_DIM), bf16),
+        ],
+        cost_estimate=cost(8),
+        compiler_params=params(56),
+        name="column_grads",
+    )(got, hidden_seq, att_seq)
+
+
+OWNED_ROWS = 4 * 96 + 16 * N_EXP + 96
+
+
+def owned_kernel(got_ref, down_ref, owned_ref, gain_ref):
+    total = got_ref[0, :96].astype(f32)
+    gains = got_ref[0, 96:, :HEAD_DIM].astype(f32)
+    for src in range(1, N_EXP):
+        total = total + got_ref[src, :96].astype(f32)
+        gains = gains + got_ref[src, 96:, :HEAD_DIM].astype(f32)
+    gain_ref[...] = gains
+    for t in range(4):
+        owned_ref[96 * t : 96 * t + 96] = total[:, HEAD_DIM * t : HEAD_DIM * (t + 1)].astype(bf16)
+    for src in range(N_EXP):
+        at = 384 + 16 * src
+        owned_ref[at : at + 16] = got_ref[src, 96:, :HEAD_DIM]
+    owned_ref[384 + 16 * N_EXP :] = down_ref[...]
+
+
+def owned_sums(got, down):
+    return pl.pallas_call(
+        owned_kernel,
+        out_shape=[
+            jax.ShapeDtypeStruct((OWNED_ROWS, HEAD_DIM), bf16),
+            jax.ShapeDtypeStruct((16, HEAD_DIM), f32),
+        ],
+        cost_estimate=cost(3),
         compiler_params=params(32),
-        name="turn_cols",
-    )(dq, pieces, grad_attn)
-
-
-def input_kernel(gqkv_ref, wq_ref, wkv_ref, x_ref, gain_ref, gm_ref, out_ref, gg_ref):
-    grad_one = dg(gqkv_ref[:, :WIDTH], wq_ref[...], NT) + dg(gqkv_ref[:, WIDTH:], wkv_ref[...], NT)
+        name="owned_sums",
+    )(got, down)
+
+
+def finish_kernel(
+    got_ref,
+    gain_in_ref,
+    wq_ref,
+    wk_ref,
+    wv_ref,
+    gain_ref,
+    q_ref,
+    k_ref,
+    v_ref,
+    out_ref,
+    sg_ref,
+    su_ref,
+    sd_ref,
+):
+    lane = lax.broadcasted_iota(jnp.int32, (96, HEAD_DIM), 1)
+
+    def tile(c, t):
+        return got_ref[c, 96 * t : 96 * t + 96].astype(f32)
+
+    for c in range(N_CTX):
+        at = HEAD_DIM * c
+        q_ref[:, at : at + HEAD_DIM] = tile(c, 0)
+        out_ref[:, at : at + HEAD_DIM] = tile(c, 2)
+    for m in range(N_CTX // 2):
+        at = HEAD_DIM * m
+        low, high = halves(tile(2 * m, 1), tile(2 * m + 1, 1), lane)
+        q_ref[:, 1024 + at : 1024 + at + HEAD_DIM] = low
+        out_ref[:, 1024 + at : 1024 + at + HEAD_DIM] = high
+        low, high = halves(tile(2 * m, 3), tile(2 * m + 1, 3), lane)
+        k_ref[:, at : at + HEAD_DIM] = low
+        v_ref[:, at : at + HEAD_DIM] = high
+    gain = (
+        jnp.sum(q_ref[...] * wq_ref[...].astype(f32), axis=1, keepdims=True)
+        + jnp.sum(k_ref[...] * wk_ref[...].astype(f32), axis=1, keepdims=True)
+        + jnp.sum(v_ref[...] * wv_ref[...].astype(f32), axis=1, keepdims=True)
+    ) / gain_in_ref[...]
+    gain_ref[...] = jnp.broadcast_to(gain, (96, HEAD_DIM))
+    row = lax.broadcasted_iota(jnp.int32, (96, HEAD_DIM), 0)
+    picks = jnp.where((lane % 16 < 12) & (row == 12 * (lane // 16) + lane % 16), 1.0, 0.0)
+    picks = picks.astype(bf16)
+
+    def shared_tile(j):
+        at = 384 + 16 * j
+        rows = jnp.concatenate([got_ref[c, at : at + 16] for c in range(N_CTX)], axis=0)
+        return dg(picks, rows, NN)
+
+    for m in range(N_EXP // 2):
+        at = HEAD_DIM * m
+        low, high = halves(shared_tile(2 * m), shared_tile(2 * m + 1), lane)
+        sg_ref[:, at : at + HEAD_DIM] = low
+        su_ref[:, at : at + HEAD_DIM] = high
+    for c in range(N_CTX):
+        rows = got_ref[c, 384 + 16 * N_EXP :].astype(f32)
+        for m in range(HEADS):
+            sd_ref[8 * c : 8 * c + 8, HEAD_DIM * m : HEAD_DIM * (m + 1)] = rows[8 * m : 8 * m + 8]
+
+
+def finish(got, gain_column, query_weight, key_weight, value_weight):
+    shapes = [(96, 128), (96, 1536), (96, 512), (96, 512), (96, 1536), (96, 1024), (96, 1024)]
+    return pl.pallas_call(
+        finish_kernel,
+        out_shape=[jax.ShapeDtypeStruct(s, f32) for s in shapes + [(SHARED, WIDTH)]],
+        cost_estimate=cost(4),
+        compiler_params=params(32),
+        name="finish",
+    )(got, gain_column, query_weight, key_weight, value_weight)
+
+
+def input_kernel(dq_ref, got_ref, wq_ref, wkv_ref, x_ref, gain_ref, gm_ref, out_ref):
+    lane = lax.broadcasted_iota(jnp.int32, (BLOCK, HEAD_DIM), 1)
+    lows, highs = [], []
+    for m in range(KV_HEADS):
+        low, high = halves(got_ref[2 * m].astype(f32), got_ref[2 * m + 1].astype(f32), lane)
+        lows.append(low.astype(bf16))
+        highs.append(high.astype(bf16))
+    grad_kv = jnp.concatenate(lows + highs, axis=1)
+    grad_one = dg(dq_ref[...], wq_ref[...], NT) + dg(grad_kv, wkv_ref[...], NT)
     inputs = x_ref[...].astype(f32)
     inv = lax.rsqrt(jnp.mean(inputs * inputs, axis=-1, keepdims=True) + epsilon)
-    normed = inputs * inv
-    gg_ref[...] = jnp.sum(grad_one * normed, axis=0, keepdims=True)
-    out_ref[...] = (gm_ref[...] + norm_back(grad_one * gain_ref[...], normed, inv)).astype(bf16)
-
-
-def input_back(grad_qkv, w_all, tokens, gain, grad_middle):
+    out_ref[...] = (gm_ref[...] + norm_back(grad_one * gain_ref[...], inputs * inv, inv)).astype(bf16)
+
+
+def input_back(grad_query, grad_kv, w_all, tokens, gain, grad_middle):
     return pl.pallas_call(
         input_kernel,
         grid=(1,),
         in_specs=[
-            whole((BLOCK, WIDTH + 2 * KV_WIDTH)),
+            whole((BLOCK, WIDTH)),
+            whole((N_CTX, BLOCK, HEAD_DIM)),
             w_cols(WIDTH, 0),
             w_cols(2 * KV_WIDTH, 3),
             whole((BLOCK, WIDTH)),
             whole((1, WIDTH)),
             whole((BLOCK, WIDTH)),
         ],
-        out_specs=[whole((BLOCK, WIDTH)), whole((1, WIDTH))],
-        out_shape=[
-            jax.ShapeDtypeStruct((BLOCK, WIDTH), bf16),
-            jax.ShapeDtypeStruct((1, WIDTH), f32),
-        ],
+        out_specs=whole((BLOCK, WIDTH)),
+        out_shape=jax.ShapeDtypeStruct((BLOCK, WIDTH), bf16),
         cost_estimate=cost(7),
         compiler_params=params(48),
         name="input_back",
-    )(grad_qkv, w_all, w_all, tokens, gain, grad_middle)
-
-
-def cols_kernel(cols_ref, rows_ref, gain_ref, shared_ref, out_ref):
-    lhs = jnp.concatenate([cols_ref[j] for j in range(N_EXP)], axis=1)
-    row = lax.broadcasted_iota(jnp.int32, (256, N_EXP * BLOCK), 0)
-    zero = jnp.zeros_like(lhs)
-    attn = dg(jnp.where(row < 160, lhs, zero), rows_ref[:, :WIDTH], NN)
-    out = dg(jnp.where(row < 160, zero, lhs), rows_ref[:, WIDTH:], NN)
-    out_ref[:, :96, :256] = (attn + out).T.astype(bf16).reshape(N_EXP, 96, 256)
-    out_ref[:, 96:, :256] = gain_ref[...]
-    out_ref[:, :96, 256:] = shared_ref[...]
-    out_ref[:, 96:, 256:] = jnp.zeros((N_EXP, 16, META), bf16)
-
-
-def cols_grad(cols, rows_all, gain_rows, shared_cols):
-    return pl.pallas_call(
-        cols_kernel,
-        out_shape=jax.ShapeDtypeStruct((N_EXP, 112, 384), bf16),
-        cost_estimate=cost(9),
-        compiler_params=params(56),
-        name="cols_grad",
-    )(cols, rows_all, gain_rows, shared_cols)
-
-
-def finish_kernel(late_ref, gain_ref, q_ref, k_ref, v_ref, out_ref, sg_ref, su_ref, sd_ref):
-    lane = lax.broadcasted_iota(jnp.int32, (96, 128), 1)
-
-    def tile(j, m):
-        return late_ref[j // 2, 112 * (j % 2) : 112 * (j % 2) + 96, 128 * m : 128 * m + 128].astype(
-            f32
-        )
-
-    def half(a, b, first):
-        if first:
-            return jnp.where(lane < 64, a, pltpu.roll(b, 64, 1))
-        return jnp.where(lane < 64, pltpu.roll(a, 64, 1), b)
-
-    def quarter(tiles, start):
-        total = jnp.zeros((96, 128), f32)
-        for i, one in enumerate(tiles):
-            shift = (32 * i - start) % 128
-            moved = one if shift == 0 else pltpu.roll(one, shift, 1)
-            total = jnp.where((lane >= 32 * i) & (lane < 32 * i + 32), moved, total)
-        return total
-
-    gains = jnp.zeros((16, 128), f32)
-    for j in range(N_EXP):
-        at = 112 * (j % 2) + 96
-        gains = gains + late_ref[j // 2, at : at + 16, :128].astype(f32)
-        whole_tile = tile(j, 0)
-        if j < 12:
-            q_ref[:, 128 * j : 128 * j + 128] = whole_tile
-        else:
-            k_ref[:, 128 * (j - 12) : 128 * (j - 12) + 128] = whole_tile
-    gain_ref[...] = gains
-    for m in range(N_EXP // 2):
-        at = 128 * m
-        a, b = tile(2 * m, 2), tile(2 * m + 1, 2)
-        sg_ref[:, at : at + 128] = half(a, b, True)
-        su_ref[:, at : at + 128] = half(a, b, False)
-        out_ref[:, at : at + 128] = half(tile(2 * m, 1), tile(2 * m + 1, 1), False)
-    for m in range(N_EXP // 4):
-        at = 128 * m
-        tiles = [tile(4 * m + i, 1) for i in range(4)]
-        v_ref[:, at : at + 128] = quarter(tiles, 0)
-        out_ref[:, 1024 + at : 1024 + at + 128] = quarter(tiles, 32)
-    for c in range(N_CTX):
-        rows = late_ref[c, 224:].astype(f32)
-        for q in range(4):
-            sd_ref[8 * c : 8 * c + 8, 384 * q : 384 * q + 384] = rows[8 * q : 8 * q + 8]
-
-
-def finish(late):
-    shapes = [(16, 128), (96, 1536), (96, 512), (96, 512), (96, 1536), (96, 1024), (96, 1024)]
-    return pl.pallas_call(
-        finish_kernel,
-        out_shape=[jax.ShapeDtypeStruct(s, f32) for s in shapes + [(SHARED, WIDTH)]],
-        cost_estimate=cost(5),
-        compiler_params=params(32),
-        name="finish",
-    )(late)
+    )(grad_query, grad_kv, w_all, w_all, tokens, gain, grad_middle)
 
 
 def norm_rows_kernel(x_ref, gain_ref, out_ref):
@@ -834,14 +955,18 @@
     gains = swap_all(jnp.broadcast_to(gains, (N_EXP, gains.shape[0])), "exp")
     gain_attn = gains[:, :96].reshape(1, WIDTH).astype(f32)
     gain_ffn = gains[:, 96:].reshape(1, WIDTH).astype(f32)
-    tokens_z = lax.ppermute(after(tokens, w_cat), "ctx", z_swap)
-    pair = jnp.where(
-        z_at == 0,
-        jnp.concatenate([tokens, tokens_z], axis=0),
-        jnp.concatenate([tokens_z, tokens], axis=0),
-    )
-    tokens_seq = swap_all(jnp.broadcast_to(pair, (4, 2, BLOCK, WIDTH)), "ctx", y_groups)
-    tokens_seq = tokens_seq.reshape(N_CTX, BLOCK, WIDTH)
+
+    def of_sequence(rows):
+        other = lax.ppermute(rows, "ctx", z_swap)
+        pair = jnp.where(
+            z_at == 0,
+            jnp.concatenate([rows, other], axis=0),
+            jnp.concatenate([other, rows], axis=0),
+        )
+        got = swap_all(jnp.broadcast_to(pair, (4, 2, BLOCK, WIDTH)), "ctx", y_groups)
+        return got.reshape(N_CTX, BLOCK, WIDTH)
+
+    tokens_seq = of_sequence(after(tokens, w_cat))
     shared_cols = jnp.concatenate(
         [shared_gate.reshape(96, N_EXP, SHARED), shared_up.reshape(96, N_EXP, SHARED)], axis=2
     ).transpose(1, 0, 2)
@@ -857,15 +982,10 @@
 
     hidden_all = lax.all_gather(hidden_two, "exp", axis=0, tiled=True)
     hidden_all = hidden_all.reshape(HALF, 2, BLOCK, WIDTH)
-    rows_all = lax.all_gather(
-        after(jnp.concatenate([hidden_one[0], attended], axis=1), hidden_two),
-        "exp",
-        axis=0,
-        tiled=True,
-    )
+    att_seq = of_sequence(attended[None])
     place, grad_eo, grad_eh, grad_sh, slot_gate = place_rows(
         exp_s,
-        after(up_all, hidden_two).reshape(HALF, 2, BLOCK, WIDTH + META),
+        after(up_all, hidden_two, att_seq).reshape(HALF, 2, BLOCK, WIDTH + META),
         expert_down,
         shared_two,
     )
@@ -895,17 +1015,28 @@
     act_late = after(shared_act, p0).reshape(N_EXP * BLOCK, META)
     grad_sdown = dg(act_late, up_all, TN)[:SHARED, :WIDTH].astype(bf16)
 
+    extra = jnp.concatenate(
+        [
+            jnp.pad(
+                grad_scols.reshape(N_EXP, N_CTX, 12, META).transpose(1, 0, 2, 3),
+                ((0, 0), (0, 0), (0, 4), (0, 0)),
+            ).reshape(N_CTX, 16 * N_EXP, META),
+            grad_sdown.reshape(N_CTX, 8, HEADS, 128).transpose(0, 2, 1, 3).reshape(N_CTX, 96, 128),
+        ],
+        axis=1,
+    )
     out_part = expert_output(
         exp_s, after(act, p0), slot_gate, place, shared_act, expert_down, shared_two
     )
 
-    grad_two = after(grad_two, out_part)
-    grad_middle, grad_attn, grad_heads, grad_gain_ffn = middle_back(
+    grad_two = after(grad_two, out_part, extra)
+    grad_middle, grad_attn, grad_heads, gain_rows = middle_back(
         grad_two, middle, cotangent[0], gain_ffn, w_all
     )
-    grad_query, part_kv = attend_back(ctx_s, queries, grad_heads, att_f, logs, kv_all)
-
-    from_1, from_3 = after((from_1, from_3), grad_heads)
+    grad_query, sent = attend_back(
+        ctx_s, queries, grad_heads, att_f, logs, kv_all, grad_attn, extra, gain_rows
+    )
+    from_1, from_3 = after((from_1, from_3), sent)
     add_a, add_b, part_0, part_1 = piece_sums(
         relay_kernel,
         (bf16, bf16, f32, f32),
@@ -919,51 +1050,52 @@
         (from_3, 1),
     )
     got_11, got_30 = to(add_b, 1), to(add_a, 3)
-    kv_pieces = swap_all(after(part_kv, add_a), "ctx")
-
-    grad_qkv, cols_sent = turn_cols(grad_query, kv_pieces, grad_attn)
-    cols = swap_all(cols_sent, "exp")
-    input_grad, grad_gain_attn = input_back(
-        grad_qkv, w_all, tokens[0], gain_attn, grad_middle
-    )
-    cols = after(cols, input_grad)
+    out_rows = lax.psum_scatter(
+        after(out_part, add_a).reshape(N_EXP * BLOCK, WIDTH),
+        "exp",
+        scatter_dimension=0,
+        tiled=True,
+    )
+
+    columns, grad_kv, grad_down = column_grads(
+        swap_all(after(sent, add_a), "ctx"), hidden_seq, att_seq
+    )
+    owned = swap_all(columns, "exp")
     own_part, side = piece_sums(
-        side_kernel, (f32, bf16), part_0, part_1, after(got_11, cols), got_30
+        side_kernel, (f32, bf16), part_0, part_1, after(got_11, columns), got_30
     )
     across = to(side, 4)
-    gain_rows = jnp.concatenate(
-        [grad_gain_attn.reshape(N_EXP, 1, 96), grad_gain_ffn.reshape(N_EXP, 1, 96)], axis=1
-    ).astype(bf16)
-    gain_rows = jnp.pad(gain_rows, ((0, 0), (0, 14), (0, 160)))
-    sent = cols_grad(
-        after(cols, side),
-        rows_all,
-        gain_rows,
-        grad_scols.reshape(N_EXP, 96, META),
-    )
-    back = swap_all(sent, "exp")
-    own = (own_part + after(across, sent).astype(f32)).astype(bf16)
+    owned, gain_sum = owned_sums(owned, grad_down)
+    own = (own_part + after(across, columns).astype(f32)).astype(bf16)
     at_1, at_3, at_z = to(own, 1), to(own, 3), to(own, 4)
-
-    sdown_rows = grad_sdown.reshape(N_CTX, 8, 4, 384).transpose(0, 2, 1, 3)
-    small = jnp.concatenate(
-        [back.reshape(N_CTX, 224, 384), sdown_rows.reshape(N_CTX, 32, 384)], axis=1
-    )
-    small, at_1, at_3, at_z = lax.optimization_barrier((small, at_1, at_3, at_z))
-    pieces = swap_all(small, "ctx")
+    owned = swap_all(
+        jnp.broadcast_to(after(owned, own), (N_CTX, OWNED_ROWS, HEAD_DIM)), "ctx"
+    )
+    gain_attn_sum, *dense = finish(
+        owned,
+        norm_attn.astype(f32).reshape(96, 1),
+        query_weight,
+        key_weight,
+        value_weight,
+    )
+
+    grad_kv, at_1, at_3, at_z = lax.optimization_barrier((grad_kv, at_1, at_3, at_z))
+    grad_kv = swap_all(after(grad_kv, owned), "ctx")
     at_z1, at_z3 = to(at_z, 1), to(at_z, 3)
-    late_own = jnp.sum(pieces.astype(f32), axis=0).astype(bf16)
-    late_own, at_z1, at_z3 = lax.optimization_barrier((late_own, at_z1, at_z3))
-    late = swap_all(jnp.broadcast_to(late_own, (N_CTX, 256, 384)), "ctx")
-    at_2, at_z2 = to(after(at_3, late_own), 1), to(at_z1, 3)
-    gain_sum, *dense = finish(late)
-    out_rows = lax.psum_scatter(
-        after(out_part, own).reshape(N_EXP * BLOCK, WIDTH), "exp", scatter_dimension=0, tiled=True
-    )
+    grad_query, at_z1, at_z3 = lax.optimization_barrier((grad_query, at_z1, at_z3))
+    at_2, at_z2 = to(after(at_3, grad_query), 1), to(at_z1, 3)
+    input_grad = input_back(grad_query, grad_kv, w_all, tokens[0], gain_attn, grad_middle)
     mixed = (middle + out_rows.astype(f32)).astype(bf16)[None]
-    near = unpack_experts(yz_s, 0, after((own, at_1, at_2, at_3), mixed, *dense))
+    near = unpack_experts(yz_s, 0, after((own, at_1, at_2, at_3), mixed, input_grad, *dense))
     experts = unpack_experts(yz_s, 1, (at_z, at_z1, at_z2, at_z3), near)
-    return (mixed, input_grad[None], gain_sum[0, :96], gain_sum[1, :96], *dense, *experts)
+    return (
+        mixed,
+        input_grad[None],
+        gain_attn_sum[:, 0],
+        gain_sum[12, :96],
+        *dense,
+        *experts,
+    )
 
 
 def solution(mesh):

time: 622 us -> 626 us (level)
  local copies, waits for them, and re-layouts: 46.9 us -> 60.7 us
  starting transfers between devices: 80 us -> 66.3 us
    ppermute x12, waiting for transfers between devices: 91.5 us -> 132 us  [to(): return lax.ppermute(rows, 'ctx', [(i, i ^ k) for i in range(N_CTX)])]
    all_gather x1, waiting for transfers between devices: 31.6 us -> 0.01 us  [on_device(): hidden_all = lax.all_gather(hidden_two, 'exp', axis=0, tiled=True)]
    ppermute x1 -> x2, waiting for transfers between devices: 6.14 us -> 27.5 us  [of_sequence(): other = lax.ppermute(rows, 'ctx', z_swap)]
    all_gather x1, waiting for transfers between devices: 20.8 us -> 0.59 us  [on_device(): up_all = lax.all_gather(after(up_meta, w_cat), 'exp', axis=0, tiled=True)]
    all_to_all x9, starting transfers between devices: 51.7 us -> 43 us  [swap_all(): lax.all_to_all(rows, axis, split_axis=0, concat_axis=0, tiled=True, axis_...]
    unnamed x129 -> x120, local copies, waits for them, and re-layouts: 34.1 us -> 41.8 us
    ppermute x12, starting transfers between devices: 23.8 us -> 16.5 us  [to(): return lax.ppermute(rows, 'ctx', [(i, i ^ k) for i in range(N_CTX)])]
  transfers between devices with their start and end apart: 28 -> 28, of which waited for: 21 -> 16; matrix products, arithmetic and copies ran while one was open for 6% -> 6% of each run, Pallas kernels for 23% -> 17%
where the time goes in v6:
time: 626 us; the launch traced here: 615 us
  waiting for transfers between devices  308 us (49%)
  Pallas kernels  146 us (23%)
  starting transfers between devices  66.3 us (11%)
  local copies, waits for them, and re-layouts  60.7 us (10%)
  between operations  14.8 us (2%)
  other arithmetic  10.3 us (2%)
  matrix products  9.46 us (2%)
    all_to_all x9, waiting for transfers between devices, swap_all(): lax.all_to_all(rows, axis, split_axis=0, concat_axis=0, tiled=True, axis_...  142 us
    ppermute x12, waiting for transfers between devices, to(): return lax.ppermute(rows, 'ctx', [(i, i ^ k) for i in range(N_CTX)])  132 us
    all_to_all x9, starting transfers between devices, swap_all(): lax.all_to_all(rows, axis, split_axis=0, concat_axis=0, tiled=True, axis_...  43 us
    unnamed x120, local copies, waits for them, and re-layouts  41.8 us
    pallas_call x1, Pallas kernels, expert_back(): pl.pallas_call(expert_kernel, grid_spec=pltpu.PrefetchScalarGridSpec(num_...  28.6 us
    ppermute x2, waiting for transfers between devices, of_sequence(): other = lax.ppermute(rows, 'ctx', z_swap)  27.5 us
    pallas_call x2, Pallas kernels, expert_weights(): pl.pallas_call(lambda *refs: expert_weights_kernel(halves, *refs), grid_s...  25.9 us
    ppermute x12, starting transfers between devices, to(): return lax.ppermute(rows, 'ctx', [(i, i ^ k) for i in range(N_CTX)])  16.5 us
  transfers between devices with their start and end apart: 28, of which 16 were waited for; matrix products, arithmetic and copies ran while one was open for 6% of the time, Pallas kernels for 17%

profile of v6, /device:TPU:0, one launch (start us, length us, event | category | flops | bytes accessed | tf_op | source)
XLA Modules:
  0.0 615.2 jit_solution(15284949720021137994)
XLA Ops:
  15.6 4.0 collective-permute-start
  20.3 4.9 all-to-all-start
  25.2 8.4 %collective-permute-done = bf16[1,128,1536]{2,1,0:T(8,128)(2,1)S(1)} collective-permute-done((bf16[1,128,1536]{2,1,0:T(8,128)(2,1)S(1)}, bf16[1,128,1536]{2,1,0:T(8,128)(2,1)S(1)}, u32[]{:S(2)}, u32[]{:S(2)}) %collective-permute-start) | collective-permute-done | bytes 393248 | tf_op jit(solution)/shard_map/ppermute | solution.py:960
  36.3 4.7 all-to-all-start.1
  48.5 30.4 %all-to-all-done.1 = bf16[4,2,128,1536]{3,2,1,0:T(8,128)(2,1)S(1)} async-done(((bf16[4,2,128,1536]{3,2,1,0:T(8,128)(2,1)}), bf16[4,2,128,1536]{3,2,1,0:T(8,128)(2,1)S(1)}, u32[]{:S(2)}, u32[]{:S(2)}) %all-to-all-start.1) | async-done | bytes 3145760 | tf_op jit(solution)/shard_map/all_to_all | solution.py:907
  79.0 5.2 all-to-all-start.2
  90.1 3.4 all-to-all-done.2
  96.3 7.7 %project.1 = (bf16[128,1536]{1,0:T(8,128)(2,1)S(1)}, bf16[8,128,1024]{2,1,0:T(8,128)(2,1)S(1)}) custom-call(bf16[1,128,1536]{2,1,0:T(8,128)(2,1)S(1)} %copy-done.18, bf16[8,128,1536]{2,1,0:T(8,128)(2,1)S(1)} %copy-done.2, bf16[1536,4096]{1,0:T(8,128)(2,1)} %all-gather.4.cloned.1.call-done.w_ref.wq_ref.wkv_ref), custom_call_target="tpu_custom_call" | custom-call | bytes 29520000 | tf_op jit(solution)/shard_map/project/pallas_call | solution.py:751
  104.0 5.8 attend.1
  111.6 4.8 copy-done
  119.0 2.5 collective-permute-start.1
  121.5 19.1 %collective-permute-done.1 = bf16[1,128,1536]{2,1,0:T(8,128)(2,1)S(1)} collective-permute-done((bf16[1,128,1536]{2,1,0:T(8,128)(2,1)S(1)}, bf16[1,128,1536]{2,1,0:T(8,128)(2,1)S(1)}, u32[]{:S(2)}, u32[]{:S(2)}) %collective-permute-start.1) | collective-permute-done | bytes 393248 | tf_op jit(solution)/shard_map/ppermute | solution.py:960
  142.6 6.0 all-to-all-start.3
  149.3 37.0 %all-to-all-done.3 = bf16[4,2,128,1536]{3,2,1,0:T(8,128)(2,1)} async-done(((bf16[4,2,128,1536]{3,2,1,0:T(8,128)(2,1)}), bf16[4,2,128,1536]{3,2,1,0:T(8,128)(2,1)}, u32[]{:S(2)}, u32[]{:S(2)}) %all-to-all-start.3) | async-done | bytes 3145760 | tf_op jit(solution)/shard_map/all_to_all | solution.py:907
  186.3 13.8 %place_rows.1 = (bf16[8,2,128,128]{3,2,1,0:T(8,128)(2,1)}, bf16[2,2,384,1536]{3,2,1,0:T(8,128)(2,1)}, f32[2,2,384,512]{3,2,1,0:T(8,128)}, f32[8,2,128,128]{3,2,1,0:T(8,128)}, f32[2,2,384,128]{3,2,1,0:T(8,128)}) custom-call(s32[1]{0:T(128)} %bitcast.7.at_ref, bf16[8,2,128,1664]{3,2,1,0:T(8,128)(2,1)} %bitcast.73, bf16[2,512,1536]{2,1,0:T(8,128)(2,1)} %wd_ref.1, ...), custom_call_target="tpu_custom_call" | custom-call | bytes 51660000 | tf_op jit(solution)/shard_map/place_rows/pallas_call | solution.py:356
  200.1 28.6 %expert_back.1 = (bf16[2,8,128,1536]{3,2,1,0:T(8,128)(2,1)}, bf16[2,2,384,1536]{3,2,1,0:T(8,128)(2,1)}, bf16[2,2,384,512]{3,2,1,0:T(8,128)(2,1)}, bf16[2,2,384,1...) custom-call(s32[1]{0:T(128)} %bitcast.7.at_ref, ...), custom_call_target="tpu_custom_call" | custom-call | bytes 103320000 | tf_op jit(solution)/shard_map/expert_back/pallas_call | solution.py:435
  228.8 2.2 slice_bitcast_fusion
  231.1 5.6 collective-permute-done.2
  236.8 2.6 fusion
  239.4 4.5 all-to-all-start.4
  244.6 12.8 %expert_weights.2 = (bf16[9216,128]{1,0:T(8,128)(2,1)}, bf16[9216,128]{1,0:T(8,128)(2,1)}) custom-call(s32[8]{0:T(128)} %stack.40.refs_0_, bf16[2,768,1536]{2,1,0:T(8,128)(2,1)} %bitcast.81, bf16[2,768,1536]{2,1,0:T(8,128)(2,1)} %bitcast.79, bf16[2,768,512]{2,1,0:T(8,128)(2,1)} %bitcast.63, bf16[2,768,1024]{2,1,0:T(8,128)(2,1)} %bitcast.74, ...), custom_call_target="tpu_custom_call" | custom-call | bytes 33210000 | tf_op jit(solution)/shard_map/expert_weights/pallas_call | solution.py:811
  259.4 13.0 %expert_weights.3 = (bf16[4608,128]{1,0:T(8,128)(2,1)}, bf16[4608,128]{1,0:T(8,128)(2,1)}, bf16[4608,128]{1,0:T(8,128)(2,1)}, bf16[4608,128]{1,0:T(8,128)(2,1)}) custom-call(s32[8]{0:T(128)} %stack.38.refs_0_, bf16[2,768,1536]{2,1,0:T(8,128)(2,1)} %bitcast.82, bf16[2,768,1536]{2,1,0:T(8,128)(2,1)} %bitcast.80, bf16[2,768,512]{2,1,0:T(8,128)(2,1)} %bitcast.64, ...), custom_call_target="tpu_custom_call" | custom-call | bytes 33210000 | tf_op jit(solution)/shard_map/expert_weights/pallas_call | solution.py:811
  272.4 5.4 convolution_convert_fusion
  283.4 9.8 %expert_output.1 = bf16[8,2,128,1536]{3,2,1,0:T(8,128)(2,1)} custom-call(s32[1]{0:T(128)} %bitcast.7.at_ref, bf16[2,2,384,512]{3,2,1,0:T(8,128)(2,1)S(1)} %copy-done.3, f32[2,2,384,128]{3,2,1,0:T(8,128)S(1)} %copy-done.35, bf16[8,2,128,128]{3,2,1,0:T(8,128)(2,1)S(1)} %copy-done.14, bf16[8,2,128,128]{3,2,1,0:T(8,128)(2,1)S(1)} %copy-done.5, ...), custom_call_target="tpu_custom_call" | custom-call | bytes 36900000 | tf_op jit(solution)/shard_map/expert_output/pallas_call | solution.py:487
  293.2 4.1 fusion.4
  299.6 5.7 middle_back.1
  306.2 8.7 %attend_back.1 = (bf16[128,1536]{1,0:T(8,128)(2,1)S(1)}, bf16[8,1776,128]{2,1,0:T(8,128)(2,1)}) custom-call(s32[1]{0:T(128)} %bitcast.ctx_ref, bf16[128,1536]{1,0:T(8,128)(2,1)S(1)} %copy-done.16, bf16[128,1536]{1,0:T(8,128)(2,1)S(1)} %get-tuple-element.133.ga_ref, f32[128,1536]{1,0:T(8,128)S(1)} %copy-done.32, f32[1536,128]{1,0:T(8,128)S(1)} %copy-done.34, ...), custom_call_target="tpu_custom_call" | custom-call | bytes 33210000 | tf_op jit(solution)/shard_map/attend_back/pallas_call | solution.py:191
  315.7 3.5 piece_sums.2
  322.6 4.7 all-to-all-start.5
  327.3 2.3 collective-permute-start.5
  331.6 47.5 %all-to-all-done.5.got_ref = bf16[8,1776,128]{2,1,0:T(8,128)(2,1)} async-done(((bf16[8,1776,128]{2,1,0:T(8,128)(2,1)}), bf16[8,1776,128]{2,1,0:T(8,128)(2,1)}, u32[]{:S(2)}, u32[]{:S(2)}) %all-to-all-start.5) | async-done | bytes 3637280 | tf_op jit(solution)/shard_map/all_to_all | solution.py:907
  379.1 7.8 %column_grads.1 = (bf16[16,112,512]{2,1,0:T(8,128)(2,1)}, bf16[8,128,128]{2,1,0:T(8,128)(2,1)}, bf16[96,128]{1,0:T(8,128)(2,1)}) custom-call(bf16[8,1776,128]{2,1,0:T(8,128)(2,1)} %all-to-all-done.5.got_ref, bf16[8,128,1536]{2,1,0:T(8,128)(2,1)} %copy-done.1, bf16[8,128,1536]{2,1,0:T(8,128)(2,1)} %bitcast.13.att_ref), custom_call_target="tpu_custom_call" | custom-call | bytes 29520000 | tf_op jit(solution)/shard_map/column_grads/pallas_call | solution.py:567
  386.9 20.4 %collective-permute-done.5.got_11 = bf16[4608,128]{1,0:T(8,128)(2,1)} collective-permute-done((bf16[4608,128]{1,0:T(8,128)(2,1)}, bf16[4608,128]{1,0:T(8,128)(2,1)}, u32[]{:S(2)}, u32[]{:S(2)}) %collective-permute-start.5) | collective-permute-done | bytes 1179680 | tf_op jit(solution)/shard_map/ppermute | solution.py:1010
  407.2 3.7 piece_sums.3
  412.4 2.6 collective-permute-start.7
  415.0 4.3 all-to-all-start.6
  419.3 56.8 %collective-permute-done.7 = bf16[4608,128]{1,0:T(8,128)(2,1)S(1)} collective-permute-done((bf16[4608,128]{1,0:T(8,128)(2,1)}, bf16[4608,128]{1,0:T(8,128)(2,1)S(1)}, u32[]{:S(2)}, u32[]{:S(2)}) %collective-permute-start.7) | collective-permute-done | bytes 1179680 | tf_op jit(solution)/shard_map/ppermute | solution.py:1010
  480.9 2.3 collective-permute-start.9
  483.2 24.5 %collective-permute-done.10.refs_0_ = bf16[4608,128]{1,0:T(8,128)(2,1)} collective-permute-done((bf16[4608,128]{1,0:T(8,128)(2,1)S(1)}, bf16[4608,128]{1,0:T(8,128)(2,1)}, u32[]{:S(2)}, u32[]{:S(2)}) %collective-permute-start.10) | collective-permute-done | bytes 1179680 | tf_op jit(solution)/shard_map/ppermute | solution.py:1010
  513.8 4.8 all-to-all-start.7
  518.5 19.4 %collective-permute-done.11.refs_1_ = bf16[4608,128]{1,0:T(8,128)(2,1)} collective-permute-done((bf16[4608,128]{1,0:T(8,128)(2,1)}, bf16[4608,128]{1,0:T(8,128)(2,1)}, u32[]{:S(2)}, u32[]{:S(2)}) %collective-permute-start.11) | collective-permute-done | bytes 1179680 | tf_op jit(solution)/shard_map/ppermute | solution.py:1010
  537.9 10.4 %collective-permute-done.12.refs_3_ = bf16[4608,128]{1,0:T(8,128)(2,1)} collective-permute-done((bf16[4608,128]{1,0:T(8,128)(2,1)}, bf16[4608,128]{1,0:T(8,128)(2,1)}, u32[]{:S(2)}, u32[]{:S(2)}) %collective-permute-start.12) | collective-permute-done | bytes 1179680 | tf_op jit(solution)/shard_map/ppermute | solution.py:1010
  550.6 7.7 %all-to-all-done.7.got_ref = bf16[8,736,128]{2,1,0:T(8,128)(2,1)S(1)} async-done(((bf16[8,736,128]{2,1,0:T(8,128)(2,1)}), bf16[8,736,128]{2,1,0:T(8,128)(2,1)S(1)}, u32[]{:S(2)}, u32[]{:S(2)}) %all-to-all-start.7) | async-done | bytes 1507360 | tf_op jit(solution)/shard_map/all_to_all | solution.py:907
  558.3 4.0 all-to-all-start.8
  567.0 15.6 %all-to-all-done.8.got_ref = bf16[8,128,128]{2,1,0:T(8,128)(2,1)} async-done(((bf16[8,128,128]{2,1,0:T(8,128)(2,1)}), bf16[8,128,128]{2,1,0:T(8,128)(2,1)}, u32[]{:S(2)}, u32[]{:S(2)}) %all-to-all-start.8) | async-done | bytes 262176 | tf_op jit(solution)/shard_map/all_to_all | solution.py:907
  585.4 7.1 %input_back.1 = bf16[128,1536]{1,0:T(8,128)(2,1)} custom-call(bf16[128,1536]{1,0:T(8,128)(2,1)S(1)} %copy-done.39, bf16[8,128,128]{2,1,0:T(8,128)(2,1)} %all-to-all-done.8.got_ref, bf16[1536,4096]{1,0:T(8,128)(2,1)} %all-gather.4.cloned.1.call-done.w_ref.wq_ref.wkv_ref, bf16[1536,4096]{1,0:T(8,128)(2,1)} %all-gather.4.cloned.1.call-done.w_ref.wq_ref.wkv_ref, ...), custom_call_target="tpu_custom_call" | custom-call | bytes 25830000 | tf_op jit(solution)/shard_map/input_back/pallas_call | solution.py:695
  595.6 5.8 unpack_experts.2
  601.4 6.8 %unpack_experts.3 = (f32[2,1536,512]{2,1,0:T(8,128)}, f32[2,1536,512]{2,1,0:T(8,128)}, f32[2,512,1536]{2,1,0:T(8,128)}) custom-call(s32[2]{0:T(128)S(1)} %copy-done.43, bf16[4608,128]{1,0:T(8,128)(2,1)} %collective-permute-done.10.refs_0_, ...), custom_call_target="tpu_custom_call", output_to_operand_aliasing={{0}: (5, {}), {1}: (6, {}), {2}: (7, {})} | custom-call | bytes 18450000 | tf_op jit(solution)/shard_map/unpack_experts/pallas_call | solution.py:848
  (187 shorter events, 77.7 us)
Async XLA Ops:
  7.2 8.4 %copy-start.4 = (bf16[1,128,1536]{2,1,0:T(8,128)(2,1)S(1)}, bf16[1,128,1536]{2,1,0:T(8,128)(2,1)}, u32[]{:S(2)}) copy-start(bf16[1,128,1536]{2,1,0:T(8,128)(2,1)} %x_ref.1) | copy-start | bytes 1179652
  7.2 12.4 %copy-start.53 = (bf16[96]{0:T(256)(128)(2,1)S(1)}, bf16[96]{0:T(256)(128)(2,1)}, u32[]{:S(2)}) copy-start(bf16[96]{0:T(256)(128)(2,1)} %param.19) | copy-start | bytes 580
  7.2 12.4 %copy-start.52 = (bf16[96]{0:T(256)(128)(2,1)S(1)}, bf16[96]{0:T(256)(128)(2,1)}, u32[]{:S(2)}) copy-start(bf16[96]{0:T(256)(128)(2,1)} %param.20) | copy-start | bytes 580
  7.2 86.2 %all-gather.4.cloned.1.call-start = ((), (), s32[]{:S(2)}) async-start(), calls=%async_computation.10 | async-start | bytes 13369344 | tf_op jit(solution)/shard_map/all_gather | solution.py:946
  12.0 137.2 %all-gather.8.cloned.1.call-start = ((), (), s32[]{:S(2)}) async-start(), calls=%async_computation.12 | async-start | bytes 7241728 | tf_op jit(solution)/shard_map/all_gather | solution.py:953
  15.6 18.1 %collective-permute-start = (bf16[1,128,1536]{2,1,0:T(8,128)(2,1)S(1)}, bf16[1,128,1536]{2,1,0:T(8,128)(2,1)S(1)}, u32[]{:S(2)}, u32[]{:S(2)}) collective-permute-start(bf16[1,128,1536]{2,1,0:T(8,128)(2,1)S(1)} %copy-done.4), channel_id=1, source_target_pairs={{0,64},{16,80},{32,96},{48,112},{64,0},{80,16},{96,32},{112,48},{1... | collective-permute-start | bytes 1179656 | tf_op jit(solution)/shard_map/ppermute | solution.py:960
  20.3 14.1 %all-to-all-start = ((bf16[16,1,192]{2,1,0:T(2,128)(2,1)}), bf16[16,1,192]{2,1,0:T(2,128)(2,1)S(1)}, u32[]{:S(2)}, u32[]{:S(2)}) async-start(bf16[16,1,192]{2,1,0:T(2,128)(2,1)} %broadcast_in_dim.24), calls=%async_computation | async-start | bytes 32768 | tf_op jit(solution)/shard_map/all_to_all | solution.py:907
  36.3 42.6 %all-to-all-start.1 = ((bf16[4,2,128,1536]{3,2,1,0:T(8,128)(2,1)}), bf16[4,2,128,1536]{3,2,1,0:T(8,128)(2,1)S(1)}, u32[]{:S(2)}, u32[]{:S(2)}) async-start(bf16[4,2,128,1536]{3,2,1,0:T(8,128)(2,1)} %broadcast_in_dim.25), calls=%async_computation.1 | async-start | bytes 6291456 | tf_op jit(solution)/shard_map/all_to_all | solution.py:907
  79.0 14.5 %all-to-all-start.2 = ((bf16[16,96,128]{2,1,0:T(8,128)(2,1)}), bf16[16,96,128]{2,1,0:T(8,128)(2,1)}, u32[]{:S(2)}, u32[]{:S(2)}) async-start(bf16[16,96,128]{2,1,0:T(8,128)(2,1)} %copy.62), calls=%async_computation.2 | async-start | bytes 786432 | tf_op jit(solution)/shard_map/all_to_all | solution.py:907
  84.2 116.0 %all-gather.6.cloned.1.call-start = ((), (), s32[]{:S(2)}) async-start(), calls=%async_computation.11 | async-start | bytes 6684672 | tf_op jit(solution)/shard_map/all_gather | solution.py:983
  104.0 14.1 %copy-start.15 = (bf16[128,1536]{1,0:T(8,128)(2,1)}, bf16[128,1536]{1,0:T(8,128)(2,1)S(1)}, u32[]{:S(2)}) copy-start(bf16[128,1536]{1,0:T(8,128)(2,1)S(1)} %get-tuple-element.103.q_ref) | copy-start | bytes 1179652
  119.0 21.6 %collective-permute-start.1 = (bf16[1,128,1536]{2,1,0:T(8,128)(2,1)S(1)}, bf16[1,128,1536]{2,1,0:T(8,128)(2,1)S(1)}, u32[]{:S(2)}, u32[]{:S(2)}) collective-permute-start(bf16[1,128,1536]{2,1,0:T(8,128)(2,1)S(1)} %bitcast.71), channel_id=1, source_target_pairs={{0,64},{16,80},{32,96},{48,112},{64,0},{80,16},{96,32},{112,48},{1... | collective-permute-start | bytes 1179656 | tf_op jit(solution)/shard_map/ppermute | solution.py:960
  142.6 43.6 %all-to-all-start.3 = ((bf16[4,2,128,1536]{3,2,1,0:T(8,128)(2,1)}), bf16[4,2,128,1536]{3,2,1,0:T(8,128)(2,1)}, u32[]{:S(2)}, u32[]{:S(2)}) async-start(bf16[4,2,128,1536]{3,2,1,0:T(8,128)(2,1)} %broadcast_in_dim.28), calls=%async_computation.3 | async-start | bytes 6291456 | tf_op jit(solution)/shard_map/all_to_all | solution.py:907
  148.7 37.6 %copy-start.9 = (bf16[128,1536]{1,0:T(8,128)(2,1)}, bf16[128,1536]{1,0:T(8,128)(2,1)S(1)}, u32[]{:S(2)}) copy-start(bf16[128,1536]{1,0:T(8,128)(2,1)S(1)} %constant_dynamic-update-slice_fusion.4.sdown_ref.sd_ref) | copy-start | bytes 1179652
  228.8 8.0 %copy-start.47 = (bf16[2,8,128,1536]{3,2,1,0:T(8,128)(2,1)S(1)}, bf16[2,8,128,1536]{3,2,1,0:T(8,128)(2,1)}, u32[]{:S(2)}) copy-start(bf16[2,8,128,1536]{3,2,1,0:T(8,128)(2,1)} %get-tuple-element.115) | copy-start | bytes 18874372
  231.0 5.7 collective-permute-start.2
  239.4 58.1 %all-to-all-start.4 = ((bf16[8,128,1536]{2,1,0:T(8,128)(2,1)}), bf16[8,128,1536]{2,1,0:T(8,128)(2,1)}, u32[]{:S(2)}, u32[]{:S(2)}) async-start(bf16[8,128,1536]{2,1,0:T(8,128)(2,1)} %fusion), calls=%async_computation.4 | async-start | bytes 6291456 | tf_op jit(solution)/shard_map/all_to_all | solution.py:907
  243.9 348.7 %reduce-scatter.2.cloned.1.call-start = ((), (), s32[]{:S(2)}) async-start(), calls=%async_computation.13 | async-start | bytes 6684672 | tf_op jit(solution)/shard_map/reduce_scatter | solution.py:1053
  257.4 58.2 %collective-permute-start.3 = (bf16[9216,128]{1,0:T(8,128)(2,1)}, bf16[9216,128]{1,0:T(8,128)(2,1)}, u32[]{:S(2)}, u32[]{:S(2)}) collective-permute-start(bf16[9216,128]{1,0:T(8,128)(2,1)} %get-tuple-element.119), channel_id=1, source_target_pairs={{0,16},{16,0},{32,48},{48,32},{64,80},{80,64},{96,112},{112,96},{1... | collective-permute-start | bytes 7077896 | tf_op jit(solution)/shard_map/ppermute | solution.py:1010
  258.1 57.6 %collective-permute-start.4 = (bf16[9216,128]{1,0:T(8,128)(2,1)}, bf16[9216,128]{1,0:T(8,128)(2,1)}, u32[]{:S(2)}, u32[]{:S(2)}) collective-permute-start(bf16[9216,128]{1,0:T(8,128)(2,1)} %get-tuple-element.128), channel_id=1, source_target_pairs={{0,48},{16,32},{32,16},{48,0},{64,112},{80,96},{96,80},{112,64},{1... | collective-permute-start | bytes 7077896 | tf_op jit(solution)/shard_map/ppermute | solution.py:1010
  259.4 13.0 %copy-start.51 = (bf16[8,2,128,128]{3,2,1,0:T(8,128)(2,1)S(1)}, bf16[8,2,128,128]{3,2,1,0:T(8,128)(2,1)}, u32[]{:S(2)}) copy-start(bf16[8,2,128,128]{3,2,1,0:T(8,128)(2,1)} %get-tuple-element.130) | copy-start | bytes 1572868
  299.6 6.6 %copy-start.34 = (f32[1536,128]{1,0:T(8,128)S(1)}, f32[1536,128]{1,0:T(8,128)}, u32[]{:S(2)}) copy-start(f32[1536,128]{1,0:T(8,128)} %copy-done.33) | copy-start | bytes 2359300
  306.2 9.4 %copy-start.20 = (bf16[4608,128]{1,0:T(8,128)(2,1)S(1)}, bf16[4608,128]{1,0:T(8,128)(2,1)}, u32[]{:S(2)}) copy-start(bf16[4608,128]{1,0:T(8,128)(2,1)} %get-tuple-element.121.p0) | copy-start | bytes 3538948
  306.2 9.4 %copy-start.21 = (bf16[4608,128]{1,0:T(8,128)(2,1)S(1)}, bf16[4608,128]{1,0:T(8,128)(2,1)}, u32[]{:S(2)}) copy-start(bf16[4608,128]{1,0:T(8,128)(2,1)} %get-tuple-element.127.p6) | copy-start | bytes 3538948
  306.2 9.4 %copy-start.22 = (bf16[4608,128]{1,0:T(8,128)(2,1)S(1)}, bf16[4608,128]{1,0:T(8,128)(2,1)}, u32[]{:S(2)}) copy-start(bf16[4608,128]{1,0:T(8,128)(2,1)} %get-tuple-element.125.p1) | copy-start | bytes 3538948
  306.2 9.4 %copy-start.23 = (bf16[4608,128]{1,0:T(8,128)(2,1)S(1)}, bf16[4608,128]{1,0:T(8,128)(2,1)}, u32[]{:S(2)}) copy-start(bf16[4608,128]{1,0:T(8,128)(2,1)} %get-tuple-element.126.p3) | copy-start | bytes 3538948
  322.6 56.5 %all-to-all-start.5 = ((bf16[8,1776,128]{2,1,0:T(8,128)(2,1)}), bf16[8,1776,128]{2,1,0:T(8,128)(2,1)}, u32[]{:S(2)}, u32[]{:S(2)}) async-start(bf16[8,1776,128]{2,1,0:T(8,128)(2,1)} %get-tuple-element.144), calls=%async_computation.6 | async-start | bytes 7274496 | tf_op jit(solution)/shard_map/all_to_all | solution.py:907
  327.3 80.0 %collective-permute-start.5 = (bf16[4608,128]{1,0:T(8,128)(2,1)}, bf16[4608,128]{1,0:T(8,128)(2,1)}, u32[]{:S(2)}, u32[]{:S(2)}) collective-permute-start(bf16[4608,128]{1,0:T(8,128)(2,1)} %copy-done.45), channel_id=1, source_target_pairs={{0,16},{16,0},{32,48},{48,32},{64,80},{80,64},{96,112},{112,96},{1... | collective-permute-start | bytes 3538952 | tf_op jit(solution)/shard_map/ppermute | solution.py:1010
  329.5 77.7 %collective-permute-start.6 = (bf16[4608,128]{1,0:T(8,128)(2,1)}, bf16[4608,128]{1,0:T(8,128)(2,1)}, u32[]{:S(2)}, u32[]{:S(2)}) collective-permute-start(bf16[4608,128]{1,0:T(8,128)(2,1)} %copy-done.44), channel_id=1, source_target_pairs={{0,48},{16,32},{32,16},{48,0},{64,112},{80,96},{96,80},{112,64},{1... | collective-permute-start | bytes 3538952 | tf_op jit(solution)/shard_map/ppermute | solution.py:1010
  379.1 28.2 %copy-start.12 = (f32[4608,128]{1,0:T(8,128)S(1)}, f32[4608,128]{1,0:T(8,128)}, u32[]{:S(2)}) copy-start(f32[4608,128]{1,0:T(8,128)} %copy-done.11) | copy-start | bytes 7077892
  412.4 63.8 %collective-permute-start.7 = (bf16[4608,128]{1,0:T(8,128)(2,1)}, bf16[4608,128]{1,0:T(8,128)(2,1)S(1)}, u32[]{:S(2)}, u32[]{:S(2)}) collective-permute-start(bf16[4608,128]{1,0:T(8,128)(2,1)} %get-tuple-element.152), channel_id=1, source_target_pairs={{0,64},{16,80},{32,96},{48,112},{64,0},{80,16},{96,32},{112,48},{1... | collective-permute-start | bytes 3538952 | tf_op jit(solution)/shard_map/ppermute | solution.py:1010
  415.0 96.6 %all-to-all-start.6 = ((bf16[16,112,512]{2,1,0:T(8,128)(2,1)}), bf16[16,112,512]{2,1,0:T(8,128)(2,1)S(1)}, u32[]{:S(2)}, u32[]{:S(2)}) async-start(bf16[16,112,512]{2,1,0:T(8,128)(2,1)} %get-tuple-element.149), calls=%async_computation.7 | async-start | bytes 3670016 | tf_op jit(solution)/shard_map/all_to_all | solution.py:907
  419.3 92.3 %copy-start.42 = (bf16[96,128]{1,0:T(8,128)(2,1)S(1)}, bf16[96,128]{1,0:T(8,128)(2,1)}, u32[]{:S(2)}) copy-start(bf16[96,128]{1,0:T(8,128)(2,1)} %get-tuple-element.157.down_ref) | copy-start | bytes 73732
  479.4 28.3 %collective-permute-start.10 = (bf16[4608,128]{1,0:T(8,128)(2,1)S(1)}, bf16[4608,128]{1,0:T(8,128)(2,1)}, u32[]{:S(2)}, u32[]{:S(2)}) collective-permute-start(bf16[4608,128]{1,0:T(8,128)(2,1)S(1)} %add_convert_fusion.refs_0_), channel_id=1, source_target_pairs={{0,64},{16,80},{32,96},{48,112},{64,0},{80,16},{96,32},{112,48},{1... | collective-permute-start | bytes 3538952 | tf_op jit(solution)/shard_map/ppermute | solution.py:1010
  479.5 28.2 %collective-permute-start.8 = (bf16[4608,128]{1,0:T(8,128)(2,1)S(1)}, bf16[4608,128]{1,0:T(8,128)(2,1)S(1)}, u32[]{:S(2)}, u32[]{:S(2)}) collective-permute-start(bf16[4608,128]{1,0:T(8,128)(2,1)S(1)} %add_convert_fusion.refs_0_), channel_id=1, source_target_pairs={{0,16},{16,0},{32,48},{48,32},{64,80},{80,64},{96,112},{112,96},{1... | collective-permute-start | bytes 3538952 | tf_op jit(solution)/shard_map/ppermute | solution.py:1010
  480.9 27.8 %collective-permute-start.9 = (bf16[4608,128]{1,0:T(8,128)(2,1)S(1)}, bf16[4608,128]{1,0:T(8,128)(2,1)S(1)}, u32[]{:S(2)}, u32[]{:S(2)}) collective-permute-start(bf16[4608,128]{1,0:T(8,128)(2,1)S(1)} %add_convert_fusion.refs_0_), channel_id=1, source_target_pairs={{0,48},{16,32},{32,16},{48,0},{64,112},{80,96},{96,80},{112,64},{1... | collective-permute-start | bytes 3538952 | tf_op jit(solution)/shard_map/ppermute | solution.py:1010
  508.7 29.2 %collective-permute-start.11 = (bf16[4608,128]{1,0:T(8,128)(2,1)}, bf16[4608,128]{1,0:T(8,128)(2,1)}, u32[]{:S(2)}, u32[]{:S(2)}) collective-permute-start(bf16[4608,128]{1,0:T(8,128)(2,1)} %collective-permute-done.10.refs_0_), channel_id=1, source_target_pairs={{0,16},{16,0},{32,48},{48,32},{64,80},{80,64},{96,112},{112,96},{1... | collective-permute-start | bytes 3538952 | tf_op jit(solution)/shard_map/ppermute | solution.py:1010
  509.8 38.5 %collective-permute-start.12 = (bf16[4608,128]{1,0:T(8,128)(2,1)}, bf16[4608,128]{1,0:T(8,128)(2,1)}, u32[]{:S(2)}, u32[]{:S(2)}) collective-permute-start(bf16[4608,128]{1,0:T(8,128)(2,1)} %collective-permute-done.10.refs_0_), channel_id=1, source_target_pairs={{0,48},{16,32},{32,16},{48,0},{64,112},{80,96},{96,80},{112,64},{1... | collective-permute-start | bytes 3538952 | tf_op jit(solution)/shard_map/ppermute | solution.py:1010
  511.6 38.3 %copy-start.54 = (bf16[96]{0:T(256)(128)(2,1)S(1)}, bf16[96]{0:T(256)(128)(2,1)}, u32[]{:S(2)}) copy-start(bf16[96]{0:T(256)(128)(2,1)} %param.19) | copy-start | bytes 580
  511.6 52.0 %copy-start.36 = (bf16[96,512]{1,0:T(8,128)(2,1)S(1)}, bf16[96,512]{1,0:T(8,128)(2,1)}, u32[]{:S(2)}) copy-start(bf16[96,512]{1,0:T(8,128)(2,1)} %wk_ref.1) | copy-start | bytes 294916
  512.4 51.2 %copy-start.28 = (bf16[96,1536]{1,0:T(8,128)(2,1)S(1)}, bf16[96,1536]{1,0:T(8,128)(2,1)}, u32[]{:S(2)}) copy-start(bf16[96,1536]{1,0:T(8,128)(2,1)} %wq_ref.1) | copy-start | bytes 884740
  513.8 44.6 %all-to-all-start.7 = ((bf16[8,736,128]{2,1,0:T(8,128)(2,1)}), bf16[8,736,128]{2,1,0:T(8,128)(2,1)S(1)}, u32[]{:S(2)}, u32[]{:S(2)}) async-start(bf16[8,736,128]{2,1,0:T(8,128)(2,1)} %broadcast_in_dim.30), calls=%async_computation.8 | async-start | bytes 3014656 | tf_op jit(solution)/shard_map/all_to_all | solution.py:907
  548.4 46.0 %collective-permute-start.14 = (bf16[4608,128]{1,0:T(8,128)(2,1)}, bf16[4608,128]{1,0:T(8,128)(2,1)}, u32[]{:S(2)}, u32[]{:S(2)}) collective-permute-start(bf16[4608,128]{1,0:T(8,128)(2,1)} %copy-done.26), channel_id=1, source_target_pairs={{0,16},{16,0},{32,48},{48,32},{64,80},{80,64},{96,112},{112,96},{1... | collective-permute-start | bytes 3538952 | tf_op jit(solution)/shard_map/ppermute | solution.py:1010
  548.4 53.0 %collective-permute-start.13 = (bf16[4608,128]{1,0:T(8,128)(2,1)}, bf16[4608,128]{1,0:T(8,128)(2,1)}, u32[]{:S(2)}, u32[]{:S(2)}) collective-permute-start(bf16[4608,128]{1,0:T(8,128)(2,1)} %collective-permute-done.11.refs_1_), channel_id=1, source_target_pairs={{0,48},{16,32},{32,16},{48,0},{64,112},{80,96},{96,80},{112,64},{1... | collective-permute-start | bytes 3538952 | tf_op jit(solution)/shard_map/ppermute | solution.py:1010
  558.3 24.2 %all-to-all-start.8 = ((bf16[8,128,128]{2,1,0:T(8,128)(2,1)}), bf16[8,128,128]{2,1,0:T(8,128)(2,1)}, u32[]{:S(2)}, u32[]{:S(2)}) async-start(bf16[8,128,128]{2,1,0:T(8,128)(2,1)} %get-tuple-element.160), calls=%async_computation.9 | async-start | bytes 524288 | tf_op jit(solution)/shard_map/all_to_all | solution.py:907
  585.4 7.2 %copy-start.8 = (f32[128,1536]{1,0:T(8,128)S(1)}, f32[128,1536]{1,0:T(8,128)}, u32[]{:S(2)}) copy-start(f32[128,1536]{1,0:T(8,128)} %copy-done.6) | copy-start | bytes 2359300
  585.4 9.0 %copy-start.25 = (bf16[4608,128]{1,0:T(8,128)(2,1)S(1)}, bf16[4608,128]{1,0:T(8,128)(2,1)}, u32[]{:S(2)}) copy-start(bf16[4608,128]{1,0:T(8,128)(2,1)} %copy-done.24) | copy-start | bytes 3538948
  585.4 9.0 %copy-start.43 = (s32[2]{0:T(128)S(1)}, s32[2]{0:T(128)}, u32[]{:S(2)}) copy-start(s32[2]{0:T(128)} %pad_add_fusion.at_ref) | copy-start | bytes 28
  (35 other events, 64.0 us)
Sparse Core Ops, SparseCore 0:
  12.1 80.4 all-gather.3
  94.9 54.3 all-gather.7
  151.5 43.1 all-gather.5
  322.7 136.4 reduce-scatter.1

commit v7 on v6

--- a/solution.py
+++ b/solution.py
@@ -478,7 +478,7 @@
     for chip in range(HALF):
         at = chip * CAP
         stacked = jnp.concatenate([outs[0][at : at + CAP], gap, outs[1][at : at + CAP], gap], 0)
-        part_ref[chip, 0] = (
+        part_ref[0, chip] = (
             dg(place_ref[chip, 0], stacked, NN) + dg(sact_ref[chip, 0], sd_ref[...], NN)
         ).astype(bf16)
 
@@ -497,9 +497,9 @@
                 whole((LOCAL_E, FF_E, WIDTH)),
                 whole((2 * SHARED, WIDTH)),
             ],
-            out_specs=by_core(WIDTH),
+            out_specs=pl.BlockSpec((1, HALF, BLOCK, WIDTH), lambda s, at: (s, 0, 0, 0)),
         ),
-        out_shape=jax.ShapeDtypeStruct((HALF, 2, BLOCK, WIDTH), bf16),
+        out_shape=jax.ShapeDtypeStruct((2, HALF, BLOCK, WIDTH), bf16),
         cost_estimate=cost(10),
         compiler_params=params(48),
         name="expert_output",
@@ -773,25 +773,24 @@
 PIECE = 2 * WIDTH + WIDTH * BLOCK // HEAD_DIM
 
 
-def expert_weights_kernel(
-    halves, at_ref, x_ref, geo_ref, act_ref, dgate_ref, dup_ref, *refs
-):
-    outs, turned = refs[:-1], refs[-1]
+def of_step(values, step):
+    out = jnp.int32(values[0])
+    for i, value in enumerate(values[1:], 1):
+        out = jnp.where(step == i, value, out)
+    return out
+
+
+def expert_weights_kernel(halved, at_ref, x_ref, geo_ref, act_ref, dgate_ref, dup_ref, *outs):
     step = pl.program_id(0)
-
-    @pl.when(step % 2 == 0)
-    def _():
-        turned[...] = x_ref[0].T
-
     rhs = jnp.concatenate([dgate_ref[0], dup_ref[0]], axis=1)
-    both = dg(turned[...], rhs, NN).astype(bf16)
+    both = dg(x_ref[0], rhs, TN).astype(bf16)
     down = dg(act_ref[0], geo_ref[0], TN).astype(bf16)
     for i in range(4):
 
         @pl.when(step == i)
         def _():
-            start = (i % 2) * PIECE if halves else 0
-            out = outs[i // 2 if halves else i].at[pl.ds(start, PIECE)]
+            start = (i % 2) * PIECE if halved else 0
+            out = outs[i // 2 if halved else i].at[pl.ds(start, PIECE)]
             out[:WIDTH] = both[:, :HEAD_DIM]
             out[WIDTH : 2 * WIDTH] = both[:, HEAD_DIM:]
             for m in range(WIDTH // HEAD_DIM):
@@ -799,35 +798,43 @@
                 out[at : at + BLOCK] = down[:, m * HEAD_DIM : (m + 1) * HEAD_DIM]
 
 
-def expert_weights(yz, steps, halves, arrived, grad_eo, act, grad_gu):
+def expert_weights(ctx_at, steps, halved, arrived, grad_eo, act, grad_gu):
     rows = 2 * ROWS
-    at = jnp.stack([yz[0] ^ r for r, _ in steps] + [yz[1] ^ side for _, side in steps])
-    rows_of = pl.BlockSpec((1, rows, WIDTH), lambda s, at: (at[4 + s], 0, 0))
+
+    def expert(s, at):
+        return (at[0] >> 2) ^ of_step([side for _, side in steps], s)
 
     def lanes(shift):
-        return pl.BlockSpec((1, rows, HEAD_DIM), lambda s, at: (at[4 + s], 0, shift + at[s]))
-
-    count, length = (2, 2 * PIECE) if halves else (4, PIECE)
-    return pl.pallas_call(
-        lambda *refs: expert_weights_kernel(halves, *refs),
+        return pl.BlockSpec(
+            (1, rows, HEAD_DIM),
+            lambda s, at: (
+                expert(s, at),
+                0,
+                shift + ((at[0] & 3) ^ of_step([r for r, _ in steps], s)),
+            ),
+        )
+
+    rows_of = pl.BlockSpec((1, rows, WIDTH), lambda s, at: (expert(s, at), 0, 0))
+    count, length = (2, 2 * PIECE) if halved else (4, PIECE)
+    return pl.pallas_call(
+        lambda *refs: expert_weights_kernel(halved, *refs),
         grid_spec=pltpu.PrefetchScalarGridSpec(
             num_scalar_prefetch=1,
             grid=(4,),
             in_specs=[rows_of, rows_of, lanes(0), lanes(0), lanes(4)],
             out_specs=[whole((length, HEAD_DIM))] * count,
-            scratch_shapes=[pltpu.VMEM((WIDTH, rows), bf16)],
         ),
         out_shape=[jax.ShapeDtypeStruct((length, HEAD_DIM), bf16)] * count,
         cost_estimate=cost(9),
         compiler_params=params(56),
         name="expert_weights",
-    )(at, arrived, grad_eo, act, grad_gu, grad_gu)
-
-
-def unpack_kernel(at_ref, *refs):
-    pieces, (gate_ref, up_ref, down_ref) = refs[:4], refs[-3:]
+    )(ctx_at, arrived, grad_eo, act, grad_gu, grad_gu)
+
+
+def unpack_kernel(count, at_ref, *refs):
+    pieces, (gate_ref, up_ref, down_ref) = refs[:count], refs[-3:]
     step = pl.program_id(0)
-    for i in range(4):
+    for i in range(count):
 
         @pl.when(step == i)
         def _():
@@ -841,16 +848,24 @@
                 )
 
 
-def unpack_experts(at, side, pieces, filled=()):
-    cols = pl.BlockSpec((1, WIDTH, HEAD_DIM), lambda s, at: (at[1] ^ side, 0, at[0] ^ s))
-    rows = pl.BlockSpec((1, BLOCK, WIDTH), lambda s, at: (at[1] ^ side, at[0] ^ s, 0))
+def unpack_experts(ctx_at, steps, pieces, filled=()):
+    count = len(steps)
+
+    def expert(s, at):
+        return (at[0] >> 2) ^ of_step([side for _, side in steps], s)
+
+    def units(s, at):
+        return (at[0] & 3) ^ of_step([r for r, _ in steps], s)
+
+    cols = pl.BlockSpec((1, WIDTH, HEAD_DIM), lambda s, at: (expert(s, at), 0, units(s, at)))
+    rows = pl.BlockSpec((1, BLOCK, WIDTH), lambda s, at: (expert(s, at), units(s, at), 0))
     anywhere = pl.BlockSpec(memory_space=pl.ANY)
     return pl.pallas_call(
-        unpack_kernel,
+        lambda *refs: unpack_kernel(count, *refs),
         grid_spec=pltpu.PrefetchScalarGridSpec(
             num_scalar_prefetch=1,
-            grid=(4,),
-            in_specs=[whole((PIECE, HEAD_DIM))] * 4 + [anywhere] * len(filled),
+            grid=(count,),
+            in_specs=[whole((PIECE, HEAD_DIM))] * count + [anywhere] * len(filled),
             out_specs=[cols, cols, rows],
         ),
         out_shape=[
@@ -858,11 +873,11 @@
             jax.ShapeDtypeStruct((LOCAL_E, WIDTH, FF_E), f32),
             jax.ShapeDtypeStruct((LOCAL_E, FF_E, WIDTH), f32),
         ],
-        input_output_aliases={5 + i: i for i in range(len(filled))},
-        cost_estimate=cost(5),
+        input_output_aliases={1 + count + i: i for i in range(len(filled))},
+        cost_estimate=cost(2 * count),
         compiler_params=params(48),
         name="unpack_experts",
-    )(at, *pieces, *filled)
+    )(ctx_at, *pieces, *filled)
 
 
 def relay_kernel(
@@ -939,8 +954,7 @@
     ctx_at = lax.axis_index("ctx").astype(jnp.int32)
     exp_s, ctx_s = exp_at.reshape(1), ctx_at.reshape(1)
 
-    y_at, z_at = ctx_at % 4, ctx_at // 4
-    yz_s = jnp.stack([y_at, z_at])
+    z_at = ctx_at // 4
 
     w_cat = jnp.concatenate([query_weight, out_weight, key_weight, value_weight], axis=1)
     w_all = lax.all_gather(w_cat, "exp", axis=0, tiled=True)
@@ -985,12 +999,12 @@
     att_seq = of_sequence(attended[None])
     place, grad_eo, grad_eh, grad_sh, slot_gate = place_rows(
         exp_s,
-        after(up_all, hidden_two, att_seq).reshape(HALF, 2, BLOCK, WIDTH + META),
+        after(up_all, hidden_two).reshape(HALF, 2, BLOCK, WIDTH + META),
         expert_down,
         shared_two,
     )
     part, arrived, act, grad_gu, shared_act, shared_grad = expert_back(
-        exp_s, hidden_all, place, grad_eh, grad_sh, expert_gate, expert_up, w_shared
+        exp_s, after(hidden_all, att_seq), place, grad_eh, grad_sh, expert_gate, expert_up, w_shared
     )
     summed = add_low(part[1], lax.ppermute(part[0], "exp", core_swap))
     grad_two = swap_all(summed, "exp", same_core)
@@ -1002,9 +1016,9 @@
         act.reshape(LOCAL_E, rows_e, FF_E),
         grad_gu.reshape(LOCAL_E, rows_e, 2 * FF_E),
     )
-    for_1, for_3 = expert_weights(yz_s, ((2, 0), (1, 0), (2, 1), (3, 1)), True, *operands)
+    for_1, for_3 = expert_weights(ctx_s, ((2, 0), (1, 0), (2, 1), (3, 1)), True, *operands)
     operands = (after(operands[0], for_1),) + operands[1:]
-    p0, p6, p1, p3 = expert_weights(yz_s, ((0, 0), (3, 0), (0, 1), (1, 1)), False, *operands)
+    p0, p6, p1, p3 = expert_weights(ctx_s, ((0, 0), (3, 0), (0, 1), (1, 1)), False, *operands)
 
     def to(rows, k):
         return lax.ppermute(rows, "ctx", [(i, i ^ k) for i in range(N_CTX)])
@@ -1025,11 +1039,7 @@
         ],
         axis=1,
     )
-    out_part = expert_output(
-        exp_s, after(act, p0), slot_gate, place, shared_act, expert_down, shared_two
-    )
-
-    grad_two = after(grad_two, out_part, extra)
+    grad_two = after(grad_two, p0, extra)
     grad_middle, grad_attn, grad_heads, gain_rows = middle_back(
         grad_two, middle, cotangent[0], gain_ffn, w_all
     )
@@ -1050,44 +1060,48 @@
         (from_3, 1),
     )
     got_11, got_30 = to(add_b, 1), to(add_a, 3)
-    out_rows = lax.psum_scatter(
-        after(out_part, add_a).reshape(N_EXP * BLOCK, WIDTH),
-        "exp",
-        scatter_dimension=0,
-        tiled=True,
-    )
-
-    columns, grad_kv, grad_down = column_grads(
-        swap_all(after(sent, add_a), "ctx"), hidden_seq, att_seq
-    )
+    got = swap_all(after(sent, add_a), "ctx")
+
+    columns, grad_kv, grad_down = column_grads(got, hidden_seq, att_seq)
+    grad_kv = swap_all(grad_kv, "ctx")
+    got_11, got_30, columns = after((got_11, got_30, columns), grad_kv)
+    own_part, side = piece_sums(side_kernel, (f32, bf16), part_0, part_1, got_11, got_30)
+    across = to(side, 4)
     owned = swap_all(columns, "exp")
-    own_part, side = piece_sums(
-        side_kernel, (f32, bf16), part_0, part_1, after(got_11, columns), got_30
-    )
-    across = to(side, 4)
+    out_part = expert_output(
+        exp_s, after(act, columns), slot_gate, place, shared_act, expert_down, shared_two
+    )
+    out_sum = add_low(out_part[1], lax.ppermute(out_part[0], "exp", core_swap))
     owned, gain_sum = owned_sums(owned, grad_down)
-    own = (own_part + after(across, columns).astype(f32)).astype(bf16)
+    own = (own_part + after(across, owned).astype(f32)).astype(bf16)
     at_1, at_3, at_z = to(own, 1), to(own, 3), to(own, 4)
-    owned = swap_all(
-        jnp.broadcast_to(after(owned, own), (N_CTX, OWNED_ROWS, HEAD_DIM)), "ctx"
+    owned = swap_all(jnp.broadcast_to(owned, (N_CTX, OWNED_ROWS, HEAD_DIM)), "ctx")
+    experts = unpack_experts(
+        ctx_s, ((0, 0), (1, 0), (3, 0), (0, 1)), (own, at_1, at_3, at_z)
     )
     gain_attn_sum, *dense = finish(
-        owned,
+        after(owned, experts[0]),
         norm_attn.astype(f32).reshape(96, 1),
         query_weight,
         key_weight,
         value_weight,
     )
 
-    grad_kv, at_1, at_3, at_z = lax.optimization_barrier((grad_kv, at_1, at_3, at_z))
-    grad_kv = swap_all(after(grad_kv, owned), "ctx")
     at_z1, at_z3 = to(at_z, 1), to(at_z, 3)
-    grad_query, at_z1, at_z3 = lax.optimization_barrier((grad_query, at_z1, at_z3))
-    at_2, at_z2 = to(after(at_3, grad_query), 1), to(at_z1, 3)
-    input_grad = input_back(grad_query, grad_kv, w_all, tokens[0], gain_attn, grad_middle)
-    mixed = (middle + out_rows.astype(f32)).astype(bf16)[None]
-    near = unpack_experts(yz_s, 0, after((own, at_1, at_2, at_3), mixed, input_grad, *dense))
-    experts = unpack_experts(yz_s, 1, (at_z, at_z1, at_z2, at_z3), near)
+    at_2, at_z2 = to(at_3, 1), to(at_z1, 3)
+    out_pieces = swap_all(after(out_sum, owned, experts[0]), "exp", same_core)
+    mixed = (middle + jnp.sum(out_pieces.astype(f32), axis=0)).astype(bf16)[None]
+    experts = unpack_experts(ctx_s, ((1, 1), (3, 1)), (at_z1, at_z3), experts)
+    input_grad = input_back(
+        after(grad_query, experts[0]),
+        grad_kv,
+        w_all,
+        tokens[0],
+        gain_attn,
+        grad_middle,
+    )
+    at_2 = after(at_2, mixed, input_grad, *dense)
+    experts = unpack_experts(ctx_s, ((2, 0), (2, 1)), (at_2, at_z2), experts)
     return (
         mixed,
         input_grad[None],

time: 626 us -> 583 us (0.931)
  waiting for transfers between devices: 308 us -> 244 us
  starting transfers between devices: 66.3 us -> 86.8 us
  other arithmetic: 10.3 us -> 17.5 us
    ppermute x12, waiting for transfers between devices: 132 us -> 91.7 us  [to(): return lax.ppermute(rows, 'ctx', [(i, i ^ k) for i in range(N_CTX)])]
    all_to_all x9 -> x10, waiting for transfers between devices: 142 us -> 108 us  [swap_all(): lax.all_to_all(rows, axis, split_axis=0, concat_axis=0, tiled=True, axis_...]
    all_to_all x9 -> x10, starting transfers between devices: 43 us -> 60 us  [swap_all(): lax.all_to_all(rows, axis, split_axis=0, concat_axis=0, tiled=True, axis_...]
    all_gather x1, waiting for transfers between devices: 0.01 us -> 9.56 us  [on_device(): hidden_all = lax.all_gather(hidden_two, 'exp', axis=0, tiled=True)]
    unnamed x120 -> x116, local copies, waits for them, and re-layouts: 41.8 us -> 37.4 us
    pallas_call x4 -> x5, Pallas kernels: 38.5 us -> 35.7 us  [the longest x2 22 us: expert_weights(): pl.pallas_call(lambda *refs: expert_weights_kernel(halved, *refs), grid_s...]
  transfers between devices with their start and end apart: 28 -> 29, of which waited for: 16 -> 21; matrix products, arithmetic and copies ran while one was open for 6% -> 8% of each run, Pallas kernels for 17% -> 19%
where the time goes in v7:
time: 583 us; the launch traced here: 572 us
  waiting for transfers between devices  244 us (42%)
  Pallas kernels  143 us (25%)
  starting transfers between devices  86.8 us (15%)
  local copies, waits for them, and re-layouts  57.3 us (10%)
  other arithmetic  17.5 us (3%)
  between operations  14.4 us (2%)
  matrix products  9.46 us (2%)
    all_to_all x10, waiting for transfers between devices, swap_all(): lax.all_to_all(rows, axis, split_axis=0, concat_axis=0, tiled=True, axis_...  108 us
    ppermute x12, waiting for transfers between devices, to(): return lax.ppermute(rows, 'ctx', [(i, i ^ k) for i in range(N_CTX)])  91.7 us
    all_to_all x10, starting transfers between devices, swap_all(): lax.all_to_all(rows, axis, split_axis=0, concat_axis=0, tiled=True, axis_...  60 us
    unnamed x116, local copies, waits for them, and re-layouts  37.4 us
    pallas_call x1, Pallas kernels, expert_back(): pl.pallas_call(expert_kernel, grid_spec=pltpu.PrefetchScalarGridSpec(num_...  28.6 us
    ppermute x2, waiting for transfers between devices, of_sequence(): other = lax.ppermute(rows, 'ctx', z_swap)  27.5 us
    pallas_call x2, Pallas kernels, expert_weights(): pl.pallas_call(lambda *refs: expert_weights_kernel(halved, *refs), grid_s...  22 us
    ppermute x12, starting transfers between devices, to(): return lax.ppermute(rows, 'ctx', [(i, i ^ k) for i in range(N_CTX)])  19.6 us
  transfers between devices with their start and end apart: 29, of which 21 were waited for; matrix products, arithmetic and copies ran while one was open for 8% of the time, Pallas kernels for 19%

profile of v7, /device:TPU:0, one launch (start us, length us, event | category | flops | bytes accessed | tf_op | source)
XLA Modules:
  0.0 572.1 jit_solution(15584238483254809212)
XLA Ops:
  15.6 4.0 collective-permute-start
  20.3 4.9 all-to-all-start
  25.2 8.4 %collective-permute-done = bf16[1,128,1536]{2,1,0:T(8,128)(2,1)S(1)} collective-permute-done((bf16[1,128,1536]{2,1,0:T(8,128)(2,1)S(1)}, bf16[1,128,1536]{2,1,0:T(8,128)(2,1)S(1)}, u32[]{:S(2)}, u32[]{:S(2)}) %collective-permute-start) | collective-permute-done | bytes 393248 | tf_op jit(solution)/shard_map/ppermute | solution.py:974
  36.3 4.7 all-to-all-start.1
  48.5 30.4 %all-to-all-done.1 = bf16[4,2,128,1536]{3,2,1,0:T(8,128)(2,1)S(1)} async-done(((bf16[4,2,128,1536]{3,2,1,0:T(8,128)(2,1)}), bf16[4,2,128,1536]{3,2,1,0:T(8,128)(2,1)S(1)}, u32[]{:S(2)}, u32[]{:S(2)}) %all-to-all-start.1) | async-done | bytes 3145760 | tf_op jit(solution)/shard_map/all_to_all | solution.py:922
  79.0 5.2 all-to-all-start.2
  90.1 3.4 all-to-all-done.2
  96.3 7.7 %project.1 = (bf16[128,1536]{1,0:T(8,128)(2,1)S(1)}, bf16[8,128,1024]{2,1,0:T(8,128)(2,1)S(1)}) custom-call(bf16[1,128,1536]{2,1,0:T(8,128)(2,1)S(1)} %copy-done.21, bf16[8,128,1536]{2,1,0:T(8,128)(2,1)S(1)} %copy-done.2, bf16[1536,4096]{1,0:T(8,128)(2,1)} %all-gather.4.cloned.1.call-done.w_ref.wq_ref.wkv_ref), custom_call_target="tpu_custom_call" | custom-call | bytes 29520000 | tf_op jit(solution)/shard_map/project/pallas_call | solution.py:751
  104.0 5.8 %attend.1 = (bf16[128,1536]{1,0:T(8,128)(2,1)S(1)}, f32[128,1536]{1,0:T(8,128)S(1)}, f32[1536,128]{1,0:T(8,128)S(1)}) custom-call(s32[1]{0:T(128)} %bitcast.ctx_ref.refs_0_, bf16[128,1536]{1,0:T(8,128)(2,1)S(1)} %get-tuple-element.98.q_ref, bf16[8,128,1024]{2,1,0:T(8,128)(2,1)S(1)} %get-tuple-element.99.k_ref.v_ref, ...), custom_call_target="tpu_custom_call" | custom-call | bytes 22140000 | tf_op jit(solution)/shard_map/attend/pallas_call | solution.py:99
  109.8 5.4 copy-done
  120.3 19.1 %collective-permute-done.1 = bf16[1,128,1536]{2,1,0:T(8,128)(2,1)S(1)} collective-permute-done((bf16[1,128,1536]{2,1,0:T(8,128)(2,1)S(1)}, bf16[1,128,1536]{2,1,0:T(8,128)(2,1)S(1)}, u32[]{:S(2)}, u32[]{:S(2)}) %collective-permute-start.1) | collective-permute-done | bytes 393248 | tf_op jit(solution)/shard_map/ppermute | solution.py:974
  141.4 6.0 %all-to-all-start.3 = ((bf16[4,2,128,1536]{3,2,1,0:T(8,128)(2,1)}), bf16[4,2,128,1536]{3,2,1,0:T(8,128)(2,1)}, u32[]{:S(2)}, u32[]{:S(2)}) async-start(bf16[4,2,128,1536]{3,2,1,0:T(8,128)(2,1)} %broadcast_in_dim.27), calls=%async_computation.3 | async-start | bytes 6291456 | tf_op jit(solution)/shard_map/all_to_all | solution.py:922
  149.3 13.7 %place_rows.1 = (bf16[8,2,128,128]{3,2,1,0:T(8,128)(2,1)}, bf16[2,2,384,1536]{3,2,1,0:T(8,128)(2,1)}, f32[2,2,384,512]{3,2,1,0:T(8,128)}, f32[8,2,128,128]{3,2,1,0:T(8,128)}, f32[2,2,384,128]{3,2,1,0:T(8,128)}) custom-call(s32[1]{0:T(128)} %bitcast.7.at_ref, bf16[8,2,128,1664]{3,2,1,0:T(8,128)(2,1)} %bitcast.73, bf16[2,512,1536]{2,1,0:T(8,128)(2,1)} %wd_ref.1, ...), custom_call_target="tpu_custom_call" | custom-call | bytes 51660000 | tf_op jit(solution)/shard_map/place_rows/pallas_call | solution.py:356
  162.9 22.1 %all-to-all-done.3 = bf16[4,2,128,1536]{3,2,1,0:T(8,128)(2,1)} async-done(((bf16[4,2,128,1536]{3,2,1,0:T(8,128)(2,1)}), bf16[4,2,128,1536]{3,2,1,0:T(8,128)(2,1)}, u32[]{:S(2)}, u32[]{:S(2)}) %all-to-all-start.3) | async-done | bytes 3145760 | tf_op jit(solution)/shard_map/all_to_all | solution.py:922
  185.1 9.6 %all-gather.6.cloned.1.call-done = bf16[2048,1536]{1,0:T(8,128)(2,1)} async-done(((bf16[128,1536]{1,0:T(8,128)(2,1)}), bf16[2048,1536]{1,0:T(8,128)(2,1)}) %all-gather.6.cloned.1.call-update) | async-done | bytes 6291472 | tf_op jit(solution)/shard_map/all_gather | solution.py:997
  194.6 28.6 %expert_back.1 = (bf16[2,8,128,1536]{3,2,1,0:T(8,128)(2,1)}, bf16[2,2,384,1536]{3,2,1,0:T(8,128)(2,1)}, bf16[2,2,384,512]{3,2,1,0:T(8,128)(2,1)}, bf16[2,2,384,1...) custom-call(s32[1]{0:T(128)} %bitcast.7.at_ref, ...), custom_call_target="tpu_custom_call" | custom-call | bytes 103320000 | tf_op jit(solution)/shard_map/expert_back/pallas_call | solution.py:435
  225.8 5.5 collective-permute-done.2
  233.9 4.8 all-to-all-start.4
  238.7 11.0 %expert_weights.2 = (bf16[9216,128]{1,0:T(8,128)(2,1)}, bf16[9216,128]{1,0:T(8,128)(2,1)}) custom-call(s32[1]{0:T(128)} %bitcast.ctx_ref.refs_0_, bf16[2,768,1536]{2,1,0:T(8,128)(2,1)} %bitcast.80, bf16[2,768,1536]{2,1,0:T(8,128)(2,1)} %bitcast.78, bf16[2,768,512]{2,1,0:T(8,128)(2,1)} %bitcast.63, bf16[2,768,1024]{2,1,0:T(8,128)(2,1)} %bitcast.74, ...), custom_call_target="tpu_custom_call" | custom-call | bytes 33210000 | tf_op jit(solution)/shard_map/expert_weights/pallas_call | solution.py:819
  253.4 11.0 %expert_weights.3 = (bf16[4608,128]{1,0:T(8,128)(2,1)}, bf16[4608,128]{1,0:T(8,128)(2,1)}, bf16[4608,128]{1,0:T(8,128)(2,1)}, bf16[4608,128]{1,0:T(8,128)(2,1)}) custom-call(s32[1]{0:T(128)} %bitcast.ctx_ref.refs_0_, bf16[2,768,1536]{2,1,0:T(8,128)(2,1)} %bitcast.81, bf16[2,768,1536]{2,1,0:T(8,128)(2,1)} %bitcast.79, bf16[2,768,512]{2,1,0:T(8,128)(2,1)} %bitcast.64, ...), custom_call_target="tpu_custom_call" | custom-call | bytes 33210000 | tf_op jit(solution)/shard_map/expert_weights/pallas_call | solution.py:819
  264.4 5.4 convolution_convert_fusion
  271.1 4.1 fusion.5
  276.1 8.4 %all-to-all-done.4.pieces_ref = bf16[8,128,1536]{2,1,0:T(8,128)(2,1)} async-done(((bf16[8,128,1536]{2,1,0:T(8,128)(2,1)}), bf16[8,128,1536]{2,1,0:T(8,128)(2,1)}, u32[]{:S(2)}, u32[]{:S(2)}) %all-to-all-start.4) | async-done | bytes 3145760 | tf_op jit(solution)/shard_map/all_to_all | solution.py:922
  286.7 5.7 middle_back.1
  293.4 8.6 %attend_back.1 = (bf16[128,1536]{1,0:T(8,128)(2,1)S(1)}, bf16[8,1776,128]{2,1,0:T(8,128)(2,1)}) custom-call(s32[1]{0:T(128)} %bitcast.ctx_ref.refs_0_, bf16[128,1536]{1,0:T(8,128)(2,1)S(1)} %copy-done.19, bf16[128,1536]{1,0:T(8,128)(2,1)S(1)} %get-tuple-element.127.ga_ref, f32[128,1536]{1,0:T(8,128)S(1)} %copy-done.36, f32[1536,128]{1,0:T(8,128)S(1)} %copy-done.38, ...), custom_call_target="tpu_custom_call" | custom-call | bytes 33210000 | tf_op jit(solution)/shard_map/attend_back/pallas_call | solution.py:191
  305.7 3.5 piece_sums.2
  314.0 5.7 all-to-all-start.5
  323.8 40.3 %all-to-all-done.5.got_ref = bf16[8,1776,128]{2,1,0:T(8,128)(2,1)} async-done(((bf16[8,1776,128]{2,1,0:T(8,128)(2,1)}), bf16[8,1776,128]{2,1,0:T(8,128)(2,1)}, u32[]{:S(2)}, u32[]{:S(2)}) %all-to-all-start.5) | async-done | bytes 3637280 | tf_op jit(solution)/shard_map/all_to_all | solution.py:922
  364.1 7.5 %column_grads.1 = (bf16[16,112,512]{2,1,0:T(8,128)(2,1)}, bf16[8,128,128]{2,1,0:T(8,128)(2,1)}, bf16[96,128]{1,0:T(8,128)(2,1)}) custom-call(bf16[8,1776,128]{2,1,0:T(8,128)(2,1)} %all-to-all-done.5.got_ref, bf16[8,128,1536]{2,1,0:T(8,128)(2,1)} %copy-done.1, bf16[8,128,1536]{2,1,0:T(8,128)(2,1)} %bitcast.10.att_ref), custom_call_target="tpu_custom_call" | custom-call | bytes 29520000 | tf_op jit(solution)/shard_map/column_grads/pallas_call | solution.py:567
  371.6 12.8 %all-to-all-start.6 = ((bf16[8,128,128]{2,1,0:T(8,128)(2,1)}), bf16[8,128,128]{2,1,0:T(8,128)(2,1)S(1)}, u32[]{:S(2)}, u32[]{:S(2)}) async-start(bf16[8,128,128]{2,1,0:T(8,128)(2,1)} %get-tuple-element.139), calls=%async_computation.6 | async-start | bytes 524288 | tf_op jit(solution)/shard_map/all_to_all | solution.py:922
  384.4 10.2 %collective-permute-done.5.got_11 = bf16[4608,128]{1,0:T(8,128)(2,1)S(1)} collective-permute-done((bf16[4608,128]{1,0:T(8,128)(2,1)}, bf16[4608,128]{1,0:T(8,128)(2,1)S(1)}, u32[]{:S(2)}, u32[]{:S(2)}) %collective-permute-start.5) | collective-permute-done | bytes 1179680 | tf_op jit(solution)/shard_map/ppermute | solution.py:1024
  397.7 4.1 all-to-all-start.7
  406.4 3.7 piece_sums.3
  412.5 9.8 %expert_output.1 = bf16[2,8,128,1536]{3,2,1,0:T(8,128)(2,1)} custom-call(s32[1]{0:T(128)} %bitcast.7.at_ref, bf16[2,2,384,512]{3,2,1,0:T(8,128)(2,1)S(1)} %copy-done.3, f32[2,2,384,128]{3,2,1,0:T(8,128)S(1)} %copy-done.34, bf16[8,2,128,128]{3,2,1,0:T(8,128)(2,1)S(1)} %copy-done.17, bf16[8,2,128,128]{3,2,1,0:T(8,128)(2,1)S(1)} %copy-done.5, ...), custom_call_target="tpu_custom_call" | custom-call | bytes 36900000 | tf_op jit(solution)/shard_map/expert_output/pallas_call | solution.py:487
  422.3 3.8 slice_bitcast_fusion
  426.9 23.5 %collective-permute-done.8 = bf16[4608,128]{1,0:T(8,128)(2,1)} collective-permute-done((bf16[4608,128]{1,0:T(8,128)(2,1)}, bf16[4608,128]{1,0:T(8,128)(2,1)}, u32[]{:S(2)}, u32[]{:S(2)}) %collective-permute-start.8) | collective-permute-done | bytes 1179680 | tf_op jit(solution)/shard_map/ppermute | solution.py:1024
  452.8 3.1 collective-permute-start.10
  459.6 3.6 all-to-all-start.8
  463.2 18.5 %collective-permute-done.9.refs_2_ = bf16[4608,128]{1,0:T(8,128)(2,1)} collective-permute-done((bf16[4608,128]{1,0:T(8,128)(2,1)S(1)}, bf16[4608,128]{1,0:T(8,128)(2,1)}, u32[]{:S(2)}, u32[]{:S(2)}) %collective-permute-start.9) | collective-permute-done | bytes 1179680 | tf_op jit(solution)/shard_map/ppermute | solution.py:1024
  483.4 9.3 %collective-permute-done.11.refs_4_ = bf16[4608,128]{1,0:T(8,128)(2,1)} collective-permute-done((bf16[4608,128]{1,0:T(8,128)(2,1)S(1)}, bf16[4608,128]{1,0:T(8,128)(2,1)}, u32[]{:S(2)}, u32[]{:S(2)}) %collective-permute-start.11) | collective-permute-done | bytes 1179680 | tf_op jit(solution)/shard_map/ppermute | solution.py:1024
  492.7 5.9 %unpack_experts.3 = (f32[2,1536,512]{2,1,0:T(8,128)}, f32[2,1536,512]{2,1,0:T(8,128)}, f32[2,512,1536]{2,1,0:T(8,128)}) custom-call(s32[1]{0:T(128)} %bitcast.ctx_ref.refs_0_, bf16[4608,128]{1,0:T(8,128)(2,1)S(1)} %add_convert_fusion.refs_1_, bf16[4608,128]{1,0:T(8,128)(2,1)} %collective-permute-done.9.refs_2_, ...), custom_call_target="tpu_custom_call" | custom-call | bytes 29520000 | tf_op jit(solution)/shard_map/unpack_experts/pallas_call | solution.py:863
  498.6 5.5 fusion
  504.1 8.4 %all-to-all-start.9 = ((bf16[8,128,1536]{2,1,0:T(8,128)(2,1)}), bf16[8,128,1536]{2,1,0:T(8,128)(2,1)}, u32[]{:S(2)}, u32[]{:S(2)}) async-start(bf16[8,128,1536]{2,1,0:T(8,128)(2,1)} %fusion), calls=%async_computation.9 | async-start | bytes 6291456 | tf_op jit(solution)/shard_map/all_to_all | solution.py:922
  512.5 3.6 collective-permute-start.13
  516.0 25.7 %collective-permute-done.12.refs_1_ = bf16[4608,128]{1,0:T(8,128)(2,1)} collective-permute-done((bf16[4608,128]{1,0:T(8,128)(2,1)}, bf16[4608,128]{1,0:T(8,128)(2,1)}, u32[]{:S(2)}, u32[]{:S(2)}) %collective-permute-start.12) | collective-permute-done | bytes 1179680 | tf_op jit(solution)/shard_map/ppermute | solution.py:1024
  547.3 4.2 unpack_experts.4
  551.4 7.0 %input_back.1 = bf16[128,1536]{1,0:T(8,128)(2,1)} custom-call(bf16[128,1536]{1,0:T(8,128)(2,1)S(1)} %copy-done.42, bf16[8,128,128]{2,1,0:T(8,128)(2,1)S(1)} %copy-done.31, bf16[1536,4096]{1,0:T(8,128)(2,1)} %all-gather.4.cloned.1.call-done.w_ref.wq_ref.wkv_ref, bf16[1536,4096]{1,0:T(8,128)(2,1)} %all-gather.4.cloned.1.call-done.w_ref.wq_ref.wkv_ref, ...), custom_call_target="tpu_custom_call" | custom-call | bytes 25830000 | tf_op jit(solution)/shard_map/input_back/pallas_call | solution.py:695
  561.7 3.7 unpack_experts.5
  (185 shorter events, 91.2 us)
Async XLA Ops:
  7.2 8.4 %copy-start.4 = (bf16[1,128,1536]{2,1,0:T(8,128)(2,1)S(1)}, bf16[1,128,1536]{2,1,0:T(8,128)(2,1)}, u32[]{:S(2)}) copy-start(bf16[1,128,1536]{2,1,0:T(8,128)(2,1)} %x_ref.1) | copy-start | bytes 1179652
  7.2 12.4 %copy-start.50 = (bf16[96]{0:T(256)(128)(2,1)S(1)}, bf16[96]{0:T(256)(128)(2,1)}, u32[]{:S(2)}) copy-start(bf16[96]{0:T(256)(128)(2,1)} %param.20) | copy-start | bytes 580
  7.2 12.4 %copy-start.51 = (bf16[96]{0:T(256)(128)(2,1)S(1)}, bf16[96]{0:T(256)(128)(2,1)}, u32[]{:S(2)}) copy-start(bf16[96]{0:T(256)(128)(2,1)} %param.19) | copy-start | bytes 580
  7.2 86.2 %all-gather.4.cloned.1.call-start = ((), (), s32[]{:S(2)}) async-start(), calls=%async_computation.10 | async-start | bytes 13369344 | tf_op jit(solution)/shard_map/all_gather | solution.py:960
  12.0 137.2 %all-gather.8.cloned.1.call-start = ((), (), s32[]{:S(2)}) async-start(), calls=%async_computation.12 | async-start | bytes 7241728 | tf_op jit(solution)/shard_map/all_gather | solution.py:967
  15.6 18.1 %collective-permute-start = (bf16[1,128,1536]{2,1,0:T(8,128)(2,1)S(1)}, bf16[1,128,1536]{2,1,0:T(8,128)(2,1)S(1)}, u32[]{:S(2)}, u32[]{:S(2)}) collective-permute-start(bf16[1,128,1536]{2,1,0:T(8,128)(2,1)S(1)} %copy-done.4), channel_id=1, source_target_pairs={{0,64},{16,80},{32,96},{48,112},{64,0},{80,16},{96,32},{112,48},{1... | collective-permute-start | bytes 1179656 | tf_op jit(solution)/shard_map/ppermute | solution.py:974
  20.3 14.1 %all-to-all-start = ((bf16[16,1,192]{2,1,0:T(2,128)(2,1)}), bf16[16,1,192]{2,1,0:T(2,128)(2,1)S(1)}, u32[]{:S(2)}, u32[]{:S(2)}) async-start(bf16[16,1,192]{2,1,0:T(2,128)(2,1)} %broadcast_in_dim.24), calls=%async_computation | async-start | bytes 32768 | tf_op jit(solution)/shard_map/all_to_all | solution.py:922
  36.3 42.6 %all-to-all-start.1 = ((bf16[4,2,128,1536]{3,2,1,0:T(8,128)(2,1)}), bf16[4,2,128,1536]{3,2,1,0:T(8,128)(2,1)S(1)}, u32[]{:S(2)}, u32[]{:S(2)}) async-start(bf16[4,2,128,1536]{3,2,1,0:T(8,128)(2,1)} %broadcast_in_dim.25), calls=%async_computation.1 | async-start | bytes 6291456 | tf_op jit(solution)/shard_map/all_to_all | solution.py:922
  79.0 14.5 %all-to-all-start.2 = ((bf16[16,96,128]{2,1,0:T(8,128)(2,1)}), bf16[16,96,128]{2,1,0:T(8,128)(2,1)}, u32[]{:S(2)}, u32[]{:S(2)}) async-start(bf16[16,96,128]{2,1,0:T(8,128)(2,1)} %copy.65), calls=%async_computation.2 | async-start | bytes 786432 | tf_op jit(solution)/shard_map/all_to_all | solution.py:922
  84.2 110.5 %all-gather.6.cloned.1.call-start = ((), (), s32[]{:S(2)}) async-start(), calls=%async_computation.11 | async-start | bytes 6684672 | tf_op jit(solution)/shard_map/all_gather | solution.py:997
  104.0 12.9 %copy-start.18 = (bf16[128,1536]{1,0:T(8,128)(2,1)}, bf16[128,1536]{1,0:T(8,128)(2,1)S(1)}, u32[]{:S(2)}) copy-start(bf16[128,1536]{1,0:T(8,128)(2,1)S(1)} %get-tuple-element.98.q_ref) | copy-start | bytes 1179652
  109.8 7.1 %copy-start.35 = (f32[128,1536]{1,0:T(8,128)}, f32[128,1536]{1,0:T(8,128)S(1)}, u32[]{:S(2)}) copy-start(f32[128,1536]{1,0:T(8,128)S(1)} %get-tuple-element.128.attf_ref) | copy-start | bytes 2359300
  109.8 7.1 %copy-start.37 = (f32[1536,128]{1,0:T(8,128)}, f32[1536,128]{1,0:T(8,128)S(1)}, u32[]{:S(2)}) copy-start(f32[1536,128]{1,0:T(8,128)S(1)} %get-tuple-element.129.log_ref) | copy-start | bytes 2359300
  117.8 21.6 %collective-permute-start.1 = (bf16[1,128,1536]{2,1,0:T(8,128)(2,1)S(1)}, bf16[1,128,1536]{2,1,0:T(8,128)(2,1)S(1)}, u32[]{:S(2)}, u32[]{:S(2)}) collective-permute-start(bf16[1,128,1536]{2,1,0:T(8,128)(2,1)S(1)} %bitcast.71), channel_id=1, source_target_pairs={{0,64},{16,80},{32,96},{48,112},{64,0},{80,16},{96,32},{112,48},{1... | collective-permute-start | bytes 1179656 | tf_op jit(solution)/shard_map/ppermute | solution.py:974
  141.4 43.6 %all-to-all-start.3 = ((bf16[4,2,128,1536]{3,2,1,0:T(8,128)(2,1)}), bf16[4,2,128,1536]{3,2,1,0:T(8,128)(2,1)}, u32[]{:S(2)}, u32[]{:S(2)}) async-start(bf16[4,2,128,1536]{3,2,1,0:T(8,128)(2,1)} %broadcast_in_dim.27), calls=%async_computation.3 | async-start | bytes 6291456 | tf_op jit(solution)/shard_map/all_to_all | solution.py:922
  223.3 8.0 %copy-start.46 = (bf16[2,8,128,1536]{3,2,1,0:T(8,128)(2,1)S(1)}, bf16[2,8,128,1536]{3,2,1,0:T(8,128)(2,1)}, u32[]{:S(2)}) copy-start(bf16[2,8,128,1536]{3,2,1,0:T(8,128)(2,1)} %get-tuple-element.111) | copy-start | bytes 18874372
  225.5 5.7 %collective-permute-start.2 = (bf16[8,128,1536]{2,1,0:T(8,128)(2,1)S(1)}, bf16[8,128,1536]{2,1,0:T(8,128)(2,1)S(1)}, u32[]{:S(2)}, u32[]{:S(2)}) collective-permute-start(bf16[8,128,1536]{2,1,0:T(8,128)(2,1)S(1)} %slice_bitcast_fusion.2), channel_id=1, source_target_pairs={{0,1},{1,0},{2,3},{3,2},{4,5},{5,4},{6,7},{7,6},{8,9},{9,8},{10,11... | collective-permute-start | bytes 9437192 | tf_op jit(solution)/shard_map/ppermute | solution.py:1009
  233.9 50.7 %all-to-all-start.4 = ((bf16[8,128,1536]{2,1,0:T(8,128)(2,1)}), bf16[8,128,1536]{2,1,0:T(8,128)(2,1)}, u32[]{:S(2)}, u32[]{:S(2)}) async-start(bf16[8,128,1536]{2,1,0:T(8,128)(2,1)} %fusion.1), calls=%async_computation.4 | async-start | bytes 6291456 | tf_op jit(solution)/shard_map/all_to_all | solution.py:922
  249.6 53.4 %collective-permute-start.3 = (bf16[9216,128]{1,0:T(8,128)(2,1)}, bf16[9216,128]{1,0:T(8,128)(2,1)}, u32[]{:S(2)}, u32[]{:S(2)}) collective-permute-start(bf16[9216,128]{1,0:T(8,128)(2,1)} %get-tuple-element.115), channel_id=1, source_target_pairs={{0,16},{16,0},{32,48},{48,32},{64,80},{80,64},{96,112},{112,96},{1... | collective-permute-start | bytes 7077896 | tf_op jit(solution)/shard_map/ppermute | solution.py:1024
  251.1 13.3 %copy-start.49 = (bf16[8,2,128,128]{3,2,1,0:T(8,128)(2,1)S(1)}, bf16[8,2,128,128]{3,2,1,0:T(8,128)(2,1)}, u32[]{:S(2)}) copy-start(bf16[8,2,128,128]{3,2,1,0:T(8,128)(2,1)} %get-tuple-element.123) | copy-start | bytes 1572868
  251.1 54.5 %collective-permute-start.4 = (bf16[9216,128]{1,0:T(8,128)(2,1)}, bf16[9216,128]{1,0:T(8,128)(2,1)}, u32[]{:S(2)}, u32[]{:S(2)}) collective-permute-start(bf16[9216,128]{1,0:T(8,128)(2,1)} %get-tuple-element.121), channel_id=1, source_target_pairs={{0,48},{16,32},{32,16},{48,0},{64,112},{80,96},{96,80},{112,64},{1... | collective-permute-start | bytes 7077896 | tf_op jit(solution)/shard_map/ppermute | solution.py:1024
  286.7 6.6 %copy-start.19 = (bf16[128,1536]{1,0:T(8,128)(2,1)S(1)}, bf16[128,1536]{1,0:T(8,128)(2,1)}, u32[]{:S(2)}) copy-start(bf16[128,1536]{1,0:T(8,128)(2,1)} %copy-done.18) | copy-start | bytes 1179652
  286.7 6.6 %copy-start.36 = (f32[128,1536]{1,0:T(8,128)S(1)}, f32[128,1536]{1,0:T(8,128)}, u32[]{:S(2)}) copy-start(f32[128,1536]{1,0:T(8,128)} %copy-done.35) | copy-start | bytes 2359300
  286.7 6.6 %copy-start.38 = (f32[1536,128]{1,0:T(8,128)S(1)}, f32[1536,128]{1,0:T(8,128)}, u32[]{:S(2)}) copy-start(f32[1536,128]{1,0:T(8,128)} %copy-done.37) | copy-start | bytes 2359300
  293.4 12.3 %copy-start.23 = (bf16[4608,128]{1,0:T(8,128)(2,1)S(1)}, bf16[4608,128]{1,0:T(8,128)(2,1)}, u32[]{:S(2)}) copy-start(bf16[4608,128]{1,0:T(8,128)(2,1)} %get-tuple-element.117.p0) | copy-start | bytes 3538948
  293.4 12.3 %copy-start.24 = (bf16[4608,128]{1,0:T(8,128)(2,1)S(1)}, bf16[4608,128]{1,0:T(8,128)(2,1)}, u32[]{:S(2)}) copy-start(bf16[4608,128]{1,0:T(8,128)(2,1)} %get-tuple-element.120.p6) | copy-start | bytes 3538948
  293.4 12.3 %copy-start.25 = (bf16[4608,128]{1,0:T(8,128)(2,1)S(1)}, bf16[4608,128]{1,0:T(8,128)(2,1)}, u32[]{:S(2)}) copy-start(bf16[4608,128]{1,0:T(8,128)(2,1)} %get-tuple-element.118.p1) | copy-start | bytes 3538948
  293.4 12.3 %copy-start.26 = (bf16[4608,128]{1,0:T(8,128)(2,1)S(1)}, bf16[4608,128]{1,0:T(8,128)(2,1)}, u32[]{:S(2)}) copy-start(bf16[4608,128]{1,0:T(8,128)(2,1)} %get-tuple-element.119.p3) | copy-start | bytes 3538948
  314.0 50.1 %all-to-all-start.5 = ((bf16[8,1776,128]{2,1,0:T(8,128)(2,1)}), bf16[8,1776,128]{2,1,0:T(8,128)(2,1)}, u32[]{:S(2)}, u32[]{:S(2)}) async-start(bf16[8,1776,128]{2,1,0:T(8,128)(2,1)} %get-tuple-element.137), calls=%async_computation.5 | async-start | bytes 7274496 | tf_op jit(solution)/shard_map/all_to_all | solution.py:922
  319.7 74.9 %collective-permute-start.5 = (bf16[4608,128]{1,0:T(8,128)(2,1)}, bf16[4608,128]{1,0:T(8,128)(2,1)S(1)}, u32[]{:S(2)}, u32[]{:S(2)}) collective-permute-start(bf16[4608,128]{1,0:T(8,128)(2,1)} %copy-done.45), channel_id=1, source_target_pairs={{0,16},{16,0},{32,48},{48,32},{64,80},{80,64},{96,112},{112,96},{1... | collective-permute-start | bytes 3538952 | tf_op jit(solution)/shard_map/ppermute | solution.py:1024
  321.7 73.9 %collective-permute-start.6 = (bf16[4608,128]{1,0:T(8,128)(2,1)}, bf16[4608,128]{1,0:T(8,128)(2,1)}, u32[]{:S(2)}, u32[]{:S(2)}) collective-permute-start(bf16[4608,128]{1,0:T(8,128)(2,1)} %copy-done.44), channel_id=1, source_target_pairs={{0,48},{16,32},{32,16},{48,0},{64,112},{80,96},{96,80},{112,64},{1... | collective-permute-start | bytes 3538952 | tf_op jit(solution)/shard_map/ppermute | solution.py:1024
  371.6 26.1 %all-to-all-start.6 = ((bf16[8,128,128]{2,1,0:T(8,128)(2,1)}), bf16[8,128,128]{2,1,0:T(8,128)(2,1)S(1)}, u32[]{:S(2)}, u32[]{:S(2)}) async-start(bf16[8,128,128]{2,1,0:T(8,128)(2,1)} %get-tuple-element.139), calls=%async_computation.6 | async-start | bytes 524288 | tf_op jit(solution)/shard_map/all_to_all | solution.py:922
  397.7 12.4 %copy-start.30 = (bf16[8,128,128]{2,1,0:T(8,128)(2,1)}, bf16[8,128,128]{2,1,0:T(8,128)(2,1)S(1)}, u32[]{:S(2)}) copy-start(bf16[8,128,128]{2,1,0:T(8,128)(2,1)S(1)} %all-to-all-done.6.got_ref) | copy-start | bytes 786436
  397.7 29.0 %all-to-all-start.7 = ((bf16[16,112,512]{2,1,0:T(8,128)(2,1)}), bf16[16,112,512]{2,1,0:T(8,128)(2,1)S(1)}, u32[]{:S(2)}, u32[]{:S(2)}) async-start(bf16[16,112,512]{2,1,0:T(8,128)(2,1)} %get-tuple-element.140), calls=%async_computation.7 | async-start | bytes 3670016 | tf_op jit(solution)/shard_map/all_to_all | solution.py:922
  411.5 38.9 %collective-permute-start.8 = (bf16[4608,128]{1,0:T(8,128)(2,1)}, bf16[4608,128]{1,0:T(8,128)(2,1)}, u32[]{:S(2)}, u32[]{:S(2)}) collective-permute-start(bf16[4608,128]{1,0:T(8,128)(2,1)} %get-tuple-element.150), channel_id=1, source_target_pairs={{0,64},{16,80},{32,96},{48,112},{64,0},{80,16},{96,32},{112,48},{1... | collective-permute-start | bytes 3538952 | tf_op jit(solution)/shard_map/ppermute | solution.py:1024
  426.1 72.5 %collective-permute-start.7 = (bf16[8,128,1536]{2,1,0:T(8,128)(2,1)}, bf16[8,128,1536]{2,1,0:T(8,128)(2,1)}, u32[]{:S(2)}, u32[]{:S(2)}) collective-permute-start(bf16[8,128,1536]{2,1,0:T(8,128)(2,1)} %slice_bitcast_fusion), channel_id=1, source_target_pairs={{0,1},{1,0},{2,3},{3,2},{4,5},{5,4},{6,7},{7,6},{8,9},{9,8},{10,11... | collective-permute-start | bytes 9437192 | tf_op jit(solution)/shard_map/ppermute | solution.py:1074
  452.7 29.0 %collective-permute-start.9 = (bf16[4608,128]{1,0:T(8,128)(2,1)S(1)}, bf16[4608,128]{1,0:T(8,128)(2,1)}, u32[]{:S(2)}, u32[]{:S(2)}) collective-permute-start(bf16[4608,128]{1,0:T(8,128)(2,1)S(1)} %add_convert_fusion.refs_1_), channel_id=1, source_target_pairs={{0,16},{16,0},{32,48},{48,32},{64,80},{80,64},{96,112},{112,96},{1... | collective-permute-start | bytes 3538952 | tf_op jit(solution)/shard_map/ppermute | solution.py:1024
  452.8 30.7 %collective-permute-start.10 = (bf16[4608,128]{1,0:T(8,128)(2,1)S(1)}, bf16[4608,128]{1,0:T(8,128)(2,1)}, u32[]{:S(2)}, u32[]{:S(2)}) collective-permute-start(bf16[4608,128]{1,0:T(8,128)(2,1)S(1)} %add_convert_fusion.refs_1_), channel_id=1, source_target_pairs={{0,48},{16,32},{32,16},{48,0},{64,112},{80,96},{96,80},{112,64},{1... | collective-permute-start | bytes 3538952 | tf_op jit(solution)/shard_map/ppermute | solution.py:1024
  455.9 36.8 %collective-permute-start.11 = (bf16[4608,128]{1,0:T(8,128)(2,1)S(1)}, bf16[4608,128]{1,0:T(8,128)(2,1)}, u32[]{:S(2)}, u32[]{:S(2)}) collective-permute-start(bf16[4608,128]{1,0:T(8,128)(2,1)S(1)} %add_convert_fusion.refs_1_), channel_id=1, source_target_pairs={{0,64},{16,80},{32,96},{48,112},{64,0},{80,16},{96,32},{112,48},{1... | collective-permute-start | bytes 3538952 | tf_op jit(solution)/shard_map/ppermute | solution.py:1024
  459.6 44.4 %all-to-all-start.8 = ((bf16[8,736,128]{2,1,0:T(8,128)(2,1)}), bf16[8,736,128]{2,1,0:T(8,128)(2,1)S(1)}, u32[]{:S(2)}, u32[]{:S(2)}) async-start(bf16[8,736,128]{2,1,0:T(8,128)(2,1)} %broadcast_in_dim.29), calls=%async_computation.8 | async-start | bytes 3014656 | tf_op jit(solution)/shard_map/all_to_all | solution.py:922
  504.1 39.2 %copy-start.52 = (bf16[96]{0:T(256)(128)(2,1)S(1)}, bf16[96]{0:T(256)(128)(2,1)}, u32[]{:S(2)}) copy-start(bf16[96]{0:T(256)(128)(2,1)} %param.19) | copy-start | bytes 580
  504.1 39.8 %copy-start.29 = (bf16[96,1536]{1,0:T(8,128)(2,1)S(1)}, bf16[96,1536]{1,0:T(8,128)(2,1)}, u32[]{:S(2)}) copy-start(bf16[96,1536]{1,0:T(8,128)(2,1)} %wq_ref.1) | copy-start | bytes 884740
  504.1 39.8 %copy-start.39 = (bf16[96,512]{1,0:T(8,128)(2,1)S(1)}, bf16[96,512]{1,0:T(8,128)(2,1)}, u32[]{:S(2)}) copy-start(bf16[96,512]{1,0:T(8,128)(2,1)} %wk_ref.1) | copy-start | bytes 294916
  504.1 54.3 %all-to-all-start.9 = ((bf16[8,128,1536]{2,1,0:T(8,128)(2,1)}), bf16[8,128,1536]{2,1,0:T(8,128)(2,1)}, u32[]{:S(2)}, u32[]{:S(2)}) async-start(bf16[8,128,1536]{2,1,0:T(8,128)(2,1)} %fusion), calls=%async_computation.9 | async-start | bytes 6291456 | tf_op jit(solution)/shard_map/all_to_all | solution.py:922
  512.5 29.2 %collective-permute-start.12 = (bf16[4608,128]{1,0:T(8,128)(2,1)}, bf16[4608,128]{1,0:T(8,128)(2,1)}, u32[]{:S(2)}, u32[]{:S(2)}) collective-permute-start(bf16[4608,128]{1,0:T(8,128)(2,1)} %collective-permute-done.11.refs_4_), channel_id=1, source_target_pairs={{0,16},{16,0},{32,48},{48,32},{64,80},{80,64},{96,112},{112,96},{1... | collective-permute-start | bytes 3538952 | tf_op jit(solution)/shard_map/ppermute | solution.py:1024
  512.5 34.8 %collective-permute-start.13 = (bf16[4608,128]{1,0:T(8,128)(2,1)}, bf16[4608,128]{1,0:T(8,128)(2,1)}, u32[]{:S(2)}, u32[]{:S(2)}) collective-permute-start(bf16[4608,128]{1,0:T(8,128)(2,1)} %collective-permute-done.11.refs_4_), channel_id=1, source_target_pairs={{0,48},{16,32},{32,16},{48,0},{64,112},{80,96},{96,80},{112,64},{1... | collective-permute-start | bytes 3538952 | tf_op jit(solution)/shard_map/ppermute | solution.py:1024
  516.0 45.7 %collective-permute-start.14 = (bf16[4608,128]{1,0:T(8,128)(2,1)}, bf16[4608,128]{1,0:T(8,128)(2,1)S(1)}, u32[]{:S(2)}, u32[]{:S(2)}) collective-permute-start(bf16[4608,128]{1,0:T(8,128)(2,1)} %collective-permute-done.10.refs_3_), channel_id=1, source_target_pairs={{0,16},{16,0},{32,48},{48,32},{64,80},{80,64},{96,112},{112,96},{1... | collective-permute-start | bytes 3538952 | tf_op jit(solution)/shard_map/ppermute | solution.py:1024
  541.7 20.0 %collective-permute-start.15 = (bf16[4608,128]{1,0:T(8,128)(2,1)}, bf16[4608,128]{1,0:T(8,128)(2,1)}, u32[]{:S(2)}, u32[]{:S(2)}) collective-permute-start(bf16[4608,128]{1,0:T(8,128)(2,1)} %collective-permute-done.12.refs_1_), channel_id=1, source_target_pairs={{0,48},{16,32},{32,16},{48,0},{64,112},{80,96},{96,80},{112,64},{1... | collective-permute-start | bytes 3538952 | tf_op jit(solution)/shard_map/ppermute | solution.py:1024
  (34 other events, 88.5 us)
Sparse Core Ops, SparseCore 0:
  12.1 80.4 all-gather.3
  94.9 54.3 all-gather.7
  151.5 43.0 all-gather.5

commit v8 on v7

--- a/solution.py
+++ b/solution.py
@@ -210,7 +210,7 @@
             jax.ShapeDtypeStruct((N_CTX, SENT_ROWS, HEAD_DIM), bf16),
         ],
         scratch_shapes=[pltpu.VMEM((KV_HEADS, BLOCK, GROUP * HEAD_DIM), f32)],
-        cost_estimate=cost(9),
+        cost_estimate=cost(2),
         compiler_params=params(48),
         name="attend_back",
     )(ctx_at, qkv, grad_att, att_f, logs, kv_all, kv_all, grad_attn, extra, gain_rows)
@@ -292,7 +292,7 @@
             jax.ShapeDtypeStruct((BLOCK, WIDTH), bf16),
             jax.ShapeDtypeStruct((16, HEAD_DIM), f32),
         ],
-        cost_estimate=cost(5),
+        cost_estimate=cost(1),
         compiler_params=params(48),
         name="middle_back",
     )(pieces, middle, upstream, gain, w_all)
@@ -378,6 +378,18 @@
     )(exp_at, up_all, expert_down, shared_two)
 
 
+def store_part(chip, rows, others, own_ref):
+    step, each = pl.program_id(0), HALF // len(others)
+
+    @pl.when(step == 0)
+    def _():
+        others[chip // each][chip % each] = rows
+
+    @pl.when(step == 1)
+    def _():
+        own_ref[chip] = rows
+
+
 def expert_kernel(
     at_ref,
     hid_ref,
@@ -387,7 +399,8 @@
     wg_ref,
     wu_ref,
     ws_ref,
-    part_ref,
+    other_ref,
+    own_ref,
     x_ref,
     act_ref,
     dgu_ref,
@@ -426,9 +439,8 @@
         sgrad_ref[chip, 0] = sgrad
         at = chip * CAP
         stacked = jnp.concatenate([pairs[0][at : at + CAP], gap, pairs[1][at : at + CAP], gap], 0)
-        part_ref[0, chip] = (
-            dg(place_ref[chip, 0], stacked, NN) + dg(sgrad, ws_ref[...], NT)
-        ).astype(bf16)
+        rows = (dg(place_ref[chip, 0], stacked, NN) + dg(sgrad, ws_ref[...], NT)).astype(bf16)
+        store_part(chip, rows, (other_ref,), own_ref)
 
 
 def expert_back(exp_at, hidden, place, geh, gsh, wg, wu, ws):
@@ -447,7 +459,8 @@
                 whole((WIDTH, 2 * SHARED)),
             ],
             out_specs=[
-                pl.BlockSpec((1, HALF, BLOCK, WIDTH), lambda s, at: (s, 0, 0, 0)),
+                whole((HALF, BLOCK, WIDTH)),
+                whole((HALF, BLOCK, WIDTH)),
                 by_step(WIDTH),
                 by_step(FF_E),
                 by_step(2 * FF_E),
@@ -456,7 +469,8 @@
             ],
         ),
         out_shape=[
-            jax.ShapeDtypeStruct((2, HALF, BLOCK, WIDTH), bf16),
+            jax.ShapeDtypeStruct((HALF, BLOCK, WIDTH), bf16),
+            jax.ShapeDtypeStruct((HALF, BLOCK, WIDTH), bf16),
             jax.ShapeDtypeStruct((LOCAL_E, 2, ROWS, WIDTH), bf16),
             jax.ShapeDtypeStruct((LOCAL_E, 2, ROWS, FF_E), bf16),
             jax.ShapeDtypeStruct((LOCAL_E, 2, ROWS, 2 * FF_E), bf16),
@@ -469,7 +483,7 @@
     )(exp_at, hidden, place, geh, gsh, wg, wu, ws)
 
 
-def output_kernel(at_ref, act_ref, gate_ref, place_ref, sact_ref, wd_ref, sd_ref, part_ref):
+def output_kernel(at_ref, act_ref, gate_ref, place_ref, sact_ref, wd_ref, sd_ref, own_ref, *others):
     outs = []
     for e in range(LOCAL_E):
         out = dg(act_ref[e, 0], wd_ref[e], NN).astype(bf16).astype(f32)
@@ -478,9 +492,8 @@
     for chip in range(HALF):
         at = chip * CAP
         stacked = jnp.concatenate([outs[0][at : at + CAP], gap, outs[1][at : at + CAP], gap], 0)
-        part_ref[0, chip] = (
-            dg(place_ref[chip, 0], stacked, NN) + dg(sact_ref[chip, 0], sd_ref[...], NN)
-        ).astype(bf16)
+        rows = dg(place_ref[chip, 0], stacked, NN) + dg(sact_ref[chip, 0], sd_ref[...], NN)
+        store_part(chip, rows.astype(bf16), others, own_ref)
 
 
 def expert_output(exp_at, act, gate, place, sact, wd, sd):
@@ -497,10 +510,10 @@
                 whole((LOCAL_E, FF_E, WIDTH)),
                 whole((2 * SHARED, WIDTH)),
             ],
-            out_specs=pl.BlockSpec((1, HALF, BLOCK, WIDTH), lambda s, at: (s, 0, 0, 0)),
+            out_specs=[whole((HALF, BLOCK, WIDTH))] * 2,
         ),
-        out_shape=jax.ShapeDtypeStruct((2, HALF, BLOCK, WIDTH), bf16),
-        cost_estimate=cost(10),
+        out_shape=[jax.ShapeDtypeStruct((HALF, BLOCK, WIDTH), bf16)] * 2,
+        cost_estimate=cost(2),
         compiler_params=params(48),
         name="expert_output",
     )(exp_at, act, gate, place, sact, wd, sd)
@@ -773,6 +786,32 @@
 PIECE = 2 * WIDTH + WIDTH * BLOCK // HEAD_DIM
 
 
+def spread_kernel(at_ref, own_ref, got_ref, *outs):
+    total = (own_ref[0].astype(f32) + got_ref[0].astype(f32)).astype(bf16)
+    for k in range(HALF):
+
+        @pl.when(pl.program_id(0) == k)
+        def _():
+            outs[k][...] = total
+
+
+def spread_sums(exp_at, own, got):
+    spec = pl.BlockSpec((1, BLOCK, WIDTH), lambda k, at: ((at[0] >> 1) ^ k, 0, 0))
+    return pl.pallas_call(
+        spread_kernel,
+        grid_spec=pltpu.PrefetchScalarGridSpec(
+            num_scalar_prefetch=1,
+            grid=(HALF,),
+            in_specs=[spec, spec],
+            out_specs=[whole((BLOCK, WIDTH))] * HALF,
+        ),
+        out_shape=[jax.ShapeDtypeStruct((BLOCK, WIDTH), bf16)] * HALF,
+        cost_estimate=cost(4),
+        compiler_params=params(32),
+        name="spread_sums",
+    )(exp_at, own, got)
+
+
 def of_step(values, step):
     out = jnp.int32(values[0])
     for i, value in enumerate(values[1:], 1):
@@ -825,7 +864,7 @@
             out_specs=[whole((length, HEAD_DIM))] * count,
         ),
         out_shape=[jax.ShapeDtypeStruct((length, HEAD_DIM), bf16)] * count,
-        cost_estimate=cost(9),
+        cost_estimate=cost(2),
         compiler_params=params(56),
         name="expert_weights",
     )(ctx_at, arrived, grad_eo, act, grad_gu, grad_gu)
@@ -906,7 +945,7 @@
         in_specs=specs,
         out_specs=[pl.BlockSpec((PIECE // 4, HEAD_DIM), lambda i: (i, 0))] * len(kinds),
         out_shape=[jax.ShapeDtypeStruct((PIECE, HEAD_DIM), kind) for kind in kinds],
-        cost_estimate=cost(4),
+        cost_estimate=cost(1),
         compiler_params=params(32),
         name="piece_sums",
     )(*arrays)
@@ -1003,10 +1042,10 @@
         expert_down,
         shared_two,
     )
-    part, arrived, act, grad_gu, shared_act, shared_grad = expert_back(
+    other, part, arrived, act, grad_gu, shared_act, shared_grad = expert_back(
         exp_s, after(hidden_all, att_seq), place, grad_eh, grad_sh, expert_gate, expert_up, w_shared
     )
-    summed = add_low(part[1], lax.ppermute(part[0], "exp", core_swap))
+    summed = add_low(part, lax.ppermute(other, "exp", core_swap))
     grad_two = swap_all(summed, "exp", same_core)
 
     rows_e = 2 * ROWS
@@ -1028,7 +1067,6 @@
     grad_scols = dg(hidden_all.reshape(N_EXP * BLOCK, WIDTH), shared_grad_late, TN).astype(bf16)
     act_late = after(shared_act, p0).reshape(N_EXP * BLOCK, META)
     grad_sdown = dg(act_late, up_all, TN)[:SHARED, :WIDTH].astype(bf16)
-
     extra = jnp.concatenate(
         [
             jnp.pad(
@@ -1039,6 +1077,7 @@
         ],
         axis=1,
     )
+
     grad_two = after(grad_two, p0, extra)
     grad_middle, grad_attn, grad_heads, gain_rows = middle_back(
         grad_two, middle, cotangent[0], gain_ffn, w_all
@@ -1059,25 +1098,38 @@
         (from_1, 1),
         (from_3, 1),
     )
-    got_11, got_30 = to(add_b, 1), to(add_a, 3)
-    got = swap_all(after(sent, add_a), "ctx")
-
-    columns, grad_kv, grad_down = column_grads(got, hidden_seq, att_seq)
-    grad_kv = swap_all(grad_kv, "ctx")
-    got_11, got_30, columns = after((got_11, got_30, columns), grad_kv)
-    own_part, side = piece_sums(side_kernel, (f32, bf16), part_0, part_1, got_11, got_30)
+    own_part, side = piece_sums(
+        side_kernel, (f32, bf16), part_0, part_1, to(add_b, 1), to(add_a, 3)
+    )
     across = to(side, 4)
+
+    got = swap_all(after(sent, side), "ctx")
+    out_part, out_other = expert_output(
+        exp_s, after(act, side), slot_gate, place, shared_act, expert_down, shared_two
+    )
+    out_sums = spread_sums(exp_s, out_part, lax.ppermute(out_other, "exp", core_swap))
+    own = (own_part + after(across, out_part).astype(f32)).astype(bf16)
+    at_1, at_3, at_z = to(own, 1), to(own, 3), to(own, 4)
+    columns, grad_kv, grad_down = column_grads(got, after(hidden_seq, own, out_sums[0]), att_seq)
+    columns, at_1, at_3 = lax.optimization_barrier((columns, at_1, at_3))
     owned = swap_all(columns, "exp")
-    out_part = expert_output(
-        exp_s, after(act, columns), slot_gate, place, shared_act, expert_down, shared_two
-    )
-    out_sum = add_low(out_part[1], lax.ppermute(out_part[0], "exp", core_swap))
     owned, gain_sum = owned_sums(owned, grad_down)
-    own = (own_part + after(across, owned).astype(f32)).astype(bf16)
-    at_1, at_3, at_z = to(own, 1), to(own, 3), to(own, 4)
+    owned, at_z1, at_z3 = lax.optimization_barrier((owned, to(at_z, 1), to(at_z, 3)))
+    at_2, at_z2 = to(at_3, 1), to(at_z1, 3)
+    out_rows = middle + out_sums[0].astype(f32)
+    for k in range(1, HALF):
+        moved = lax.ppermute(
+            after(out_sums[k], owned), "exp", [(i, i ^ (2 * k)) for i in range(N_EXP)]
+        )
+        out_rows = out_rows + moved.astype(f32)
+    mixed = out_rows.astype(bf16)[None]
+    experts = unpack_experts(
+        ctx_s, ((0, 0), (1, 0), (3, 0), (0, 1)), (after(own, owned), at_1, at_3, at_z)
+    )
     owned = swap_all(jnp.broadcast_to(owned, (N_CTX, OWNED_ROWS, HEAD_DIM)), "ctx")
+    grad_kv = swap_all(after(grad_kv, owned), "ctx")
     experts = unpack_experts(
-        ctx_s, ((0, 0), (1, 0), (3, 0), (0, 1)), (own, at_1, at_3, at_z)
+        ctx_s, ((2, 0), (1, 1), (3, 1), (2, 1)), (at_2, at_z1, at_z3, at_z2), experts
     )
     gain_attn_sum, *dense = finish(
         after(owned, experts[0]),
@@ -1086,22 +1138,9 @@
         key_weight,
         value_weight,
     )
-
-    at_z1, at_z3 = to(at_z, 1), to(at_z, 3)
-    at_2, at_z2 = to(at_3, 1), to(at_z1, 3)
-    out_pieces = swap_all(after(out_sum, owned, experts[0]), "exp", same_core)
-    mixed = (middle + jnp.sum(out_pieces.astype(f32), axis=0)).astype(bf16)[None]
-    experts = unpack_experts(ctx_s, ((1, 1), (3, 1)), (at_z1, at_z3), experts)
     input_grad = input_back(
-        after(grad_query, experts[0]),
-        grad_kv,
-        w_all,
-        tokens[0],
-        gain_attn,
-        grad_middle,
-    )
-    at_2 = after(at_2, mixed, input_grad, *dense)
-    experts = unpack_experts(ctx_s, ((2, 0), (2, 1)), (at_2, at_z2), experts)
+        after(grad_query, dense[0]), grad_kv, w_all, tokens[0], gain_attn, grad_middle
+    )
     return (
         mixed,
         input_grad[None],

time: 583 us -> 574 us (0.985)
  local copies, waits for them, and re-layouts: 57.3 us -> 48.9 us
  Pallas kernels: 143 us -> 149 us
    ppermute x2 -> x9, waiting for transfers between devices: 5.47 us -> 41.4 us  [the longest x7 35.8 us: on_device(): lax.ppermute(after(out_sums[k], owned), 'exp', [(i, i ^ 2 * k) for i in r...]
    all_to_all x10 -> x9, waiting for transfers between devices: 108 us -> 87 us  [swap_all(): lax.all_to_all(rows, axis, split_axis=0, concat_axis=0, tiled=True, axis_...]
    ppermute x12, waiting for transfers between devices: 91.7 us -> 76.7 us  [to(): return lax.ppermute(rows, 'ctx', [(i, i ^ k) for i in range(N_CTX)])]
    all_to_all x10 -> x9, starting transfers between devices: 60 us -> 46.1 us  [swap_all(): lax.all_to_all(rows, axis, split_axis=0, concat_axis=0, tiled=True, axis_...]
    ppermute x2 -> x9, starting transfers between devices: 0.49 us -> 14.1 us  [the longest x7 13.8 us: on_device(): lax.ppermute(after(out_sums[k], owned), 'exp', [(i, i ^ 2 * k) for i in r...]
    squeeze x2 -> x0, local copies, waits for them, and re-layouts: 6.02 us -> none  [the longest x1 3.78 us: on_device(): out_sum = add_low(out_part[1], lax.ppermute(out_part[0], 'exp', core_swap))]
    unnamed x116 -> x118, local copies, waits for them, and re-layouts: 37.4 us -> 34.9 us
    pallas_call x3 -> x2, Pallas kernels: 13.7 us -> 11.9 us  [unpack_experts(): pl.pallas_call(lambda *refs: unpack_kernel(count, *refs), grid_spec=pltpu...]
  transfers between devices with their start and end apart: 29 -> 35, of which waited for: 21 -> 23; matrix products, arithmetic and copies ran while one was open for 8% -> 6% of each run, Pallas kernels for 19% -> 18%
where the time goes in v8:
time: 574 us; the launch traced here: 564 us
  waiting for transfers between devices  242 us (42%)
  Pallas kernels  149 us (26%)
  starting transfers between devices  88.1 us (15%)
  local copies, waits for them, and re-layouts  48.9 us (9%)
  between operations  14.7 us (3%)
  other arithmetic  13 us (2%)
  matrix products  9.51 us (2%)
    all_to_all x9, waiting for transfers between devices, swap_all(): lax.all_to_all(rows, axis, split_axis=0, concat_axis=0, tiled=True, axis_...  87 us
    ppermute x12, waiting for transfers between devices, to(): return lax.ppermute(rows, 'ctx', [(i, i ^ k) for i in range(N_CTX)])  76.7 us
    all_to_all x9, starting transfers between devices, swap_all(): lax.all_to_all(rows, axis, split_axis=0, concat_axis=0, tiled=True, axis_...  46.1 us
    ppermute x7, waiting for transfers between devices, on_device(): lax.ppermute(after(out_sums[k], owned), 'exp', [(i, i ^ 2 * k) for i in r...  35.8 us
    unnamed x118, local copies, waits for them, and re-layouts  34.9 us
    pallas_call x1, Pallas kernels, expert_back(): pl.pallas_call(expert_kernel, grid_spec=pltpu.PrefetchScalarGridSpec(num_...  32.6 us
    ppermute x2, waiting for transfers between devices, of_sequence(): other = lax.ppermute(rows, 'ctx', z_swap)  27.5 us
    pallas_call x2, Pallas kernels, expert_weights(): pl.pallas_call(lambda *refs: expert_weights_kernel(halved, *refs), grid_s...  22 us
  transfers between devices with their start and end apart: 35, of which 23 were waited for; matrix products, arithmetic and copies ran while one was open for 6% of the time, Pallas kernels for 18%

profile of v8, /device:TPU:0, one launch (start us, length us, event | category | flops | bytes accessed | tf_op | source)
XLA Modules:
  0.0 564.5 jit_solution(10473132616858938812)
XLA Ops:
  15.6 4.0 collective-permute-start
  20.3 4.9 all-to-all-start
  25.2 8.4 %collective-permute-done = bf16[1,128,1536]{2,1,0:T(8,128)(2,1)S(1)} collective-permute-done((bf16[1,128,1536]{2,1,0:T(8,128)(2,1)S(1)}, bf16[1,128,1536]{2,1,0:T(8,128)(2,1)S(1)}, u32[]{:S(2)}, u32[]{:S(2)}) %collective-permute-start) | collective-permute-done | bytes 393248 | tf_op jit(solution)/shard_map/ppermute | solution.py:1013
  36.3 4.7 all-to-all-start.1
  48.5 30.4 %all-to-all-done.1 = bf16[4,2,128,1536]{3,2,1,0:T(8,128)(2,1)S(1)} async-done(((bf16[4,2,128,1536]{3,2,1,0:T(8,128)(2,1)}), bf16[4,2,128,1536]{3,2,1,0:T(8,128)(2,1)S(1)}, u32[]{:S(2)}, u32[]{:S(2)}) %all-to-all-start.1) | async-done | bytes 3145760 | tf_op jit(solution)/shard_map/all_to_all | solution.py:961
  79.0 5.2 all-to-all-start.2
  89.9 3.5 all-to-all-done.2
  96.3 7.7 %project.1 = (bf16[128,1536]{1,0:T(8,128)(2,1)S(1)}, bf16[8,128,1024]{2,1,0:T(8,128)(2,1)S(1)}) custom-call(bf16[1,128,1536]{2,1,0:T(8,128)(2,1)S(1)} %copy-done.18, bf16[8,128,1536]{2,1,0:T(8,128)(2,1)S(1)} %copy-done.2, bf16[1536,4096]{1,0:T(8,128)(2,1)} %all-gather.4.cloned.1.call-done.w_ref.wq_ref.wkv_ref), custom_call_target="tpu_custom_call" | custom-call | bytes 29520000 | tf_op jit(solution)/shard_map/project/pallas_call | solution.py:764
  104.0 5.8 %attend.1 = (bf16[128,1536]{1,0:T(8,128)(2,1)S(1)}, f32[128,1536]{1,0:T(8,128)S(1)}, f32[1536,128]{1,0:T(8,128)S(1)}) custom-call(s32[1]{0:T(128)} %bitcast.ctx_ref.refs_0_, bf16[128,1536]{1,0:T(8,128)(2,1)S(1)} %get-tuple-element.117.q_ref, bf16[8,128,1024]{2,1,0:T(8,128)(2,1)S(1)} %get-tuple-element.118.k_ref.v_ref, ...), custom_call_target="tpu_custom_call" | custom-call | bytes 22140000 | tf_op jit(solution)/shard_map/attend/pallas_call | solution.py:99
  111.6 4.8 copy-done
  121.5 19.1 %collective-permute-done.1 = bf16[1,128,1536]{2,1,0:T(8,128)(2,1)S(1)} collective-permute-done((bf16[1,128,1536]{2,1,0:T(8,128)(2,1)S(1)}, bf16[1,128,1536]{2,1,0:T(8,128)(2,1)S(1)}, u32[]{:S(2)}, u32[]{:S(2)}) %collective-permute-start.1) | collective-permute-done | bytes 393248 | tf_op jit(solution)/shard_map/ppermute | solution.py:1013
  142.6 6.0 %all-to-all-start.3 = ((bf16[4,2,128,1536]{3,2,1,0:T(8,128)(2,1)}), bf16[4,2,128,1536]{3,2,1,0:T(8,128)(2,1)}, u32[]{:S(2)}, u32[]{:S(2)}) async-start(bf16[4,2,128,1536]{3,2,1,0:T(8,128)(2,1)} %broadcast_in_dim.27), calls=%async_computation.3 | async-start | bytes 6291456 | tf_op jit(solution)/shard_map/all_to_all | solution.py:961
  149.4 13.7 %place_rows.1 = (bf16[8,2,128,128]{3,2,1,0:T(8,128)(2,1)}, bf16[2,2,384,1536]{3,2,1,0:T(8,128)(2,1)}, f32[2,2,384,512]{3,2,1,0:T(8,128)}, f32[8,2,128,128]{3,2,1,0:T(8,128)}, f32[2,2,384,128]{3,2,1,0:T(8,128)}) custom-call(s32[1]{0:T(128)} %bitcast.7.at_ref, bf16[8,2,128,1664]{3,2,1,0:T(8,128)(2,1)} %bitcast.61, bf16[2,512,1536]{2,1,0:T(8,128)(2,1)} %wd_ref.1, ...), custom_call_target="tpu_custom_call" | custom-call | bytes 51660000 | tf_op jit(solution)/shard_map/place_rows/pallas_call | solution.py:356
  163.1 23.2 %all-to-all-done.3 = bf16[4,2,128,1536]{3,2,1,0:T(8,128)(2,1)} async-done(((bf16[4,2,128,1536]{3,2,1,0:T(8,128)(2,1)}), bf16[4,2,128,1536]{3,2,1,0:T(8,128)(2,1)}, u32[]{:S(2)}, u32[]{:S(2)}) %all-to-all-start.3) | async-done | bytes 3145760 | tf_op jit(solution)/shard_map/all_to_all | solution.py:961
  186.3 8.3 %all-gather.6.cloned.1.call-done = bf16[2048,1536]{1,0:T(8,128)(2,1)} async-done(((bf16[128,1536]{1,0:T(8,128)(2,1)}), bf16[2048,1536]{1,0:T(8,128)(2,1)}) %all-gather.6.cloned.1.call-update) | async-done | bytes 6291472 | tf_op jit(solution)/shard_map/all_gather | solution.py:1036
  194.6 32.6 %expert_back.1 = (bf16[8,128,1536]{2,1,0:T(8,128)(2,1)}, bf16[8,128,1536]{2,1,0:T(8,128)(2,1)}, bf16[2,2,384,1536]{3,2,1,0:T(8,128)(2,1)}, bf16[2,2,384,512]{3,2...) custom-call(s32[1]{0:T(128)} %bitcast.7.at_ref, ...), custom_call_target="tpu_custom_call" | custom-call | bytes 103320000 | tf_op jit(solution)/shard_map/expert_back/pallas_call | solution.py:447
  227.5 5.6 collective-permute-done.2
  233.2 4.5 add_convert_fusion
  237.6 4.8 all-to-all-start.4
  242.4 11.0 %expert_weights.2 = (bf16[9216,128]{1,0:T(8,128)(2,1)}, bf16[9216,128]{1,0:T(8,128)(2,1)}) custom-call(s32[1]{0:T(128)} %bitcast.ctx_ref.refs_0_, bf16[2,768,1536]{2,1,0:T(8,128)(2,1)} %bitcast.68, bf16[2,768,1536]{2,1,0:T(8,128)(2,1)} %bitcast.66, bf16[2,768,512]{2,1,0:T(8,128)(2,1)} %bitcast.51, bf16[2,768,1024]{2,1,0:T(8,128)(2,1)} %bitcast.62, ...), custom_call_target="tpu_custom_call" | custom-call | bytes 7380000 | tf_op jit(solution)/shard_map/expert_weights/pallas_call | solution.py:858
  257.1 11.1 %expert_weights.3 = (bf16[4608,128]{1,0:T(8,128)(2,1)}, bf16[4608,128]{1,0:T(8,128)(2,1)}, bf16[4608,128]{1,0:T(8,128)(2,1)}, bf16[4608,128]{1,0:T(8,128)(2,1)}) custom-call(s32[1]{0:T(128)} %bitcast.ctx_ref.refs_0_, bf16[2,768,1536]{2,1,0:T(8,128)(2,1)} %bitcast.69, bf16[2,768,1536]{2,1,0:T(8,128)(2,1)} %bitcast.67, bf16[2,768,512]{2,1,0:T(8,128)(2,1)} %bitcast.52, ...), custom_call_target="tpu_custom_call" | custom-call | bytes 7380000 | tf_op jit(solution)/shard_map/expert_weights/pallas_call | solution.py:858
  268.2 5.4 convolution_convert_fusion
  274.9 4.1 fusion.3
  280.0 8.4 %all-to-all-done.4.pieces_ref = bf16[8,128,1536]{2,1,0:T(8,128)(2,1)} async-done(((bf16[8,128,1536]{2,1,0:T(8,128)(2,1)}), bf16[8,128,1536]{2,1,0:T(8,128)(2,1)}, u32[]{:S(2)}, u32[]{:S(2)}) %all-to-all-start.4) | async-done | bytes 3145760 | tf_op jit(solution)/shard_map/all_to_all | solution.py:961
  289.5 5.7 %middle_back.1 = (f32[128,1536]{1,0:T(8,128)S(1)}, bf16[128,1536]{1,0:T(8,128)(2,1)S(1)}, bf16[128,1536]{1,0:T(8,128)(2,1)S(1)}, f32[16,128]{1,0:T(8,128)S(1)}) custom-call(bf16[8,128,1536]{2,1,0:T(8,128)(2,1)} %all-to-all-done.4.pieces_ref, f32[128,1536]{1,0:T(8,128)S(1)} %copy-done.7, bf16[128,1536]{1,0:T(8,128)(2,1)S(1)} %bitcast.58, ...), custom_call_target="tpu_custom_call" | custom-call | bytes 3690000 | tf_op jit(solution)/shard_map/middle_back/pallas_call | solution.py:278
  296.2 8.7 %attend_back.1 = (bf16[128,1536]{1,0:T(8,128)(2,1)S(1)}, bf16[8,1776,128]{2,1,0:T(8,128)(2,1)}) custom-call(s32[1]{0:T(128)} %bitcast.ctx_ref.refs_0_, bf16[128,1536]{1,0:T(8,128)(2,1)S(1)} %copy-done.16, bf16[128,1536]{1,0:T(8,128)(2,1)S(1)} %get-tuple-element.147.ga_ref, f32[128,1536]{1,0:T(8,128)S(1)} %copy-done.30, f32[1536,128]{1,0:T(8,128)S(1)} %copy-done.32, ...), custom_call_target="tpu_custom_call" | custom-call | bytes 7380000 | tf_op jit(solution)/shard_map/attend_back/pallas_call | solution.py:191
  309.4 3.5 piece_sums.2
  315.1 24.5 %collective-permute-done.5.got_11 = bf16[4608,128]{1,0:T(8,128)(2,1)S(1)} collective-permute-done((bf16[4608,128]{1,0:T(8,128)(2,1)S(1)}, bf16[4608,128]{1,0:T(8,128)(2,1)S(1)}, u32[]{:S(2)}, u32[]{:S(2)}) %collective-permute-start.5) | collective-permute-done | bytes 1179680 | tf_op jit(solution)/shard_map/ppermute | solution.py:1063
  344.1 3.0 collective-permute-start.8
  347.1 4.7 all-to-all-start.5
  353.0 13.5 %expert_output.1 = (bf16[8,128,1536]{2,1,0:T(8,128)(2,1)}, bf16[8,128,1536]{2,1,0:T(8,128)(2,1)}) custom-call(s32[1]{0:T(128)} %bitcast.7.at_ref, bf16[2,2,384,512]{3,2,1,0:T(8,128)(2,1)S(1)} %copy-done.3, f32[2,2,384,128]{3,2,1,0:T(8,128)S(1)} %copy-done.33, bf16[8,2,128,128]{3,2,1,0:T(8,128)(2,1)S(1)} %copy-done.14, ...), custom_call_target="tpu_custom_call" | custom-call | bytes 7380000 | tf_op jit(solution)/shard_map/expert_output/pallas_call | solution.py:500
  366.5 37.5 %collective-permute-done.8 = bf16[4608,128]{1,0:T(8,128)(2,1)} collective-permute-done((bf16[4608,128]{1,0:T(8,128)(2,1)}, bf16[4608,128]{1,0:T(8,128)(2,1)}, u32[]{:S(2)}, u32[]{:S(2)}) %collective-permute-start.8) | collective-permute-done | bytes 1179680 | tf_op jit(solution)/shard_map/ppermute | solution.py:1063
  407.7 3.0 collective-permute-start.11
  418.6 7.5 %column_grads.1 = (bf16[16,112,512]{2,1,0:T(8,128)(2,1)}, bf16[8,128,128]{2,1,0:T(8,128)(2,1)}, bf16[96,128]{1,0:T(8,128)(2,1)}) custom-call(bf16[8,1776,128]{2,1,0:T(8,128)(2,1)} %all-to-all-done.5.got_ref, bf16[8,128,1536]{2,1,0:T(8,128)(2,1)} %copy-done.1, bf16[8,128,1536]{2,1,0:T(8,128)(2,1)} %bitcast.10.att_ref), custom_call_target="tpu_custom_call" | custom-call | bytes 29520000 | tf_op jit(solution)/shard_map/column_grads/pallas_call | solution.py:580
  429.5 4.6 all-to-all-start.6
  438.2 20.9 %all-to-all-done.6.got_ref = bf16[16,112,512]{2,1,0:T(8,128)(2,1)S(1)} async-done(((bf16[16,112,512]{2,1,0:T(8,128)(2,1)}), bf16[16,112,512]{2,1,0:T(8,128)(2,1)S(1)}, u32[]{:S(2)}, u32[]{:S(2)}) %all-to-all-start.6) | async-done | bytes 1835040 | tf_op jit(solution)/shard_map/all_to_all | solution.py:961
  459.3 3.5 collective-permute-done.12.refs_2_
  465.4 5.9 %all-to-all-start.7 = ((bf16[8,736,128]{2,1,0:T(8,128)(2,1)}), bf16[8,736,128]{2,1,0:T(8,128)(2,1)S(1)}, u32[]{:S(2)}, u32[]{:S(2)}) async-start(bf16[8,736,128]{2,1,0:T(8,128)(2,1)} %broadcast_in_dim.30), calls=%async_computation.7 | async-start | bytes 3014656 | tf_op jit(solution)/shard_map/all_to_all | solution.py:961
  474.8 3.2 collective-permute-start.17
  480.0 24.5 %collective-permute-done.14 = bf16[128,1536]{1,0:T(8,128)(2,1)} collective-permute-done((bf16[128,1536]{1,0:T(8,128)(2,1)}, bf16[128,1536]{1,0:T(8,128)(2,1)}, u32[]{:S(2)}, u32[]{:S(2)}) %collective-permute-start.14) | collective-permute-done | bytes 393248 | tf_op jit(solution)/shard_map/ppermute | solution.py:1121
  504.5 2.7 collective-permute-start.22
  507.2 3.5 collective-permute-start.18
  515.7 5.5 unpack_experts.2
  521.7 5.4 all-to-all-start.8
  527.2 11.2 %collective-permute-done.20 = bf16[128,1536]{1,0:T(8,128)(2,1)} collective-permute-done((bf16[128,1536]{1,0:T(8,128)(2,1)}, bf16[128,1536]{1,0:T(8,128)(2,1)}, u32[]{:S(2)}, u32[]{:S(2)}) %collective-permute-start.20) | collective-permute-done | bytes 393248 | tf_op jit(solution)/shard_map/ppermute | solution.py:1121
  538.4 3.2 fusion
  541.6 6.4 %unpack_experts.3 = (f32[2,1536,512]{2,1,0:T(8,128)}, f32[2,1536,512]{2,1,0:T(8,128)}, f32[2,512,1536]{2,1,0:T(8,128)}) custom-call(s32[1]{0:T(128)} %bitcast.ctx_ref.refs_0_, bf16[4608,128]{1,0:T(8,128)(2,1)} %collective-permute-done.21.refs_1_, ...), custom_call_target="tpu_custom_call", output_to_operand_aliasing={{0}: (5, {}), {1}: (6, {}), {2}: (7, {})} | custom-call | bytes 29520000 | tf_op jit(solution)/shard_map/unpack_experts/pallas_call | solution.py:902
  550.6 6.9 %input_back.1 = bf16[128,1536]{1,0:T(8,128)(2,1)} custom-call(bf16[128,1536]{1,0:T(8,128)(2,1)S(1)} %copy-done.39, bf16[8,128,128]{2,1,0:T(8,128)(2,1)S(1)} %all-to-all-done.8.got_ref, bf16[1536,4096]{1,0:T(8,128)(2,1)} %all-gather.4.cloned.1.call-done.w_ref.wq_ref.wkv_ref, bf16[1536,4096]{1,0:T(8,128)(2,1)} %all-gather.4.cloned.1.call-done.w_ref.wq_ref.wkv_ref, ...), custom_call_target="tpu_custom_call" | custom-call | bytes 25830000 | tf_op jit(solution)/shard_map/input_back/pallas_call | solution.py:708
  (195 shorter events, 93.6 us)
Async XLA Ops:
  7.2 12.4 %copy-start.52 = (bf16[96]{0:T(256)(128)(2,1)S(1)}, bf16[96]{0:T(256)(128)(2,1)}, u32[]{:S(2)}) copy-start(bf16[96]{0:T(256)(128)(2,1)} %param.19) | copy-start | bytes 580
  7.2 86.2 %all-gather.4.cloned.1.call-start = ((), (), s32[]{:S(2)}) async-start(), calls=%async_computation.9 | async-start | bytes 13369344 | tf_op jit(solution)/shard_map/all_gather | solution.py:999
  12.0 137.2 %all-gather.8.cloned.1.call-start = ((), (), s32[]{:S(2)}) async-start(), calls=%async_computation.11 | async-start | bytes 7241728 | tf_op jit(solution)/shard_map/all_gather | solution.py:1006
  15.6 18.1 %collective-permute-start = (bf16[1,128,1536]{2,1,0:T(8,128)(2,1)S(1)}, bf16[1,128,1536]{2,1,0:T(8,128)(2,1)S(1)}, u32[]{:S(2)}, u32[]{:S(2)}) collective-permute-start(bf16[1,128,1536]{2,1,0:T(8,128)(2,1)S(1)} %copy-done.4), channel_id=1, source_target_pairs={{0,64},{16,80},{32,96},{48,112},{64,0},{80,16},{96,32},{112,48},{1... | collective-permute-start | bytes 1179656 | tf_op jit(solution)/shard_map/ppermute | solution.py:1013
  20.3 14.1 %all-to-all-start = ((bf16[16,1,192]{2,1,0:T(2,128)(2,1)}), bf16[16,1,192]{2,1,0:T(2,128)(2,1)S(1)}, u32[]{:S(2)}, u32[]{:S(2)}) async-start(bf16[16,1,192]{2,1,0:T(2,128)(2,1)} %broadcast_in_dim.24), calls=%async_computation | async-start | bytes 32768 | tf_op jit(solution)/shard_map/all_to_all | solution.py:961
  36.3 42.6 %all-to-all-start.1 = ((bf16[4,2,128,1536]{3,2,1,0:T(8,128)(2,1)}), bf16[4,2,128,1536]{3,2,1,0:T(8,128)(2,1)S(1)}, u32[]{:S(2)}, u32[]{:S(2)}) async-start(bf16[4,2,128,1536]{3,2,1,0:T(8,128)(2,1)} %broadcast_in_dim.25), calls=%async_computation.1 | async-start | bytes 6291456 | tf_op jit(solution)/shard_map/all_to_all | solution.py:961
  79.0 14.5 %all-to-all-start.2 = ((bf16[16,96,128]{2,1,0:T(8,128)(2,1)}), bf16[16,96,128]{2,1,0:T(8,128)(2,1)}, u32[]{:S(2)}, u32[]{:S(2)}) async-start(bf16[16,96,128]{2,1,0:T(8,128)(2,1)} %copy.62), calls=%async_computation.2 | async-start | bytes 786432 | tf_op jit(solution)/shard_map/all_to_all | solution.py:961
  84.2 110.4 %all-gather.6.cloned.1.call-start = ((), (), s32[]{:S(2)}) async-start(), calls=%async_computation.10 | async-start | bytes 6684672 | tf_op jit(solution)/shard_map/all_gather | solution.py:1036
  104.0 14.1 %copy-start.15 = (bf16[128,1536]{1,0:T(8,128)(2,1)}, bf16[128,1536]{1,0:T(8,128)(2,1)S(1)}, u32[]{:S(2)}) copy-start(bf16[128,1536]{1,0:T(8,128)(2,1)S(1)} %get-tuple-element.117.q_ref) | copy-start | bytes 1179652
  119.0 21.6 %collective-permute-start.1 = (bf16[1,128,1536]{2,1,0:T(8,128)(2,1)S(1)}, bf16[1,128,1536]{2,1,0:T(8,128)(2,1)S(1)}, u32[]{:S(2)}, u32[]{:S(2)}) collective-permute-start(bf16[1,128,1536]{2,1,0:T(8,128)(2,1)S(1)} %bitcast.59), channel_id=1, source_target_pairs={{0,64},{16,80},{32,96},{48,112},{64,0},{80,16},{96,32},{112,48},{1... | collective-permute-start | bytes 1179656 | tf_op jit(solution)/shard_map/ppermute | solution.py:1013
  142.6 43.7 %all-to-all-start.3 = ((bf16[4,2,128,1536]{3,2,1,0:T(8,128)(2,1)}), bf16[4,2,128,1536]{3,2,1,0:T(8,128)(2,1)}, u32[]{:S(2)}, u32[]{:S(2)}) async-start(bf16[4,2,128,1536]{3,2,1,0:T(8,128)(2,1)} %broadcast_in_dim.27), calls=%async_computation.3 | async-start | bytes 6291456 | tf_op jit(solution)/shard_map/all_to_all | solution.py:961
  227.2 5.9 %collective-permute-start.2 = (bf16[8,128,1536]{2,1,0:T(8,128)(2,1)}, bf16[8,128,1536]{2,1,0:T(8,128)(2,1)S(1)}, u32[]{:S(2)}, u32[]{:S(2)}) collective-permute-start(bf16[8,128,1536]{2,1,0:T(8,128)(2,1)} %get-tuple-element.131), channel_id=1, source_target_pairs={{0,1},{1,0},{2,3},{3,2},{4,5},{5,4},{6,7},{7,6},{8,9},{9,8},{10,11... | collective-permute-start | bytes 9437192 | tf_op jit(solution)/shard_map/ppermute | solution.py:1048
  237.6 50.8 %all-to-all-start.4 = ((bf16[8,128,1536]{2,1,0:T(8,128)(2,1)}), bf16[8,128,1536]{2,1,0:T(8,128)(2,1)}, u32[]{:S(2)}, u32[]{:S(2)}) async-start(bf16[8,128,1536]{2,1,0:T(8,128)(2,1)} %add_convert_fusion), calls=%async_computation.4 | async-start | bytes 6291456 | tf_op jit(solution)/shard_map/all_to_all | solution.py:961
  253.4 53.6 %collective-permute-start.3 = (bf16[9216,128]{1,0:T(8,128)(2,1)}, bf16[9216,128]{1,0:T(8,128)(2,1)}, u32[]{:S(2)}, u32[]{:S(2)}) collective-permute-start(bf16[9216,128]{1,0:T(8,128)(2,1)} %get-tuple-element.135), channel_id=1, source_target_pairs={{0,16},{16,0},{32,48},{48,32},{64,80},{80,64},{96,112},{112,96},{1... | collective-permute-start | bytes 7077896 | tf_op jit(solution)/shard_map/ppermute | solution.py:1063
  255.0 13.2 %copy-start.50 = (bf16[8,2,128,128]{3,2,1,0:T(8,128)(2,1)S(1)}, bf16[8,2,128,128]{3,2,1,0:T(8,128)(2,1)}, u32[]{:S(2)}) copy-start(bf16[8,2,128,128]{3,2,1,0:T(8,128)(2,1)} %get-tuple-element.143) | copy-start | bytes 1572868
  255.0 54.4 %collective-permute-start.4 = (bf16[9216,128]{1,0:T(8,128)(2,1)}, bf16[9216,128]{1,0:T(8,128)(2,1)}, u32[]{:S(2)}, u32[]{:S(2)}) collective-permute-start(bf16[9216,128]{1,0:T(8,128)(2,1)} %get-tuple-element.141), channel_id=1, source_target_pairs={{0,48},{16,32},{32,16},{48,0},{64,112},{80,96},{96,80},{112,64},{1... | collective-permute-start | bytes 7077896 | tf_op jit(solution)/shard_map/ppermute | solution.py:1063
  274.9 13.5 %copy-start.19 = (bf16[1,128,1536]{2,1,0:T(8,128)(2,1)S(1)}, bf16[1,128,1536]{2,1,0:T(8,128)(2,1)}, u32[]{:S(2)}) copy-start(bf16[1,128,1536]{2,1,0:T(8,128)(2,1)} %param.31) | copy-start | bytes 1179652
  296.1 13.2 %copy-start.20 = (bf16[4608,128]{1,0:T(8,128)(2,1)S(1)}, bf16[4608,128]{1,0:T(8,128)(2,1)}, u32[]{:S(2)}) copy-start(bf16[4608,128]{1,0:T(8,128)(2,1)} %get-tuple-element.137.p0) | copy-start | bytes 3538948
  296.1 13.2 %copy-start.21 = (bf16[4608,128]{1,0:T(8,128)(2,1)S(1)}, bf16[4608,128]{1,0:T(8,128)(2,1)}, u32[]{:S(2)}) copy-start(bf16[4608,128]{1,0:T(8,128)(2,1)} %get-tuple-element.140.p6) | copy-start | bytes 3538948
  296.2 13.2 %copy-start.22 = (bf16[4608,128]{1,0:T(8,128)(2,1)S(1)}, bf16[4608,128]{1,0:T(8,128)(2,1)}, u32[]{:S(2)}) copy-start(bf16[4608,128]{1,0:T(8,128)(2,1)} %get-tuple-element.138.p1) | copy-start | bytes 3538948
  296.2 13.2 %copy-start.23 = (bf16[4608,128]{1,0:T(8,128)(2,1)S(1)}, bf16[4608,128]{1,0:T(8,128)(2,1)}, u32[]{:S(2)}) copy-start(bf16[4608,128]{1,0:T(8,128)(2,1)} %get-tuple-element.139.p3) | copy-start | bytes 3538948
  312.9 26.7 %collective-permute-start.5 = (bf16[4608,128]{1,0:T(8,128)(2,1)S(1)}, bf16[4608,128]{1,0:T(8,128)(2,1)S(1)}, u32[]{:S(2)}, u32[]{:S(2)}) collective-permute-start(bf16[4608,128]{1,0:T(8,128)(2,1)S(1)} %get-tuple-element.157), channel_id=1, source_target_pairs={{0,16},{16,0},{32,48},{48,32},{64,80},{80,64},{96,112},{112,96},{1... | collective-permute-start | bytes 3538952 | tf_op jit(solution)/shard_map/ppermute | solution.py:1063
  313.0 27.9 %collective-permute-start.6 = (bf16[4608,128]{1,0:T(8,128)(2,1)S(1)}, bf16[4608,128]{1,0:T(8,128)(2,1)S(1)}, u32[]{:S(2)}, u32[]{:S(2)}) collective-permute-start(bf16[4608,128]{1,0:T(8,128)(2,1)S(1)} %get-tuple-element.158), channel_id=1, source_target_pairs={{0,48},{16,32},{32,16},{48,0},{64,112},{80,96},{96,80},{112,64},{1... | collective-permute-start | bytes 3538952 | tf_op jit(solution)/shard_map/ppermute | solution.py:1063
  344.1 60.0 %collective-permute-start.8 = (bf16[4608,128]{1,0:T(8,128)(2,1)}, bf16[4608,128]{1,0:T(8,128)(2,1)}, u32[]{:S(2)}, u32[]{:S(2)}) collective-permute-start(bf16[4608,128]{1,0:T(8,128)(2,1)} %get-tuple-element.159), channel_id=1, source_target_pairs={{0,64},{16,80},{32,96},{48,112},{64,0},{80,16},{96,32},{112,48},{1... | collective-permute-start | bytes 3538952 | tf_op jit(solution)/shard_map/ppermute | solution.py:1063
  347.1 71.5 %all-to-all-start.5 = ((bf16[8,1776,128]{2,1,0:T(8,128)(2,1)}), bf16[8,1776,128]{2,1,0:T(8,128)(2,1)}, u32[]{:S(2)}, u32[]{:S(2)}) async-start(bf16[8,1776,128]{2,1,0:T(8,128)(2,1)} %get-tuple-element.166), calls=%async_computation.5 | async-start | bytes 7274496 | tf_op jit(solution)/shard_map/all_to_all | solution.py:961
  353.0 51.0 %copy-start.13 = (f32[4608,128]{1,0:T(8,128)S(1)}, f32[4608,128]{1,0:T(8,128)}, u32[]{:S(2)}) copy-start(f32[4608,128]{1,0:T(8,128)} %copy-done.12) | copy-start | bytes 7077892
  366.5 44.2 %copy-start.8 = (bf16[8,128,1536]{2,1,0:T(8,128)(2,1)S(1)}, bf16[8,128,1536]{2,1,0:T(8,128)(2,1)}, u32[]{:S(2)}) copy-start(bf16[8,128,1536]{2,1,0:T(8,128)(2,1)} %get-tuple-element.162.own_ref) | copy-start | bytes 9437188
  366.5 44.2 %collective-permute-start.7 = (bf16[8,128,1536]{2,1,0:T(8,128)(2,1)}, bf16[8,128,1536]{2,1,0:T(8,128)(2,1)S(1)}, u32[]{:S(2)}, u32[]{:S(2)}) collective-permute-start(bf16[8,128,1536]{2,1,0:T(8,128)(2,1)} %get-tuple-element.163), channel_id=1, source_target_pairs={{0,1},{1,0},{2,3},{3,2},{4,5},{5,4},{6,7},{7,6},{8,9},{9,8},{10,11... | collective-permute-start | bytes 9437192 | tf_op jit(solution)/shard_map/ppermute | solution.py:1110
  405.5 22.9 %collective-permute-start.10 = (bf16[4608,128]{1,0:T(8,128)(2,1)S(1)}, bf16[4608,128]{1,0:T(8,128)(2,1)S(1)}, u32[]{:S(2)}, u32[]{:S(2)}) collective-permute-start(bf16[4608,128]{1,0:T(8,128)(2,1)S(1)} %add_convert_fusion.1.refs_1_), channel_id=1, source_target_pairs={{0,48},{16,32},{32,16},{48,0},{64,112},{80,96},{96,80},{112,64},{1... | collective-permute-start | bytes 3538952 | tf_op jit(solution)/shard_map/ppermute | solution.py:1063
  407.7 21.5 %collective-permute-start.9 = (bf16[4608,128]{1,0:T(8,128)(2,1)S(1)}, bf16[4608,128]{1,0:T(8,128)(2,1)}, u32[]{:S(2)}, u32[]{:S(2)}) collective-permute-start(bf16[4608,128]{1,0:T(8,128)(2,1)S(1)} %add_convert_fusion.1.refs_1_), channel_id=1, source_target_pairs={{0,16},{16,0},{32,48},{48,32},{64,80},{80,64},{96,112},{112,96},{1... | collective-permute-start | bytes 3538952 | tf_op jit(solution)/shard_map/ppermute | solution.py:1063
  407.7 28.1 %collective-permute-start.11 = (bf16[4608,128]{1,0:T(8,128)(2,1)S(1)}, bf16[4608,128]{1,0:T(8,128)(2,1)}, u32[]{:S(2)}, u32[]{:S(2)}) collective-permute-start(bf16[4608,128]{1,0:T(8,128)(2,1)S(1)} %add_convert_fusion.1.refs_1_), channel_id=1, source_target_pairs={{0,64},{16,80},{32,96},{48,112},{64,0},{80,16},{96,32},{112,48},{1... | collective-permute-start | bytes 3538952 | tf_op jit(solution)/shard_map/ppermute | solution.py:1063
  426.1 32.9 %copy-start.40 = (bf16[96,128]{1,0:T(8,128)(2,1)S(1)}, bf16[96,128]{1,0:T(8,128)(2,1)}, u32[]{:S(2)}) copy-start(bf16[96,128]{1,0:T(8,128)(2,1)} %get-tuple-element.172.down_ref) | copy-start | bytes 73732
  429.5 29.5 %all-to-all-start.6 = ((bf16[16,112,512]{2,1,0:T(8,128)(2,1)}), bf16[16,112,512]{2,1,0:T(8,128)(2,1)S(1)}, u32[]{:S(2)}, u32[]{:S(2)}) async-start(bf16[16,112,512]{2,1,0:T(8,128)(2,1)} %get-tuple-element.171), calls=%async_computation.6 | async-start | bytes 3670016 | tf_op jit(solution)/shard_map/all_to_all | solution.py:961
  435.9 26.9 %collective-permute-start.12 = (bf16[4608,128]{1,0:T(8,128)(2,1)}, bf16[4608,128]{1,0:T(8,128)(2,1)}, u32[]{:S(2)}, u32[]{:S(2)}) collective-permute-start(bf16[4608,128]{1,0:T(8,128)(2,1)} %collective-permute-done.11.refs_4_), channel_id=1, source_target_pairs={{0,16},{16,0},{32,48},{48,32},{64,80},{80,64},{96,112},{112,96},{1... | collective-permute-start | bytes 3538952 | tf_op jit(solution)/shard_map/ppermute | solution.py:1063
  436.0 28.1 %collective-permute-start.13 = (bf16[4608,128]{1,0:T(8,128)(2,1)}, bf16[4608,128]{1,0:T(8,128)(2,1)}, u32[]{:S(2)}, u32[]{:S(2)}) collective-permute-start(bf16[4608,128]{1,0:T(8,128)(2,1)} %collective-permute-done.11.refs_4_), channel_id=1, source_target_pairs={{0,48},{16,32},{32,16},{48,0},{64,112},{80,96},{96,80},{112,64},{1... | collective-permute-start | bytes 3538952 | tf_op jit(solution)/shard_map/ppermute | solution.py:1063
  459.0 55.3 %copy-start.53 = (bf16[96]{0:T(256)(128)(2,1)S(1)}, bf16[96]{0:T(256)(128)(2,1)}, u32[]{:S(2)}) copy-start(bf16[96]{0:T(256)(128)(2,1)} %param.19) | copy-start | bytes 580
  465.4 73.0 %copy-start.37 = (bf16[128,1536]{1,0:T(8,128)(2,1)S(1)}, bf16[128,1536]{1,0:T(8,128)(2,1)}, u32[]{:S(2)}) copy-start(bf16[128,1536]{1,0:T(8,128)(2,1)} %copy-done.36) | copy-start | bytes 1179652
  465.4 56.3 %all-to-all-start.7 = ((bf16[8,736,128]{2,1,0:T(8,128)(2,1)}), bf16[8,736,128]{2,1,0:T(8,128)(2,1)S(1)}, u32[]{:S(2)}, u32[]{:S(2)}) async-start(bf16[8,736,128]{2,1,0:T(8,128)(2,1)} %broadcast_in_dim.30), calls=%async_computation.7 | async-start | bytes 3014656 | tf_op jit(solution)/shard_map/all_to_all | solution.py:961
  471.3 33.2 %collective-permute-start.14 = (bf16[128,1536]{1,0:T(8,128)(2,1)}, bf16[128,1536]{1,0:T(8,128)(2,1)}, u32[]{:S(2)}, u32[]{:S(2)}) collective-permute-start(bf16[128,1536]{1,0:T(8,128)(2,1)} %copy-done.47), channel_id=1, source_target_pairs={{0,2},{1,3},{2,0},{3,1},{4,6},{5,7},{6,4},{7,5},{8,10},{9,11},{10,... | collective-permute-start | bytes 1179656 | tf_op jit(solution)/shard_map/ppermute | solution.py:1121
  472.4 34.8 %collective-permute-start.15 = (bf16[128,1536]{1,0:T(8,128)(2,1)}, bf16[128,1536]{1,0:T(8,128)(2,1)}, u32[]{:S(2)}, u32[]{:S(2)}) collective-permute-start(bf16[128,1536]{1,0:T(8,128)(2,1)} %copy-done.46), channel_id=1, source_target_pairs={{0,4},{1,5},{2,6},{3,7},{4,0},{5,1},{6,2},{7,3},{8,12},{9,13},{10,... | collective-permute-start | bytes 1179656 | tf_op jit(solution)/shard_map/ppermute | solution.py:1121
  473.8 36.9 %collective-permute-start.16 = (bf16[128,1536]{1,0:T(8,128)(2,1)}, bf16[128,1536]{1,0:T(8,128)(2,1)}, u32[]{:S(2)}, u32[]{:S(2)}) collective-permute-start(bf16[128,1536]{1,0:T(8,128)(2,1)} %copy-done.45), channel_id=1, source_target_pairs={{0,6},{1,7},{2,4},{3,5},{4,2},{5,3},{6,0},{7,1},{8,14},{9,15},{10,... | collective-permute-start | bytes 1179656 | tf_op jit(solution)/shard_map/ppermute | solution.py:1121
  474.8 37.1 %collective-permute-start.17 = (bf16[128,1536]{1,0:T(8,128)(2,1)}, bf16[128,1536]{1,0:T(8,128)(2,1)}, u32[]{:S(2)}, u32[]{:S(2)}) collective-permute-start(bf16[128,1536]{1,0:T(8,128)(2,1)} %copy-done.44), channel_id=1, source_target_pairs={{0,8},{1,9},{2,10},{3,11},{4,12},{5,13},{6,14},{7,15},{8,0},{9,1},... | collective-permute-start | bytes 1179656 | tf_op jit(solution)/shard_map/ppermute | solution.py:1121
  478.0 63.6 %collective-permute-start.21 = (bf16[4608,128]{1,0:T(8,128)(2,1)}, bf16[4608,128]{1,0:T(8,128)(2,1)}, u32[]{:S(2)}, u32[]{:S(2)}) collective-permute-start(bf16[4608,128]{1,0:T(8,128)(2,1)} %copy-done.24), channel_id=1, source_target_pairs={{0,16},{16,0},{32,48},{48,32},{64,80},{80,64},{96,112},{112,96},{1... | collective-permute-start | bytes 3538952 | tf_op jit(solution)/shard_map/ppermute | solution.py:1063
  504.5 37.1 %collective-permute-start.22 = (bf16[4608,128]{1,0:T(8,128)(2,1)}, bf16[4608,128]{1,0:T(8,128)(2,1)}, u32[]{:S(2)}, u32[]{:S(2)}) collective-permute-start(bf16[4608,128]{1,0:T(8,128)(2,1)} %collective-permute-done.12.refs_2_), channel_id=1, source_target_pairs={{0,48},{16,32},{32,16},{48,0},{64,112},{80,96},{96,80},{112,64},{1... | collective-permute-start | bytes 3538952 | tf_op jit(solution)/shard_map/ppermute | solution.py:1063
  507.2 20.0 %collective-permute-start.18 = (bf16[128,1536]{1,0:T(8,128)(2,1)}, bf16[128,1536]{1,0:T(8,128)(2,1)}, u32[]{:S(2)}, u32[]{:S(2)}) collective-permute-start(bf16[128,1536]{1,0:T(8,128)(2,1)} %copy-done.43), channel_id=1, source_target_pairs={{0,10},{1,11},{2,8},{3,9},{4,14},{5,15},{6,12},{7,13},{8,2},{9,3},... | collective-permute-start | bytes 1179656 | tf_op jit(solution)/shard_map/ppermute | solution.py:1121
  510.7 16.5 %collective-permute-start.19 = (bf16[128,1536]{1,0:T(8,128)(2,1)}, bf16[128,1536]{1,0:T(8,128)(2,1)}, u32[]{:S(2)}, u32[]{:S(2)}) collective-permute-start(bf16[128,1536]{1,0:T(8,128)(2,1)} %copy-done.42), channel_id=1, source_target_pairs={{0,12},{1,13},{2,14},{3,15},{4,8},{5,9},{6,10},{7,11},{8,4},{9,5},... | collective-permute-start | bytes 1179656 | tf_op jit(solution)/shard_map/ppermute | solution.py:1121
  511.9 26.6 %collective-permute-start.20 = (bf16[128,1536]{1,0:T(8,128)(2,1)}, bf16[128,1536]{1,0:T(8,128)(2,1)}, u32[]{:S(2)}, u32[]{:S(2)}) collective-permute-start(bf16[128,1536]{1,0:T(8,128)(2,1)} %copy-done.41), channel_id=1, source_target_pairs={{0,14},{1,15},{2,12},{3,13},{4,10},{5,11},{6,8},{7,9},{8,6},{9,7},... | collective-permute-start | bytes 1179656 | tf_op jit(solution)/shard_map/ppermute | solution.py:1121
  521.7 28.8 %all-to-all-start.8 = ((bf16[8,128,128]{2,1,0:T(8,128)(2,1)}), bf16[8,128,128]{2,1,0:T(8,128)(2,1)S(1)}, u32[]{:S(2)}, u32[]{:S(2)}) async-start(bf16[8,128,128]{2,1,0:T(8,128)(2,1)} %get-tuple-element.202), calls=%async_computation.8 | async-start | bytes 524288 | tf_op jit(solution)/shard_map/all_to_all | solution.py:961
  (41 other events, 143.2 us)
Sparse Core Ops, SparseCore 0:
  12.1 80.4 all-gather.3
  94.9 54.3 all-gather.7
  151.5 43.0 all-gather.5

commit v9 on v7

--- a/solution.py
+++ b/solution.py
@@ -142,10 +142,22 @@
     extra_ref,
     gain_ref,
     dq_ref,
-    sent_ref,
+    near_ref,
+    far_ref,
     kept_ref,
 ):
     group = pl.program_id(0)
+    z_at = ctx_ref[0] // 4
+
+    def send(dest, z, start, stop, rows):
+        @pl.when(z_at == z)
+        def _():
+            near_ref[dest, start:stop] = rows
+
+        @pl.when(z_at != z)
+        def _():
+            far_ref[dest, start:stop] = rows
+
     q = stack_heads(q_ref[...])
     grad = stack_heads(ga_ref[...])
     delta = jnp.sum(grad.astype(f32) * stack_heads(attf_ref[...]), axis=-1, keepdims=True)
@@ -162,8 +174,9 @@
     grad_k = dg(grad_raw, q, TN) * scale
     grad_v = dg(weights.astype(bf16), grad, TN)
     low, high = halves(grad_k, grad_v, lax.broadcasted_iota(jnp.int32, (SEQ, HEAD_DIM), 1))
-    sent_ref[2 * group, :SEQ] = low.astype(bf16)
-    sent_ref[2 * group + 1, :SEQ] = high.astype(bf16)
+    low, high = low.astype(bf16), high.astype(bf16)
+    send(2 * (group % 2), group // 2, 0, SEQ, low)
+    send(2 * (group % 2) + 1, group // 2, 0, SEQ, high)
 
     @pl.when(group == KV_HEADS - 1)
     def _():
@@ -175,16 +188,14 @@
         def ga_tile(m):
             return all_ga_ref[:, HEAD_DIM * m : HEAD_DIM * (m + 1)].astype(f32)
 
+        mixed = []
         for m in range(KV_HEADS):
-            low, high = halves(dq_tile(N_CTX + m), ga_tile(N_CTX + m), lane)
-            sent_ref[2 * m, AT_MIXED:AT_OUT] = low.astype(bf16)
-            sent_ref[2 * m + 1, AT_MIXED:AT_OUT] = high.astype(bf16)
+            mixed += halves(dq_tile(N_CTX + m), ga_tile(N_CTX + m), lane)
         gains = gain_ref[...].astype(bf16)
         for c in range(N_CTX):
-            sent_ref[c, AT_QUERY:AT_MIXED] = dq_tile(c).astype(bf16)
-            sent_ref[c, AT_OUT:AT_SHARED] = ga_tile(c).astype(bf16)
-            sent_ref[c, AT_SHARED:AT_GAIN] = extra_ref[c]
-            sent_ref[c, AT_GAIN:] = gains
+            tiles = [dq_tile(c).astype(bf16), mixed[c].astype(bf16), ga_tile(c).astype(bf16)]
+            rows = jnp.concatenate(tiles + [extra_ref[c], gains], axis=0)
+            send(c % 4, c // 4, AT_QUERY, SENT_ROWS, rows)
 
 
 def attend_back(ctx_at, qkv, grad_att, att_f, logs, kv_all, grad_attn, extra, gain_rows):
@@ -204,13 +215,14 @@
             whole((N_CTX, AT_GAIN - AT_SHARED, HEAD_DIM)),
             whole((16, HEAD_DIM)),
         ],
-        out_specs=[head_spec(), whole((N_CTX, SENT_ROWS, HEAD_DIM))],
+        out_specs=[head_spec()] + [whole((4, SENT_ROWS, HEAD_DIM))] * 2,
         out_shape=[
             jax.ShapeDtypeStruct((BLOCK, WIDTH), bf16),
-            jax.ShapeDtypeStruct((N_CTX, SENT_ROWS, HEAD_DIM), bf16),
+            jax.ShapeDtypeStruct((4, SENT_ROWS, HEAD_DIM), bf16),
+            jax.ShapeDtypeStruct((4, SENT_ROWS, HEAD_DIM), bf16),
         ],
         scratch_shapes=[pltpu.VMEM((KV_HEADS, BLOCK, GROUP * HEAD_DIM), f32)],
-        cost_estimate=cost(9),
+        cost_estimate=cost(2),
         compiler_params=params(48),
         name="attend_back",
     )(ctx_at, qkv, grad_att, att_f, logs, kv_all, kv_all, grad_attn, extra, gain_rows)
@@ -292,7 +304,7 @@
             jax.ShapeDtypeStruct((BLOCK, WIDTH), bf16),
             jax.ShapeDtypeStruct((16, HEAD_DIM), f32),
         ],
-        cost_estimate=cost(5),
+        cost_estimate=cost(1),
         compiler_params=params(48),
         name="middle_back",
     )(pieces, middle, upstream, gain, w_all)
@@ -500,30 +512,71 @@
             out_specs=pl.BlockSpec((1, HALF, BLOCK, WIDTH), lambda s, at: (s, 0, 0, 0)),
         ),
         out_shape=jax.ShapeDtypeStruct((2, HALF, BLOCK, WIDTH), bf16),
-        cost_estimate=cost(10),
+        cost_estimate=cost(2),
         compiler_params=params(48),
         name="expert_output",
     )(exp_at, act, gate, place, sact, wd, sd)
 
 
+SHARE = 3 * BLOCK
+TO_SHARED = SEQ + 2 * SHARE
+TO_DOWN = TO_SHARED + 16 * N_EXP
+TO_GAIN = TO_DOWN + 96
+MERGED_ROWS = TO_GAIN + 16
+
+
+def merge_kernel(ctx_ref, near_ref, got_ref, out_ref):
+    z_at = ctx_ref[0] // 4
+    near, got = near_ref[0], got_ref[0]
+
+    def add(a, b):
+        return (a.astype(f32) + b.astype(f32)).astype(bf16)
+
+    out_ref[0, :SEQ] = add(near[:SEQ], got[:SEQ])
+    out_ref[0, TO_SHARED:] = add(near[AT_SHARED:], got[AT_SHARED:])
+    mine, theirs = near[AT_QUERY:AT_SHARED], got[AT_QUERY:AT_SHARED]
+    out_ref[0, SEQ : SEQ + SHARE] = jnp.where(z_at == 0, mine, theirs)
+    out_ref[0, SEQ + SHARE : TO_SHARED] = jnp.where(z_at == 0, theirs, mine)
+
+
+def merge_shares(ctx_at, near, got):
+    spec = pl.BlockSpec((1, SENT_ROWS, HEAD_DIM), lambda i: (i, 0, 0))
+    return pl.pallas_call(
+        merge_kernel,
+        grid=(4,),
+        in_specs=[pl.BlockSpec(memory_space=pltpu.SMEM), spec, spec],
+        out_specs=pl.BlockSpec((1, MERGED_ROWS, HEAD_DIM), lambda i: (i, 0, 0)),
+        out_shape=jax.ShapeDtypeStruct((4, MERGED_ROWS, HEAD_DIM), bf16),
+        cost_estimate=cost(3),
+        compiler_params=params(32),
+        name="merge_shares",
+    )(ctx_at, near, got)
+
+
 def columns_kernel(got_ref, hidden_ref, att_ref, sent_ref, kv_ref, down_ref):
-    total = got_ref[0, :SEQ].astype(f32)
-    for src in range(1, N_CTX):
-        total = total + got_ref[src, :SEQ].astype(f32)
-    grad_kv = total.astype(bf16)
+    def summed(start, stop):
+        out = got_ref[0, start:stop].astype(f32)
+        for src in range(1, 4):
+            out = out + got_ref[src, start:stop].astype(f32)
+        return out
+
+    grad_kv = summed(0, SEQ).astype(bf16)
     kv_ref[...] = grad_kv.reshape(N_CTX, BLOCK, HEAD_DIM)
 
-    def rows_of(at, order):
-        return jnp.concatenate([got_ref[src, at : at + BLOCK] for src in order], axis=0)
-
-    in_order = list(range(N_CTX))
-    y_order = [(i % 2) * 4 + i // 2 for i in range(N_CTX)]
+    def rows_of(tile, order):
+        at = SEQ + BLOCK * tile
+        return jnp.concatenate(
+            [got_ref[y, at + SHARE * z : at + SHARE * z + BLOCK] for z, y in order], axis=0
+        )
+
+    in_order = [(i // 4, i % 4) for i in range(N_CTX)]
+    y_order = [(i % 2, i // 2) for i in range(N_CTX)]
     lane = lax.broadcasted_iota(jnp.int32, (SEQ, HEAD_DIM), 1)
     zero = jnp.zeros((SEQ, HEAD_DIM), bf16)
-    mixed_q = jnp.where(lane < 64, rows_of(AT_MIXED, in_order), zero)
-    mixed_o = jnp.where(lane < 64, zero, rows_of(AT_MIXED, y_order))
-    left = jnp.concatenate([rows_of(AT_QUERY, in_order).T, mixed_q.T, grad_kv.T], axis=0)
-    right = jnp.concatenate([mixed_o.T, rows_of(AT_OUT, y_order).T], axis=0)
+    mixed_q = jnp.where(lane < 64, rows_of(1, in_order), zero)
+    mixed_o = jnp.where(lane < 64, zero, rows_of(1, y_order))
+    left = jnp.concatenate([rows_of(0, in_order).T, mixed_q.T, grad_kv.T], axis=0)
+    right = jnp.concatenate([mixed_o.T, rows_of(2, y_order).T], axis=0)
     by_hidden = dg(left, hidden_ref[...].reshape(SEQ, WIDTH), NN)
     by_att = dg(right, att_ref[...].reshape(SEQ, WIDTH), NN)
     tiles = [
@@ -537,15 +590,9 @@
             tile.T.astype(bf16).reshape(N_EXP, 96, HEAD_DIM)
         )
 
-    def summed(start, stop):
-        out = got_ref[0, start:stop].astype(f32)
-        for src in range(1, N_CTX):
-            out = out + got_ref[src, start:stop].astype(f32)
-        return out
-
-    down_ref[...] = summed(AT_DOWN, AT_GAIN).astype(bf16)
-    shared = summed(AT_SHARED, AT_DOWN)
-    gains = summed(AT_GAIN, SENT_ROWS)
+    down_ref[...] = summed(TO_DOWN, TO_GAIN).astype(bf16)
+    shared = summed(TO_SHARED, TO_DOWN)
+    gains = summed(TO_GAIN, MERGED_ROWS)
     row = lax.broadcasted_iota(jnp.int32, (16, HEAD_DIM), 0)
     one_lane = lax.broadcasted_iota(jnp.int32, (1, HEAD_DIM), 1)
     for i in range(N_EXP):
@@ -773,6 +820,34 @@
 PIECE = 2 * WIDTH + WIDTH * BLOCK // HEAD_DIM
 
 
+def spread_kernel(at_ref, own_ref, got_ref, *outs):
+    total = (own_ref[0, 0].astype(f32) + got_ref[0].astype(f32)).astype(bf16)
+    for k in range(HALF):
+
+        @pl.when(pl.program_id(0) == k)
+        def _():
+            outs[k // 2][k % 2] = total
+
+
+def spread_sums(exp_at, parts, got):
+    return pl.pallas_call(
+        spread_kernel,
+        grid_spec=pltpu.PrefetchScalarGridSpec(
+            num_scalar_prefetch=1,
+            grid=(HALF,),
+            in_specs=[
+                pl.BlockSpec((1, 1, BLOCK, WIDTH), lambda k, at: (1, (at[0] >> 1) ^ k, 0, 0)),
+                pl.BlockSpec((1, BLOCK, WIDTH), lambda k, at: ((at[0] >> 1) ^ k, 0, 0)),
+            ],
+            out_specs=[whole((2, BLOCK, WIDTH))] * 4,
+        ),
+        out_shape=[jax.ShapeDtypeStruct((2, BLOCK, WIDTH), bf16)] * 4,
+        cost_estimate=cost(4),
+        compiler_params=params(32),
+        name="spread_sums",
+    )(exp_at, parts, got)
+
+
 def of_step(values, step):
     out = jnp.int32(values[0])
     for i, value in enumerate(values[1:], 1):
@@ -825,7 +900,7 @@
             out_specs=[whole((length, HEAD_DIM))] * count,
         ),
         out_shape=[jax.ShapeDtypeStruct((length, HEAD_DIM), bf16)] * count,
-        cost_estimate=cost(9),
+        cost_estimate=cost(2),
         compiler_params=params(56),
         name="expert_weights",
     )(ctx_at, arrived, grad_eo, act, grad_gu, grad_gu)
@@ -906,7 +981,7 @@
         in_specs=specs,
         out_specs=[pl.BlockSpec((PIECE // 4, HEAD_DIM), lambda i: (i, 0))] * len(kinds),
         out_shape=[jax.ShapeDtypeStruct((PIECE, HEAD_DIM), kind) for kind in kinds],
-        cost_estimate=cost(4),
+        cost_estimate=cost(1),
         compiler_params=params(32),
         name="piece_sums",
     )(*arrays)
@@ -1028,7 +1103,6 @@
     grad_scols = dg(hidden_all.reshape(N_EXP * BLOCK, WIDTH), shared_grad_late, TN).astype(bf16)
     act_late = after(shared_act, p0).reshape(N_EXP * BLOCK, META)
     grad_sdown = dg(act_late, up_all, TN)[:SHARED, :WIDTH].astype(bf16)
-
     extra = jnp.concatenate(
         [
             jnp.pad(
@@ -1039,14 +1113,19 @@
         ],
         axis=1,
     )
-    grad_two = after(grad_two, p0, extra)
+
+    out_part = expert_output(
+        exp_s, after(act, p0), slot_gate, place, shared_act, expert_down, shared_two
+    )
+    grad_two = after(grad_two, extra, out_part)
     grad_middle, grad_attn, grad_heads, gain_rows = middle_back(
         grad_two, middle, cotangent[0], gain_ffn, w_all
     )
-    grad_query, sent = attend_back(
+    grad_query, near, far = attend_back(
         ctx_s, queries, grad_heads, att_f, logs, kv_all, grad_attn, extra, gain_rows
     )
-    from_1, from_3 = after((from_1, from_3), sent)
+    far = lax.ppermute(far, "ctx", z_swap)
+    from_1, from_3 = after((from_1, from_3), near)
     add_a, add_b, part_0, part_1 = piece_sums(
         relay_kernel,
         (bf16, bf16, f32, f32),
@@ -1060,24 +1139,39 @@
         (from_3, 1),
     )
     got_11, got_30 = to(add_b, 1), to(add_a, 3)
-    got = swap_all(after(sent, add_a), "ctx")
-
-    columns, grad_kv, grad_down = column_grads(got, hidden_seq, att_seq)
-    grad_kv = swap_all(grad_kv, "ctx")
-    got_11, got_30, columns = after((got_11, got_30, columns), grad_kv)
+
+    out_sums = spread_sums(
+        exp_s, out_part, lax.ppermute(after(out_part[0], near), "exp", core_swap)
+    )
+    got_11, got_30 = after((got_11, got_30), out_sums[0])
     own_part, side = piece_sums(side_kernel, (f32, bf16), part_0, part_1, got_11, got_30)
+    out_rows = out_sums[0].astype(f32)
+    for k in range(1, 4):
+        moved = lax.ppermute(out_sums[k], "exp", [(i, i ^ (4 * k)) for i in range(N_EXP)])
+        out_rows = out_rows + moved.astype(f32)
+    out_across = lax.ppermute(
+        out_rows[1].astype(bf16), "exp", [(i, i ^ 2) for i in range(N_EXP)]
+    )
     across = to(side, 4)
+
+    shares = merge_shares(ctx_s, near, after(far, side))
+    got = swap_all(shares, "ctx", y_groups)
+    own = (own_part + after(across, shares).astype(f32)).astype(bf16)
+    at_1, at_3, at_z = to(own, 1), to(own, 3), to(own, 4)
+    columns, grad_kv, grad_down = column_grads(got, after(hidden_seq, own, out_rows), att_seq)
+    columns, at_1, at_3 = lax.optimization_barrier((columns, at_1, at_3))
     owned = swap_all(columns, "exp")
-    out_part = expert_output(
-        exp_s, after(act, columns), slot_gate, place, shared_act, expert_down, shared_two
-    )
-    out_sum = add_low(out_part[1], lax.ppermute(out_part[0], "exp", core_swap))
     owned, gain_sum = owned_sums(owned, grad_down)
-    own = (own_part + after(across, owned).astype(f32)).astype(bf16)
-    at_1, at_3, at_z = to(own, 1), to(own, 3), to(own, 4)
+    owned, at_z1, at_z3 = lax.optimization_barrier((owned, to(at_z, 1), to(at_z, 3)))
+    at_2, at_z2 = to(at_3, 1), to(at_z1, 3)
+    mixed = (middle + out_rows[0] + out_across.astype(f32)).astype(bf16)[None]
+    experts = unpack_experts(
+        ctx_s, ((0, 0), (1, 0), (3, 0), (0, 1)), (after(own, owned), at_1, at_3, at_z)
+    )
     owned = swap_all(jnp.broadcast_to(owned, (N_CTX, OWNED_ROWS, HEAD_DIM)), "ctx")
+    grad_kv = swap_all(after(grad_kv, owned, mixed), "ctx")
     experts = unpack_experts(
-        ctx_s, ((0, 0), (1, 0), (3, 0), (0, 1)), (own, at_1, at_3, at_z)
+        ctx_s, ((2, 0), (1, 1), (3, 1), (2, 1)), (at_2, at_z1, at_z3, at_z2), experts
     )
     gain_attn_sum, *dense = finish(
         after(owned, experts[0]),
@@ -1086,22 +1180,9 @@
         key_weight,
         value_weight,
     )
-
-    at_z1, at_z3 = to(at_z, 1), to(at_z, 3)
-    at_2, at_z2 = to(at_3, 1), to(at_z1, 3)
-    out_pieces = swap_all(after(out_sum, owned, experts[0]), "exp", same_core)
-    mixed = (middle + jnp.sum(out_pieces.astype(f32), axis=0)).astype(bf16)[None]
-    experts = unpack_experts(ctx_s, ((1, 1), (3, 1)), (at_z1, at_z3), experts)
     input_grad = input_back(
-        after(grad_query, experts[0]),
-        grad_kv,
-        w_all,
-        tokens[0],
-        gain_attn,
-        grad_middle,
-    )
-    at_2 = after(at_2, mixed, input_grad, *dense)
-    experts = unpack_experts(ctx_s, ((2, 0), (2, 1)), (at_2, at_z2), experts)
+        after(grad_query, dense[0]), grad_kv, w_all, tokens[0], gain_attn, grad_middle
+    )
     return (
         mixed,
         input_grad[None],

time: 583 us -> 544 us (0.933)
  waiting for transfers between devices: 244 us -> 223 us
  local copies, waits for them, and re-layouts: 57.3 us -> 47.3 us
    ppermute x1 -> x6, waiting for transfers between devices: 0.01 us -> 34.4 us  [the longest x1 13.9 us: on_device(): far = lax.ppermute(far, 'ctx', z_swap)]
    ppermute x12, waiting for transfers between devices: 91.7 us -> 57.6 us  [to(): return lax.ppermute(rows, 'ctx', [(i, i ^ k) for i in range(N_CTX)])]
    all_to_all x10 -> x9, waiting for transfers between devices: 108 us -> 86.5 us  [swap_all(): lax.all_to_all(rows, axis, split_axis=0, concat_axis=0, tiled=True, axis_...]
    unnamed x116, local copies, waits for them, and re-layouts: 37.4 us -> 26.7 us
    all_to_all x10 -> x9, starting transfers between devices: 60 us -> 49.4 us  [swap_all(): lax.all_to_all(rows, axis, split_axis=0, concat_axis=0, tiled=True, axis_...]
    ppermute x1 -> x6, starting transfers between devices: 0.22 us -> 8.74 us  [the longest x3 4.7 us: on_device(): lax.ppermute(out_sums[k], 'exp', [(i, i ^ 4 * k) for i in range(N_EXP)])]
    pallas_call x3 -> x2, Pallas kernels: 13.7 us -> 11.9 us  [unpack_experts(): pl.pallas_call(lambda *refs: unpack_kernel(count, *refs), grid_spec=pltpu...]
  transfers between devices with their start and end apart: 29 -> 33, of which waited for: 21 -> 25; matrix products, arithmetic and copies ran while one was open for 8% -> 8% of each run, Pallas kernels for 19% -> 20%
where the time goes in v9:
time: 544 us; the launch traced here: 534 us
  waiting for transfers between devices  223 us (41%)
  Pallas kernels  144 us (26%)
  starting transfers between devices  83.8 us (15%)
  local copies, waits for them, and re-layouts  47.3 us (9%)
  between operations  14.6 us (3%)
  other arithmetic  13.7 us (3%)
  matrix products  7.44 us (1%)
    all_to_all x9, waiting for transfers between devices, swap_all(): lax.all_to_all(rows, axis, split_axis=0, concat_axis=0, tiled=True, axis_...  86.5 us
    ppermute x12, waiting for transfers between devices, to(): return lax.ppermute(rows, 'ctx', [(i, i ^ k) for i in range(N_CTX)])  57.6 us
    all_to_all x9, starting transfers between devices, swap_all(): lax.all_to_all(rows, axis, split_axis=0, concat_axis=0, tiled=True, axis_...  49.4 us
    pallas_call x1, Pallas kernels, expert_back(): pl.pallas_call(expert_kernel, grid_spec=pltpu.PrefetchScalarGridSpec(num_...  28.6 us
    unnamed x116, local copies, waits for them, and re-layouts  26.7 us
    ppermute x2, waiting for transfers between devices, of_sequence(): other = lax.ppermute(rows, 'ctx', z_swap)  26.2 us
    pallas_call x2, Pallas kernels, expert_weights(): pl.pallas_call(lambda *refs: expert_weights_kernel(halved, *refs), grid_s...  22.5 us
    ppermute x12, starting transfers between devices, to(): return lax.ppermute(rows, 'ctx', [(i, i ^ k) for i in range(N_CTX)])  19.5 us
  transfers between devices with their start and end apart: 33, of which 25 were waited for; matrix products, arithmetic and copies ran while one was open for 8% of the time, Pallas kernels for 20%

profile of v9, /device:TPU:0, one launch (start us, length us, event | category | flops | bytes accessed | tf_op | source)
XLA Modules:
  0.0 533.9 jit_solution(10406880272461385540)
XLA Ops:
  13.3 4.1 collective-permute-start
  18.0 4.8 all-to-all-start
  22.9 6.1 %collective-permute-done = bf16[1,128,1536]{2,1,0:T(8,128)(2,1)S(1)} collective-permute-done((bf16[1,128,1536]{2,1,0:T(8,128)(2,1)S(1)}, bf16[1,128,1536]{2,1,0:T(8,128)(2,1)S(1)}, u32[]{:S(2)}, u32[]{:S(2)}) %collective-permute-start) | collective-permute-done | bytes 393248 | tf_op jit(solution)/shard_map/ppermute | solution.py:1049
  31.7 4.6 all-to-all-start.1
  43.9 30.5 %all-to-all-done.1 = bf16[4,2,128,1536]{3,2,1,0:T(8,128)(2,1)S(1)} async-done(((bf16[4,2,128,1536]{3,2,1,0:T(8,128)(2,1)}), bf16[4,2,128,1536]{3,2,1,0:T(8,128)(2,1)S(1)}, u32[]{:S(2)}, u32[]{:S(2)}) %all-to-all-start.1) | async-done | bytes 3145760 | tf_op jit(solution)/shard_map/all_to_all | solution.py:997
  74.3 5.2 all-to-all-start.2
  85.4 5.0 all-to-all-done.2
  95.1 7.7 %project.1 = (bf16[128,1536]{1,0:T(8,128)(2,1)S(1)}, bf16[8,128,1024]{2,1,0:T(8,128)(2,1)S(1)}) custom-call(bf16[1,128,1536]{2,1,0:T(8,128)(2,1)S(1)} %copy-done.18, bf16[8,128,1536]{2,1,0:T(8,128)(2,1)S(1)} %copy-done.4, bf16[1536,4096]{1,0:T(8,128)(2,1)} %all-gather.4.cloned.1.call-done.w_ref.wq_ref.wkv_ref), custom_call_target="tpu_custom_call" | custom-call | bytes 29520000 | tf_op jit(solution)/shard_map/project/pallas_call | solution.py:798
  102.8 5.8 %attend.1 = (bf16[128,1536]{1,0:T(8,128)(2,1)S(1)}, f32[128,1536]{1,0:T(8,128)S(1)}, f32[1536,128]{1,0:T(8,128)S(1)}) custom-call(s32[1]{0:T(128)} %bitcast.ctx_ref.refs_0_, bf16[128,1536]{1,0:T(8,128)(2,1)S(1)} %get-tuple-element.107.q_ref, bf16[8,128,1024]{2,1,0:T(8,128)(2,1)S(1)} %get-tuple-element.108.k_ref.v_ref, ...), custom_call_target="tpu_custom_call" | custom-call | bytes 22140000 | tf_op jit(solution)/shard_map/attend/pallas_call | solution.py:99
  108.6 5.4 %copy-done = bf16[1536,4096]{1,0:T(8,128)(2,1)S(1)} copy-done((bf16[1536,4096]{1,0:T(8,128)(2,1)S(1)}, bf16[1536,4096]{1,0:T(8,128)(2,1)}, u32[]{:S(2)}) %copy-start) | copy-done | bytes 12582936
  118.2 20.1 %collective-permute-done.1 = bf16[1,128,1536]{2,1,0:T(8,128)(2,1)S(1)} collective-permute-done((bf16[1,128,1536]{2,1,0:T(8,128)(2,1)S(1)}, bf16[1,128,1536]{2,1,0:T(8,128)(2,1)S(1)}, u32[]{:S(2)}, u32[]{:S(2)}) %collective-permute-start.1) | collective-permute-done | bytes 393248 | tf_op jit(solution)/shard_map/ppermute | solution.py:1049
  140.4 4.8 all-to-all-start.3
  147.0 13.7 %place_rows.1 = (bf16[8,2,128,128]{3,2,1,0:T(8,128)(2,1)}, bf16[2,2,384,1536]{3,2,1,0:T(8,128)(2,1)}, f32[2,2,384,512]{3,2,1,0:T(8,128)}, f32[8,2,128,128]{3,2,1,0:T(8,128)}, f32[2,2,384,128]{3,2,1,0:T(8,128)}) custom-call(s32[1]{0:T(128)} %bitcast.7.at_ref, bf16[8,2,128,1664]{3,2,1,0:T(8,128)(2,1)} %bitcast.82, bf16[2,512,1536]{2,1,0:T(8,128)(2,1)} %wd_ref.1, ...), custom_call_target="tpu_custom_call" | custom-call | bytes 51660000 | tf_op jit(solution)/shard_map/place_rows/pallas_call | solution.py:368
  160.7 22.1 %all-to-all-done.3 = bf16[4,2,128,1536]{3,2,1,0:T(8,128)(2,1)} async-done(((bf16[4,2,128,1536]{3,2,1,0:T(8,128)(2,1)}), bf16[4,2,128,1536]{3,2,1,0:T(8,128)(2,1)}, u32[]{:S(2)}, u32[]{:S(2)}) %all-to-all-start.3) | async-done | bytes 3145760 | tf_op jit(solution)/shard_map/all_to_all | solution.py:997
  182.8 9.6 %all-gather.6.cloned.1.call-done = bf16[2048,1536]{1,0:T(8,128)(2,1)} async-done(((bf16[128,1536]{1,0:T(8,128)(2,1)}), bf16[2048,1536]{1,0:T(8,128)(2,1)}) %all-gather.6.cloned.1.call-update) | async-done | bytes 6291472 | tf_op jit(solution)/shard_map/all_gather | solution.py:1072
  192.3 28.6 %expert_back.1 = (bf16[2,8,128,1536]{3,2,1,0:T(8,128)(2,1)}, bf16[2,2,384,1536]{3,2,1,0:T(8,128)(2,1)}, bf16[2,2,384,512]{3,2,1,0:T(8,128)(2,1)}, bf16[2,2,384,1...) custom-call(s32[1]{0:T(128)} %bitcast.7.at_ref, ...), custom_call_target="tpu_custom_call" | custom-call | bytes 103320000 | tf_op jit(solution)/shard_map/expert_back/pallas_call | solution.py:447
  223.6 5.4 %collective-permute-done.2 = bf16[8,128,1536]{2,1,0:T(8,128)(2,1)S(1)} collective-permute-done((bf16[8,128,1536]{2,1,0:T(8,128)(2,1)S(1)}, bf16[8,128,1536]{2,1,0:T(8,128)(2,1)S(1)}, u32[]{:S(2)}, u32[]{:S(2)}) %collective-permute-start.2) | collective-permute-done | bytes 3145760 | tf_op jit(solution)/shard_map/ppermute | solution.py:1084
  231.6 4.8 all-to-all-start.4
  236.4 11.0 %expert_weights.2 = (bf16[9216,128]{1,0:T(8,128)(2,1)}, bf16[9216,128]{1,0:T(8,128)(2,1)}) custom-call(s32[1]{0:T(128)} %bitcast.ctx_ref.refs_0_, bf16[2,768,1536]{2,1,0:T(8,128)(2,1)} %bitcast.91, bf16[2,768,1536]{2,1,0:T(8,128)(2,1)} %bitcast.89, bf16[2,768,512]{2,1,0:T(8,128)(2,1)} %bitcast.72, bf16[2,768,1024]{2,1,0:T(8,128)(2,1)} %bitcast.85, ...), custom_call_target="tpu_custom_call" | custom-call | bytes 7380000 | tf_op jit(solution)/shard_map/expert_weights/pallas_call | solution.py:894
  249.0 11.4 %expert_weights.3 = (bf16[4608,128]{1,0:T(8,128)(2,1)}, bf16[4608,128]{1,0:T(8,128)(2,1)}, bf16[4608,128]{1,0:T(8,128)(2,1)}, bf16[4608,128]{1,0:T(8,128)(2,1)}) custom-call(s32[1]{0:T(128)} %bitcast.ctx_ref.refs_0_, bf16[2,768,1536]{2,1,0:T(8,128)(2,1)} %bitcast.92, bf16[2,768,1536]{2,1,0:T(8,128)(2,1)} %bitcast.90, bf16[2,768,512]{2,1,0:T(8,128)(2,1)} %bitcast.73, ...), custom_call_target="tpu_custom_call" | custom-call | bytes 7380000 | tf_op jit(solution)/shard_map/expert_weights/pallas_call | solution.py:894
  262.5 10.0 %expert_output.1.own_ref = bf16[2,8,128,1536]{3,2,1,0:T(8,128)(2,1)} custom-call(s32[1]{0:T(128)} %bitcast.7.at_ref, bf16[2,2,384,512]{3,2,1,0:T(8,128)(2,1)S(1)} %copy-done.5, f32[2,2,384,128]{3,2,1,0:T(8,128)S(1)} %copy-done.34, bf16[8,2,128,128]{3,2,1,0:T(8,128)(2,1)S(1)} %copy-done.14, bf16[8,2,128,128]{3,2,1,0:T(8,128)(2,1)S(1)} %copy-done.7, ...), custom_call_target="tpu_custom_call" | custom-call | bytes 7380000 | tf_op jit(solution)/shard_map/expert_output/pallas_call | solution.py:499
  272.5 5.5 %convolution_convert_fusion = bf16[1536,128]{1,0:T(8,128)(2,1)} fusion(bf16[2048,1536]{1,0:T(8,128)(2,1)} %all-gather.6.cloned.1.call-done, bf16[2048,128]{1,0:T(8,128)(2,1)S(1)} %bitcast.100), kind=kOutput, calls=%fused_computation.4 | convolution fusion | flops 805502976 | bytes 7208960 | tf_op jit(solution)/shard_map/dot_general | solution.py:39
  288.9 4.8 middle_back.1
  294.6 9.1 %attend_back.1 = (bf16[128,1536]{1,0:T(8,128)(2,1)S(1)}, bf16[4,1776,128]{2,1,0:T(8,128)(2,1)S(1)}, bf16[4,1776,128]{2,1,0:T(8,128)(2,1)}) custom-call(s32[1]{0:T(128)} %bitcast.ctx_ref.refs_0_, bf16[128,1536]{1,0:T(8,128)(2,1)S(1)} %copy-done.16, bf16[128,1536]{1,0:T(8,128)(2,1)S(1)} %get-tuple-element.134.ga_ref, f32[128,1536]{1,0:T(8,128)S(1)} %copy-done.31, ...), custom_call_target="tpu_custom_call" | custom-call | bytes 7380000 | tf_op jit(solution)/shard_map/attend_back/pallas_call | solution.py:202
  304.6 10.1 %collective-permute-done.10.relay_b.got_31 = bf16[9216,128]{1,0:T(8,128)(2,1)} collective-permute-done((bf16[9216,128]{1,0:T(8,128)(2,1)}, bf16[9216,128]{1,0:T(8,128)(2,1)}, u32[]{:S(2)}, u32[]{:S(2)}) %collective-permute-start.10) | collective-permute-done | bytes 2359328 | tf_op jit(solution)/shard_map/ppermute | solution.py:1099
  314.8 4.4 piece_sums.2
  324.4 3.3 spread_sums.1
  327.8 18.2 %collective-permute-done.11.got_11 = bf16[4608,128]{1,0:T(8,128)(2,1)S(1)} collective-permute-done((bf16[4608,128]{1,0:T(8,128)(2,1)S(1)}, bf16[4608,128]{1,0:T(8,128)(2,1)S(1)}, u32[]{:S(2)}, u32[]{:S(2)}) %collective-permute-start.11) | collective-permute-done | bytes 1179680 | tf_op jit(solution)/shard_map/ppermute | solution.py:1099
  349.1 2.9 collective-permute-start.13
  352.0 13.9 %collective-permute-done.8.got_ref = bf16[4,1776,128]{2,1,0:T(8,128)(2,1)S(1)} collective-permute-done((bf16[4,1776,128]{2,1,0:T(8,128)(2,1)}, bf16[4,1776,128]{2,1,0:T(8,128)(2,1)S(1)}, u32[]{:S(2)}, u32[]{:S(2)}) %collective-permute-start.8) | collective-permute-done | bytes 1818656 | tf_op jit(solution)/shard_map/ppermute | solution.py:1127
  372.6 4.5 all-to-all-start.5
  377.1 11.7 %collective-permute-done.13 = bf16[4608,128]{1,0:T(8,128)(2,1)S(1)} collective-permute-done((bf16[4608,128]{1,0:T(8,128)(2,1)S(1)}, bf16[4608,128]{1,0:T(8,128)(2,1)S(1)}, u32[]{:S(2)}, u32[]{:S(2)}) %collective-permute-start.13) | collective-permute-done | bytes 1179680 | tf_op jit(solution)/shard_map/ppermute | solution.py:1099
  392.7 2.9 collective-permute-start.16
  395.6 6.1 %collective-permute-done.5 = bf16[2,128,1536]{2,1,0:T(8,128)(2,1)} collective-permute-done((bf16[2,128,1536]{2,1,0:T(8,128)(2,1)}, bf16[2,128,1536]{2,1,0:T(8,128)(2,1)}, u32[]{:S(2)}, u32[]{:S(2)}) %collective-permute-start.5) | collective-permute-done | bytes 786464 | tf_op jit(solution)/shard_map/ppermute | solution.py:1150
  404.2 3.1 convert_add_fusion.1
  407.3 7.1 %column_grads.1 = (bf16[16,112,512]{2,1,0:T(8,128)(2,1)}, bf16[8,128,128]{2,1,0:T(8,128)(2,1)}, bf16[96,128]{1,0:T(8,128)(2,1)}) custom-call(bf16[4,2160,128]{2,1,0:T(8,128)(2,1)} %all-to-all-done.5.got_ref, bf16[8,128,1536]{2,1,0:T(8,128)(2,1)} %copy-done.3, bf16[8,128,1536]{2,1,0:T(8,128)(2,1)} %bitcast.10.att_ref), custom_call_target="tpu_custom_call" | custom-call | bytes 29520000 | tf_op jit(solution)/shard_map/column_grads/pallas_call | solution.py:614
  414.4 9.0 %collective-permute-done.14.refs_2_ = bf16[4608,128]{1,0:T(8,128)(2,1)} collective-permute-done((bf16[4608,128]{1,0:T(8,128)(2,1)S(1)}, bf16[4608,128]{1,0:T(8,128)(2,1)}, u32[]{:S(2)}, u32[]{:S(2)}) %collective-permute-start.14) | collective-permute-done | bytes 1179680 | tf_op jit(solution)/shard_map/ppermute | solution.py:1099
  425.8 4.6 all-to-all-start.6
  432.9 22.4 %all-to-all-done.6.got_ref = bf16[16,112,512]{2,1,0:T(8,128)(2,1)S(1)} async-done(((bf16[16,112,512]{2,1,0:T(8,128)(2,1)}), bf16[16,112,512]{2,1,0:T(8,128)(2,1)S(1)}, u32[]{:S(2)}, u32[]{:S(2)}) %all-to-all-start.6) | async-done | bytes 1835040 | tf_op jit(solution)/shard_map/all_to_all | solution.py:997
  455.5 4.0 collective-permute-done.17.refs_2_
  461.9 4.8 all-to-all-start.7
  466.8 3.2 collective-permute-start.20
  473.1 11.8 %collective-permute-done.7 = bf16[128,1536]{1,0:T(8,128)(2,1)S(1)} collective-permute-done((bf16[128,1536]{1,0:T(8,128)(2,1)}, bf16[128,1536]{1,0:T(8,128)(2,1)S(1)}, u32[]{:S(2)}, u32[]{:S(2)}) %collective-permute-start.7) | collective-permute-done | bytes 393248 | tf_op jit(solution)/shard_map/ppermute | solution.py:1152
  487.1 5.5 %unpack_experts.2 = (f32[2,1536,512]{2,1,0:T(8,128)}, f32[2,1536,512]{2,1,0:T(8,128)}, f32[2,512,1536]{2,1,0:T(8,128)}) custom-call(s32[1]{0:T(128)} %bitcast.ctx_ref.refs_0_, bf16[4608,128]{1,0:T(8,128)(2,1)S(1)} %add_convert_fusion.refs_1_, bf16[4608,128]{1,0:T(8,128)(2,1)} %collective-permute-done.14.refs_2_, bf16[4608,128]{1,0:T(8,128)(2,1)S(1)} %copy-done.26, ...), custom_call_target="tpu_custom_call" | custom-call | bytes 29520000 | tf_op jit(solution)/shard_map/unpack_experts/pallas_call | solution.py:938
  492.7 6.0 %all-to-all-done.7.got_ref = bf16[8,736,128]{2,1,0:T(8,128)(2,1)S(1)} async-done(((bf16[8,736,128]{2,1,0:T(8,128)(2,1)}), bf16[8,736,128]{2,1,0:T(8,128)(2,1)S(1)}, u32[]{:S(2)}, u32[]{:S(2)}) %all-to-all-start.7) | async-done | bytes 1507360 | tf_op jit(solution)/shard_map/all_to_all | solution.py:997
  498.7 11.3 %all-to-all-start.8 = ((bf16[8,128,128]{2,1,0:T(8,128)(2,1)}), bf16[8,128,128]{2,1,0:T(8,128)(2,1)S(1)}, u32[]{:S(2)}, u32[]{:S(2)}) async-start(bf16[8,128,128]{2,1,0:T(8,128)(2,1)} %get-tuple-element.182), calls=%async_computation.8 | async-start | bytes 524288 | tf_op jit(solution)/shard_map/all_to_all | solution.py:997
  511.3 6.4 %unpack_experts.3 = (f32[2,1536,512]{2,1,0:T(8,128)}, f32[2,1536,512]{2,1,0:T(8,128)}, f32[2,512,1536]{2,1,0:T(8,128)}) custom-call(s32[1]{0:T(128)} %bitcast.ctx_ref.refs_0_, bf16[4608,128]{1,0:T(8,128)(2,1)} %collective-permute-done.19.refs_1_, ...), custom_call_target="tpu_custom_call", output_to_operand_aliasing={{0}: (5, {}), {1}: (6, {}), {2}: (7, {})} | custom-call | bytes 29520000 | tf_op jit(solution)/shard_map/unpack_experts/pallas_call | solution.py:938
  520.2 6.9 %input_back.1 = bf16[128,1536]{1,0:T(8,128)(2,1)} custom-call(bf16[128,1536]{1,0:T(8,128)(2,1)S(1)} %copy-done.38, bf16[8,128,128]{2,1,0:T(8,128)(2,1)S(1)} %all-to-all-done.8.got_ref, bf16[1536,4096]{1,0:T(8,128)(2,1)} %all-gather.4.cloned.1.call-done.w_ref.wq_ref.wkv_ref, bf16[1536,4096]{1,0:T(8,128)(2,1)} %all-gather.4.cloned.1.call-done.w_ref.wq_ref.wkv_ref, ...), custom_call_target="tpu_custom_call" | custom-call | bytes 25830000 | tf_op jit(solution)/shard_map/input_back/pallas_call | solution.py:742
  (196 shorter events, 95.2 us)
Async XLA Ops:
  7.2 85.0 %all-gather.4.cloned.1.call-start = ((), (), s32[]{:S(2)}) async-start(), calls=%async_computation.9 | async-start | bytes 13369344 | tf_op jit(solution)/shard_map/all_gather | solution.py:1035
  12.0 135.0 %all-gather.8.cloned.1.call-start = ((), (), s32[]{:S(2)}) async-start(), calls=%async_computation.11 | async-start | bytes 7241728 | tf_op jit(solution)/shard_map/all_gather | solution.py:1042
  13.3 15.8 %collective-permute-start = (bf16[1,128,1536]{2,1,0:T(8,128)(2,1)S(1)}, bf16[1,128,1536]{2,1,0:T(8,128)(2,1)S(1)}, u32[]{:S(2)}, u32[]{:S(2)}) collective-permute-start(bf16[1,128,1536]{2,1,0:T(8,128)(2,1)S(1)} %copy-done.6), channel_id=1, source_target_pairs={{0,64},{16,80},{32,96},{48,112},{64,0},{80,16},{96,32},{112,48},{1... | collective-permute-start | bytes 1179656 | tf_op jit(solution)/shard_map/ppermute | solution.py:1049
  18.0 11.7 %all-to-all-start = ((bf16[16,1,192]{2,1,0:T(2,128)(2,1)}), bf16[16,1,192]{2,1,0:T(2,128)(2,1)S(1)}, u32[]{:S(2)}, u32[]{:S(2)}) async-start(bf16[16,1,192]{2,1,0:T(2,128)(2,1)} %broadcast_in_dim.24), calls=%async_computation | async-start | bytes 32768 | tf_op jit(solution)/shard_map/all_to_all | solution.py:997
  31.7 42.6 %all-to-all-start.1 = ((bf16[4,2,128,1536]{3,2,1,0:T(8,128)(2,1)}), bf16[4,2,128,1536]{3,2,1,0:T(8,128)(2,1)S(1)}, u32[]{:S(2)}, u32[]{:S(2)}) async-start(bf16[4,2,128,1536]{3,2,1,0:T(8,128)(2,1)} %broadcast_in_dim.25), calls=%async_computation.1 | async-start | bytes 6291456 | tf_op jit(solution)/shard_map/all_to_all | solution.py:997
  74.3 16.1 %all-to-all-start.2 = ((bf16[16,96,128]{2,1,0:T(8,128)(2,1)}), bf16[16,96,128]{2,1,0:T(8,128)(2,1)}, u32[]{:S(2)}, u32[]{:S(2)}) async-start(bf16[16,96,128]{2,1,0:T(8,128)(2,1)} %copy.62), calls=%async_computation.2 | async-start | bytes 786432 | tf_op jit(solution)/shard_map/all_to_all | solution.py:997
  79.5 112.8 %all-gather.6.cloned.1.call-start = ((), (), s32[]{:S(2)}) async-start(), calls=%async_computation.10 | async-start | bytes 6684672 | tf_op jit(solution)/shard_map/all_gather | solution.py:1072
  102.7 12.9 %copy-start.2 = (bf16[8,128,1024]{2,1,0:T(8,128)(2,1)}, bf16[8,128,1024]{2,1,0:T(8,128)(2,1)S(1)}, u32[]{:S(2)}) copy-start(bf16[8,128,1024]{2,1,0:T(8,128)(2,1)S(1)} %get-tuple-element.108.k_ref.v_ref) | copy-start | bytes 6291460
  102.8 12.9 %copy-start.15 = (bf16[128,1536]{1,0:T(8,128)(2,1)}, bf16[128,1536]{1,0:T(8,128)(2,1)S(1)}, u32[]{:S(2)}) copy-start(bf16[128,1536]{1,0:T(8,128)(2,1)S(1)} %get-tuple-element.107.q_ref) | copy-start | bytes 1179652
  116.6 21.7 %collective-permute-start.1 = (bf16[1,128,1536]{2,1,0:T(8,128)(2,1)S(1)}, bf16[1,128,1536]{2,1,0:T(8,128)(2,1)S(1)}, u32[]{:S(2)}, u32[]{:S(2)}) collective-permute-start(bf16[1,128,1536]{2,1,0:T(8,128)(2,1)S(1)} %bitcast.80), channel_id=1, source_target_pairs={{0,64},{16,80},{32,96},{48,112},{64,0},{80,16},{96,32},{112,48},{1... | collective-permute-start | bytes 1179656 | tf_op jit(solution)/shard_map/ppermute | solution.py:1049
  140.4 42.4 %all-to-all-start.3 = ((bf16[4,2,128,1536]{3,2,1,0:T(8,128)(2,1)}), bf16[4,2,128,1536]{3,2,1,0:T(8,128)(2,1)}, u32[]{:S(2)}, u32[]{:S(2)}) async-start(bf16[4,2,128,1536]{3,2,1,0:T(8,128)(2,1)} %broadcast_in_dim.27), calls=%async_computation.3 | async-start | bytes 6291456 | tf_op jit(solution)/shard_map/all_to_all | solution.py:997
  223.2 5.7 %collective-permute-start.2 = (bf16[8,128,1536]{2,1,0:T(8,128)(2,1)S(1)}, bf16[8,128,1536]{2,1,0:T(8,128)(2,1)S(1)}, u32[]{:S(2)}, u32[]{:S(2)}) collective-permute-start(bf16[8,128,1536]{2,1,0:T(8,128)(2,1)S(1)} %slice_bitcast_fusion.1), channel_id=1, source_target_pairs={{0,1},{1,0},{2,3},{3,2},{4,5},{5,4},{6,7},{7,6},{8,9},{9,8},{10,11... | collective-permute-start | bytes 9437192 | tf_op jit(solution)/shard_map/ppermute | solution.py:1084
  231.6 55.2 %all-to-all-start.4 = ((bf16[8,128,1536]{2,1,0:T(8,128)(2,1)}), bf16[8,128,1536]{2,1,0:T(8,128)(2,1)S(1)}, u32[]{:S(2)}, u32[]{:S(2)}) async-start(bf16[8,128,1536]{2,1,0:T(8,128)(2,1)} %fusion), calls=%async_computation.4 | async-start | bytes 6291456 | tf_op jit(solution)/shard_map/all_to_all | solution.py:997
  247.4 15.1 %copy-start.5 = (bf16[2,2,384,512]{3,2,1,0:T(8,128)(2,1)S(1)}, bf16[2,2,384,512]{3,2,1,0:T(8,128)(2,1)}, u32[]{:S(2)}) copy-start(bf16[2,2,384,512]{3,2,1,0:T(8,128)(2,1)} %get-tuple-element.127.act_ref) | copy-start | bytes 4718596
  247.4 15.1 %copy-start.7 = (bf16[8,2,128,128]{3,2,1,0:T(8,128)(2,1)S(1)}, bf16[8,2,128,128]{3,2,1,0:T(8,128)(2,1)}, u32[]{:S(2)}) copy-start(bf16[8,2,128,128]{3,2,1,0:T(8,128)(2,1)} %get-tuple-element.132.sact_ref) | copy-start | bytes 1572868
  247.4 15.1 %copy-start.12 = (bf16[128,1536]{1,0:T(8,128)(2,1)S(1)}, bf16[128,1536]{1,0:T(8,128)(2,1)}, u32[]{:S(2)}) copy-start(bf16[128,1536]{1,0:T(8,128)(2,1)} %copy-done.11) | copy-start | bytes 1179652
  247.4 15.1 %copy-start.14 = (bf16[8,2,128,128]{3,2,1,0:T(8,128)(2,1)S(1)}, bf16[8,2,128,128]{3,2,1,0:T(8,128)(2,1)}, u32[]{:S(2)}) copy-start(bf16[8,2,128,128]{3,2,1,0:T(8,128)(2,1)} %get-tuple-element.115.place_ref) | copy-start | bytes 1572868
  247.4 15.1 %copy-start.34 = (f32[2,2,384,128]{3,2,1,0:T(8,128)S(1)}, f32[2,2,384,128]{3,2,1,0:T(8,128)}, u32[]{:S(2)}) copy-start(f32[2,2,384,128]{3,2,1,0:T(8,128)} %get-tuple-element.128.gate_ref) | copy-start | bytes 2359300
  247.4 67.4 %collective-permute-start.9 = (bf16[9216,128]{1,0:T(8,128)(2,1)}, bf16[9216,128]{1,0:T(8,128)(2,1)}, u32[]{:S(2)}, u32[]{:S(2)}) collective-permute-start(bf16[9216,128]{1,0:T(8,128)(2,1)} %get-tuple-element.124), channel_id=1, source_target_pairs={{0,16},{16,0},{32,48},{48,32},{64,80},{80,64},{96,112},{112,96},{1... | collective-permute-start | bytes 7077896 | tf_op jit(solution)/shard_map/ppermute | solution.py:1099
  260.4 54.4 %collective-permute-start.10 = (bf16[9216,128]{1,0:T(8,128)(2,1)}, bf16[9216,128]{1,0:T(8,128)(2,1)}, u32[]{:S(2)}, u32[]{:S(2)}) collective-permute-start(bf16[9216,128]{1,0:T(8,128)(2,1)} %get-tuple-element.150), channel_id=1, source_target_pairs={{0,48},{16,32},{32,16},{48,0},{64,112},{80,96},{96,80},{112,64},{1... | collective-permute-start | bytes 7077896 | tf_op jit(solution)/shard_map/ppermute | solution.py:1099
  262.5 17.4 %slice-start.2 = ((s8[6815744]{0:T(1024)(128)(4,1)}), s8[2621440]{0:T(1024)(128)(4,1)S(1)}, s32[]{:S(2)}) async-start(s8[6815744]{0:T(1024)(128)(4,1)} %bitcast.83), calls=%async_computation.14 | async-start | bytes 5242880
  294.5 20.2 %copy-start.21 = (bf16[4608,128]{1,0:T(8,128)(2,1)S(1)}, bf16[4608,128]{1,0:T(8,128)(2,1)}, u32[]{:S(2)}) copy-start(bf16[4608,128]{1,0:T(8,128)(2,1)} %get-tuple-element.126.p0) | copy-start | bytes 3538948
  294.6 20.2 %copy-start.22 = (bf16[4608,128]{1,0:T(8,128)(2,1)S(1)}, bf16[4608,128]{1,0:T(8,128)(2,1)}, u32[]{:S(2)}) copy-start(bf16[4608,128]{1,0:T(8,128)(2,1)} %get-tuple-element.149.p6) | copy-start | bytes 3538948
  294.6 20.2 %copy-start.23 = (bf16[4608,128]{1,0:T(8,128)(2,1)S(1)}, bf16[4608,128]{1,0:T(8,128)(2,1)}, u32[]{:S(2)}) copy-start(bf16[4608,128]{1,0:T(8,128)(2,1)} %get-tuple-element.147.p1) | copy-start | bytes 3538948
  294.6 20.2 %copy-start.24 = (bf16[4608,128]{1,0:T(8,128)(2,1)S(1)}, bf16[4608,128]{1,0:T(8,128)(2,1)}, u32[]{:S(2)}) copy-start(bf16[4608,128]{1,0:T(8,128)(2,1)} %get-tuple-element.148.p3) | copy-start | bytes 3538948
  304.5 19.9 %collective-permute-start.3 = (bf16[8,128,1536]{2,1,0:T(8,128)(2,1)}, bf16[8,128,1536]{2,1,0:T(8,128)(2,1)S(1)}, u32[]{:S(2)}, u32[]{:S(2)}) collective-permute-start(bf16[8,128,1536]{2,1,0:T(8,128)(2,1)} %slice_bitcast_fusion), channel_id=1, source_target_pairs={{0,1},{1,0},{2,3},{3,2},{4,5},{5,4},{6,7},{7,6},{8,9},{9,8},{10,11... | collective-permute-start | bytes 9437192 | tf_op jit(solution)/shard_map/ppermute | solution.py:1144
  319.2 26.7 %collective-permute-start.11 = (bf16[4608,128]{1,0:T(8,128)(2,1)S(1)}, bf16[4608,128]{1,0:T(8,128)(2,1)S(1)}, u32[]{:S(2)}, u32[]{:S(2)}) collective-permute-start(bf16[4608,128]{1,0:T(8,128)(2,1)S(1)} %get-tuple-element.155), channel_id=1, source_target_pairs={{0,16},{16,0},{32,48},{48,32},{64,80},{80,64},{96,112},{112,96},{1... | collective-permute-start | bytes 3538952 | tf_op jit(solution)/shard_map/ppermute | solution.py:1099
  319.3 28.0 %collective-permute-start.12 = (bf16[4608,128]{1,0:T(8,128)(2,1)S(1)}, bf16[4608,128]{1,0:T(8,128)(2,1)S(1)}, u32[]{:S(2)}, u32[]{:S(2)}) collective-permute-start(bf16[4608,128]{1,0:T(8,128)(2,1)S(1)} %get-tuple-element.156), channel_id=1, source_target_pairs={{0,48},{16,32},{32,16},{48,0},{64,112},{80,96},{96,80},{112,64},{1... | collective-permute-start | bytes 3538952 | tf_op jit(solution)/shard_map/ppermute | solution.py:1099
  321.6 44.3 %collective-permute-start.8 = (bf16[4,1776,128]{2,1,0:T(8,128)(2,1)}, bf16[4,1776,128]{2,1,0:T(8,128)(2,1)S(1)}, u32[]{:S(2)}, u32[]{:S(2)}) collective-permute-start(bf16[4,1776,128]{2,1,0:T(8,128)(2,1)} %get-tuple-element.146), channel_id=1, source_target_pairs={{0,64},{16,80},{32,96},{48,112},{64,0},{80,16},{96,32},{112,48},{1... | collective-permute-start | bytes 5455880 | tf_op jit(solution)/shard_map/ppermute | solution.py:1127
  349.1 39.6 %collective-permute-start.13 = (bf16[4608,128]{1,0:T(8,128)(2,1)S(1)}, bf16[4608,128]{1,0:T(8,128)(2,1)S(1)}, u32[]{:S(2)}, u32[]{:S(2)}) collective-permute-start(bf16[4608,128]{1,0:T(8,128)(2,1)S(1)} %get-tuple-element.159), channel_id=1, source_target_pairs={{0,64},{16,80},{32,96},{48,112},{64,0},{80,16},{96,32},{112,48},{1... | collective-permute-start | bytes 3538952 | tf_op jit(solution)/shard_map/ppermute | solution.py:1099
  367.9 24.8 %collective-permute-start.4 = (bf16[2,128,1536]{2,1,0:T(8,128)(2,1)}, bf16[2,128,1536]{2,1,0:T(8,128)(2,1)}, u32[]{:S(2)}, u32[]{:S(2)}) collective-permute-start(bf16[2,128,1536]{2,1,0:T(8,128)(2,1)} %get-tuple-element.142), channel_id=1, source_target_pairs={{0,4},{1,5},{2,6},{3,7},{4,0},{5,1},{6,2},{7,3},{8,12},{9,13},{10,... | collective-permute-start | bytes 2359304 | tf_op jit(solution)/shard_map/ppermute | solution.py:1150
  369.6 32.0 %collective-permute-start.5 = (bf16[2,128,1536]{2,1,0:T(8,128)(2,1)}, bf16[2,128,1536]{2,1,0:T(8,128)(2,1)}, u32[]{:S(2)}, u32[]{:S(2)}) collective-permute-start(bf16[2,128,1536]{2,1,0:T(8,128)(2,1)} %get-tuple-element.143), channel_id=1, source_target_pairs={{0,8},{1,9},{2,10},{3,11},{4,12},{5,13},{6,14},{7,15},{8,0},{9,1},... | collective-permute-start | bytes 2359304 | tf_op jit(solution)/shard_map/ppermute | solution.py:1150
  372.3 31.9 %collective-permute-start.6 = (bf16[2,128,1536]{2,1,0:T(8,128)(2,1)}, bf16[2,128,1536]{2,1,0:T(8,128)(2,1)}, u32[]{:S(2)}, u32[]{:S(2)}) collective-permute-start(bf16[2,128,1536]{2,1,0:T(8,128)(2,1)} %get-tuple-element.144), channel_id=1, source_target_pairs={{0,12},{1,13},{2,14},{3,15},{4,8},{5,9},{6,10},{7,11},{8,4},{9,5},... | collective-permute-start | bytes 2359304 | tf_op jit(solution)/shard_map/ppermute | solution.py:1150
  372.6 34.7 %all-to-all-start.5 = ((bf16[4,2160,128]{2,1,0:T(8,128)(2,1)}), bf16[4,2160,128]{2,1,0:T(8,128)(2,1)}, u32[]{:S(2)}, u32[]{:S(2)}) async-start(bf16[4,2160,128]{2,1,0:T(8,128)(2,1)} %merge_shares.1), calls=%async_computation.5 | async-start | bytes 4423680 | tf_op jit(solution)/shard_map/all_to_all | solution.py:997
  390.6 32.7 %collective-permute-start.14 = (bf16[4608,128]{1,0:T(8,128)(2,1)S(1)}, bf16[4608,128]{1,0:T(8,128)(2,1)}, u32[]{:S(2)}, u32[]{:S(2)}) collective-permute-start(bf16[4608,128]{1,0:T(8,128)(2,1)S(1)} %add_convert_fusion.refs_1_), channel_id=1, source_target_pairs={{0,16},{16,0},{32,48},{48,32},{64,80},{80,64},{96,112},{112,96},{1... | collective-permute-start | bytes 3538952 | tf_op jit(solution)/shard_map/ppermute | solution.py:1099
  391.8 33.0 %collective-permute-start.15 = (bf16[4608,128]{1,0:T(8,128)(2,1)S(1)}, bf16[4608,128]{1,0:T(8,128)(2,1)S(1)}, u32[]{:S(2)}, u32[]{:S(2)}) collective-permute-start(bf16[4608,128]{1,0:T(8,128)(2,1)S(1)} %add_convert_fusion.refs_1_), channel_id=1, source_target_pairs={{0,48},{16,32},{32,16},{48,0},{64,112},{80,96},{96,80},{112,64},{1... | collective-permute-start | bytes 3538952 | tf_op jit(solution)/shard_map/ppermute | solution.py:1099
  392.7 37.7 %collective-permute-start.16 = (bf16[4608,128]{1,0:T(8,128)(2,1)S(1)}, bf16[4608,128]{1,0:T(8,128)(2,1)}, u32[]{:S(2)}, u32[]{:S(2)}) collective-permute-start(bf16[4608,128]{1,0:T(8,128)(2,1)S(1)} %add_convert_fusion.refs_1_), channel_id=1, source_target_pairs={{0,64},{16,80},{32,96},{48,112},{64,0},{80,16},{96,32},{112,48},{1... | collective-permute-start | bytes 3538952 | tf_op jit(solution)/shard_map/ppermute | solution.py:1099
  414.4 40.9 %copy-start.39 = (bf16[96,128]{1,0:T(8,128)(2,1)S(1)}, bf16[96,128]{1,0:T(8,128)(2,1)}, u32[]{:S(2)}) copy-start(bf16[96,128]{1,0:T(8,128)(2,1)} %get-tuple-element.166.down_ref) | copy-start | bytes 73732
  425.8 29.5 %all-to-all-start.6 = ((bf16[16,112,512]{2,1,0:T(8,128)(2,1)}), bf16[16,112,512]{2,1,0:T(8,128)(2,1)S(1)}, u32[]{:S(2)}, u32[]{:S(2)}) async-start(bf16[16,112,512]{2,1,0:T(8,128)(2,1)} %get-tuple-element.165), calls=%async_computation.6 | async-start | bytes 3670016 | tf_op jit(solution)/shard_map/all_to_all | solution.py:997
  430.4 29.2 %collective-permute-start.17 = (bf16[4608,128]{1,0:T(8,128)(2,1)}, bf16[4608,128]{1,0:T(8,128)(2,1)}, u32[]{:S(2)}, u32[]{:S(2)}) collective-permute-start(bf16[4608,128]{1,0:T(8,128)(2,1)} %collective-permute-done.16.refs_4_), channel_id=1, source_target_pairs={{0,16},{16,0},{32,48},{48,32},{64,80},{80,64},{96,112},{112,96},{1... | collective-permute-start | bytes 3538952 | tf_op jit(solution)/shard_map/ppermute | solution.py:1099
  431.1 29.5 %collective-permute-start.18 = (bf16[4608,128]{1,0:T(8,128)(2,1)}, bf16[4608,128]{1,0:T(8,128)(2,1)}, u32[]{:S(2)}, u32[]{:S(2)}) collective-permute-start(bf16[4608,128]{1,0:T(8,128)(2,1)} %collective-permute-done.16.refs_4_), channel_id=1, source_target_pairs={{0,48},{16,32},{32,16},{48,0},{64,112},{80,96},{96,80},{112,64},{1... | collective-permute-start | bytes 3538952 | tf_op jit(solution)/shard_map/ppermute | solution.py:1099
  432.3 78.1 %collective-permute-start.19 = (bf16[4608,128]{1,0:T(8,128)(2,1)}, bf16[4608,128]{1,0:T(8,128)(2,1)}, u32[]{:S(2)}, u32[]{:S(2)}) collective-permute-start(bf16[4608,128]{1,0:T(8,128)(2,1)} %copy-done.25), channel_id=1, source_target_pairs={{0,16},{16,0},{32,48},{48,32},{64,80},{80,64},{96,112},{112,96},{1... | collective-permute-start | bytes 3538952 | tf_op jit(solution)/shard_map/ppermute | solution.py:1099
  460.6 12.3 %copy-start.48 = (bf16[96]{0:T(256)(128)(2,1)S(1)}, bf16[96]{0:T(256)(128)(2,1)}, u32[]{:S(2)}) copy-start(bf16[96]{0:T(256)(128)(2,1)} %param.19) | copy-start | bytes 580
  461.9 36.7 %all-to-all-start.7 = ((bf16[8,736,128]{2,1,0:T(8,128)(2,1)}), bf16[8,736,128]{2,1,0:T(8,128)(2,1)S(1)}, u32[]{:S(2)}, u32[]{:S(2)}) async-start(bf16[8,736,128]{2,1,0:T(8,128)(2,1)} %broadcast_in_dim.30), calls=%async_computation.7 | async-start | bytes 3014656 | tf_op jit(solution)/shard_map/all_to_all | solution.py:997
  466.8 44.6 %collective-permute-start.20 = (bf16[4608,128]{1,0:T(8,128)(2,1)}, bf16[4608,128]{1,0:T(8,128)(2,1)}, u32[]{:S(2)}, u32[]{:S(2)}) collective-permute-start(bf16[4608,128]{1,0:T(8,128)(2,1)} %collective-permute-done.17.refs_2_), channel_id=1, source_target_pairs={{0,48},{16,32},{32,16},{48,0},{64,112},{80,96},{96,80},{112,64},{1... | collective-permute-start | bytes 3538952 | tf_op jit(solution)/shard_map/ppermute | solution.py:1099
  471.9 13.0 %collective-permute-start.7 = (bf16[128,1536]{1,0:T(8,128)(2,1)}, bf16[128,1536]{1,0:T(8,128)(2,1)S(1)}, u32[]{:S(2)}, u32[]{:S(2)}) collective-permute-start(bf16[128,1536]{1,0:T(8,128)(2,1)} %fusion.5), channel_id=1, source_target_pairs={{0,2},{1,3},{2,0},{3,1},{4,6},{5,7},{6,4},{7,5},{8,10},{9,11},{10,... | collective-permute-start | bytes 1179656 | tf_op jit(solution)/shard_map/ppermute | solution.py:1152
  473.1 14.1 %copy-start.26 = (bf16[4608,128]{1,0:T(8,128)(2,1)S(1)}, bf16[4608,128]{1,0:T(8,128)(2,1)}, u32[]{:S(2)}) copy-start(bf16[4608,128]{1,0:T(8,128)(2,1)} %copy-done.25) | copy-start | bytes 3538948
  498.7 21.6 %all-to-all-start.8 = ((bf16[8,128,128]{2,1,0:T(8,128)(2,1)}), bf16[8,128,128]{2,1,0:T(8,128)(2,1)S(1)}, u32[]{:S(2)}, u32[]{:S(2)}) async-start(bf16[8,128,128]{2,1,0:T(8,128)(2,1)} %get-tuple-element.182), calls=%async_computation.8 | async-start | bytes 524288 | tf_op jit(solution)/shard_map/all_to_all | solution.py:997
  (38 other events, 178.0 us)
Sparse Core Ops, SparseCore 0:
  12.2 79.9 all-gather.3
  94.5 52.5 all-gather.7
  149.3 42.9 all-gather.5

commit v10 on v9

--- a/solution.py
+++ b/solution.py
@@ -820,8 +820,10 @@
 PIECE = 2 * WIDTH + WIDTH * BLOCK // HEAD_DIM
 
 
-def spread_kernel(at_ref, own_ref, got_ref, *outs):
-    total = (own_ref[0, 0].astype(f32) + got_ref[0].astype(f32)).astype(bf16)
+def spread_kernel(at_ref, own_ref, low_ref, high_ref, *outs):
+    chip = (at_ref[0] >> 1) ^ pl.program_id(0)
+    got = jnp.where(chip < 4, low_ref[0], high_ref[0])
+    total = (own_ref[0, 0].astype(f32) + got.astype(f32)).astype(bf16)
     for k in range(HALF):
 
         @pl.when(pl.program_id(0) == k)
@@ -829,7 +831,8 @@
             outs[k // 2][k % 2] = total
 
 
-def spread_sums(exp_at, parts, got):
+def spread_sums(exp_at, parts, low, high):
+    half = pl.BlockSpec((1, BLOCK, WIDTH), lambda k, at: (((at[0] >> 1) ^ k) & 3, 0, 0))
     return pl.pallas_call(
         spread_kernel,
         grid_spec=pltpu.PrefetchScalarGridSpec(
@@ -837,7 +840,8 @@
             grid=(HALF,),
             in_specs=[
                 pl.BlockSpec((1, 1, BLOCK, WIDTH), lambda k, at: (1, (at[0] >> 1) ^ k, 0, 0)),
-                pl.BlockSpec((1, BLOCK, WIDTH), lambda k, at: ((at[0] >> 1) ^ k, 0, 0)),
+                half,
+                half,
             ],
             out_specs=[whole((2, BLOCK, WIDTH))] * 4,
         ),
@@ -845,7 +849,7 @@
         cost_estimate=cost(4),
         compiler_params=params(32),
         name="spread_sums",
-    )(exp_at, parts, got)
+    )(exp_at, parts, low, high)
 
 
 def of_step(values, step):
@@ -1114,10 +1118,7 @@
         axis=1,
     )
 
-    out_part = expert_output(
-        exp_s, after(act, p0), slot_gate, place, shared_act, expert_down, shared_two
-    )
-    grad_two = after(grad_two, extra, out_part)
+    grad_two = after(grad_two, p0, extra)
     grad_middle, grad_attn, grad_heads, gain_rows = middle_back(
         grad_two, middle, cotangent[0], gain_ffn, w_all
     )
@@ -1140,11 +1141,28 @@
     )
     got_11, got_30 = to(add_b, 1), to(add_a, 3)
 
+    got_11, got_30 = after((got_11, got_30), far)
+    own_part, side = piece_sums(side_kernel, (f32, bf16), part_0, part_1, got_11, got_30)
+    across = to(side, 4)
+
+    shares = merge_shares(ctx_s, near, after(far, side))
+    got = swap_all(shares, "ctx", y_groups)
+    own = (own_part + after(across, shares).astype(f32)).astype(bf16)
+    at_1, at_3, at_z = to(own, 1), to(own, 3), to(own, 4)
+
+    out_part = expert_output(
+        exp_s, after(act, side), slot_gate, place, shared_act, expert_down, shared_two
+    )
     out_sums = spread_sums(
-        exp_s, out_part, lax.ppermute(after(out_part[0], near), "exp", core_swap)
-    )
-    got_11, got_30 = after((got_11, got_30), out_sums[0])
-    own_part, side = piece_sums(side_kernel, (f32, bf16), part_0, part_1, got_11, got_30)
+        exp_s,
+        out_part,
+        lax.ppermute(out_part[0, :4], "exp", core_swap),
+        lax.ppermute(out_part[0, 4:], "exp", core_swap),
+    )
+    columns, grad_kv, grad_down = column_grads(got, after(hidden_seq, own), att_seq)
+    grad_kv = swap_all(grad_kv, "ctx")
+    columns = after(columns, grad_kv, at_1, at_3, out_sums[0])
+    owned = swap_all(columns, "exp")
     out_rows = out_sums[0].astype(f32)
     for k in range(1, 4):
         moved = lax.ppermute(out_sums[k], "exp", [(i, i ^ (4 * k)) for i in range(N_EXP)])
@@ -1152,36 +1170,26 @@
     out_across = lax.ppermute(
         out_rows[1].astype(bf16), "exp", [(i, i ^ 2) for i in range(N_EXP)]
     )
-    across = to(side, 4)
-
-    shares = merge_shares(ctx_s, near, after(far, side))
-    got = swap_all(shares, "ctx", y_groups)
-    own = (own_part + after(across, shares).astype(f32)).astype(bf16)
-    at_1, at_3, at_z = to(own, 1), to(own, 3), to(own, 4)
-    columns, grad_kv, grad_down = column_grads(got, after(hidden_seq, own, out_rows), att_seq)
-    columns, at_1, at_3 = lax.optimization_barrier((columns, at_1, at_3))
-    owned = swap_all(columns, "exp")
+    input_grad = input_back(grad_query, grad_kv, w_all, tokens[0], gain_attn, grad_middle)
     owned, gain_sum = owned_sums(owned, grad_down)
-    owned, at_z1, at_z3 = lax.optimization_barrier((owned, to(at_z, 1), to(at_z, 3)))
+    owned, at_z1, at_z3 = lax.optimization_barrier(
+        (after(owned, out_rows, input_grad), to(at_z, 1), to(at_z, 3))
+    )
     at_2, at_z2 = to(at_3, 1), to(at_z1, 3)
     mixed = (middle + out_rows[0] + out_across.astype(f32)).astype(bf16)[None]
     experts = unpack_experts(
         ctx_s, ((0, 0), (1, 0), (3, 0), (0, 1)), (after(own, owned), at_1, at_3, at_z)
     )
     owned = swap_all(jnp.broadcast_to(owned, (N_CTX, OWNED_ROWS, HEAD_DIM)), "ctx")
-    grad_kv = swap_all(after(grad_kv, owned, mixed), "ctx")
     experts = unpack_experts(
         ctx_s, ((2, 0), (1, 1), (3, 1), (2, 1)), (at_2, at_z1, at_z3, at_z2), experts
     )
     gain_attn_sum, *dense = finish(
-        after(owned, experts[0]),
+        after(owned, experts[0], mixed),
         norm_attn.astype(f32).reshape(96, 1),
         query_weight,
         key_weight,
         value_weight,
-    )
-    input_grad = input_back(
-        after(grad_query, dense[0]), grad_kv, w_all, tokens[0], gain_attn, grad_middle
     )
     return (
         mixed,

time: 544 us -> 541 us (level)
  local copies, waits for them, and re-layouts: 47.3 us -> 59.8 us
  waiting for transfers between devices: 223 us -> 214 us
  starting transfers between devices: 83.8 us -> 75.5 us
    ppermute x3, waiting for transfers between devices: 8.63 us -> 41.8 us  [on_device(): lax.ppermute(out_sums[k], 'exp', [(i, i ^ 4 * k) for i in range(N_EXP)])]
    ppermute x12, waiting for transfers between devices: 57.6 us -> 30.4 us  [to(): return lax.ppermute(rows, 'ctx', [(i, i ^ k) for i in range(N_CTX)])]
    all_to_all x9, waiting for transfers between devices: 86.5 us -> 72.4 us  [swap_all(): lax.all_to_all(rows, axis, split_axis=0, concat_axis=0, tiled=True, axis_...]
    unnamed x116 -> x126, local copies, waits for them, and re-layouts: 26.7 us -> 38.1 us
    all_to_all x9, starting transfers between devices: 49.4 us -> 41.5 us  [swap_all(): lax.all_to_all(rows, axis, split_axis=0, concat_axis=0, tiled=True, axis_...]
    ppermute x1, waiting for transfers between devices: 13.9 us -> 6.64 us  [on_device(): far = lax.ppermute(far, 'ctx', z_swap)]
    ppermute x1, waiting for transfers between devices: 11.8 us -> 18.4 us  [on_device(): lax.ppermute(out_rows[1].astype(bf16), 'exp', [(i, i ^ 2) for i in range(...]
  transfers between devices with their start and end apart: 33 -> 34, of which waited for: 25 -> 23; matrix products, arithmetic and copies ran while one was open for 8% -> 8% of each run, Pallas kernels for 20% -> 21%
where the time goes in v10:
time: 541 us; the launch traced here: 531 us
  waiting for transfers between devices  214 us (40%)
  Pallas kernels  145 us (27%)
  starting transfers between devices  75.5 us (14%)
  local copies, waits for them, and re-layouts  59.8 us (11%)
  between operations  14.9 us (3%)
  other arithmetic  11.8 us (2%)
  matrix products  9.46 us (2%)
    all_to_all x9, waiting for transfers between devices, swap_all(): lax.all_to_all(rows, axis, split_axis=0, concat_axis=0, tiled=True, axis_...  72.4 us
    ppermute x3, waiting for transfers between devices, on_device(): lax.ppermute(out_sums[k], 'exp', [(i, i ^ 4 * k) for i in range(N_EXP)])  41.8 us
    all_to_all x9, starting transfers between devices, swap_all(): lax.all_to_all(rows, axis, split_axis=0, concat_axis=0, tiled=True, axis_...  41.5 us
    unnamed x126, local copies, waits for them, and re-layouts  38.1 us
    ppermute x12, waiting for transfers between devices, to(): return lax.ppermute(rows, 'ctx', [(i, i ^ k) for i in range(N_CTX)])  30.4 us
    pallas_call x1, Pallas kernels, expert_back(): pl.pallas_call(expert_kernel, grid_spec=pltpu.PrefetchScalarGridSpec(num_...  28.9 us
    ppermute x2, waiting for transfers between devices, of_sequence(): other = lax.ppermute(rows, 'ctx', z_swap)  26.2 us
    pallas_call x2, Pallas kernels, expert_weights(): pl.pallas_call(lambda *refs: expert_weights_kernel(halved, *refs), grid_s...  22.1 us
  transfers between devices with their start and end apart: 34, of which 23 were waited for; matrix products, arithmetic and copies ran while one was open for 8% of the time, Pallas kernels for 21%

profile of v10, /device:TPU:0, one launch (start us, length us, event | category | flops | bytes accessed | tf_op | source)
XLA Modules:
  0.0 530.9 jit_solution(5152757538740435405)
XLA Ops:
  13.3 4.1 collective-permute-start
  18.0 4.8 all-to-all-start
  22.9 6.1 %collective-permute-done = bf16[1,128,1536]{2,1,0:T(8,128)(2,1)S(1)} collective-permute-done((bf16[1,128,1536]{2,1,0:T(8,128)(2,1)S(1)}, bf16[1,128,1536]{2,1,0:T(8,128)(2,1)S(1)}, u32[]{:S(2)}, u32[]{:S(2)}) %collective-permute-start) | collective-permute-done | bytes 393248 | tf_op jit(solution)/shard_map/ppermute | solution.py:1053
  31.7 4.7 all-to-all-start.1
  43.9 30.5 %all-to-all-done.1 = bf16[4,2,128,1536]{3,2,1,0:T(8,128)(2,1)S(1)} async-done(((bf16[4,2,128,1536]{3,2,1,0:T(8,128)(2,1)}), bf16[4,2,128,1536]{3,2,1,0:T(8,128)(2,1)S(1)}, u32[]{:S(2)}, u32[]{:S(2)}) %all-to-all-start.1) | async-done | bytes 3145760 | tf_op jit(solution)/shard_map/all_to_all | solution.py:1001
  74.3 5.2 all-to-all-start.2
  86.2 4.3 all-to-all-done.2
  95.1 7.7 %project.1 = (bf16[128,1536]{1,0:T(8,128)(2,1)S(1)}, bf16[8,128,1024]{2,1,0:T(8,128)(2,1)S(1)}) custom-call(bf16[1,128,1536]{2,1,0:T(8,128)(2,1)S(1)} %copy-done.21, bf16[8,128,1536]{2,1,0:T(8,128)(2,1)S(1)} %copy-done.4, bf16[1536,4096]{1,0:T(8,128)(2,1)} %all-gather.4.cloned.1.call-done.w_ref.wq_ref.wkv_ref), custom_call_target="tpu_custom_call" | custom-call | bytes 29520000 | tf_op jit(solution)/shard_map/project/pallas_call | solution.py:798
  102.8 5.8 %attend.1 = (bf16[128,1536]{1,0:T(8,128)(2,1)S(1)}, f32[128,1536]{1,0:T(8,128)S(1)}, f32[1536,128]{1,0:T(8,128)S(1)}) custom-call(s32[1]{0:T(128)} %bitcast.ctx_ref.refs_0_, bf16[128,1536]{1,0:T(8,128)(2,1)S(1)} %get-tuple-element.103.q_ref, bf16[8,128,1024]{2,1,0:T(8,128)(2,1)S(1)} %get-tuple-element.104.k_ref.v_ref, ...), custom_call_target="tpu_custom_call" | custom-call | bytes 22140000 | tf_op jit(solution)/shard_map/attend/pallas_call | solution.py:99
  108.6 5.4 %copy-done = bf16[1536,4096]{1,0:T(8,128)(2,1)S(1)} copy-done((bf16[1536,4096]{1,0:T(8,128)(2,1)S(1)}, bf16[1536,4096]{1,0:T(8,128)(2,1)}, u32[]{:S(2)}) %copy-start) | copy-done | bytes 12582936
  118.3 20.1 %collective-permute-done.1 = bf16[1,128,1536]{2,1,0:T(8,128)(2,1)S(1)} collective-permute-done((bf16[1,128,1536]{2,1,0:T(8,128)(2,1)S(1)}, bf16[1,128,1536]{2,1,0:T(8,128)(2,1)S(1)}, u32[]{:S(2)}, u32[]{:S(2)}) %collective-permute-start.1) | collective-permute-done | bytes 393248 | tf_op jit(solution)/shard_map/ppermute | solution.py:1053
  140.4 4.8 all-to-all-start.3
  147.0 13.7 %place_rows.1 = (bf16[8,2,128,128]{3,2,1,0:T(8,128)(2,1)}, bf16[2,2,384,1536]{3,2,1,0:T(8,128)(2,1)}, f32[2,2,384,512]{3,2,1,0:T(8,128)}, f32[8,2,128,128]{3,2,1,0:T(8,128)}, f32[2,2,384,128]{3,2,1,0:T(8,128)}) custom-call(s32[1]{0:T(128)} %bitcast.7.at_ref, bf16[8,2,128,1664]{3,2,1,0:T(8,128)(2,1)} %bitcast.82, bf16[2,512,1536]{2,1,0:T(8,128)(2,1)} %wd_ref.1, ...), custom_call_target="tpu_custom_call" | custom-call | bytes 51660000 | tf_op jit(solution)/shard_map/place_rows/pallas_call | solution.py:368
  160.7 22.2 %all-to-all-done.3 = bf16[4,2,128,1536]{3,2,1,0:T(8,128)(2,1)} async-done(((bf16[4,2,128,1536]{3,2,1,0:T(8,128)(2,1)}), bf16[4,2,128,1536]{3,2,1,0:T(8,128)(2,1)}, u32[]{:S(2)}, u32[]{:S(2)}) %all-to-all-start.3) | async-done | bytes 3145760 | tf_op jit(solution)/shard_map/all_to_all | solution.py:1001
  182.9 9.5 %all-gather.6.cloned.1.call-done = bf16[2048,1536]{1,0:T(8,128)(2,1)} async-done(((bf16[128,1536]{1,0:T(8,128)(2,1)}), bf16[2048,1536]{1,0:T(8,128)(2,1)}) %all-gather.6.cloned.1.call-update) | async-done | bytes 6291472 | tf_op jit(solution)/shard_map/all_gather | solution.py:1076
  192.3 28.9 %expert_back.1 = (bf16[2,8,128,1536]{3,2,1,0:T(8,128)(2,1)}, bf16[2,2,384,1536]{3,2,1,0:T(8,128)(2,1)}, bf16[2,2,384,512]{3,2,1,0:T(8,128)(2,1)}, bf16[2,2,384,1...) custom-call(s32[1]{0:T(128)} %bitcast.7.at_ref, ...), custom_call_target="tpu_custom_call" | custom-call | bytes 103320000 | tf_op jit(solution)/shard_map/expert_back/pallas_call | solution.py:447
  223.9 5.4 %collective-permute-done.2 = bf16[8,128,1536]{2,1,0:T(8,128)(2,1)S(1)} collective-permute-done((bf16[8,128,1536]{2,1,0:T(8,128)(2,1)S(1)}, bf16[8,128,1536]{2,1,0:T(8,128)(2,1)S(1)}, u32[]{:S(2)}, u32[]{:S(2)}) %collective-permute-start.2) | collective-permute-done | bytes 3145760 | tf_op jit(solution)/shard_map/ppermute | solution.py:1088
  231.9 4.8 all-to-all-start.4
  236.7 10.9 %expert_weights.2 = (bf16[9216,128]{1,0:T(8,128)(2,1)}, bf16[9216,128]{1,0:T(8,128)(2,1)}) custom-call(s32[1]{0:T(128)} %bitcast.ctx_ref.refs_0_, bf16[2,768,1536]{2,1,0:T(8,128)(2,1)} %bitcast.89, bf16[2,768,1536]{2,1,0:T(8,128)(2,1)} %bitcast.87, bf16[2,768,512]{2,1,0:T(8,128)(2,1)} %bitcast.72, bf16[2,768,1024]{2,1,0:T(8,128)(2,1)} %bitcast.83, ...), custom_call_target="tpu_custom_call" | custom-call | bytes 7380000 | tf_op jit(solution)/shard_map/expert_weights/pallas_call | solution.py:898
  251.2 11.2 %expert_weights.3 = (bf16[4608,128]{1,0:T(8,128)(2,1)}, bf16[4608,128]{1,0:T(8,128)(2,1)}, bf16[4608,128]{1,0:T(8,128)(2,1)}, bf16[4608,128]{1,0:T(8,128)(2,1)}) custom-call(s32[1]{0:T(128)} %bitcast.ctx_ref.refs_0_, bf16[2,768,1536]{2,1,0:T(8,128)(2,1)} %bitcast.90, bf16[2,768,1536]{2,1,0:T(8,128)(2,1)} %bitcast.88, bf16[2,768,512]{2,1,0:T(8,128)(2,1)} %bitcast.73, ...), custom_call_target="tpu_custom_call" | custom-call | bytes 7380000 | tf_op jit(solution)/shard_map/expert_weights/pallas_call | solution.py:898
  262.3 5.4 %convolution_convert_fusion = bf16[1536,128]{1,0:T(8,128)(2,1)} fusion(bf16[2048,1536]{1,0:T(8,128)(2,1)} %all-gather.6.cloned.1.call-done, bf16[2048,128]{1,0:T(8,128)(2,1)S(1)} %bitcast.98), kind=kOutput, calls=%fused_computation.3 | convolution fusion | flops 805502976 | bytes 7208960 | tf_op jit(solution)/shard_map/dot_general | solution.py:39
  270.8 4.1 fusion.8
  275.8 6.7 %all-to-all-done.4.pieces_ref = bf16[8,128,1536]{2,1,0:T(8,128)(2,1)S(1)} async-done(((bf16[8,128,1536]{2,1,0:T(8,128)(2,1)}), bf16[8,128,1536]{2,1,0:T(8,128)(2,1)S(1)}, u32[]{:S(2)}, u32[]{:S(2)}) %all-to-all-start.4) | async-done | bytes 3145760 | tf_op jit(solution)/shard_map/all_to_all | solution.py:1001
  284.7 4.8 middle_back.1
  289.6 9.3 %attend_back.1 = (bf16[128,1536]{1,0:T(8,128)(2,1)S(1)}, bf16[4,1776,128]{2,1,0:T(8,128)(2,1)S(1)}, bf16[4,1776,128]{2,1,0:T(8,128)(2,1)}) custom-call(s32[1]{0:T(128)} %bitcast.ctx_ref.refs_0_, bf16[128,1536]{1,0:T(8,128)(2,1)S(1)} %copy-done.19, bf16[128,1536]{1,0:T(8,128)(2,1)S(1)} %get-tuple-element.132.ga_ref, f32[128,1536]{1,0:T(8,128)S(1)} %copy-done.35, ...), custom_call_target="tpu_custom_call" | custom-call | bytes 7380000 | tf_op jit(solution)/shard_map/attend_back/pallas_call | solution.py:202
  299.6 2.9 collective-permute-start.7
  303.5 3.7 piece_sums.2
  309.8 24.1 %collective-permute-done.5.got_11 = bf16[4608,128]{1,0:T(8,128)(2,1)S(1)} collective-permute-done((bf16[4608,128]{1,0:T(8,128)(2,1)S(1)}, bf16[4608,128]{1,0:T(8,128)(2,1)S(1)}, u32[]{:S(2)}, u32[]{:S(2)}) %collective-permute-start.5) | collective-permute-done | bytes 1179680 | tf_op jit(solution)/shard_map/ppermute | solution.py:1103
  335.4 6.6 %collective-permute-done.7.got_ref = bf16[4,1776,128]{2,1,0:T(8,128)(2,1)S(1)} collective-permute-done((bf16[4,1776,128]{2,1,0:T(8,128)(2,1)}, bf16[4,1776,128]{2,1,0:T(8,128)(2,1)S(1)}, u32[]{:S(2)}, u32[]{:S(2)}) %collective-permute-start.7) | collective-permute-done | bytes 1818656 | tf_op jit(solution)/shard_map/ppermute | solution.py:1128
  345.2 2.8 collective-permute-start.14
  349.9 5.0 all-to-all-start.5
  356.1 9.8 %expert_output.1.own_ref = bf16[2,8,128,1536]{3,2,1,0:T(8,128)(2,1)} custom-call(s32[1]{0:T(128)} %bitcast.7.at_ref, bf16[2,2,384,512]{3,2,1,0:T(8,128)(2,1)S(1)} %copy-done.5, f32[2,2,384,128]{3,2,1,0:T(8,128)S(1)} %copy-done.33, bf16[8,2,128,128]{3,2,1,0:T(8,128)(2,1)S(1)} %copy-done.17, bf16[8,2,128,128]{3,2,1,0:T(8,128)(2,1)S(1)} %copy-done.9, ...), custom_call_target="tpu_custom_call" | custom-call | bytes 7380000 | tf_op jit(solution)/shard_map/expert_output/pallas_call | solution.py:499
  365.8 3.9 slice_bitcast_fusion.1
  370.2 2.8 collective-permute-done.14
  378.3 2.8 collective-permute-start.17
  381.1 2.9 all-to-all-done.5.got_ref
  384.0 7.1 %column_grads.1 = (bf16[16,112,512]{2,1,0:T(8,128)(2,1)}, bf16[8,128,128]{2,1,0:T(8,128)(2,1)}, bf16[96,128]{1,0:T(8,128)(2,1)}) custom-call(bf16[4,2160,128]{2,1,0:T(8,128)(2,1)} %all-to-all-done.5.got_ref, bf16[8,128,1536]{2,1,0:T(8,128)(2,1)} %copy-done.3, bf16[8,128,1536]{2,1,0:T(8,128)(2,1)} %bitcast.10.att_ref), custom_call_target="tpu_custom_call" | custom-call | bytes 29520000 | tf_op jit(solution)/shard_map/column_grads/pallas_call | solution.py:614
  391.0 3.4 all-to-all-start.6
  397.3 5.3 %spread_sums.1 = (bf16[2,128,1536]{2,1,0:T(8,128)(2,1)S(1)}, bf16[2,128,1536]{2,1,0:T(8,128)(2,1)S(1)}, bf16[2,128,1536]{2,1,0:T(8,128)(2,1)S(1)}, bf16[2,128,1536]{2,1,0:T(8,128)(2,1)S(1)}) custom-call(s32[1]{0:T(128)} %bitcast.7.at_ref, bf16[2,8,128,1536]{3,2,1,0:T(8,128)(2,1)S(1)} %copy-done.1, bf16[4,128,1536]{2,1,0:T(8,128)(2,1)S(1)} %collective-permute-done.8.low_ref, ...), custom_call_target="tpu_custom_call" | custom-call | bytes 14760000 | tf_op jit(solution)/shard_map/spread_sums/pallas_call | solution.py:836
  406.1 2.9 all-to-all-done.6.got_ref
  409.8 3.7 all-to-all-start.7
  423.0 7.0 %input_back.1 = bf16[128,1536]{1,0:T(8,128)(2,1)} custom-call(bf16[128,1536]{1,0:T(8,128)(2,1)S(1)} %copy-done.43, bf16[8,128,128]{2,1,0:T(8,128)(2,1)S(1)} %copy-done.30, bf16[1536,4096]{1,0:T(8,128)(2,1)} %all-gather.4.cloned.1.call-done.w_ref.wq_ref.wkv_ref, bf16[1536,4096]{1,0:T(8,128)(2,1)} %all-gather.4.cloned.1.call-done.w_ref.wq_ref.wkv_ref, ...), custom_call_target="tpu_custom_call" | custom-call | bytes 25830000 | tf_op jit(solution)/shard_map/input_back/pallas_call | solution.py:742
  430.0 23.6 %collective-permute-done.10 = bf16[2,128,1536]{2,1,0:T(8,128)(2,1)S(1)} collective-permute-done((bf16[2,128,1536]{2,1,0:T(8,128)(2,1)}, bf16[2,128,1536]{2,1,0:T(8,128)(2,1)S(1)}, u32[]{:S(2)}, u32[]{:S(2)}) %collective-permute-start.10) | collective-permute-done | bytes 786464 | tf_op jit(solution)/shard_map/ppermute | solution.py:1168
  454.1 18.2 %collective-permute-done.11 = bf16[2,128,1536]{2,1,0:T(8,128)(2,1)S(1)} collective-permute-done((bf16[2,128,1536]{2,1,0:T(8,128)(2,1)}, bf16[2,128,1536]{2,1,0:T(8,128)(2,1)S(1)}, u32[]{:S(2)}, u32[]{:S(2)}) %collective-permute-start.11) | collective-permute-done | bytes 786464 | tf_op jit(solution)/shard_map/ppermute | solution.py:1168
  477.1 5.1 all-to-all-start.8
  484.5 18.4 %collective-permute-done.13 = bf16[128,1536]{1,0:T(8,128)(2,1)S(1)} collective-permute-done((bf16[128,1536]{1,0:T(8,128)(2,1)}, bf16[128,1536]{1,0:T(8,128)(2,1)S(1)}, u32[]{:S(2)}, u32[]{:S(2)}) %collective-permute-start.13) | collective-permute-done | bytes 393248 | tf_op jit(solution)/shard_map/ppermute | solution.py:1170
  505.2 5.9 %unpack_experts.2 = (f32[2,1536,512]{2,1,0:T(8,128)}, f32[2,1536,512]{2,1,0:T(8,128)}, f32[2,512,1536]{2,1,0:T(8,128)}) custom-call(s32[1]{0:T(128)} %bitcast.ctx_ref.refs_0_, bf16[4608,128]{1,0:T(8,128)(2,1)S(1)} %add_convert_fusion.refs_1_, bf16[4608,128]{1,0:T(8,128)(2,1)} %collective-permute-done.15.refs_2_, ...), custom_call_target="tpu_custom_call" | custom-call | bytes 29520000 | tf_op jit(solution)/shard_map/unpack_experts/pallas_call | solution.py:942
  512.6 6.4 %unpack_experts.3 = (f32[2,1536,512]{2,1,0:T(8,128)}, f32[2,1536,512]{2,1,0:T(8,128)}, f32[2,512,1536]{2,1,0:T(8,128)}) custom-call(s32[1]{0:T(128)} %bitcast.ctx_ref.refs_0_, bf16[4608,128]{1,0:T(8,128)(2,1)} %collective-permute-done.20.refs_1_, ...), custom_call_target="tpu_custom_call", output_to_operand_aliasing={{0}: (5, {}), {1}: (6, {}), {2}: (7, {})} | custom-call | bytes 29520000 | tf_op jit(solution)/shard_map/unpack_experts/pallas_call | solution.py:942
  (206 shorter events, 101.7 us)
Async XLA Ops:
  7.2 10.1 %copy-start.56 = (bf16[96]{0:T(256)(128)(2,1)S(1)}, bf16[96]{0:T(256)(128)(2,1)}, u32[]{:S(2)}) copy-start(bf16[96]{0:T(256)(128)(2,1)} %param.19) | copy-start | bytes 580
  7.2 10.1 %copy-start.55 = (bf16[96]{0:T(256)(128)(2,1)S(1)}, bf16[96]{0:T(256)(128)(2,1)}, u32[]{:S(2)}) copy-start(bf16[96]{0:T(256)(128)(2,1)} %param.20) | copy-start | bytes 580
  7.2 85.0 %all-gather.4.cloned.1.call-start = ((), (), s32[]{:S(2)}) async-start(), calls=%async_computation.9 | async-start | bytes 13369344 | tf_op jit(solution)/shard_map/all_gather | solution.py:1039
  12.0 135.0 %all-gather.8.cloned.1.call-start = ((), (), s32[]{:S(2)}) async-start(), calls=%async_computation.11 | async-start | bytes 7241728 | tf_op jit(solution)/shard_map/all_gather | solution.py:1046
  13.3 15.8 %collective-permute-start = (bf16[1,128,1536]{2,1,0:T(8,128)(2,1)S(1)}, bf16[1,128,1536]{2,1,0:T(8,128)(2,1)S(1)}, u32[]{:S(2)}, u32[]{:S(2)}) collective-permute-start(bf16[1,128,1536]{2,1,0:T(8,128)(2,1)S(1)} %copy-done.7), channel_id=1, source_target_pairs={{0,64},{16,80},{32,96},{48,112},{64,0},{80,16},{96,32},{112,48},{1... | collective-permute-start | bytes 1179656 | tf_op jit(solution)/shard_map/ppermute | solution.py:1053
  18.0 11.7 %all-to-all-start = ((bf16[16,1,192]{2,1,0:T(2,128)(2,1)}), bf16[16,1,192]{2,1,0:T(2,128)(2,1)S(1)}, u32[]{:S(2)}, u32[]{:S(2)}) async-start(bf16[16,1,192]{2,1,0:T(2,128)(2,1)} %broadcast_in_dim.24), calls=%async_computation | async-start | bytes 32768 | tf_op jit(solution)/shard_map/all_to_all | solution.py:1001
  31.7 42.6 %all-to-all-start.1 = ((bf16[4,2,128,1536]{3,2,1,0:T(8,128)(2,1)}), bf16[4,2,128,1536]{3,2,1,0:T(8,128)(2,1)S(1)}, u32[]{:S(2)}, u32[]{:S(2)}) async-start(bf16[4,2,128,1536]{3,2,1,0:T(8,128)(2,1)} %broadcast_in_dim.25), calls=%async_computation.1 | async-start | bytes 6291456 | tf_op jit(solution)/shard_map/all_to_all | solution.py:1001
  74.3 16.1 %all-to-all-start.2 = ((bf16[16,96,128]{2,1,0:T(8,128)(2,1)}), bf16[16,96,128]{2,1,0:T(8,128)(2,1)}, u32[]{:S(2)}, u32[]{:S(2)}) async-start(bf16[16,96,128]{2,1,0:T(8,128)(2,1)} %copy.62), calls=%async_computation.2 | async-start | bytes 786432 | tf_op jit(solution)/shard_map/all_to_all | solution.py:1001
  79.6 112.8 %all-gather.6.cloned.1.call-start = ((), (), s32[]{:S(2)}) async-start(), calls=%async_computation.10 | async-start | bytes 6684672 | tf_op jit(solution)/shard_map/all_gather | solution.py:1076
  102.8 12.9 %copy-start.2 = (bf16[8,128,1024]{2,1,0:T(8,128)(2,1)}, bf16[8,128,1024]{2,1,0:T(8,128)(2,1)S(1)}, u32[]{:S(2)}) copy-start(bf16[8,128,1024]{2,1,0:T(8,128)(2,1)S(1)} %get-tuple-element.104.k_ref.v_ref) | copy-start | bytes 6291460
  102.8 12.9 %copy-start.18 = (bf16[128,1536]{1,0:T(8,128)(2,1)}, bf16[128,1536]{1,0:T(8,128)(2,1)S(1)}, u32[]{:S(2)}) copy-start(bf16[128,1536]{1,0:T(8,128)(2,1)S(1)} %get-tuple-element.103.q_ref) | copy-start | bytes 1179652
  116.6 21.7 %collective-permute-start.1 = (bf16[1,128,1536]{2,1,0:T(8,128)(2,1)S(1)}, bf16[1,128,1536]{2,1,0:T(8,128)(2,1)S(1)}, u32[]{:S(2)}, u32[]{:S(2)}) collective-permute-start(bf16[1,128,1536]{2,1,0:T(8,128)(2,1)S(1)} %bitcast.80), channel_id=1, source_target_pairs={{0,64},{16,80},{32,96},{48,112},{64,0},{80,16},{96,32},{112,48},{1... | collective-permute-start | bytes 1179656 | tf_op jit(solution)/shard_map/ppermute | solution.py:1053
  140.4 42.4 %all-to-all-start.3 = ((bf16[4,2,128,1536]{3,2,1,0:T(8,128)(2,1)}), bf16[4,2,128,1536]{3,2,1,0:T(8,128)(2,1)}, u32[]{:S(2)}, u32[]{:S(2)}) async-start(bf16[4,2,128,1536]{3,2,1,0:T(8,128)(2,1)} %broadcast_in_dim.27), calls=%async_computation.3 | async-start | bytes 6291456 | tf_op jit(solution)/shard_map/all_to_all | solution.py:1001
  223.5 5.7 %collective-permute-start.2 = (bf16[8,128,1536]{2,1,0:T(8,128)(2,1)S(1)}, bf16[8,128,1536]{2,1,0:T(8,128)(2,1)S(1)}, u32[]{:S(2)}, u32[]{:S(2)}) collective-permute-start(bf16[8,128,1536]{2,1,0:T(8,128)(2,1)S(1)} %slice_bitcast_fusion), channel_id=1, source_target_pairs={{0,1},{1,0},{2,3},{3,2},{4,5},{5,4},{6,7},{7,6},{8,9},{9,8},{10,11... | collective-permute-start | bytes 9437192 | tf_op jit(solution)/shard_map/ppermute | solution.py:1088
  231.9 50.7 %all-to-all-start.4 = ((bf16[8,128,1536]{2,1,0:T(8,128)(2,1)}), bf16[8,128,1536]{2,1,0:T(8,128)(2,1)S(1)}, u32[]{:S(2)}, u32[]{:S(2)}) async-start(bf16[8,128,1536]{2,1,0:T(8,128)(2,1)} %fusion), calls=%async_computation.4 | async-start | bytes 6291456 | tf_op jit(solution)/shard_map/all_to_all | solution.py:1001
  247.6 54.9 %collective-permute-start.3 = (bf16[9216,128]{1,0:T(8,128)(2,1)}, bf16[9216,128]{1,0:T(8,128)(2,1)}, u32[]{:S(2)}, u32[]{:S(2)}) collective-permute-start(bf16[9216,128]{1,0:T(8,128)(2,1)} %get-tuple-element.120), channel_id=1, source_target_pairs={{0,16},{16,0},{32,48},{48,32},{64,80},{80,64},{96,112},{112,96},{1... | collective-permute-start | bytes 7077896 | tf_op jit(solution)/shard_map/ppermute | solution.py:1103
  249.1 13.3 %copy-start.54 = (bf16[8,2,128,128]{3,2,1,0:T(8,128)(2,1)S(1)}, bf16[8,2,128,128]{3,2,1,0:T(8,128)(2,1)}, u32[]{:S(2)}) copy-start(bf16[8,2,128,128]{3,2,1,0:T(8,128)(2,1)} %get-tuple-element.128) | copy-start | bytes 1572868
  249.1 54.4 %collective-permute-start.4 = (bf16[9216,128]{1,0:T(8,128)(2,1)}, bf16[9216,128]{1,0:T(8,128)(2,1)}, u32[]{:S(2)}, u32[]{:S(2)}) collective-permute-start(bf16[9216,128]{1,0:T(8,128)(2,1)} %get-tuple-element.126), channel_id=1, source_target_pairs={{0,48},{16,32},{32,16},{48,0},{64,112},{80,96},{96,80},{112,64},{1... | collective-permute-start | bytes 7077896 | tf_op jit(solution)/shard_map/ppermute | solution.py:1103
  289.5 9.4 %copy-start.31 = (f32[128,1536]{1,0:T(8,128)}, f32[128,1536]{1,0:T(8,128)S(1)}, u32[]{:S(2)}) copy-start(f32[128,1536]{1,0:T(8,128)S(1)} %get-tuple-element.160.gm_ref) | copy-start | bytes 2359300
  289.5 13.9 %copy-start.24 = (bf16[4608,128]{1,0:T(8,128)(2,1)S(1)}, bf16[4608,128]{1,0:T(8,128)(2,1)}, u32[]{:S(2)}) copy-start(bf16[4608,128]{1,0:T(8,128)(2,1)} %get-tuple-element.122.p0) | copy-start | bytes 3538948
  289.5 13.9 %copy-start.25 = (bf16[4608,128]{1,0:T(8,128)(2,1)S(1)}, bf16[4608,128]{1,0:T(8,128)(2,1)}, u32[]{:S(2)}) copy-start(bf16[4608,128]{1,0:T(8,128)(2,1)} %get-tuple-element.125.p6) | copy-start | bytes 3538948
  289.5 13.9 %copy-start.26 = (bf16[4608,128]{1,0:T(8,128)(2,1)S(1)}, bf16[4608,128]{1,0:T(8,128)(2,1)}, u32[]{:S(2)}) copy-start(bf16[4608,128]{1,0:T(8,128)(2,1)} %get-tuple-element.123.p1) | copy-start | bytes 3538948
  289.5 13.9 %copy-start.27 = (bf16[4608,128]{1,0:T(8,128)(2,1)S(1)}, bf16[4608,128]{1,0:T(8,128)(2,1)}, u32[]{:S(2)}) copy-start(bf16[4608,128]{1,0:T(8,128)(2,1)} %get-tuple-element.124.p3) | copy-start | bytes 3538948
  299.6 42.4 %collective-permute-start.7 = (bf16[4,1776,128]{2,1,0:T(8,128)(2,1)}, bf16[4,1776,128]{2,1,0:T(8,128)(2,1)S(1)}, u32[]{:S(2)}, u32[]{:S(2)}) collective-permute-start(bf16[4,1776,128]{2,1,0:T(8,128)(2,1)} %get-tuple-element.144), channel_id=1, source_target_pairs={{0,64},{16,80},{32,96},{48,112},{64,0},{80,16},{96,32},{112,48},{1... | collective-permute-start | bytes 5455880 | tf_op jit(solution)/shard_map/ppermute | solution.py:1128
  307.1 26.8 %collective-permute-start.5 = (bf16[4608,128]{1,0:T(8,128)(2,1)S(1)}, bf16[4608,128]{1,0:T(8,128)(2,1)S(1)}, u32[]{:S(2)}, u32[]{:S(2)}) collective-permute-start(bf16[4608,128]{1,0:T(8,128)(2,1)S(1)} %get-tuple-element.142), channel_id=1, source_target_pairs={{0,16},{16,0},{32,48},{48,32},{64,80},{80,64},{96,112},{112,96},{1... | collective-permute-start | bytes 3538952 | tf_op jit(solution)/shard_map/ppermute | solution.py:1103
  307.7 27.7 %collective-permute-start.6 = (bf16[4608,128]{1,0:T(8,128)(2,1)S(1)}, bf16[4608,128]{1,0:T(8,128)(2,1)S(1)}, u32[]{:S(2)}, u32[]{:S(2)}) collective-permute-start(bf16[4608,128]{1,0:T(8,128)(2,1)S(1)} %get-tuple-element.143), channel_id=1, source_target_pairs={{0,48},{16,32},{32,16},{48,0},{64,112},{80,96},{96,80},{112,64},{1... | collective-permute-start | bytes 3538952 | tf_op jit(solution)/shard_map/ppermute | solution.py:1103
  345.2 27.9 %collective-permute-start.14 = (bf16[4608,128]{1,0:T(8,128)(2,1)}, bf16[4608,128]{1,0:T(8,128)(2,1)}, u32[]{:S(2)}, u32[]{:S(2)}) collective-permute-start(bf16[4608,128]{1,0:T(8,128)(2,1)} %get-tuple-element.147), channel_id=1, source_target_pairs={{0,64},{16,80},{32,96},{48,112},{64,0},{80,16},{96,32},{112,48},{1... | collective-permute-start | bytes 3538952 | tf_op jit(solution)/shard_map/ppermute | solution.py:1103
  349.9 34.1 %all-to-all-start.5 = ((bf16[4,2160,128]{2,1,0:T(8,128)(2,1)}), bf16[4,2160,128]{2,1,0:T(8,128)(2,1)}, u32[]{:S(2)}, u32[]{:S(2)}) async-start(bf16[4,2160,128]{2,1,0:T(8,128)(2,1)} %copy-done.6), calls=%async_computation.5 | async-start | bytes 4423680 | tf_op jit(solution)/shard_map/all_to_all | solution.py:1001
  369.7 24.7 %collective-permute-start.8 = (bf16[4,128,1536]{2,1,0:T(8,128)(2,1)}, bf16[4,128,1536]{2,1,0:T(8,128)(2,1)S(1)}, u32[]{:S(2)}, u32[]{:S(2)}) collective-permute-start(bf16[4,128,1536]{2,1,0:T(8,128)(2,1)} %get-tuple-element.189), channel_id=1, source_target_pairs={{0,1},{1,0},{2,3},{3,2},{4,5},{5,4},{6,7},{7,6},{8,9},{9,8},{10,11... | collective-permute-start | bytes 4718600 | tf_op jit(solution)/shard_map/ppermute | solution.py:1159
  369.7 24.7 %collective-permute-start.9 = (bf16[4,128,1536]{2,1,0:T(8,128)(2,1)}, bf16[4,128,1536]{2,1,0:T(8,128)(2,1)}, u32[]{:S(2)}, u32[]{:S(2)}) collective-permute-start(bf16[4,128,1536]{2,1,0:T(8,128)(2,1)} %get-tuple-element.188), channel_id=1, source_target_pairs={{0,1},{1,0},{2,3},{3,2},{4,5},{5,4},{6,7},{7,6},{8,9},{9,8},{10,11... | collective-permute-start | bytes 4718600 | tf_op jit(solution)/shard_map/ppermute | solution.py:1160
  374.6 35.1 %collective-permute-start.15 = (bf16[4608,128]{1,0:T(8,128)(2,1)S(1)}, bf16[4608,128]{1,0:T(8,128)(2,1)}, u32[]{:S(2)}, u32[]{:S(2)}) collective-permute-start(bf16[4608,128]{1,0:T(8,128)(2,1)S(1)} %add_convert_fusion.refs_1_), channel_id=1, source_target_pairs={{0,16},{16,0},{32,48},{48,32},{64,80},{80,64},{96,112},{112,96},{1... | collective-permute-start | bytes 3538952 | tf_op jit(solution)/shard_map/ppermute | solution.py:1103
  376.2 33.6 %collective-permute-start.16 = (bf16[4608,128]{1,0:T(8,128)(2,1)S(1)}, bf16[4608,128]{1,0:T(8,128)(2,1)}, u32[]{:S(2)}, u32[]{:S(2)}) collective-permute-start(bf16[4608,128]{1,0:T(8,128)(2,1)S(1)} %add_convert_fusion.refs_1_), channel_id=1, source_target_pairs={{0,48},{16,32},{32,16},{48,0},{64,112},{80,96},{96,80},{112,64},{1... | collective-permute-start | bytes 3538952 | tf_op jit(solution)/shard_map/ppermute | solution.py:1103
  378.3 40.0 %collective-permute-start.17 = (bf16[4608,128]{1,0:T(8,128)(2,1)S(1)}, bf16[4608,128]{1,0:T(8,128)(2,1)}, u32[]{:S(2)}, u32[]{:S(2)}) collective-permute-start(bf16[4608,128]{1,0:T(8,128)(2,1)S(1)} %add_convert_fusion.refs_1_), channel_id=1, source_target_pairs={{0,64},{16,80},{32,96},{48,112},{64,0},{80,16},{96,32},{112,48},{1... | collective-permute-start | bytes 3538952 | tf_op jit(solution)/shard_map/ppermute | solution.py:1103
  391.0 18.0 %all-to-all-start.6 = ((bf16[8,128,128]{2,1,0:T(8,128)(2,1)}), bf16[8,128,128]{2,1,0:T(8,128)(2,1)S(1)}, u32[]{:S(2)}, u32[]{:S(2)}) async-start(bf16[8,128,128]{2,1,0:T(8,128)(2,1)} %get-tuple-element.159), calls=%async_computation.6 | async-start | bytes 524288 | tf_op jit(solution)/shard_map/all_to_all | solution.py:1001
  409.8 64.0 %all-to-all-start.7 = ((bf16[16,112,512]{2,1,0:T(8,128)(2,1)}), bf16[16,112,512]{2,1,0:T(8,128)(2,1)S(1)}, u32[]{:S(2)}, u32[]{:S(2)}) async-start(bf16[16,112,512]{2,1,0:T(8,128)(2,1)} %get-tuple-element.162), calls=%async_computation.7 | async-start | bytes 3670016 | tf_op jit(solution)/shard_map/all_to_all | solution.py:1001
  413.5 40.1 %collective-permute-start.10 = (bf16[2,128,1536]{2,1,0:T(8,128)(2,1)}, bf16[2,128,1536]{2,1,0:T(8,128)(2,1)S(1)}, u32[]{:S(2)}, u32[]{:S(2)}) collective-permute-start(bf16[2,128,1536]{2,1,0:T(8,128)(2,1)} %copy-done.47), channel_id=1, source_target_pairs={{0,4},{1,5},{2,6},{3,7},{4,0},{5,1},{6,2},{7,3},{8,12},{9,13},{10,... | collective-permute-start | bytes 2359304 | tf_op jit(solution)/shard_map/ppermute | solution.py:1168
  415.3 56.9 %collective-permute-start.11 = (bf16[2,128,1536]{2,1,0:T(8,128)(2,1)}, bf16[2,128,1536]{2,1,0:T(8,128)(2,1)S(1)}, u32[]{:S(2)}, u32[]{:S(2)}) collective-permute-start(bf16[2,128,1536]{2,1,0:T(8,128)(2,1)} %copy-done.46), channel_id=1, source_target_pairs={{0,8},{1,9},{2,10},{3,11},{4,12},{5,13},{6,14},{7,15},{8,0},{9,1},... | collective-permute-start | bytes 2359304 | tf_op jit(solution)/shard_map/ppermute | solution.py:1168
  418.0 54.2 %collective-permute-start.12 = (bf16[2,128,1536]{2,1,0:T(8,128)(2,1)}, bf16[2,128,1536]{2,1,0:T(8,128)(2,1)S(1)}, u32[]{:S(2)}, u32[]{:S(2)}) collective-permute-start(bf16[2,128,1536]{2,1,0:T(8,128)(2,1)} %copy-done.45), channel_id=1, source_target_pairs={{0,12},{1,13},{2,14},{3,15},{4,8},{5,9},{6,10},{7,11},{8,4},{9,5},... | collective-permute-start | bytes 2359304 | tf_op jit(solution)/shard_map/ppermute | solution.py:1168
  418.3 55.8 %collective-permute-start.18 = (bf16[4608,128]{1,0:T(8,128)(2,1)}, bf16[4608,128]{1,0:T(8,128)(2,1)}, u32[]{:S(2)}, u32[]{:S(2)}) collective-permute-start(bf16[4608,128]{1,0:T(8,128)(2,1)} %collective-permute-done.17.refs_4_), channel_id=1, source_target_pairs={{0,16},{16,0},{32,48},{48,32},{64,80},{80,64},{96,112},{112,96},{1... | collective-permute-start | bytes 3538952 | tf_op jit(solution)/shard_map/ppermute | solution.py:1103
  418.8 55.3 %collective-permute-start.19 = (bf16[4608,128]{1,0:T(8,128)(2,1)}, bf16[4608,128]{1,0:T(8,128)(2,1)}, u32[]{:S(2)}, u32[]{:S(2)}) collective-permute-start(bf16[4608,128]{1,0:T(8,128)(2,1)} %collective-permute-done.17.refs_4_), channel_id=1, source_target_pairs={{0,48},{16,32},{32,16},{48,0},{64,112},{80,96},{96,80},{112,64},{1... | collective-permute-start | bytes 3538952 | tf_op jit(solution)/shard_map/ppermute | solution.py:1103
  423.0 49.3 %copy-start.39 = (bf16[2,128,1536]{2,1,0:T(8,128)(2,1)S(1)}, bf16[2,128,1536]{2,1,0:T(8,128)(2,1)}, u32[]{:S(2)}) copy-start(bf16[2,128,1536]{2,1,0:T(8,128)(2,1)} %copy-done.38) | copy-start | bytes 2359300
  430.0 43.8 %copy-start.44 = (bf16[96,128]{1,0:T(8,128)(2,1)S(1)}, bf16[96,128]{1,0:T(8,128)(2,1)}, u32[]{:S(2)}) copy-start(bf16[96,128]{1,0:T(8,128)(2,1)} %get-tuple-element.163.down_ref) | copy-start | bytes 73732
  453.6 58.0 %collective-permute-start.20 = (bf16[4608,128]{1,0:T(8,128)(2,1)}, bf16[4608,128]{1,0:T(8,128)(2,1)}, u32[]{:S(2)}, u32[]{:S(2)}) collective-permute-start(bf16[4608,128]{1,0:T(8,128)(2,1)} %collective-permute-done.16.refs_3_), channel_id=1, source_target_pairs={{0,16},{16,0},{32,48},{48,32},{64,80},{80,64},{96,112},{112,96},{1... | collective-permute-start | bytes 3538952 | tf_op jit(solution)/shard_map/ppermute | solution.py:1103
  474.0 10.4 %copy-start.57 = (bf16[96]{0:T(256)(128)(2,1)S(1)}, bf16[96]{0:T(256)(128)(2,1)}, u32[]{:S(2)}) copy-start(bf16[96]{0:T(256)(128)(2,1)} %param.19) | copy-start | bytes 580
  474.1 38.6 %collective-permute-start.21 = (bf16[4608,128]{1,0:T(8,128)(2,1)}, bf16[4608,128]{1,0:T(8,128)(2,1)}, u32[]{:S(2)}, u32[]{:S(2)}) collective-permute-start(bf16[4608,128]{1,0:T(8,128)(2,1)} %collective-permute-done.18.refs_2_), channel_id=1, source_target_pairs={{0,48},{16,32},{32,16},{48,0},{64,112},{80,96},{96,80},{112,64},{1... | collective-permute-start | bytes 3538952 | tf_op jit(solution)/shard_map/ppermute | solution.py:1103
  477.1 44.3 %all-to-all-start.8 = ((bf16[8,736,128]{2,1,0:T(8,128)(2,1)}), bf16[8,736,128]{2,1,0:T(8,128)(2,1)S(1)}, u32[]{:S(2)}, u32[]{:S(2)}) async-start(bf16[8,736,128]{2,1,0:T(8,128)(2,1)} %broadcast_in_dim.31), calls=%async_computation.8 | async-start | bytes 3014656 | tf_op jit(solution)/shard_map/all_to_all | solution.py:1001
  484.1 18.9 %collective-permute-start.13 = (bf16[128,1536]{1,0:T(8,128)(2,1)}, bf16[128,1536]{1,0:T(8,128)(2,1)S(1)}, u32[]{:S(2)}, u32[]{:S(2)}) collective-permute-start(bf16[128,1536]{1,0:T(8,128)(2,1)} %fusion.5), channel_id=1, source_target_pairs={{0,2},{1,3},{2,0},{3,1},{4,6},{5,7},{6,4},{7,5},{8,10},{9,11},{10,... | collective-permute-start | bytes 1179656 | tf_op jit(solution)/shard_map/ppermute | solution.py:1170
  512.6 8.8 %copy-start.41 = (bf16[96,512]{1,0:T(8,128)(2,1)S(1)}, bf16[96,512]{1,0:T(8,128)(2,1)}, u32[]{:S(2)}) copy-start(bf16[96,512]{1,0:T(8,128)(2,1)} %wv_ref.1) | copy-start | bytes 294916
  (44 other events, 146.6 us)
Sparse Core Ops, SparseCore 0:
  12.2 79.9 all-gather.3
  94.5 52.5 all-gather.7
  149.3 42.9 all-gather.5

commit v11 on v10

--- a/solution.py
+++ b/solution.py
@@ -1118,7 +1118,10 @@
         axis=1,
     )
 
-    grad_two = after(grad_two, p0, extra)
+    out_part = expert_output(
+        exp_s, after(act, p0), slot_gate, place, shared_act, expert_down, shared_two
+    )
+    grad_two = after(grad_two, extra, out_part)
     grad_middle, grad_attn, grad_heads, gain_rows = middle_back(
         grad_two, middle, cotangent[0], gain_ffn, w_all
     )
@@ -1141,39 +1144,38 @@
     )
     got_11, got_30 = to(add_b, 1), to(add_a, 3)
 
-    got_11, got_30 = after((got_11, got_30), far)
-    own_part, side = piece_sums(side_kernel, (f32, bf16), part_0, part_1, got_11, got_30)
-    across = to(side, 4)
-
-    shares = merge_shares(ctx_s, near, after(far, side))
-    got = swap_all(shares, "ctx", y_groups)
-    own = (own_part + after(across, shares).astype(f32)).astype(bf16)
-    at_1, at_3, at_z = to(own, 1), to(own, 3), to(own, 4)
-
-    out_part = expert_output(
-        exp_s, after(act, side), slot_gate, place, shared_act, expert_down, shared_two
-    )
+    def from_x(rows, k):
+        moved = lax.ppermute(rows, "exp", [(i, i ^ (4 * k)) for i in range(N_EXP)])
+        return moved.astype(f32)
+
     out_sums = spread_sums(
         exp_s,
         out_part,
         lax.ppermute(out_part[0, :4], "exp", core_swap),
         lax.ppermute(out_part[0, 4:], "exp", core_swap),
     )
-    columns, grad_kv, grad_down = column_grads(got, after(hidden_seq, own), att_seq)
-    grad_kv = swap_all(grad_kv, "ctx")
-    columns = after(columns, grad_kv, at_1, at_3, out_sums[0])
-    owned = swap_all(columns, "exp")
-    out_rows = out_sums[0].astype(f32)
-    for k in range(1, 4):
-        moved = lax.ppermute(out_sums[k], "exp", [(i, i ^ (4 * k)) for i in range(N_EXP)])
-        out_rows = out_rows + moved.astype(f32)
+    out_rows = out_sums[0].astype(f32) + from_x(out_sums[1], 1) + from_x(out_sums[3], 3)
+    got_11, got_30 = after((got_11, got_30), far, out_rows)
+    own_part, side = piece_sums(side_kernel, (f32, bf16), part_0, part_1, got_11, got_30)
+    across = to(side, 4)
+    out_rows = out_rows + from_x(after(out_sums[2], side), 2)
     out_across = lax.ppermute(
         out_rows[1].astype(bf16), "exp", [(i, i ^ 2) for i in range(N_EXP)]
     )
+
+    shares = merge_shares(ctx_s, near, after(far, side))
+    got = swap_all(shares, "ctx", y_groups)
+    own = (own_part + after(across, shares).astype(f32)).astype(bf16)
+    at_1, at_3, at_z = to(own, 1), to(own, 3), to(own, 4)
+
+    columns, grad_kv, grad_down = column_grads(got, after(hidden_seq, own, out_rows), att_seq)
+    grad_kv = swap_all(grad_kv, "ctx")
+    columns = after(columns, grad_kv, at_1, at_3, out_across)
+    owned = swap_all(columns, "exp")
     input_grad = input_back(grad_query, grad_kv, w_all, tokens[0], gain_attn, grad_middle)
     owned, gain_sum = owned_sums(owned, grad_down)
     owned, at_z1, at_z3 = lax.optimization_barrier(
-        (after(owned, out_rows, input_grad), to(at_z, 1), to(at_z, 3))
+        (after(owned, input_grad), to(at_z, 1), to(at_z, 3))
     )
     at_2, at_z2 = to(at_3, 1), to(at_z1, 3)
     mixed = (middle + out_rows[0] + out_across.astype(f32)).astype(bf16)[None]

time: 541 us -> 539 us (level)
  local copies, waits for them, and re-layouts: 59.8 us -> 47.7 us
    ppermute x12, waiting for transfers between devices: 30.4 us -> 66.4 us  [to(): return lax.ppermute(rows, 'ctx', [(i, i ^ k) for i in range(N_CTX)])]
    ppermute x3, waiting for transfers between devices: 41.8 us -> 13.3 us  [from_x(): moved = lax.ppermute(rows, 'exp', [(i, i ^ 4 * k) for i in range(N_EXP)])]
    unnamed x126 -> x122, local copies, waits for them, and re-layouts: 38.1 us -> 29.6 us
    ppermute x1, waiting for transfers between devices: 6.64 us -> 0.01 us  [on_device(): far = lax.ppermute(far, 'ctx', z_swap)]
  transfers between devices with their start and end apart: 34 -> 34, of which waited for: 23 -> 22; matrix products, arithmetic and copies ran while one was open for 8% -> 7% of each run, Pallas kernels for 21% -> 22%
where the time goes in v11:
time: 539 us; the launch traced here: 530 us
  waiting for transfers between devices  219 us (41%)
  Pallas kernels  146 us (27%)
  starting transfers between devices  79.7 us (15%)
  local copies, waits for them, and re-layouts  47.7 us (9%)
  between operations  14.9 us (3%)
  other arithmetic  13 us (2%)
  matrix products  8.71 us (2%)
    all_to_all x9, waiting for transfers between devices, swap_all(): lax.all_to_all(rows, axis, split_axis=0, concat_axis=0, tiled=True, axis_...  69.8 us
    ppermute x12, waiting for transfers between devices, to(): return lax.ppermute(rows, 'ctx', [(i, i ^ k) for i in range(N_CTX)])  66.4 us
    all_to_all x9, starting transfers between devices, swap_all(): lax.all_to_all(rows, axis, split_axis=0, concat_axis=0, tiled=True, axis_...  43.5 us
    unnamed x122, local copies, waits for them, and re-layouts  29.6 us
    pallas_call x1, Pallas kernels, expert_back(): pl.pallas_call(expert_kernel, grid_spec=pltpu.PrefetchScalarGridSpec(num_...  29 us
    ppermute x2, waiting for transfers between devices, of_sequence(): other = lax.ppermute(rows, 'ctx', z_swap)  26.3 us
    pallas_call x2, Pallas kernels, expert_weights(): pl.pallas_call(lambda *refs: expert_weights_kernel(halved, *refs), grid_s...  22 us
    ppermute x1, waiting for transfers between devices, on_device(): lax.ppermute(out_rows[1].astype(bf16), 'exp', [(i, i ^ 2) for i in range(...  19.5 us
  transfers between devices with their start and end apart: 34, of which 22 were waited for; matrix products, arithmetic and copies ran while one was open for 7% of the time, Pallas kernels for 22%

profile of v11, /device:TPU:0, one launch (start us, length us, event | category | flops | bytes accessed | tf_op | source)
XLA Modules:
  0.0 529.5 jit_solution(7009042171148662750)
XLA Ops:
  13.3 4.1 collective-permute-start
  18.0 4.8 all-to-all-start
  22.9 6.1 %collective-permute-done = bf16[1,128,1536]{2,1,0:T(8,128)(2,1)S(1)} collective-permute-done((bf16[1,128,1536]{2,1,0:T(8,128)(2,1)S(1)}, bf16[1,128,1536]{2,1,0:T(8,128)(2,1)S(1)}, u32[]{:S(2)}, u32[]{:S(2)}) %collective-permute-start) | collective-permute-done | bytes 393248 | tf_op jit(solution)/shard_map/ppermute | solution.py:1053
  31.7 4.6 all-to-all-start.1
  43.9 30.5 %all-to-all-done.1 = bf16[4,2,128,1536]{3,2,1,0:T(8,128)(2,1)S(1)} async-done(((bf16[4,2,128,1536]{3,2,1,0:T(8,128)(2,1)}), bf16[4,2,128,1536]{3,2,1,0:T(8,128)(2,1)S(1)}, u32[]{:S(2)}, u32[]{:S(2)}) %all-to-all-start.1) | async-done | bytes 3145760 | tf_op jit(solution)/shard_map/all_to_all | solution.py:1001
  76.0 5.2 all-to-all-start.2
  86.0 4.5 all-to-all-done.2
  93.2 7.7 %project.1 = (bf16[128,1536]{1,0:T(8,128)(2,1)S(1)}, bf16[8,128,1024]{2,1,0:T(8,128)(2,1)S(1)}) custom-call(bf16[1,128,1536]{2,1,0:T(8,128)(2,1)S(1)} %copy-done.17, bf16[8,128,1536]{2,1,0:T(8,128)(2,1)S(1)} %norm_rows.3.seq_ref.hidden_ref, bf16[1536,4096]{1,0:T(8,128)(2,1)} %all-gather.4.cloned.1.call-done.w_ref.wq_ref.wkv_ref), custom_call_target="tpu_custom_call" | custom-call | bytes 29520000 | tf_op jit(solution)/shard_map/project/pallas_call | solution.py:798
  100.9 5.8 %attend.1 = (bf16[128,1536]{1,0:T(8,128)(2,1)S(1)}, f32[128,1536]{1,0:T(8,128)S(1)}, f32[1536,128]{1,0:T(8,128)S(1)}) custom-call(s32[1]{0:T(128)} %bitcast.ctx_ref.refs_0_, bf16[128,1536]{1,0:T(8,128)(2,1)S(1)} %get-tuple-element.104.q_ref, bf16[8,128,1024]{2,1,0:T(8,128)(2,1)S(1)} %get-tuple-element.105.k_ref.v_ref, ...), custom_call_target="tpu_custom_call" | custom-call | bytes 22140000 | tf_op jit(solution)/shard_map/attend/pallas_call | solution.py:99
  106.7 5.4 %copy-done = bf16[1536,4096]{1,0:T(8,128)(2,1)S(1)} copy-done((bf16[1536,4096]{1,0:T(8,128)(2,1)S(1)}, bf16[1536,4096]{1,0:T(8,128)(2,1)}, u32[]{:S(2)}) %copy-start) | copy-done | bytes 12582936
  115.4 20.1 %collective-permute-done.1 = bf16[1,128,1536]{2,1,0:T(8,128)(2,1)S(1)} collective-permute-done((bf16[1,128,1536]{2,1,0:T(8,128)(2,1)S(1)}, bf16[1,128,1536]{2,1,0:T(8,128)(2,1)S(1)}, u32[]{:S(2)}, u32[]{:S(2)}) %collective-permute-start.1) | collective-permute-done | bytes 393248 | tf_op jit(solution)/shard_map/ppermute | solution.py:1053
  137.6 4.8 all-to-all-start.3
  142.5 4.6 all-gather.8.cloned.1.call-done
  147.0 13.7 %place_rows.1 = (bf16[8,2,128,128]{3,2,1,0:T(8,128)(2,1)}, bf16[2,2,384,1536]{3,2,1,0:T(8,128)(2,1)}, f32[2,2,384,512]{3,2,1,0:T(8,128)}, f32[8,2,128,128]{3,2,1,0:T(8,128)}, f32[2,2,384,128]{3,2,1,0:T(8,128)}) custom-call(s32[1]{0:T(128)} %bitcast.7.at_ref, bf16[8,2,128,1664]{3,2,1,0:T(8,128)(2,1)} %bitcast.84, bf16[2,512,1536]{2,1,0:T(8,128)(2,1)} %wd_ref.1, ...), custom_call_target="tpu_custom_call" | custom-call | bytes 51660000 | tf_op jit(solution)/shard_map/place_rows/pallas_call | solution.py:368
  160.7 19.3 %all-to-all-done.3 = bf16[4,2,128,1536]{3,2,1,0:T(8,128)(2,1)} async-done(((bf16[4,2,128,1536]{3,2,1,0:T(8,128)(2,1)}), bf16[4,2,128,1536]{3,2,1,0:T(8,128)(2,1)}, u32[]{:S(2)}, u32[]{:S(2)}) %all-to-all-start.3) | async-done | bytes 3145760 | tf_op jit(solution)/shard_map/all_to_all | solution.py:1001
  180.0 12.4 %all-gather.6.cloned.1.call-done = bf16[2048,1536]{1,0:T(8,128)(2,1)} async-done(((bf16[128,1536]{1,0:T(8,128)(2,1)}), bf16[2048,1536]{1,0:T(8,128)(2,1)}) %all-gather.6.cloned.1.call-update) | async-done | bytes 6291472 | tf_op jit(solution)/shard_map/all_gather | solution.py:1076
  192.4 29.0 %expert_back.1 = (bf16[2,8,128,1536]{3,2,1,0:T(8,128)(2,1)}, bf16[2,2,384,1536]{3,2,1,0:T(8,128)(2,1)}, bf16[2,2,384,512]{3,2,1,0:T(8,128)(2,1)}, bf16[2,2,384,1...) custom-call(s32[1]{0:T(128)} %bitcast.7.at_ref, ...), custom_call_target="tpu_custom_call" | custom-call | bytes 103320000 | tf_op jit(solution)/shard_map/expert_back/pallas_call | solution.py:447
  223.9 5.4 %collective-permute-done.2 = bf16[8,128,1536]{2,1,0:T(8,128)(2,1)S(1)} collective-permute-done((bf16[8,128,1536]{2,1,0:T(8,128)(2,1)S(1)}, bf16[8,128,1536]{2,1,0:T(8,128)(2,1)S(1)}, u32[]{:S(2)}, u32[]{:S(2)}) %collective-permute-start.2) | collective-permute-done | bytes 3145760 | tf_op jit(solution)/shard_map/ppermute | solution.py:1088
  232.0 4.8 all-to-all-start.4
  236.8 10.9 %expert_weights.2 = (bf16[9216,128]{1,0:T(8,128)(2,1)}, bf16[9216,128]{1,0:T(8,128)(2,1)}) custom-call(s32[1]{0:T(128)} %bitcast.ctx_ref.refs_0_, bf16[2,768,1536]{2,1,0:T(8,128)(2,1)} %bitcast.91, bf16[2,768,1536]{2,1,0:T(8,128)(2,1)} %bitcast.89, bf16[2,768,512]{2,1,0:T(8,128)(2,1)} %bitcast.74, bf16[2,768,1024]{2,1,0:T(8,128)(2,1)} %bitcast.85, ...), custom_call_target="tpu_custom_call" | custom-call | bytes 7380000 | tf_op jit(solution)/shard_map/expert_weights/pallas_call | solution.py:898
  249.3 11.1 %expert_weights.3 = (bf16[4608,128]{1,0:T(8,128)(2,1)}, bf16[4608,128]{1,0:T(8,128)(2,1)}, bf16[4608,128]{1,0:T(8,128)(2,1)}, bf16[4608,128]{1,0:T(8,128)(2,1)}) custom-call(s32[1]{0:T(128)} %bitcast.ctx_ref.refs_0_, bf16[2,768,1536]{2,1,0:T(8,128)(2,1)} %bitcast.92, bf16[2,768,1536]{2,1,0:T(8,128)(2,1)} %bitcast.90, bf16[2,768,512]{2,1,0:T(8,128)(2,1)} %bitcast.75, ...), custom_call_target="tpu_custom_call" | custom-call | bytes 7380000 | tf_op jit(solution)/shard_map/expert_weights/pallas_call | solution.py:898
  262.5 9.8 %expert_output.1.own_ref = bf16[2,8,128,1536]{3,2,1,0:T(8,128)(2,1)} custom-call(s32[1]{0:T(128)} %bitcast.7.at_ref, bf16[2,2,384,512]{3,2,1,0:T(8,128)(2,1)S(1)} %copy-done.3, f32[2,2,384,128]{3,2,1,0:T(8,128)S(1)} %copy-done.35, bf16[8,2,128,128]{3,2,1,0:T(8,128)(2,1)S(1)} %copy-done.13, bf16[8,2,128,128]{3,2,1,0:T(8,128)(2,1)S(1)} %copy-done.7, ...), custom_call_target="tpu_custom_call" | custom-call | bytes 7380000 | tf_op jit(solution)/shard_map/expert_output/pallas_call | solution.py:499
  272.3 3.9 slice_bitcast_fusion.1
  276.7 4.6 convolution_convert_fusion
  281.6 4.1 fusion.8
  287.6 5.7 %middle_back.1 = (f32[128,1536]{1,0:T(8,128)S(1)}, bf16[128,1536]{1,0:T(8,128)(2,1)S(1)}, bf16[128,1536]{1,0:T(8,128)(2,1)S(1)}, f32[16,128]{1,0:T(8,128)S(1)}) custom-call(bf16[8,128,1536]{2,1,0:T(8,128)(2,1)} %all-to-all-done.4.pieces_ref, f32[128,1536]{1,0:T(8,128)S(1)} %get-tuple-element.107.middle_ref, bf16[128,1536]{1,0:T(8,128)(2,1)S(1)} %bitcast.81, ...), custom_call_target="tpu_custom_call" | custom-call | bytes 3690000 | tf_op jit(solution)/shard_map/middle_back/pallas_call | solution.py:290
  296.5 9.2 %attend_back.1 = (bf16[128,1536]{1,0:T(8,128)(2,1)S(1)}, bf16[4,1776,128]{2,1,0:T(8,128)(2,1)S(1)}, bf16[4,1776,128]{2,1,0:T(8,128)(2,1)}) custom-call(s32[1]{0:T(128)} %bitcast.ctx_ref.refs_0_, bf16[128,1536]{1,0:T(8,128)(2,1)S(1)} %copy-done.15, bf16[128,1536]{1,0:T(8,128)(2,1)S(1)} %get-tuple-element.139.ga_ref, f32[128,1536]{1,0:T(8,128)S(1)} %copy-done.32, ...), custom_call_target="tpu_custom_call" | custom-call | bytes 7380000 | tf_op jit(solution)/shard_map/attend_back/pallas_call | solution.py:202
  306.4 2.9 collective-permute-start.11
  309.4 5.9 %spread_sums.1 = (bf16[2,128,1536]{2,1,0:T(8,128)(2,1)S(1)}, bf16[2,128,1536]{2,1,0:T(8,128)(2,1)S(1)}, bf16[2,128,1536]{2,1,0:T(8,128)(2,1)S(1)}, bf16[2,128,1536]{2,1,0:T(8,128)(2,1)S(1)}) custom-call(s32[1]{0:T(128)} %bitcast.7.at_ref, bf16[2,8,128,1536]{3,2,1,0:T(8,128)(2,1)S(1)} %bitcast.73, bf16[4,128,1536]{2,1,0:T(8,128)(2,1)} %collective-permute-done.3.low_ref, ...), custom_call_target="tpu_custom_call" | custom-call | bytes 14760000 | tf_op jit(solution)/shard_map/spread_sums/pallas_call | solution.py:836
  319.5 3.5 piece_sums.2
  324.2 10.6 %collective-permute-done.5 = bf16[2,128,1536]{2,1,0:T(8,128)(2,1)S(1)} collective-permute-done((bf16[2,128,1536]{2,1,0:T(8,128)(2,1)S(1)}, bf16[2,128,1536]{2,1,0:T(8,128)(2,1)S(1)}, u32[]{:S(2)}, u32[]{:S(2)}) %collective-permute-start.5) | collective-permute-done | bytes 786464 | tf_op jit(solution)/shard_map/ppermute | solution.py:1148
  334.8 2.7 collective-permute-done.6
  338.9 12.4 %collective-permute-done.10.got_30 = bf16[4608,128]{1,0:T(8,128)(2,1)S(1)} collective-permute-done((bf16[4608,128]{1,0:T(8,128)(2,1)S(1)}, bf16[4608,128]{1,0:T(8,128)(2,1)S(1)}, u32[]{:S(2)}, u32[]{:S(2)}) %collective-permute-start.10) | collective-permute-done | bytes 1179680 | tf_op jit(solution)/shard_map/ppermute | solution.py:1103
  356.5 3.5 collective-permute-start.12
  360.0 4.5 all-to-all-start.5
  364.5 16.2 %collective-permute-done.14 = bf16[4608,128]{1,0:T(8,128)(2,1)S(1)} collective-permute-done((bf16[4608,128]{1,0:T(8,128)(2,1)S(1)}, bf16[4608,128]{1,0:T(8,128)(2,1)S(1)}, u32[]{:S(2)}, u32[]{:S(2)}) %collective-permute-start.14) | collective-permute-done | bytes 1179680 | tf_op jit(solution)/shard_map/ppermute | solution.py:1103
  390.2 3.5 all-to-all-done.5.got_ref
  393.7 7.1 %column_grads.1 = (bf16[16,112,512]{2,1,0:T(8,128)(2,1)}, bf16[8,128,128]{2,1,0:T(8,128)(2,1)}, bf16[96,128]{1,0:T(8,128)(2,1)}) custom-call(bf16[4,2160,128]{2,1,0:T(8,128)(2,1)} %all-to-all-done.5.got_ref, bf16[8,128,1536]{2,1,0:T(8,128)(2,1)} %copy-done.2, bf16[8,128,1536]{2,1,0:T(8,128)(2,1)} %bitcast.10.att_ref), custom_call_target="tpu_custom_call" | custom-call | bytes 29520000 | tf_op jit(solution)/shard_map/column_grads/pallas_call | solution.py:614
  400.7 3.4 all-to-all-start.6
  404.1 19.5 %collective-permute-done.13 = bf16[128,1536]{1,0:T(8,128)(2,1)S(1)} collective-permute-done((bf16[128,1536]{1,0:T(8,128)(2,1)}, bf16[128,1536]{1,0:T(8,128)(2,1)S(1)}, u32[]{:S(2)}, u32[]{:S(2)}) %collective-permute-start.13) | collective-permute-done | bytes 393248 | tf_op jit(solution)/shard_map/ppermute | solution.py:1162
  425.5 5.7 %all-to-all-start.7 = ((bf16[16,112,512]{2,1,0:T(8,128)(2,1)}), bf16[16,112,512]{2,1,0:T(8,128)(2,1)S(1)}, u32[]{:S(2)}, u32[]{:S(2)}) async-start(bf16[16,112,512]{2,1,0:T(8,128)(2,1)} %get-tuple-element.164), calls=%async_computation.7 | async-start | bytes 3670016 | tf_op jit(solution)/shard_map/all_to_all | solution.py:1001
  437.7 6.9 %input_back.1 = bf16[128,1536]{1,0:T(8,128)(2,1)} custom-call(bf16[128,1536]{1,0:T(8,128)(2,1)S(1)} %copy-done.39, bf16[8,128,128]{2,1,0:T(8,128)(2,1)S(1)} %copy-done.28, bf16[1536,4096]{1,0:T(8,128)(2,1)} %all-gather.4.cloned.1.call-done.w_ref.wq_ref.wkv_ref, bf16[1536,4096]{1,0:T(8,128)(2,1)} %all-gather.4.cloned.1.call-done.w_ref.wq_ref.wkv_ref, ...), custom_call_target="tpu_custom_call" | custom-call | bytes 25830000 | tf_op jit(solution)/shard_map/input_back/pallas_call | solution.py:742
  444.6 11.4 %all-to-all-done.7.got_ref = bf16[16,112,512]{2,1,0:T(8,128)(2,1)S(1)} async-done(((bf16[16,112,512]{2,1,0:T(8,128)(2,1)}), bf16[16,112,512]{2,1,0:T(8,128)(2,1)S(1)}, u32[]{:S(2)}, u32[]{:S(2)}) %all-to-all-start.7) | async-done | bytes 1835040 | tf_op jit(solution)/shard_map/all_to_all | solution.py:1001
  456.3 3.5 collective-permute-done.18.refs_2_
  463.4 5.7 %all-to-all-start.8 = ((bf16[8,736,128]{2,1,0:T(8,128)(2,1)}), bf16[8,736,128]{2,1,0:T(8,128)(2,1)S(1)}, u32[]{:S(2)}, u32[]{:S(2)}) async-start(bf16[8,736,128]{2,1,0:T(8,128)(2,1)} %broadcast_in_dim.31), calls=%async_computation.8 | async-start | bytes 3014656 | tf_op jit(solution)/shard_map/all_to_all | solution.py:1001
  475.6 5.5 %unpack_experts.2 = (f32[2,1536,512]{2,1,0:T(8,128)}, f32[2,1536,512]{2,1,0:T(8,128)}, f32[2,512,1536]{2,1,0:T(8,128)}) custom-call(s32[1]{0:T(128)} %bitcast.ctx_ref.refs_0_, bf16[4608,128]{1,0:T(8,128)(2,1)S(1)} %add_convert_fusion.refs_1_, bf16[4608,128]{1,0:T(8,128)(2,1)S(1)} %copy-done.25, bf16[4608,128]{1,0:T(8,128)(2,1)} %collective-permute-done.16.refs_3_, ...), custom_call_target="tpu_custom_call" | custom-call | bytes 29520000 | tf_op jit(solution)/shard_map/unpack_experts/pallas_call | solution.py:942
  481.7 30.8 %collective-permute-done.20.refs_1_ = bf16[4608,128]{1,0:T(8,128)(2,1)} collective-permute-done((bf16[4608,128]{1,0:T(8,128)(2,1)}, bf16[4608,128]{1,0:T(8,128)(2,1)}, u32[]{:S(2)}, u32[]{:S(2)}) %collective-permute-start.20) | collective-permute-done | bytes 1179680 | tf_op jit(solution)/shard_map/ppermute | solution.py:1103
  513.7 6.4 %unpack_experts.3 = (f32[2,1536,512]{2,1,0:T(8,128)}, f32[2,1536,512]{2,1,0:T(8,128)}, f32[2,512,1536]{2,1,0:T(8,128)}) custom-call(s32[1]{0:T(128)} %bitcast.ctx_ref.refs_0_, bf16[4608,128]{1,0:T(8,128)(2,1)} %collective-permute-done.20.refs_1_, ...), custom_call_target="tpu_custom_call", output_to_operand_aliasing={{0}: (5, {}), {1}: (6, {}), {2}: (7, {})} | custom-call | bytes 29520000 | tf_op jit(solution)/shard_map/unpack_experts/pallas_call | solution.py:942
  (204 shorter events, 91.1 us)
Async XLA Ops:
  7.2 85.0 %all-gather.4.cloned.1.call-start = ((), (), s32[]{:S(2)}) async-start(), calls=%async_computation.9 | async-start | bytes 13369344 | tf_op jit(solution)/shard_map/all_gather | solution.py:1039
  12.0 135.0 %all-gather.8.cloned.1.call-start = ((), (), s32[]{:S(2)}) async-start(), calls=%async_computation.11 | async-start | bytes 7241728 | tf_op jit(solution)/shard_map/all_gather | solution.py:1046
  13.3 15.8 %collective-permute-start = (bf16[1,128,1536]{2,1,0:T(8,128)(2,1)S(1)}, bf16[1,128,1536]{2,1,0:T(8,128)(2,1)S(1)}, u32[]{:S(2)}, u32[]{:S(2)}) collective-permute-start(bf16[1,128,1536]{2,1,0:T(8,128)(2,1)S(1)} %copy-done.6), channel_id=1, source_target_pairs={{0,64},{16,80},{32,96},{48,112},{64,0},{80,16},{96,32},{112,48},{1... | collective-permute-start | bytes 1179656 | tf_op jit(solution)/shard_map/ppermute | solution.py:1053
  18.0 11.7 %all-to-all-start = ((bf16[16,1,192]{2,1,0:T(2,128)(2,1)}), bf16[16,1,192]{2,1,0:T(2,128)(2,1)S(1)}, u32[]{:S(2)}, u32[]{:S(2)}) async-start(bf16[16,1,192]{2,1,0:T(2,128)(2,1)} %broadcast_in_dim.24), calls=%async_computation | async-start | bytes 32768 | tf_op jit(solution)/shard_map/all_to_all | solution.py:1001
  31.7 42.6 %all-to-all-start.1 = ((bf16[4,2,128,1536]{3,2,1,0:T(8,128)(2,1)}), bf16[4,2,128,1536]{3,2,1,0:T(8,128)(2,1)S(1)}, u32[]{:S(2)}, u32[]{:S(2)}) async-start(bf16[4,2,128,1536]{3,2,1,0:T(8,128)(2,1)} %broadcast_in_dim.25), calls=%async_computation.1 | async-start | bytes 6291456 | tf_op jit(solution)/shard_map/all_to_all | solution.py:1001
  76.0 14.5 %all-to-all-start.2 = ((bf16[16,96,128]{2,1,0:T(8,128)(2,1)}), bf16[16,96,128]{2,1,0:T(8,128)(2,1)}, u32[]{:S(2)}, u32[]{:S(2)}) async-start(bf16[16,96,128]{2,1,0:T(8,128)(2,1)} %copy.62), calls=%async_computation.2 | async-start | bytes 786432 | tf_op jit(solution)/shard_map/all_to_all | solution.py:1001
  81.2 111.2 %all-gather.6.cloned.1.call-start = ((), (), s32[]{:S(2)}) async-start(), calls=%async_computation.10 | async-start | bytes 6684672 | tf_op jit(solution)/shard_map/all_gather | solution.py:1076
  86.0 14.9 %copy-start.2 = (bf16[8,128,1536]{2,1,0:T(8,128)(2,1)}, bf16[8,128,1536]{2,1,0:T(8,128)(2,1)S(1)}, u32[]{:S(2)}) copy-start(bf16[8,128,1536]{2,1,0:T(8,128)(2,1)S(1)} %norm_rows.3.seq_ref.hidden_ref) | copy-start | bytes 9437188
  113.8 172.8 %copy-start.8 = (f32[128,1536]{1,0:T(8,128)}, f32[128,1536]{1,0:T(8,128)S(1)}, u32[]{:S(2)}) copy-start(f32[128,1536]{1,0:T(8,128)S(1)} %get-tuple-element.107.middle_ref) | copy-start | bytes 2359300
  113.8 21.7 %collective-permute-start.1 = (bf16[1,128,1536]{2,1,0:T(8,128)(2,1)S(1)}, bf16[1,128,1536]{2,1,0:T(8,128)(2,1)S(1)}, u32[]{:S(2)}, u32[]{:S(2)}) collective-permute-start(bf16[1,128,1536]{2,1,0:T(8,128)(2,1)S(1)} %bitcast.82), channel_id=1, source_target_pairs={{0,64},{16,80},{32,96},{48,112},{64,0},{80,16},{96,32},{112,48},{1... | collective-permute-start | bytes 1179656 | tf_op jit(solution)/shard_map/ppermute | solution.py:1053
  137.6 42.4 %all-to-all-start.3 = ((bf16[4,2,128,1536]{3,2,1,0:T(8,128)(2,1)}), bf16[4,2,128,1536]{3,2,1,0:T(8,128)(2,1)}, u32[]{:S(2)}, u32[]{:S(2)}) async-start(bf16[4,2,128,1536]{3,2,1,0:T(8,128)(2,1)} %broadcast_in_dim.27), calls=%async_computation.3 | async-start | bytes 6291456 | tf_op jit(solution)/shard_map/all_to_all | solution.py:1001
  223.6 5.7 %collective-permute-start.2 = (bf16[8,128,1536]{2,1,0:T(8,128)(2,1)S(1)}, bf16[8,128,1536]{2,1,0:T(8,128)(2,1)S(1)}, u32[]{:S(2)}, u32[]{:S(2)}) collective-permute-start(bf16[8,128,1536]{2,1,0:T(8,128)(2,1)S(1)} %slice_bitcast_fusion), channel_id=1, source_target_pairs={{0,1},{1,0},{2,3},{3,2},{4,5},{5,4},{6,7},{7,6},{8,9},{9,8},{10,11... | collective-permute-start | bytes 9437192 | tf_op jit(solution)/shard_map/ppermute | solution.py:1088
  232.0 54.6 %all-to-all-start.4 = ((bf16[8,128,1536]{2,1,0:T(8,128)(2,1)}), bf16[8,128,1536]{2,1,0:T(8,128)(2,1)}, u32[]{:S(2)}, u32[]{:S(2)}) async-start(bf16[8,128,1536]{2,1,0:T(8,128)(2,1)} %fusion), calls=%async_computation.4 | async-start | bytes 6291456 | tf_op jit(solution)/shard_map/all_to_all | solution.py:1001
  247.7 14.8 %copy-start.3 = (bf16[2,2,384,512]{3,2,1,0:T(8,128)(2,1)S(1)}, bf16[2,2,384,512]{3,2,1,0:T(8,128)(2,1)}, u32[]{:S(2)}) copy-start(bf16[2,2,384,512]{3,2,1,0:T(8,128)(2,1)} %get-tuple-element.124.act_ref) | copy-start | bytes 4718596
  247.7 14.8 %copy-start.7 = (bf16[8,2,128,128]{3,2,1,0:T(8,128)(2,1)S(1)}, bf16[8,2,128,128]{3,2,1,0:T(8,128)(2,1)}, u32[]{:S(2)}) copy-start(bf16[8,2,128,128]{3,2,1,0:T(8,128)(2,1)} %get-tuple-element.137.sact_ref) | copy-start | bytes 1572868
  247.7 14.8 %copy-start.11 = (bf16[128,1536]{1,0:T(8,128)(2,1)S(1)}, bf16[128,1536]{1,0:T(8,128)(2,1)}, u32[]{:S(2)}) copy-start(bf16[128,1536]{1,0:T(8,128)(2,1)} %copy-done.10) | copy-start | bytes 1179652
  247.7 14.8 %copy-start.13 = (bf16[8,2,128,128]{3,2,1,0:T(8,128)(2,1)S(1)}, bf16[8,2,128,128]{3,2,1,0:T(8,128)(2,1)}, u32[]{:S(2)}) copy-start(bf16[8,2,128,128]{3,2,1,0:T(8,128)(2,1)} %get-tuple-element.112.place_ref) | copy-start | bytes 1572868
  247.7 14.8 %copy-start.35 = (f32[2,2,384,128]{3,2,1,0:T(8,128)S(1)}, f32[2,2,384,128]{3,2,1,0:T(8,128)}, u32[]{:S(2)}) copy-start(f32[2,2,384,128]{3,2,1,0:T(8,128)} %get-tuple-element.125.gate_ref) | copy-start | bytes 2359300
  247.7 71.7 %collective-permute-start.7 = (bf16[9216,128]{1,0:T(8,128)(2,1)}, bf16[9216,128]{1,0:T(8,128)(2,1)}, u32[]{:S(2)}, u32[]{:S(2)}) collective-permute-start(bf16[9216,128]{1,0:T(8,128)(2,1)} %get-tuple-element.121), channel_id=1, source_target_pairs={{0,16},{16,0},{32,48},{48,32},{64,80},{80,64},{96,112},{112,96},{1... | collective-permute-start | bytes 7077896 | tf_op jit(solution)/shard_map/ppermute | solution.py:1103
  260.4 59.1 %collective-permute-start.8 = (bf16[9216,128]{1,0:T(8,128)(2,1)}, bf16[9216,128]{1,0:T(8,128)(2,1)}, u32[]{:S(2)}, u32[]{:S(2)}) collective-permute-start(bf16[9216,128]{1,0:T(8,128)(2,1)} %get-tuple-element.134), channel_id=1, source_target_pairs={{0,48},{16,32},{32,16},{48,0},{64,112},{80,96},{96,80},{112,64},{1... | collective-permute-start | bytes 7077896 | tf_op jit(solution)/shard_map/ppermute | solution.py:1103
  276.2 33.2 %collective-permute-start.3 = (bf16[4,128,1536]{2,1,0:T(8,128)(2,1)}, bf16[4,128,1536]{2,1,0:T(8,128)(2,1)}, u32[]{:S(2)}, u32[]{:S(2)}) collective-permute-start(bf16[4,128,1536]{2,1,0:T(8,128)(2,1)} %get-tuple-element.191), channel_id=1, source_target_pairs={{0,1},{1,0},{2,3},{3,2},{4,5},{5,4},{6,7},{7,6},{8,9},{9,8},{10,11... | collective-permute-start | bytes 4718600 | tf_op jit(solution)/shard_map/ppermute | solution.py:1154
  276.2 33.2 %collective-permute-start.4 = (bf16[4,128,1536]{2,1,0:T(8,128)(2,1)}, bf16[4,128,1536]{2,1,0:T(8,128)(2,1)}, u32[]{:S(2)}, u32[]{:S(2)}) collective-permute-start(bf16[4,128,1536]{2,1,0:T(8,128)(2,1)} %get-tuple-element.190), channel_id=1, source_target_pairs={{0,1},{1,0},{2,3},{3,2},{4,5},{5,4},{6,7},{7,6},{8,9},{9,8},{10,11... | collective-permute-start | bytes 4718600 | tf_op jit(solution)/shard_map/ppermute | solution.py:1155
  285.7 23.7 %slice-start = ((s8[6291456]{0:T(1024)(128)(4,1)}), s8[2097152]{0:T(1024)(128)(4,1)S(1)}, s32[]{:S(2)}) async-start(s8[6291456]{0:T(1024)(128)(4,1)} %bitcast.72), calls=%async_computation.12 | async-start | bytes 4194304
  287.6 21.8 %slice-start.1 = ((s8[6291456]{0:T(1024)(128)(4,1)}), s8[4194304]{0:T(1024)(128)(4,1)S(1)}, s32[]{:S(2)}) async-start(s8[6291456]{0:T(1024)(128)(4,1)} %bitcast.72), calls=%async_computation.13 | async-start | bytes 8388608
  306.4 13.0 %copy-start.22 = (bf16[4608,128]{1,0:T(8,128)(2,1)S(1)}, bf16[4608,128]{1,0:T(8,128)(2,1)}, u32[]{:S(2)}) copy-start(bf16[4608,128]{1,0:T(8,128)(2,1)} %get-tuple-element.131.p1) | copy-start | bytes 3538948
  306.4 13.0 %copy-start.23 = (bf16[4608,128]{1,0:T(8,128)(2,1)S(1)}, bf16[4608,128]{1,0:T(8,128)(2,1)}, u32[]{:S(2)}) copy-start(bf16[4608,128]{1,0:T(8,128)(2,1)} %get-tuple-element.132.p3) | copy-start | bytes 3538948
  306.4 44.9 %collective-permute-start.11 = (bf16[4,1776,128]{2,1,0:T(8,128)(2,1)}, bf16[4,1776,128]{2,1,0:T(8,128)(2,1)S(1)}, u32[]{:S(2)}, u32[]{:S(2)}) collective-permute-start(bf16[4,1776,128]{2,1,0:T(8,128)(2,1)} %get-tuple-element.151), channel_id=1, source_target_pairs={{0,64},{16,80},{32,96},{48,112},{64,0},{80,16},{96,32},{112,48},{1... | collective-permute-start | bytes 5455880 | tf_op jit(solution)/shard_map/ppermute | solution.py:1131
  315.3 19.5 %collective-permute-start.5 = (bf16[2,128,1536]{2,1,0:T(8,128)(2,1)S(1)}, bf16[2,128,1536]{2,1,0:T(8,128)(2,1)S(1)}, u32[]{:S(2)}, u32[]{:S(2)}) collective-permute-start(bf16[2,128,1536]{2,1,0:T(8,128)(2,1)S(1)} %get-tuple-element.128), channel_id=1, source_target_pairs={{0,4},{1,5},{2,6},{3,7},{4,0},{5,1},{6,2},{7,3},{8,12},{9,13},{10,... | collective-permute-start | bytes 2359304 | tf_op jit(solution)/shard_map/ppermute | solution.py:1148
  317.4 20.1 %collective-permute-start.6 = (bf16[2,128,1536]{2,1,0:T(8,128)(2,1)S(1)}, bf16[2,128,1536]{2,1,0:T(8,128)(2,1)S(1)}, u32[]{:S(2)}, u32[]{:S(2)}) collective-permute-start(bf16[2,128,1536]{2,1,0:T(8,128)(2,1)S(1)} %get-tuple-element.129), channel_id=1, source_target_pairs={{0,12},{1,13},{2,14},{3,15},{4,8},{5,9},{6,10},{7,11},{8,4},{9,5},... | collective-permute-start | bytes 2359304 | tf_op jit(solution)/shard_map/ppermute | solution.py:1148
  323.0 28.3 %collective-permute-start.10 = (bf16[4608,128]{1,0:T(8,128)(2,1)S(1)}, bf16[4608,128]{1,0:T(8,128)(2,1)S(1)}, u32[]{:S(2)}, u32[]{:S(2)}) collective-permute-start(bf16[4608,128]{1,0:T(8,128)(2,1)S(1)} %get-tuple-element.150), channel_id=1, source_target_pairs={{0,48},{16,32},{32,16},{48,0},{64,112},{80,96},{96,80},{112,64},{1... | collective-permute-start | bytes 3538952 | tf_op jit(solution)/shard_map/ppermute | solution.py:1103
  324.2 27.1 %collective-permute-start.9 = (bf16[4608,128]{1,0:T(8,128)(2,1)S(1)}, bf16[4608,128]{1,0:T(8,128)(2,1)S(1)}, u32[]{:S(2)}, u32[]{:S(2)}) collective-permute-start(bf16[4608,128]{1,0:T(8,128)(2,1)S(1)} %get-tuple-element.149), channel_id=1, source_target_pairs={{0,16},{16,0},{32,48},{48,32},{64,80},{80,64},{96,112},{112,96},{1... | collective-permute-start | bytes 3538952 | tf_op jit(solution)/shard_map/ppermute | solution.py:1103
  353.1 27.6 %collective-permute-start.14 = (bf16[4608,128]{1,0:T(8,128)(2,1)S(1)}, bf16[4608,128]{1,0:T(8,128)(2,1)S(1)}, u32[]{:S(2)}, u32[]{:S(2)}) collective-permute-start(bf16[4608,128]{1,0:T(8,128)(2,1)S(1)} %get-tuple-element.154), channel_id=1, source_target_pairs={{0,64},{16,80},{32,96},{48,112},{64,0},{80,16},{96,32},{112,48},{1... | collective-permute-start | bytes 3538952 | tf_op jit(solution)/shard_map/ppermute | solution.py:1103
  356.5 28.4 %collective-permute-start.12 = (bf16[2,128,1536]{2,1,0:T(8,128)(2,1)S(1)}, bf16[2,128,1536]{2,1,0:T(8,128)(2,1)}, u32[]{:S(2)}, u32[]{:S(2)}) collective-permute-start(bf16[2,128,1536]{2,1,0:T(8,128)(2,1)S(1)} %get-tuple-element.155), channel_id=1, source_target_pairs={{0,8},{1,9},{2,10},{3,11},{4,12},{5,13},{6,14},{7,15},{8,0},{9,1},... | collective-permute-start | bytes 2359304 | tf_op jit(solution)/shard_map/ppermute | solution.py:1148
  360.0 33.6 %all-to-all-start.5 = ((bf16[4,2160,128]{2,1,0:T(8,128)(2,1)}), bf16[4,2160,128]{2,1,0:T(8,128)(2,1)}, u32[]{:S(2)}, u32[]{:S(2)}) async-start(bf16[4,2160,128]{2,1,0:T(8,128)(2,1)} %merge_shares.1), calls=%async_computation.5 | async-start | bytes 4423680 | tf_op jit(solution)/shard_map/all_to_all | solution.py:1001
  382.8 41.6 %collective-permute-start.15 = (bf16[4608,128]{1,0:T(8,128)(2,1)S(1)}, bf16[4608,128]{1,0:T(8,128)(2,1)S(1)}, u32[]{:S(2)}, u32[]{:S(2)}) collective-permute-start(bf16[4608,128]{1,0:T(8,128)(2,1)S(1)} %add_convert_fusion.refs_1_), channel_id=1, source_target_pairs={{0,16},{16,0},{32,48},{48,32},{64,80},{80,64},{96,112},{112,96},{1... | collective-permute-start | bytes 3538952 | tf_op jit(solution)/shard_map/ppermute | solution.py:1103
  382.9 42.6 %collective-permute-start.16 = (bf16[4608,128]{1,0:T(8,128)(2,1)S(1)}, bf16[4608,128]{1,0:T(8,128)(2,1)}, u32[]{:S(2)}, u32[]{:S(2)}) collective-permute-start(bf16[4608,128]{1,0:T(8,128)(2,1)S(1)} %add_convert_fusion.refs_1_), channel_id=1, source_target_pairs={{0,48},{16,32},{32,16},{48,0},{64,112},{80,96},{96,80},{112,64},{1... | collective-permute-start | bytes 3538952 | tf_op jit(solution)/shard_map/ppermute | solution.py:1103
  386.3 44.9 %collective-permute-start.17 = (bf16[4608,128]{1,0:T(8,128)(2,1)S(1)}, bf16[4608,128]{1,0:T(8,128)(2,1)}, u32[]{:S(2)}, u32[]{:S(2)}) collective-permute-start(bf16[4608,128]{1,0:T(8,128)(2,1)S(1)} %add_convert_fusion.refs_1_), channel_id=1, source_target_pairs={{0,64},{16,80},{32,96},{48,112},{64,0},{80,16},{96,32},{112,48},{1... | collective-permute-start | bytes 3538952 | tf_op jit(solution)/shard_map/ppermute | solution.py:1103
  388.8 34.8 %collective-permute-start.13 = (bf16[128,1536]{1,0:T(8,128)(2,1)}, bf16[128,1536]{1,0:T(8,128)(2,1)S(1)}, u32[]{:S(2)}, u32[]{:S(2)}) collective-permute-start(bf16[128,1536]{1,0:T(8,128)(2,1)} %fusion.5), channel_id=1, source_target_pairs={{0,2},{1,3},{2,0},{3,1},{4,6},{5,7},{6,4},{7,5},{8,10},{9,11},{10,... | collective-permute-start | bytes 1179656 | tf_op jit(solution)/shard_map/ppermute | solution.py:1162
  400.7 23.0 %all-to-all-start.6 = ((bf16[8,128,128]{2,1,0:T(8,128)(2,1)}), bf16[8,128,128]{2,1,0:T(8,128)(2,1)S(1)}, u32[]{:S(2)}, u32[]{:S(2)}) async-start(bf16[8,128,128]{2,1,0:T(8,128)(2,1)} %get-tuple-element.161), calls=%async_computation.6 | async-start | bytes 524288 | tf_op jit(solution)/shard_map/all_to_all | solution.py:1001
  425.5 30.6 %all-to-all-start.7 = ((bf16[16,112,512]{2,1,0:T(8,128)(2,1)}), bf16[16,112,512]{2,1,0:T(8,128)(2,1)S(1)}, u32[]{:S(2)}, u32[]{:S(2)}) async-start(bf16[16,112,512]{2,1,0:T(8,128)(2,1)} %get-tuple-element.164), calls=%async_computation.7 | async-start | bytes 3670016 | tf_op jit(solution)/shard_map/all_to_all | solution.py:1001
  431.2 28.7 %collective-permute-start.18 = (bf16[4608,128]{1,0:T(8,128)(2,1)}, bf16[4608,128]{1,0:T(8,128)(2,1)}, u32[]{:S(2)}, u32[]{:S(2)}) collective-permute-start(bf16[4608,128]{1,0:T(8,128)(2,1)} %collective-permute-done.17.refs_4_), channel_id=1, source_target_pairs={{0,16},{16,0},{32,48},{48,32},{64,80},{80,64},{96,112},{112,96},{1... | collective-permute-start | bytes 3538952 | tf_op jit(solution)/shard_map/ppermute | solution.py:1103
  432.3 29.8 %collective-permute-start.19 = (bf16[4608,128]{1,0:T(8,128)(2,1)}, bf16[4608,128]{1,0:T(8,128)(2,1)}, u32[]{:S(2)}, u32[]{:S(2)}) collective-permute-start(bf16[4608,128]{1,0:T(8,128)(2,1)} %collective-permute-done.17.refs_4_), channel_id=1, source_target_pairs={{0,48},{16,32},{32,16},{48,0},{64,112},{80,96},{96,80},{112,64},{1... | collective-permute-start | bytes 3538952 | tf_op jit(solution)/shard_map/ppermute | solution.py:1103
  437.7 18.3 %copy-start.40 = (bf16[96,128]{1,0:T(8,128)(2,1)S(1)}, bf16[96,128]{1,0:T(8,128)(2,1)}, u32[]{:S(2)}) copy-start(bf16[96,128]{1,0:T(8,128)(2,1)} %get-tuple-element.165.down_ref) | copy-start | bytes 73732
  456.3 16.9 %copy-start.53 = (bf16[96]{0:T(256)(128)(2,1)S(1)}, bf16[96]{0:T(256)(128)(2,1)}, u32[]{:S(2)}) copy-start(bf16[96]{0:T(256)(128)(2,1)} %param.19) | copy-start | bytes 580
  456.3 17.0 %copy-start.47 = (bf16[128,1536]{1,0:T(8,128)(2,1)S(1)}, bf16[128,1536]{1,0:T(8,128)(2,1)}, u32[]{:S(2)}) copy-start(bf16[128,1536]{1,0:T(8,128)(2,1)} %copy-done.46) | copy-start | bytes 1179652
  463.4 56.6 %all-to-all-start.8 = ((bf16[8,736,128]{2,1,0:T(8,128)(2,1)}), bf16[8,736,128]{2,1,0:T(8,128)(2,1)S(1)}, u32[]{:S(2)}, u32[]{:S(2)}) async-start(bf16[8,736,128]{2,1,0:T(8,128)(2,1)} %broadcast_in_dim.31), calls=%async_computation.8 | async-start | bytes 3014656 | tf_op jit(solution)/shard_map/all_to_all | solution.py:1001
  469.1 43.4 %collective-permute-start.20 = (bf16[4608,128]{1,0:T(8,128)(2,1)}, bf16[4608,128]{1,0:T(8,128)(2,1)}, u32[]{:S(2)}, u32[]{:S(2)}) collective-permute-start(bf16[4608,128]{1,0:T(8,128)(2,1)} %collective-permute-done.16.refs_3_), channel_id=1, source_target_pairs={{0,16},{16,0},{32,48},{48,32},{64,80},{80,64},{96,112},{112,96},{1... | collective-permute-start | bytes 3538952 | tf_op jit(solution)/shard_map/ppermute | solution.py:1103
  471.1 42.6 %collective-permute-start.21 = (bf16[4608,128]{1,0:T(8,128)(2,1)}, bf16[4608,128]{1,0:T(8,128)(2,1)}, u32[]{:S(2)}, u32[]{:S(2)}) collective-permute-start(bf16[4608,128]{1,0:T(8,128)(2,1)} %collective-permute-done.18.refs_2_), channel_id=1, source_target_pairs={{0,48},{16,32},{32,16},{48,0},{64,112},{80,96},{96,80},{112,64},{1... | collective-permute-start | bytes 3538952 | tf_op jit(solution)/shard_map/ppermute | solution.py:1103
  (42 other events, 194.3 us)
Sparse Core Ops, SparseCore 0:
  12.2 79.9 all-gather.3
  94.5 52.5 all-gather.7
  149.3 43.0 all-gather.5

commit v12 on v11

--- a/solution.py
+++ b/solution.py
@@ -1145,37 +1145,41 @@
     got_11, got_30 = to(add_b, 1), to(add_a, 3)
 
     def from_x(rows, k):
-        moved = lax.ppermute(rows, "exp", [(i, i ^ (4 * k)) for i in range(N_EXP)])
-        return moved.astype(f32)
+        return lax.ppermute(rows, "exp", [(i, i ^ (4 * k)) for i in range(N_EXP)])
 
     out_sums = spread_sums(
         exp_s,
-        out_part,
+        after(out_part, add_a),
         lax.ppermute(out_part[0, :4], "exp", core_swap),
         lax.ppermute(out_part[0, 4:], "exp", core_swap),
     )
-    out_rows = out_sums[0].astype(f32) + from_x(out_sums[1], 1) + from_x(out_sums[3], 3)
-    got_11, got_30 = after((got_11, got_30), far, out_rows)
+    out_near = (
+        out_sums[0].astype(f32)
+        + from_x(out_sums[1], 1).astype(f32)
+        + from_x(out_sums[3], 3).astype(f32)
+    )
+    got_11, got_30 = after((got_11, got_30), far)
     own_part, side = piece_sums(side_kernel, (f32, bf16), part_0, part_1, got_11, got_30)
     across = to(side, 4)
-    out_rows = out_rows + from_x(after(out_sums[2], side), 2)
-    out_across = lax.ppermute(
-        out_rows[1].astype(bf16), "exp", [(i, i ^ 2) for i in range(N_EXP)]
-    )
-
-    shares = merge_shares(ctx_s, near, after(far, side))
+    out_2 = from_x(after(out_sums[2], side), 2)
+
+    shares = merge_shares(ctx_s, near, after(far, side, out_near))
     got = swap_all(shares, "ctx", y_groups)
     own = (own_part + after(across, shares).astype(f32)).astype(bf16)
     at_1, at_3, at_z = to(own, 1), to(own, 3), to(own, 4)
 
-    columns, grad_kv, grad_down = column_grads(got, after(hidden_seq, own, out_rows), att_seq)
+    columns, grad_kv, grad_down = column_grads(got, after(hidden_seq, own, out_2), att_seq)
+    out_rows = after(out_near, columns) + out_2.astype(f32)
+    out_across = lax.ppermute(
+        out_rows[1].astype(bf16), "exp", [(i, i ^ 2) for i in range(N_EXP)]
+    )
     grad_kv = swap_all(grad_kv, "ctx")
-    columns = after(columns, grad_kv, at_1, at_3, out_across)
+    columns = after(columns, grad_kv, at_1, at_3)
     owned = swap_all(columns, "exp")
     input_grad = input_back(grad_query, grad_kv, w_all, tokens[0], gain_attn, grad_middle)
     owned, gain_sum = owned_sums(owned, grad_down)
     owned, at_z1, at_z3 = lax.optimization_barrier(
-        (after(owned, input_grad), to(at_z, 1), to(at_z, 3))
+        (after(owned, input_grad, out_across), to(at_z, 1), to(at_z, 3))
     )
     at_2, at_z2 = to(at_3, 1), to(at_z1, 3)
     mixed = (middle + out_rows[0] + out_across.astype(f32)).astype(bf16)[None]

time: 539 us -> 533 us (0.989)
  blocking collectives: 0 us -> 14.2 us
  waiting for transfers between devices: 219 us -> 208 us
    all_to_all x0 -> x1, blocking collectives: none -> 14.2 us  [swap_all(): lax.all_to_all(rows, axis, split_axis=0, concat_axis=0, tiled=True, axis_...]
    ppermute x1, waiting for transfers between devices: 19.5 us -> 6.09 us  [on_device(): lax.ppermute(out_rows[1].astype(bf16), 'exp', [(i, i ^ 2) for i in range(...]
    all_to_all x9 -> x8, starting transfers between devices: 43.5 us -> 36.6 us  [swap_all(): lax.all_to_all(rows, axis, split_axis=0, concat_axis=0, tiled=True, axis_...]
    ppermute x12, waiting for transfers between devices: 66.4 us -> 71.9 us  [to(): return lax.ppermute(rows, 'ctx', [(i, i ^ k) for i in range(N_CTX)])]
    all_to_all x9 -> x8, waiting for transfers between devices: 69.8 us -> 66.7 us  [swap_all(): lax.all_to_all(rows, axis, split_axis=0, concat_axis=0, tiled=True, axis_...]
  transfers between devices with their start and end apart: 34 -> 33, of which waited for: 22 -> 20; matrix products, arithmetic and copies ran while one was open for 7% -> 7% of each run, Pallas kernels for 22% -> 21%
where the time goes in v12:
time: 533 us; the launch traced here: 523 us
  waiting for transfers between devices  208 us (39%)
  Pallas kernels  142 us (27%)
  starting transfers between devices  74.6 us (14%)
  local copies, waits for them, and re-layouts  48.9 us (9%)
  between operations  14.8 us (3%)
  blocking collectives  14.2 us (3%)
  other arithmetic  13.5 us (3%)
  matrix products  6.68 us (1%)
    ppermute x12, waiting for transfers between devices, to(): return lax.ppermute(rows, 'ctx', [(i, i ^ k) for i in range(N_CTX)])  71.9 us
    all_to_all x8, waiting for transfers between devices, swap_all(): lax.all_to_all(rows, axis, split_axis=0, concat_axis=0, tiled=True, axis_...  66.7 us
    all_to_all x8, starting transfers between devices, swap_all(): lax.all_to_all(rows, axis, split_axis=0, concat_axis=0, tiled=True, axis_...  36.6 us
    unnamed x122, local copies, waits for them, and re-layouts  30.7 us
    pallas_call x1, Pallas kernels, expert_back(): pl.pallas_call(expert_kernel, grid_spec=pltpu.PrefetchScalarGridSpec(num_...  28.9 us
    ppermute x2, waiting for transfers between devices, of_sequence(): other = lax.ppermute(rows, 'ctx', z_swap)  26.3 us
    pallas_call x2, Pallas kernels, expert_weights(): pl.pallas_call(lambda *refs: expert_weights_kernel(halved, *refs), grid_s...  22.3 us
    ppermute x12, starting transfers between devices, to(): return lax.ppermute(rows, 'ctx', [(i, i ^ k) for i in range(N_CTX)])  19.4 us
  transfers between devices with their start and end apart: 33, of which 20 were waited for; matrix products, arithmetic and copies ran while one was open for 7% of the time, Pallas kernels for 21%

profile of v12, /device:TPU:0, one launch (start us, length us, event | category | flops | bytes accessed | tf_op | source)
XLA Modules:
  0.0 522.9 jit_solution(1806816212604535083)
XLA Ops:
  13.3 4.1 collective-permute-start
  18.0 4.8 all-to-all-start
  22.9 6.1 %collective-permute-done = bf16[1,128,1536]{2,1,0:T(8,128)(2,1)S(1)} collective-permute-done((bf16[1,128,1536]{2,1,0:T(8,128)(2,1)S(1)}, bf16[1,128,1536]{2,1,0:T(8,128)(2,1)S(1)}, u32[]{:S(2)}, u32[]{:S(2)}) %collective-permute-start) | collective-permute-done | bytes 393248 | tf_op jit(solution)/shard_map/ppermute | solution.py:1053
  31.7 4.6 all-to-all-start.1
  43.9 30.5 %all-to-all-done.1 = bf16[4,2,128,1536]{3,2,1,0:T(8,128)(2,1)S(1)} async-done(((bf16[4,2,128,1536]{3,2,1,0:T(8,128)(2,1)}), bf16[4,2,128,1536]{3,2,1,0:T(8,128)(2,1)S(1)}, u32[]{:S(2)}, u32[]{:S(2)}) %all-to-all-start.1) | async-done | bytes 3145760 | tf_op jit(solution)/shard_map/all_to_all | solution.py:1001
  76.0 5.2 all-to-all-start.2
  86.0 4.5 all-to-all-done.2
  93.2 7.7 %project.1 = (bf16[128,1536]{1,0:T(8,128)(2,1)S(1)}, bf16[8,128,1024]{2,1,0:T(8,128)(2,1)S(1)}) custom-call(bf16[1,128,1536]{2,1,0:T(8,128)(2,1)S(1)} %copy-done.19, bf16[8,128,1536]{2,1,0:T(8,128)(2,1)S(1)} %norm_rows.3.seq_ref.hidden_ref, bf16[1536,4096]{1,0:T(8,128)(2,1)} %all-gather.4.cloned.1.call-done.w_ref.wq_ref.wkv_ref), custom_call_target="tpu_custom_call" | custom-call | bytes 29520000 | tf_op jit(solution)/shard_map/project/pallas_call | solution.py:798
  100.9 5.8 %attend.1 = (bf16[128,1536]{1,0:T(8,128)(2,1)S(1)}, f32[128,1536]{1,0:T(8,128)S(1)}, f32[1536,128]{1,0:T(8,128)S(1)}) custom-call(s32[1]{0:T(128)} %bitcast.ctx_ref.refs_0_, bf16[128,1536]{1,0:T(8,128)(2,1)S(1)} %get-tuple-element.106.q_ref, bf16[8,128,1024]{2,1,0:T(8,128)(2,1)S(1)} %get-tuple-element.107.k_ref.v_ref, ...), custom_call_target="tpu_custom_call" | custom-call | bytes 22140000 | tf_op jit(solution)/shard_map/attend/pallas_call | solution.py:99
  106.7 5.4 %copy-done = bf16[1536,4096]{1,0:T(8,128)(2,1)S(1)} copy-done((bf16[1536,4096]{1,0:T(8,128)(2,1)S(1)}, bf16[1536,4096]{1,0:T(8,128)(2,1)}, u32[]{:S(2)}) %copy-start) | copy-done | bytes 12582936
  115.4 20.1 %collective-permute-done.1 = bf16[1,128,1536]{2,1,0:T(8,128)(2,1)S(1)} collective-permute-done((bf16[1,128,1536]{2,1,0:T(8,128)(2,1)S(1)}, bf16[1,128,1536]{2,1,0:T(8,128)(2,1)S(1)}, u32[]{:S(2)}, u32[]{:S(2)}) %collective-permute-start.1) | collective-permute-done | bytes 393248 | tf_op jit(solution)/shard_map/ppermute | solution.py:1053
  137.6 4.8 all-to-all-start.3
  142.5 4.6 all-gather.8.cloned.1.call-done
  147.0 13.7 %place_rows.1 = (bf16[8,2,128,128]{3,2,1,0:T(8,128)(2,1)}, bf16[2,2,384,1536]{3,2,1,0:T(8,128)(2,1)}, f32[2,2,384,512]{3,2,1,0:T(8,128)}, f32[8,2,128,128]{3,2,1,0:T(8,128)}, f32[2,2,384,128]{3,2,1,0:T(8,128)}) custom-call(s32[1]{0:T(128)} %bitcast.7.at_ref, bf16[8,2,128,1664]{3,2,1,0:T(8,128)(2,1)} %bitcast.84, bf16[2,512,1536]{2,1,0:T(8,128)(2,1)} %wd_ref.1, ...), custom_call_target="tpu_custom_call" | custom-call | bytes 51660000 | tf_op jit(solution)/shard_map/place_rows/pallas_call | solution.py:368
  160.7 19.3 %all-to-all-done.3 = bf16[4,2,128,1536]{3,2,1,0:T(8,128)(2,1)} async-done(((bf16[4,2,128,1536]{3,2,1,0:T(8,128)(2,1)}), bf16[4,2,128,1536]{3,2,1,0:T(8,128)(2,1)}, u32[]{:S(2)}, u32[]{:S(2)}) %all-to-all-start.3) | async-done | bytes 3145760 | tf_op jit(solution)/shard_map/all_to_all | solution.py:1001
  180.0 12.4 %all-gather.6.cloned.1.call-done = bf16[2048,1536]{1,0:T(8,128)(2,1)} async-done(((bf16[128,1536]{1,0:T(8,128)(2,1)}), bf16[2048,1536]{1,0:T(8,128)(2,1)}) %all-gather.6.cloned.1.call-update) | async-done | bytes 6291472 | tf_op jit(solution)/shard_map/all_gather | solution.py:1076
  192.4 28.9 %expert_back.1 = (bf16[2,8,128,1536]{3,2,1,0:T(8,128)(2,1)}, bf16[2,2,384,1536]{3,2,1,0:T(8,128)(2,1)}, bf16[2,2,384,512]{3,2,1,0:T(8,128)(2,1)}, bf16[2,2,384,1...) custom-call(s32[1]{0:T(128)} %bitcast.7.at_ref, ...), custom_call_target="tpu_custom_call" | custom-call | bytes 103320000 | tf_op jit(solution)/shard_map/expert_back/pallas_call | solution.py:447
  223.9 5.5 %collective-permute-done.2 = bf16[8,128,1536]{2,1,0:T(8,128)(2,1)S(1)} collective-permute-done((bf16[8,128,1536]{2,1,0:T(8,128)(2,1)S(1)}, bf16[8,128,1536]{2,1,0:T(8,128)(2,1)S(1)}, u32[]{:S(2)}, u32[]{:S(2)}) %collective-permute-start.2) | collective-permute-done | bytes 3145760 | tf_op jit(solution)/shard_map/ppermute | solution.py:1088
  229.3 2.6 fusion
  231.9 4.8 all-to-all-start.4
  236.7 10.9 %expert_weights.2 = (bf16[9216,128]{1,0:T(8,128)(2,1)}, bf16[9216,128]{1,0:T(8,128)(2,1)}) custom-call(s32[1]{0:T(128)} %bitcast.ctx_ref.refs_0_, bf16[2,768,1536]{2,1,0:T(8,128)(2,1)} %bitcast.91, bf16[2,768,1536]{2,1,0:T(8,128)(2,1)} %bitcast.89, bf16[2,768,512]{2,1,0:T(8,128)(2,1)} %bitcast.74, bf16[2,768,1024]{2,1,0:T(8,128)(2,1)} %bitcast.85, ...), custom_call_target="tpu_custom_call" | custom-call | bytes 7380000 | tf_op jit(solution)/shard_map/expert_weights/pallas_call | solution.py:898
  249.2 11.4 %expert_weights.3 = (bf16[4608,128]{1,0:T(8,128)(2,1)}, bf16[4608,128]{1,0:T(8,128)(2,1)}, bf16[4608,128]{1,0:T(8,128)(2,1)}, bf16[4608,128]{1,0:T(8,128)(2,1)}) custom-call(s32[1]{0:T(128)} %bitcast.ctx_ref.refs_0_, bf16[2,768,1536]{2,1,0:T(8,128)(2,1)} %bitcast.92, bf16[2,768,1536]{2,1,0:T(8,128)(2,1)} %bitcast.90, bf16[2,768,512]{2,1,0:T(8,128)(2,1)} %bitcast.75, ...), custom_call_target="tpu_custom_call" | custom-call | bytes 7380000 | tf_op jit(solution)/shard_map/expert_weights/pallas_call | solution.py:898
  262.9 2.6 convolution_convert_fusion
  270.0 9.8 %expert_output.1.own_ref = bf16[2,8,128,1536]{3,2,1,0:T(8,128)(2,1)} custom-call(s32[1]{0:T(128)} %bitcast.7.at_ref, bf16[2,2,384,512]{3,2,1,0:T(8,128)(2,1)S(1)} %copy-done.3, f32[2,2,384,128]{3,2,1,0:T(8,128)S(1)} %copy-done.36, bf16[8,2,128,128]{3,2,1,0:T(8,128)(2,1)S(1)} %copy-done.13, bf16[8,2,128,128]{3,2,1,0:T(8,128)(2,1)S(1)} %copy-done.7, ...), custom_call_target="tpu_custom_call" | custom-call | bytes 7380000 | tf_op jit(solution)/shard_map/expert_output/pallas_call | solution.py:499
  279.8 4.1 fusion.8
  285.8 5.7 %middle_back.1 = (f32[128,1536]{1,0:T(8,128)S(1)}, bf16[128,1536]{1,0:T(8,128)(2,1)S(1)}, bf16[128,1536]{1,0:T(8,128)(2,1)S(1)}, f32[16,128]{1,0:T(8,128)S(1)}) custom-call(bf16[8,128,1536]{2,1,0:T(8,128)(2,1)} %all-to-all-done.4.pieces_ref, f32[128,1536]{1,0:T(8,128)S(1)} %get-tuple-element.109.middle_ref, bf16[128,1536]{1,0:T(8,128)(2,1)S(1)} %bitcast.81, ...), custom_call_target="tpu_custom_call" | custom-call | bytes 3690000 | tf_op jit(solution)/shard_map/middle_back/pallas_call | solution.py:290
  294.7 9.0 %attend_back.1 = (bf16[128,1536]{1,0:T(8,128)(2,1)S(1)}, bf16[4,1776,128]{2,1,0:T(8,128)(2,1)S(1)}, bf16[4,1776,128]{2,1,0:T(8,128)(2,1)}) custom-call(s32[1]{0:T(128)} %bitcast.ctx_ref.refs_0_, bf16[128,1536]{1,0:T(8,128)(2,1)S(1)} %copy-done.15, bf16[128,1536]{1,0:T(8,128)(2,1)S(1)} %get-tuple-element.137.ga_ref, f32[128,1536]{1,0:T(8,128)S(1)} %copy-done.33, ...), custom_call_target="tpu_custom_call" | custom-call | bytes 7380000 | tf_op jit(solution)/shard_map/attend_back/pallas_call | solution.py:202
  304.4 3.1 collective-permute-start.9
  310.1 5.1 collective-permute-done.4.relay_b.got_31
  315.2 3.5 piece_sums.2
  329.3 16.4 %collective-permute-done.10.got_11 = bf16[4608,128]{1,0:T(8,128)(2,1)S(1)} collective-permute-done((bf16[4608,128]{1,0:T(8,128)(2,1)S(1)}, bf16[4608,128]{1,0:T(8,128)(2,1)S(1)}, u32[]{:S(2)}, u32[]{:S(2)}) %collective-permute-start.10) | collective-permute-done | bytes 1179680 | tf_op jit(solution)/shard_map/ppermute | solution.py:1103
  349.1 2.9 collective-permute-start.12
  355.4 4.5 all-to-all-start.5
  359.9 16.9 %collective-permute-done.12 = bf16[4608,128]{1,0:T(8,128)(2,1)S(1)} collective-permute-done((bf16[4608,128]{1,0:T(8,128)(2,1)S(1)}, bf16[4608,128]{1,0:T(8,128)(2,1)S(1)}, u32[]{:S(2)}, u32[]{:S(2)}) %collective-permute-start.12) | collective-permute-done | bytes 1179680 | tf_op jit(solution)/shard_map/ppermute | solution.py:1103
  380.7 3.1 collective-permute-start.13
  383.8 2.8 collective-permute-start.17
  386.6 12.6 %collective-permute-done.13 = bf16[2,128,1536]{2,1,0:T(8,128)(2,1)} collective-permute-done((bf16[2,128,1536]{2,1,0:T(8,128)(2,1)S(1)}, bf16[2,128,1536]{2,1,0:T(8,128)(2,1)}, u32[]{:S(2)}, u32[]{:S(2)}) %collective-permute-start.13) | collective-permute-done | bytes 786464 | tf_op jit(solution)/shard_map/ppermute | solution.py:1148
  399.2 7.1 %column_grads.1 = (bf16[16,112,512]{2,1,0:T(8,128)(2,1)}, bf16[8,128,128]{2,1,0:T(8,128)(2,1)}, bf16[96,128]{1,0:T(8,128)(2,1)}) custom-call(bf16[4,2160,128]{2,1,0:T(8,128)(2,1)} %all-to-all-done.5.got_ref, bf16[8,128,1536]{2,1,0:T(8,128)(2,1)} %copy-done.2, bf16[8,128,1536]{2,1,0:T(8,128)(2,1)} %bitcast.10.att_ref), custom_call_target="tpu_custom_call" | custom-call | bytes 29520000 | tf_op jit(solution)/shard_map/column_grads/pallas_call | solution.py:614
  406.2 14.2 %all_to_all.49.got_ref = bf16[8,128,128]{2,1,0:T(8,128)(2,1)} all-to-all(bf16[8,128,128]{2,1,0:T(8,128)(2,1)} %get-tuple-element.166), channel_id=1, replica_groups=mesh['ctx'=8,'exp'=16] {'ctx'}, dimensions={0} | all-to-all | bytes 524288 | tf_op jit(solution)/shard_map/all_to_all | solution.py:1001
  421.5 4.3 all-to-all-start.7
  431.9 6.9 %input_back.1 = bf16[128,1536]{1,0:T(8,128)(2,1)} custom-call(bf16[128,1536]{1,0:T(8,128)(2,1)S(1)} %copy-done.40, bf16[8,128,128]{2,1,0:T(8,128)(2,1)S(1)} %copy-done.29, bf16[1536,4096]{1,0:T(8,128)(2,1)} %all-gather.4.cloned.1.call-done.w_ref.wq_ref.wkv_ref, bf16[1536,4096]{1,0:T(8,128)(2,1)} %all-gather.4.cloned.1.call-done.w_ref.wq_ref.wkv_ref, ...), custom_call_target="tpu_custom_call" | custom-call | bytes 25830000 | tf_op jit(solution)/shard_map/input_back/pallas_call | solution.py:742
  438.8 11.9 %all-to-all-done.7.got_ref = bf16[16,112,512]{2,1,0:T(8,128)(2,1)S(1)} async-done(((bf16[16,112,512]{2,1,0:T(8,128)(2,1)}), bf16[16,112,512]{2,1,0:T(8,128)(2,1)S(1)}, u32[]{:S(2)}, u32[]{:S(2)}) %all-to-all-start.7) | async-done | bytes 1835040 | tf_op jit(solution)/shard_map/all_to_all | solution.py:1001
  451.0 6.1 %collective-permute-done.14 = bf16[128,1536]{1,0:T(8,128)(2,1)} collective-permute-done((bf16[128,1536]{1,0:T(8,128)(2,1)}, bf16[128,1536]{1,0:T(8,128)(2,1)}, u32[]{:S(2)}, u32[]{:S(2)}) %collective-permute-start.14) | collective-permute-done | bytes 393248 | tf_op jit(solution)/shard_map/ppermute | solution.py:1173
  458.4 3.6 all-to-all-start.8
  466.3 2.5 fusion.4
  468.8 5.5 %unpack_experts.2 = (f32[2,1536,512]{2,1,0:T(8,128)}, f32[2,1536,512]{2,1,0:T(8,128)}, f32[2,512,1536]{2,1,0:T(8,128)}) custom-call(s32[1]{0:T(128)} %bitcast.ctx_ref.refs_0_, bf16[4608,128]{1,0:T(8,128)(2,1)S(1)} %add_convert_fusion.refs_1_, bf16[4608,128]{1,0:T(8,128)(2,1)S(1)} %copy-done.27, bf16[4608,128]{1,0:T(8,128)(2,1)} %collective-permute-done.16.refs_3_, ...), custom_call_target="tpu_custom_call" | custom-call | bytes 29520000 | tf_op jit(solution)/shard_map/unpack_experts/pallas_call | solution.py:942
  474.8 31.2 %collective-permute-done.20.refs_1_ = bf16[4608,128]{1,0:T(8,128)(2,1)} collective-permute-done((bf16[4608,128]{1,0:T(8,128)(2,1)}, bf16[4608,128]{1,0:T(8,128)(2,1)}, u32[]{:S(2)}, u32[]{:S(2)}) %collective-permute-start.20) | collective-permute-done | bytes 1179680 | tf_op jit(solution)/shard_map/ppermute | solution.py:1103
  507.1 6.4 %unpack_experts.3 = (f32[2,1536,512]{2,1,0:T(8,128)}, f32[2,1536,512]{2,1,0:T(8,128)}, f32[2,512,1536]{2,1,0:T(8,128)}) custom-call(s32[1]{0:T(128)} %bitcast.ctx_ref.refs_0_, bf16[4608,128]{1,0:T(8,128)(2,1)} %collective-permute-done.20.refs_1_, ...), custom_call_target="tpu_custom_call", output_to_operand_aliasing={{0}: (5, {}), {1}: (6, {}), {2}: (7, {})} | custom-call | bytes 29520000 | tf_op jit(solution)/shard_map/unpack_experts/pallas_call | solution.py:942
  (204 shorter events, 89.0 us)
Async XLA Ops:
  7.2 85.0 %all-gather.4.cloned.1.call-start = ((), (), s32[]{:S(2)}) async-start(), calls=%async_computation.9 | async-start | bytes 13369344 | tf_op jit(solution)/shard_map/all_gather | solution.py:1039
  12.0 135.0 %all-gather.8.cloned.1.call-start = ((), (), s32[]{:S(2)}) async-start(), calls=%async_computation.11 | async-start | bytes 7241728 | tf_op jit(solution)/shard_map/all_gather | solution.py:1046
  13.3 15.8 %collective-permute-start = (bf16[1,128,1536]{2,1,0:T(8,128)(2,1)S(1)}, bf16[1,128,1536]{2,1,0:T(8,128)(2,1)S(1)}, u32[]{:S(2)}, u32[]{:S(2)}) collective-permute-start(bf16[1,128,1536]{2,1,0:T(8,128)(2,1)S(1)} %copy-done.6), channel_id=1, source_target_pairs={{0,64},{16,80},{32,96},{48,112},{64,0},{80,16},{96,32},{112,48},{1... | collective-permute-start | bytes 1179656 | tf_op jit(solution)/shard_map/ppermute | solution.py:1053
  18.0 11.7 %all-to-all-start = ((bf16[16,1,192]{2,1,0:T(2,128)(2,1)}), bf16[16,1,192]{2,1,0:T(2,128)(2,1)S(1)}, u32[]{:S(2)}, u32[]{:S(2)}) async-start(bf16[16,1,192]{2,1,0:T(2,128)(2,1)} %broadcast_in_dim.24), calls=%async_computation | async-start | bytes 32768 | tf_op jit(solution)/shard_map/all_to_all | solution.py:1001
  31.7 42.6 %all-to-all-start.1 = ((bf16[4,2,128,1536]{3,2,1,0:T(8,128)(2,1)}), bf16[4,2,128,1536]{3,2,1,0:T(8,128)(2,1)S(1)}, u32[]{:S(2)}, u32[]{:S(2)}) async-start(bf16[4,2,128,1536]{3,2,1,0:T(8,128)(2,1)} %broadcast_in_dim.25), calls=%async_computation.1 | async-start | bytes 6291456 | tf_op jit(solution)/shard_map/all_to_all | solution.py:1001
  76.0 14.5 %all-to-all-start.2 = ((bf16[16,96,128]{2,1,0:T(8,128)(2,1)}), bf16[16,96,128]{2,1,0:T(8,128)(2,1)}, u32[]{:S(2)}, u32[]{:S(2)}) async-start(bf16[16,96,128]{2,1,0:T(8,128)(2,1)} %copy.62), calls=%async_computation.2 | async-start | bytes 786432 | tf_op jit(solution)/shard_map/all_to_all | solution.py:1001
  81.2 111.2 %all-gather.6.cloned.1.call-start = ((), (), s32[]{:S(2)}) async-start(), calls=%async_computation.10 | async-start | bytes 6684672 | tf_op jit(solution)/shard_map/all_gather | solution.py:1076
  86.0 14.9 %copy-start.2 = (bf16[8,128,1536]{2,1,0:T(8,128)(2,1)}, bf16[8,128,1536]{2,1,0:T(8,128)(2,1)S(1)}, u32[]{:S(2)}) copy-start(bf16[8,128,1536]{2,1,0:T(8,128)(2,1)S(1)} %norm_rows.3.seq_ref.hidden_ref) | copy-start | bytes 9437188
  100.9 12.9 %copy-start.1 = (bf16[8,128,1024]{2,1,0:T(8,128)(2,1)}, bf16[8,128,1024]{2,1,0:T(8,128)(2,1)S(1)}, u32[]{:S(2)}) copy-start(bf16[8,128,1024]{2,1,0:T(8,128)(2,1)S(1)} %get-tuple-element.107.k_ref.v_ref) | copy-start | bytes 6291460
  100.9 12.9 %copy-start.14 = (bf16[128,1536]{1,0:T(8,128)(2,1)}, bf16[128,1536]{1,0:T(8,128)(2,1)S(1)}, u32[]{:S(2)}) copy-start(bf16[128,1536]{1,0:T(8,128)(2,1)S(1)} %get-tuple-element.106.q_ref) | copy-start | bytes 1179652
  113.8 171.0 %copy-start.8 = (f32[128,1536]{1,0:T(8,128)}, f32[128,1536]{1,0:T(8,128)S(1)}, u32[]{:S(2)}) copy-start(f32[128,1536]{1,0:T(8,128)S(1)} %get-tuple-element.109.middle_ref) | copy-start | bytes 2359300
  113.8 21.7 %collective-permute-start.1 = (bf16[1,128,1536]{2,1,0:T(8,128)(2,1)S(1)}, bf16[1,128,1536]{2,1,0:T(8,128)(2,1)S(1)}, u32[]{:S(2)}, u32[]{:S(2)}) collective-permute-start(bf16[1,128,1536]{2,1,0:T(8,128)(2,1)S(1)} %bitcast.82), channel_id=1, source_target_pairs={{0,64},{16,80},{32,96},{48,112},{64,0},{80,16},{96,32},{112,48},{1... | collective-permute-start | bytes 1179656 | tf_op jit(solution)/shard_map/ppermute | solution.py:1053
  137.6 42.4 %all-to-all-start.3 = ((bf16[4,2,128,1536]{3,2,1,0:T(8,128)(2,1)}), bf16[4,2,128,1536]{3,2,1,0:T(8,128)(2,1)}, u32[]{:S(2)}, u32[]{:S(2)}) async-start(bf16[4,2,128,1536]{3,2,1,0:T(8,128)(2,1)} %broadcast_in_dim.27), calls=%async_computation.3 | async-start | bytes 6291456 | tf_op jit(solution)/shard_map/all_to_all | solution.py:1001
  223.6 5.7 %collective-permute-start.2 = (bf16[8,128,1536]{2,1,0:T(8,128)(2,1)S(1)}, bf16[8,128,1536]{2,1,0:T(8,128)(2,1)S(1)}, u32[]{:S(2)}, u32[]{:S(2)}) collective-permute-start(bf16[8,128,1536]{2,1,0:T(8,128)(2,1)S(1)} %slice_bitcast_fusion), channel_id=1, source_target_pairs={{0,1},{1,0},{2,3},{3,2},{4,5},{5,4},{6,7},{7,6},{8,9},{9,8},{10,11... | collective-permute-start | bytes 9437192 | tf_op jit(solution)/shard_map/ppermute | solution.py:1088
  231.9 52.9 %all-to-all-start.4 = ((bf16[8,128,1536]{2,1,0:T(8,128)(2,1)}), bf16[8,128,1536]{2,1,0:T(8,128)(2,1)}, u32[]{:S(2)}, u32[]{:S(2)}) async-start(bf16[8,128,1536]{2,1,0:T(8,128)(2,1)} %fusion), calls=%async_computation.4 | async-start | bytes 6291456 | tf_op jit(solution)/shard_map/all_to_all | solution.py:1001
  247.7 15.3 %slice-start.2 = ((s8[6291456]{0:T(1024)(128)(4,1)}), s8[4194304]{0:T(1024)(128)(4,1)S(1)}, s32[]{:S(2)}) async-start(s8[6291456]{0:T(1024)(128)(4,1)} %bitcast.94), calls=%async_computation.14 | async-start | bytes 8388608
  247.7 15.3 %slice-start.3 = ((s8[6291456]{0:T(1024)(128)(4,1)}), s8[2097152]{0:T(1024)(128)(4,1)S(1)}, s32[]{:S(2)}) async-start(s8[6291456]{0:T(1024)(128)(4,1)} %bitcast.94), calls=%async_computation.15 | async-start | bytes 4194304
  247.7 15.3 %copy-start.48 = (bf16[8,2,128,128]{3,2,1,0:T(8,128)(2,1)S(1)}, bf16[8,2,128,128]{3,2,1,0:T(8,128)(2,1)}, u32[]{:S(2)}) copy-start(bf16[8,2,128,128]{3,2,1,0:T(8,128)(2,1)} %get-tuple-element.134) | copy-start | bytes 1572868
  247.7 62.4 %collective-permute-start.3 = (bf16[9216,128]{1,0:T(8,128)(2,1)}, bf16[9216,128]{1,0:T(8,128)(2,1)}, u32[]{:S(2)}, u32[]{:S(2)}) collective-permute-start(bf16[9216,128]{1,0:T(8,128)(2,1)} %get-tuple-element.123), channel_id=1, source_target_pairs={{0,16},{16,0},{32,48},{48,32},{64,80},{80,64},{96,112},{112,96},{1... | collective-permute-start | bytes 7077896 | tf_op jit(solution)/shard_map/ppermute | solution.py:1103
  260.6 54.6 %collective-permute-start.4 = (bf16[9216,128]{1,0:T(8,128)(2,1)}, bf16[9216,128]{1,0:T(8,128)(2,1)}, u32[]{:S(2)}, u32[]{:S(2)}) collective-permute-start(bf16[9216,128]{1,0:T(8,128)(2,1)} %get-tuple-element.132), channel_id=1, source_target_pairs={{0,48},{16,32},{32,16},{48,0},{64,112},{80,96},{96,80},{112,64},{1... | collective-permute-start | bytes 7077896 | tf_op jit(solution)/shard_map/ppermute | solution.py:1103
  283.9 23.7 %slice-start = ((s8[6291456]{0:T(1024)(128)(4,1)}), s8[2097152]{0:T(1024)(128)(4,1)S(1)}, s32[]{:S(2)}) async-start(s8[6291456]{0:T(1024)(128)(4,1)} %bitcast.72), calls=%async_computation.12 | async-start | bytes 4194304
  285.8 21.8 %slice-start.1 = ((s8[6291456]{0:T(1024)(128)(4,1)}), s8[4194304]{0:T(1024)(128)(4,1)S(1)}, s32[]{:S(2)}) async-start(s8[6291456]{0:T(1024)(128)(4,1)} %bitcast.72), calls=%async_computation.13 | async-start | bytes 8388608
  304.4 10.8 %copy-start.22 = (bf16[4608,128]{1,0:T(8,128)(2,1)S(1)}, bf16[4608,128]{1,0:T(8,128)(2,1)}, u32[]{:S(2)}) copy-start(bf16[4608,128]{1,0:T(8,128)(2,1)} %get-tuple-element.125.p0) | copy-start | bytes 3538948
  304.4 10.8 %copy-start.23 = (bf16[4608,128]{1,0:T(8,128)(2,1)S(1)}, bf16[4608,128]{1,0:T(8,128)(2,1)}, u32[]{:S(2)}) copy-start(bf16[4608,128]{1,0:T(8,128)(2,1)} %get-tuple-element.131.p6) | copy-start | bytes 3538948
  304.4 10.8 %copy-start.24 = (bf16[4608,128]{1,0:T(8,128)(2,1)S(1)}, bf16[4608,128]{1,0:T(8,128)(2,1)}, u32[]{:S(2)}) copy-start(bf16[4608,128]{1,0:T(8,128)(2,1)} %get-tuple-element.129.p1) | copy-start | bytes 3538948
  304.4 10.8 %copy-start.25 = (bf16[4608,128]{1,0:T(8,128)(2,1)S(1)}, bf16[4608,128]{1,0:T(8,128)(2,1)}, u32[]{:S(2)}) copy-start(bf16[4608,128]{1,0:T(8,128)(2,1)} %get-tuple-element.130.p3) | copy-start | bytes 3538948
  304.4 42.8 %collective-permute-start.9 = (bf16[4,1776,128]{2,1,0:T(8,128)(2,1)}, bf16[4,1776,128]{2,1,0:T(8,128)(2,1)S(1)}, u32[]{:S(2)}, u32[]{:S(2)}) collective-permute-start(bf16[4,1776,128]{2,1,0:T(8,128)(2,1)} %get-tuple-element.150), channel_id=1, source_target_pairs={{0,64},{16,80},{32,96},{48,112},{64,0},{80,16},{96,32},{112,48},{1... | collective-permute-start | bytes 5455880 | tf_op jit(solution)/shard_map/ppermute | solution.py:1131
  309.6 11.3 %collective-permute-start.5 = (bf16[4,128,1536]{2,1,0:T(8,128)(2,1)}, bf16[4,128,1536]{2,1,0:T(8,128)(2,1)S(1)}, u32[]{:S(2)}, u32[]{:S(2)}) collective-permute-start(bf16[4,128,1536]{2,1,0:T(8,128)(2,1)} %get-tuple-element.195), channel_id=1, source_target_pairs={{0,1},{1,0},{2,3},{3,2},{4,5},{5,4},{6,7},{7,6},{8,9},{9,8},{10,11... | collective-permute-start | bytes 4718600 | tf_op jit(solution)/shard_map/ppermute | solution.py:1153
  309.6 11.3 %collective-permute-start.6 = (bf16[4,128,1536]{2,1,0:T(8,128)(2,1)}, bf16[4,128,1536]{2,1,0:T(8,128)(2,1)S(1)}, u32[]{:S(2)}, u32[]{:S(2)}) collective-permute-start(bf16[4,128,1536]{2,1,0:T(8,128)(2,1)} %get-tuple-element.194), channel_id=1, source_target_pairs={{0,1},{1,0},{2,3},{3,2},{4,5},{5,4},{6,7},{7,6},{8,9},{9,8},{10,11... | collective-permute-start | bytes 4718600 | tf_op jit(solution)/shard_map/ppermute | solution.py:1154
  318.7 27.0 %collective-permute-start.10 = (bf16[4608,128]{1,0:T(8,128)(2,1)S(1)}, bf16[4608,128]{1,0:T(8,128)(2,1)S(1)}, u32[]{:S(2)}, u32[]{:S(2)}) collective-permute-start(bf16[4608,128]{1,0:T(8,128)(2,1)S(1)} %get-tuple-element.153), channel_id=1, source_target_pairs={{0,16},{16,0},{32,48},{48,32},{64,80},{80,64},{96,112},{112,96},{1... | collective-permute-start | bytes 3538952 | tf_op jit(solution)/shard_map/ppermute | solution.py:1103
  318.8 28.2 %collective-permute-start.11 = (bf16[4608,128]{1,0:T(8,128)(2,1)S(1)}, bf16[4608,128]{1,0:T(8,128)(2,1)S(1)}, u32[]{:S(2)}, u32[]{:S(2)}) collective-permute-start(bf16[4608,128]{1,0:T(8,128)(2,1)S(1)} %get-tuple-element.145), channel_id=1, source_target_pairs={{0,48},{16,32},{32,16},{48,0},{64,112},{80,96},{96,80},{112,64},{1... | collective-permute-start | bytes 3538952 | tf_op jit(solution)/shard_map/ppermute | solution.py:1103
  325.4 26.6 %collective-permute-start.7 = (bf16[2,128,1536]{2,1,0:T(8,128)(2,1)S(1)}, bf16[2,128,1536]{2,1,0:T(8,128)(2,1)S(1)}, u32[]{:S(2)}, u32[]{:S(2)}) collective-permute-start(bf16[2,128,1536]{2,1,0:T(8,128)(2,1)S(1)} %get-tuple-element.148), channel_id=1, source_target_pairs={{0,4},{1,5},{2,6},{3,7},{4,0},{5,1},{6,2},{7,3},{8,12},{9,13},{10,... | collective-permute-start | bytes 2359304 | tf_op jit(solution)/shard_map/ppermute | solution.py:1148
  327.2 24.8 %collective-permute-start.8 = (bf16[2,128,1536]{2,1,0:T(8,128)(2,1)S(1)}, bf16[2,128,1536]{2,1,0:T(8,128)(2,1)S(1)}, u32[]{:S(2)}, u32[]{:S(2)}) collective-permute-start(bf16[2,128,1536]{2,1,0:T(8,128)(2,1)S(1)} %get-tuple-element.149), channel_id=1, source_target_pairs={{0,12},{1,13},{2,14},{3,15},{4,8},{5,9},{6,10},{7,11},{8,4},{9,5},... | collective-permute-start | bytes 2359304 | tf_op jit(solution)/shard_map/ppermute | solution.py:1148
  349.1 27.7 %collective-permute-start.12 = (bf16[4608,128]{1,0:T(8,128)(2,1)S(1)}, bf16[4608,128]{1,0:T(8,128)(2,1)S(1)}, u32[]{:S(2)}, u32[]{:S(2)}) collective-permute-start(bf16[4608,128]{1,0:T(8,128)(2,1)S(1)} %get-tuple-element.156), channel_id=1, source_target_pairs={{0,64},{16,80},{32,96},{48,112},{64,0},{80,16},{96,32},{112,48},{1... | collective-permute-start | bytes 3538952 | tf_op jit(solution)/shard_map/ppermute | solution.py:1103
  355.4 43.7 %all-to-all-start.5 = ((bf16[4,2160,128]{2,1,0:T(8,128)(2,1)}), bf16[4,2160,128]{2,1,0:T(8,128)(2,1)}, u32[]{:S(2)}, u32[]{:S(2)}) async-start(bf16[4,2160,128]{2,1,0:T(8,128)(2,1)} %merge_shares.1), calls=%async_computation.5 | async-start | bytes 4423680 | tf_op jit(solution)/shard_map/all_to_all | solution.py:1001
  378.7 41.8 %collective-permute-start.15 = (bf16[4608,128]{1,0:T(8,128)(2,1)S(1)}, bf16[4608,128]{1,0:T(8,128)(2,1)S(1)}, u32[]{:S(2)}, u32[]{:S(2)}) collective-permute-start(bf16[4608,128]{1,0:T(8,128)(2,1)S(1)} %add_convert_fusion.refs_1_), channel_id=1, source_target_pairs={{0,16},{16,0},{32,48},{48,32},{64,80},{80,64},{96,112},{112,96},{1... | collective-permute-start | bytes 3538952 | tf_op jit(solution)/shard_map/ppermute | solution.py:1103
  379.6 41.8 %collective-permute-start.16 = (bf16[4608,128]{1,0:T(8,128)(2,1)S(1)}, bf16[4608,128]{1,0:T(8,128)(2,1)}, u32[]{:S(2)}, u32[]{:S(2)}) collective-permute-start(bf16[4608,128]{1,0:T(8,128)(2,1)S(1)} %add_convert_fusion.refs_1_), channel_id=1, source_target_pairs={{0,48},{16,32},{32,16},{48,0},{64,112},{80,96},{96,80},{112,64},{1... | collective-permute-start | bytes 3538952 | tf_op jit(solution)/shard_map/ppermute | solution.py:1103
  380.7 18.5 %collective-permute-start.13 = (bf16[2,128,1536]{2,1,0:T(8,128)(2,1)S(1)}, bf16[2,128,1536]{2,1,0:T(8,128)(2,1)}, u32[]{:S(2)}, u32[]{:S(2)}) collective-permute-start(bf16[2,128,1536]{2,1,0:T(8,128)(2,1)S(1)} %get-tuple-element.161), channel_id=1, source_target_pairs={{0,8},{1,9},{2,10},{3,11},{4,12},{5,13},{6,14},{7,15},{8,0},{9,1},... | collective-permute-start | bytes 2359304 | tf_op jit(solution)/shard_map/ppermute | solution.py:1148
  383.8 42.0 %collective-permute-start.17 = (bf16[4608,128]{1,0:T(8,128)(2,1)S(1)}, bf16[4608,128]{1,0:T(8,128)(2,1)}, u32[]{:S(2)}, u32[]{:S(2)}) collective-permute-start(bf16[4608,128]{1,0:T(8,128)(2,1)S(1)} %add_convert_fusion.refs_1_), channel_id=1, source_target_pairs={{0,64},{16,80},{32,96},{48,112},{64,0},{80,16},{96,32},{112,48},{1... | collective-permute-start | bytes 3538952 | tf_op jit(solution)/shard_map/ppermute | solution.py:1103
  421.5 29.2 %all-to-all-start.7 = ((bf16[16,112,512]{2,1,0:T(8,128)(2,1)}), bf16[16,112,512]{2,1,0:T(8,128)(2,1)S(1)}, u32[]{:S(2)}, u32[]{:S(2)}) async-start(bf16[16,112,512]{2,1,0:T(8,128)(2,1)} %get-tuple-element.168), calls=%async_computation.7 | async-start | bytes 3670016 | tf_op jit(solution)/shard_map/all_to_all | solution.py:1001
  425.8 31.3 %collective-permute-start.18 = (bf16[4608,128]{1,0:T(8,128)(2,1)}, bf16[4608,128]{1,0:T(8,128)(2,1)}, u32[]{:S(2)}, u32[]{:S(2)}) collective-permute-start(bf16[4608,128]{1,0:T(8,128)(2,1)} %collective-permute-done.17.refs_4_), channel_id=1, source_target_pairs={{0,16},{16,0},{32,48},{48,32},{64,80},{80,64},{96,112},{112,96},{1... | collective-permute-start | bytes 3538952 | tf_op jit(solution)/shard_map/ppermute | solution.py:1103
  426.7 30.4 %collective-permute-start.19 = (bf16[4608,128]{1,0:T(8,128)(2,1)}, bf16[4608,128]{1,0:T(8,128)(2,1)}, u32[]{:S(2)}, u32[]{:S(2)}) collective-permute-start(bf16[4608,128]{1,0:T(8,128)(2,1)} %collective-permute-done.17.refs_4_), channel_id=1, source_target_pairs={{0,48},{16,32},{32,16},{48,0},{64,112},{80,96},{96,80},{112,64},{1... | collective-permute-start | bytes 3538952 | tf_op jit(solution)/shard_map/ppermute | solution.py:1103
  430.0 27.1 %collective-permute-start.14 = (bf16[128,1536]{1,0:T(8,128)(2,1)}, bf16[128,1536]{1,0:T(8,128)(2,1)}, u32[]{:S(2)}, u32[]{:S(2)}) collective-permute-start(bf16[128,1536]{1,0:T(8,128)(2,1)} %fusion.5), channel_id=1, source_target_pairs={{0,2},{1,3},{2,0},{3,1},{4,6},{5,7},{6,4},{7,5},{8,10},{9,11},{10,... | collective-permute-start | bytes 1179656 | tf_op jit(solution)/shard_map/ppermute | solution.py:1173
  431.9 18.8 %copy-start.41 = (bf16[96,128]{1,0:T(8,128)(2,1)S(1)}, bf16[96,128]{1,0:T(8,128)(2,1)}, u32[]{:S(2)}) copy-start(bf16[96,128]{1,0:T(8,128)(2,1)} %get-tuple-element.169.down_ref) | copy-start | bytes 73732
  451.0 15.3 %copy-start.51 = (bf16[96]{0:T(256)(128)(2,1)S(1)}, bf16[96]{0:T(256)(128)(2,1)}, u32[]{:S(2)}) copy-start(bf16[96]{0:T(256)(128)(2,1)} %param.19) | copy-start | bytes 580
  458.4 55.1 %all-to-all-start.8 = ((bf16[8,736,128]{2,1,0:T(8,128)(2,1)}), bf16[8,736,128]{2,1,0:T(8,128)(2,1)S(1)}, u32[]{:S(2)}, u32[]{:S(2)}) async-start(bf16[8,736,128]{2,1,0:T(8,128)(2,1)} %broadcast_in_dim.31), calls=%async_computation.8 | async-start | bytes 3014656 | tf_op jit(solution)/shard_map/all_to_all | solution.py:1001
  462.0 44.0 %collective-permute-start.20 = (bf16[4608,128]{1,0:T(8,128)(2,1)}, bf16[4608,128]{1,0:T(8,128)(2,1)}, u32[]{:S(2)}, u32[]{:S(2)}) collective-permute-start(bf16[4608,128]{1,0:T(8,128)(2,1)} %collective-permute-done.16.refs_3_), channel_id=1, source_target_pairs={{0,16},{16,0},{32,48},{48,32},{64,80},{80,64},{96,112},{112,96},{1... | collective-permute-start | bytes 3538952 | tf_op jit(solution)/shard_map/ppermute | solution.py:1103
  463.9 43.2 %collective-permute-start.21 = (bf16[4608,128]{1,0:T(8,128)(2,1)}, bf16[4608,128]{1,0:T(8,128)(2,1)}, u32[]{:S(2)}, u32[]{:S(2)}) collective-permute-start(bf16[4608,128]{1,0:T(8,128)(2,1)} %collective-permute-done.18.refs_2_), channel_id=1, source_target_pairs={{0,48},{16,32},{32,16},{48,0},{64,112},{80,96},{96,80},{112,64},{1... | collective-permute-start | bytes 3538952 | tf_op jit(solution)/shard_map/ppermute | solution.py:1103
  (41 other events, 160.8 us)
Sparse Core Ops, SparseCore 0:
  12.2 79.9 all-gather.3
  94.5 52.5 all-gather.7
  149.3 43.0 all-gather.5

commit v13 on v12

--- a/solution.py
+++ b/solution.py
@@ -673,7 +673,8 @@
     lane = lax.broadcasted_iota(jnp.int32, (96, HEAD_DIM), 1)
 
     def tile(c, t):
-        return got_ref[c, 96 * t : 96 * t + 96].astype(f32)
+        at = BLOCK + 96 * t
+        return got_ref[c, at : at + 96].astype(f32)
 
     for c in range(N_CTX):
         at = HEAD_DIM * c
@@ -698,7 +699,7 @@
     picks = picks.astype(bf16)
 
     def shared_tile(j):
-        at = 384 + 16 * j
+        at = BLOCK + 384 + 16 * j
         rows = jnp.concatenate([got_ref[c, at : at + 16] for c in range(N_CTX)], axis=0)
         return dg(picks, rows, NN)
 
@@ -708,7 +709,7 @@
         sg_ref[:, at : at + HEAD_DIM] = low
         su_ref[:, at : at + HEAD_DIM] = high
     for c in range(N_CTX):
-        rows = got_ref[c, 384 + 16 * N_EXP :].astype(f32)
+        rows = got_ref[c, BLOCK + 384 + 16 * N_EXP :].astype(f32)
         for m in range(HEADS):
             sd_ref[8 * c : 8 * c + 8, HEAD_DIM * m : HEAD_DIM * (m + 1)] = rows[8 * m : 8 * m + 8]
 
@@ -1168,28 +1169,28 @@
     own = (own_part + after(across, shares).astype(f32)).astype(bf16)
     at_1, at_3, at_z = to(own, 1), to(own, 3), to(own, 4)
 
-    columns, grad_kv, grad_down = column_grads(got, after(hidden_seq, own, out_2), att_seq)
+    columns, grad_kv, grad_down = column_grads(got, after(hidden_seq, own), att_seq)
     out_rows = after(out_near, columns) + out_2.astype(f32)
     out_across = lax.ppermute(
         out_rows[1].astype(bf16), "exp", [(i, i ^ 2) for i in range(N_EXP)]
     )
-    grad_kv = swap_all(grad_kv, "ctx")
-    columns = after(columns, grad_kv, at_1, at_3)
+    columns = after(columns, at_1, at_3, out_2)
     owned = swap_all(columns, "exp")
-    input_grad = input_back(grad_query, grad_kv, w_all, tokens[0], gain_attn, grad_middle)
     owned, gain_sum = owned_sums(owned, grad_down)
     owned, at_z1, at_z3 = lax.optimization_barrier(
-        (after(owned, input_grad, out_across), to(at_z, 1), to(at_z, 3))
+        (after(owned, out_across), to(at_z, 1), to(at_z, 3))
     )
     at_2, at_z2 = to(at_3, 1), to(at_z1, 3)
     mixed = (middle + out_rows[0] + out_across.astype(f32)).astype(bf16)[None]
     experts = unpack_experts(
-        ctx_s, ((0, 0), (1, 0), (3, 0), (0, 1)), (after(own, owned), at_1, at_3, at_z)
-    )
-    owned = swap_all(jnp.broadcast_to(owned, (N_CTX, OWNED_ROWS, HEAD_DIM)), "ctx")
+        ctx_s, ((0, 0), (1, 0), (3, 0), (2, 0)), (after(own, owned), at_1, at_3, at_2)
+    )
+    owned = jnp.broadcast_to(owned, (N_CTX, OWNED_ROWS, HEAD_DIM))
+    owned = swap_all(jnp.concatenate([grad_kv, owned], axis=1), "ctx")
     experts = unpack_experts(
-        ctx_s, ((2, 0), (1, 1), (3, 1), (2, 1)), (at_2, at_z1, at_z3, at_z2), experts
-    )
+        ctx_s, ((0, 1), (1, 1), (3, 1), (2, 1)), (at_z, at_z1, at_z3, at_z2), experts
+    )
+    input_grad = input_back(grad_query, owned, w_all, tokens[0], gain_attn, grad_middle)
     gain_attn_sum, *dense = finish(
         after(owned, experts[0], mixed),
         norm_attn.astype(f32).reshape(96, 1),

time: 533 us -> 541 us (1.015)
  the two profiles are of different devices: /device:TPU:0 before, /device:TPU:6 now
where the time goes in v13:
time: 541 us; the launch traced here: 531 us
  waiting for transfers between devices  230 us (43%)
  Pallas kernels  142 us (26%)
  starting transfers between devices  75 us (14%)
  local copies, waits for them, and re-layouts  48.1 us (9%)
  other arithmetic  14.8 us (3%)
  between operations  14.8 us (3%)
  matrix products  6.68 us (1%)
    ppermute x12, waiting for transfers between devices, to(): return lax.ppermute(rows, 'ctx', [(i, i ^ k) for i in range(N_CTX)])  91.5 us
    all_to_all x8, waiting for transfers between devices, swap_all(): lax.all_to_all(rows, axis, split_axis=0, concat_axis=0, tiled=True, axis_...  73.5 us
    all_to_all x8, starting transfers between devices, swap_all(): lax.all_to_all(rows, axis, split_axis=0, concat_axis=0, tiled=True, axis_...  40 us
    unnamed x122, local copies, waits for them, and re-layouts  31 us
    pallas_call x1, Pallas kernels, expert_back(): pl.pallas_call(expert_kernel, grid_spec=pltpu.PrefetchScalarGridSpec(num_...  29 us
    ppermute x2, waiting for transfers between devices, of_sequence(): other = lax.ppermute(rows, 'ctx', z_swap)  26.3 us
    pallas_call x2, Pallas kernels, expert_weights(): pl.pallas_call(lambda *refs: expert_weights_kernel(halved, *refs), grid_s...  22.3 us
    ppermute x12, starting transfers between devices, to(): return lax.ppermute(rows, 'ctx', [(i, i ^ k) for i in range(N_CTX)])  21 us
  transfers between devices with their start and end apart: 33, of which 22 were waited for; matrix products, arithmetic and copies ran while one was open for 7% of the time, Pallas kernels for 20%

profile of v13, /device:TPU:6, one launch (start us, length us, event | category | flops | bytes accessed | tf_op | source)
XLA Modules:
  0.0 531.4 jit_solution(15460482885775674628)
XLA Ops:
  13.3 4.0 collective-permute-start
  17.9 5.2 all-to-all-start
  23.2 5.6 %collective-permute-done = bf16[1,128,1536]{2,1,0:T(8,128)(2,1)S(1)} collective-permute-done((bf16[1,128,1536]{2,1,0:T(8,128)(2,1)S(1)}, bf16[1,128,1536]{2,1,0:T(8,128)(2,1)S(1)}, u32[]{:S(2)}, u32[]{:S(2)}) %collective-permute-start) | collective-permute-done | bytes 393248 | tf_op jit(solution)/shard_map/ppermute | solution.py:1054
  31.7 4.6 all-to-all-start.1
  43.8 30.5 %all-to-all-done.1 = bf16[4,2,128,1536]{3,2,1,0:T(8,128)(2,1)S(1)} async-done(((bf16[4,2,128,1536]{3,2,1,0:T(8,128)(2,1)}), bf16[4,2,128,1536]{3,2,1,0:T(8,128)(2,1)S(1)}, u32[]{:S(2)}, u32[]{:S(2)}) %all-to-all-start.1) | async-done | bytes 3145760 | tf_op jit(solution)/shard_map/all_to_all | solution.py:1002
  76.0 5.5 %all-to-all-start.2 = ((bf16[16,96,128]{2,1,0:T(8,128)(2,1)}), bf16[16,96,128]{2,1,0:T(8,128)(2,1)}, u32[]{:S(2)}, u32[]{:S(2)}) async-start(bf16[16,96,128]{2,1,0:T(8,128)(2,1)} %copy.62), calls=%async_computation.2 | async-start | bytes 786432 | tf_op jit(solution)/shard_map/all_to_all | solution.py:1002
  86.2 3.3 all-to-all-done.2
  89.4 2.7 all-gather.4.cloned.1.call-done.w_ref.wq_ref.wkv_ref
  93.1 7.7 %project.1 = (bf16[128,1536]{1,0:T(8,128)(2,1)S(1)}, bf16[8,128,1024]{2,1,0:T(8,128)(2,1)S(1)}) custom-call(bf16[1,128,1536]{2,1,0:T(8,128)(2,1)S(1)} %copy-done.19, bf16[8,128,1536]{2,1,0:T(8,128)(2,1)S(1)} %norm_rows.3.seq_ref.hidden_ref, bf16[1536,4096]{1,0:T(8,128)(2,1)} %all-gather.4.cloned.1.call-done.w_ref.wq_ref.wkv_ref), custom_call_target="tpu_custom_call" | custom-call | bytes 29520000 | tf_op jit(solution)/shard_map/project/pallas_call | solution.py:799
  100.8 5.8 %attend.1 = (bf16[128,1536]{1,0:T(8,128)(2,1)S(1)}, f32[128,1536]{1,0:T(8,128)S(1)}, f32[1536,128]{1,0:T(8,128)S(1)}) custom-call(s32[1]{0:T(128)} %bitcast.ctx_ref.refs_0_, bf16[128,1536]{1,0:T(8,128)(2,1)S(1)} %get-tuple-element.106.q_ref, bf16[8,128,1024]{2,1,0:T(8,128)(2,1)S(1)} %get-tuple-element.107.k_ref.v_ref, ...), custom_call_target="tpu_custom_call" | custom-call | bytes 22140000 | tf_op jit(solution)/shard_map/attend/pallas_call | solution.py:99
  106.7 5.4 %copy-done = bf16[1536,4096]{1,0:T(8,128)(2,1)S(1)} copy-done((bf16[1536,4096]{1,0:T(8,128)(2,1)S(1)}, bf16[1536,4096]{1,0:T(8,128)(2,1)}, u32[]{:S(2)}) %copy-start) | copy-done | bytes 12582936
  114.8 20.7 %collective-permute-done.1 = bf16[1,128,1536]{2,1,0:T(8,128)(2,1)S(1)} collective-permute-done((bf16[1,128,1536]{2,1,0:T(8,128)(2,1)S(1)}, bf16[1,128,1536]{2,1,0:T(8,128)(2,1)S(1)}, u32[]{:S(2)}, u32[]{:S(2)}) %collective-permute-start.1) | collective-permute-done | bytes 393248 | tf_op jit(solution)/shard_map/ppermute | solution.py:1054
  137.6 4.8 all-to-all-start.3
  142.4 4.4 all-gather.8.cloned.1.call-done
  146.8 13.7 %place_rows.1 = (bf16[8,2,128,128]{3,2,1,0:T(8,128)(2,1)}, bf16[2,2,384,1536]{3,2,1,0:T(8,128)(2,1)}, f32[2,2,384,512]{3,2,1,0:T(8,128)}, f32[8,2,128,128]{3,2,1,0:T(8,128)}, f32[2,2,384,128]{3,2,1,0:T(8,128)}) custom-call(s32[1]{0:T(128)} %bitcast.7.at_ref, bf16[8,2,128,1664]{3,2,1,0:T(8,128)(2,1)} %bitcast.84, bf16[2,512,1536]{2,1,0:T(8,128)(2,1)} %wd_ref.1, ...), custom_call_target="tpu_custom_call" | custom-call | bytes 51660000 | tf_op jit(solution)/shard_map/place_rows/pallas_call | solution.py:368
  160.5 19.3 %all-to-all-done.3 = bf16[4,2,128,1536]{3,2,1,0:T(8,128)(2,1)} async-done(((bf16[4,2,128,1536]{3,2,1,0:T(8,128)(2,1)}), bf16[4,2,128,1536]{3,2,1,0:T(8,128)(2,1)}, u32[]{:S(2)}, u32[]{:S(2)}) %all-to-all-start.3) | async-done | bytes 3145760 | tf_op jit(solution)/shard_map/all_to_all | solution.py:1002
  179.8 12.3 %all-gather.6.cloned.1.call-done = bf16[2048,1536]{1,0:T(8,128)(2,1)} async-done(((bf16[128,1536]{1,0:T(8,128)(2,1)}), bf16[2048,1536]{1,0:T(8,128)(2,1)}) %all-gather.6.cloned.1.call-update) | async-done | bytes 6291472 | tf_op jit(solution)/shard_map/all_gather | solution.py:1077
  192.1 29.0 %expert_back.1 = (bf16[2,8,128,1536]{3,2,1,0:T(8,128)(2,1)}, bf16[2,2,384,1536]{3,2,1,0:T(8,128)(2,1)}, bf16[2,2,384,512]{3,2,1,0:T(8,128)(2,1)}, bf16[2,2,384,1...) custom-call(s32[1]{0:T(128)} %bitcast.7.at_ref, ...), custom_call_target="tpu_custom_call" | custom-call | bytes 103320000 | tf_op jit(solution)/shard_map/expert_back/pallas_call | solution.py:447
  223.6 5.5 %collective-permute-done.2 = bf16[8,128,1536]{2,1,0:T(8,128)(2,1)S(1)} collective-permute-done((bf16[8,128,1536]{2,1,0:T(8,128)(2,1)S(1)}, bf16[8,128,1536]{2,1,0:T(8,128)(2,1)S(1)}, u32[]{:S(2)}, u32[]{:S(2)}) %collective-permute-start.2) | collective-permute-done | bytes 3145760 | tf_op jit(solution)/shard_map/ppermute | solution.py:1089
  229.1 2.6 fusion
  231.7 5.5 %all-to-all-start.4 = ((bf16[8,128,1536]{2,1,0:T(8,128)(2,1)}), bf16[8,128,1536]{2,1,0:T(8,128)(2,1)}, u32[]{:S(2)}, u32[]{:S(2)}) async-start(bf16[8,128,1536]{2,1,0:T(8,128)(2,1)} %fusion), calls=%async_computation.4 | async-start | bytes 6291456 | tf_op jit(solution)/shard_map/all_to_all | solution.py:1002
  237.1 10.9 %expert_weights.2 = (bf16[9216,128]{1,0:T(8,128)(2,1)}, bf16[9216,128]{1,0:T(8,128)(2,1)}) custom-call(s32[1]{0:T(128)} %bitcast.ctx_ref.refs_0_, bf16[2,768,1536]{2,1,0:T(8,128)(2,1)} %bitcast.91, bf16[2,768,1536]{2,1,0:T(8,128)(2,1)} %bitcast.89, bf16[2,768,512]{2,1,0:T(8,128)(2,1)} %bitcast.74, bf16[2,768,1024]{2,1,0:T(8,128)(2,1)} %bitcast.85, ...), custom_call_target="tpu_custom_call" | custom-call | bytes 7380000 | tf_op jit(solution)/shard_map/expert_weights/pallas_call | solution.py:899
  249.6 11.4 %expert_weights.3 = (bf16[4608,128]{1,0:T(8,128)(2,1)}, bf16[4608,128]{1,0:T(8,128)(2,1)}, bf16[4608,128]{1,0:T(8,128)(2,1)}, bf16[4608,128]{1,0:T(8,128)(2,1)}) custom-call(s32[1]{0:T(128)} %bitcast.ctx_ref.refs_0_, bf16[2,768,1536]{2,1,0:T(8,128)(2,1)} %bitcast.92, bf16[2,768,1536]{2,1,0:T(8,128)(2,1)} %bitcast.90, bf16[2,768,512]{2,1,0:T(8,128)(2,1)} %bitcast.75, ...), custom_call_target="tpu_custom_call" | custom-call | bytes 7380000 | tf_op jit(solution)/shard_map/expert_weights/pallas_call | solution.py:899
  263.3 2.6 convolution_convert_fusion
  270.4 9.8 %expert_output.1.own_ref = bf16[2,8,128,1536]{3,2,1,0:T(8,128)(2,1)} custom-call(s32[1]{0:T(128)} %bitcast.7.at_ref, bf16[2,2,384,512]{3,2,1,0:T(8,128)(2,1)S(1)} %copy-done.3, f32[2,2,384,128]{3,2,1,0:T(8,128)S(1)} %copy-done.33, bf16[8,2,128,128]{3,2,1,0:T(8,128)(2,1)S(1)} %copy-done.13, bf16[8,2,128,128]{3,2,1,0:T(8,128)(2,1)S(1)} %copy-done.7, ...), custom_call_target="tpu_custom_call" | custom-call | bytes 7380000 | tf_op jit(solution)/shard_map/expert_output/pallas_call | solution.py:499
  280.2 4.1 fusion.8
  286.2 5.7 %middle_back.1 = (f32[128,1536]{1,0:T(8,128)S(1)}, bf16[128,1536]{1,0:T(8,128)(2,1)S(1)}, bf16[128,1536]{1,0:T(8,128)(2,1)S(1)}, f32[16,128]{1,0:T(8,128)S(1)}) custom-call(bf16[8,128,1536]{2,1,0:T(8,128)(2,1)} %all-to-all-done.4.pieces_ref, f32[128,1536]{1,0:T(8,128)S(1)} %get-tuple-element.109.middle_ref, bf16[128,1536]{1,0:T(8,128)(2,1)S(1)} %bitcast.81, ...), custom_call_target="tpu_custom_call" | custom-call | bytes 3690000 | tf_op jit(solution)/shard_map/middle_back/pallas_call | solution.py:290
  295.1 9.0 %attend_back.1 = (bf16[128,1536]{1,0:T(8,128)(2,1)S(1)}, bf16[4,1776,128]{2,1,0:T(8,128)(2,1)S(1)}, bf16[4,1776,128]{2,1,0:T(8,128)(2,1)}) custom-call(s32[1]{0:T(128)} %bitcast.ctx_ref.refs_0_, bf16[128,1536]{1,0:T(8,128)(2,1)S(1)} %copy-done.15, bf16[128,1536]{1,0:T(8,128)(2,1)S(1)} %get-tuple-element.137.ga_ref, f32[128,1536]{1,0:T(8,128)S(1)} %copy-done.30, ...), custom_call_target="tpu_custom_call" | custom-call | bytes 7380000 | tf_op jit(solution)/shard_map/attend_back/pallas_call | solution.py:202
  304.8 3.1 collective-permute-start.9
  310.5 4.8 collective-permute-done.4.relay_b.got_31
  315.3 3.5 piece_sums.2
  327.6 17.9 %collective-permute-done.10.got_11 = bf16[4608,128]{1,0:T(8,128)(2,1)S(1)} collective-permute-done((bf16[4608,128]{1,0:T(8,128)(2,1)S(1)}, bf16[4608,128]{1,0:T(8,128)(2,1)S(1)}, u32[]{:S(2)}, u32[]{:S(2)}) %collective-permute-start.10) | collective-permute-done | bytes 1179680 | tf_op jit(solution)/shard_map/ppermute | solution.py:1104
  349.2 2.9 collective-permute-start.12
  355.5 4.5 all-to-all-start.5
  360.0 16.6 %collective-permute-done.12 = bf16[4608,128]{1,0:T(8,128)(2,1)S(1)} collective-permute-done((bf16[4608,128]{1,0:T(8,128)(2,1)S(1)}, bf16[4608,128]{1,0:T(8,128)(2,1)S(1)}, u32[]{:S(2)}, u32[]{:S(2)}) %collective-permute-start.12) | collective-permute-done | bytes 1179680 | tf_op jit(solution)/shard_map/ppermute | solution.py:1104
  380.7 2.8 collective-permute-start.17
  384.9 4.2 all-to-all-done.5.got_ref
  389.1 7.1 %column_grads.1 = (bf16[16,112,512]{2,1,0:T(8,128)(2,1)}, bf16[8,128,128]{2,1,0:T(8,128)(2,1)}, bf16[96,128]{1,0:T(8,128)(2,1)}) custom-call(bf16[4,2160,128]{2,1,0:T(8,128)(2,1)} %all-to-all-done.5.got_ref, bf16[8,128,1536]{2,1,0:T(8,128)(2,1)} %copy-done.2, bf16[8,128,1536]{2,1,0:T(8,128)(2,1)} %bitcast.10.att_ref), custom_call_target="tpu_custom_call" | custom-call | bytes 29520000 | tf_op jit(solution)/shard_map/column_grads/pallas_call | solution.py:614
  396.2 5.1 collective-permute-done.13
  401.3 8.3 %collective-permute-done.15.refs_2_ = bf16[4608,128]{1,0:T(8,128)(2,1)S(1)} collective-permute-done((bf16[4608,128]{1,0:T(8,128)(2,1)S(1)}, bf16[4608,128]{1,0:T(8,128)(2,1)S(1)}, u32[]{:S(2)}, u32[]{:S(2)}) %collective-permute-start.15) | collective-permute-done | bytes 1179680 | tf_op jit(solution)/shard_map/ppermute | solution.py:1104
  411.1 5.1 all-to-all-start.6
  423.6 15.4 %all-to-all-done.6.got_ref = bf16[16,112,512]{2,1,0:T(8,128)(2,1)S(1)} async-done(((bf16[16,112,512]{2,1,0:T(8,128)(2,1)}), bf16[16,112,512]{2,1,0:T(8,128)(2,1)S(1)}, u32[]{:S(2)}, u32[]{:S(2)}) %all-to-all-start.6) | async-done | bytes 1835040 | tf_op jit(solution)/shard_map/all_to_all | solution.py:1002
  439.3 7.9 %collective-permute-done.14 = bf16[128,1536]{1,0:T(8,128)(2,1)} collective-permute-done((bf16[128,1536]{1,0:T(8,128)(2,1)}, bf16[128,1536]{1,0:T(8,128)(2,1)}, u32[]{:S(2)}, u32[]{:S(2)}) %collective-permute-start.14) | collective-permute-done | bytes 393248 | tf_op jit(solution)/shard_map/ppermute | solution.py:1174
  448.7 4.8 all-to-all-start.7
  460.4 42.1 %collective-permute-done.21.refs_4_ = bf16[4608,128]{1,0:T(8,128)(2,1)} collective-permute-done((bf16[4608,128]{1,0:T(8,128)(2,1)}, bf16[4608,128]{1,0:T(8,128)(2,1)}, u32[]{:S(2)}, u32[]{:S(2)}) %collective-permute-start.21) | collective-permute-done | bytes 1179680 | tf_op jit(solution)/shard_map/ppermute | solution.py:1104
  502.5 5.5 %unpack_experts.2 = (f32[2,1536,512]{2,1,0:T(8,128)}, f32[2,1536,512]{2,1,0:T(8,128)}, f32[2,512,1536]{2,1,0:T(8,128)}) custom-call(s32[1]{0:T(128)} %bitcast.ctx_ref.refs_0_, bf16[4608,128]{1,0:T(8,128)(2,1)S(1)} %add_convert_fusion.refs_1_, bf16[4608,128]{1,0:T(8,128)(2,1)S(1)} %copy-done.28, bf16[4608,128]{1,0:T(8,128)(2,1)} %collective-permute-done.16.refs_3_, ...), custom_call_target="tpu_custom_call" | custom-call | bytes 29520000 | tf_op jit(solution)/shard_map/unpack_experts/pallas_call | solution.py:943
  508.5 6.4 %unpack_experts.3 = (f32[2,1536,512]{2,1,0:T(8,128)}, f32[2,1536,512]{2,1,0:T(8,128)}, f32[2,512,1536]{2,1,0:T(8,128)}) custom-call(s32[1]{0:T(128)} %bitcast.ctx_ref.refs_0_, bf16[4608,128]{1,0:T(8,128)(2,1)} %collective-permute-done.17.refs_1_, ...), custom_call_target="tpu_custom_call", output_to_operand_aliasing={{0}: (5, {}), {1}: (6, {}), {2}: (7, {})} | custom-call | bytes 29520000 | tf_op jit(solution)/shard_map/unpack_experts/pallas_call | solution.py:943
  517.5 7.0 %input_back.1 = bf16[128,1536]{1,0:T(8,128)(2,1)} custom-call(bf16[128,1536]{1,0:T(8,128)(2,1)S(1)} %copy-done.37, bf16[8,864,128]{2,1,0:T(8,128)(2,1)S(1)} %all-to-all-done.7.got_ref, bf16[1536,4096]{1,0:T(8,128)(2,1)} %all-gather.4.cloned.1.call-done.w_ref.wq_ref.wkv_ref, bf16[1536,4096]{1,0:T(8,128)(2,1)} %all-gather.4.cloned.1.call-done.w_ref.wq_ref.wkv_ref, ...), custom_call_target="tpu_custom_call" | custom-call | bytes 25830000 | tf_op jit(solution)/shard_map/input_back/pallas_call | solution.py:743
  (204 shorter events, 90.4 us)
Async XLA Ops:
  7.2 10.0 %copy-start.50 = (bf16[96]{0:T(256)(128)(2,1)S(1)}, bf16[96]{0:T(256)(128)(2,1)}, u32[]{:S(2)}) copy-start(bf16[96]{0:T(256)(128)(2,1)} %param.19) | copy-start | bytes 580
  7.2 10.0 %copy-start.49 = (bf16[96]{0:T(256)(128)(2,1)S(1)}, bf16[96]{0:T(256)(128)(2,1)}, u32[]{:S(2)}) copy-start(bf16[96]{0:T(256)(128)(2,1)} %param.20) | copy-start | bytes 580
  7.2 84.9 %all-gather.4.cloned.1.call-start = ((), (), s32[]{:S(2)}) async-start(), calls=%async_computation.8 | async-start | bytes 13369344 | tf_op jit(solution)/shard_map/all_gather | solution.py:1040
  12.0 134.8 %all-gather.8.cloned.1.call-start = ((), (), s32[]{:S(2)}) async-start(), calls=%async_computation.10 | async-start | bytes 7241728 | tf_op jit(solution)/shard_map/all_gather | solution.py:1047
  13.3 15.5 %collective-permute-start = (bf16[1,128,1536]{2,1,0:T(8,128)(2,1)S(1)}, bf16[1,128,1536]{2,1,0:T(8,128)(2,1)S(1)}, u32[]{:S(2)}, u32[]{:S(2)}) collective-permute-start(bf16[1,128,1536]{2,1,0:T(8,128)(2,1)S(1)} %copy-done.6), channel_id=1, source_target_pairs={{0,64},{16,80},{32,96},{48,112},{64,0},{80,16},{96,32},{112,48},{1... | collective-permute-start | bytes 1179656 | tf_op jit(solution)/shard_map/ppermute | solution.py:1054
  17.9 11.8 %all-to-all-start = ((bf16[16,1,192]{2,1,0:T(2,128)(2,1)}), bf16[16,1,192]{2,1,0:T(2,128)(2,1)S(1)}, u32[]{:S(2)}, u32[]{:S(2)}) async-start(bf16[16,1,192]{2,1,0:T(2,128)(2,1)} %broadcast_in_dim.24), calls=%async_computation | async-start | bytes 32768 | tf_op jit(solution)/shard_map/all_to_all | solution.py:1002
  31.7 42.6 %all-to-all-start.1 = ((bf16[4,2,128,1536]{3,2,1,0:T(8,128)(2,1)}), bf16[4,2,128,1536]{3,2,1,0:T(8,128)(2,1)S(1)}, u32[]{:S(2)}, u32[]{:S(2)}) async-start(bf16[4,2,128,1536]{3,2,1,0:T(8,128)(2,1)} %broadcast_in_dim.25), calls=%async_computation.1 | async-start | bytes 6291456 | tf_op jit(solution)/shard_map/all_to_all | solution.py:1002
  76.0 13.5 %all-to-all-start.2 = ((bf16[16,96,128]{2,1,0:T(8,128)(2,1)}), bf16[16,96,128]{2,1,0:T(8,128)(2,1)}, u32[]{:S(2)}, u32[]{:S(2)}) async-start(bf16[16,96,128]{2,1,0:T(8,128)(2,1)} %copy.62), calls=%async_computation.2 | async-start | bytes 786432 | tf_op jit(solution)/shard_map/all_to_all | solution.py:1002
  81.5 110.7 %all-gather.6.cloned.1.call-start = ((), (), s32[]{:S(2)}) async-start(), calls=%async_computation.9 | async-start | bytes 6684672 | tf_op jit(solution)/shard_map/all_gather | solution.py:1077
  86.2 14.6 %copy-start.2 = (bf16[8,128,1536]{2,1,0:T(8,128)(2,1)}, bf16[8,128,1536]{2,1,0:T(8,128)(2,1)S(1)}, u32[]{:S(2)}) copy-start(bf16[8,128,1536]{2,1,0:T(8,128)(2,1)S(1)} %norm_rows.3.seq_ref.hidden_ref) | copy-start | bytes 9437188
  113.7 171.4 %copy-start.8 = (f32[128,1536]{1,0:T(8,128)}, f32[128,1536]{1,0:T(8,128)S(1)}, u32[]{:S(2)}) copy-start(f32[128,1536]{1,0:T(8,128)S(1)} %get-tuple-element.109.middle_ref) | copy-start | bytes 2359300
  113.8 21.7 %collective-permute-start.1 = (bf16[1,128,1536]{2,1,0:T(8,128)(2,1)S(1)}, bf16[1,128,1536]{2,1,0:T(8,128)(2,1)S(1)}, u32[]{:S(2)}, u32[]{:S(2)}) collective-permute-start(bf16[1,128,1536]{2,1,0:T(8,128)(2,1)S(1)} %bitcast.82), channel_id=1, source_target_pairs={{0,64},{16,80},{32,96},{48,112},{64,0},{80,16},{96,32},{112,48},{1... | collective-permute-start | bytes 1179656 | tf_op jit(solution)/shard_map/ppermute | solution.py:1054
  137.6 42.3 %all-to-all-start.3 = ((bf16[4,2,128,1536]{3,2,1,0:T(8,128)(2,1)}), bf16[4,2,128,1536]{3,2,1,0:T(8,128)(2,1)}, u32[]{:S(2)}, u32[]{:S(2)}) async-start(bf16[4,2,128,1536]{3,2,1,0:T(8,128)(2,1)} %broadcast_in_dim.27), calls=%async_computation.3 | async-start | bytes 6291456 | tf_op jit(solution)/shard_map/all_to_all | solution.py:1002
  223.3 5.7 %collective-permute-start.2 = (bf16[8,128,1536]{2,1,0:T(8,128)(2,1)S(1)}, bf16[8,128,1536]{2,1,0:T(8,128)(2,1)S(1)}, u32[]{:S(2)}, u32[]{:S(2)}) collective-permute-start(bf16[8,128,1536]{2,1,0:T(8,128)(2,1)S(1)} %slice_bitcast_fusion), channel_id=1, source_target_pairs={{0,1},{1,0},{2,3},{3,2},{4,5},{5,4},{6,7},{7,6},{8,9},{9,8},{10,11... | collective-permute-start | bytes 9437192 | tf_op jit(solution)/shard_map/ppermute | solution.py:1089
  231.7 53.5 %all-to-all-start.4 = ((bf16[8,128,1536]{2,1,0:T(8,128)(2,1)}), bf16[8,128,1536]{2,1,0:T(8,128)(2,1)}, u32[]{:S(2)}, u32[]{:S(2)}) async-start(bf16[8,128,1536]{2,1,0:T(8,128)(2,1)} %fusion), calls=%async_computation.4 | async-start | bytes 6291456 | tf_op jit(solution)/shard_map/all_to_all | solution.py:1002
  248.0 15.3 %slice-start.2 = ((s8[6291456]{0:T(1024)(128)(4,1)}), s8[4194304]{0:T(1024)(128)(4,1)S(1)}, s32[]{:S(2)}) async-start(s8[6291456]{0:T(1024)(128)(4,1)} %bitcast.94), calls=%async_computation.13 | async-start | bytes 8388608
  248.0 15.3 %slice-start.3 = ((s8[6291456]{0:T(1024)(128)(4,1)}), s8[2097152]{0:T(1024)(128)(4,1)S(1)}, s32[]{:S(2)}) async-start(s8[6291456]{0:T(1024)(128)(4,1)} %bitcast.94), calls=%async_computation.14 | async-start | bytes 4194304
  248.0 15.3 %copy-start.48 = (bf16[8,2,128,128]{3,2,1,0:T(8,128)(2,1)S(1)}, bf16[8,2,128,128]{3,2,1,0:T(8,128)(2,1)}, u32[]{:S(2)}) copy-start(bf16[8,2,128,128]{3,2,1,0:T(8,128)(2,1)} %get-tuple-element.134) | copy-start | bytes 1572868
  248.0 62.4 %collective-permute-start.3 = (bf16[9216,128]{1,0:T(8,128)(2,1)}, bf16[9216,128]{1,0:T(8,128)(2,1)}, u32[]{:S(2)}, u32[]{:S(2)}) collective-permute-start(bf16[9216,128]{1,0:T(8,128)(2,1)} %get-tuple-element.123), channel_id=1, source_target_pairs={{0,16},{16,0},{32,48},{48,32},{64,80},{80,64},{96,112},{112,96},{1... | collective-permute-start | bytes 7077896 | tf_op jit(solution)/shard_map/ppermute | solution.py:1104
  261.0 54.3 %collective-permute-start.4 = (bf16[9216,128]{1,0:T(8,128)(2,1)}, bf16[9216,128]{1,0:T(8,128)(2,1)}, u32[]{:S(2)}, u32[]{:S(2)}) collective-permute-start(bf16[9216,128]{1,0:T(8,128)(2,1)} %get-tuple-element.132), channel_id=1, source_target_pairs={{0,48},{16,32},{32,16},{48,0},{64,112},{80,96},{96,80},{112,64},{1... | collective-permute-start | bytes 7077896 | tf_op jit(solution)/shard_map/ppermute | solution.py:1104
  284.3 23.7 %slice-start = ((s8[6291456]{0:T(1024)(128)(4,1)}), s8[2097152]{0:T(1024)(128)(4,1)S(1)}, s32[]{:S(2)}) async-start(s8[6291456]{0:T(1024)(128)(4,1)} %bitcast.72), calls=%async_computation.11 | async-start | bytes 4194304
  286.2 21.8 %slice-start.1 = ((s8[6291456]{0:T(1024)(128)(4,1)}), s8[4194304]{0:T(1024)(128)(4,1)S(1)}, s32[]{:S(2)}) async-start(s8[6291456]{0:T(1024)(128)(4,1)} %bitcast.72), calls=%async_computation.12 | async-start | bytes 8388608
  304.8 10.5 %copy-start.22 = (bf16[4608,128]{1,0:T(8,128)(2,1)S(1)}, bf16[4608,128]{1,0:T(8,128)(2,1)}, u32[]{:S(2)}) copy-start(bf16[4608,128]{1,0:T(8,128)(2,1)} %get-tuple-element.125.p0) | copy-start | bytes 3538948
  304.8 10.5 %copy-start.23 = (bf16[4608,128]{1,0:T(8,128)(2,1)S(1)}, bf16[4608,128]{1,0:T(8,128)(2,1)}, u32[]{:S(2)}) copy-start(bf16[4608,128]{1,0:T(8,128)(2,1)} %get-tuple-element.131.p6) | copy-start | bytes 3538948
  304.8 10.5 %copy-start.24 = (bf16[4608,128]{1,0:T(8,128)(2,1)S(1)}, bf16[4608,128]{1,0:T(8,128)(2,1)}, u32[]{:S(2)}) copy-start(bf16[4608,128]{1,0:T(8,128)(2,1)} %get-tuple-element.129.p1) | copy-start | bytes 3538948
  304.8 10.5 %copy-start.25 = (bf16[4608,128]{1,0:T(8,128)(2,1)S(1)}, bf16[4608,128]{1,0:T(8,128)(2,1)}, u32[]{:S(2)}) copy-start(bf16[4608,128]{1,0:T(8,128)(2,1)} %get-tuple-element.130.p3) | copy-start | bytes 3538948
  304.8 42.5 %collective-permute-start.9 = (bf16[4,1776,128]{2,1,0:T(8,128)(2,1)}, bf16[4,1776,128]{2,1,0:T(8,128)(2,1)S(1)}, u32[]{:S(2)}, u32[]{:S(2)}) collective-permute-start(bf16[4,1776,128]{2,1,0:T(8,128)(2,1)} %get-tuple-element.150), channel_id=1, source_target_pairs={{0,64},{16,80},{32,96},{48,112},{64,0},{80,16},{96,32},{112,48},{1... | collective-permute-start | bytes 5455880 | tf_op jit(solution)/shard_map/ppermute | solution.py:1132
  310.0 11.0 %collective-permute-start.5 = (bf16[4,128,1536]{2,1,0:T(8,128)(2,1)}, bf16[4,128,1536]{2,1,0:T(8,128)(2,1)S(1)}, u32[]{:S(2)}, u32[]{:S(2)}) collective-permute-start(bf16[4,128,1536]{2,1,0:T(8,128)(2,1)} %get-tuple-element.195), channel_id=1, source_target_pairs={{0,1},{1,0},{2,3},{3,2},{4,5},{5,4},{6,7},{7,6},{8,9},{9,8},{10,11... | collective-permute-start | bytes 4718600 | tf_op jit(solution)/shard_map/ppermute | solution.py:1154
  310.0 11.0 %collective-permute-start.6 = (bf16[4,128,1536]{2,1,0:T(8,128)(2,1)}, bf16[4,128,1536]{2,1,0:T(8,128)(2,1)S(1)}, u32[]{:S(2)}, u32[]{:S(2)}) collective-permute-start(bf16[4,128,1536]{2,1,0:T(8,128)(2,1)} %get-tuple-element.194), channel_id=1, source_target_pairs={{0,1},{1,0},{2,3},{3,2},{4,5},{5,4},{6,7},{7,6},{8,9},{9,8},{10,11... | collective-permute-start | bytes 4718600 | tf_op jit(solution)/shard_map/ppermute | solution.py:1155
  318.8 26.7 %collective-permute-start.10 = (bf16[4608,128]{1,0:T(8,128)(2,1)S(1)}, bf16[4608,128]{1,0:T(8,128)(2,1)S(1)}, u32[]{:S(2)}, u32[]{:S(2)}) collective-permute-start(bf16[4608,128]{1,0:T(8,128)(2,1)S(1)} %get-tuple-element.153), channel_id=1, source_target_pairs={{0,16},{16,0},{32,48},{48,32},{64,80},{80,64},{96,112},{112,96},{1... | collective-permute-start | bytes 3538952 | tf_op jit(solution)/shard_map/ppermute | solution.py:1104
  318.9 27.9 %collective-permute-start.11 = (bf16[4608,128]{1,0:T(8,128)(2,1)S(1)}, bf16[4608,128]{1,0:T(8,128)(2,1)S(1)}, u32[]{:S(2)}, u32[]{:S(2)}) collective-permute-start(bf16[4608,128]{1,0:T(8,128)(2,1)S(1)} %get-tuple-element.145), channel_id=1, source_target_pairs={{0,48},{16,32},{32,16},{48,0},{64,112},{80,96},{96,80},{112,64},{1... | collective-permute-start | bytes 3538952 | tf_op jit(solution)/shard_map/ppermute | solution.py:1104
  325.5 26.6 %collective-permute-start.7 = (bf16[2,128,1536]{2,1,0:T(8,128)(2,1)S(1)}, bf16[2,128,1536]{2,1,0:T(8,128)(2,1)S(1)}, u32[]{:S(2)}, u32[]{:S(2)}) collective-permute-start(bf16[2,128,1536]{2,1,0:T(8,128)(2,1)S(1)} %get-tuple-element.148), channel_id=1, source_target_pairs={{0,4},{1,5},{2,6},{3,7},{4,0},{5,1},{6,2},{7,3},{8,12},{9,13},{10,... | collective-permute-start | bytes 2359304 | tf_op jit(solution)/shard_map/ppermute | solution.py:1149
  326.4 25.6 %collective-permute-start.8 = (bf16[2,128,1536]{2,1,0:T(8,128)(2,1)S(1)}, bf16[2,128,1536]{2,1,0:T(8,128)(2,1)S(1)}, u32[]{:S(2)}, u32[]{:S(2)}) collective-permute-start(bf16[2,128,1536]{2,1,0:T(8,128)(2,1)S(1)} %get-tuple-element.149), channel_id=1, source_target_pairs={{0,12},{1,13},{2,14},{3,15},{4,8},{5,9},{6,10},{7,11},{8,4},{9,5},... | collective-permute-start | bytes 2359304 | tf_op jit(solution)/shard_map/ppermute | solution.py:1149
  349.2 27.4 %collective-permute-start.12 = (bf16[4608,128]{1,0:T(8,128)(2,1)S(1)}, bf16[4608,128]{1,0:T(8,128)(2,1)S(1)}, u32[]{:S(2)}, u32[]{:S(2)}) collective-permute-start(bf16[4608,128]{1,0:T(8,128)(2,1)S(1)} %get-tuple-element.156), channel_id=1, source_target_pairs={{0,64},{16,80},{32,96},{48,112},{64,0},{80,16},{96,32},{112,48},{1... | collective-permute-start | bytes 3538952 | tf_op jit(solution)/shard_map/ppermute | solution.py:1104
  355.5 33.6 %all-to-all-start.5 = ((bf16[4,2160,128]{2,1,0:T(8,128)(2,1)}), bf16[4,2160,128]{2,1,0:T(8,128)(2,1)}, u32[]{:S(2)}, u32[]{:S(2)}) async-start(bf16[4,2160,128]{2,1,0:T(8,128)(2,1)} %merge_shares.1), calls=%async_computation.5 | async-start | bytes 4423680 | tf_op jit(solution)/shard_map/all_to_all | solution.py:1002
  378.5 31.0 %collective-permute-start.15 = (bf16[4608,128]{1,0:T(8,128)(2,1)S(1)}, bf16[4608,128]{1,0:T(8,128)(2,1)S(1)}, u32[]{:S(2)}, u32[]{:S(2)}) collective-permute-start(bf16[4608,128]{1,0:T(8,128)(2,1)S(1)} %add_convert_fusion.refs_1_), channel_id=1, source_target_pairs={{0,16},{16,0},{32,48},{48,32},{64,80},{80,64},{96,112},{112,96},{1... | collective-permute-start | bytes 3538952 | tf_op jit(solution)/shard_map/ppermute | solution.py:1104
  379.5 31.7 %collective-permute-start.16 = (bf16[4608,128]{1,0:T(8,128)(2,1)S(1)}, bf16[4608,128]{1,0:T(8,128)(2,1)}, u32[]{:S(2)}, u32[]{:S(2)}) collective-permute-start(bf16[4608,128]{1,0:T(8,128)(2,1)S(1)} %add_convert_fusion.refs_1_), channel_id=1, source_target_pairs={{0,48},{16,32},{32,16},{48,0},{64,112},{80,96},{96,80},{112,64},{1... | collective-permute-start | bytes 3538952 | tf_op jit(solution)/shard_map/ppermute | solution.py:1104
  380.7 35.6 %collective-permute-start.17 = (bf16[4608,128]{1,0:T(8,128)(2,1)S(1)}, bf16[4608,128]{1,0:T(8,128)(2,1)}, u32[]{:S(2)}, u32[]{:S(2)}) collective-permute-start(bf16[4608,128]{1,0:T(8,128)(2,1)S(1)} %add_convert_fusion.refs_1_), channel_id=1, source_target_pairs={{0,64},{16,80},{32,96},{48,112},{64,0},{80,16},{96,32},{112,48},{1... | collective-permute-start | bytes 3538952 | tf_op jit(solution)/shard_map/ppermute | solution.py:1104
  383.5 17.8 %collective-permute-start.13 = (bf16[2,128,1536]{2,1,0:T(8,128)(2,1)S(1)}, bf16[2,128,1536]{2,1,0:T(8,128)(2,1)}, u32[]{:S(2)}, u32[]{:S(2)}) collective-permute-start(bf16[2,128,1536]{2,1,0:T(8,128)(2,1)S(1)} %get-tuple-element.164), channel_id=1, source_target_pairs={{0,8},{1,9},{2,10},{3,11},{4,12},{5,13},{6,14},{7,15},{8,0},{9,1},... | collective-permute-start | bytes 2359304 | tf_op jit(solution)/shard_map/ppermute | solution.py:1149
  411.1 27.9 %all-to-all-start.6 = ((bf16[16,112,512]{2,1,0:T(8,128)(2,1)}), bf16[16,112,512]{2,1,0:T(8,128)(2,1)S(1)}, u32[]{:S(2)}, u32[]{:S(2)}) async-start(bf16[16,112,512]{2,1,0:T(8,128)(2,1)} %get-tuple-element.167), calls=%async_computation.6 | async-start | bytes 3670016 | tf_op jit(solution)/shard_map/all_to_all | solution.py:1002
  416.3 22.8 %copy-start.40 = (bf16[96,128]{1,0:T(8,128)(2,1)S(1)}, bf16[96,128]{1,0:T(8,128)(2,1)}, u32[]{:S(2)}) copy-start(bf16[96,128]{1,0:T(8,128)(2,1)} %get-tuple-element.168.down_ref) | copy-start | bytes 73732
  416.3 30.8 %collective-permute-start.18 = (bf16[4608,128]{1,0:T(8,128)(2,1)}, bf16[4608,128]{1,0:T(8,128)(2,1)}, u32[]{:S(2)}, u32[]{:S(2)}) collective-permute-start(bf16[4608,128]{1,0:T(8,128)(2,1)} %collective-permute-done.17.refs_1_), channel_id=1, source_target_pairs={{0,16},{16,0},{32,48},{48,32},{64,80},{80,64},{96,112},{112,96},{1... | collective-permute-start | bytes 3538952 | tf_op jit(solution)/shard_map/ppermute | solution.py:1104
  416.9 30.2 %collective-permute-start.19 = (bf16[4608,128]{1,0:T(8,128)(2,1)}, bf16[4608,128]{1,0:T(8,128)(2,1)}, u32[]{:S(2)}, u32[]{:S(2)}) collective-permute-start(bf16[4608,128]{1,0:T(8,128)(2,1)} %collective-permute-done.17.refs_1_), channel_id=1, source_target_pairs={{0,48},{16,32},{32,16},{48,0},{64,112},{80,96},{96,80},{112,64},{1... | collective-permute-start | bytes 3538952 | tf_op jit(solution)/shard_map/ppermute | solution.py:1104
  422.2 24.9 %collective-permute-start.14 = (bf16[128,1536]{1,0:T(8,128)(2,1)}, bf16[128,1536]{1,0:T(8,128)(2,1)}, u32[]{:S(2)}, u32[]{:S(2)}) collective-permute-start(bf16[128,1536]{1,0:T(8,128)(2,1)} %fusion.5), channel_id=1, source_target_pairs={{0,2},{1,3},{2,0},{3,1},{4,6},{5,7},{6,4},{7,5},{8,10},{9,11},{10,... | collective-permute-start | bytes 1179656 | tf_op jit(solution)/shard_map/ppermute | solution.py:1174
  448.7 66.2 %all-to-all-start.7 = ((bf16[8,864,128]{2,1,0:T(8,128)(2,1)}), bf16[8,864,128]{2,1,0:T(8,128)(2,1)S(1)}, u32[]{:S(2)}, u32[]{:S(2)}) async-start(bf16[8,864,128]{2,1,0:T(8,128)(2,1)} %pad_maximum_fusion), calls=%async_computation.7 | async-start | bytes 3538944 | tf_op jit(solution)/shard_map/all_to_all | solution.py:1002
  453.5 49.0 %collective-permute-start.21 = (bf16[4608,128]{1,0:T(8,128)(2,1)}, bf16[4608,128]{1,0:T(8,128)(2,1)}, u32[]{:S(2)}, u32[]{:S(2)}) collective-permute-start(bf16[4608,128]{1,0:T(8,128)(2,1)} %collective-permute-done.16.refs_3_), channel_id=1, source_target_pairs={{0,16},{16,0},{32,48},{48,32},{64,80},{80,64},{96,112},{112,96},{1... | collective-permute-start | bytes 3538952 | tf_op jit(solution)/shard_map/ppermute | solution.py:1104
  455.5 53.0 %collective-permute-start.20 = (bf16[4608,128]{1,0:T(8,128)(2,1)}, bf16[4608,128]{1,0:T(8,128)(2,1)}, u32[]{:S(2)}, u32[]{:S(2)}) collective-permute-start(bf16[4608,128]{1,0:T(8,128)(2,1)} %collective-permute-done.18.refs_2_), channel_id=1, source_target_pairs={{0,48},{16,32},{32,16},{48,0},{64,112},{80,96},{96,80},{112,64},{1... | collective-permute-start | bytes 3538952 | tf_op jit(solution)/shard_map/ppermute | solution.py:1104
  457.9 44.6 %copy-start.28 = (bf16[4608,128]{1,0:T(8,128)(2,1)S(1)}, bf16[4608,128]{1,0:T(8,128)(2,1)}, u32[]{:S(2)}) copy-start(bf16[4608,128]{1,0:T(8,128)(2,1)} %copy-done.27) | copy-start | bytes 3538948
  (41 other events, 152.3 us)
Sparse Core Ops, SparseCore 0:
  12.2 79.9 all-gather.3
  94.4 52.3 all-gather.7
  149.1 42.9 all-gather.5

commit v14 on v13

--- a/solution.py
+++ b/solution.py
@@ -223,7 +223,7 @@
         ],
         scratch_shapes=[pltpu.VMEM((KV_HEADS, BLOCK, GROUP * HEAD_DIM), f32)],
         cost_estimate=cost(2),
-        compiler_params=params(48),
+        compiler_params=params(60),
         name="attend_back",
     )(ctx_at, qkv, grad_att, att_f, logs, kv_all, kv_all, grad_attn, extra, gain_rows)
 
@@ -255,7 +255,7 @@
             jax.ShapeDtypeStruct((BLOCK, WIDTH), bf16),
         ],
         cost_estimate=cost(2),
-        compiler_params=params(32),
+        compiler_params=params(60),
         name="middle_norm",
     )(attended, w_all, tokens, gain)
 
@@ -1183,20 +1183,21 @@
     at_2, at_z2 = to(at_3, 1), to(at_z1, 3)
     mixed = (middle + out_rows[0] + out_across.astype(f32)).astype(bf16)[None]
     experts = unpack_experts(
-        ctx_s, ((0, 0), (1, 0), (3, 0), (2, 0)), (after(own, owned), at_1, at_3, at_2)
+        ctx_s, ((0, 0), (1, 0), (3, 0), (0, 1)), (after(own, owned), at_1, at_3, at_z)
     )
     owned = jnp.broadcast_to(owned, (N_CTX, OWNED_ROWS, HEAD_DIM))
     owned = swap_all(jnp.concatenate([grad_kv, owned], axis=1), "ctx")
-    experts = unpack_experts(
-        ctx_s, ((0, 1), (1, 1), (3, 1), (2, 1)), (at_z, at_z1, at_z3, at_z2), experts
-    )
-    input_grad = input_back(grad_query, owned, w_all, tokens[0], gain_attn, grad_middle)
     gain_attn_sum, *dense = finish(
         after(owned, experts[0], mixed),
         norm_attn.astype(f32).reshape(96, 1),
         query_weight,
         key_weight,
         value_weight,
+    )
+    input_grad = input_back(grad_query, owned, w_all, tokens[0], gain_attn, grad_middle)
+    at_2 = after(at_2, input_grad, *dense)
+    experts = unpack_experts(
+        ctx_s, ((2, 0), (1, 1), (3, 1), (2, 1)), (at_2, at_z1, at_z3, at_z2), experts
     )
     return (
         mixed,

time: 541 us -> 525 us (0.970)
  the two profiles are of different devices: /device:TPU:6 before, /device:TPU:0 now
where the time goes in v14:
time: 525 us; the launch traced here: 514 us
  waiting for transfers between devices  210 us (40%)
  Pallas kernels  148 us (28%)
  starting transfers between devices  76.2 us (15%)
  local copies, waits for them, and re-layouts  44.1 us (8%)
  other arithmetic  14.9 us (3%)
  between operations  14.9 us (3%)
  matrix products  6.73 us (1%)
    all_to_all x8, waiting for transfers between devices, swap_all(): lax.all_to_all(rows, axis, split_axis=0, concat_axis=0, tiled=True, axis_...  88.7 us
    ppermute x12, waiting for transfers between devices, to(): return lax.ppermute(rows, 'ctx', [(i, i ^ k) for i in range(N_CTX)])  63.9 us
    all_to_all x8, starting transfers between devices, swap_all(): lax.all_to_all(rows, axis, split_axis=0, concat_axis=0, tiled=True, axis_...  37.7 us
    pallas_call x1, Pallas kernels, expert_back(): pl.pallas_call(expert_kernel, grid_spec=pltpu.PrefetchScalarGridSpec(num_...  29 us
    ppermute x2, waiting for transfers between devices, of_sequence(): other = lax.ppermute(rows, 'ctx', z_swap)  26.3 us
    unnamed x122, local copies, waits for them, and re-layouts  25.3 us
    pallas_call x2, Pallas kernels, expert_weights(): pl.pallas_call(lambda *refs: expert_weights_kernel(halved, *refs), grid_s...  22.3 us
    ppermute x12, starting transfers between devices, to(): return lax.ppermute(rows, 'ctx', [(i, i ^ k) for i in range(N_CTX)])  20.4 us
  transfers between devices with their start and end apart: 33, of which 22 were waited for; matrix products, arithmetic and copies ran while one was open for 7% of the time, Pallas kernels for 22%

profile of v14, /device:TPU:0, one launch (start us, length us, event | category | flops | bytes accessed | tf_op | source)
XLA Modules:
  0.0 514.4 jit_solution(14947437032138203590)
XLA Ops:
  13.3 4.1 collective-permute-start
  18.0 4.8 all-to-all-start
  22.9 6.1 %collective-permute-done = bf16[1,128,1536]{2,1,0:T(8,128)(2,1)S(1)} collective-permute-done((bf16[1,128,1536]{2,1,0:T(8,128)(2,1)S(1)}, bf16[1,128,1536]{2,1,0:T(8,128)(2,1)S(1)}, u32[]{:S(2)}, u32[]{:S(2)}) %collective-permute-start) | collective-permute-done | bytes 393248 | tf_op jit(solution)/shard_map/ppermute | solution.py:1054
  31.7 4.6 all-to-all-start.1
  43.9 30.5 %all-to-all-done.1 = bf16[4,2,128,1536]{3,2,1,0:T(8,128)(2,1)S(1)} async-done(((bf16[4,2,128,1536]{3,2,1,0:T(8,128)(2,1)}), bf16[4,2,128,1536]{3,2,1,0:T(8,128)(2,1)S(1)}, u32[]{:S(2)}, u32[]{:S(2)}) %all-to-all-start.1) | async-done | bytes 3145760 | tf_op jit(solution)/shard_map/all_to_all | solution.py:1002
  74.3 5.2 %all-to-all-start.2 = ((bf16[16,96,128]{2,1,0:T(8,128)(2,1)}), bf16[16,96,128]{2,1,0:T(8,128)(2,1)}, u32[]{:S(2)}, u32[]{:S(2)}) async-start(bf16[16,96,128]{2,1,0:T(8,128)(2,1)} %copy.62), calls=%async_computation.2 | async-start | bytes 786432 | tf_op jit(solution)/shard_map/all_to_all | solution.py:1002
  86.0 4.5 all-to-all-done.2
  94.1 7.6 %project.1 = (bf16[128,1536]{1,0:T(8,128)(2,1)S(1)}, bf16[8,128,1024]{2,1,0:T(8,128)(2,1)S(1)}) custom-call(bf16[1,128,1536]{2,1,0:T(8,128)(2,1)S(1)} %copy-done.14, bf16[8,128,1536]{2,1,0:T(8,128)(2,1)S(1)} %copy-done.2, bf16[1536,4096]{1,0:T(8,128)(2,1)} %all-gather.4.cloned.1.call-done.w_ref.wq_ref.wkv_ref), custom_call_target="tpu_custom_call" | custom-call | bytes 29520000 | tf_op jit(solution)/shard_map/project/pallas_call | solution.py:799
  101.8 5.8 %attend.1 = (bf16[128,1536]{1,0:T(8,128)(2,1)S(1)}, f32[128,1536]{1,0:T(8,128)S(1)}, f32[1536,128]{1,0:T(8,128)S(1)}) custom-call(s32[1]{0:T(128)} %bitcast.ctx_ref.refs_0_, bf16[128,1536]{1,0:T(8,128)(2,1)S(1)} %get-tuple-element.107.q_ref, bf16[8,128,1024]{2,1,0:T(8,128)(2,1)S(1)} %get-tuple-element.108.k_ref.v_ref, ...), custom_call_target="tpu_custom_call" | custom-call | bytes 22140000 | tf_op jit(solution)/shard_map/attend/pallas_call | solution.py:99
  110.2 4.5 middle_norm.1
  116.4 20.1 %collective-permute-done.1 = bf16[1,128,1536]{2,1,0:T(8,128)(2,1)S(1)} collective-permute-done((bf16[1,128,1536]{2,1,0:T(8,128)(2,1)S(1)}, bf16[1,128,1536]{2,1,0:T(8,128)(2,1)S(1)}, u32[]{:S(2)}, u32[]{:S(2)}) %collective-permute-start.1) | collective-permute-done | bytes 393248 | tf_op jit(solution)/shard_map/ppermute | solution.py:1054
  138.5 4.6 all-to-all-start.3
  147.1 13.7 %place_rows.1 = (bf16[8,2,128,128]{3,2,1,0:T(8,128)(2,1)}, bf16[2,2,384,1536]{3,2,1,0:T(8,128)(2,1)}, f32[2,2,384,512]{3,2,1,0:T(8,128)}, f32[8,2,128,128]{3,2,1,0:T(8,128)}, f32[2,2,384,128]{3,2,1,0:T(8,128)}) custom-call(s32[1]{0:T(128)} %bitcast.7.at_ref, bf16[8,2,128,1664]{3,2,1,0:T(8,128)(2,1)} %bitcast.84, bf16[2,512,1536]{2,1,0:T(8,128)(2,1)} %wd_ref.1, ...), custom_call_target="tpu_custom_call" | custom-call | bytes 51660000 | tf_op jit(solution)/shard_map/place_rows/pallas_call | solution.py:368
  160.8 19.5 %all-to-all-done.3 = bf16[4,2,128,1536]{3,2,1,0:T(8,128)(2,1)S(1)} async-done(((bf16[4,2,128,1536]{3,2,1,0:T(8,128)(2,1)}), bf16[4,2,128,1536]{3,2,1,0:T(8,128)(2,1)S(1)}, u32[]{:S(2)}, u32[]{:S(2)}) %all-to-all-start.3) | async-done | bytes 3145760 | tf_op jit(solution)/shard_map/all_to_all | solution.py:1002
  180.3 12.1 %all-gather.6.cloned.1.call-done = bf16[2048,1536]{1,0:T(8,128)(2,1)} async-done(((bf16[128,1536]{1,0:T(8,128)(2,1)}), bf16[2048,1536]{1,0:T(8,128)(2,1)}) %all-gather.6.cloned.1.call-update) | async-done | bytes 6291472 | tf_op jit(solution)/shard_map/all_gather | solution.py:1077
  192.4 29.0 %expert_back.1 = (bf16[2,8,128,1536]{3,2,1,0:T(8,128)(2,1)}, bf16[2,2,384,1536]{3,2,1,0:T(8,128)(2,1)}, bf16[2,2,384,512]{3,2,1,0:T(8,128)(2,1)}, bf16[2,2,384,1...) custom-call(s32[1]{0:T(128)} %bitcast.7.at_ref, ...), custom_call_target="tpu_custom_call" | custom-call | bytes 103320000 | tf_op jit(solution)/shard_map/expert_back/pallas_call | solution.py:447
  223.9 5.5 %collective-permute-done.2 = bf16[8,128,1536]{2,1,0:T(8,128)(2,1)S(1)} collective-permute-done((bf16[8,128,1536]{2,1,0:T(8,128)(2,1)S(1)}, bf16[8,128,1536]{2,1,0:T(8,128)(2,1)S(1)}, u32[]{:S(2)}, u32[]{:S(2)}) %collective-permute-start.2) | collective-permute-done | bytes 3145760 | tf_op jit(solution)/shard_map/ppermute | solution.py:1089
  229.4 2.6 fusion
  232.0 4.8 all-to-all-start.4
  236.8 10.9 %expert_weights.2 = (bf16[9216,128]{1,0:T(8,128)(2,1)}, bf16[9216,128]{1,0:T(8,128)(2,1)}) custom-call(s32[1]{0:T(128)} %bitcast.ctx_ref.refs_0_, bf16[2,768,1536]{2,1,0:T(8,128)(2,1)} %bitcast.91, bf16[2,768,1536]{2,1,0:T(8,128)(2,1)} %bitcast.89, bf16[2,768,512]{2,1,0:T(8,128)(2,1)} %bitcast.74, bf16[2,768,1024]{2,1,0:T(8,128)(2,1)} %bitcast.85, ...), custom_call_target="tpu_custom_call" | custom-call | bytes 7380000 | tf_op jit(solution)/shard_map/expert_weights/pallas_call | solution.py:899
  249.2 11.4 %expert_weights.3 = (bf16[4608,128]{1,0:T(8,128)(2,1)}, bf16[4608,128]{1,0:T(8,128)(2,1)}, bf16[4608,128]{1,0:T(8,128)(2,1)}, bf16[4608,128]{1,0:T(8,128)(2,1)}) custom-call(s32[1]{0:T(128)} %bitcast.ctx_ref.refs_0_, bf16[2,768,1536]{2,1,0:T(8,128)(2,1)} %bitcast.92, bf16[2,768,1536]{2,1,0:T(8,128)(2,1)} %bitcast.90, bf16[2,768,512]{2,1,0:T(8,128)(2,1)} %bitcast.75, ...), custom_call_target="tpu_custom_call" | custom-call | bytes 7380000 | tf_op jit(solution)/shard_map/expert_weights/pallas_call | solution.py:899
  268.6 9.8 %expert_output.1.own_ref = bf16[2,8,128,1536]{3,2,1,0:T(8,128)(2,1)} custom-call(s32[1]{0:T(128)} %bitcast.7.at_ref, bf16[2,2,384,512]{3,2,1,0:T(8,128)(2,1)S(1)} %copy-done.3, f32[2,2,384,128]{3,2,1,0:T(8,128)S(1)} %copy-done.30, bf16[8,2,128,128]{3,2,1,0:T(8,128)(2,1)S(1)} %copy-done.10, bf16[8,2,128,128]{3,2,1,0:T(8,128)(2,1)S(1)} %copy-done.6, ...), custom_call_target="tpu_custom_call" | custom-call | bytes 7380000 | tf_op jit(solution)/shard_map/expert_output/pallas_call | solution.py:499
  278.4 4.1 fusion.8
  283.9 5.6 %middle_back.1 = (f32[128,1536]{1,0:T(8,128)S(1)}, bf16[128,1536]{1,0:T(8,128)(2,1)S(1)}, bf16[128,1536]{1,0:T(8,128)(2,1)S(1)}, f32[16,128]{1,0:T(8,128)S(1)}) custom-call(bf16[8,128,1536]{2,1,0:T(8,128)(2,1)} %all-to-all-done.4.pieces_ref, f32[128,1536]{1,0:T(8,128)S(1)} %copy-done.7, bf16[128,1536]{1,0:T(8,128)(2,1)S(1)} %bitcast.81, ...), custom_call_target="tpu_custom_call" | custom-call | bytes 3690000 | tf_op jit(solution)/shard_map/middle_back/pallas_call | solution.py:290
  292.5 10.3 %attend_back.1 = (bf16[128,1536]{1,0:T(8,128)(2,1)}, bf16[4,1776,128]{2,1,0:T(8,128)(2,1)}, bf16[4,1776,128]{2,1,0:T(8,128)(2,1)}) custom-call(s32[1]{0:T(128)} %bitcast.ctx_ref.refs_0_, bf16[128,1536]{1,0:T(8,128)(2,1)} %copy-done.12, bf16[128,1536]{1,0:T(8,128)(2,1)} %copy-done.35, f32[128,1536]{1,0:T(8,128)} %copy-done.28, f32[1536,128]{1,0:T(8,128)} %copy-done.29, ...), custom_call_target="tpu_custom_call" | custom-call | bytes 7380000 | tf_op jit(solution)/shard_map/attend_back/pallas_call | solution.py:202
  302.8 3.2 collective-permute-start.9
  308.8 6.5 %collective-permute-done.4.relay_b.got_31 = bf16[9216,128]{1,0:T(8,128)(2,1)} collective-permute-done((bf16[9216,128]{1,0:T(8,128)(2,1)}, bf16[9216,128]{1,0:T(8,128)(2,1)}, u32[]{:S(2)}, u32[]{:S(2)}) %collective-permute-start.4) | collective-permute-done | bytes 2359328 | tf_op jit(solution)/shard_map/ppermute | solution.py:1104
  315.3 4.4 piece_sums.2
  321.8 3.0 spread_sums.1
  328.6 18.1 %collective-permute-done.10.got_11 = bf16[4608,128]{1,0:T(8,128)(2,1)S(1)} collective-permute-done((bf16[4608,128]{1,0:T(8,128)(2,1)S(1)}, bf16[4608,128]{1,0:T(8,128)(2,1)S(1)}, u32[]{:S(2)}, u32[]{:S(2)}) %collective-permute-start.10) | collective-permute-done | bytes 1179680 | tf_op jit(solution)/shard_map/ppermute | solution.py:1104
  348.5 3.0 collective-permute-start.12
  354.9 4.5 all-to-all-start.5
  359.4 16.8 %collective-permute-done.12 = bf16[4608,128]{1,0:T(8,128)(2,1)} collective-permute-done((bf16[4608,128]{1,0:T(8,128)(2,1)S(1)}, bf16[4608,128]{1,0:T(8,128)(2,1)}, u32[]{:S(2)}, u32[]{:S(2)}) %collective-permute-start.12) | collective-permute-done | bytes 1179680 | tf_op jit(solution)/shard_map/ppermute | solution.py:1104
  379.0 2.9 collective-permute-start.17
  381.8 2.6 collective-permute-start.13
  384.5 4.1 all-to-all-done.5.got_ref
  388.5 7.1 %column_grads.1 = (bf16[16,112,512]{2,1,0:T(8,128)(2,1)}, bf16[8,128,128]{2,1,0:T(8,128)(2,1)}, bf16[96,128]{1,0:T(8,128)(2,1)}) custom-call(bf16[4,2160,128]{2,1,0:T(8,128)(2,1)} %all-to-all-done.5.got_ref, bf16[8,128,1536]{2,1,0:T(8,128)(2,1)} %copy-done.1, bf16[8,128,1536]{2,1,0:T(8,128)(2,1)} %bitcast.93), custom_call_target="tpu_custom_call" | custom-call | bytes 29520000 | tf_op jit(solution)/shard_map/column_grads/pallas_call | solution.py:614
  395.6 3.6 collective-permute-done.13
  399.2 9.9 %collective-permute-done.15.refs_2_ = bf16[4608,128]{1,0:T(8,128)(2,1)S(1)} collective-permute-done((bf16[4608,128]{1,0:T(8,128)(2,1)S(1)}, bf16[4608,128]{1,0:T(8,128)(2,1)S(1)}, u32[]{:S(2)}, u32[]{:S(2)}) %collective-permute-start.15) | collective-permute-done | bytes 1179680 | tf_op jit(solution)/shard_map/ppermute | solution.py:1104
  411.5 4.2 all-to-all-start.6
  423.6 17.1 %all-to-all-done.6.got_ref = bf16[16,112,512]{2,1,0:T(8,128)(2,1)S(1)} async-done(((bf16[16,112,512]{2,1,0:T(8,128)(2,1)}), bf16[16,112,512]{2,1,0:T(8,128)(2,1)S(1)}, u32[]{:S(2)}, u32[]{:S(2)}) %all-to-all-start.6) | async-done | bytes 1835040 | tf_op jit(solution)/shard_map/all_to_all | solution.py:1002
  440.9 6.0 %collective-permute-done.14 = bf16[128,1536]{1,0:T(8,128)(2,1)S(1)} collective-permute-done((bf16[128,1536]{1,0:T(8,128)(2,1)}, bf16[128,1536]{1,0:T(8,128)(2,1)S(1)}, u32[]{:S(2)}, u32[]{:S(2)}) %collective-permute-start.14) | collective-permute-done | bytes 393248 | tf_op jit(solution)/shard_map/ppermute | solution.py:1174
  448.5 5.0 all-to-all-start.7
  460.4 5.3 %unpack_experts.2 = (f32[2,1536,512]{2,1,0:T(8,128)}, f32[2,1536,512]{2,1,0:T(8,128)}, f32[2,512,1536]{2,1,0:T(8,128)}) custom-call(s32[1]{0:T(128)} %bitcast.ctx_ref.refs_0_, bf16[4608,128]{1,0:T(8,128)(2,1)S(1)} %add_convert_fusion.refs_1_, bf16[4608,128]{1,0:T(8,128)(2,1)S(1)} %copy-done.27, bf16[4608,128]{1,0:T(8,128)(2,1)S(1)} %copy-done.25, ...), custom_call_target="tpu_custom_call" | custom-call | bytes 29520000 | tf_op jit(solution)/shard_map/unpack_experts/pallas_call | solution.py:943
  466.2 12.5 %all-to-all-done.7.got_ref = bf16[8,864,128]{2,1,0:T(8,128)(2,1)S(1)} async-done(((bf16[8,864,128]{2,1,0:T(8,128)(2,1)}), bf16[8,864,128]{2,1,0:T(8,128)(2,1)S(1)}, u32[]{:S(2)}, u32[]{:S(2)}) %all-to-all-start.7) | async-done | bytes 1769504 | tf_op jit(solution)/shard_map/all_to_all | solution.py:1002
  482.7 7.0 %input_back.1 = bf16[128,1536]{1,0:T(8,128)(2,1)} custom-call(bf16[128,1536]{1,0:T(8,128)(2,1)S(1)} %copy-done.33, bf16[8,864,128]{2,1,0:T(8,128)(2,1)S(1)} %all-to-all-done.7.got_ref, bf16[1536,4096]{1,0:T(8,128)(2,1)} %all-gather.4.cloned.1.call-done.w_ref.wq_ref.wkv_ref, bf16[1536,4096]{1,0:T(8,128)(2,1)} %all-gather.4.cloned.1.call-done.w_ref.wq_ref.wkv_ref, ...), custom_call_target="tpu_custom_call" | custom-call | bytes 25830000 | tf_op jit(solution)/shard_map/input_back/pallas_call | solution.py:743
  489.6 10.9 %collective-permute-done.20.refs_1_ = bf16[4608,128]{1,0:T(8,128)(2,1)} collective-permute-done((bf16[4608,128]{1,0:T(8,128)(2,1)}, bf16[4608,128]{1,0:T(8,128)(2,1)}, u32[]{:S(2)}, u32[]{:S(2)}) %collective-permute-start.20) | collective-permute-done | bytes 1179680 | tf_op jit(solution)/shard_map/ppermute | solution.py:1104
  501.2 6.2 %unpack_experts.3 = (f32[2,1536,512]{2,1,0:T(8,128)}, f32[2,1536,512]{2,1,0:T(8,128)}, f32[2,512,1536]{2,1,0:T(8,128)}) custom-call(s32[1]{0:T(128)} %bitcast.ctx_ref.refs_0_, bf16[4608,128]{1,0:T(8,128)(2,1)} %collective-permute-done.20.refs_1_, ...), custom_call_target="tpu_custom_call", output_to_operand_aliasing={{0}: (5, {}), {1}: (6, {}), {2}: (7, {})} | custom-call | bytes 29520000 | tf_op jit(solution)/shard_map/unpack_experts/pallas_call | solution.py:943
  (204 shorter events, 94.4 us)
Async XLA Ops:
  7.2 10.1 %copy-start.50 = (bf16[96]{0:T(256)(128)(2,1)S(1)}, bf16[96]{0:T(256)(128)(2,1)}, u32[]{:S(2)}) copy-start(bf16[96]{0:T(256)(128)(2,1)} %param.19) | copy-start | bytes 580
  7.2 10.1 %copy-start.49 = (bf16[96]{0:T(256)(128)(2,1)S(1)}, bf16[96]{0:T(256)(128)(2,1)}, u32[]{:S(2)}) copy-start(bf16[96]{0:T(256)(128)(2,1)} %param.20) | copy-start | bytes 580
  7.2 85.0 %all-gather.4.cloned.1.call-start = ((), (), s32[]{:S(2)}) async-start(), calls=%async_computation.8 | async-start | bytes 13369344 | tf_op jit(solution)/shard_map/all_gather | solution.py:1040
  12.0 135.1 %all-gather.8.cloned.1.call-start = ((), (), s32[]{:S(2)}) async-start(), calls=%async_computation.10 | async-start | bytes 7241728 | tf_op jit(solution)/shard_map/all_gather | solution.py:1047
  13.3 15.8 %collective-permute-start = (bf16[1,128,1536]{2,1,0:T(8,128)(2,1)S(1)}, bf16[1,128,1536]{2,1,0:T(8,128)(2,1)S(1)}, u32[]{:S(2)}, u32[]{:S(2)}) collective-permute-start(bf16[1,128,1536]{2,1,0:T(8,128)(2,1)S(1)} %copy-done.4), channel_id=1, source_target_pairs={{0,64},{16,80},{32,96},{48,112},{64,0},{80,16},{96,32},{112,48},{1... | collective-permute-start | bytes 1179656 | tf_op jit(solution)/shard_map/ppermute | solution.py:1054
  18.0 11.7 %all-to-all-start = ((bf16[16,1,192]{2,1,0:T(2,128)(2,1)}), bf16[16,1,192]{2,1,0:T(2,128)(2,1)S(1)}, u32[]{:S(2)}, u32[]{:S(2)}) async-start(bf16[16,1,192]{2,1,0:T(2,128)(2,1)} %broadcast_in_dim.24), calls=%async_computation | async-start | bytes 32768 | tf_op jit(solution)/shard_map/all_to_all | solution.py:1002
  31.7 42.6 %all-to-all-start.1 = ((bf16[4,2,128,1536]{3,2,1,0:T(8,128)(2,1)}), bf16[4,2,128,1536]{3,2,1,0:T(8,128)(2,1)S(1)}, u32[]{:S(2)}, u32[]{:S(2)}) async-start(bf16[4,2,128,1536]{3,2,1,0:T(8,128)(2,1)} %broadcast_in_dim.25), calls=%async_computation.1 | async-start | bytes 6291456 | tf_op jit(solution)/shard_map/all_to_all | solution.py:1002
  74.3 16.1 %all-to-all-start.2 = ((bf16[16,96,128]{2,1,0:T(8,128)(2,1)}), bf16[16,96,128]{2,1,0:T(8,128)(2,1)}, u32[]{:S(2)}, u32[]{:S(2)}) async-start(bf16[16,96,128]{2,1,0:T(8,128)(2,1)} %copy.62), calls=%async_computation.2 | async-start | bytes 786432 | tf_op jit(solution)/shard_map/all_to_all | solution.py:1002
  79.5 112.9 %all-gather.6.cloned.1.call-start = ((), (), s32[]{:S(2)}) async-start(), calls=%async_computation.9 | async-start | bytes 6684672 | tf_op jit(solution)/shard_map/all_gather | solution.py:1077
  114.8 21.7 %collective-permute-start.1 = (bf16[1,128,1536]{2,1,0:T(8,128)(2,1)S(1)}, bf16[1,128,1536]{2,1,0:T(8,128)(2,1)S(1)}, u32[]{:S(2)}, u32[]{:S(2)}) collective-permute-start(bf16[1,128,1536]{2,1,0:T(8,128)(2,1)S(1)} %bitcast.82), channel_id=1, source_target_pairs={{0,64},{16,80},{32,96},{48,112},{64,0},{80,16},{96,32},{112,48},{1... | collective-permute-start | bytes 1179656 | tf_op jit(solution)/shard_map/ppermute | solution.py:1054
  138.5 41.8 %all-to-all-start.3 = ((bf16[4,2,128,1536]{3,2,1,0:T(8,128)(2,1)}), bf16[4,2,128,1536]{3,2,1,0:T(8,128)(2,1)S(1)}, u32[]{:S(2)}, u32[]{:S(2)}) async-start(bf16[4,2,128,1536]{3,2,1,0:T(8,128)(2,1)} %broadcast_in_dim.27), calls=%async_computation.3 | async-start | bytes 6291456 | tf_op jit(solution)/shard_map/all_to_all | solution.py:1002
  180.3 41.0 %copy-start.41 = (bf16[4,2,128,1536]{3,2,1,0:T(8,128)(2,1)}, bf16[4,2,128,1536]{3,2,1,0:T(8,128)(2,1)S(1)}, u32[]{:S(2)}) copy-start(bf16[4,2,128,1536]{3,2,1,0:T(8,128)(2,1)S(1)} %all-to-all-done.3) | copy-start | bytes 9437188
  223.6 5.7 %collective-permute-start.2 = (bf16[8,128,1536]{2,1,0:T(8,128)(2,1)S(1)}, bf16[8,128,1536]{2,1,0:T(8,128)(2,1)S(1)}, u32[]{:S(2)}, u32[]{:S(2)}) collective-permute-start(bf16[8,128,1536]{2,1,0:T(8,128)(2,1)S(1)} %slice_bitcast_fusion), channel_id=1, source_target_pairs={{0,1},{1,0},{2,3},{3,2},{4,5},{5,4},{6,7},{7,6},{8,9},{9,8},{10,11... | collective-permute-start | bytes 9437192 | tf_op jit(solution)/shard_map/ppermute | solution.py:1089
  232.0 51.5 %all-to-all-start.4 = ((bf16[8,128,1536]{2,1,0:T(8,128)(2,1)}), bf16[8,128,1536]{2,1,0:T(8,128)(2,1)}, u32[]{:S(2)}, u32[]{:S(2)}) async-start(bf16[8,128,1536]{2,1,0:T(8,128)(2,1)} %fusion), calls=%async_computation.4 | async-start | bytes 6291456 | tf_op jit(solution)/shard_map/all_to_all | solution.py:1002
  247.7 15.3 %slice-start.2 = ((s8[6291456]{0:T(1024)(128)(4,1)}), s8[4194304]{0:T(1024)(128)(4,1)S(1)}, s32[]{:S(2)}) async-start(s8[6291456]{0:T(1024)(128)(4,1)} %bitcast.95), calls=%async_computation.13 | async-start | bytes 8388608
  247.7 15.3 %slice-start.3 = ((s8[6291456]{0:T(1024)(128)(4,1)}), s8[2097152]{0:T(1024)(128)(4,1)S(1)}, s32[]{:S(2)}) async-start(s8[6291456]{0:T(1024)(128)(4,1)} %bitcast.95), calls=%async_computation.14 | async-start | bytes 4194304
  247.7 15.3 %copy-start.48 = (bf16[8,2,128,128]{3,2,1,0:T(8,128)(2,1)S(1)}, bf16[8,2,128,128]{3,2,1,0:T(8,128)(2,1)}, u32[]{:S(2)}) copy-start(bf16[8,2,128,128]{3,2,1,0:T(8,128)(2,1)} %get-tuple-element.135) | copy-start | bytes 1572868
  247.7 61.1 %collective-permute-start.3 = (bf16[9216,128]{1,0:T(8,128)(2,1)}, bf16[9216,128]{1,0:T(8,128)(2,1)}, u32[]{:S(2)}, u32[]{:S(2)}) collective-permute-start(bf16[9216,128]{1,0:T(8,128)(2,1)} %get-tuple-element.124), channel_id=1, source_target_pairs={{0,16},{16,0},{32,48},{48,32},{64,80},{80,64},{96,112},{112,96},{1... | collective-permute-start | bytes 7077896 | tf_op jit(solution)/shard_map/ppermute | solution.py:1104
  260.6 54.6 %collective-permute-start.4 = (bf16[9216,128]{1,0:T(8,128)(2,1)}, bf16[9216,128]{1,0:T(8,128)(2,1)}, u32[]{:S(2)}, u32[]{:S(2)}) collective-permute-start(bf16[9216,128]{1,0:T(8,128)(2,1)} %get-tuple-element.133), channel_id=1, source_target_pairs={{0,48},{16,32},{32,16},{48,0},{64,112},{80,96},{96,80},{112,64},{1... | collective-permute-start | bytes 7077896 | tf_op jit(solution)/shard_map/ppermute | solution.py:1104
  302.8 12.5 %copy-start.19 = (bf16[4608,128]{1,0:T(8,128)(2,1)S(1)}, bf16[4608,128]{1,0:T(8,128)(2,1)}, u32[]{:S(2)}) copy-start(bf16[4608,128]{1,0:T(8,128)(2,1)} %get-tuple-element.126.p0) | copy-start | bytes 3538948
  302.8 12.5 %copy-start.20 = (bf16[4608,128]{1,0:T(8,128)(2,1)S(1)}, bf16[4608,128]{1,0:T(8,128)(2,1)}, u32[]{:S(2)}) copy-start(bf16[4608,128]{1,0:T(8,128)(2,1)} %get-tuple-element.132.p6) | copy-start | bytes 3538948
  302.8 12.5 %copy-start.21 = (bf16[4608,128]{1,0:T(8,128)(2,1)S(1)}, bf16[4608,128]{1,0:T(8,128)(2,1)}, u32[]{:S(2)}) copy-start(bf16[4608,128]{1,0:T(8,128)(2,1)} %get-tuple-element.130.p1) | copy-start | bytes 3538948
  302.8 12.5 %copy-start.22 = (bf16[4608,128]{1,0:T(8,128)(2,1)S(1)}, bf16[4608,128]{1,0:T(8,128)(2,1)}, u32[]{:S(2)}) copy-start(bf16[4608,128]{1,0:T(8,128)(2,1)} %get-tuple-element.131.p3) | copy-start | bytes 3538948
  302.8 45.2 %collective-permute-start.9 = (bf16[4,1776,128]{2,1,0:T(8,128)(2,1)}, bf16[4,1776,128]{2,1,0:T(8,128)(2,1)S(1)}, u32[]{:S(2)}, u32[]{:S(2)}) collective-permute-start(bf16[4,1776,128]{2,1,0:T(8,128)(2,1)} %get-tuple-element.151), channel_id=1, source_target_pairs={{0,64},{16,80},{32,96},{48,112},{64,0},{80,16},{96,32},{112,48},{1... | collective-permute-start | bytes 5455880 | tf_op jit(solution)/shard_map/ppermute | solution.py:1132
  308.2 13.6 %collective-permute-start.5 = (bf16[4,128,1536]{2,1,0:T(8,128)(2,1)S(1)}, bf16[4,128,1536]{2,1,0:T(8,128)(2,1)S(1)}, u32[]{:S(2)}, u32[]{:S(2)}) collective-permute-start(bf16[4,128,1536]{2,1,0:T(8,128)(2,1)S(1)} %get-tuple-element.197), channel_id=1, source_target_pairs={{0,1},{1,0},{2,3},{3,2},{4,5},{5,4},{6,7},{7,6},{8,9},{9,8},{10,11... | collective-permute-start | bytes 4718600 | tf_op jit(solution)/shard_map/ppermute | solution.py:1154
  308.3 13.5 %collective-permute-start.6 = (bf16[4,128,1536]{2,1,0:T(8,128)(2,1)S(1)}, bf16[4,128,1536]{2,1,0:T(8,128)(2,1)S(1)}, u32[]{:S(2)}, u32[]{:S(2)}) collective-permute-start(bf16[4,128,1536]{2,1,0:T(8,128)(2,1)S(1)} %get-tuple-element.196), channel_id=1, source_target_pairs={{0,1},{1,0},{2,3},{3,2},{4,5},{5,4},{6,7},{7,6},{8,9},{9,8},{10,11... | collective-permute-start | bytes 4718600 | tf_op jit(solution)/shard_map/ppermute | solution.py:1155
  319.7 27.0 %collective-permute-start.10 = (bf16[4608,128]{1,0:T(8,128)(2,1)S(1)}, bf16[4608,128]{1,0:T(8,128)(2,1)S(1)}, u32[]{:S(2)}, u32[]{:S(2)}) collective-permute-start(bf16[4608,128]{1,0:T(8,128)(2,1)S(1)} %get-tuple-element.154), channel_id=1, source_target_pairs={{0,16},{16,0},{32,48},{48,32},{64,80},{80,64},{96,112},{112,96},{1... | collective-permute-start | bytes 3538952 | tf_op jit(solution)/shard_map/ppermute | solution.py:1104
  319.8 28.2 %collective-permute-start.11 = (bf16[4608,128]{1,0:T(8,128)(2,1)S(1)}, bf16[4608,128]{1,0:T(8,128)(2,1)S(1)}, u32[]{:S(2)}, u32[]{:S(2)}) collective-permute-start(bf16[4608,128]{1,0:T(8,128)(2,1)S(1)} %get-tuple-element.146), channel_id=1, source_target_pairs={{0,48},{16,32},{32,16},{48,0},{64,112},{80,96},{96,80},{112,64},{1... | collective-permute-start | bytes 3538952 | tf_op jit(solution)/shard_map/ppermute | solution.py:1104
  324.8 26.7 %collective-permute-start.7 = (bf16[2,128,1536]{2,1,0:T(8,128)(2,1)S(1)}, bf16[2,128,1536]{2,1,0:T(8,128)(2,1)S(1)}, u32[]{:S(2)}, u32[]{:S(2)}) collective-permute-start(bf16[2,128,1536]{2,1,0:T(8,128)(2,1)S(1)} %get-tuple-element.149), channel_id=1, source_target_pairs={{0,4},{1,5},{2,6},{3,7},{4,0},{5,1},{6,2},{7,3},{8,12},{9,13},{10,... | collective-permute-start | bytes 2359304 | tf_op jit(solution)/shard_map/ppermute | solution.py:1149
  326.5 24.9 %collective-permute-start.8 = (bf16[2,128,1536]{2,1,0:T(8,128)(2,1)S(1)}, bf16[2,128,1536]{2,1,0:T(8,128)(2,1)S(1)}, u32[]{:S(2)}, u32[]{:S(2)}) collective-permute-start(bf16[2,128,1536]{2,1,0:T(8,128)(2,1)S(1)} %get-tuple-element.150), channel_id=1, source_target_pairs={{0,12},{1,13},{2,14},{3,15},{4,8},{5,9},{6,10},{7,11},{8,4},{9,5},... | collective-permute-start | bytes 2359304 | tf_op jit(solution)/shard_map/ppermute | solution.py:1149
  348.5 27.7 %collective-permute-start.12 = (bf16[4608,128]{1,0:T(8,128)(2,1)S(1)}, bf16[4608,128]{1,0:T(8,128)(2,1)}, u32[]{:S(2)}, u32[]{:S(2)}) collective-permute-start(bf16[4608,128]{1,0:T(8,128)(2,1)S(1)} %get-tuple-element.157), channel_id=1, source_target_pairs={{0,64},{16,80},{32,96},{48,112},{64,0},{80,16},{96,32},{112,48},{1... | collective-permute-start | bytes 3538952 | tf_op jit(solution)/shard_map/ppermute | solution.py:1104
  354.9 33.6 %all-to-all-start.5 = ((bf16[4,2160,128]{2,1,0:T(8,128)(2,1)}), bf16[4,2160,128]{2,1,0:T(8,128)(2,1)}, u32[]{:S(2)}, u32[]{:S(2)}) async-start(bf16[4,2160,128]{2,1,0:T(8,128)(2,1)} %merge_shares.1), calls=%async_computation.5 | async-start | bytes 4423680 | tf_op jit(solution)/shard_map/all_to_all | solution.py:1002
  377.7 31.4 %collective-permute-start.15 = (bf16[4608,128]{1,0:T(8,128)(2,1)S(1)}, bf16[4608,128]{1,0:T(8,128)(2,1)S(1)}, u32[]{:S(2)}, u32[]{:S(2)}) collective-permute-start(bf16[4608,128]{1,0:T(8,128)(2,1)S(1)} %add_convert_fusion.refs_1_), channel_id=1, source_target_pairs={{0,16},{16,0},{32,48},{48,32},{64,80},{80,64},{96,112},{112,96},{1... | collective-permute-start | bytes 3538952 | tf_op jit(solution)/shard_map/ppermute | solution.py:1104
  377.9 32.6 %collective-permute-start.16 = (bf16[4608,128]{1,0:T(8,128)(2,1)S(1)}, bf16[4608,128]{1,0:T(8,128)(2,1)S(1)}, u32[]{:S(2)}, u32[]{:S(2)}) collective-permute-start(bf16[4608,128]{1,0:T(8,128)(2,1)S(1)} %add_convert_fusion.refs_1_), channel_id=1, source_target_pairs={{0,48},{16,32},{32,16},{48,0},{64,112},{80,96},{96,80},{112,64},{1... | collective-permute-start | bytes 3538952 | tf_op jit(solution)/shard_map/ppermute | solution.py:1104
  379.0 36.8 %collective-permute-start.17 = (bf16[4608,128]{1,0:T(8,128)(2,1)S(1)}, bf16[4608,128]{1,0:T(8,128)(2,1)}, u32[]{:S(2)}, u32[]{:S(2)}) collective-permute-start(bf16[4608,128]{1,0:T(8,128)(2,1)S(1)} %add_convert_fusion.refs_1_), channel_id=1, source_target_pairs={{0,64},{16,80},{32,96},{48,112},{64,0},{80,16},{96,32},{112,48},{1... | collective-permute-start | bytes 3538952 | tf_op jit(solution)/shard_map/ppermute | solution.py:1104
  381.8 17.3 %collective-permute-start.13 = (bf16[2,128,1536]{2,1,0:T(8,128)(2,1)}, bf16[2,128,1536]{2,1,0:T(8,128)(2,1)}, u32[]{:S(2)}, u32[]{:S(2)}) collective-permute-start(bf16[2,128,1536]{2,1,0:T(8,128)(2,1)} %get-tuple-element.165), channel_id=1, source_target_pairs={{0,8},{1,9},{2,10},{3,11},{4,12},{5,13},{6,14},{7,15},{8,0},{9,1},... | collective-permute-start | bytes 2359304 | tf_op jit(solution)/shard_map/ppermute | solution.py:1149
  411.5 29.2 %all-to-all-start.6 = ((bf16[16,112,512]{2,1,0:T(8,128)(2,1)}), bf16[16,112,512]{2,1,0:T(8,128)(2,1)S(1)}, u32[]{:S(2)}, u32[]{:S(2)}) async-start(bf16[16,112,512]{2,1,0:T(8,128)(2,1)} %get-tuple-element.168), calls=%async_computation.6 | async-start | bytes 3670016 | tf_op jit(solution)/shard_map/all_to_all | solution.py:1002
  415.7 25.0 %copy-start.39 = (bf16[96,128]{1,0:T(8,128)(2,1)S(1)}, bf16[96,128]{1,0:T(8,128)(2,1)}, u32[]{:S(2)}) copy-start(bf16[96,128]{1,0:T(8,128)(2,1)} %get-tuple-element.169.down_ref) | copy-start | bytes 73732
  415.8 31.2 %collective-permute-start.18 = (bf16[4608,128]{1,0:T(8,128)(2,1)}, bf16[4608,128]{1,0:T(8,128)(2,1)}, u32[]{:S(2)}, u32[]{:S(2)}) collective-permute-start(bf16[4608,128]{1,0:T(8,128)(2,1)} %collective-permute-done.17.refs_4_), channel_id=1, source_target_pairs={{0,16},{16,0},{32,48},{48,32},{64,80},{80,64},{96,112},{112,96},{1... | collective-permute-start | bytes 3538952 | tf_op jit(solution)/shard_map/ppermute | solution.py:1104
  416.4 30.6 %collective-permute-start.19 = (bf16[4608,128]{1,0:T(8,128)(2,1)}, bf16[4608,128]{1,0:T(8,128)(2,1)}, u32[]{:S(2)}, u32[]{:S(2)}) collective-permute-start(bf16[4608,128]{1,0:T(8,128)(2,1)} %collective-permute-done.17.refs_4_), channel_id=1, source_target_pairs={{0,48},{16,32},{32,16},{48,0},{64,112},{80,96},{96,80},{112,64},{1... | collective-permute-start | bytes 3538952 | tf_op jit(solution)/shard_map/ppermute | solution.py:1104
  421.7 25.2 %collective-permute-start.14 = (bf16[128,1536]{1,0:T(8,128)(2,1)}, bf16[128,1536]{1,0:T(8,128)(2,1)S(1)}, u32[]{:S(2)}, u32[]{:S(2)}) collective-permute-start(bf16[128,1536]{1,0:T(8,128)(2,1)} %fusion.5), channel_id=1, source_target_pairs={{0,2},{1,3},{2,0},{3,1},{4,6},{5,7},{6,4},{7,5},{8,10},{9,11},{10,... | collective-permute-start | bytes 1179656 | tf_op jit(solution)/shard_map/ppermute | solution.py:1174
  448.5 30.1 %all-to-all-start.7 = ((bf16[8,864,128]{2,1,0:T(8,128)(2,1)}), bf16[8,864,128]{2,1,0:T(8,128)(2,1)S(1)}, u32[]{:S(2)}, u32[]{:S(2)}) async-start(bf16[8,864,128]{2,1,0:T(8,128)(2,1)} %pad_maximum_fusion), calls=%async_computation.7 | async-start | bytes 3538944 | tf_op jit(solution)/shard_map/all_to_all | solution.py:1002
  453.5 47.1 %collective-permute-start.20 = (bf16[4608,128]{1,0:T(8,128)(2,1)}, bf16[4608,128]{1,0:T(8,128)(2,1)}, u32[]{:S(2)}, u32[]{:S(2)}) collective-permute-start(bf16[4608,128]{1,0:T(8,128)(2,1)} %copy-done.24), channel_id=1, source_target_pairs={{0,16},{16,0},{32,48},{48,32},{64,80},{80,64},{96,112},{112,96},{1... | collective-permute-start | bytes 3538952 | tf_op jit(solution)/shard_map/ppermute | solution.py:1104
  455.5 45.7 %collective-permute-start.21 = (bf16[4608,128]{1,0:T(8,128)(2,1)}, bf16[4608,128]{1,0:T(8,128)(2,1)}, u32[]{:S(2)}, u32[]{:S(2)}) collective-permute-start(bf16[4608,128]{1,0:T(8,128)(2,1)} %collective-permute-done.18.refs_2_), channel_id=1, source_target_pairs={{0,48},{16,32},{32,16},{48,0},{64,112},{80,96},{96,80},{112,64},{1... | collective-permute-start | bytes 3538952 | tf_op jit(solution)/shard_map/ppermute | solution.py:1104
  460.3 18.3 %copy-start.23 = (bf16[96,1536]{1,0:T(8,128)(2,1)S(1)}, bf16[96,1536]{1,0:T(8,128)(2,1)}, u32[]{:S(2)}) copy-start(bf16[96,1536]{1,0:T(8,128)(2,1)} %wq_ref.1) | copy-start | bytes 884740
  460.4 18.3 %copy-start.36 = (bf16[96,512]{1,0:T(8,128)(2,1)S(1)}, bf16[96,512]{1,0:T(8,128)(2,1)}, u32[]{:S(2)}) copy-start(bf16[96,512]{1,0:T(8,128)(2,1)} %wk_ref.1) | copy-start | bytes 294916
  460.4 18.3 %copy-start.37 = (bf16[96,512]{1,0:T(8,128)(2,1)S(1)}, bf16[96,512]{1,0:T(8,128)(2,1)}, u32[]{:S(2)}) copy-start(bf16[96,512]{1,0:T(8,128)(2,1)} %wv_ref.1) | copy-start | bytes 294916
  465.7 14.8 %copy-start.5 = (bf16[1,128,1536]{2,1,0:T(8,128)(2,1)S(1)}, bf16[1,128,1536]{2,1,0:T(8,128)(2,1)}, u32[]{:S(2)}) copy-start(bf16[1,128,1536]{2,1,0:T(8,128)(2,1)} %x_ref.1) | copy-start | bytes 1179652
  (41 other events, 131.2 us)
Sparse Core Ops, SparseCore 0:
  12.2 79.9 all-gather.3
  94.5 52.5 all-gather.7
  149.4 42.9 all-gather.5

commit v15 on v14

--- a/solution.py
+++ b/solution.py
@@ -1174,12 +1174,10 @@
     out_across = lax.ppermute(
         out_rows[1].astype(bf16), "exp", [(i, i ^ 2) for i in range(N_EXP)]
     )
-    columns = after(columns, at_1, at_3, out_2)
     owned = swap_all(columns, "exp")
     owned, gain_sum = owned_sums(owned, grad_down)
-    owned, at_z1, at_z3 = lax.optimization_barrier(
-        (after(owned, out_across), to(at_z, 1), to(at_z, 3))
-    )
+    at_z, at_1, at_3 = lax.optimization_barrier((after(at_z, out_2), at_1, at_3))
+    owned, at_z1, at_z3 = lax.optimization_barrier((owned, to(at_z, 1), to(at_z, 3)))
     at_2, at_z2 = to(at_3, 1), to(at_z1, 3)
     mixed = (middle + out_rows[0] + out_across.astype(f32)).astype(bf16)[None]
     experts = unpack_experts(

time: 525 us -> 519 us (0.989)
  the two profiles are of different devices: /device:TPU:0 before, /device:TPU:108 now
where the time goes in v15:
time: 519 us; the launch traced here: 510 us
  waiting for transfers between devices  185 us (36%)
  Pallas kernels  150 us (29%)
  starting transfers between devices  92.9 us (18%)
  local copies, waits for them, and re-layouts  42.3 us (8%)
  other arithmetic  15.9 us (3%)
  between operations  14.8 us (3%)
  matrix products  9.51 us (2%)
    ppermute x12, waiting for transfers between devices, to(): return lax.ppermute(rows, 'ctx', [(i, i ^ k) for i in range(N_CTX)])  59.4 us
    all_to_all x8, starting transfers between devices, swap_all(): lax.all_to_all(rows, axis, split_axis=0, concat_axis=0, tiled=True, axis_...  58.2 us
    all_to_all x8, waiting for transfers between devices, swap_all(): lax.all_to_all(rows, axis, split_axis=0, concat_axis=0, tiled=True, axis_...  45.3 us
    ppermute x12, starting transfers between devices, to(): return lax.ppermute(rows, 'ctx', [(i, i ^ k) for i in range(N_CTX)])  29.2 us
    pallas_call x1, Pallas kernels, expert_back(): pl.pallas_call(expert_kernel, grid_spec=pltpu.PrefetchScalarGridSpec(num_...  29 us
    all_gather x1, waiting for transfers between devices, on_device(): hidden_all = lax.all_gather(hidden_two, 'exp', axis=0, tiled=True)  23.6 us
    pallas_call x2, Pallas kernels, expert_weights(): pl.pallas_call(lambda *refs: expert_weights_kernel(halved, *refs), grid_s...  22 us
    unnamed x110, local copies, waits for them, and re-layouts  21.4 us
  transfers between devices with their start and end apart: 33, of which 18 were waited for; matrix products, arithmetic and copies ran while one was open for 9% of the time, Pallas kernels for 22%

profile of v15, /device:TPU:108, one launch (start us, length us, event | category | flops | bytes accessed | tf_op | source)
XLA Modules:
  0.0 509.9 jit_solution(3653959128300472465)
XLA Ops:
  14.6 5.7 %all-to-all-start = ((bf16[16,1,192]{2,1,0:T(2,128)(2,1)}), bf16[16,1,192]{2,1,0:T(2,128)(2,1)S(1)}, u32[]{:S(2)}, u32[]{:S(2)}) async-start(bf16[16,1,192]{2,1,0:T(2,128)(2,1)} %broadcast_in_dim.24), calls=%async_computation | async-start | bytes 32768 | tf_op jit(solution)/shard_map/all_to_all | solution.py:1002
  20.3 5.5 %collective-permute-done = bf16[1,128,1536]{2,1,0:T(8,128)(2,1)S(1)} collective-permute-done((bf16[1,128,1536]{2,1,0:T(8,128)(2,1)S(1)}, bf16[1,128,1536]{2,1,0:T(8,128)(2,1)S(1)}, u32[]{:S(2)}, u32[]{:S(2)}) %collective-permute-start) | collective-permute-done | bytes 393248 | tf_op jit(solution)/shard_map/ppermute | solution.py:1054
  28.0 4.9 all-to-all-start.1
  40.4 27.6 %all-to-all-done.1 = bf16[4,2,128,1536]{3,2,1,0:T(8,128)(2,1)S(1)} async-done(((bf16[4,2,128,1536]{3,2,1,0:T(8,128)(2,1)}), bf16[4,2,128,1536]{3,2,1,0:T(8,128)(2,1)S(1)}, u32[]{:S(2)}, u32[]{:S(2)}) %all-to-all-start.1) | async-done | bytes 3145760 | tf_op jit(solution)/shard_map/all_to_all | solution.py:1002
  68.0 5.8 %all-to-all-start.2 = ((bf16[16,96,128]{2,1,0:T(8,128)(2,1)}), bf16[16,96,128]{2,1,0:T(8,128)(2,1)}, u32[]{:S(2)}, u32[]{:S(2)}) async-start(bf16[16,96,128]{2,1,0:T(8,128)(2,1)} %copy.62), calls=%async_computation.2 | async-start | bytes 786432 | tf_op jit(solution)/shard_map/all_to_all | solution.py:1002
  81.0 3.6 all-to-all-done.2
  84.5 4.6 all-gather.4.cloned.1.call-done.w_ref.wq_ref.wkv_ref
  91.0 7.7 %project.1 = (bf16[128,1536]{1,0:T(8,128)(2,1)S(1)}, bf16[8,128,1024]{2,1,0:T(8,128)(2,1)S(1)}) custom-call(bf16[1,128,1536]{2,1,0:T(8,128)(2,1)S(1)} %copy-done.14, bf16[8,128,1536]{2,1,0:T(8,128)(2,1)S(1)} %copy-done.2, bf16[1536,4096]{1,0:T(8,128)(2,1)} %all-gather.4.cloned.1.call-done.w_ref.wq_ref.wkv_ref), custom_call_target="tpu_custom_call" | custom-call | bytes 29520000 | tf_op jit(solution)/shard_map/project/pallas_call | solution.py:799
  98.7 5.8 %attend.1 = (bf16[128,1536]{1,0:T(8,128)(2,1)S(1)}, f32[128,1536]{1,0:T(8,128)S(1)}, f32[1536,128]{1,0:T(8,128)S(1)}) custom-call(s32[1]{0:T(128)} %bitcast.ctx_ref.refs_0_, bf16[128,1536]{1,0:T(8,128)(2,1)S(1)} %get-tuple-element.109.q_ref, bf16[8,128,1024]{2,1,0:T(8,128)(2,1)S(1)} %get-tuple-element.110.k_ref.v_ref, ...), custom_call_target="tpu_custom_call" | custom-call | bytes 22140000 | tf_op jit(solution)/shard_map/attend/pallas_call | solution.py:99
  107.1 4.5 middle_norm.1
  112.4 12.1 %collective-permute-done.1 = bf16[1,128,1536]{2,1,0:T(8,128)(2,1)S(1)} collective-permute-done((bf16[1,128,1536]{2,1,0:T(8,128)(2,1)S(1)}, bf16[1,128,1536]{2,1,0:T(8,128)(2,1)S(1)}, u32[]{:S(2)}, u32[]{:S(2)}) %collective-permute-start.1) | collective-permute-done | bytes 393248 | tf_op jit(solution)/shard_map/ppermute | solution.py:1054
  126.5 4.8 all-to-all-start.3
  133.3 11.0 %all-gather.8.cloned.1.call-done = bf16[2048,1664]{1,0:T(8,128)(2,1)} async-done(((bf16[128,1664]{1,0:T(8,128)(2,1)}), bf16[2048,1664]{1,0:T(8,128)(2,1)}) %all-gather.8.cloned.1.call-update) | async-done | bytes 6815760 | tf_op jit(solution)/shard_map/all_gather | solution.py:1047
  144.3 13.7 %place_rows.1 = (bf16[8,2,128,128]{3,2,1,0:T(8,128)(2,1)}, bf16[2,2,384,1536]{3,2,1,0:T(8,128)(2,1)}, f32[2,2,384,512]{3,2,1,0:T(8,128)}, f32[8,2,128,128]{3,2,1,0:T(8,128)}, f32[2,2,384,128]{3,2,1,0:T(8,128)}) custom-call(s32[1]{0:T(128)} %bitcast.7.at_ref, bf16[8,2,128,1664]{3,2,1,0:T(8,128)(2,1)} %bitcast.84, bf16[2,512,1536]{2,1,0:T(8,128)(2,1)} %wd_ref.1, ...), custom_call_target="tpu_custom_call" | custom-call | bytes 51660000 | tf_op jit(solution)/shard_map/place_rows/pallas_call | solution.py:368
  158.0 9.0 %all-to-all-done.3 = bf16[4,2,128,1536]{3,2,1,0:T(8,128)(2,1)S(1)} async-done(((bf16[4,2,128,1536]{3,2,1,0:T(8,128)(2,1)}), bf16[4,2,128,1536]{3,2,1,0:T(8,128)(2,1)S(1)}, u32[]{:S(2)}, u32[]{:S(2)}) %all-to-all-start.3) | async-done | bytes 3145760 | tf_op jit(solution)/shard_map/all_to_all | solution.py:1002
  167.0 23.6 %all-gather.6.cloned.1.call-done = bf16[2048,1536]{1,0:T(8,128)(2,1)} async-done(((bf16[128,1536]{1,0:T(8,128)(2,1)}), bf16[2048,1536]{1,0:T(8,128)(2,1)}) %all-gather.6.cloned.1.call-update) | async-done | bytes 6291472 | tf_op jit(solution)/shard_map/all_gather | solution.py:1077
  190.7 29.0 %expert_back.1 = (bf16[2,8,128,1536]{3,2,1,0:T(8,128)(2,1)}, bf16[2,2,384,1536]{3,2,1,0:T(8,128)(2,1)}, bf16[2,2,384,512]{3,2,1,0:T(8,128)(2,1)}, bf16[2,2,384,1...) custom-call(s32[1]{0:T(128)} %bitcast.7.at_ref, ...), custom_call_target="tpu_custom_call" | custom-call | bytes 103320000 | tf_op jit(solution)/shard_map/expert_back/pallas_call | solution.py:447
  222.1 5.5 %collective-permute-done.2 = bf16[8,128,1536]{2,1,0:T(8,128)(2,1)S(1)} collective-permute-done((bf16[8,128,1536]{2,1,0:T(8,128)(2,1)S(1)}, bf16[8,128,1536]{2,1,0:T(8,128)(2,1)S(1)}, u32[]{:S(2)}, u32[]{:S(2)}) %collective-permute-start.2) | collective-permute-done | bytes 3145760 | tf_op jit(solution)/shard_map/ppermute | solution.py:1089
  227.7 2.6 fusion
  230.3 5.7 %all-to-all-start.4 = ((bf16[8,128,1536]{2,1,0:T(8,128)(2,1)}), bf16[8,128,1536]{2,1,0:T(8,128)(2,1)}, u32[]{:S(2)}, u32[]{:S(2)}) async-start(bf16[8,128,1536]{2,1,0:T(8,128)(2,1)} %fusion), calls=%async_computation.4 | async-start | bytes 6291456 | tf_op jit(solution)/shard_map/all_to_all | solution.py:1002
  236.0 10.9 %expert_weights.2 = (bf16[9216,128]{1,0:T(8,128)(2,1)}, bf16[9216,128]{1,0:T(8,128)(2,1)}) custom-call(s32[1]{0:T(128)} %bitcast.ctx_ref.refs_0_, bf16[2,768,1536]{2,1,0:T(8,128)(2,1)} %bitcast.91, bf16[2,768,1536]{2,1,0:T(8,128)(2,1)} %bitcast.89, bf16[2,768,512]{2,1,0:T(8,128)(2,1)} %bitcast.74, bf16[2,768,1024]{2,1,0:T(8,128)(2,1)} %bitcast.85, ...), custom_call_target="tpu_custom_call" | custom-call | bytes 7380000 | tf_op jit(solution)/shard_map/expert_weights/pallas_call | solution.py:899
  247.4 11.1 %expert_weights.3 = (bf16[4608,128]{1,0:T(8,128)(2,1)}, bf16[4608,128]{1,0:T(8,128)(2,1)}, bf16[4608,128]{1,0:T(8,128)(2,1)}, bf16[4608,128]{1,0:T(8,128)(2,1)}) custom-call(s32[1]{0:T(128)} %bitcast.ctx_ref.refs_0_, bf16[2,768,1536]{2,1,0:T(8,128)(2,1)} %bitcast.92, bf16[2,768,1536]{2,1,0:T(8,128)(2,1)} %bitcast.90, bf16[2,768,512]{2,1,0:T(8,128)(2,1)} %bitcast.75, ...), custom_call_target="tpu_custom_call" | custom-call | bytes 7380000 | tf_op jit(solution)/shard_map/expert_weights/pallas_call | solution.py:899
  260.7 5.4 %convolution_convert_fusion = bf16[1536,128]{1,0:T(8,128)(2,1)} fusion(bf16[2048,1536]{1,0:T(8,128)(2,1)} %all-gather.6.cloned.1.call-done, bf16[2048,128]{1,0:T(8,128)(2,1)S(1)} %bitcast.101), kind=kOutput, calls=%fused_computation.3 | convolution fusion | flops 805502976 | bytes 7208960 | tf_op jit(solution)/shard_map/dot_general | solution.py:39
  269.1 9.8 %expert_output.1.own_ref = bf16[2,8,128,1536]{3,2,1,0:T(8,128)(2,1)} custom-call(s32[1]{0:T(128)} %bitcast.7.at_ref, bf16[2,2,384,512]{3,2,1,0:T(8,128)(2,1)S(1)} %copy-done.3, f32[2,2,384,128]{3,2,1,0:T(8,128)S(1)} %copy-done.26, bf16[8,2,128,128]{3,2,1,0:T(8,128)(2,1)S(1)} %copy-done.10, bf16[8,2,128,128]{3,2,1,0:T(8,128)(2,1)S(1)} %copy-done.6, ...), custom_call_target="tpu_custom_call" | custom-call | bytes 7380000 | tf_op jit(solution)/shard_map/expert_output/pallas_call | solution.py:499
  278.9 4.1 fusion.8
  284.4 5.6 %middle_back.1 = (f32[128,1536]{1,0:T(8,128)S(1)}, bf16[128,1536]{1,0:T(8,128)(2,1)S(1)}, bf16[128,1536]{1,0:T(8,128)(2,1)S(1)}, f32[16,128]{1,0:T(8,128)S(1)}) custom-call(bf16[8,128,1536]{2,1,0:T(8,128)(2,1)} %all-to-all-done.4.pieces_ref, f32[128,1536]{1,0:T(8,128)S(1)} %copy-done.7, bf16[128,1536]{1,0:T(8,128)(2,1)S(1)} %bitcast.81, ...), custom_call_target="tpu_custom_call" | custom-call | bytes 3690000 | tf_op jit(solution)/shard_map/middle_back/pallas_call | solution.py:290
  293.0 10.3 %attend_back.1 = (bf16[128,1536]{1,0:T(8,128)(2,1)}, bf16[4,1776,128]{2,1,0:T(8,128)(2,1)}, bf16[4,1776,128]{2,1,0:T(8,128)(2,1)}) custom-call(s32[1]{0:T(128)} %bitcast.ctx_ref.refs_0_, bf16[128,1536]{1,0:T(8,128)(2,1)} %copy-done.12, bf16[128,1536]{1,0:T(8,128)(2,1)} %copy-done.31, f32[128,1536]{1,0:T(8,128)} %copy-done.24, f32[1536,128]{1,0:T(8,128)} %copy-done.25, ...), custom_call_target="tpu_custom_call" | custom-call | bytes 7380000 | tf_op jit(solution)/shard_map/attend_back/pallas_call | solution.py:202
  304.9 3.3 slice_bitcast_fusion.1
  308.8 2.9 collective-permute-done.4.relay_b.got_31
  311.7 4.4 piece_sums.2
  316.1 2.4 collective-permute-start.10
  320.0 2.9 spread_sums.1
  324.2 18.9 %collective-permute-done.10.got_11 = bf16[4608,128]{1,0:T(8,128)(2,1)S(1)} collective-permute-done((bf16[4608,128]{1,0:T(8,128)(2,1)S(1)}, bf16[4608,128]{1,0:T(8,128)(2,1)S(1)}, u32[]{:S(2)}, u32[]{:S(2)}) %collective-permute-start.10) | collective-permute-done | bytes 1179680 | tf_op jit(solution)/shard_map/ppermute | solution.py:1104
  352.4 5.9 %all-to-all-start.5 = ((bf16[4,2160,128]{2,1,0:T(8,128)(2,1)}), bf16[4,2160,128]{2,1,0:T(8,128)(2,1)}, u32[]{:S(2)}, u32[]{:S(2)}) async-start(bf16[4,2160,128]{2,1,0:T(8,128)(2,1)} %merge_shares.1), calls=%async_computation.5 | async-start | bytes 4423680 | tf_op jit(solution)/shard_map/all_to_all | solution.py:1002
  358.2 17.2 %collective-permute-done.12 = bf16[4608,128]{1,0:T(8,128)(2,1)} collective-permute-done((bf16[4608,128]{1,0:T(8,128)(2,1)}, bf16[4608,128]{1,0:T(8,128)(2,1)}, u32[]{:S(2)}, u32[]{:S(2)}) %collective-permute-start.12) | collective-permute-done | bytes 1179680 | tf_op jit(solution)/shard_map/ppermute | solution.py:1104
  380.9 5.1 all-to-all-done.5.got_ref
  385.9 7.1 %column_grads.1 = (bf16[16,112,512]{2,1,0:T(8,128)(2,1)}, bf16[8,128,128]{2,1,0:T(8,128)(2,1)}, bf16[96,128]{1,0:T(8,128)(2,1)}) custom-call(bf16[4,2160,128]{2,1,0:T(8,128)(2,1)} %all-to-all-done.5.got_ref, bf16[8,128,1536]{2,1,0:T(8,128)(2,1)} %copy-done.1, bf16[8,128,1536]{2,1,0:T(8,128)(2,1)} %bitcast.93), custom_call_target="tpu_custom_call" | custom-call | bytes 29520000 | tf_op jit(solution)/shard_map/column_grads/pallas_call | solution.py:614
  393.0 5.7 %all-to-all-start.6 = ((bf16[16,112,512]{2,1,0:T(8,128)(2,1)}), bf16[16,112,512]{2,1,0:T(8,128)(2,1)S(1)}, u32[]{:S(2)}, u32[]{:S(2)}) async-start(bf16[16,112,512]{2,1,0:T(8,128)(2,1)} %get-tuple-element.164), calls=%async_computation.6 | async-start | bytes 3670016 | tf_op jit(solution)/shard_map/all_to_all | solution.py:1002
  398.7 9.3 %collective-permute-done.15.refs_4_ = bf16[4608,128]{1,0:T(8,128)(2,1)} collective-permute-done((bf16[4608,128]{1,0:T(8,128)(2,1)S(1)}, bf16[4608,128]{1,0:T(8,128)(2,1)}, u32[]{:S(2)}, u32[]{:S(2)}) %collective-permute-start.15) | collective-permute-done | bytes 1179680 | tf_op jit(solution)/shard_map/ppermute | solution.py:1104
  409.4 12.4 %collective-permute-start.19 = (bf16[4608,128]{1,0:T(8,128)(2,1)}, bf16[4608,128]{1,0:T(8,128)(2,1)}, u32[]{:S(2)}, u32[]{:S(2)}) collective-permute-start(bf16[4608,128]{1,0:T(8,128)(2,1)} %collective-permute-done.15.refs_4_), channel_id=1, source_target_pairs={{0,48},{16,32},{32,16},{48,0},{64,112},{80,96},{96,80},{112,64},{1... | collective-permute-start | bytes 3538952 | tf_op jit(solution)/shard_map/ppermute | solution.py:1104
  421.8 3.0 convert_add_fusion.1
  424.8 2.5 collective-permute-start.20
  427.6 9.7 %collective-permute-done.18.refs_2_ = bf16[4608,128]{1,0:T(8,128)(2,1)} collective-permute-done((bf16[4608,128]{1,0:T(8,128)(2,1)}, bf16[4608,128]{1,0:T(8,128)(2,1)}, u32[]{:S(2)}, u32[]{:S(2)}) %collective-permute-start.18) | collective-permute-done | bytes 1179680 | tf_op jit(solution)/shard_map/ppermute | solution.py:1104
  438.8 19.6 %all-to-all-start.7 = ((bf16[8,864,128]{2,1,0:T(8,128)(2,1)}), bf16[8,864,128]{2,1,0:T(8,128)(2,1)S(1)}, u32[]{:S(2)}, u32[]{:S(2)}) async-start(bf16[8,864,128]{2,1,0:T(8,128)(2,1)} %pad_maximum_fusion), calls=%async_computation.7 | async-start | bytes 3538944 | tf_op jit(solution)/shard_map/all_to_all | solution.py:1002
  462.1 16.3 %collective-permute-done.14 = bf16[128,1536]{1,0:T(8,128)(2,1)S(1)} collective-permute-done((bf16[128,1536]{1,0:T(8,128)(2,1)}, bf16[128,1536]{1,0:T(8,128)(2,1)S(1)}, u32[]{:S(2)}, u32[]{:S(2)}) %collective-permute-start.14) | collective-permute-done | bytes 393248 | tf_op jit(solution)/shard_map/ppermute | solution.py:1174
  481.2 6.0 %unpack_experts.2 = (f32[2,1536,512]{2,1,0:T(8,128)}, f32[2,1536,512]{2,1,0:T(8,128)}, f32[2,512,1536]{2,1,0:T(8,128)}) custom-call(s32[1]{0:T(128)} %bitcast.ctx_ref.refs_0_, bf16[4608,128]{1,0:T(8,128)(2,1)S(1)} %add_convert_fusion.refs_1_, bf16[4608,128]{1,0:T(8,128)(2,1)} %collective-permute-done.16.refs_2_, ...), custom_call_target="tpu_custom_call" | custom-call | bytes 29520000 | tf_op jit(solution)/shard_map/unpack_experts/pallas_call | solution.py:943
  489.1 7.0 %input_back.1 = bf16[128,1536]{1,0:T(8,128)(2,1)} custom-call(bf16[128,1536]{1,0:T(8,128)(2,1)S(1)} %copy-done.29, bf16[8,864,128]{2,1,0:T(8,128)(2,1)S(1)} %all-to-all-done.7.got_ref, bf16[1536,4096]{1,0:T(8,128)(2,1)} %all-gather.4.cloned.1.call-done.w_ref.wq_ref.wkv_ref, bf16[1536,4096]{1,0:T(8,128)(2,1)} %all-gather.4.cloned.1.call-done.w_ref.wq_ref.wkv_ref, ...), custom_call_target="tpu_custom_call" | custom-call | bytes 25830000 | tf_op jit(solution)/shard_map/input_back/pallas_call | solution.py:743
  496.7 6.2 %unpack_experts.3 = (f32[2,1536,512]{2,1,0:T(8,128)}, f32[2,1536,512]{2,1,0:T(8,128)}, f32[2,512,1536]{2,1,0:T(8,128)}) custom-call(s32[1]{0:T(128)} %bitcast.ctx_ref.refs_0_, bf16[4608,128]{1,0:T(8,128)(2,1)} %collective-permute-done.20.refs_1_, ...), custom_call_target="tpu_custom_call", output_to_operand_aliasing={{0}: (5, {}), {1}: (6, {}), {2}: (7, {})} | custom-call | bytes 29520000 | tf_op jit(solution)/shard_map/unpack_experts/pallas_call | solution.py:943
  (191 shorter events, 77.4 us)
Async XLA Ops:
  7.2 6.7 %copy-start.46 = (bf16[96]{0:T(256)(128)(2,1)S(1)}, bf16[96]{0:T(256)(128)(2,1)}, u32[]{:S(2)}) copy-start(bf16[96]{0:T(256)(128)(2,1)} %param.19) | copy-start | bytes 580
  7.2 81.8 %all-gather.4.cloned.1.call-start = ((), (), s32[]{:S(2)}) async-start(), calls=%async_computation.8 | async-start | bytes 13369344 | tf_op jit(solution)/shard_map/all_gather | solution.py:1040
  12.0 132.3 %all-gather.8.cloned.1.call-start = ((), (), s32[]{:S(2)}) async-start(), calls=%async_computation.10 | async-start | bytes 7241728 | tf_op jit(solution)/shard_map/all_gather | solution.py:1047
  13.3 12.6 %collective-permute-start = (bf16[1,128,1536]{2,1,0:T(8,128)(2,1)S(1)}, bf16[1,128,1536]{2,1,0:T(8,128)(2,1)S(1)}, u32[]{:S(2)}, u32[]{:S(2)}) collective-permute-start(bf16[1,128,1536]{2,1,0:T(8,128)(2,1)S(1)} %copy-done.4), channel_id=1, source_target_pairs={{0,64},{16,80},{32,96},{48,112},{64,0},{80,16},{96,32},{112,48},{1... | collective-permute-start | bytes 1179656 | tf_op jit(solution)/shard_map/ppermute | solution.py:1054
  14.6 11.4 %all-to-all-start = ((bf16[16,1,192]{2,1,0:T(2,128)(2,1)}), bf16[16,1,192]{2,1,0:T(2,128)(2,1)S(1)}, u32[]{:S(2)}, u32[]{:S(2)}) async-start(bf16[16,1,192]{2,1,0:T(2,128)(2,1)} %broadcast_in_dim.24), calls=%async_computation | async-start | bytes 32768 | tf_op jit(solution)/shard_map/all_to_all | solution.py:1002
  28.0 40.0 %all-to-all-start.1 = ((bf16[4,2,128,1536]{3,2,1,0:T(8,128)(2,1)}), bf16[4,2,128,1536]{3,2,1,0:T(8,128)(2,1)S(1)}, u32[]{:S(2)}, u32[]{:S(2)}) async-start(bf16[4,2,128,1536]{3,2,1,0:T(8,128)(2,1)} %broadcast_in_dim.25), calls=%async_computation.1 | async-start | bytes 6291456 | tf_op jit(solution)/shard_map/all_to_all | solution.py:1002
  68.0 16.5 %all-to-all-start.2 = ((bf16[16,96,128]{2,1,0:T(8,128)(2,1)}), bf16[16,96,128]{2,1,0:T(8,128)(2,1)}, u32[]{:S(2)}, u32[]{:S(2)}) async-start(bf16[16,96,128]{2,1,0:T(8,128)(2,1)} %copy.62), calls=%async_computation.2 | async-start | bytes 786432 | tf_op jit(solution)/shard_map/all_to_all | solution.py:1002
  73.8 116.8 %all-gather.6.cloned.1.call-start = ((), (), s32[]{:S(2)}) async-start(), calls=%async_computation.9 | async-start | bytes 6684672 | tf_op jit(solution)/shard_map/all_gather | solution.py:1077
  77.6 11.5 %copy-start.14 = (bf16[1,128,1536]{2,1,0:T(8,128)(2,1)S(1)}, bf16[1,128,1536]{2,1,0:T(8,128)(2,1)}, u32[]{:S(2)}) copy-start(bf16[1,128,1536]{2,1,0:T(8,128)(2,1)} %copy-done.13) | copy-start | bytes 1179652
  111.6 12.8 %collective-permute-start.1 = (bf16[1,128,1536]{2,1,0:T(8,128)(2,1)S(1)}, bf16[1,128,1536]{2,1,0:T(8,128)(2,1)S(1)}, u32[]{:S(2)}, u32[]{:S(2)}) collective-permute-start(bf16[1,128,1536]{2,1,0:T(8,128)(2,1)S(1)} %bitcast.82), channel_id=1, source_target_pairs={{0,64},{16,80},{32,96},{48,112},{64,0},{80,16},{96,32},{112,48},{1... | collective-permute-start | bytes 1179656 | tf_op jit(solution)/shard_map/ppermute | solution.py:1054
  126.5 40.5 %all-to-all-start.3 = ((bf16[4,2,128,1536]{3,2,1,0:T(8,128)(2,1)}), bf16[4,2,128,1536]{3,2,1,0:T(8,128)(2,1)S(1)}, u32[]{:S(2)}, u32[]{:S(2)}) async-start(bf16[4,2,128,1536]{3,2,1,0:T(8,128)(2,1)} %broadcast_in_dim.27), calls=%async_computation.3 | async-start | bytes 6291456 | tf_op jit(solution)/shard_map/all_to_all | solution.py:1002
  133.2 11.1 %copy-start.8 = (bf16[128,1536]{1,0:T(8,128)(2,1)}, bf16[128,1536]{1,0:T(8,128)(2,1)S(1)}, u32[]{:S(2)}) copy-start(bf16[128,1536]{1,0:T(8,128)(2,1)S(1)} %constant_dynamic-update-slice_fusion.4.sdown_ref.sd_ref) | copy-start | bytes 1179652
  167.0 52.6 %copy-start.37 = (bf16[4,2,128,1536]{3,2,1,0:T(8,128)(2,1)}, bf16[4,2,128,1536]{3,2,1,0:T(8,128)(2,1)S(1)}, u32[]{:S(2)}) copy-start(bf16[4,2,128,1536]{3,2,1,0:T(8,128)(2,1)S(1)} %all-to-all-done.3) | copy-start | bytes 9437188
  219.7 8.0 %copy-start.38 = (bf16[2,8,128,1536]{3,2,1,0:T(8,128)(2,1)S(1)}, bf16[2,8,128,1536]{3,2,1,0:T(8,128)(2,1)}, u32[]{:S(2)}) copy-start(bf16[2,8,128,1536]{3,2,1,0:T(8,128)(2,1)} %get-tuple-element.122) | copy-start | bytes 18874372
  221.9 5.7 %collective-permute-start.2 = (bf16[8,128,1536]{2,1,0:T(8,128)(2,1)S(1)}, bf16[8,128,1536]{2,1,0:T(8,128)(2,1)S(1)}, u32[]{:S(2)}, u32[]{:S(2)}) collective-permute-start(bf16[8,128,1536]{2,1,0:T(8,128)(2,1)S(1)} %slice_bitcast_fusion), channel_id=1, source_target_pairs={{0,1},{1,0},{2,3},{3,2},{4,5},{5,4},{6,7},{7,6},{8,9},{9,8},{10,11... | collective-permute-start | bytes 9437192 | tf_op jit(solution)/shard_map/ppermute | solution.py:1089
  230.3 53.7 %all-to-all-start.4 = ((bf16[8,128,1536]{2,1,0:T(8,128)(2,1)}), bf16[8,128,1536]{2,1,0:T(8,128)(2,1)}, u32[]{:S(2)}, u32[]{:S(2)}) async-start(bf16[8,128,1536]{2,1,0:T(8,128)(2,1)} %fusion), calls=%async_computation.4 | async-start | bytes 6291456 | tf_op jit(solution)/shard_map/all_to_all | solution.py:1002
  246.9 13.8 %copy-start.44 = (bf16[8,2,128,128]{3,2,1,0:T(8,128)(2,1)S(1)}, bf16[8,2,128,128]{3,2,1,0:T(8,128)(2,1)}, u32[]{:S(2)}) copy-start(bf16[8,2,128,128]{3,2,1,0:T(8,128)(2,1)} %get-tuple-element.137) | copy-start | bytes 1572868
  246.9 61.9 %collective-permute-start.3 = (bf16[9216,128]{1,0:T(8,128)(2,1)}, bf16[9216,128]{1,0:T(8,128)(2,1)}, u32[]{:S(2)}, u32[]{:S(2)}) collective-permute-start(bf16[9216,128]{1,0:T(8,128)(2,1)} %get-tuple-element.126), channel_id=1, source_target_pairs={{0,16},{16,0},{32,48},{48,32},{64,80},{80,64},{96,112},{112,96},{1... | collective-permute-start | bytes 7077896 | tf_op jit(solution)/shard_map/ppermute | solution.py:1104
  258.5 53.1 %collective-permute-start.4 = (bf16[9216,128]{1,0:T(8,128)(2,1)}, bf16[9216,128]{1,0:T(8,128)(2,1)}, u32[]{:S(2)}, u32[]{:S(2)}) collective-permute-start(bf16[9216,128]{1,0:T(8,128)(2,1)} %get-tuple-element.135), channel_id=1, source_target_pairs={{0,48},{16,32},{32,16},{48,0},{64,112},{80,96},{96,80},{112,64},{1... | collective-permute-start | bytes 7077896 | tf_op jit(solution)/shard_map/ppermute | solution.py:1104
  303.3 8.4 %copy-start.19 = (bf16[4608,128]{1,0:T(8,128)(2,1)S(1)}, bf16[4608,128]{1,0:T(8,128)(2,1)}, u32[]{:S(2)}) copy-start(bf16[4608,128]{1,0:T(8,128)(2,1)} %get-tuple-element.128.p0) | copy-start | bytes 3538948
  303.3 8.4 %copy-start.20 = (bf16[4608,128]{1,0:T(8,128)(2,1)S(1)}, bf16[4608,128]{1,0:T(8,128)(2,1)}, u32[]{:S(2)}) copy-start(bf16[4608,128]{1,0:T(8,128)(2,1)} %get-tuple-element.134.p6) | copy-start | bytes 3538948
  303.3 8.4 %copy-start.21 = (bf16[4608,128]{1,0:T(8,128)(2,1)S(1)}, bf16[4608,128]{1,0:T(8,128)(2,1)}, u32[]{:S(2)}) copy-start(bf16[4608,128]{1,0:T(8,128)(2,1)} %get-tuple-element.132.p1) | copy-start | bytes 3538948
  303.3 8.4 %copy-start.22 = (bf16[4608,128]{1,0:T(8,128)(2,1)S(1)}, bf16[4608,128]{1,0:T(8,128)(2,1)}, u32[]{:S(2)}) copy-start(bf16[4608,128]{1,0:T(8,128)(2,1)} %get-tuple-element.133.p3) | copy-start | bytes 3538948
  303.3 42.6 %collective-permute-start.9 = (bf16[4,1776,128]{2,1,0:T(8,128)(2,1)}, bf16[4,1776,128]{2,1,0:T(8,128)(2,1)S(1)}, u32[]{:S(2)}, u32[]{:S(2)}) collective-permute-start(bf16[4,1776,128]{2,1,0:T(8,128)(2,1)} %get-tuple-element.153), channel_id=1, source_target_pairs={{0,64},{16,80},{32,96},{48,112},{64,0},{80,16},{96,32},{112,48},{1... | collective-permute-start | bytes 5455880 | tf_op jit(solution)/shard_map/ppermute | solution.py:1132
  308.2 11.8 %collective-permute-start.5 = (bf16[4,128,1536]{2,1,0:T(8,128)(2,1)}, bf16[4,128,1536]{2,1,0:T(8,128)(2,1)S(1)}, u32[]{:S(2)}, u32[]{:S(2)}) collective-permute-start(bf16[4,128,1536]{2,1,0:T(8,128)(2,1)} %get-tuple-element.201), channel_id=1, source_target_pairs={{0,1},{1,0},{2,3},{3,2},{4,5},{5,4},{6,7},{7,6},{8,9},{9,8},{10,11... | collective-permute-start | bytes 4718600 | tf_op jit(solution)/shard_map/ppermute | solution.py:1154
  308.2 11.8 %collective-permute-start.6 = (bf16[4,128,1536]{2,1,0:T(8,128)(2,1)S(1)}, bf16[4,128,1536]{2,1,0:T(8,128)(2,1)S(1)}, u32[]{:S(2)}, u32[]{:S(2)}) collective-permute-start(bf16[4,128,1536]{2,1,0:T(8,128)(2,1)S(1)} %get-tuple-element.200), channel_id=1, source_target_pairs={{0,1},{1,0},{2,3},{3,2},{4,5},{5,4},{6,7},{7,6},{8,9},{9,8},{10,11... | collective-permute-start | bytes 4718600 | tf_op jit(solution)/shard_map/ppermute | solution.py:1155
  311.7 8.3 %slice-start = ((s8[6291456]{0:T(1024)(128)(4,1)}), s8[4194304]{0:T(1024)(128)(4,1)S(1)}, s32[]{:S(2)}) async-start(s8[6291456]{0:T(1024)(128)(4,1)} %bitcast.72), calls=%async_computation.11 | async-start | bytes 8388608
  311.7 8.3 %slice-start.1 = ((s8[6291456]{0:T(1024)(128)(4,1)}), s8[2097152]{0:T(1024)(128)(4,1)S(1)}, s32[]{:S(2)}) async-start(s8[6291456]{0:T(1024)(128)(4,1)} %bitcast.72), calls=%async_computation.12 | async-start | bytes 4194304
  316.1 26.9 %collective-permute-start.10 = (bf16[4608,128]{1,0:T(8,128)(2,1)S(1)}, bf16[4608,128]{1,0:T(8,128)(2,1)S(1)}, u32[]{:S(2)}, u32[]{:S(2)}) collective-permute-start(bf16[4608,128]{1,0:T(8,128)(2,1)S(1)} %get-tuple-element.156), channel_id=1, source_target_pairs={{0,16},{16,0},{32,48},{48,32},{64,80},{80,64},{96,112},{112,96},{1... | collective-permute-start | bytes 3538952 | tf_op jit(solution)/shard_map/ppermute | solution.py:1104
  318.5 26.0 %collective-permute-start.11 = (bf16[4608,128]{1,0:T(8,128)(2,1)S(1)}, bf16[4608,128]{1,0:T(8,128)(2,1)S(1)}, u32[]{:S(2)}, u32[]{:S(2)}) collective-permute-start(bf16[4608,128]{1,0:T(8,128)(2,1)S(1)} %get-tuple-element.148), channel_id=1, source_target_pairs={{0,48},{16,32},{32,16},{48,0},{64,112},{80,96},{96,80},{112,64},{1... | collective-permute-start | bytes 3538952 | tf_op jit(solution)/shard_map/ppermute | solution.py:1104
  323.0 26.0 %collective-permute-start.7 = (bf16[2,128,1536]{2,1,0:T(8,128)(2,1)S(1)}, bf16[2,128,1536]{2,1,0:T(8,128)(2,1)S(1)}, u32[]{:S(2)}, u32[]{:S(2)}) collective-permute-start(bf16[2,128,1536]{2,1,0:T(8,128)(2,1)S(1)} %get-tuple-element.151), channel_id=1, source_target_pairs={{0,4},{1,5},{2,6},{3,7},{4,0},{5,1},{6,2},{7,3},{8,12},{9,13},{10,... | collective-permute-start | bytes 2359304 | tf_op jit(solution)/shard_map/ppermute | solution.py:1149
  324.1 24.8 %collective-permute-start.8 = (bf16[2,128,1536]{2,1,0:T(8,128)(2,1)S(1)}, bf16[2,128,1536]{2,1,0:T(8,128)(2,1)S(1)}, u32[]{:S(2)}, u32[]{:S(2)}) collective-permute-start(bf16[2,128,1536]{2,1,0:T(8,128)(2,1)S(1)} %get-tuple-element.152), channel_id=1, source_target_pairs={{0,12},{1,13},{2,14},{3,15},{4,8},{5,9},{6,10},{7,11},{8,4},{9,5},... | collective-permute-start | bytes 2359304 | tf_op jit(solution)/shard_map/ppermute | solution.py:1149
  347.6 27.8 %collective-permute-start.12 = (bf16[4608,128]{1,0:T(8,128)(2,1)}, bf16[4608,128]{1,0:T(8,128)(2,1)}, u32[]{:S(2)}, u32[]{:S(2)}) collective-permute-start(bf16[4608,128]{1,0:T(8,128)(2,1)} %get-tuple-element.159), channel_id=1, source_target_pairs={{0,64},{16,80},{32,96},{48,112},{64,0},{80,16},{96,32},{112,48},{1... | collective-permute-start | bytes 3538952 | tf_op jit(solution)/shard_map/ppermute | solution.py:1104
  352.4 33.6 %all-to-all-start.5 = ((bf16[4,2160,128]{2,1,0:T(8,128)(2,1)}), bf16[4,2160,128]{2,1,0:T(8,128)(2,1)}, u32[]{:S(2)}, u32[]{:S(2)}) async-start(bf16[4,2160,128]{2,1,0:T(8,128)(2,1)} %merge_shares.1), calls=%async_computation.5 | async-start | bytes 4423680 | tf_op jit(solution)/shard_map/all_to_all | solution.py:1002
  376.9 31.1 %collective-permute-start.15 = (bf16[4608,128]{1,0:T(8,128)(2,1)S(1)}, bf16[4608,128]{1,0:T(8,128)(2,1)}, u32[]{:S(2)}, u32[]{:S(2)}) collective-permute-start(bf16[4608,128]{1,0:T(8,128)(2,1)S(1)} %add_convert_fusion.refs_1_), channel_id=1, source_target_pairs={{0,64},{16,80},{32,96},{48,112},{64,0},{80,16},{96,32},{112,48},{1... | collective-permute-start | bytes 3538952 | tf_op jit(solution)/shard_map/ppermute | solution.py:1104
  378.3 29.7 %collective-permute-start.16 = (bf16[4608,128]{1,0:T(8,128)(2,1)S(1)}, bf16[4608,128]{1,0:T(8,128)(2,1)}, u32[]{:S(2)}, u32[]{:S(2)}) collective-permute-start(bf16[4608,128]{1,0:T(8,128)(2,1)S(1)} %add_convert_fusion.refs_1_), channel_id=1, source_target_pairs={{0,16},{16,0},{32,48},{48,32},{64,80},{80,64},{96,112},{112,96},{1... | collective-permute-start | bytes 3538952 | tf_op jit(solution)/shard_map/ppermute | solution.py:1104
  379.7 28.3 %collective-permute-start.17 = (bf16[4608,128]{1,0:T(8,128)(2,1)S(1)}, bf16[4608,128]{1,0:T(8,128)(2,1)}, u32[]{:S(2)}, u32[]{:S(2)}) collective-permute-start(bf16[4608,128]{1,0:T(8,128)(2,1)S(1)} %add_convert_fusion.refs_1_), channel_id=1, source_target_pairs={{0,48},{16,32},{32,16},{48,0},{64,112},{80,96},{96,80},{112,64},{1... | collective-permute-start | bytes 3538952 | tf_op jit(solution)/shard_map/ppermute | solution.py:1104
  380.3 18.4 %collective-permute-start.13 = (bf16[2,128,1536]{2,1,0:T(8,128)(2,1)}, bf16[2,128,1536]{2,1,0:T(8,128)(2,1)}, u32[]{:S(2)}, u32[]{:S(2)}) collective-permute-start(bf16[2,128,1536]{2,1,0:T(8,128)(2,1)} %get-tuple-element.167), channel_id=1, source_target_pairs={{0,8},{1,9},{2,10},{3,11},{4,12},{5,13},{6,14},{7,15},{8,0},{9,1},... | collective-permute-start | bytes 2359304 | tf_op jit(solution)/shard_map/ppermute | solution.py:1149
  393.0 34.3 %all-to-all-start.6 = ((bf16[16,112,512]{2,1,0:T(8,128)(2,1)}), bf16[16,112,512]{2,1,0:T(8,128)(2,1)S(1)}, u32[]{:S(2)}, u32[]{:S(2)}) async-start(bf16[16,112,512]{2,1,0:T(8,128)(2,1)} %get-tuple-element.164), calls=%async_computation.6 | async-start | bytes 3670016 | tf_op jit(solution)/shard_map/all_to_all | solution.py:1002
  398.7 28.6 %copy-start.35 = (bf16[96,128]{1,0:T(8,128)(2,1)S(1)}, bf16[96,128]{1,0:T(8,128)(2,1)}, u32[]{:S(2)}) copy-start(bf16[96,128]{1,0:T(8,128)(2,1)} %get-tuple-element.170.down_ref) | copy-start | bytes 73732
  408.0 29.2 %collective-permute-start.18 = (bf16[4608,128]{1,0:T(8,128)(2,1)}, bf16[4608,128]{1,0:T(8,128)(2,1)}, u32[]{:S(2)}, u32[]{:S(2)}) collective-permute-start(bf16[4608,128]{1,0:T(8,128)(2,1)} %collective-permute-done.15.refs_4_), channel_id=1, source_target_pairs={{0,16},{16,0},{32,48},{48,32},{64,80},{80,64},{96,112},{112,96},{1... | collective-permute-start | bytes 3538952 | tf_op jit(solution)/shard_map/ppermute | solution.py:1104
  409.4 27.8 %collective-permute-start.19 = (bf16[4608,128]{1,0:T(8,128)(2,1)}, bf16[4608,128]{1,0:T(8,128)(2,1)}, u32[]{:S(2)}, u32[]{:S(2)}) collective-permute-start(bf16[4608,128]{1,0:T(8,128)(2,1)} %collective-permute-done.15.refs_4_), channel_id=1, source_target_pairs={{0,48},{16,32},{32,16},{48,0},{64,112},{80,96},{96,80},{112,64},{1... | collective-permute-start | bytes 3538952 | tf_op jit(solution)/shard_map/ppermute | solution.py:1104
  424.8 12.7 %copy-start.40 = (bf16[8,128,128]{2,1,0:T(8,128)(2,1)S(1)}, bf16[8,128,128]{2,1,0:T(8,128)(2,1)}, u32[]{:S(2)}) copy-start(bf16[8,128,128]{2,1,0:T(8,128)(2,1)} %get-tuple-element.169) | copy-start | bytes 786436
  424.8 71.3 %collective-permute-start.20 = (bf16[4608,128]{1,0:T(8,128)(2,1)}, bf16[4608,128]{1,0:T(8,128)(2,1)}, u32[]{:S(2)}, u32[]{:S(2)}) collective-permute-start(bf16[4608,128]{1,0:T(8,128)(2,1)} %collective-permute-done.17.refs_3_), channel_id=1, source_target_pairs={{0,16},{16,0},{32,48},{48,32},{64,80},{80,64},{96,112},{112,96},{1... | collective-permute-start | bytes 3538952 | tf_op jit(solution)/shard_map/ppermute | solution.py:1104
  438.8 23.2 %copy-start.47 = (bf16[96]{0:T(256)(128)(2,1)S(1)}, bf16[96]{0:T(256)(128)(2,1)}, u32[]{:S(2)}) copy-start(bf16[96]{0:T(256)(128)(2,1)} %param.19) | copy-start | bytes 580
  438.8 48.4 %all-to-all-start.7 = ((bf16[8,864,128]{2,1,0:T(8,128)(2,1)}), bf16[8,864,128]{2,1,0:T(8,128)(2,1)S(1)}, u32[]{:S(2)}, u32[]{:S(2)}) async-start(bf16[8,864,128]{2,1,0:T(8,128)(2,1)} %pad_maximum_fusion), calls=%async_computation.7 | async-start | bytes 3538944 | tf_op jit(solution)/shard_map/all_to_all | solution.py:1002
  460.3 18.1 %collective-permute-start.14 = (bf16[128,1536]{1,0:T(8,128)(2,1)}, bf16[128,1536]{1,0:T(8,128)(2,1)S(1)}, u32[]{:S(2)}, u32[]{:S(2)}) collective-permute-start(bf16[128,1536]{1,0:T(8,128)(2,1)} %fusion.5), channel_id=1, source_target_pairs={{0,2},{1,3},{2,0},{3,1},{4,6},{5,7},{6,4},{7,5},{8,10},{9,11},{10,... | collective-permute-start | bytes 1179656 | tf_op jit(solution)/shard_map/ppermute | solution.py:1174
  460.3 36.4 %collective-permute-start.21 = (bf16[4608,128]{1,0:T(8,128)(2,1)}, bf16[4608,128]{1,0:T(8,128)(2,1)}, u32[]{:S(2)}, u32[]{:S(2)}) collective-permute-start(bf16[4608,128]{1,0:T(8,128)(2,1)} %collective-permute-done.18.refs_2_), channel_id=1, source_target_pairs={{0,48},{16,32},{32,16},{48,0},{64,112},{80,96},{96,80},{112,64},{1... | collective-permute-start | bytes 3538952 | tf_op jit(solution)/shard_map/ppermute | solution.py:1104
  (35 other events, 103.0 us)
Sparse Core Ops, SparseCore 0:
  12.2 76.8 all-gather.3
  91.4 52.8 all-gather.7
  146.6 44.0 all-gather.5

commit v16 on v15

--- a/solution.py
+++ b/solution.py
@@ -725,7 +725,7 @@
     )(got, gain_column, query_weight, key_weight, value_weight)
 
 
-def input_kernel(dq_ref, got_ref, wq_ref, wkv_ref, x_ref, gain_ref, gm_ref, out_ref):
+def input_kernel(part_ref, got_ref, wkv_ref, x_ref, gain_ref, gm_ref, out_ref):
     lane = lax.broadcasted_iota(jnp.int32, (BLOCK, HEAD_DIM), 1)
     lows, highs = [], []
     for m in range(KV_HEADS):
@@ -733,20 +733,36 @@
         lows.append(low.astype(bf16))
         highs.append(high.astype(bf16))
     grad_kv = jnp.concatenate(lows + highs, axis=1)
-    grad_one = dg(dq_ref[...], wq_ref[...], NT) + dg(grad_kv, wkv_ref[...], NT)
+    grad_one = part_ref[...] + dg(grad_kv, wkv_ref[...], NT)
     inputs = x_ref[...].astype(f32)
     inv = lax.rsqrt(jnp.mean(inputs * inputs, axis=-1, keepdims=True) + epsilon)
     out_ref[...] = (gm_ref[...] + norm_back(grad_one * gain_ref[...], inputs * inv, inv)).astype(bf16)
 
 
-def input_back(grad_query, grad_kv, w_all, tokens, gain, grad_middle):
+def query_kernel(dq_ref, wq_ref, out_ref):
+    out_ref[...] = dg(dq_ref[...], wq_ref[...], NT)
+
+
+def query_back(grad_query, w_all):
+    return pl.pallas_call(
+        query_kernel,
+        grid=(1,),
+        in_specs=[whole((BLOCK, WIDTH)), w_cols(WIDTH, 0)],
+        out_specs=whole((BLOCK, WIDTH)),
+        out_shape=jax.ShapeDtypeStruct((BLOCK, WIDTH), f32),
+        cost_estimate=cost(4),
+        compiler_params=params(32),
+        name="query_back",
+    )(grad_query, w_all)
+
+
+def input_back(query_part, grad_kv, w_all, tokens, gain, grad_middle):
     return pl.pallas_call(
         input_kernel,
         grid=(1,),
         in_specs=[
             whole((BLOCK, WIDTH)),
             whole((N_CTX, BLOCK, HEAD_DIM)),
-            w_cols(WIDTH, 0),
             w_cols(2 * KV_WIDTH, 3),
             whole((BLOCK, WIDTH)),
             whole((1, WIDTH)),
@@ -754,10 +770,10 @@
         ],
         out_specs=whole((BLOCK, WIDTH)),
         out_shape=jax.ShapeDtypeStruct((BLOCK, WIDTH), bf16),
-        cost_estimate=cost(7),
-        compiler_params=params(48),
+        cost_estimate=cost(4),
+        compiler_params=params(32),
         name="input_back",
-    )(grad_query, grad_kv, w_all, w_all, tokens, gain, grad_middle)
+    )(query_part, grad_kv, w_all, tokens, gain, grad_middle)
 
 
 def norm_rows_kernel(x_ref, gain_ref, out_ref):
@@ -1175,27 +1191,30 @@
         out_rows[1].astype(bf16), "exp", [(i, i ^ 2) for i in range(N_EXP)]
     )
     owned = swap_all(columns, "exp")
+    query_part = query_back(after(grad_query, columns), w_all)
     owned, gain_sum = owned_sums(owned, grad_down)
     at_z, at_1, at_3 = lax.optimization_barrier((after(at_z, out_2), at_1, at_3))
     owned, at_z1, at_z3 = lax.optimization_barrier((owned, to(at_z, 1), to(at_z, 3)))
     at_2, at_z2 = to(at_3, 1), to(at_z1, 3)
     mixed = (middle + out_rows[0] + out_across.astype(f32)).astype(bf16)[None]
     experts = unpack_experts(
-        ctx_s, ((0, 0), (1, 0), (3, 0), (0, 1)), (after(own, owned), at_1, at_3, at_z)
+        ctx_s,
+        ((0, 0), (1, 0), (3, 0), (0, 1), (1, 1), (3, 1)),
+        (after(own, owned), at_1, at_3, at_z, at_z1, at_z3),
     )
     owned = jnp.broadcast_to(owned, (N_CTX, OWNED_ROWS, HEAD_DIM))
     owned = swap_all(jnp.concatenate([grad_kv, owned], axis=1), "ctx")
     gain_attn_sum, *dense = finish(
-        after(owned, experts[0], mixed),
+        after(owned, experts[0], mixed, query_part),
         norm_attn.astype(f32).reshape(96, 1),
         query_weight,
         key_weight,
         value_weight,
     )
-    input_grad = input_back(grad_query, owned, w_all, tokens[0], gain_attn, grad_middle)
+    input_grad = input_back(query_part, owned, w_all, tokens[0], gain_attn, grad_middle)
     at_2 = after(at_2, input_grad, *dense)
     experts = unpack_experts(
-        ctx_s, ((2, 0), (1, 1), (3, 1), (2, 1)), (at_2, at_z1, at_z3, at_z2), experts
+        ctx_s, ((2, 0), (2, 1)), (at_2, at_z2), experts
     )
     return (
         mixed,

time: 519 us -> 510 us (0.983)
  the two profiles are of different devices: /device:TPU:108 before, /device:TPU:0 now
where the time goes in v16:
time: 510 us; the launch traced here: 500 us
  waiting for transfers between devices  196 us (38%)
  Pallas kernels  145 us (28%)
  starting transfers between devices  72.6 us (14%)
  local copies, waits for them, and re-layouts  49.7 us (10%)
  other arithmetic  15.5 us (3%)
  between operations  14.9 us (3%)
  matrix products  6.73 us (1%)
    all_to_all x8, waiting for transfers between devices, swap_all(): lax.all_to_all(rows, axis, split_axis=0, concat_axis=0, tiled=True, axis_...  75.4 us
    ppermute x12, waiting for transfers between devices, to(): return lax.ppermute(rows, 'ctx', [(i, i ^ k) for i in range(N_CTX)])  68.5 us
    all_to_all x8, starting transfers between devices, swap_all(): lax.all_to_all(rows, axis, split_axis=0, concat_axis=0, tiled=True, axis_...  36.8 us
    unnamed x124, local copies, waits for them, and re-layouts  29.9 us
    pallas_call x1, Pallas kernels, expert_back(): pl.pallas_call(expert_kernel, grid_spec=pltpu.PrefetchScalarGridSpec(num_...  28.9 us
    ppermute x2, waiting for transfers between devices, of_sequence(): other = lax.ppermute(rows, 'ctx', z_swap)  26.2 us
    pallas_call x2, Pallas kernels, expert_weights(): pl.pallas_call(lambda *refs: expert_weights_kernel(halved, *refs), grid_s...  22.3 us
    ppermute x12, starting transfers between devices, to(): return lax.ppermute(rows, 'ctx', [(i, i ^ k) for i in range(N_CTX)])  19.2 us
  transfers between devices with their start and end apart: 33, of which 23 were waited for; matrix products, arithmetic and copies ran while one was open for 8% of the time, Pallas kernels for 22%

profile of v16, /device:TPU:0, one launch (start us, length us, event | category | flops | bytes accessed | tf_op | source)
XLA Modules:
  0.0 500.2 jit_solution(13959286074423983242)
XLA Ops:
  13.3 4.1 collective-permute-start
  18.0 4.8 all-to-all-start
  22.9 6.1 %collective-permute-done = bf16[1,128,1536]{2,1,0:T(8,128)(2,1)S(1)} collective-permute-done((bf16[1,128,1536]{2,1,0:T(8,128)(2,1)S(1)}, bf16[1,128,1536]{2,1,0:T(8,128)(2,1)S(1)}, u32[]{:S(2)}, u32[]{:S(2)}) %collective-permute-start) | collective-permute-done | bytes 393248 | tf_op jit(solution)/shard_map/ppermute | solution.py:1070
  31.7 4.6 all-to-all-start.1
  43.9 30.5 %all-to-all-done.1 = bf16[4,2,128,1536]{3,2,1,0:T(8,128)(2,1)S(1)} async-done(((bf16[4,2,128,1536]{3,2,1,0:T(8,128)(2,1)}), bf16[4,2,128,1536]{3,2,1,0:T(8,128)(2,1)S(1)}, u32[]{:S(2)}, u32[]{:S(2)}) %all-to-all-start.1) | async-done | bytes 3145760 | tf_op jit(solution)/shard_map/all_to_all | solution.py:1018
  74.3 5.2 %all-to-all-start.2 = ((bf16[16,96,128]{2,1,0:T(8,128)(2,1)}), bf16[16,96,128]{2,1,0:T(8,128)(2,1)}, u32[]{:S(2)}, u32[]{:S(2)}) async-start(bf16[16,96,128]{2,1,0:T(8,128)(2,1)} %copy.62), calls=%async_computation.2 | async-start | bytes 786432 | tf_op jit(solution)/shard_map/all_to_all | solution.py:1018
  86.0 4.5 all-to-all-done.2
  94.1 7.6 %project.1 = (bf16[128,1536]{1,0:T(8,128)(2,1)S(1)}, bf16[8,128,1024]{2,1,0:T(8,128)(2,1)S(1)}) custom-call(bf16[1,128,1536]{2,1,0:T(8,128)(2,1)S(1)} %copy-done.19, bf16[8,128,1536]{2,1,0:T(8,128)(2,1)S(1)} %copy-done.4, bf16[1536,4096]{1,0:T(8,128)(2,1)} %all-gather.4.cloned.1.call-done.w_ref.wq_ref.wkv_ref), custom_call_target="tpu_custom_call" | custom-call | bytes 29520000 | tf_op jit(solution)/shard_map/project/pallas_call | solution.py:815
  101.8 5.8 %attend.1 = (bf16[128,1536]{1,0:T(8,128)(2,1)S(1)}, f32[128,1536]{1,0:T(8,128)S(1)}, f32[1536,128]{1,0:T(8,128)S(1)}) custom-call(s32[1]{0:T(128)} %bitcast.ctx_ref.refs_0_, bf16[128,1536]{1,0:T(8,128)(2,1)S(1)} %get-tuple-element.110.q_ref, bf16[8,128,1024]{2,1,0:T(8,128)(2,1)S(1)} %get-tuple-element.111.k_ref.v_ref, ...), custom_call_target="tpu_custom_call" | custom-call | bytes 22140000 | tf_op jit(solution)/shard_map/attend/pallas_call | solution.py:99
  110.2 4.5 middle_norm.1
  116.4 20.1 %collective-permute-done.1 = bf16[1,128,1536]{2,1,0:T(8,128)(2,1)S(1)} collective-permute-done((bf16[1,128,1536]{2,1,0:T(8,128)(2,1)S(1)}, bf16[1,128,1536]{2,1,0:T(8,128)(2,1)S(1)}, u32[]{:S(2)}, u32[]{:S(2)}) %collective-permute-start.1) | collective-permute-done | bytes 393248 | tf_op jit(solution)/shard_map/ppermute | solution.py:1070
  138.5 4.6 all-to-all-start.3
  147.1 13.7 %place_rows.1 = (bf16[8,2,128,128]{3,2,1,0:T(8,128)(2,1)}, bf16[2,2,384,1536]{3,2,1,0:T(8,128)(2,1)}, f32[2,2,384,512]{3,2,1,0:T(8,128)}, f32[8,2,128,128]{3,2,1,0:T(8,128)}, f32[2,2,384,128]{3,2,1,0:T(8,128)}) custom-call(s32[1]{0:T(128)} %bitcast.7.at_ref, bf16[8,2,128,1664]{3,2,1,0:T(8,128)(2,1)} %bitcast.84, bf16[2,512,1536]{2,1,0:T(8,128)(2,1)} %wd_ref.1, ...), custom_call_target="tpu_custom_call" | custom-call | bytes 51660000 | tf_op jit(solution)/shard_map/place_rows/pallas_call | solution.py:368
  160.8 19.5 %all-to-all-done.3 = bf16[4,2,128,1536]{3,2,1,0:T(8,128)(2,1)S(1)} async-done(((bf16[4,2,128,1536]{3,2,1,0:T(8,128)(2,1)}), bf16[4,2,128,1536]{3,2,1,0:T(8,128)(2,1)S(1)}, u32[]{:S(2)}, u32[]{:S(2)}) %all-to-all-start.3) | async-done | bytes 3145760 | tf_op jit(solution)/shard_map/all_to_all | solution.py:1018
  180.3 12.1 %all-gather.6.cloned.1.call-done = bf16[2048,1536]{1,0:T(8,128)(2,1)} async-done(((bf16[128,1536]{1,0:T(8,128)(2,1)}), bf16[2048,1536]{1,0:T(8,128)(2,1)}) %all-gather.6.cloned.1.call-update) | async-done | bytes 6291472 | tf_op jit(solution)/shard_map/all_gather | solution.py:1093
  192.4 28.9 %expert_back.1 = (bf16[2,8,128,1536]{3,2,1,0:T(8,128)(2,1)}, bf16[2,2,384,1536]{3,2,1,0:T(8,128)(2,1)}, bf16[2,2,384,512]{3,2,1,0:T(8,128)(2,1)}, bf16[2,2,384,1...) custom-call(s32[1]{0:T(128)} %bitcast.7.at_ref, ...), custom_call_target="tpu_custom_call" | custom-call | bytes 103320000 | tf_op jit(solution)/shard_map/expert_back/pallas_call | solution.py:447
  223.9 5.4 %collective-permute-done.2 = bf16[8,128,1536]{2,1,0:T(8,128)(2,1)S(1)} collective-permute-done((bf16[8,128,1536]{2,1,0:T(8,128)(2,1)S(1)}, bf16[8,128,1536]{2,1,0:T(8,128)(2,1)S(1)}, u32[]{:S(2)}, u32[]{:S(2)}) %collective-permute-start.2) | collective-permute-done | bytes 3145760 | tf_op jit(solution)/shard_map/ppermute | solution.py:1105
  231.9 4.8 all-to-all-start.4
  236.7 10.9 %expert_weights.2 = (bf16[9216,128]{1,0:T(8,128)(2,1)}, bf16[9216,128]{1,0:T(8,128)(2,1)}) custom-call(s32[1]{0:T(128)} %bitcast.ctx_ref.refs_0_, bf16[2,768,1536]{2,1,0:T(8,128)(2,1)} %bitcast.91, bf16[2,768,1536]{2,1,0:T(8,128)(2,1)} %bitcast.89, bf16[2,768,512]{2,1,0:T(8,128)(2,1)} %bitcast.74, bf16[2,768,1024]{2,1,0:T(8,128)(2,1)} %bitcast.85, ...), custom_call_target="tpu_custom_call" | custom-call | bytes 7380000 | tf_op jit(solution)/shard_map/expert_weights/pallas_call | solution.py:915
  249.2 11.4 %expert_weights.3 = (bf16[4608,128]{1,0:T(8,128)(2,1)}, bf16[4608,128]{1,0:T(8,128)(2,1)}, bf16[4608,128]{1,0:T(8,128)(2,1)}, bf16[4608,128]{1,0:T(8,128)(2,1)}) custom-call(s32[1]{0:T(128)} %bitcast.ctx_ref.refs_0_, bf16[2,768,1536]{2,1,0:T(8,128)(2,1)} %bitcast.92, bf16[2,768,1536]{2,1,0:T(8,128)(2,1)} %bitcast.90, bf16[2,768,512]{2,1,0:T(8,128)(2,1)} %bitcast.75, ...), custom_call_target="tpu_custom_call" | custom-call | bytes 7380000 | tf_op jit(solution)/shard_map/expert_weights/pallas_call | solution.py:915
  268.5 9.8 %expert_output.1.own_ref = bf16[2,8,128,1536]{3,2,1,0:T(8,128)(2,1)} custom-call(s32[1]{0:T(128)} %bitcast.7.at_ref, bf16[2,2,384,512]{3,2,1,0:T(8,128)(2,1)S(1)} %copy-done.5, f32[2,2,384,128]{3,2,1,0:T(8,128)S(1)} %copy-done.33, bf16[8,2,128,128]{3,2,1,0:T(8,128)(2,1)S(1)} %copy-done.15, bf16[8,2,128,128]{3,2,1,0:T(8,128)(2,1)S(1)} %copy-done.8, ...), custom_call_target="tpu_custom_call" | custom-call | bytes 7380000 | tf_op jit(solution)/shard_map/expert_output/pallas_call | solution.py:499
  278.3 4.1 fusion.8
  283.8 5.6 %middle_back.1 = (f32[128,1536]{1,0:T(8,128)S(1)}, bf16[128,1536]{1,0:T(8,128)(2,1)S(1)}, bf16[128,1536]{1,0:T(8,128)(2,1)S(1)}, f32[16,128]{1,0:T(8,128)S(1)}) custom-call(bf16[8,128,1536]{2,1,0:T(8,128)(2,1)} %all-to-all-done.4.pieces_ref, f32[128,1536]{1,0:T(8,128)S(1)} %copy-done.9, bf16[128,1536]{1,0:T(8,128)(2,1)S(1)} %bitcast.81, ...), custom_call_target="tpu_custom_call" | custom-call | bytes 3690000 | tf_op jit(solution)/shard_map/middle_back/pallas_call | solution.py:290
  292.4 10.3 %attend_back.1 = (bf16[128,1536]{1,0:T(8,128)(2,1)}, bf16[4,1776,128]{2,1,0:T(8,128)(2,1)}, bf16[4,1776,128]{2,1,0:T(8,128)(2,1)}) custom-call(s32[1]{0:T(128)} %bitcast.ctx_ref.refs_0_, bf16[128,1536]{1,0:T(8,128)(2,1)} %copy-done.17, bf16[128,1536]{1,0:T(8,128)(2,1)} %copy-done.35, f32[128,1536]{1,0:T(8,128)} %copy-done.31, f32[1536,128]{1,0:T(8,128)} %copy-done.32, ...), custom_call_target="tpu_custom_call" | custom-call | bytes 7380000 | tf_op jit(solution)/shard_map/attend_back/pallas_call | solution.py:202
  302.7 3.1 collective-permute-start.9
  308.7 6.5 %collective-permute-done.4.relay_b.got_31 = bf16[9216,128]{1,0:T(8,128)(2,1)} collective-permute-done((bf16[9216,128]{1,0:T(8,128)(2,1)}, bf16[9216,128]{1,0:T(8,128)(2,1)}, u32[]{:S(2)}, u32[]{:S(2)}) %collective-permute-start.4) | collective-permute-done | bytes 2359328 | tf_op jit(solution)/shard_map/ppermute | solution.py:1120
  315.2 4.4 piece_sums.2
  328.5 18.2 %collective-permute-done.10.got_11 = bf16[4608,128]{1,0:T(8,128)(2,1)S(1)} collective-permute-done((bf16[4608,128]{1,0:T(8,128)(2,1)S(1)}, bf16[4608,128]{1,0:T(8,128)(2,1)S(1)}, u32[]{:S(2)}, u32[]{:S(2)}) %collective-permute-start.10) | collective-permute-done | bytes 1179680 | tf_op jit(solution)/shard_map/ppermute | solution.py:1120
  348.5 3.0 collective-permute-start.12
  354.9 4.5 all-to-all-start.5
  359.4 16.8 %collective-permute-done.12 = bf16[4608,128]{1,0:T(8,128)(2,1)} collective-permute-done((bf16[4608,128]{1,0:T(8,128)(2,1)S(1)}, bf16[4608,128]{1,0:T(8,128)(2,1)}, u32[]{:S(2)}, u32[]{:S(2)}) %collective-permute-start.12) | collective-permute-done | bytes 1179680 | tf_op jit(solution)/shard_map/ppermute | solution.py:1120
  377.7 3.0 collective-permute-start.15
  384.5 4.0 all-to-all-done.5.got_ref
  388.5 7.1 %column_grads.1 = (bf16[16,112,512]{2,1,0:T(8,128)(2,1)}, bf16[8,128,128]{2,1,0:T(8,128)(2,1)}, bf16[96,128]{1,0:T(8,128)(2,1)}) custom-call(bf16[4,2160,128]{2,1,0:T(8,128)(2,1)} %all-to-all-done.5.got_ref, bf16[8,128,1536]{2,1,0:T(8,128)(2,1)} %copy-done.3, bf16[8,128,1536]{2,1,0:T(8,128)(2,1)} %bitcast.93), custom_call_target="tpu_custom_call" | custom-call | bytes 29520000 | tf_op jit(solution)/shard_map/column_grads/pallas_call | solution.py:614
  395.6 4.5 all-to-all-start.6
  400.1 5.5 %collective-permute-done.15.refs_4_ = bf16[4608,128]{1,0:T(8,128)(2,1)} collective-permute-done((bf16[4608,128]{1,0:T(8,128)(2,1)S(1)}, bf16[4608,128]{1,0:T(8,128)(2,1)}, u32[]{:S(2)}, u32[]{:S(2)}) %collective-permute-start.15) | collective-permute-done | bytes 1179680 | tf_op jit(solution)/shard_map/ppermute | solution.py:1120
  405.6 3.6 collective-permute-done.16.refs_2_
  412.4 3.0 convert_add_fusion.1
  416.2 8.8 %all-to-all-done.6.got_ref = bf16[16,112,512]{2,1,0:T(8,128)(2,1)S(1)} async-done(((bf16[16,112,512]{2,1,0:T(8,128)(2,1)}), bf16[16,112,512]{2,1,0:T(8,128)(2,1)S(1)}, u32[]{:S(2)}, u32[]{:S(2)}) %all-to-all-start.6) | async-done | bytes 1835040 | tf_op jit(solution)/shard_map/all_to_all | solution.py:1018
  425.2 14.7 %collective-permute-done.18.refs_5_ = bf16[4608,128]{1,0:T(8,128)(2,1)} collective-permute-done((bf16[4608,128]{1,0:T(8,128)(2,1)}, bf16[4608,128]{1,0:T(8,128)(2,1)}, u32[]{:S(2)}, u32[]{:S(2)}) %collective-permute-start.18) | collective-permute-done | bytes 1179680 | tf_op jit(solution)/shard_map/ppermute | solution.py:1120
  441.5 3.7 all-to-all-start.7
  447.5 3.4 collective-permute-start.21
  451.0 4.6 copy-done
  457.2 4.1 collective-permute-done.14
  463.7 8.3 %unpack_experts.2 = (f32[2,1536,512]{2,1,0:T(8,128)}, f32[2,1536,512]{2,1,0:T(8,128)}, f32[2,512,1536]{2,1,0:T(8,128)}) custom-call(s32[1]{0:T(128)} %bitcast.ctx_ref.refs_0_, bf16[4608,128]{1,0:T(8,128)(2,1)S(1)} %add_convert_fusion.refs_1_, bf16[4608,128]{1,0:T(8,128)(2,1)} %collective-permute-done.16.refs_2_, ...), custom_call_target="tpu_custom_call" | custom-call | bytes 44280000 | tf_op jit(solution)/shard_map/unpack_experts/pallas_call | solution.py:959
  472.0 7.5 %all-to-all-done.7.got_ref = bf16[8,864,128]{2,1,0:T(8,128)(2,1)S(1)} async-done(((bf16[8,864,128]{2,1,0:T(8,128)(2,1)}), bf16[8,864,128]{2,1,0:T(8,128)(2,1)S(1)}, u32[]{:S(2)}, u32[]{:S(2)}) %all-to-all-start.7) | async-done | bytes 1769504 | tf_op jit(solution)/shard_map/all_to_all | solution.py:1018
  481.4 4.6 copy-done.1
  489.3 4.0 unpack_experts.3
  (207 shorter events, 95.7 us)
Async XLA Ops:
  7.2 10.1 %copy-start.51 = (bf16[96]{0:T(256)(128)(2,1)S(1)}, bf16[96]{0:T(256)(128)(2,1)}, u32[]{:S(2)}) copy-start(bf16[96]{0:T(256)(128)(2,1)} %param.19) | copy-start | bytes 580
  7.2 10.1 %copy-start.50 = (bf16[96]{0:T(256)(128)(2,1)S(1)}, bf16[96]{0:T(256)(128)(2,1)}, u32[]{:S(2)}) copy-start(bf16[96]{0:T(256)(128)(2,1)} %param.20) | copy-start | bytes 580
  7.2 85.0 %all-gather.4.cloned.1.call-start = ((), (), s32[]{:S(2)}) async-start(), calls=%async_computation.8 | async-start | bytes 13369344 | tf_op jit(solution)/shard_map/all_gather | solution.py:1056
  12.0 135.1 %all-gather.8.cloned.1.call-start = ((), (), s32[]{:S(2)}) async-start(), calls=%async_computation.10 | async-start | bytes 7241728 | tf_op jit(solution)/shard_map/all_gather | solution.py:1063
  13.3 15.8 %collective-permute-start = (bf16[1,128,1536]{2,1,0:T(8,128)(2,1)S(1)}, bf16[1,128,1536]{2,1,0:T(8,128)(2,1)S(1)}, u32[]{:S(2)}, u32[]{:S(2)}) collective-permute-start(bf16[1,128,1536]{2,1,0:T(8,128)(2,1)S(1)} %copy-done.6), channel_id=1, source_target_pairs={{0,64},{16,80},{32,96},{48,112},{64,0},{80,16},{96,32},{112,48},{1... | collective-permute-start | bytes 1179656 | tf_op jit(solution)/shard_map/ppermute | solution.py:1070
  18.0 11.7 %all-to-all-start = ((bf16[16,1,192]{2,1,0:T(2,128)(2,1)}), bf16[16,1,192]{2,1,0:T(2,128)(2,1)S(1)}, u32[]{:S(2)}, u32[]{:S(2)}) async-start(bf16[16,1,192]{2,1,0:T(2,128)(2,1)} %broadcast_in_dim.24), calls=%async_computation | async-start | bytes 32768 | tf_op jit(solution)/shard_map/all_to_all | solution.py:1018
  31.7 42.6 %all-to-all-start.1 = ((bf16[4,2,128,1536]{3,2,1,0:T(8,128)(2,1)}), bf16[4,2,128,1536]{3,2,1,0:T(8,128)(2,1)S(1)}, u32[]{:S(2)}, u32[]{:S(2)}) async-start(bf16[4,2,128,1536]{3,2,1,0:T(8,128)(2,1)} %broadcast_in_dim.25), calls=%async_computation.1 | async-start | bytes 6291456 | tf_op jit(solution)/shard_map/all_to_all | solution.py:1018
  74.3 16.1 %all-to-all-start.2 = ((bf16[16,96,128]{2,1,0:T(8,128)(2,1)}), bf16[16,96,128]{2,1,0:T(8,128)(2,1)}, u32[]{:S(2)}, u32[]{:S(2)}) async-start(bf16[16,96,128]{2,1,0:T(8,128)(2,1)} %copy.62), calls=%async_computation.2 | async-start | bytes 786432 | tf_op jit(solution)/shard_map/all_to_all | solution.py:1018
  79.5 112.9 %all-gather.6.cloned.1.call-start = ((), (), s32[]{:S(2)}) async-start(), calls=%async_computation.9 | async-start | bytes 6684672 | tf_op jit(solution)/shard_map/all_gather | solution.py:1093
  114.8 21.7 %collective-permute-start.1 = (bf16[1,128,1536]{2,1,0:T(8,128)(2,1)S(1)}, bf16[1,128,1536]{2,1,0:T(8,128)(2,1)S(1)}, u32[]{:S(2)}, u32[]{:S(2)}) collective-permute-start(bf16[1,128,1536]{2,1,0:T(8,128)(2,1)S(1)} %bitcast.82), channel_id=1, source_target_pairs={{0,64},{16,80},{32,96},{48,112},{64,0},{80,16},{96,32},{112,48},{1... | collective-permute-start | bytes 1179656 | tf_op jit(solution)/shard_map/ppermute | solution.py:1070
  138.5 41.8 %all-to-all-start.3 = ((bf16[4,2,128,1536]{3,2,1,0:T(8,128)(2,1)}), bf16[4,2,128,1536]{3,2,1,0:T(8,128)(2,1)S(1)}, u32[]{:S(2)}, u32[]{:S(2)}) async-start(bf16[4,2,128,1536]{3,2,1,0:T(8,128)(2,1)} %broadcast_in_dim.27), calls=%async_computation.3 | async-start | bytes 6291456 | tf_op jit(solution)/shard_map/all_to_all | solution.py:1018
  180.3 41.0 %copy-start.42 = (bf16[4,2,128,1536]{3,2,1,0:T(8,128)(2,1)}, bf16[4,2,128,1536]{3,2,1,0:T(8,128)(2,1)S(1)}, u32[]{:S(2)}) copy-start(bf16[4,2,128,1536]{3,2,1,0:T(8,128)(2,1)S(1)} %all-to-all-done.3) | copy-start | bytes 9437188
  223.6 5.7 %collective-permute-start.2 = (bf16[8,128,1536]{2,1,0:T(8,128)(2,1)S(1)}, bf16[8,128,1536]{2,1,0:T(8,128)(2,1)S(1)}, u32[]{:S(2)}, u32[]{:S(2)}) collective-permute-start(bf16[8,128,1536]{2,1,0:T(8,128)(2,1)S(1)} %slice_bitcast_fusion), channel_id=1, source_target_pairs={{0,1},{1,0},{2,3},{3,2},{4,5},{5,4},{6,7},{7,6},{8,9},{9,8},{10,11... | collective-permute-start | bytes 9437192 | tf_op jit(solution)/shard_map/ppermute | solution.py:1105
  231.9 51.5 %all-to-all-start.4 = ((bf16[8,128,1536]{2,1,0:T(8,128)(2,1)}), bf16[8,128,1536]{2,1,0:T(8,128)(2,1)}, u32[]{:S(2)}, u32[]{:S(2)}) async-start(bf16[8,128,1536]{2,1,0:T(8,128)(2,1)} %fusion), calls=%async_computation.4 | async-start | bytes 6291456 | tf_op jit(solution)/shard_map/all_to_all | solution.py:1018
  247.6 15.3 %slice-start.2 = ((s8[6291456]{0:T(1024)(128)(4,1)}), s8[4194304]{0:T(1024)(128)(4,1)S(1)}, s32[]{:S(2)}) async-start(s8[6291456]{0:T(1024)(128)(4,1)} %bitcast.95), calls=%async_computation.13 | async-start | bytes 8388608
  247.6 15.3 %slice-start.3 = ((s8[6291456]{0:T(1024)(128)(4,1)}), s8[2097152]{0:T(1024)(128)(4,1)S(1)}, s32[]{:S(2)}) async-start(s8[6291456]{0:T(1024)(128)(4,1)} %bitcast.95), calls=%async_computation.14 | async-start | bytes 4194304
  247.6 15.3 %copy-start.49 = (bf16[8,2,128,128]{3,2,1,0:T(8,128)(2,1)S(1)}, bf16[8,2,128,128]{3,2,1,0:T(8,128)(2,1)}, u32[]{:S(2)}) copy-start(bf16[8,2,128,128]{3,2,1,0:T(8,128)(2,1)} %get-tuple-element.138) | copy-start | bytes 1572868
  247.6 61.1 %collective-permute-start.3 = (bf16[9216,128]{1,0:T(8,128)(2,1)}, bf16[9216,128]{1,0:T(8,128)(2,1)}, u32[]{:S(2)}, u32[]{:S(2)}) collective-permute-start(bf16[9216,128]{1,0:T(8,128)(2,1)} %get-tuple-element.127), channel_id=1, source_target_pairs={{0,16},{16,0},{32,48},{48,32},{64,80},{80,64},{96,112},{112,96},{1... | collective-permute-start | bytes 7077896 | tf_op jit(solution)/shard_map/ppermute | solution.py:1120
  260.6 54.6 %collective-permute-start.4 = (bf16[9216,128]{1,0:T(8,128)(2,1)}, bf16[9216,128]{1,0:T(8,128)(2,1)}, u32[]{:S(2)}, u32[]{:S(2)}) collective-permute-start(bf16[9216,128]{1,0:T(8,128)(2,1)} %get-tuple-element.136), channel_id=1, source_target_pairs={{0,48},{16,32},{32,16},{48,0},{64,112},{80,96},{96,80},{112,64},{1... | collective-permute-start | bytes 7077896 | tf_op jit(solution)/shard_map/ppermute | solution.py:1120
  302.7 12.5 %copy-start.24 = (bf16[4608,128]{1,0:T(8,128)(2,1)S(1)}, bf16[4608,128]{1,0:T(8,128)(2,1)}, u32[]{:S(2)}) copy-start(bf16[4608,128]{1,0:T(8,128)(2,1)} %get-tuple-element.129.p0) | copy-start | bytes 3538948
  302.7 12.5 %copy-start.25 = (bf16[4608,128]{1,0:T(8,128)(2,1)S(1)}, bf16[4608,128]{1,0:T(8,128)(2,1)}, u32[]{:S(2)}) copy-start(bf16[4608,128]{1,0:T(8,128)(2,1)} %get-tuple-element.135.p6) | copy-start | bytes 3538948
  302.7 12.5 %copy-start.26 = (bf16[4608,128]{1,0:T(8,128)(2,1)S(1)}, bf16[4608,128]{1,0:T(8,128)(2,1)}, u32[]{:S(2)}) copy-start(bf16[4608,128]{1,0:T(8,128)(2,1)} %get-tuple-element.133.p1) | copy-start | bytes 3538948
  302.7 12.5 %copy-start.27 = (bf16[4608,128]{1,0:T(8,128)(2,1)S(1)}, bf16[4608,128]{1,0:T(8,128)(2,1)}, u32[]{:S(2)}) copy-start(bf16[4608,128]{1,0:T(8,128)(2,1)} %get-tuple-element.134.p3) | copy-start | bytes 3538948
  302.7 45.3 %collective-permute-start.9 = (bf16[4,1776,128]{2,1,0:T(8,128)(2,1)}, bf16[4,1776,128]{2,1,0:T(8,128)(2,1)S(1)}, u32[]{:S(2)}, u32[]{:S(2)}) collective-permute-start(bf16[4,1776,128]{2,1,0:T(8,128)(2,1)} %get-tuple-element.154), channel_id=1, source_target_pairs={{0,64},{16,80},{32,96},{48,112},{64,0},{80,16},{96,32},{112,48},{1... | collective-permute-start | bytes 5455880 | tf_op jit(solution)/shard_map/ppermute | solution.py:1148
  308.1 13.7 %collective-permute-start.5 = (bf16[4,128,1536]{2,1,0:T(8,128)(2,1)S(1)}, bf16[4,128,1536]{2,1,0:T(8,128)(2,1)S(1)}, u32[]{:S(2)}, u32[]{:S(2)}) collective-permute-start(bf16[4,128,1536]{2,1,0:T(8,128)(2,1)S(1)} %get-tuple-element.203), channel_id=1, source_target_pairs={{0,1},{1,0},{2,3},{3,2},{4,5},{5,4},{6,7},{7,6},{8,9},{9,8},{10,11... | collective-permute-start | bytes 4718600 | tf_op jit(solution)/shard_map/ppermute | solution.py:1170
  308.2 13.6 %collective-permute-start.6 = (bf16[4,128,1536]{2,1,0:T(8,128)(2,1)S(1)}, bf16[4,128,1536]{2,1,0:T(8,128)(2,1)S(1)}, u32[]{:S(2)}, u32[]{:S(2)}) collective-permute-start(bf16[4,128,1536]{2,1,0:T(8,128)(2,1)S(1)} %get-tuple-element.202), channel_id=1, source_target_pairs={{0,1},{1,0},{2,3},{3,2},{4,5},{5,4},{6,7},{7,6},{8,9},{9,8},{10,11... | collective-permute-start | bytes 4718600 | tf_op jit(solution)/shard_map/ppermute | solution.py:1171
  319.6 27.1 %collective-permute-start.10 = (bf16[4608,128]{1,0:T(8,128)(2,1)S(1)}, bf16[4608,128]{1,0:T(8,128)(2,1)S(1)}, u32[]{:S(2)}, u32[]{:S(2)}) collective-permute-start(bf16[4608,128]{1,0:T(8,128)(2,1)S(1)} %get-tuple-element.157), channel_id=1, source_target_pairs={{0,16},{16,0},{32,48},{48,32},{64,80},{80,64},{96,112},{112,96},{1... | collective-permute-start | bytes 3538952 | tf_op jit(solution)/shard_map/ppermute | solution.py:1120
  319.7 28.3 %collective-permute-start.11 = (bf16[4608,128]{1,0:T(8,128)(2,1)S(1)}, bf16[4608,128]{1,0:T(8,128)(2,1)S(1)}, u32[]{:S(2)}, u32[]{:S(2)}) collective-permute-start(bf16[4608,128]{1,0:T(8,128)(2,1)S(1)} %get-tuple-element.149), channel_id=1, source_target_pairs={{0,48},{16,32},{32,16},{48,0},{64,112},{80,96},{96,80},{112,64},{1... | collective-permute-start | bytes 3538952 | tf_op jit(solution)/shard_map/ppermute | solution.py:1120
  324.7 26.7 %collective-permute-start.7 = (bf16[2,128,1536]{2,1,0:T(8,128)(2,1)S(1)}, bf16[2,128,1536]{2,1,0:T(8,128)(2,1)S(1)}, u32[]{:S(2)}, u32[]{:S(2)}) collective-permute-start(bf16[2,128,1536]{2,1,0:T(8,128)(2,1)S(1)} %get-tuple-element.152), channel_id=1, source_target_pairs={{0,4},{1,5},{2,6},{3,7},{4,0},{5,1},{6,2},{7,3},{8,12},{9,13},{10,... | collective-permute-start | bytes 2359304 | tf_op jit(solution)/shard_map/ppermute | solution.py:1165
  326.5 25.0 %collective-permute-start.8 = (bf16[2,128,1536]{2,1,0:T(8,128)(2,1)S(1)}, bf16[2,128,1536]{2,1,0:T(8,128)(2,1)S(1)}, u32[]{:S(2)}, u32[]{:S(2)}) collective-permute-start(bf16[2,128,1536]{2,1,0:T(8,128)(2,1)S(1)} %get-tuple-element.153), channel_id=1, source_target_pairs={{0,12},{1,13},{2,14},{3,15},{4,8},{5,9},{6,10},{7,11},{8,4},{9,5},... | collective-permute-start | bytes 2359304 | tf_op jit(solution)/shard_map/ppermute | solution.py:1165
  348.5 27.7 %collective-permute-start.12 = (bf16[4608,128]{1,0:T(8,128)(2,1)S(1)}, bf16[4608,128]{1,0:T(8,128)(2,1)}, u32[]{:S(2)}, u32[]{:S(2)}) collective-permute-start(bf16[4608,128]{1,0:T(8,128)(2,1)S(1)} %get-tuple-element.160), channel_id=1, source_target_pairs={{0,64},{16,80},{32,96},{48,112},{64,0},{80,16},{96,32},{112,48},{1... | collective-permute-start | bytes 3538952 | tf_op jit(solution)/shard_map/ppermute | solution.py:1120
  354.9 33.6 %all-to-all-start.5 = ((bf16[4,2160,128]{2,1,0:T(8,128)(2,1)}), bf16[4,2160,128]{2,1,0:T(8,128)(2,1)}, u32[]{:S(2)}, u32[]{:S(2)}) async-start(bf16[4,2160,128]{2,1,0:T(8,128)(2,1)} %merge_shares.1), calls=%async_computation.5 | async-start | bytes 4423680 | tf_op jit(solution)/shard_map/all_to_all | solution.py:1018
  377.7 27.9 %collective-permute-start.15 = (bf16[4608,128]{1,0:T(8,128)(2,1)S(1)}, bf16[4608,128]{1,0:T(8,128)(2,1)}, u32[]{:S(2)}, u32[]{:S(2)}) collective-permute-start(bf16[4608,128]{1,0:T(8,128)(2,1)S(1)} %add_convert_fusion.refs_1_), channel_id=1, source_target_pairs={{0,64},{16,80},{32,96},{48,112},{64,0},{80,16},{96,32},{112,48},{1... | collective-permute-start | bytes 3538952 | tf_op jit(solution)/shard_map/ppermute | solution.py:1120
  380.7 28.4 %collective-permute-start.16 = (bf16[4608,128]{1,0:T(8,128)(2,1)S(1)}, bf16[4608,128]{1,0:T(8,128)(2,1)}, u32[]{:S(2)}, u32[]{:S(2)}) collective-permute-start(bf16[4608,128]{1,0:T(8,128)(2,1)S(1)} %add_convert_fusion.refs_1_), channel_id=1, source_target_pairs={{0,16},{16,0},{32,48},{48,32},{64,80},{80,64},{96,112},{112,96},{1... | collective-permute-start | bytes 3538952 | tf_op jit(solution)/shard_map/ppermute | solution.py:1120
  380.9 29.8 %collective-permute-start.17 = (bf16[4608,128]{1,0:T(8,128)(2,1)S(1)}, bf16[4608,128]{1,0:T(8,128)(2,1)}, u32[]{:S(2)}, u32[]{:S(2)}) collective-permute-start(bf16[4608,128]{1,0:T(8,128)(2,1)S(1)} %add_convert_fusion.refs_1_), channel_id=1, source_target_pairs={{0,48},{16,32},{32,16},{48,0},{64,112},{80,96},{96,80},{112,64},{1... | collective-permute-start | bytes 3538952 | tf_op jit(solution)/shard_map/ppermute | solution.py:1120
  381.9 18.2 %collective-permute-start.13 = (bf16[2,128,1536]{2,1,0:T(8,128)(2,1)}, bf16[2,128,1536]{2,1,0:T(8,128)(2,1)}, u32[]{:S(2)}, u32[]{:S(2)}) collective-permute-start(bf16[2,128,1536]{2,1,0:T(8,128)(2,1)} %get-tuple-element.168), channel_id=1, source_target_pairs={{0,8},{1,9},{2,10},{3,11},{4,12},{5,13},{6,14},{7,15},{8,0},{9,1},... | collective-permute-start | bytes 2359304 | tf_op jit(solution)/shard_map/ppermute | solution.py:1165
  395.6 29.4 %all-to-all-start.6 = ((bf16[16,112,512]{2,1,0:T(8,128)(2,1)}), bf16[16,112,512]{2,1,0:T(8,128)(2,1)S(1)}, u32[]{:S(2)}, u32[]{:S(2)}) async-start(bf16[16,112,512]{2,1,0:T(8,128)(2,1)} %get-tuple-element.165), calls=%async_computation.6 | async-start | bytes 3670016 | tf_op jit(solution)/shard_map/all_to_all | solution.py:1018
  400.1 24.9 %copy-start.40 = (bf16[96,128]{1,0:T(8,128)(2,1)S(1)}, bf16[96,128]{1,0:T(8,128)(2,1)}, u32[]{:S(2)}) copy-start(bf16[96,128]{1,0:T(8,128)(2,1)} %get-tuple-element.172.down_ref) | copy-start | bytes 73732
  410.7 29.2 %collective-permute-start.18 = (bf16[4608,128]{1,0:T(8,128)(2,1)}, bf16[4608,128]{1,0:T(8,128)(2,1)}, u32[]{:S(2)}, u32[]{:S(2)}) collective-permute-start(bf16[4608,128]{1,0:T(8,128)(2,1)} %collective-permute-done.15.refs_4_), channel_id=1, source_target_pairs={{0,16},{16,0},{32,48},{48,32},{64,80},{80,64},{96,112},{112,96},{1... | collective-permute-start | bytes 3538952 | tf_op jit(solution)/shard_map/ppermute | solution.py:1120
  411.2 28.7 %collective-permute-start.19 = (bf16[4608,128]{1,0:T(8,128)(2,1)}, bf16[4608,128]{1,0:T(8,128)(2,1)}, u32[]{:S(2)}, u32[]{:S(2)}) collective-permute-start(bf16[4608,128]{1,0:T(8,128)(2,1)} %collective-permute-done.15.refs_4_), channel_id=1, source_target_pairs={{0,48},{16,32},{32,16},{48,0},{64,112},{80,96},{96,80},{112,64},{1... | collective-permute-start | bytes 3538952 | tf_op jit(solution)/shard_map/ppermute | solution.py:1120
  415.4 24.7 %copy-start.46 = (bf16[8,128,128]{2,1,0:T(8,128)(2,1)S(1)}, bf16[8,128,128]{2,1,0:T(8,128)(2,1)}, u32[]{:S(2)}) copy-start(bf16[8,128,128]{2,1,0:T(8,128)(2,1)} %get-tuple-element.171) | copy-start | bytes 786436
  415.4 72.8 %collective-permute-start.20 = (bf16[4608,128]{1,0:T(8,128)(2,1)}, bf16[4608,128]{1,0:T(8,128)(2,1)}, u32[]{:S(2)}, u32[]{:S(2)}) collective-permute-start(bf16[4608,128]{1,0:T(8,128)(2,1)} %collective-permute-done.17.refs_3_), channel_id=1, source_target_pairs={{0,16},{16,0},{32,48},{48,32},{64,80},{80,64},{96,112},{112,96},{1... | collective-permute-start | bytes 3538952 | tf_op jit(solution)/shard_map/ppermute | solution.py:1120
  441.5 38.0 %all-to-all-start.7 = ((bf16[8,864,128]{2,1,0:T(8,128)(2,1)}), bf16[8,864,128]{2,1,0:T(8,128)(2,1)S(1)}, u32[]{:S(2)}, u32[]{:S(2)}) async-start(bf16[8,864,128]{2,1,0:T(8,128)(2,1)} %pad_maximum_fusion), calls=%async_computation.7 | async-start | bytes 3538944 | tf_op jit(solution)/shard_map/all_to_all | solution.py:1018
  447.1 14.2 %collective-permute-start.14 = (bf16[128,1536]{1,0:T(8,128)(2,1)}, bf16[128,1536]{1,0:T(8,128)(2,1)}, u32[]{:S(2)}, u32[]{:S(2)}) collective-permute-start(bf16[128,1536]{1,0:T(8,128)(2,1)} %fusion.5), channel_id=1, source_target_pairs={{0,2},{1,3},{2,0},{3,1},{4,6},{5,7},{6,4},{7,5},{8,10},{9,11},{10,... | collective-permute-start | bytes 1179656 | tf_op jit(solution)/shard_map/ppermute | solution.py:1190
  447.5 41.8 %collective-permute-start.21 = (bf16[4608,128]{1,0:T(8,128)(2,1)}, bf16[4608,128]{1,0:T(8,128)(2,1)}, u32[]{:S(2)}, u32[]{:S(2)}) collective-permute-start(bf16[4608,128]{1,0:T(8,128)(2,1)} %collective-permute-done.18.refs_5_), channel_id=1, source_target_pairs={{0,48},{16,32},{32,16},{48,0},{64,112},{80,96},{96,80},{112,64},{1... | collective-permute-start | bytes 3538952 | tf_op jit(solution)/shard_map/ppermute | solution.py:1120
  463.7 15.8 %copy-start.28 = (bf16[96,1536]{1,0:T(8,128)(2,1)S(1)}, bf16[96,1536]{1,0:T(8,128)(2,1)}, u32[]{:S(2)}) copy-start(bf16[96,1536]{1,0:T(8,128)(2,1)} %wq_ref.1) | copy-start | bytes 884740
  463.7 15.8 %copy-start.36 = (bf16[96,512]{1,0:T(8,128)(2,1)S(1)}, bf16[96,512]{1,0:T(8,128)(2,1)}, u32[]{:S(2)}) copy-start(bf16[96,512]{1,0:T(8,128)(2,1)} %wk_ref.1) | copy-start | bytes 294916
  463.7 15.8 %copy-start.37 = (bf16[96,512]{1,0:T(8,128)(2,1)S(1)}, bf16[96,512]{1,0:T(8,128)(2,1)}, u32[]{:S(2)}) copy-start(bf16[96,512]{1,0:T(8,128)(2,1)} %wv_ref.1) | copy-start | bytes 294916
  (42 other events, 171.4 us)
Sparse Core Ops, SparseCore 0:
  12.2 79.9 all-gather.3
  94.5 52.5 all-gather.7
  149.4 42.9 all-gather.5

commit v17 on v16

--- a/solution.py
+++ b/solution.py
@@ -751,7 +751,7 @@
         out_specs=whole((BLOCK, WIDTH)),
         out_shape=jax.ShapeDtypeStruct((BLOCK, WIDTH), f32),
         cost_estimate=cost(4),
-        compiler_params=params(32),
+        compiler_params=params(60),
         name="query_back",
     )(grad_query, w_all)
 
@@ -771,7 +771,7 @@
         out_specs=whole((BLOCK, WIDTH)),
         out_shape=jax.ShapeDtypeStruct((BLOCK, WIDTH), bf16),
         cost_estimate=cost(4),
-        compiler_params=params(32),
+        compiler_params=params(60),
         name="input_back",
     )(query_part, grad_kv, w_all, tokens, gain, grad_middle)
 

time: 510 us -> 511 us (level)
  local copies, waits for them, and re-layouts: 49.7 us -> 41.5 us
  Pallas kernels: 145 us -> 153 us
    unnamed x124 -> x112, local copies, waits for them, and re-layouts: 29.9 us -> 21.7 us
  transfers between devices with their start and end apart: 33 -> 33, of which waited for: 23 -> 23; matrix products, arithmetic and copies ran while one was open for 8% -> 8% of each run, Pallas kernels for 22% -> 24%
where the time goes in v17:
time: 511 us; the launch traced here: 501 us
  waiting for transfers between devices  193 us (38%)
  Pallas kernels  153 us (30%)
  starting transfers between devices  76.4 us (15%)
  local copies, waits for them, and re-layouts  41.5 us (8%)
  other arithmetic  15.9 us (3%)
  between operations  14.8 us (3%)
  matrix products  6.73 us (1%)
    all_to_all x8, waiting for transfers between devices, swap_all(): lax.all_to_all(rows, axis, split_axis=0, concat_axis=0, tiled=True, axis_...  74.1 us
    ppermute x12, waiting for transfers between devices, to(): return lax.ppermute(rows, 'ctx', [(i, i ^ k) for i in range(N_CTX)])  70.6 us
    all_to_all x8, starting transfers between devices, swap_all(): lax.all_to_all(rows, axis, split_axis=0, concat_axis=0, tiled=True, axis_...  41.4 us
    pallas_call x1, Pallas kernels, expert_back(): pl.pallas_call(expert_kernel, grid_spec=pltpu.PrefetchScalarGridSpec(num_...  28.9 us
    ppermute x2, waiting for transfers between devices, of_sequence(): other = lax.ppermute(rows, 'ctx', z_swap)  26.2 us
    pallas_call x2, Pallas kernels, expert_weights(): pl.pallas_call(lambda *refs: expert_weights_kernel(halved, *refs), grid_s...  22.3 us
    unnamed x112, local copies, waits for them, and re-layouts  21.7 us
    ppermute x12, starting transfers between devices, to(): return lax.ppermute(rows, 'ctx', [(i, i ^ k) for i in range(N_CTX)])  18.8 us
  transfers between devices with their start and end apart: 33, of which 23 were waited for; matrix products, arithmetic and copies ran while one was open for 8% of the time, Pallas kernels for 24%

profile of v17, /device:TPU:0, one launch (start us, length us, event | category | flops | bytes accessed | tf_op | source)
XLA Modules:
  0.0 501.1 jit_solution(3982938448340784622)
XLA Ops:
  13.3 4.1 collective-permute-start
  18.0 4.8 all-to-all-start
  22.9 6.1 %collective-permute-done = bf16[1,128,1536]{2,1,0:T(8,128)(2,1)S(1)} collective-permute-done((bf16[1,128,1536]{2,1,0:T(8,128)(2,1)S(1)}, bf16[1,128,1536]{2,1,0:T(8,128)(2,1)S(1)}, u32[]{:S(2)}, u32[]{:S(2)}) %collective-permute-start) | collective-permute-done | bytes 393248 | tf_op jit(solution)/shard_map/ppermute | solution.py:1070
  31.7 4.6 all-to-all-start.1
  43.9 30.5 %all-to-all-done.1 = bf16[4,2,128,1536]{3,2,1,0:T(8,128)(2,1)S(1)} async-done(((bf16[4,2,128,1536]{3,2,1,0:T(8,128)(2,1)}), bf16[4,2,128,1536]{3,2,1,0:T(8,128)(2,1)S(1)}, u32[]{:S(2)}, u32[]{:S(2)}) %all-to-all-start.1) | async-done | bytes 3145760 | tf_op jit(solution)/shard_map/all_to_all | solution.py:1018
  74.3 5.2 %all-to-all-start.2 = ((bf16[16,96,128]{2,1,0:T(8,128)(2,1)}), bf16[16,96,128]{2,1,0:T(8,128)(2,1)}, u32[]{:S(2)}, u32[]{:S(2)}) async-start(bf16[16,96,128]{2,1,0:T(8,128)(2,1)} %copy.62), calls=%async_computation.2 | async-start | bytes 786432 | tf_op jit(solution)/shard_map/all_to_all | solution.py:1018
  86.0 4.5 all-to-all-done.2
  94.1 7.6 %project.1 = (bf16[128,1536]{1,0:T(8,128)(2,1)S(1)}, bf16[8,128,1024]{2,1,0:T(8,128)(2,1)S(1)}) custom-call(bf16[1,128,1536]{2,1,0:T(8,128)(2,1)S(1)} %copy-done.14, bf16[8,128,1536]{2,1,0:T(8,128)(2,1)S(1)} %copy-done.2, bf16[1536,4096]{1,0:T(8,128)(2,1)} %all-gather.4.cloned.1.call-done.w_ref.wq_ref.wkv_ref), custom_call_target="tpu_custom_call" | custom-call | bytes 29520000 | tf_op jit(solution)/shard_map/project/pallas_call | solution.py:815
  101.8 5.8 %attend.1 = (bf16[128,1536]{1,0:T(8,128)(2,1)S(1)}, f32[128,1536]{1,0:T(8,128)S(1)}, f32[1536,128]{1,0:T(8,128)S(1)}) custom-call(s32[1]{0:T(128)} %bitcast.ctx_ref.refs_0_, bf16[128,1536]{1,0:T(8,128)(2,1)S(1)} %get-tuple-element.110.q_ref, bf16[8,128,1024]{2,1,0:T(8,128)(2,1)S(1)} %get-tuple-element.111.k_ref.v_ref, ...), custom_call_target="tpu_custom_call" | custom-call | bytes 22140000 | tf_op jit(solution)/shard_map/attend/pallas_call | solution.py:99
  110.2 4.5 middle_norm.1
  116.3 20.1 %collective-permute-done.1 = bf16[1,128,1536]{2,1,0:T(8,128)(2,1)S(1)} collective-permute-done((bf16[1,128,1536]{2,1,0:T(8,128)(2,1)S(1)}, bf16[1,128,1536]{2,1,0:T(8,128)(2,1)S(1)}, u32[]{:S(2)}, u32[]{:S(2)}) %collective-permute-start.1) | collective-permute-done | bytes 393248 | tf_op jit(solution)/shard_map/ppermute | solution.py:1070
  138.5 4.6 all-to-all-start.3
  147.1 13.7 %place_rows.1 = (bf16[8,2,128,128]{3,2,1,0:T(8,128)(2,1)}, bf16[2,2,384,1536]{3,2,1,0:T(8,128)(2,1)}, f32[2,2,384,512]{3,2,1,0:T(8,128)}, f32[8,2,128,128]{3,2,1,0:T(8,128)}, f32[2,2,384,128]{3,2,1,0:T(8,128)}) custom-call(s32[1]{0:T(128)} %bitcast.7.at_ref, bf16[8,2,128,1664]{3,2,1,0:T(8,128)(2,1)} %bitcast.84, bf16[2,512,1536]{2,1,0:T(8,128)(2,1)} %wd_ref.1, ...), custom_call_target="tpu_custom_call" | custom-call | bytes 51660000 | tf_op jit(solution)/shard_map/place_rows/pallas_call | solution.py:368
  160.8 19.5 %all-to-all-done.3 = bf16[4,2,128,1536]{3,2,1,0:T(8,128)(2,1)S(1)} async-done(((bf16[4,2,128,1536]{3,2,1,0:T(8,128)(2,1)}), bf16[4,2,128,1536]{3,2,1,0:T(8,128)(2,1)S(1)}, u32[]{:S(2)}, u32[]{:S(2)}) %all-to-all-start.3) | async-done | bytes 3145760 | tf_op jit(solution)/shard_map/all_to_all | solution.py:1018
  180.3 12.1 %all-gather.6.cloned.1.call-done = bf16[2048,1536]{1,0:T(8,128)(2,1)} async-done(((bf16[128,1536]{1,0:T(8,128)(2,1)}), bf16[2048,1536]{1,0:T(8,128)(2,1)}) %all-gather.6.cloned.1.call-update) | async-done | bytes 6291472 | tf_op jit(solution)/shard_map/all_gather | solution.py:1093
  192.4 28.9 %expert_back.1 = (bf16[2,8,128,1536]{3,2,1,0:T(8,128)(2,1)}, bf16[2,2,384,1536]{3,2,1,0:T(8,128)(2,1)}, bf16[2,2,384,512]{3,2,1,0:T(8,128)(2,1)}, bf16[2,2,384,1...) custom-call(s32[1]{0:T(128)} %bitcast.7.at_ref, ...), custom_call_target="tpu_custom_call" | custom-call | bytes 103320000 | tf_op jit(solution)/shard_map/expert_back/pallas_call | solution.py:447
  223.9 5.4 %collective-permute-done.2 = bf16[8,128,1536]{2,1,0:T(8,128)(2,1)S(1)} collective-permute-done((bf16[8,128,1536]{2,1,0:T(8,128)(2,1)S(1)}, bf16[8,128,1536]{2,1,0:T(8,128)(2,1)S(1)}, u32[]{:S(2)}, u32[]{:S(2)}) %collective-permute-start.2) | collective-permute-done | bytes 3145760 | tf_op jit(solution)/shard_map/ppermute | solution.py:1105
  229.3 2.6 fusion
  231.9 4.8 all-to-all-start.4
  236.7 10.9 %expert_weights.2 = (bf16[9216,128]{1,0:T(8,128)(2,1)}, bf16[9216,128]{1,0:T(8,128)(2,1)}) custom-call(s32[1]{0:T(128)} %bitcast.ctx_ref.refs_0_, bf16[2,768,1536]{2,1,0:T(8,128)(2,1)} %bitcast.91, bf16[2,768,1536]{2,1,0:T(8,128)(2,1)} %bitcast.89, bf16[2,768,512]{2,1,0:T(8,128)(2,1)} %bitcast.74, bf16[2,768,1024]{2,1,0:T(8,128)(2,1)} %bitcast.85, ...), custom_call_target="tpu_custom_call" | custom-call | bytes 7380000 | tf_op jit(solution)/shard_map/expert_weights/pallas_call | solution.py:915
  249.2 11.4 %expert_weights.3 = (bf16[4608,128]{1,0:T(8,128)(2,1)}, bf16[4608,128]{1,0:T(8,128)(2,1)}, bf16[4608,128]{1,0:T(8,128)(2,1)}, bf16[4608,128]{1,0:T(8,128)(2,1)}) custom-call(s32[1]{0:T(128)} %bitcast.ctx_ref.refs_0_, bf16[2,768,1536]{2,1,0:T(8,128)(2,1)} %bitcast.92, bf16[2,768,1536]{2,1,0:T(8,128)(2,1)} %bitcast.90, bf16[2,768,512]{2,1,0:T(8,128)(2,1)} %bitcast.75, ...), custom_call_target="tpu_custom_call" | custom-call | bytes 7380000 | tf_op jit(solution)/shard_map/expert_weights/pallas_call | solution.py:915
  268.5 9.8 %expert_output.1.own_ref = bf16[2,8,128,1536]{3,2,1,0:T(8,128)(2,1)} custom-call(s32[1]{0:T(128)} %bitcast.7.at_ref, bf16[2,2,384,512]{3,2,1,0:T(8,128)(2,1)S(1)} %copy-done.4, f32[2,2,384,128]{3,2,1,0:T(8,128)S(1)} %copy-done.27, bf16[8,2,128,128]{3,2,1,0:T(8,128)(2,1)S(1)} %copy-done.10, bf16[8,2,128,128]{3,2,1,0:T(8,128)(2,1)S(1)} %copy-done.6, ...), custom_call_target="tpu_custom_call" | custom-call | bytes 7380000 | tf_op jit(solution)/shard_map/expert_output/pallas_call | solution.py:499
  278.3 4.1 fusion.8
  283.9 5.6 %middle_back.1 = (f32[128,1536]{1,0:T(8,128)S(1)}, bf16[128,1536]{1,0:T(8,128)(2,1)S(1)}, bf16[128,1536]{1,0:T(8,128)(2,1)S(1)}, f32[16,128]{1,0:T(8,128)S(1)}) custom-call(bf16[8,128,1536]{2,1,0:T(8,128)(2,1)} %all-to-all-done.4.pieces_ref, f32[128,1536]{1,0:T(8,128)S(1)} %copy-done.7, bf16[128,1536]{1,0:T(8,128)(2,1)S(1)} %bitcast.81, ...), custom_call_target="tpu_custom_call" | custom-call | bytes 3690000 | tf_op jit(solution)/shard_map/middle_back/pallas_call | solution.py:290
  292.4 10.3 %attend_back.1 = (bf16[128,1536]{1,0:T(8,128)(2,1)}, bf16[4,1776,128]{2,1,0:T(8,128)(2,1)}, bf16[4,1776,128]{2,1,0:T(8,128)(2,1)}) custom-call(s32[1]{0:T(128)} %bitcast.ctx_ref.refs_0_, bf16[128,1536]{1,0:T(8,128)(2,1)} %copy-done.12, bf16[128,1536]{1,0:T(8,128)(2,1)} %copy-done.29, f32[128,1536]{1,0:T(8,128)} %copy-done.25, f32[1536,128]{1,0:T(8,128)} %copy-done.26, ...), custom_call_target="tpu_custom_call" | custom-call | bytes 7380000 | tf_op jit(solution)/shard_map/attend_back/pallas_call | solution.py:202
  302.8 3.2 collective-permute-start.9
  308.7 6.5 %collective-permute-done.4.relay_b.got_31 = bf16[9216,128]{1,0:T(8,128)(2,1)} collective-permute-done((bf16[9216,128]{1,0:T(8,128)(2,1)}, bf16[9216,128]{1,0:T(8,128)(2,1)}, u32[]{:S(2)}, u32[]{:S(2)}) %collective-permute-start.4) | collective-permute-done | bytes 2359328 | tf_op jit(solution)/shard_map/ppermute | solution.py:1120
  315.3 4.4 piece_sums.2
  321.8 2.9 spread_sums.1
  328.6 18.2 %collective-permute-done.10.got_11 = bf16[4608,128]{1,0:T(8,128)(2,1)S(1)} collective-permute-done((bf16[4608,128]{1,0:T(8,128)(2,1)S(1)}, bf16[4608,128]{1,0:T(8,128)(2,1)S(1)}, u32[]{:S(2)}, u32[]{:S(2)}) %collective-permute-start.10) | collective-permute-done | bytes 1179680 | tf_op jit(solution)/shard_map/ppermute | solution.py:1120
  349.8 2.9 collective-permute-start.12
  356.1 4.5 all-to-all-start.5
  360.6 17.0 %collective-permute-done.12 = bf16[4608,128]{1,0:T(8,128)(2,1)S(1)} collective-permute-done((bf16[4608,128]{1,0:T(8,128)(2,1)}, bf16[4608,128]{1,0:T(8,128)(2,1)S(1)}, u32[]{:S(2)}, u32[]{:S(2)}) %collective-permute-start.12) | collective-permute-done | bytes 1179680 | tf_op jit(solution)/shard_map/ppermute | solution.py:1120
  380.1 3.0 collective-permute-start.15
  386.8 2.9 all-to-all-done.5.got_ref
  389.7 7.1 %column_grads.1 = (bf16[16,112,512]{2,1,0:T(8,128)(2,1)}, bf16[8,128,128]{2,1,0:T(8,128)(2,1)}, bf16[96,128]{1,0:T(8,128)(2,1)}) custom-call(bf16[4,2160,128]{2,1,0:T(8,128)(2,1)} %all-to-all-done.5.got_ref, bf16[8,128,1536]{2,1,0:T(8,128)(2,1)} %copy-done.1, bf16[8,128,1536]{2,1,0:T(8,128)(2,1)} %bitcast.93), custom_call_target="tpu_custom_call" | custom-call | bytes 29520000 | tf_op jit(solution)/shard_map/column_grads/pallas_call | solution.py:614
  396.8 4.5 all-to-all-start.6
  401.6 9.4 %collective-permute-done.15.refs_4_ = bf16[4608,128]{1,0:T(8,128)(2,1)} collective-permute-done((bf16[4608,128]{1,0:T(8,128)(2,1)S(1)}, bf16[4608,128]{1,0:T(8,128)(2,1)}, u32[]{:S(2)}, u32[]{:S(2)}) %collective-permute-start.15) | collective-permute-done | bytes 1179680 | tf_op jit(solution)/shard_map/ppermute | solution.py:1120
  413.6 3.0 convert_add_fusion.1
  417.4 8.8 %all-to-all-done.6.got_ref = bf16[16,112,512]{2,1,0:T(8,128)(2,1)S(1)} async-done(((bf16[16,112,512]{2,1,0:T(8,128)(2,1)}), bf16[16,112,512]{2,1,0:T(8,128)(2,1)S(1)}, u32[]{:S(2)}, u32[]{:S(2)}) %all-to-all-start.6) | async-done | bytes 1835040 | tf_op jit(solution)/shard_map/all_to_all | solution.py:1018
  426.5 14.9 %collective-permute-done.18.refs_5_ = bf16[4608,128]{1,0:T(8,128)(2,1)} collective-permute-done((bf16[4608,128]{1,0:T(8,128)(2,1)}, bf16[4608,128]{1,0:T(8,128)(2,1)}, u32[]{:S(2)}, u32[]{:S(2)}) %collective-permute-start.18) | collective-permute-done | bytes 1179680 | tf_op jit(solution)/shard_map/ppermute | solution.py:1120
  442.9 8.2 %all-to-all-start.7 = ((bf16[8,864,128]{2,1,0:T(8,128)(2,1)}), bf16[8,864,128]{2,1,0:T(8,128)(2,1)S(1)}, u32[]{:S(2)}, u32[]{:S(2)}) async-start(bf16[8,864,128]{2,1,0:T(8,128)(2,1)} %pad_maximum_fusion), calls=%async_computation.7 | async-start | bytes 3538944 | tf_op jit(solution)/shard_map/all_to_all | solution.py:1018
  453.1 3.5 collective-permute-start.21
  456.7 5.0 query_back.1.part_ref
  465.0 8.3 %unpack_experts.2 = (f32[2,1536,512]{2,1,0:T(8,128)}, f32[2,1536,512]{2,1,0:T(8,128)}, f32[2,512,1536]{2,1,0:T(8,128)}) custom-call(s32[1]{0:T(128)} %bitcast.ctx_ref.refs_0_, bf16[4608,128]{1,0:T(8,128)(2,1)S(1)} %add_convert_fusion.refs_1_, bf16[4608,128]{1,0:T(8,128)(2,1)} %collective-permute-done.16.refs_2_, ...), custom_call_target="tpu_custom_call" | custom-call | bytes 44280000 | tf_op jit(solution)/shard_map/unpack_experts/pallas_call | solution.py:959
  473.3 7.4 %all-to-all-done.7.got_ref = bf16[8,864,128]{2,1,0:T(8,128)(2,1)S(1)} async-done(((bf16[8,864,128]{2,1,0:T(8,128)(2,1)}), bf16[8,864,128]{2,1,0:T(8,128)(2,1)S(1)}, u32[]{:S(2)}, u32[]{:S(2)}) %all-to-all-start.7) | async-done | bytes 1769504 | tf_op jit(solution)/shard_map/all_to_all | solution.py:1018
  482.8 4.7 input_back.1
  490.2 4.0 unpack_experts.3
  (195 shorter events, 90.6 us)
Async XLA Ops:
  7.2 10.1 %copy-start.45 = (bf16[96]{0:T(256)(128)(2,1)S(1)}, bf16[96]{0:T(256)(128)(2,1)}, u32[]{:S(2)}) copy-start(bf16[96]{0:T(256)(128)(2,1)} %param.19) | copy-start | bytes 580
  7.2 85.0 %all-gather.4.cloned.1.call-start = ((), (), s32[]{:S(2)}) async-start(), calls=%async_computation.8 | async-start | bytes 13369344 | tf_op jit(solution)/shard_map/all_gather | solution.py:1056
  12.0 135.1 %all-gather.8.cloned.1.call-start = ((), (), s32[]{:S(2)}) async-start(), calls=%async_computation.10 | async-start | bytes 7241728 | tf_op jit(solution)/shard_map/all_gather | solution.py:1063
  13.3 15.8 %collective-permute-start = (bf16[1,128,1536]{2,1,0:T(8,128)(2,1)S(1)}, bf16[1,128,1536]{2,1,0:T(8,128)(2,1)S(1)}, u32[]{:S(2)}, u32[]{:S(2)}) collective-permute-start(bf16[1,128,1536]{2,1,0:T(8,128)(2,1)S(1)} %copy-done.5), channel_id=1, source_target_pairs={{0,64},{16,80},{32,96},{48,112},{64,0},{80,16},{96,32},{112,48},{1... | collective-permute-start | bytes 1179656 | tf_op jit(solution)/shard_map/ppermute | solution.py:1070
  18.0 11.7 %all-to-all-start = ((bf16[16,1,192]{2,1,0:T(2,128)(2,1)}), bf16[16,1,192]{2,1,0:T(2,128)(2,1)S(1)}, u32[]{:S(2)}, u32[]{:S(2)}) async-start(bf16[16,1,192]{2,1,0:T(2,128)(2,1)} %broadcast_in_dim.24), calls=%async_computation | async-start | bytes 32768 | tf_op jit(solution)/shard_map/all_to_all | solution.py:1018
  31.7 42.6 %all-to-all-start.1 = ((bf16[4,2,128,1536]{3,2,1,0:T(8,128)(2,1)}), bf16[4,2,128,1536]{3,2,1,0:T(8,128)(2,1)S(1)}, u32[]{:S(2)}, u32[]{:S(2)}) async-start(bf16[4,2,128,1536]{3,2,1,0:T(8,128)(2,1)} %broadcast_in_dim.25), calls=%async_computation.1 | async-start | bytes 6291456 | tf_op jit(solution)/shard_map/all_to_all | solution.py:1018
  74.3 16.1 %all-to-all-start.2 = ((bf16[16,96,128]{2,1,0:T(8,128)(2,1)}), bf16[16,96,128]{2,1,0:T(8,128)(2,1)}, u32[]{:S(2)}, u32[]{:S(2)}) async-start(bf16[16,96,128]{2,1,0:T(8,128)(2,1)} %copy.62), calls=%async_computation.2 | async-start | bytes 786432 | tf_op jit(solution)/shard_map/all_to_all | solution.py:1018
  79.5 112.9 %all-gather.6.cloned.1.call-start = ((), (), s32[]{:S(2)}) async-start(), calls=%async_computation.9 | async-start | bytes 6684672 | tf_op jit(solution)/shard_map/all_gather | solution.py:1093
  114.7 21.7 %collective-permute-start.1 = (bf16[1,128,1536]{2,1,0:T(8,128)(2,1)S(1)}, bf16[1,128,1536]{2,1,0:T(8,128)(2,1)S(1)}, u32[]{:S(2)}, u32[]{:S(2)}) collective-permute-start(bf16[1,128,1536]{2,1,0:T(8,128)(2,1)S(1)} %bitcast.82), channel_id=1, source_target_pairs={{0,64},{16,80},{32,96},{48,112},{64,0},{80,16},{96,32},{112,48},{1... | collective-permute-start | bytes 1179656 | tf_op jit(solution)/shard_map/ppermute | solution.py:1070
  138.5 41.8 %all-to-all-start.3 = ((bf16[4,2,128,1536]{3,2,1,0:T(8,128)(2,1)}), bf16[4,2,128,1536]{3,2,1,0:T(8,128)(2,1)S(1)}, u32[]{:S(2)}, u32[]{:S(2)}) async-start(bf16[4,2,128,1536]{3,2,1,0:T(8,128)(2,1)} %broadcast_in_dim.27), calls=%async_computation.3 | async-start | bytes 6291456 | tf_op jit(solution)/shard_map/all_to_all | solution.py:1018
  180.3 41.0 %copy-start.36 = (bf16[4,2,128,1536]{3,2,1,0:T(8,128)(2,1)}, bf16[4,2,128,1536]{3,2,1,0:T(8,128)(2,1)S(1)}, u32[]{:S(2)}) copy-start(bf16[4,2,128,1536]{3,2,1,0:T(8,128)(2,1)S(1)} %all-to-all-done.3) | copy-start | bytes 9437188
  223.6 5.7 %collective-permute-start.2 = (bf16[8,128,1536]{2,1,0:T(8,128)(2,1)S(1)}, bf16[8,128,1536]{2,1,0:T(8,128)(2,1)S(1)}, u32[]{:S(2)}, u32[]{:S(2)}) collective-permute-start(bf16[8,128,1536]{2,1,0:T(8,128)(2,1)S(1)} %slice_bitcast_fusion), channel_id=1, source_target_pairs={{0,1},{1,0},{2,3},{3,2},{4,5},{5,4},{6,7},{7,6},{8,9},{9,8},{10,11... | collective-permute-start | bytes 9437192 | tf_op jit(solution)/shard_map/ppermute | solution.py:1105
  231.9 51.5 %all-to-all-start.4 = ((bf16[8,128,1536]{2,1,0:T(8,128)(2,1)}), bf16[8,128,1536]{2,1,0:T(8,128)(2,1)}, u32[]{:S(2)}, u32[]{:S(2)}) async-start(bf16[8,128,1536]{2,1,0:T(8,128)(2,1)} %fusion), calls=%async_computation.4 | async-start | bytes 6291456 | tf_op jit(solution)/shard_map/all_to_all | solution.py:1018
  247.6 15.3 %slice-start.2 = ((s8[6291456]{0:T(1024)(128)(4,1)}), s8[4194304]{0:T(1024)(128)(4,1)S(1)}, s32[]{:S(2)}) async-start(s8[6291456]{0:T(1024)(128)(4,1)} %bitcast.95), calls=%async_computation.13 | async-start | bytes 8388608
  247.6 15.3 %slice-start.3 = ((s8[6291456]{0:T(1024)(128)(4,1)}), s8[2097152]{0:T(1024)(128)(4,1)S(1)}, s32[]{:S(2)}) async-start(s8[6291456]{0:T(1024)(128)(4,1)} %bitcast.95), calls=%async_computation.14 | async-start | bytes 4194304
  247.6 15.3 %copy-start.43 = (bf16[8,2,128,128]{3,2,1,0:T(8,128)(2,1)S(1)}, bf16[8,2,128,128]{3,2,1,0:T(8,128)(2,1)}, u32[]{:S(2)}) copy-start(bf16[8,2,128,128]{3,2,1,0:T(8,128)(2,1)} %get-tuple-element.138) | copy-start | bytes 1572868
  247.6 61.1 %collective-permute-start.3 = (bf16[9216,128]{1,0:T(8,128)(2,1)}, bf16[9216,128]{1,0:T(8,128)(2,1)}, u32[]{:S(2)}, u32[]{:S(2)}) collective-permute-start(bf16[9216,128]{1,0:T(8,128)(2,1)} %get-tuple-element.127), channel_id=1, source_target_pairs={{0,16},{16,0},{32,48},{48,32},{64,80},{80,64},{96,112},{112,96},{1... | collective-permute-start | bytes 7077896 | tf_op jit(solution)/shard_map/ppermute | solution.py:1120
  260.6 54.7 %collective-permute-start.4 = (bf16[9216,128]{1,0:T(8,128)(2,1)}, bf16[9216,128]{1,0:T(8,128)(2,1)}, u32[]{:S(2)}, u32[]{:S(2)}) collective-permute-start(bf16[9216,128]{1,0:T(8,128)(2,1)} %get-tuple-element.136), channel_id=1, source_target_pairs={{0,48},{16,32},{32,16},{48,0},{64,112},{80,96},{96,80},{112,64},{1... | collective-permute-start | bytes 7077896 | tf_op jit(solution)/shard_map/ppermute | solution.py:1120
  302.7 12.5 %copy-start.19 = (bf16[4608,128]{1,0:T(8,128)(2,1)S(1)}, bf16[4608,128]{1,0:T(8,128)(2,1)}, u32[]{:S(2)}) copy-start(bf16[4608,128]{1,0:T(8,128)(2,1)} %get-tuple-element.129.p0) | copy-start | bytes 3538948
  302.7 12.5 %copy-start.20 = (bf16[4608,128]{1,0:T(8,128)(2,1)S(1)}, bf16[4608,128]{1,0:T(8,128)(2,1)}, u32[]{:S(2)}) copy-start(bf16[4608,128]{1,0:T(8,128)(2,1)} %get-tuple-element.135.p6) | copy-start | bytes 3538948
  302.7 12.5 %copy-start.21 = (bf16[4608,128]{1,0:T(8,128)(2,1)S(1)}, bf16[4608,128]{1,0:T(8,128)(2,1)}, u32[]{:S(2)}) copy-start(bf16[4608,128]{1,0:T(8,128)(2,1)} %get-tuple-element.133.p1) | copy-start | bytes 3538948
  302.8 12.5 %copy-start.22 = (bf16[4608,128]{1,0:T(8,128)(2,1)S(1)}, bf16[4608,128]{1,0:T(8,128)(2,1)}, u32[]{:S(2)}) copy-start(bf16[4608,128]{1,0:T(8,128)(2,1)} %get-tuple-element.134.p3) | copy-start | bytes 3538948
  302.8 45.3 %collective-permute-start.9 = (bf16[4,1776,128]{2,1,0:T(8,128)(2,1)}, bf16[4,1776,128]{2,1,0:T(8,128)(2,1)S(1)}, u32[]{:S(2)}, u32[]{:S(2)}) collective-permute-start(bf16[4,1776,128]{2,1,0:T(8,128)(2,1)} %get-tuple-element.154), channel_id=1, source_target_pairs={{0,64},{16,80},{32,96},{48,112},{64,0},{80,16},{96,32},{112,48},{1... | collective-permute-start | bytes 5455880 | tf_op jit(solution)/shard_map/ppermute | solution.py:1148
  308.1 13.7 %collective-permute-start.5 = (bf16[4,128,1536]{2,1,0:T(8,128)(2,1)S(1)}, bf16[4,128,1536]{2,1,0:T(8,128)(2,1)S(1)}, u32[]{:S(2)}, u32[]{:S(2)}) collective-permute-start(bf16[4,128,1536]{2,1,0:T(8,128)(2,1)S(1)} %get-tuple-element.203), channel_id=1, source_target_pairs={{0,1},{1,0},{2,3},{3,2},{4,5},{5,4},{6,7},{7,6},{8,9},{9,8},{10,11... | collective-permute-start | bytes 4718600 | tf_op jit(solution)/shard_map/ppermute | solution.py:1170
  308.2 13.6 %collective-permute-start.6 = (bf16[4,128,1536]{2,1,0:T(8,128)(2,1)S(1)}, bf16[4,128,1536]{2,1,0:T(8,128)(2,1)S(1)}, u32[]{:S(2)}, u32[]{:S(2)}) collective-permute-start(bf16[4,128,1536]{2,1,0:T(8,128)(2,1)S(1)} %get-tuple-element.202), channel_id=1, source_target_pairs={{0,1},{1,0},{2,3},{3,2},{4,5},{5,4},{6,7},{7,6},{8,9},{9,8},{10,11... | collective-permute-start | bytes 4718600 | tf_op jit(solution)/shard_map/ppermute | solution.py:1171
  319.7 27.1 %collective-permute-start.10 = (bf16[4608,128]{1,0:T(8,128)(2,1)S(1)}, bf16[4608,128]{1,0:T(8,128)(2,1)S(1)}, u32[]{:S(2)}, u32[]{:S(2)}) collective-permute-start(bf16[4608,128]{1,0:T(8,128)(2,1)S(1)} %get-tuple-element.157), channel_id=1, source_target_pairs={{0,16},{16,0},{32,48},{48,32},{64,80},{80,64},{96,112},{112,96},{1... | collective-permute-start | bytes 3538952 | tf_op jit(solution)/shard_map/ppermute | solution.py:1120
  319.8 28.3 %collective-permute-start.11 = (bf16[4608,128]{1,0:T(8,128)(2,1)S(1)}, bf16[4608,128]{1,0:T(8,128)(2,1)S(1)}, u32[]{:S(2)}, u32[]{:S(2)}) collective-permute-start(bf16[4608,128]{1,0:T(8,128)(2,1)S(1)} %get-tuple-element.149), channel_id=1, source_target_pairs={{0,48},{16,32},{32,16},{48,0},{64,112},{80,96},{96,80},{112,64},{1... | collective-permute-start | bytes 3538952 | tf_op jit(solution)/shard_map/ppermute | solution.py:1120
  324.8 27.9 %collective-permute-start.7 = (bf16[2,128,1536]{2,1,0:T(8,128)(2,1)S(1)}, bf16[2,128,1536]{2,1,0:T(8,128)(2,1)S(1)}, u32[]{:S(2)}, u32[]{:S(2)}) collective-permute-start(bf16[2,128,1536]{2,1,0:T(8,128)(2,1)S(1)} %get-tuple-element.152), channel_id=1, source_target_pairs={{0,4},{1,5},{2,6},{3,7},{4,0},{5,1},{6,2},{7,3},{8,12},{9,13},{10,... | collective-permute-start | bytes 2359304 | tf_op jit(solution)/shard_map/ppermute | solution.py:1165
  326.5 26.2 %collective-permute-start.8 = (bf16[2,128,1536]{2,1,0:T(8,128)(2,1)S(1)}, bf16[2,128,1536]{2,1,0:T(8,128)(2,1)S(1)}, u32[]{:S(2)}, u32[]{:S(2)}) collective-permute-start(bf16[2,128,1536]{2,1,0:T(8,128)(2,1)S(1)} %get-tuple-element.153), channel_id=1, source_target_pairs={{0,12},{1,13},{2,14},{3,15},{4,8},{5,9},{6,10},{7,11},{8,4},{9,5},... | collective-permute-start | bytes 2359304 | tf_op jit(solution)/shard_map/ppermute | solution.py:1165
  349.8 27.8 %collective-permute-start.12 = (bf16[4608,128]{1,0:T(8,128)(2,1)}, bf16[4608,128]{1,0:T(8,128)(2,1)S(1)}, u32[]{:S(2)}, u32[]{:S(2)}) collective-permute-start(bf16[4608,128]{1,0:T(8,128)(2,1)} %get-tuple-element.160), channel_id=1, source_target_pairs={{0,64},{16,80},{32,96},{48,112},{64,0},{80,16},{96,32},{112,48},{1... | collective-permute-start | bytes 3538952 | tf_op jit(solution)/shard_map/ppermute | solution.py:1120
  356.1 33.6 %all-to-all-start.5 = ((bf16[4,2160,128]{2,1,0:T(8,128)(2,1)}), bf16[4,2160,128]{2,1,0:T(8,128)(2,1)}, u32[]{:S(2)}, u32[]{:S(2)}) async-start(bf16[4,2160,128]{2,1,0:T(8,128)(2,1)} %merge_shares.1), calls=%async_computation.5 | async-start | bytes 4423680 | tf_op jit(solution)/shard_map/all_to_all | solution.py:1018
  380.1 30.9 %collective-permute-start.15 = (bf16[4608,128]{1,0:T(8,128)(2,1)S(1)}, bf16[4608,128]{1,0:T(8,128)(2,1)}, u32[]{:S(2)}, u32[]{:S(2)}) collective-permute-start(bf16[4608,128]{1,0:T(8,128)(2,1)S(1)} %add_convert_fusion.refs_1_), channel_id=1, source_target_pairs={{0,64},{16,80},{32,96},{48,112},{64,0},{80,16},{96,32},{112,48},{1... | collective-permute-start | bytes 3538952 | tf_op jit(solution)/shard_map/ppermute | solution.py:1120
  383.0 28.0 %collective-permute-start.16 = (bf16[4608,128]{1,0:T(8,128)(2,1)S(1)}, bf16[4608,128]{1,0:T(8,128)(2,1)}, u32[]{:S(2)}, u32[]{:S(2)}) collective-permute-start(bf16[4608,128]{1,0:T(8,128)(2,1)S(1)} %add_convert_fusion.refs_1_), channel_id=1, source_target_pairs={{0,16},{16,0},{32,48},{48,32},{64,80},{80,64},{96,112},{112,96},{1... | collective-permute-start | bytes 3538952 | tf_op jit(solution)/shard_map/ppermute | solution.py:1120
  383.2 29.0 %collective-permute-start.17 = (bf16[4608,128]{1,0:T(8,128)(2,1)S(1)}, bf16[4608,128]{1,0:T(8,128)(2,1)}, u32[]{:S(2)}, u32[]{:S(2)}) collective-permute-start(bf16[4608,128]{1,0:T(8,128)(2,1)S(1)} %add_convert_fusion.refs_1_), channel_id=1, source_target_pairs={{0,48},{16,32},{32,16},{48,0},{64,112},{80,96},{96,80},{112,64},{1... | collective-permute-start | bytes 3538952 | tf_op jit(solution)/shard_map/ppermute | solution.py:1120
  384.2 17.3 %collective-permute-start.13 = (bf16[2,128,1536]{2,1,0:T(8,128)(2,1)}, bf16[2,128,1536]{2,1,0:T(8,128)(2,1)}, u32[]{:S(2)}, u32[]{:S(2)}) collective-permute-start(bf16[2,128,1536]{2,1,0:T(8,128)(2,1)} %get-tuple-element.168), channel_id=1, source_target_pairs={{0,8},{1,9},{2,10},{3,11},{4,12},{5,13},{6,14},{7,15},{8,0},{9,1},... | collective-permute-start | bytes 2359304 | tf_op jit(solution)/shard_map/ppermute | solution.py:1165
  396.8 29.5 %all-to-all-start.6 = ((bf16[16,112,512]{2,1,0:T(8,128)(2,1)}), bf16[16,112,512]{2,1,0:T(8,128)(2,1)S(1)}, u32[]{:S(2)}, u32[]{:S(2)}) async-start(bf16[16,112,512]{2,1,0:T(8,128)(2,1)} %get-tuple-element.165), calls=%async_computation.6 | async-start | bytes 3670016 | tf_op jit(solution)/shard_map/all_to_all | solution.py:1018
  401.3 24.9 %copy-start.34 = (bf16[96,128]{1,0:T(8,128)(2,1)S(1)}, bf16[96,128]{1,0:T(8,128)(2,1)}, u32[]{:S(2)}) copy-start(bf16[96,128]{1,0:T(8,128)(2,1)} %get-tuple-element.172.down_ref) | copy-start | bytes 73732
  412.2 29.2 %collective-permute-start.18 = (bf16[4608,128]{1,0:T(8,128)(2,1)}, bf16[4608,128]{1,0:T(8,128)(2,1)}, u32[]{:S(2)}, u32[]{:S(2)}) collective-permute-start(bf16[4608,128]{1,0:T(8,128)(2,1)} %collective-permute-done.15.refs_4_), channel_id=1, source_target_pairs={{0,16},{16,0},{32,48},{48,32},{64,80},{80,64},{96,112},{112,96},{1... | collective-permute-start | bytes 3538952 | tf_op jit(solution)/shard_map/ppermute | solution.py:1120
  412.7 28.7 %collective-permute-start.19 = (bf16[4608,128]{1,0:T(8,128)(2,1)}, bf16[4608,128]{1,0:T(8,128)(2,1)}, u32[]{:S(2)}, u32[]{:S(2)}) collective-permute-start(bf16[4608,128]{1,0:T(8,128)(2,1)} %collective-permute-done.15.refs_4_), channel_id=1, source_target_pairs={{0,48},{16,32},{32,16},{48,0},{64,112},{80,96},{96,80},{112,64},{1... | collective-permute-start | bytes 3538952 | tf_op jit(solution)/shard_map/ppermute | solution.py:1120
  416.6 25.0 %copy-start.40 = (bf16[8,128,128]{2,1,0:T(8,128)(2,1)S(1)}, bf16[8,128,128]{2,1,0:T(8,128)(2,1)}, u32[]{:S(2)}) copy-start(bf16[8,128,128]{2,1,0:T(8,128)(2,1)} %get-tuple-element.171) | copy-start | bytes 786436
  416.6 70.9 %collective-permute-start.20 = (bf16[4608,128]{1,0:T(8,128)(2,1)}, bf16[4608,128]{1,0:T(8,128)(2,1)}, u32[]{:S(2)}, u32[]{:S(2)}) collective-permute-start(bf16[4608,128]{1,0:T(8,128)(2,1)} %collective-permute-done.17.refs_3_), channel_id=1, source_target_pairs={{0,16},{16,0},{32,48},{48,32},{64,80},{80,64},{96,112},{112,96},{1... | collective-permute-start | bytes 3538952 | tf_op jit(solution)/shard_map/ppermute | solution.py:1120
  442.9 13.6 %copy-start.46 = (bf16[96]{0:T(256)(128)(2,1)S(1)}, bf16[96]{0:T(256)(128)(2,1)}, u32[]{:S(2)}) copy-start(bf16[96]{0:T(256)(128)(2,1)} %param.19) | copy-start | bytes 580
  442.9 37.8 %all-to-all-start.7 = ((bf16[8,864,128]{2,1,0:T(8,128)(2,1)}), bf16[8,864,128]{2,1,0:T(8,128)(2,1)S(1)}, u32[]{:S(2)}, u32[]{:S(2)}) async-start(bf16[8,864,128]{2,1,0:T(8,128)(2,1)} %pad_maximum_fusion), calls=%async_computation.7 | async-start | bytes 3538944 | tf_op jit(solution)/shard_map/all_to_all | solution.py:1018
  453.1 9.2 %collective-permute-start.14 = (bf16[128,1536]{1,0:T(8,128)(2,1)}, bf16[128,1536]{1,0:T(8,128)(2,1)S(1)}, u32[]{:S(2)}, u32[]{:S(2)}) collective-permute-start(bf16[128,1536]{1,0:T(8,128)(2,1)} %fusion.5), channel_id=1, source_target_pairs={{0,2},{1,3},{2,0},{3,1},{4,6},{5,7},{6,4},{7,5},{8,10},{9,11},{10,... | collective-permute-start | bytes 1179656 | tf_op jit(solution)/shard_map/ppermute | solution.py:1190
  453.1 37.1 %collective-permute-start.21 = (bf16[4608,128]{1,0:T(8,128)(2,1)}, bf16[4608,128]{1,0:T(8,128)(2,1)}, u32[]{:S(2)}, u32[]{:S(2)}) collective-permute-start(bf16[4608,128]{1,0:T(8,128)(2,1)} %collective-permute-done.18.refs_5_), channel_id=1, source_target_pairs={{0,48},{16,32},{32,16},{48,0},{64,112},{80,96},{96,80},{112,64},{1... | collective-permute-start | bytes 3538952 | tf_op jit(solution)/shard_map/ppermute | solution.py:1120
  465.0 15.7 %copy-start.23 = (bf16[96,1536]{1,0:T(8,128)(2,1)S(1)}, bf16[96,1536]{1,0:T(8,128)(2,1)}, u32[]{:S(2)}) copy-start(bf16[96,1536]{1,0:T(8,128)(2,1)} %wq_ref.1) | copy-start | bytes 884740
  465.0 15.7 %copy-start.30 = (bf16[96,512]{1,0:T(8,128)(2,1)S(1)}, bf16[96,512]{1,0:T(8,128)(2,1)}, u32[]{:S(2)}) copy-start(bf16[96,512]{1,0:T(8,128)(2,1)} %wk_ref.1) | copy-start | bytes 294916
  465.0 15.7 %copy-start.31 = (bf16[96,512]{1,0:T(8,128)(2,1)S(1)}, bf16[96,512]{1,0:T(8,128)(2,1)}, u32[]{:S(2)}) copy-start(bf16[96,512]{1,0:T(8,128)(2,1)} %wv_ref.1) | copy-start | bytes 294916
  (36 other events, 121.4 us)
Sparse Core Ops, SparseCore 0:
  12.2 79.9 all-gather.3
  94.5 52.5 all-gather.7
  149.4 42.9 all-gather.5

commit v18 on v16

--- a/solution.py
+++ b/solution.py
@@ -1080,15 +1080,14 @@
     shared_cols = jnp.concatenate(
         [shared_gate.reshape(96, N_EXP, SHARED), shared_up.reshape(96, N_EXP, SHARED)], axis=2
     ).transpose(1, 0, 2)
-    w_shared = swap_all(shared_cols, "exp").reshape(WIDTH, 2 * SHARED)
     shared_two = jnp.concatenate([shared_down, shared_down], axis=0)
 
     hidden_one = norm_rows(tokens, gain_attn)
     hidden_seq = norm_rows(tokens_seq, gain_attn)
-    hidden_seq = after(hidden_seq, w_shared)
     queries, kv_all = project(hidden_one, hidden_seq, w_all)
     attended, att_f, logs = attend(ctx_s, queries, kv_all)
     middle, hidden_two = middle_norm(attended, w_all, tokens[0], gain_ffn)
+    w_shared = swap_all(after(shared_cols, hidden_two), "exp").reshape(WIDTH, 2 * SHARED)
 
     hidden_all = lax.all_gather(hidden_two, "exp", axis=0, tiled=True)
     hidden_all = hidden_all.reshape(HALF, 2, BLOCK, WIDTH)

time: 510 us -> 513 us (level)
  the two profiles are of different devices: /device:TPU:0 before, /device:TPU:8 now
where the time goes in v18:
time: 513 us; the launch traced here: 504 us
  waiting for transfers between devices  201 us (39%)
  Pallas kernels  145 us (28%)
  starting transfers between devices  71.1 us (14%)
  local copies, waits for them, and re-layouts  49.4 us (10%)
  other arithmetic  15.4 us (3%)
  between operations  14.8 us (3%)
  matrix products  6.73 us (1%)
    all_to_all x8, waiting for transfers between devices, swap_all(): lax.all_to_all(rows, axis, split_axis=0, concat_axis=0, tiled=True, axis_...  86.8 us
    ppermute x12, waiting for transfers between devices, to(): return lax.ppermute(rows, 'ctx', [(i, i ^ k) for i in range(N_CTX)])  67.3 us
    all_to_all x8, starting transfers between devices, swap_all(): lax.all_to_all(rows, axis, split_axis=0, concat_axis=0, tiled=True, axis_...  42.3 us
    unnamed x124, local copies, waits for them, and re-layouts  29.4 us
    pallas_call x1, Pallas kernels, expert_back(): pl.pallas_call(expert_kernel, grid_spec=pltpu.PrefetchScalarGridSpec(num_...  28.9 us
    ppermute x2, waiting for transfers between devices, of_sequence(): other = lax.ppermute(rows, 'ctx', z_swap)  26.3 us
    pallas_call x2, Pallas kernels, expert_weights(): pl.pallas_call(lambda *refs: expert_weights_kernel(halved, *refs), grid_s...  22.3 us
    pallas_call x1, Pallas kernels, place_rows(): pl.pallas_call(place_kernel, grid_spec=pltpu.PrefetchScalarGridSpec(num_s...  13.7 us
  transfers between devices with their start and end apart: 33, of which 20 were waited for; matrix products, arithmetic and copies ran while one was open for 8% of the time, Pallas kernels for 22%

profile of v18, /device:TPU:8, one launch (start us, length us, event | category | flops | bytes accessed | tf_op | source)
XLA Modules:
  0.0 504.0 jit_solution(13772137013165832769)
XLA Ops:
  13.3 4.0 collective-permute-start
  17.9 4.9 all-to-all-start
  22.8 6.0 %collective-permute-done = bf16[1,128,1536]{2,1,0:T(8,128)(2,1)S(1)} collective-permute-done((bf16[1,128,1536]{2,1,0:T(8,128)(2,1)S(1)}, bf16[1,128,1536]{2,1,0:T(8,128)(2,1)S(1)}, u32[]{:S(2)}, u32[]{:S(2)}) %collective-permute-start) | collective-permute-done | bytes 393248 | tf_op jit(solution)/shard_map/ppermute | solution.py:1070
  31.7 5.0 all-to-all-start.1
  39.7 33.5 %all-to-all-done.1 = bf16[4,2,128,1536]{3,2,1,0:T(8,128)(2,1)S(1)} async-done(((bf16[4,2,128,1536]{3,2,1,0:T(8,128)(2,1)}), bf16[4,2,128,1536]{3,2,1,0:T(8,128)(2,1)S(1)}, u32[]{:S(2)}, u32[]{:S(2)}) %all-to-all-start.1) | async-done | bytes 3145760 | tf_op jit(solution)/shard_map/all_to_all | solution.py:1018
  76.6 11.5 %all-gather.4.cloned.1.call-done.w_ref.wq_ref.wkv_ref = bf16[1536,4096]{1,0:T(8,128)(2,1)} async-done(((bf16[96,4096]{1,0:T(8,128)(2,1)}), bf16[1536,4096]{1,0:T(8,128)(2,1)}) %all-gather.4.cloned.1.call-update) | async-done | bytes 12582928 | tf_op jit(solution)/shard_map/all_gather | solution.py:1056
  90.0 7.7 %project.1 = (bf16[128,1536]{1,0:T(8,128)(2,1)S(1)}, bf16[8,128,1024]{2,1,0:T(8,128)(2,1)S(1)}) custom-call(bf16[1,128,1536]{2,1,0:T(8,128)(2,1)S(1)} %copy-done.19, bf16[8,128,1536]{2,1,0:T(8,128)(2,1)S(1)} %copy-done.4, bf16[1536,4096]{1,0:T(8,128)(2,1)} %all-gather.4.cloned.1.call-done.w_ref.wq_ref.wkv_ref), custom_call_target="tpu_custom_call" | custom-call | bytes 29520000 | tf_op jit(solution)/shard_map/project/pallas_call | solution.py:815
  97.6 5.8 %attend.1 = (bf16[128,1536]{1,0:T(8,128)(2,1)S(1)}, f32[128,1536]{1,0:T(8,128)S(1)}, f32[1536,128]{1,0:T(8,128)S(1)}) custom-call(s32[1]{0:T(128)} %bitcast.ctx_ref.refs_0_, bf16[128,1536]{1,0:T(8,128)(2,1)S(1)} %get-tuple-element.109.q_ref, bf16[8,128,1024]{2,1,0:T(8,128)(2,1)S(1)} %get-tuple-element.110.k_ref.v_ref, ...), custom_call_target="tpu_custom_call" | custom-call | bytes 22140000 | tf_op jit(solution)/shard_map/attend/pallas_call | solution.py:99
  106.0 4.5 middle_norm.1
  112.0 20.3 %collective-permute-done.1 = bf16[1,128,1536]{2,1,0:T(8,128)(2,1)S(1)} collective-permute-done((bf16[1,128,1536]{2,1,0:T(8,128)(2,1)S(1)}, bf16[1,128,1536]{2,1,0:T(8,128)(2,1)S(1)}, u32[]{:S(2)}, u32[]{:S(2)}) %collective-permute-start.1) | collective-permute-done | bytes 393248 | tf_op jit(solution)/shard_map/ppermute | solution.py:1070
  134.4 4.9 all-to-all-start.2
  146.0 29.0 %all-to-all-done.2 = bf16[4,2,128,1536]{3,2,1,0:T(8,128)(2,1)S(1)} async-done(((bf16[4,2,128,1536]{3,2,1,0:T(8,128)(2,1)}), bf16[4,2,128,1536]{3,2,1,0:T(8,128)(2,1)S(1)}, u32[]{:S(2)}, u32[]{:S(2)}) %all-to-all-start.2) | async-done | bytes 3145760 | tf_op jit(solution)/shard_map/all_to_all | solution.py:1018
  175.0 4.6 all-to-all-start.3
  182.2 13.7 %place_rows.1 = (bf16[8,2,128,128]{3,2,1,0:T(8,128)(2,1)}, bf16[2,2,384,1536]{3,2,1,0:T(8,128)(2,1)}, f32[2,2,384,512]{3,2,1,0:T(8,128)}, f32[8,2,128,128]{3,2,1,0:T(8,128)}, f32[2,2,384,128]{3,2,1,0:T(8,128)}) custom-call(s32[1]{0:T(128)} %bitcast.3.at_ref, bf16[8,2,128,1664]{3,2,1,0:T(8,128)(2,1)} %bitcast.84, bf16[2,512,1536]{2,1,0:T(8,128)(2,1)} %wd_ref.1, ...), custom_call_target="tpu_custom_call" | custom-call | bytes 51660000 | tf_op jit(solution)/shard_map/place_rows/pallas_call | solution.py:368
  196.0 28.9 %expert_back.1 = (bf16[2,8,128,1536]{3,2,1,0:T(8,128)(2,1)}, bf16[2,2,384,1536]{3,2,1,0:T(8,128)(2,1)}, bf16[2,2,384,512]{3,2,1,0:T(8,128)(2,1)}, bf16[2,2,384,1...) custom-call(s32[1]{0:T(128)} %bitcast.3.at_ref, ...), custom_call_target="tpu_custom_call" | custom-call | bytes 103320000 | tf_op jit(solution)/shard_map/expert_back/pallas_call | solution.py:447
  227.6 5.3 %collective-permute-done.2 = bf16[8,128,1536]{2,1,0:T(8,128)(2,1)S(1)} collective-permute-done((bf16[8,128,1536]{2,1,0:T(8,128)(2,1)S(1)}, bf16[8,128,1536]{2,1,0:T(8,128)(2,1)S(1)}, u32[]{:S(2)}, u32[]{:S(2)}) %collective-permute-start.2) | collective-permute-done | bytes 3145760 | tf_op jit(solution)/shard_map/ppermute | solution.py:1104
  232.9 2.6 fusion
  235.5 5.5 %all-to-all-start.4 = ((bf16[8,128,1536]{2,1,0:T(8,128)(2,1)}), bf16[8,128,1536]{2,1,0:T(8,128)(2,1)}, u32[]{:S(2)}, u32[]{:S(2)}) async-start(bf16[8,128,1536]{2,1,0:T(8,128)(2,1)} %fusion), calls=%async_computation.4 | async-start | bytes 6291456 | tf_op jit(solution)/shard_map/all_to_all | solution.py:1018
  241.0 10.9 %expert_weights.2 = (bf16[9216,128]{1,0:T(8,128)(2,1)}, bf16[9216,128]{1,0:T(8,128)(2,1)}) custom-call(s32[1]{0:T(128)} %bitcast.ctx_ref.refs_0_, bf16[2,768,1536]{2,1,0:T(8,128)(2,1)} %bitcast.91, bf16[2,768,1536]{2,1,0:T(8,128)(2,1)} %bitcast.89, bf16[2,768,512]{2,1,0:T(8,128)(2,1)} %bitcast.74, bf16[2,768,1024]{2,1,0:T(8,128)(2,1)} %bitcast.85, ...), custom_call_target="tpu_custom_call" | custom-call | bytes 7380000 | tf_op jit(solution)/shard_map/expert_weights/pallas_call | solution.py:915
  253.4 11.4 %expert_weights.3 = (bf16[4608,128]{1,0:T(8,128)(2,1)}, bf16[4608,128]{1,0:T(8,128)(2,1)}, bf16[4608,128]{1,0:T(8,128)(2,1)}, bf16[4608,128]{1,0:T(8,128)(2,1)}) custom-call(s32[1]{0:T(128)} %bitcast.ctx_ref.refs_0_, bf16[2,768,1536]{2,1,0:T(8,128)(2,1)} %bitcast.92, bf16[2,768,1536]{2,1,0:T(8,128)(2,1)} %bitcast.90, bf16[2,768,512]{2,1,0:T(8,128)(2,1)} %bitcast.75, ...), custom_call_target="tpu_custom_call" | custom-call | bytes 7380000 | tf_op jit(solution)/shard_map/expert_weights/pallas_call | solution.py:915
  265.2 2.6 convolution_convert_fusion
  270.9 9.8 %expert_output.1.own_ref = bf16[2,8,128,1536]{3,2,1,0:T(8,128)(2,1)} custom-call(s32[1]{0:T(128)} %bitcast.3.at_ref, bf16[2,2,384,512]{3,2,1,0:T(8,128)(2,1)S(1)} %copy-done.5, f32[2,2,384,128]{3,2,1,0:T(8,128)S(1)} %copy-done.33, bf16[8,2,128,128]{3,2,1,0:T(8,128)(2,1)S(1)} %copy-done.15, bf16[8,2,128,128]{3,2,1,0:T(8,128)(2,1)S(1)} %copy-done.8, ...), custom_call_target="tpu_custom_call" | custom-call | bytes 7380000 | tf_op jit(solution)/shard_map/expert_output/pallas_call | solution.py:499
  280.6 4.1 fusion.8
  286.9 5.6 %middle_back.1 = (f32[128,1536]{1,0:T(8,128)S(1)}, bf16[128,1536]{1,0:T(8,128)(2,1)S(1)}, bf16[128,1536]{1,0:T(8,128)(2,1)S(1)}, f32[16,128]{1,0:T(8,128)S(1)}) custom-call(bf16[8,128,1536]{2,1,0:T(8,128)(2,1)} %all-to-all-done.4.pieces_ref, f32[128,1536]{1,0:T(8,128)S(1)} %copy-done.9, bf16[128,1536]{1,0:T(8,128)(2,1)S(1)} %bitcast.81, ...), custom_call_target="tpu_custom_call" | custom-call | bytes 3690000 | tf_op jit(solution)/shard_map/middle_back/pallas_call | solution.py:290
  295.5 10.3 %attend_back.1 = (bf16[128,1536]{1,0:T(8,128)(2,1)}, bf16[4,1776,128]{2,1,0:T(8,128)(2,1)}, bf16[4,1776,128]{2,1,0:T(8,128)(2,1)}) custom-call(s32[1]{0:T(128)} %bitcast.ctx_ref.refs_0_, bf16[128,1536]{1,0:T(8,128)(2,1)} %copy-done.17, bf16[128,1536]{1,0:T(8,128)(2,1)} %copy-done.35, f32[128,1536]{1,0:T(8,128)} %copy-done.31, f32[1536,128]{1,0:T(8,128)} %copy-done.32, ...), custom_call_target="tpu_custom_call" | custom-call | bytes 7380000 | tf_op jit(solution)/shard_map/attend_back/pallas_call | solution.py:202
  310.0 8.2 %collective-permute-done.4.relay_b.got_31 = bf16[9216,128]{1,0:T(8,128)(2,1)} collective-permute-done((bf16[9216,128]{1,0:T(8,128)(2,1)}, bf16[9216,128]{1,0:T(8,128)(2,1)}, u32[]{:S(2)}, u32[]{:S(2)}) %collective-permute-start.4) | collective-permute-done | bytes 2359328 | tf_op jit(solution)/shard_map/ppermute | solution.py:1119
  318.2 4.4 piece_sums.2
  324.5 2.9 spread_sums.1
  331.2 18.4 %collective-permute-done.10.got_11 = bf16[4608,128]{1,0:T(8,128)(2,1)S(1)} collective-permute-done((bf16[4608,128]{1,0:T(8,128)(2,1)S(1)}, bf16[4608,128]{1,0:T(8,128)(2,1)S(1)}, u32[]{:S(2)}, u32[]{:S(2)}) %collective-permute-start.10) | collective-permute-done | bytes 1179680 | tf_op jit(solution)/shard_map/ppermute | solution.py:1119
  355.2 6.7 %all-to-all-start.5 = ((bf16[4,2160,128]{2,1,0:T(8,128)(2,1)}), bf16[4,2160,128]{2,1,0:T(8,128)(2,1)}, u32[]{:S(2)}, u32[]{:S(2)}) async-start(bf16[4,2160,128]{2,1,0:T(8,128)(2,1)} %merge_shares.1), calls=%async_computation.5 | async-start | bytes 4423680 | tf_op jit(solution)/shard_map/all_to_all | solution.py:1018
  361.9 15.8 %collective-permute-done.12 = bf16[4608,128]{1,0:T(8,128)(2,1)} collective-permute-done((bf16[4608,128]{1,0:T(8,128)(2,1)S(1)}, bf16[4608,128]{1,0:T(8,128)(2,1)}, u32[]{:S(2)}, u32[]{:S(2)}) %collective-permute-start.12) | collective-permute-done | bytes 1179680 | tf_op jit(solution)/shard_map/ppermute | solution.py:1119
  380.2 2.7 collective-permute-start.16
  383.2 2.6 collective-permute-start.13
  385.8 3.8 all-to-all-done.5.got_ref
  389.6 7.1 %column_grads.1 = (bf16[16,112,512]{2,1,0:T(8,128)(2,1)}, bf16[8,128,128]{2,1,0:T(8,128)(2,1)}, bf16[96,128]{1,0:T(8,128)(2,1)}) custom-call(bf16[4,2160,128]{2,1,0:T(8,128)(2,1)} %all-to-all-done.5.got_ref, bf16[8,128,1536]{2,1,0:T(8,128)(2,1)} %copy-done.3, bf16[8,128,1536]{2,1,0:T(8,128)(2,1)} %bitcast.93), custom_call_target="tpu_custom_call" | custom-call | bytes 29520000 | tf_op jit(solution)/shard_map/column_grads/pallas_call | solution.py:614
  396.7 4.6 all-to-all-start.6
  401.3 4.0 collective-permute-done.15.refs_4_
  405.3 4.4 collective-permute-done.16.refs_2_
  413.4 3.0 convert_add_fusion.1
  417.5 8.6 %all-to-all-done.6.got_ref = bf16[16,112,512]{2,1,0:T(8,128)(2,1)S(1)} async-done(((bf16[16,112,512]{2,1,0:T(8,128)(2,1)}), bf16[16,112,512]{2,1,0:T(8,128)(2,1)S(1)}, u32[]{:S(2)}, u32[]{:S(2)}) %all-to-all-start.6) | async-done | bytes 1835040 | tf_op jit(solution)/shard_map/all_to_all | solution.py:1018
  426.4 14.2 %collective-permute-done.18.refs_5_ = bf16[4608,128]{1,0:T(8,128)(2,1)} collective-permute-done((bf16[4608,128]{1,0:T(8,128)(2,1)}, bf16[4608,128]{1,0:T(8,128)(2,1)}, u32[]{:S(2)}, u32[]{:S(2)}) %collective-permute-start.18) | collective-permute-done | bytes 1179680 | tf_op jit(solution)/shard_map/ppermute | solution.py:1119
  442.2 6.1 %all-to-all-start.7 = ((bf16[8,864,128]{2,1,0:T(8,128)(2,1)}), bf16[8,864,128]{2,1,0:T(8,128)(2,1)S(1)}, u32[]{:S(2)}, u32[]{:S(2)}) async-start(bf16[8,864,128]{2,1,0:T(8,128)(2,1)} %pad_maximum_fusion), calls=%async_computation.7 | async-start | bytes 3538944 | tf_op jit(solution)/shard_map/all_to_all | solution.py:1018
  453.0 4.6 copy-done
  459.3 4.1 collective-permute-done.14
  465.8 8.3 %unpack_experts.2 = (f32[2,1536,512]{2,1,0:T(8,128)}, f32[2,1536,512]{2,1,0:T(8,128)}, f32[2,512,1536]{2,1,0:T(8,128)}) custom-call(s32[1]{0:T(128)} %bitcast.ctx_ref.refs_0_, bf16[4608,128]{1,0:T(8,128)(2,1)S(1)} %add_convert_fusion.refs_1_, bf16[4608,128]{1,0:T(8,128)(2,1)} %collective-permute-done.16.refs_2_, ...), custom_call_target="tpu_custom_call" | custom-call | bytes 44280000 | tf_op jit(solution)/shard_map/unpack_experts/pallas_call | solution.py:959
  474.1 9.8 %all-to-all-done.7.got_ref = bf16[8,864,128]{2,1,0:T(8,128)(2,1)S(1)} async-done(((bf16[8,864,128]{2,1,0:T(8,128)(2,1)}), bf16[8,864,128]{2,1,0:T(8,128)(2,1)S(1)}, u32[]{:S(2)}, u32[]{:S(2)}) %all-to-all-start.7) | async-done | bytes 1769504 | tf_op jit(solution)/shard_map/all_to_all | solution.py:1018
  485.7 4.6 copy-done.1
  493.1 4.0 unpack_experts.3
  (207 shorter events, 84.3 us)
Async XLA Ops:
  7.2 80.8 %all-gather.4.cloned.1.call-start = ((), (), s32[]{:S(2)}) async-start(), calls=%async_computation.8 | async-start | bytes 13369344 | tf_op jit(solution)/shard_map/all_gather | solution.py:1056
  12.0 169.5 %all-gather.8.cloned.1.call-start = ((), (), s32[]{:S(2)}) async-start(), calls=%async_computation.10 | async-start | bytes 7241728 | tf_op jit(solution)/shard_map/all_gather | solution.py:1063
  13.3 15.5 %collective-permute-start = (bf16[1,128,1536]{2,1,0:T(8,128)(2,1)S(1)}, bf16[1,128,1536]{2,1,0:T(8,128)(2,1)S(1)}, u32[]{:S(2)}, u32[]{:S(2)}) collective-permute-start(bf16[1,128,1536]{2,1,0:T(8,128)(2,1)S(1)} %copy-done.6), channel_id=1, source_target_pairs={{0,64},{16,80},{32,96},{48,112},{64,0},{80,16},{96,32},{112,48},{1... | collective-permute-start | bytes 1179656 | tf_op jit(solution)/shard_map/ppermute | solution.py:1070
  17.9 11.8 %all-to-all-start = ((bf16[16,1,192]{2,1,0:T(2,128)(2,1)}), bf16[16,1,192]{2,1,0:T(2,128)(2,1)S(1)}, u32[]{:S(2)}, u32[]{:S(2)}) async-start(bf16[16,1,192]{2,1,0:T(2,128)(2,1)} %broadcast_in_dim.24), calls=%async_computation | async-start | bytes 32768 | tf_op jit(solution)/shard_map/all_to_all | solution.py:1018
  31.7 41.5 %all-to-all-start.1 = ((bf16[4,2,128,1536]{3,2,1,0:T(8,128)(2,1)}), bf16[4,2,128,1536]{3,2,1,0:T(8,128)(2,1)S(1)}, u32[]{:S(2)}, u32[]{:S(2)}) async-start(bf16[4,2,128,1536]{3,2,1,0:T(8,128)(2,1)} %broadcast_in_dim.25), calls=%async_computation.1 | async-start | bytes 6291456 | tf_op jit(solution)/shard_map/all_to_all | solution.py:1018
  36.7 159.3 %all-gather.6.cloned.1.call-start = ((), (), s32[]{:S(2)}) async-start(), calls=%async_computation.9 | async-start | bytes 6684672 | tf_op jit(solution)/shard_map/all_gather | solution.py:1092
  73.2 14.8 %copy-start.19 = (bf16[1,128,1536]{2,1,0:T(8,128)(2,1)S(1)}, bf16[1,128,1536]{2,1,0:T(8,128)(2,1)}, u32[]{:S(2)}) copy-start(bf16[1,128,1536]{2,1,0:T(8,128)(2,1)} %copy-done.18) | copy-start | bytes 1179652
  110.6 21.7 %collective-permute-start.1 = (bf16[1,128,1536]{2,1,0:T(8,128)(2,1)S(1)}, bf16[1,128,1536]{2,1,0:T(8,128)(2,1)S(1)}, u32[]{:S(2)}, u32[]{:S(2)}) collective-permute-start(bf16[1,128,1536]{2,1,0:T(8,128)(2,1)S(1)} %bitcast.82), channel_id=1, source_target_pairs={{0,64},{16,80},{32,96},{48,112},{64,0},{80,16},{96,32},{112,48},{1... | collective-permute-start | bytes 1179656 | tf_op jit(solution)/shard_map/ppermute | solution.py:1070
  134.4 40.6 %all-to-all-start.2 = ((bf16[4,2,128,1536]{3,2,1,0:T(8,128)(2,1)}), bf16[4,2,128,1536]{3,2,1,0:T(8,128)(2,1)S(1)}, u32[]{:S(2)}, u32[]{:S(2)}) async-start(bf16[4,2,128,1536]{3,2,1,0:T(8,128)(2,1)} %broadcast_in_dim.27), calls=%async_computation.2 | async-start | bytes 6291456 | tf_op jit(solution)/shard_map/all_to_all | solution.py:1018
  175.0 49.9 %copy-start.42 = (bf16[4,2,128,1536]{3,2,1,0:T(8,128)(2,1)}, bf16[4,2,128,1536]{3,2,1,0:T(8,128)(2,1)S(1)}, u32[]{:S(2)}) copy-start(bf16[4,2,128,1536]{3,2,1,0:T(8,128)(2,1)S(1)} %all-to-all-done.2) | copy-start | bytes 9437188
  175.0 21.0 %all-to-all-start.3 = ((bf16[16,96,128]{2,1,0:T(8,128)(2,1)}), bf16[16,96,128]{2,1,0:T(8,128)(2,1)}, u32[]{:S(2)}, u32[]{:S(2)}) async-start(bf16[16,96,128]{2,1,0:T(8,128)(2,1)} %copy.64), calls=%async_computation.3 | async-start | bytes 786432 | tf_op jit(solution)/shard_map/all_to_all | solution.py:1018
  227.2 5.7 %collective-permute-start.2 = (bf16[8,128,1536]{2,1,0:T(8,128)(2,1)S(1)}, bf16[8,128,1536]{2,1,0:T(8,128)(2,1)S(1)}, u32[]{:S(2)}, u32[]{:S(2)}) collective-permute-start(bf16[8,128,1536]{2,1,0:T(8,128)(2,1)S(1)} %slice_bitcast_fusion), channel_id=1, source_target_pairs={{0,1},{1,0},{2,3},{3,2},{4,5},{5,4},{6,7},{7,6},{8,9},{9,8},{10,11... | collective-permute-start | bytes 9437192 | tf_op jit(solution)/shard_map/ppermute | solution.py:1104
  235.5 51.4 %all-to-all-start.4 = ((bf16[8,128,1536]{2,1,0:T(8,128)(2,1)}), bf16[8,128,1536]{2,1,0:T(8,128)(2,1)}, u32[]{:S(2)}, u32[]{:S(2)}) async-start(bf16[8,128,1536]{2,1,0:T(8,128)(2,1)} %fusion), calls=%async_computation.4 | async-start | bytes 6291456 | tf_op jit(solution)/shard_map/all_to_all | solution.py:1018
  251.9 13.3 %slice-start.2 = ((s8[6291456]{0:T(1024)(128)(4,1)}), s8[4194304]{0:T(1024)(128)(4,1)S(1)}, s32[]{:S(2)}) async-start(s8[6291456]{0:T(1024)(128)(4,1)} %bitcast.95), calls=%async_computation.13 | async-start | bytes 8388608
  251.9 13.3 %slice-start.3 = ((s8[6291456]{0:T(1024)(128)(4,1)}), s8[2097152]{0:T(1024)(128)(4,1)S(1)}, s32[]{:S(2)}) async-start(s8[6291456]{0:T(1024)(128)(4,1)} %bitcast.95), calls=%async_computation.14 | async-start | bytes 4194304
  251.9 13.3 %copy-start.49 = (bf16[8,2,128,128]{3,2,1,0:T(8,128)(2,1)S(1)}, bf16[8,2,128,128]{3,2,1,0:T(8,128)(2,1)}, u32[]{:S(2)}) copy-start(bf16[8,2,128,128]{3,2,1,0:T(8,128)(2,1)} %get-tuple-element.138) | copy-start | bytes 1572868
  251.9 58.0 %collective-permute-start.3 = (bf16[9216,128]{1,0:T(8,128)(2,1)}, bf16[9216,128]{1,0:T(8,128)(2,1)}, u32[]{:S(2)}, u32[]{:S(2)}) collective-permute-start(bf16[9216,128]{1,0:T(8,128)(2,1)} %get-tuple-element.127), channel_id=1, source_target_pairs={{0,16},{16,0},{32,48},{48,32},{64,80},{80,64},{96,112},{112,96},{1... | collective-permute-start | bytes 7077896 | tf_op jit(solution)/shard_map/ppermute | solution.py:1119
  264.9 53.3 %collective-permute-start.4 = (bf16[9216,128]{1,0:T(8,128)(2,1)}, bf16[9216,128]{1,0:T(8,128)(2,1)}, u32[]{:S(2)}, u32[]{:S(2)}) collective-permute-start(bf16[9216,128]{1,0:T(8,128)(2,1)} %get-tuple-element.136), channel_id=1, source_target_pairs={{0,48},{16,32},{32,16},{48,0},{64,112},{80,96},{96,80},{112,64},{1... | collective-permute-start | bytes 7077896 | tf_op jit(solution)/shard_map/ppermute | solution.py:1119
  305.8 12.4 %copy-start.24 = (bf16[4608,128]{1,0:T(8,128)(2,1)S(1)}, bf16[4608,128]{1,0:T(8,128)(2,1)}, u32[]{:S(2)}) copy-start(bf16[4608,128]{1,0:T(8,128)(2,1)} %get-tuple-element.129.p0) | copy-start | bytes 3538948
  305.8 12.4 %copy-start.25 = (bf16[4608,128]{1,0:T(8,128)(2,1)S(1)}, bf16[4608,128]{1,0:T(8,128)(2,1)}, u32[]{:S(2)}) copy-start(bf16[4608,128]{1,0:T(8,128)(2,1)} %get-tuple-element.135.p6) | copy-start | bytes 3538948
  305.8 12.4 %copy-start.26 = (bf16[4608,128]{1,0:T(8,128)(2,1)S(1)}, bf16[4608,128]{1,0:T(8,128)(2,1)}, u32[]{:S(2)}) copy-start(bf16[4608,128]{1,0:T(8,128)(2,1)} %get-tuple-element.133.p1) | copy-start | bytes 3538948
  305.8 12.4 %copy-start.27 = (bf16[4608,128]{1,0:T(8,128)(2,1)S(1)}, bf16[4608,128]{1,0:T(8,128)(2,1)}, u32[]{:S(2)}) copy-start(bf16[4608,128]{1,0:T(8,128)(2,1)} %get-tuple-element.134.p3) | copy-start | bytes 3538948
  305.8 44.5 %collective-permute-start.9 = (bf16[4,1776,128]{2,1,0:T(8,128)(2,1)}, bf16[4,1776,128]{2,1,0:T(8,128)(2,1)S(1)}, u32[]{:S(2)}, u32[]{:S(2)}) collective-permute-start(bf16[4,1776,128]{2,1,0:T(8,128)(2,1)} %get-tuple-element.154), channel_id=1, source_target_pairs={{0,64},{16,80},{32,96},{48,112},{64,0},{80,16},{96,32},{112,48},{1... | collective-permute-start | bytes 5455880 | tf_op jit(solution)/shard_map/ppermute | solution.py:1147
  309.4 15.1 %collective-permute-start.5 = (bf16[4,128,1536]{2,1,0:T(8,128)(2,1)S(1)}, bf16[4,128,1536]{2,1,0:T(8,128)(2,1)S(1)}, u32[]{:S(2)}, u32[]{:S(2)}) collective-permute-start(bf16[4,128,1536]{2,1,0:T(8,128)(2,1)S(1)} %get-tuple-element.203), channel_id=1, source_target_pairs={{0,1},{1,0},{2,3},{3,2},{4,5},{5,4},{6,7},{7,6},{8,9},{9,8},{10,11... | collective-permute-start | bytes 4718600 | tf_op jit(solution)/shard_map/ppermute | solution.py:1169
  309.5 15.0 %collective-permute-start.6 = (bf16[4,128,1536]{2,1,0:T(8,128)(2,1)S(1)}, bf16[4,128,1536]{2,1,0:T(8,128)(2,1)S(1)}, u32[]{:S(2)}, u32[]{:S(2)}) collective-permute-start(bf16[4,128,1536]{2,1,0:T(8,128)(2,1)S(1)} %get-tuple-element.202), channel_id=1, source_target_pairs={{0,1},{1,0},{2,3},{3,2},{4,5},{5,4},{6,7},{7,6},{8,9},{9,8},{10,11... | collective-permute-start | bytes 4718600 | tf_op jit(solution)/shard_map/ppermute | solution.py:1170
  322.6 26.9 %collective-permute-start.10 = (bf16[4608,128]{1,0:T(8,128)(2,1)S(1)}, bf16[4608,128]{1,0:T(8,128)(2,1)S(1)}, u32[]{:S(2)}, u32[]{:S(2)}) collective-permute-start(bf16[4608,128]{1,0:T(8,128)(2,1)S(1)} %get-tuple-element.157), channel_id=1, source_target_pairs={{0,16},{16,0},{32,48},{48,32},{64,80},{80,64},{96,112},{112,96},{1... | collective-permute-start | bytes 3538952 | tf_op jit(solution)/shard_map/ppermute | solution.py:1119
  324.2 26.1 %collective-permute-start.11 = (bf16[4608,128]{1,0:T(8,128)(2,1)S(1)}, bf16[4608,128]{1,0:T(8,128)(2,1)S(1)}, u32[]{:S(2)}, u32[]{:S(2)}) collective-permute-start(bf16[4608,128]{1,0:T(8,128)(2,1)S(1)} %get-tuple-element.149), channel_id=1, source_target_pairs={{0,48},{16,32},{32,16},{48,0},{64,112},{80,96},{96,80},{112,64},{1... | collective-permute-start | bytes 3538952 | tf_op jit(solution)/shard_map/ppermute | solution.py:1119
  327.4 24.4 %collective-permute-start.7 = (bf16[2,128,1536]{2,1,0:T(8,128)(2,1)S(1)}, bf16[2,128,1536]{2,1,0:T(8,128)(2,1)S(1)}, u32[]{:S(2)}, u32[]{:S(2)}) collective-permute-start(bf16[2,128,1536]{2,1,0:T(8,128)(2,1)S(1)} %get-tuple-element.152), channel_id=1, source_target_pairs={{0,4},{1,5},{2,6},{3,7},{4,0},{5,1},{6,2},{7,3},{8,12},{9,13},{10,... | collective-permute-start | bytes 2359304 | tf_op jit(solution)/shard_map/ppermute | solution.py:1164
  329.2 22.6 %collective-permute-start.8 = (bf16[2,128,1536]{2,1,0:T(8,128)(2,1)S(1)}, bf16[2,128,1536]{2,1,0:T(8,128)(2,1)S(1)}, u32[]{:S(2)}, u32[]{:S(2)}) collective-permute-start(bf16[2,128,1536]{2,1,0:T(8,128)(2,1)S(1)} %get-tuple-element.153), channel_id=1, source_target_pairs={{0,12},{1,13},{2,14},{3,15},{4,8},{5,9},{6,10},{7,11},{8,4},{9,5},... | collective-permute-start | bytes 2359304 | tf_op jit(solution)/shard_map/ppermute | solution.py:1164
  350.7 27.0 %collective-permute-start.12 = (bf16[4608,128]{1,0:T(8,128)(2,1)S(1)}, bf16[4608,128]{1,0:T(8,128)(2,1)}, u32[]{:S(2)}, u32[]{:S(2)}) collective-permute-start(bf16[4608,128]{1,0:T(8,128)(2,1)S(1)} %get-tuple-element.160), channel_id=1, source_target_pairs={{0,64},{16,80},{32,96},{48,112},{64,0},{80,16},{96,32},{112,48},{1... | collective-permute-start | bytes 3538952 | tf_op jit(solution)/shard_map/ppermute | solution.py:1119
  355.2 34.4 %all-to-all-start.5 = ((bf16[4,2160,128]{2,1,0:T(8,128)(2,1)}), bf16[4,2160,128]{2,1,0:T(8,128)(2,1)}, u32[]{:S(2)}, u32[]{:S(2)}) async-start(bf16[4,2160,128]{2,1,0:T(8,128)(2,1)} %merge_shares.1), calls=%async_computation.5 | async-start | bytes 4423680 | tf_op jit(solution)/shard_map/all_to_all | solution.py:1018
  379.2 26.1 %collective-permute-start.15 = (bf16[4608,128]{1,0:T(8,128)(2,1)S(1)}, bf16[4608,128]{1,0:T(8,128)(2,1)}, u32[]{:S(2)}, u32[]{:S(2)}) collective-permute-start(bf16[4608,128]{1,0:T(8,128)(2,1)S(1)} %add_convert_fusion.refs_1_), channel_id=1, source_target_pairs={{0,64},{16,80},{32,96},{48,112},{64,0},{80,16},{96,32},{112,48},{1... | collective-permute-start | bytes 3538952 | tf_op jit(solution)/shard_map/ppermute | solution.py:1119
  380.2 29.4 %collective-permute-start.16 = (bf16[4608,128]{1,0:T(8,128)(2,1)S(1)}, bf16[4608,128]{1,0:T(8,128)(2,1)}, u32[]{:S(2)}, u32[]{:S(2)}) collective-permute-start(bf16[4608,128]{1,0:T(8,128)(2,1)S(1)} %add_convert_fusion.refs_1_), channel_id=1, source_target_pairs={{0,16},{16,0},{32,48},{48,32},{64,80},{80,64},{96,112},{112,96},{1... | collective-permute-start | bytes 3538952 | tf_op jit(solution)/shard_map/ppermute | solution.py:1119
  382.9 28.5 %collective-permute-start.17 = (bf16[4608,128]{1,0:T(8,128)(2,1)S(1)}, bf16[4608,128]{1,0:T(8,128)(2,1)}, u32[]{:S(2)}, u32[]{:S(2)}) collective-permute-start(bf16[4608,128]{1,0:T(8,128)(2,1)S(1)} %add_convert_fusion.refs_1_), channel_id=1, source_target_pairs={{0,48},{16,32},{32,16},{48,0},{64,112},{80,96},{96,80},{112,64},{1... | collective-permute-start | bytes 3538952 | tf_op jit(solution)/shard_map/ppermute | solution.py:1119
  383.2 18.1 %collective-permute-start.13 = (bf16[2,128,1536]{2,1,0:T(8,128)(2,1)}, bf16[2,128,1536]{2,1,0:T(8,128)(2,1)}, u32[]{:S(2)}, u32[]{:S(2)}) collective-permute-start(bf16[2,128,1536]{2,1,0:T(8,128)(2,1)} %get-tuple-element.168), channel_id=1, source_target_pairs={{0,8},{1,9},{2,10},{3,11},{4,12},{5,13},{6,14},{7,15},{8,0},{9,1},... | collective-permute-start | bytes 2359304 | tf_op jit(solution)/shard_map/ppermute | solution.py:1164
  396.7 29.5 %all-to-all-start.6 = ((bf16[16,112,512]{2,1,0:T(8,128)(2,1)}), bf16[16,112,512]{2,1,0:T(8,128)(2,1)S(1)}, u32[]{:S(2)}, u32[]{:S(2)}) async-start(bf16[16,112,512]{2,1,0:T(8,128)(2,1)} %get-tuple-element.165), calls=%async_computation.6 | async-start | bytes 3670016 | tf_op jit(solution)/shard_map/all_to_all | solution.py:1018
  401.3 24.9 %copy-start.40 = (bf16[96,128]{1,0:T(8,128)(2,1)S(1)}, bf16[96,128]{1,0:T(8,128)(2,1)}, u32[]{:S(2)}) copy-start(bf16[96,128]{1,0:T(8,128)(2,1)} %get-tuple-element.172.down_ref) | copy-start | bytes 73732
  411.4 29.2 %collective-permute-start.18 = (bf16[4608,128]{1,0:T(8,128)(2,1)}, bf16[4608,128]{1,0:T(8,128)(2,1)}, u32[]{:S(2)}, u32[]{:S(2)}) collective-permute-start(bf16[4608,128]{1,0:T(8,128)(2,1)} %collective-permute-done.15.refs_4_), channel_id=1, source_target_pairs={{0,16},{16,0},{32,48},{48,32},{64,80},{80,64},{96,112},{112,96},{1... | collective-permute-start | bytes 3538952 | tf_op jit(solution)/shard_map/ppermute | solution.py:1119
  412.8 27.8 %collective-permute-start.19 = (bf16[4608,128]{1,0:T(8,128)(2,1)}, bf16[4608,128]{1,0:T(8,128)(2,1)}, u32[]{:S(2)}, u32[]{:S(2)}) collective-permute-start(bf16[4608,128]{1,0:T(8,128)(2,1)} %collective-permute-done.15.refs_4_), channel_id=1, source_target_pairs={{0,48},{16,32},{32,16},{48,0},{64,112},{80,96},{96,80},{112,64},{1... | collective-permute-start | bytes 3538952 | tf_op jit(solution)/shard_map/ppermute | solution.py:1119
  416.4 24.4 %copy-start.46 = (bf16[8,128,128]{2,1,0:T(8,128)(2,1)S(1)}, bf16[8,128,128]{2,1,0:T(8,128)(2,1)}, u32[]{:S(2)}) copy-start(bf16[8,128,128]{2,1,0:T(8,128)(2,1)} %get-tuple-element.171) | copy-start | bytes 786436
  416.4 76.1 %collective-permute-start.20 = (bf16[4608,128]{1,0:T(8,128)(2,1)}, bf16[4608,128]{1,0:T(8,128)(2,1)}, u32[]{:S(2)}, u32[]{:S(2)}) collective-permute-start(bf16[4608,128]{1,0:T(8,128)(2,1)} %collective-permute-done.17.refs_3_), channel_id=1, source_target_pairs={{0,16},{16,0},{32,48},{48,32},{64,80},{80,64},{96,112},{112,96},{1... | collective-permute-start | bytes 3538952 | tf_op jit(solution)/shard_map/ppermute | solution.py:1119
  442.2 41.7 %all-to-all-start.7 = ((bf16[8,864,128]{2,1,0:T(8,128)(2,1)}), bf16[8,864,128]{2,1,0:T(8,128)(2,1)S(1)}, u32[]{:S(2)}, u32[]{:S(2)}) async-start(bf16[8,864,128]{2,1,0:T(8,128)(2,1)} %pad_maximum_fusion), calls=%async_computation.7 | async-start | bytes 3538944 | tf_op jit(solution)/shard_map/all_to_all | solution.py:1018
  450.2 13.2 %collective-permute-start.14 = (bf16[128,1536]{1,0:T(8,128)(2,1)}, bf16[128,1536]{1,0:T(8,128)(2,1)}, u32[]{:S(2)}, u32[]{:S(2)}) collective-permute-start(bf16[128,1536]{1,0:T(8,128)(2,1)} %fusion.5), channel_id=1, source_target_pairs={{0,2},{1,3},{2,0},{3,1},{4,6},{5,7},{6,4},{7,5},{8,10},{9,11},{10,... | collective-permute-start | bytes 1179656 | tf_op jit(solution)/shard_map/ppermute | solution.py:1189
  451.2 41.9 %collective-permute-start.21 = (bf16[4608,128]{1,0:T(8,128)(2,1)}, bf16[4608,128]{1,0:T(8,128)(2,1)}, u32[]{:S(2)}, u32[]{:S(2)}) collective-permute-start(bf16[4608,128]{1,0:T(8,128)(2,1)} %collective-permute-done.18.refs_5_), channel_id=1, source_target_pairs={{0,48},{16,32},{32,16},{48,0},{64,112},{80,96},{96,80},{112,64},{1... | collective-permute-start | bytes 3538952 | tf_op jit(solution)/shard_map/ppermute | solution.py:1119
  465.8 18.1 %copy-start.28 = (bf16[96,1536]{1,0:T(8,128)(2,1)S(1)}, bf16[96,1536]{1,0:T(8,128)(2,1)}, u32[]{:S(2)}) copy-start(bf16[96,1536]{1,0:T(8,128)(2,1)} %wq_ref.1) | copy-start | bytes 884740
  465.8 18.1 %copy-start.36 = (bf16[96,512]{1,0:T(8,128)(2,1)S(1)}, bf16[96,512]{1,0:T(8,128)(2,1)}, u32[]{:S(2)}) copy-start(bf16[96,512]{1,0:T(8,128)(2,1)} %wk_ref.1) | copy-start | bytes 294916
  465.8 18.1 %copy-start.37 = (bf16[96,512]{1,0:T(8,128)(2,1)S(1)}, bf16[96,512]{1,0:T(8,128)(2,1)}, u32[]{:S(2)}) copy-start(bf16[96,512]{1,0:T(8,128)(2,1)} %wv_ref.1) | copy-start | bytes 294916
  474.0 11.7 %copy-start.12 = (f32[128,1536]{1,0:T(8,128)S(1)}, f32[128,1536]{1,0:T(8,128)}, u32[]{:S(2)}) copy-start(f32[128,1536]{1,0:T(8,128)} %copy-done.11) | copy-start | bytes 2359300
  (42 other events, 176.5 us)
Sparse Core Ops, SparseCore 0:
  12.2 75.8 all-gather.3
  90.3 52.3 all-gather.7
  145.0 46.8 all-gather.5
